TPU v7x, 32 devices: a whole 2x2x4 slice. The times are simulated.
32 devices in a mesh: groups: 2 (over y), tiles: 16 (over z, x, core).
Axes of the slice: x: 2, y: 2, z: 4, core: 2. Of those that a mesh axis runs over, the one named last changes fastest.
Arguments:
- hidden: bfloat16 [6144, 3072], P(('groups', 'tiles')), parts along dimension 0, may hold values from -6 to 6
- queries: bfloat16 [6144, 1536], P(('groups', 'tiles')), parts along dimension 0, may hold values from -5 to 5
- keys: bfloat16 [6144, 1536], P(('groups', 'tiles')), parts along dimension 0, may hold values from -5 to 5
- values: bfloat16 [6144, 1536], P(('groups', 'tiles')), parts along dimension 0, may hold values from -6 to 6
- control: bfloat16 [6144, 3072], P(('groups', 'tiles')), parts along dimension 0, may hold values from -6 to 6
- out_weight: bfloat16 [1536, 3072], P('tiles'), may hold values from -2 to 2
- pattern: int32 [32, 6], P(('groups', 'tiles')), parts along dimension 0, may hold values 0 or 1
Outputs:
- block_out: bfloat16 [6144, 3072], P(('groups', 'tiles')), parts along dimension 0
There are 2 independent parts, one for each index of `groups`. A program takes and returns all parts, laid end to end along the dimension named above; an argument that names none is the same for every part. Nothing has to cross between parts.
All inputs are finite; a program needn't handle non-finite values. No bound on the sum of `pattern` on one device may be relied on, other than what follows from the above.
Results may differ from a plain program's by a relative error of at most 0.0055.
Values may be sent and summed in bfloat16 or wider, within the bound.
No kernel may reach another device: no remote copies, remote signals or barrier semaphores. Data moves between devices by JAX's collectives and lax.ppermute only.
A program may use at most 128 MiB of HBM per device.

v0:
```python
import jax
import jax.numpy as jnp
from jax import lax
from jax.sharding import PartitionSpec as P

HEAD_DIM = 128
TILE_W = 8


def swapped(block, axis, distance):
    count = lax.axis_size(axis)
    route = []
    for low in range(count):
        high = low | 1 << distance
        if high != low and high < count:
            route += [(low, high), (high, low)]
    return lax.ppermute(block, axis, route)


def passed_along(block, axis, distance):
    devices = range(lax.axis_size(axis))
    route = [(i - distance, i) for i in devices if i - distance in devices]
    return lax.ppermute(block, axis, route)


def pair_terms(query_tile, key_tile, value_tile):
    scores = jnp.einsum(
        "qhd,khd->hqk", query_tile, key_tile, preferred_element_type=jnp.float32
    ) * HEAD_DIM ** (-0.5)
    peak_rows = jnp.max(scores, axis=-1)
    weights = jnp.exp(scores - peak_rows[:, :, None]).astype(jnp.bfloat16)
    total = jnp.sum(weights, axis=-1, dtype=jnp.float32)
    output = jnp.einsum("hqk,khd->qhd", weights, value_tile, preferred_element_type=jnp.float32)
    return (output, peak_rows, total)


def combine(partials, active_list):
    peak_stack = jnp.stack(
        [jnp.where(active, item[1], -1e30) for item, active in zip(partials, active_list)]
    )
    largest = jnp.max(peak_stack, axis=0)
    factors = jnp.exp(peak_stack - largest[None])
    numerator = jnp.zeros_like(partials[0][0])
    denominator = jnp.zeros_like(partials[0][2])
    for number in range(len(partials)):
        numerator = numerator + factors[number].T[:, :, None] * partials[number][0]
        denominator = denominator + factors[number] * partials[number][2]
    result = numerator / denominator.T[:, :, None]
    return result.reshape(result.shape[0], -1).astype(jnp.bfloat16)


def relay_control(control, across, grid_width):
    rows, width = control.shape
    slab_lines = rows // (grid_width * TILE_W)
    slab_blocks = control.reshape(slab_lines, grid_width, TILE_W, width).transpose(1, 0, 2, 3)
    slab_blocks = slab_blocks.reshape(grid_width, rows // grid_width, width)
    positions = jnp.arange(grid_width, dtype=jnp.int32)
    order = jnp.bitwise_xor(across, positions)
    buffer = jnp.take(slab_blocks, order, axis=0)
    for bit in range(grid_width.bit_length() - 1):
        low = 1 << bit
        shaped = buffer.reshape(grid_width // (2 * low), 2, low, rows // grid_width, width)
        incoming = swapped(shaped[:, 1], "tiles", bit)
        buffer = jnp.stack([shaped[:, 0], incoming], axis=1).reshape(
            grid_width, rows // grid_width, width
        )
    arranged = jnp.take(buffer, order, axis=0)
    return arranged.reshape(rows, width)


def on_device(hidden, queries, keys, values, control, out_weight, pattern):
    rows, width = hidden.shape
    inner = queries.shape[1]
    heads = inner // HEAD_DIM
    tile_count = lax.axis_size("tiles")
    grid_width = min(8, tile_count // 4)
    grid_height = min(4, tile_count // 8)
    layer = grid_width * grid_height
    frame_count = tile_count // layer
    position = lax.axis_index("tiles")
    frame_tile = position // layer
    row_tile = position // grid_width % grid_height
    across = position % grid_width
    limits = (
        frame_tile >= 1,
        frame_tile <= frame_count - 2,
        row_tile >= 1,
        row_tile <= grid_height - 2,
        across >= 1,
        across <= grid_width - 2,
    )
    offsets = (-layer, layer, -grid_width, grid_width, -1, 1)
    query_tile = queries.reshape(rows, heads, HEAD_DIM)
    key_tile = keys.reshape(rows, heads, HEAD_DIM)
    value_tile = values.reshape(rows, heads, HEAD_DIM)
    partials = [pair_terms(query_tile, key_tile, value_tile)]
    active_list = [jnp.array(True)]
    for direction in range(6):
        offset = offsets[direction]
        active_list.append(limits[direction] & (pattern[0, direction] == 1))
        near_keys, near_values = passed_along((keys, values), "tiles", -offset)
        partials.append(
            pair_terms(
                query_tile,
                near_keys.reshape(rows, heads, HEAD_DIM),
                near_values.reshape(rows, heads, HEAD_DIM),
            )
        )
    attention = combine(partials, active_list)
    control_tiles = relay_control(control, across, grid_width)
    full_weight = lax.all_gather(out_weight, "tiles", axis=0, tiled=True)
    projected = jnp.dot(attention, full_weight, preferred_element_type=jnp.float32)
    block_out = hidden.astype(jnp.float32) + projected + control_tiles.astype(jnp.float32)
    return block_out.astype(jnp.bfloat16)


def solution(mesh):
    placed = (
        P(("groups", "tiles"), None),
        P(("groups", "tiles"), None),
        P(("groups", "tiles"), None),
        P(("groups", "tiles"), None),
        P(("groups", "tiles"), None),
        P("tiles", None),
        P(("groups", "tiles"), None),
    )
    return jax.shard_map(
        on_device,
        mesh=mesh,
        in_specs=placed,
        out_specs=P(("groups", "tiles"), None),
        check_vma=False,
    )
```

profile of v0, /device:TPU:20, one launch (start us, length us, event | category | flops | bytes accessed | tf_op | source)
XLA Modules:
  0.0 186.5 jit_solution(16145475063628953243)
XLA Ops:
  6.5 0.7 all-gather.2.cloned.1.call-update
  7.3 1.3 collective-permute-start
  8.6 7.1 %collective-permute-start.1 = (bf16[192,1536]{1,0:T(8,128)(2,1)}, bf16[192,1536]{1,0:T(8,128)(2,1)}, u32[]{:S(2)}, u32[]{:S(2)}) collective-permute-start(bf16[192,1536]{1,0:T(8,128)(2,1)} %param.11), channel_id=1, source_target_pairs={{8,0},{9,1},{10,2},{11,3},{12,4},{13,5},{14,6},{15,7},{24,16},{25,... | collective-permute-start | bytes 1769480 | tf_op jit(solution)/shard_map/ppermute | solution.py:23
  15.6 3.5 %collective-permute-start.2 = (bf16[192,1536]{1,0:T(8,128)(2,1)}, bf16[192,1536]{1,0:T(8,128)(2,1)}, u32[]{:S(2)}, u32[]{:S(2)}) collective-permute-start(bf16[192,1536]{1,0:T(8,128)(2,1)} %param.11), channel_id=1, source_target_pairs={{0,4},{1,5},{2,6},{3,7},{4,8},{5,9},{6,10},{7,11},{8,12},{9,13},{1... | collective-permute-start | bytes 1769480 | tf_op jit(solution)/shard_map/ppermute | solution.py:23
  19.1 2.4 %collective-permute-start.3 = (bf16[192,1536]{1,0:T(8,128)(2,1)}, bf16[192,1536]{1,0:T(8,128)(2,1)}, u32[]{:S(2)}, u32[]{:S(2)}) collective-permute-start(bf16[192,1536]{1,0:T(8,128)(2,1)} %param.11), channel_id=1, source_target_pairs={{4,0},{5,1},{6,2},{7,3},{8,4},{9,5},{10,6},{11,7},{12,8},{13,9},{1... | collective-permute-start | bytes 1769480 | tf_op jit(solution)/shard_map/ppermute | solution.py:23
  21.5 1.9 %collective-permute-start.4 = (bf16[192,1536]{1,0:T(8,128)(2,1)}, bf16[192,1536]{1,0:T(8,128)(2,1)}, u32[]{:S(2)}, u32[]{:S(2)}) collective-permute-start(bf16[192,1536]{1,0:T(8,128)(2,1)} %param.11), channel_id=1, source_target_pairs={{0,1},{1,2},{2,3},{3,4},{4,5},{5,6},{6,7},{7,8},{8,9},{9,10},{10,1... | collective-permute-start | bytes 1769480 | tf_op jit(solution)/shard_map/ppermute | solution.py:23
  23.4 1.4 copy.231
  24.9 1.6 gather_fusion
  26.6 0.5 multiply_reduce_fusion.6
  27.1 0.6 bitcast_dynamic-update-slice_fusion.6
  27.7 0.1 copy-done.1
  27.8 0.2 broadcast_select_fusion
  28.0 0.9 slice_bitcast_fusion.3
  28.9 0.7 fusion.83
  33.4 24.7 %collective-permute-start.5 = (bf16[192,1536]{1,0:T(8,128)(2,1)}, bf16[192,1536]{1,0:T(8,128)(2,1)S(1)}, u32[]{:S(2)}, u32[]{:S(2)}) collective-permute-start(bf16[192,1536]{1,0:T(8,128)(2,1)} %param.11), channel_id=1, source_target_pairs={{1,0},{2,1},{3,2},{4,3},{5,4},{6,5},{7,6},{8,7},{9,8},{10,9},{11,1... | collective-permute-start | bytes 1769480 | tf_op jit(solution)/shard_map/ppermute | solution.py:23
  58.1 1.6 multiply_reduce_fusion.5
  59.7 0.5 collective-permute-done.1
  60.2 1.3 collective-permute-start.6
  61.5 1.6 multiply_reduce_fusion.4
  63.1 38.0 %collective-permute-done.2 = bf16[192,1536]{1,0:T(8,128)(2,1)} collective-permute-done((bf16[192,1536]{1,0:T(8,128)(2,1)}, bf16[192,1536]{1,0:T(8,128)(2,1)}, u32[]{:S(2)}, u32[]{:S(2)}) %collective-permute-start.2) | collective-permute-done | bytes 589856 | tf_op jit(solution)/shard_map/ppermute | solution.py:23
  101.0 1.3 collective-permute-start.7
  102.3 1.6 multiply_reduce_fusion.3
  103.9 3.3 %collective-permute-start.8 = (bf16[192,1536]{1,0:T(8,128)(2,1)S(1)}, bf16[192,1536]{1,0:T(8,128)(2,1)S(1)}, u32[]{:S(2)}, u32[]{:S(2)}) collective-permute-start(bf16[192,1536]{1,0:T(8,128)(2,1)S(1)} %copy-done.3), channel_id=1, source_target_pairs={{0,4},{1,5},{2,6},{3,7},{4,8},{5,9},{6,10},{7,11},{8,12},{9,13},{1... | collective-permute-start | bytes 1769480 | tf_op jit(solution)/shard_map/ppermute | solution.py:23
  107.2 1.6 multiply_reduce_fusion.2
  108.8 24.4 %collective-permute-done.4 = bf16[192,1536]{1,0:T(8,128)(2,1)} collective-permute-done((bf16[192,1536]{1,0:T(8,128)(2,1)}, bf16[192,1536]{1,0:T(8,128)(2,1)}, u32[]{:S(2)}, u32[]{:S(2)}) %collective-permute-start.4) | collective-permute-done | bytes 589856 | tf_op jit(solution)/shard_map/ppermute | solution.py:23
  133.2 1.9 %collective-permute-start.9 = (bf16[192,1536]{1,0:T(8,128)(2,1)S(1)}, bf16[192,1536]{1,0:T(8,128)(2,1)S(1)}, u32[]{:S(2)}, u32[]{:S(2)}) collective-permute-start(bf16[192,1536]{1,0:T(8,128)(2,1)S(1)} %copy-done.3), channel_id=1, source_target_pairs={{4,0},{5,1},{6,2},{7,3},{8,4},{9,5},{10,6},{11,7},{12,8},{13,9},{1... | collective-permute-start | bytes 1769480 | tf_op jit(solution)/shard_map/ppermute | solution.py:23
  135.1 1.6 multiply_reduce_fusion.1
  136.8 0.5 multiply_reduce_fusion
  137.4 1.0 fusion.15
  138.4 0.3 collective-permute-done.12
  138.7 2.1 %collective-permute-start.10 = (bf16[192,1536]{1,0:T(8,128)(2,1)S(1)}, bf16[192,1536]{1,0:T(8,128)(2,1)S(1)}, u32[]{:S(2)}, u32[]{:S(2)}) collective-permute-start(bf16[192,1536]{1,0:T(8,128)(2,1)S(1)} %copy-done.3), channel_id=1, source_target_pairs={{0,1},{1,2},{2,3},{3,4},{4,5},{5,6},{6,7},{7,8},{8,9},{9,10},{10,1... | collective-permute-start | bytes 1769480 | tf_op jit(solution)/shard_map/ppermute | solution.py:23
  140.8 0.1 maximum_bitcast_fusion
  141.1 6.5 %collective-permute-start.11 = (bf16[192,1536]{1,0:T(8,128)(2,1)S(1)}, bf16[192,1536]{1,0:T(8,128)(2,1)S(1)}, u32[]{:S(2)}, u32[]{:S(2)}) collective-permute-start(bf16[192,1536]{1,0:T(8,128)(2,1)S(1)} %copy-done.3), channel_id=1, source_target_pairs={{1,0},{2,1},{3,2},{4,3},{5,4},{6,5},{7,6},{8,7},{9,8},{10,9},{11,1... | collective-permute-start | bytes 1769480 | tf_op jit(solution)/shard_map/ppermute | solution.py:23
  147.6 1.2 fusion.14
  148.8 0.9 convert_reduce_fusion.3
  149.8 1.2 fusion.12
  151.0 1.2 fusion.10
  152.1 1.0 convert_reduce_fusion.5
  153.1 0.9 convert_reduce_fusion.1
  154.0 0.4 convert_reduce_fusion
  154.5 1.2 fusion.8
  155.7 3.4 %collective-permute-done.10 = bf16[192,1536]{1,0:T(8,128)(2,1)S(1)} collective-permute-done((bf16[192,1536]{1,0:T(8,128)(2,1)S(1)}, bf16[192,1536]{1,0:T(8,128)(2,1)S(1)}, u32[]{:S(2)}, u32[]{:S(2)}) %collective-permute-start.10) | collective-permute-done | bytes 589856 | tf_op jit(solution)/shard_map/ppermute | solution.py:23
  159.1 1.1 fusion.6
  160.3 1.4 fusion.17
  161.7 9.7 %collective-permute-done.13 = bf16[1,2,48,3072]{3,2,1,0:T(8,128)(2,1)S(1)} collective-permute-done((bf16[1,2,48,3072]{3,2,1,0:T(8,128)(2,1)S(1)}, bf16[1,2,48,3072]{3,2,1,0:T(8,128)(2,1)S(1)}, u32[]{:S(2)}, u32[]{:S(2)}) %collective-permute-start.13) | collective-permute-done | bytes 589856 | tf_op jit(solution)/shard_map/ppermute | solution.py:17
  171.5 0.7 gather_fusion.1
  172.3 0.2 broadcast_select_fusion.1
  172.5 7.2 %fusion.1 = bf16[192,3072]{1,0:T(8,128)(2,1)} fusion(bf16[1536,3072]{1,0:T(8,128)(2,1)} %all-gather.2.cloned.1.call-done, bf16[192,3072]{1,0:T(8,128)(2,1)S(1)} %bitcast.323, bf16[192,3072]{1,0:T(8,128)(2,1)} %param.9, bf16[12,24,8,128]{3,2,1,0:T(8,128)(2,1)S(1)} %fusion.17), kind=kOutput, calls=%fused_computation.4 | convolution fusion | flops 1814888448 | bytes 13565952 | tf_op jit(solution)/shard_map/dot_general | solution.py:112
  (46 shorter events, 0.6 us)
Async XLA Ops:
  6.5 20.0 %copy-start = (bf16[192,1536]{1,0:T(8,128)(2,1)S(1)}, bf16[192,1536]{1,0:T(8,128)(2,1)}, u32[]{:S(2)}) copy-start(bf16[192,1536]{1,0:T(8,128)(2,1)} %param.10) | copy-start | bytes 1769476
  6.5 166.0 %all-gather.2.cloned.1.call-start = ((), (), s32[]{:S(2)}) async-start(), calls=%async_computation | async-start | bytes 10027008 | tf_op jit(solution)/shard_map/all_gather | solution.py:111
  7.3 26.1 %collective-permute-start = (bf16[192,1536]{1,0:T(8,128)(2,1)}, bf16[192,1536]{1,0:T(8,128)(2,1)}, u32[]{:S(2)}, u32[]{:S(2)}) collective-permute-start(bf16[192,1536]{1,0:T(8,128)(2,1)} %param.11), channel_id=1, source_target_pairs={{0,8},{1,9},{2,10},{3,11},{4,12},{5,13},{6,14},{7,15},{16,24},{17,... | collective-permute-start | bytes 1769480 | tf_op jit(solution)/shard_map/ppermute | solution.py:23
  8.6 51.6 %collective-permute-start.1 = (bf16[192,1536]{1,0:T(8,128)(2,1)}, bf16[192,1536]{1,0:T(8,128)(2,1)}, u32[]{:S(2)}, u32[]{:S(2)}) collective-permute-start(bf16[192,1536]{1,0:T(8,128)(2,1)} %param.11), channel_id=1, source_target_pairs={{8,0},{9,1},{10,2},{11,3},{12,4},{13,5},{14,6},{15,7},{24,16},{25,... | collective-permute-start | bytes 1769480 | tf_op jit(solution)/shard_map/ppermute | solution.py:23
  15.6 85.4 %collective-permute-start.2 = (bf16[192,1536]{1,0:T(8,128)(2,1)}, bf16[192,1536]{1,0:T(8,128)(2,1)}, u32[]{:S(2)}, u32[]{:S(2)}) collective-permute-start(bf16[192,1536]{1,0:T(8,128)(2,1)} %param.11), channel_id=1, source_target_pairs={{0,4},{1,5},{2,6},{3,7},{4,8},{5,9},{6,10},{7,11},{8,12},{9,13},{1... | collective-permute-start | bytes 1769480 | tf_op jit(solution)/shard_map/ppermute | solution.py:23
  19.1 84.8 %collective-permute-start.3 = (bf16[192,1536]{1,0:T(8,128)(2,1)}, bf16[192,1536]{1,0:T(8,128)(2,1)}, u32[]{:S(2)}, u32[]{:S(2)}) collective-permute-start(bf16[192,1536]{1,0:T(8,128)(2,1)} %param.11), channel_id=1, source_target_pairs={{4,0},{5,1},{6,2},{7,3},{8,4},{9,5},{10,6},{11,7},{12,8},{13,9},{1... | collective-permute-start | bytes 1769480 | tf_op jit(solution)/shard_map/ppermute | solution.py:23
  21.5 111.7 %collective-permute-start.4 = (bf16[192,1536]{1,0:T(8,128)(2,1)}, bf16[192,1536]{1,0:T(8,128)(2,1)}, u32[]{:S(2)}, u32[]{:S(2)}) collective-permute-start(bf16[192,1536]{1,0:T(8,128)(2,1)} %param.11), channel_id=1, source_target_pairs={{0,1},{1,2},{2,3},{3,4},{4,5},{5,6},{6,7},{7,8},{8,9},{9,10},{10,1... | collective-permute-start | bytes 1769480 | tf_op jit(solution)/shard_map/ppermute | solution.py:23
  23.4 3.1 %copy-start.2 = (bf16[192,1536]{1,0:T(8,128)(2,1)S(1)}, bf16[192,1536]{1,0:T(8,128)(2,1)}, u32[]{:S(2)}) copy-start(bf16[192,1536]{1,0:T(8,128)(2,1)} %param.11) | copy-start | bytes 1769476
  24.9 1.6 copy-start.7
  26.5 1.3 copy-start.1
  26.6 1.4 copy-start.8
  27.8 1.1 copy-start.6
  33.4 26.3 %copy-start.5 = (f32[7,12,192]{2,1,0:T(8,128)S(1)}, f32[7,12,192]{2,1,0:T(8,128)}, u32[]{:S(2)}) copy-start(f32[7,12,192]{2,1,0:T(8,128)} %bitcast_dynamic-update-slice_fusion.6) | copy-start | bytes 193540
  33.4 26.8 %copy-start.3 = (bf16[192,1536]{1,0:T(8,128)(2,1)S(1)}, bf16[192,1536]{1,0:T(8,128)(2,1)}, u32[]{:S(2)}) copy-start(bf16[192,1536]{1,0:T(8,128)(2,1)} %param.12) | copy-start | bytes 1769476
  33.4 103.3 %collective-permute-start.5 = (bf16[192,1536]{1,0:T(8,128)(2,1)}, bf16[192,1536]{1,0:T(8,128)(2,1)S(1)}, u32[]{:S(2)}, u32[]{:S(2)}) collective-permute-start(bf16[192,1536]{1,0:T(8,128)(2,1)} %param.11), channel_id=1, source_target_pairs={{1,0},{2,1},{3,2},{4,3},{5,4},{6,5},{7,6},{8,7},{9,8},{10,9},{11,1... | collective-permute-start | bytes 1769480 | tf_op jit(solution)/shard_map/ppermute | solution.py:23
  60.2 80.9 %collective-permute-start.6 = (bf16[192,1536]{1,0:T(8,128)(2,1)S(1)}, bf16[192,1536]{1,0:T(8,128)(2,1)S(1)}, u32[]{:S(2)}, u32[]{:S(2)}) collective-permute-start(bf16[192,1536]{1,0:T(8,128)(2,1)S(1)} %copy-done.3), channel_id=1, source_target_pairs={{0,8},{1,9},{2,10},{3,11},{4,12},{5,13},{6,14},{7,15},{16,24},{17,... | collective-permute-start | bytes 1769480 | tf_op jit(solution)/shard_map/ppermute | solution.py:23
  101.0 48.7 %collective-permute-start.7 = (bf16[192,1536]{1,0:T(8,128)(2,1)S(1)}, bf16[192,1536]{1,0:T(8,128)(2,1)S(1)}, u32[]{:S(2)}, u32[]{:S(2)}) collective-permute-start(bf16[192,1536]{1,0:T(8,128)(2,1)S(1)} %copy-done.3), channel_id=1, source_target_pairs={{8,0},{9,1},{10,2},{11,3},{12,4},{13,5},{14,6},{15,7},{24,16},{25,... | collective-permute-start | bytes 1769480 | tf_op jit(solution)/shard_map/ppermute | solution.py:23
  103.9 47.0 %collective-permute-start.8 = (bf16[192,1536]{1,0:T(8,128)(2,1)S(1)}, bf16[192,1536]{1,0:T(8,128)(2,1)S(1)}, u32[]{:S(2)}, u32[]{:S(2)}) collective-permute-start(bf16[192,1536]{1,0:T(8,128)(2,1)S(1)} %copy-done.3), channel_id=1, source_target_pairs={{0,4},{1,5},{2,6},{3,7},{4,8},{5,9},{6,10},{7,11},{8,12},{9,13},{1... | collective-permute-start | bytes 1769480 | tf_op jit(solution)/shard_map/ppermute | solution.py:23
  108.8 27.9 %copy-start.4 = (bf16[2,1,48,3072]{3,2,0,1:T(8,128)(2,1)S(1)}, bf16[2,1,48,3072]{3,2,0,1:T(8,128)(2,1)}, u32[]{:S(2)}) copy-start(bf16[2,1,48,3072]{3,2,0,1:T(8,128)(2,1)} %get-tuple-element.9) | copy-start | bytes 1769476
  133.2 21.3 %collective-permute-start.9 = (bf16[192,1536]{1,0:T(8,128)(2,1)S(1)}, bf16[192,1536]{1,0:T(8,128)(2,1)S(1)}, u32[]{:S(2)}, u32[]{:S(2)}) collective-permute-start(bf16[192,1536]{1,0:T(8,128)(2,1)S(1)} %copy-done.3), channel_id=1, source_target_pairs={{4,0},{5,1},{6,2},{7,3},{8,4},{9,5},{10,6},{11,7},{12,8},{13,9},{1... | collective-permute-start | bytes 1769480 | tf_op jit(solution)/shard_map/ppermute | solution.py:23
  136.7 2.1 %collective-permute-start.12 = (bf16[2,1,48,3072]{3,2,0,1:T(8,128)(2,1)S(1)}, bf16[2,1,48,3072]{3,2,0,1:T(8,128)(2,1)S(1)}, u32[]{:S(2)}, u32[]{:S(2)}) collective-permute-start(bf16[2,1,48,3072]{3,2,0,1:T(8,128)(2,1)S(1)} %copy-done.4), channel_id=1, source_target_pairs={{0,1},{1,0},{2,3},{3,2},{4,5},{5,4},{6,7},{7,6},{8,9},{9,8},{10,11... | collective-permute-start | bytes 1769480 | tf_op jit(solution)/shard_map/ppermute | solution.py:17
  138.7 20.3 %collective-permute-start.10 = (bf16[192,1536]{1,0:T(8,128)(2,1)S(1)}, bf16[192,1536]{1,0:T(8,128)(2,1)S(1)}, u32[]{:S(2)}, u32[]{:S(2)}) collective-permute-start(bf16[192,1536]{1,0:T(8,128)(2,1)S(1)} %copy-done.3), channel_id=1, source_target_pairs={{0,1},{1,2},{2,3},{3,4},{4,5},{5,6},{6,7},{7,8},{8,9},{9,10},{10,1... | collective-permute-start | bytes 1769480 | tf_op jit(solution)/shard_map/ppermute | solution.py:23
  141.1 19.2 %collective-permute-start.11 = (bf16[192,1536]{1,0:T(8,128)(2,1)S(1)}, bf16[192,1536]{1,0:T(8,128)(2,1)S(1)}, u32[]{:S(2)}, u32[]{:S(2)}) collective-permute-start(bf16[192,1536]{1,0:T(8,128)(2,1)S(1)} %copy-done.3), channel_id=1, source_target_pairs={{1,0},{2,1},{3,2},{4,3},{5,4},{6,5},{7,6},{8,7},{9,8},{10,9},{11,1... | collective-permute-start | bytes 1769480 | tf_op jit(solution)/shard_map/ppermute | solution.py:23
  149.7 21.7 %collective-permute-start.13 = (bf16[1,2,48,3072]{3,2,1,0:T(8,128)(2,1)S(1)}, bf16[1,2,48,3072]{3,2,1,0:T(8,128)(2,1)S(1)}, u32[]{:S(2)}, u32[]{:S(2)}) collective-permute-start(bf16[1,2,48,3072]{3,2,1,0:T(8,128)(2,1)S(1)} %get-tuple-element.7), channel_id=1, source_target_pairs={{0,2},{2,0},{1,3},{3,1},{4,6},{6,4},{5,7},{7,5},{8,10},{10,8},{9,1... | collective-permute-start | bytes 1769480 | tf_op jit(solution)/shard_map/ppermute | solution.py:17
  171.4 0.9 copy-start.9
Sparse Core Ops, SparseCore 0:
  9.6 124.5 all-gather.1
where the time goes:
time: 187 us
  waiting for transfers between devices  77 us (41%)
  starting transfers between devices  57.3 us (31%)
  matrix products  24.3 us (13%)
  between operations  17.7 us (9%)
  local copies, waits for them, and re-layouts  6.23 us (3%)
  other arithmetic  3.94 us (2%)
    ppermute x12, waiting for transfers between devices, passed_along(): return lax.ppermute(block, axis, route)  66.2 us
    ppermute x12, starting transfers between devices, passed_along(): return lax.ppermute(block, axis, route)  57.2 us
    ppermute x2, waiting for transfers between devices, swapped(): return lax.ppermute(block, axis, route)  10.1 us
    dot_general x7, matrix products, pair_terms(): jnp.einsum('qhd,khd->hqk', query_tile, key_tile, preferred_element_type=j...  8.8 us
    dot_general x7, matrix products, pair_terms(): jnp.einsum('hqk,khd->qhd', weights, value_tile, preferred_element_type=jn...  8.26 us
    dot_general x1, matrix products, on_device(): jnp.dot(attention, full_weight, preferred_element_type=jnp.float32)  7.2 us
  transfers between devices with their start and end apart: 15, of which 6 were waited for; matrix products, arithmetic and copies ran while one was open for 15% of the time, Pallas kernels for 0%

commit v1 on v0

v1 whole, which is shorter than its diff:
```python
import functools
import math

import jax
import jax.numpy as jnp
from jax import lax
from jax.experimental import pallas as pl
from jax.experimental.pallas import tpu as pltpu
from jax.sharding import Mesh
from jax.sharding import PartitionSpec as P

HEAD_DIM = 128
TILE_W = 8
SCALE = HEAD_DIM**-0.5 * math.log2(math.e)
TILES = ("outer", "pair", "core")
VMEM_LIMIT = 40 * 1024 * 1024


def head_part(q, k, v):
    scores = lax.dot_general(q, k, (((1,), (1,)), ((), ())), preferred_element_type=jnp.float32)
    peak = jnp.max(scores, axis=1, keepdims=True)
    weights = jnp.exp2((scores - peak) * SCALE).astype(jnp.bfloat16)
    ones = jnp.ones((v.shape[0], HEAD_DIM), jnp.bfloat16)
    both = jnp.dot(weights, jnp.concatenate([v, ones], axis=1), preferred_element_type=jnp.float32)
    return both[:, :HEAD_DIM], both[:, HEAD_DIM:], jnp.broadcast_to(peak, v.shape)


def merge(old, new):
    part, total, peak = old
    part_new, total_new, peak_new = new
    top = jnp.maximum(peak, peak_new)
    f_old = jnp.exp2((peak - top) * SCALE)
    f_new = jnp.exp2((peak_new - top) * SCALE)
    return f_old * part + f_new * part_new, f_old * total + f_new * total_new, top


def attend_kernel(slots, first, active, q, *refs):
    kv = refs[: 2 * slots]
    refs = refs[2 * slots :]
    if not first:
        state_in, refs = refs[:3], refs[3:]
    state = refs[:3]
    heads = q.shape[1] // HEAD_DIM
    for h in range(heads):
        at = pl.ds(h * HEAD_DIM, HEAD_DIM)
        if first:
            now = head_part(q[:, at], kv[0][:, at], kv[1][:, at])
        else:
            now = tuple(r[:, at] for r in state_in)
        for r, x in zip(state, now):
            r[:, at] = x
    for slot in range(1 if first else 0, slots):

        @pl.when(active[slot] == 1)
        def _():
            for h in range(heads):
                at = pl.ds(h * HEAD_DIM, HEAD_DIM)
                new = head_part(q[:, at], kv[2 * slot][:, at], kv[2 * slot + 1][:, at])
                for r, x in zip(state, merge(tuple(r[:, at] for r in state), new)):
                    r[:, at] = x


def attend(active, q, kv, state):
    slots = len(kv) // 2
    rows, inner = q.shape
    shape = jax.ShapeDtypeStruct((rows, inner), jnp.float32)
    first = state is None
    return pl.pallas_call(
        functools.partial(attend_kernel, slots, first),
        out_shape=[shape] * 3,
        in_specs=[pl.BlockSpec(memory_space=pltpu.SMEM)]
        + [pl.BlockSpec(memory_space=pltpu.VMEM)] * (1 + 2 * slots + (0 if first else 3)),
        out_specs=[pl.BlockSpec(memory_space=pltpu.VMEM)] * 3,
        compiler_params=pltpu.CompilerParams(vmem_limit_bytes=VMEM_LIMIT),
        cost_estimate=pl.CostEstimate(
            flops=slots * 6 * rows * rows * inner, bytes_accessed=rows * inner * (2 + 4 * slots + 12), transcendentals=0
        ),
        name="attend",
    )(active, q, *kv, *([] if first else state))


def finish_kernel(moves, info, q, k, v, part, total, peak, hidden, control, *refs):
    pieces = len({m[0] for m in moves})
    weight = refs[:pieces]
    out, attention, held, hidden_v, control_v, sems, res_sems = refs[pieces:]
    copies = []
    for number, (piece, index, group, start, share) in enumerate(moves):
        count = weight[piece].shape[-2]
        if share:
            side = info[1] if share > 0 else 1 - info[1]
            start = pl.multiple_of(start + side * count, count)
        copies.append(
            pltpu.make_async_copy(
                weight[piece].at[index], held.at[group, pl.ds(start, count), :], sems.at[number]
            )
        )
    residual = [
        pltpu.make_async_copy(hidden, hidden_v, res_sems.at[0]),
        pltpu.make_async_copy(control, control_v, res_sems.at[1]),
    ]
    for copy in copies + residual:
        copy.start()
    heads = q.shape[1] // HEAD_DIM

    def normal(state, at):
        attention[:, at] = (state[0] / state[1]).astype(jnp.bfloat16)

    @pl.when(info[0] == 1)
    def _():
        for h in range(heads):
            at = pl.ds(h * HEAD_DIM, HEAD_DIM)
            new = head_part(q[:, at], k[:, at], v[:, at])
            normal(merge((part[:, at], total[:, at], peak[:, at]), new), at)

    @pl.when(info[0] != 1)
    def _():
        for h in range(heads):
            at = pl.ds(h * HEAD_DIM, HEAD_DIM)
            normal((part[:, at], total[:, at]), at)

    for copy in copies + residual:
        copy.wait()
    groups, _, columns = held.shape
    step = 512 if columns % 512 == 0 else columns
    for group in range(groups):
        for j in range(columns // step):
            at = pl.ds(group * columns + j * step, step)
            projected = jnp.dot(
                attention[...], held[group, :, pl.ds(j * step, step)], preferred_element_type=jnp.float32
            )
            out[:, at] = (
                hidden_v[:, at].astype(jnp.float32) + projected + control_v[:, at].astype(jnp.float32)
            ).astype(jnp.bfloat16)


def finish(info, q, kv, state, hidden, control, weight, moves):
    rows, inner = q.shape
    width = hidden.shape[1]
    groups = len({m[2] for m in moves})
    any_space = pl.BlockSpec(memory_space=pl.ANY)
    vmem = pl.BlockSpec(memory_space=pltpu.VMEM)
    return pl.pallas_call(
        functools.partial(finish_kernel, moves),
        out_shape=jax.ShapeDtypeStruct((rows, width), jnp.bfloat16),
        in_specs=[pl.BlockSpec(memory_space=pltpu.SMEM)] + [vmem] * 6 + [any_space] * (2 + len(weight)),
        out_specs=vmem,
        scratch_shapes=[
            pltpu.VMEM((rows, inner), jnp.bfloat16),
            pltpu.VMEM((groups, inner, width // groups), jnp.bfloat16),
            pltpu.VMEM((rows, width), jnp.bfloat16),
            pltpu.VMEM((rows, width), jnp.bfloat16),
            pltpu.SemaphoreType.DMA((len(moves),)),
            pltpu.SemaphoreType.DMA((2,)),
        ],
        compiler_params=pltpu.CompilerParams(vmem_limit_bytes=VMEM_LIMIT),
        cost_estimate=pl.CostEstimate(
            flops=2 * rows * inner * width, bytes_accessed=2 * inner * width + 6 * rows * width, transcendentals=0
        ),
        name="finish",
    )(info, q, *kv, *state, hidden, control, *weight)


def swapped(block, axis, distance):
    count = lax.axis_size(axis)
    route = []
    for low in range(count):
        high = low | 1 << distance
        if high != low and high < count:
            route += [(low, high), (high, low)]
    return lax.ppermute(block, axis, route)


def relay_control(control, across, grid_width):
    rows, width = control.shape
    slab_lines = rows // (grid_width * TILE_W)
    slab_blocks = control.reshape(slab_lines, grid_width, TILE_W, width).transpose(1, 0, 2, 3)
    slab_blocks = slab_blocks.reshape(grid_width, rows // grid_width, width)
    positions = jnp.arange(grid_width, dtype=jnp.int32)
    order = jnp.bitwise_xor(across, positions)
    buffer = jnp.take(slab_blocks, order, axis=0)
    for bit in range(grid_width.bit_length() - 1):
        low = 1 << bit
        shaped = buffer.reshape(grid_width // (2 * low), 2, low, rows // grid_width, width)
        incoming = swapped(shaped[:, 1], TILES, bit)
        buffer = jnp.stack([shaped[:, 0], incoming], axis=1).reshape(
            grid_width, rows // grid_width, width
        )
    arranged = jnp.take(buffer, order, axis=0)
    return arranged.reshape(rows, width)


def gather_weight(out_weight):
    groups = lax.axis_size("groups")
    outer, pair, cores = (lax.axis_size(a) for a in TILES)
    rows, width = out_weight.shape
    columns = width // groups
    share = lax.dynamic_slice(out_weight, (0, lax.axis_index("groups") * columns), (rows, columns))
    line = lax.all_gather(share, "outer")
    mine = lax.all_gather(line, ("groups", "pair")).reshape(groups, pair, outer, rows, columns)
    other = lax.ppermute(mine, "core", [(0, 1), (1, 0)])
    if rows % 16 == 0:
        moves = tuple(
            (piece, (g, p, o), g, (o * pair + p) * cores * rows, 1 - 2 * piece)
            for g in range(groups)
            for p in range(pair)
            for o in range(outer)
            for piece in range(2)
        )
        return (mine, other), moves
    first = lax.axis_index("core") == 0
    both = jnp.stack([jnp.where(first, mine, other), jnp.where(first, other, mine)], axis=3)
    whole = both.transpose(0, 2, 1, 3, 4, 5).reshape(groups, outer * pair * cores * rows, columns)
    return (whole,), tuple((0, (g,), g, 0, 0) for g in range(groups))


def neighbour_slots(tile_count, strides, counts):
    slots = []
    for axis, (stride, count) in enumerate(zip(strides, counts)):
        for odd in range(2):
            route = []
            for t in range(tile_count):
                place = t // stride % count
                if place % 2 == odd and place + 1 < count:
                    route += [(t, t + stride), (t + stride, t)]
            if route:
                slots.append((axis, odd, route))
    return slots


def on_device(hidden, queries, keys, values, control, out_weight, pattern):
    sizes = [lax.axis_size(a) for a in TILES]
    tile_count = math.prod(sizes)
    grid_width = min(8, tile_count // 4)
    grid_height = min(4, tile_count // 8)
    layer = grid_width * grid_height
    strides = (layer, grid_width, 1)
    counts = (tile_count // layer, grid_height, grid_width)
    position = lax.axis_index(TILES)
    weight, moves = gather_weight(out_weight)
    slots = neighbour_slots(tile_count, strides, counts)
    slots = [s for s in slots if s[0] == 2] + [s for s in slots if s[0] == 0] + [s for s in slots if s[0] == 1]
    active, near = [], []
    for axis, odd, route in slots:
        place = position // strides[axis] % counts[axis]
        up = (place % 2 == odd).astype(jnp.int32)
        valid = jnp.where(up == 1, place + 1 < counts[axis], place >= 1)
        active.append((valid & (pattern[0, 2 * axis + up] == 1)).astype(jnp.int32))
        near.append(tuple(lax.ppermute(x, TILES, route) for x in (keys, values)))
    control_tiles = relay_control(control, position % grid_width, grid_width)
    early = len([s for s in slots if s[0] == 2])
    flags = jnp.stack([jnp.ones((), jnp.int32)] + active[:early])
    state = attend(flags, queries, [keys, values] + [x for kv in near[:early] for x in kv], None)
    for number in range(early, len(slots) - 1):
        state = attend(active[number][None], queries, list(near[number]), state)
    info = jnp.stack([active[-1], lax.axis_index("core").astype(jnp.int32)])
    return finish(info, queries, near[-1], state, hidden, control_tiles, weight, moves)


def solution(mesh):
    groups = mesh.shape["groups"]
    tiles = mesh.shape["tiles"]
    split = Mesh(mesh.devices.reshape(groups, tiles // 4, 2, 2), ("groups",) + TILES)
    rows = P(("groups",) + TILES, None)
    placed = (rows, rows, rows, rows, rows, P(TILES, None), rows)
    return jax.shard_map(
        on_device,
        mesh=split,
        in_specs=placed,
        out_specs=rows,
        check_vma=False,
    )
```

time: 187 us -> 192 us (1.027)
  the two profiles are of different devices: /device:TPU:20 before, /device:TPU:1 now
where the time goes in v1:
time: 192 us; the launch traced here: 191 us
  waiting for transfers between devices  134 us (70%)
  between operations  16.1 us (8%)
  Pallas kernels  14.5 us (8%)
  starting transfers between devices  12.7 us (7%)
  local copies, waits for them, and re-layouts  9.65 us (5%)
  other arithmetic  4.68 us (2%)
    all_gather x1, waiting for transfers between devices, gather_weight(): lax.all_gather(line, ('groups', 'pair'))  57.8 us
    ppermute x8, waiting for transfers between devices, on_device(): near.append(tuple((lax.ppermute(x, TILES, route) for x in (keys, values))))  40.5 us
    all_gather x1, waiting for transfers between devices, gather_weight(): line = lax.all_gather(share, 'outer')  32.5 us
    ppermute x8, starting transfers between devices, on_device(): near.append(tuple((lax.ppermute(x, TILES, route) for x in (keys, values))))  11.9 us
    pallas_call x1, Pallas kernels, finish(): pl.pallas_call(functools.partial(finish_kernel, moves), out_shape=jax.Sha...  7.64 us
    pallas_call x2, Pallas kernels, attend(): pl.pallas_call(functools.partial(attend_kernel, slots, first), out_shape=...  6.84 us
    unnamed x20, local copies, waits for them, and re-layouts  4.61 us
  transfers between devices with their start and end apart: 13, of which 9 were waited for; matrix products, arithmetic and copies ran while one was open for 5% of the time, Pallas kernels for 4%

profile of v1, /device:TPU:1, one launch (start us, length us, event | category | flops | bytes accessed | tf_op | source)
XLA Modules:
  0.0 191.5 jit_solution(966005475594224632)
XLA Ops:
  6.5 1.1 copy-done
  7.6 0.7 constant_dynamic-slice_fusion
  8.3 0.0 all-gather.5.cloned.1.call-update
  8.4 0.0 all-gather.7.cloned.1.call-start
  8.4 32.5 %all-gather.5.cloned.1.call-done = bf16[384,1536]{1,0:T(8,128)(2,1)} async-done(((bf16[96,1536]{1,0:T(8,128)(2,1)}), bf16[384,1536]{1,0:T(8,128)(2,1)}) %all-gather.5.cloned.1.call-update) | async-done | bytes 1179664 | tf_op jit(solution)/shard_map/all_gather | solution.py:198
  40.9 0.0 all-gather.7.cloned.1.call-update
  41.0 0.1 copy.21
  41.1 0.6 gather_fusion
  41.7 57.8 %all-gather.7.cloned.1.call-done = bf16[16,96,1536]{2,1,0:T(8,128)(2,1)} async-done(((bf16[4,96,1536]{2,1,0:T(8,128)(2,1)}), bf16[16,96,1536]{2,1,0:T(8,128)(2,1)}) %all-gather.7.cloned.1.call-update) | async-done | bytes 4718608 | tf_op jit(solution)/shard_map/all_gather | solution.py:199
  99.5 0.7 collective-permute-start.10
  100.2 0.2 broadcast_select_fusion
  100.4 0.1 slice_bitcast_fusion.3
  100.5 0.1 collective-permute-start.8
  100.6 0.5 collective-permute-start.4
  101.1 3.1 %collective-permute-start.6 = (bf16[192,1536]{1,0:T(8,128)(2,1)}, bf16[192,1536]{1,0:T(8,128)(2,1)S(1)}, u32[]{:S(2)}, u32[]{:S(2)}) collective-permute-start(bf16[192,1536]{1,0:T(8,128)(2,1)} %refs_0_.1), channel_id=1, source_target_pairs={{1,2},{2,1},{5,6},{6,5},{9,10},{10,9},{13,14},{14,13},{17,18},{18,... | collective-permute-start | bytes 1769480 | tf_op jit(solution)/shard_map/ppermute | solution.py:248
  104.1 2.2 %collective-permute-start.2 = (bf16[192,1536]{1,0:T(8,128)(2,1)}, bf16[192,1536]{1,0:T(8,128)(2,1)}, u32[]{:S(2)}, u32[]{:S(2)}) collective-permute-start(bf16[192,1536]{1,0:T(8,128)(2,1)} %refs_0_.1), channel_id=1, source_target_pairs={{0,8},{8,0},{1,9},{9,1},{2,10},{10,2},{3,11},{11,3},{4,12},{12,4},... | collective-permute-start | bytes 1769480 | tf_op jit(solution)/shard_map/ppermute | solution.py:248
  106.3 3.0 %collective-permute-done.8 = bf16[2,1,48,3072]{3,2,0,1:T(8,128)(2,1)S(1)} collective-permute-done((bf16[2,1,48,3072]{3,2,0,1:T(8,128)(2,1)S(1)}, bf16[2,1,48,3072]{3,2,0,1:T(8,128)(2,1)S(1)}, u32[]{:S(2)}, u32[]{:S(2)}) %collective-permute-start.8) | collective-permute-done | bytes 589856 | tf_op jit(solution)/shard_map/ppermute | solution.py:170
  109.3 0.1 collective-permute-start.5
  109.4 0.1 maximum_bitcast_fusion
  109.6 0.0 copy-start.8
  109.6 0.0 copy-start.1
  109.6 0.0 collective-permute-done.4.refs_2_
  109.6 2.2 %collective-permute-start.3 = (bf16[192,1536]{1,0:T(8,128)(2,1)}, bf16[192,1536]{1,0:T(8,128)(2,1)}, u32[]{:S(2)}, u32[]{:S(2)}) collective-permute-start(bf16[192,1536]{1,0:T(8,128)(2,1)} %refs_1_.1), channel_id=1, source_target_pairs={{0,8},{8,0},{1,9},{9,1},{2,10},{10,2},{3,11},{11,3},{4,12},{12,4},... | collective-permute-start | bytes 1769480 | tf_op jit(solution)/shard_map/ppermute | solution.py:248
  111.8 1.1 collective-permute-done.6.refs_4_
  112.9 2.7 %collective-permute-start.7 = (bf16[192,1536]{1,0:T(8,128)(2,1)}, bf16[192,1536]{1,0:T(8,128)(2,1)S(1)}, u32[]{:S(2)}, u32[]{:S(2)}) collective-permute-start(bf16[192,1536]{1,0:T(8,128)(2,1)} %refs_1_.1), channel_id=1, source_target_pairs={{1,2},{2,1},{5,6},{6,5},{9,10},{10,9},{13,14},{14,13},{17,18},{18,... | collective-permute-start | bytes 1769480 | tf_op jit(solution)/shard_map/ppermute | solution.py:248
  115.5 1.1 slice_bitcast_fusion.1
  116.6 0.0 collective-permute-done.5.refs_3_
  116.6 0.0 collective-permute-start.9
  116.6 0.7 constant_dynamic-slice_fusion.2
  119.9 0.1 pad_add_fusion.info
  119.9 0.1 add_convert_fusion.active
  120.0 9.6 %collective-permute-done.7.refs_5_ = bf16[192,1536]{1,0:T(8,128)(2,1)S(1)} collective-permute-done((bf16[192,1536]{1,0:T(8,128)(2,1)}, bf16[192,1536]{1,0:T(8,128)(2,1)S(1)}, u32[]{:S(2)}, u32[]{:S(2)}) %collective-permute-start.7) | collective-permute-done | bytes 589856 | tf_op jit(solution)/shard_map/ppermute | solution.py:248
  129.6 1.2 collective-permute-start
  130.8 3.9 %attend.2 = (f32[192,1536]{1,0:T(8,128)S(1)}, f32[192,1536]{1,0:T(8,128)S(1)}, f32[192,1536]{1,0:T(8,128)S(1)}) custom-call(s32[3]{0:T(128)S(1)} %add_convert_fusion.active, bf16[192,1536]{1,0:T(8,128)(2,1)S(1)} %copy-done.1, bf16[192,1536]{1,0:T(8,128)(2,1)} %refs_0_.1, bf16[192,1536]{1,0:T(8,128)(2,1)} %refs_1_.1, ...), custom_call_target="tpu_custom_call" | custom-call | flops 1019215872 | bytes 7667712 | tf_op jit(solution)/shard_map/attend/pallas_call | solution.py:68
  134.7 10.6 %collective-permute-done.2.refs_0_ = bf16[192,1536]{1,0:T(8,128)(2,1)} collective-permute-done((bf16[192,1536]{1,0:T(8,128)(2,1)}, bf16[192,1536]{1,0:T(8,128)(2,1)}, u32[]{:S(2)}, u32[]{:S(2)}) %collective-permute-start.2) | collective-permute-done | bytes 589856 | tf_op jit(solution)/shard_map/ppermute | solution.py:248
  145.3 0.0 collective-permute-start.1
  145.3 11.3 %collective-permute-done.3.refs_1_ = bf16[192,1536]{1,0:T(8,128)(2,1)} collective-permute-done((bf16[192,1536]{1,0:T(8,128)(2,1)}, bf16[192,1536]{1,0:T(8,128)(2,1)}, u32[]{:S(2)}, u32[]{:S(2)}) %collective-permute-start.3) | collective-permute-done | bytes 589856 | tf_op jit(solution)/shard_map/ppermute | solution.py:248
  156.7 3.0 %attend.3 = (f32[192,1536]{1,0:T(8,128)S(1)}, f32[192,1536]{1,0:T(8,128)S(1)}, f32[192,1536]{1,0:T(8,128)S(1)}) custom-call(s32[1]{0:T(128)} %bitcast.4.active, bf16[192,1536]{1,0:T(8,128)(2,1)S(1)} %copy-done.1, bf16[192,1536]{1,0:T(8,128)(2,1)} %collective-permute-done.2.refs_0_, bf16[192,1536]{1,0:T(8,128)(2,1)} %collective-permute-done.3.refs_1_, ...), custom_call_target="tpu_custom_call" | custom-call | flops 339738624 | bytes 5308416 | tf_op jit(solution)/shard_map/attend/pallas_call | solution.py:68
  159.6 0.0 copy-start.4
  159.6 0.0 collective-permute-done.9
  159.7 2.6 %pad_maximum_fusion = bf16[1,2,2,48,3072]{4,3,2,1,0:T(8,128)(2,1)} fusion(bf16[1,1,2,48,3072]{4,3,2,1,0:T(8,128)(2,1)} %bitcast.17, bf16[1,1,2,48,3072]{4,3,2,1,0:T(8,128)(2,1)S(1)} %copy-done.6), kind=kLoop, calls=%fused_computation.3 | loop fusion | flops 589824 | bytes 2359296 | tf_op jit(solution)/shard_map/stack | solution.py:185
  162.3 2.9 %gather_fusion.1 = bf16[4,48,3072]{2,1,0:T(8,128)(2,1)} fusion(bf16[4,48,3072]{2,1,0:T(8,128)(2,1)} %bitcast.37, s32[1024]{0:T(1024)S(1)} %pad_clamp_fusion), kind=kCustom, calls=%fused_computation.1.clone | custom fusion | bytes 2359312 | tf_op jit(solution)/shard_map/jit(_take)/gather | solution.py:188
  165.2 1.6 broadcast_select_fusion.1
  166.8 0.8 collective-permute-done.k
  167.6 7.1 %collective-permute-done.1.v = bf16[192,1536]{1,0:T(8,128)(2,1)} collective-permute-done((bf16[192,1536]{1,0:T(8,128)(2,1)}, bf16[192,1536]{1,0:T(8,128)(2,1)}, u32[]{:S(2)}, u32[]{:S(2)}) %collective-permute-start.1) | collective-permute-done | bytes 589856 | tf_op jit(solution)/shard_map/ppermute | solution.py:248
  174.6 0.0 collective-permute-done.10.refs_1_
  174.7 2.3 %copy-done.2 = bf16[16,96,1536]{2,1,0:T(8,128)(2,1)S(1)} copy-done((bf16[16,96,1536]{2,1,0:T(8,128)(2,1)S(1)}, bf16[16,96,1536]{2,1,0:T(8,128)(2,1)}, u32[]{:S(2)}) %copy-start.2) | copy-done | bytes 4718616
  177.0 7.6 %finish.1 = bf16[192,3072]{1,0:T(8,128)(2,1)} custom-call(s32[2]{0:T(128)S(1)} %pad_add_fusion.info, bf16[192,1536]{1,0:T(8,128)(2,1)S(1)} %copy-done.1, bf16[192,1536]{1,0:T(8,128)(2,1)} %collective-permute-done.k, bf16[192,1536]{1,0:T(8,128)(2,1)} %collective-permute-done.1.v, f32[192,1536]{1,0:T(8,128)S(1)} %get-tuple-element.15.part, ...), custom_call_target="tpu_custom_call" | custom-call | flops 1811939328 | bytes 12976128 | tf_op jit(solution)/shard_map/finish/pallas_call | solution.py:142
  (17 shorter events, 0.0 us)
Async XLA Ops:
  6.5 1.1 copy-start
  6.5 34.4 %copy-start.7 = (bf16[192,3072]{1,0:T(8,128)(2,1)S(1)}, bf16[192,3072]{1,0:T(8,128)(2,1)}, u32[]{:S(2)}) copy-start(bf16[192,3072]{1,0:T(8,128)(2,1)} %param.13) | copy-start | bytes 3538948
  6.5 34.4 %all-gather.5.cloned.1.call-start = ((), (), s32[]{:S(2)}) async-start(), calls=%async_computation | async-start | bytes 1474560 | tf_op jit(solution)/shard_map/all_gather | solution.py:198
  8.4 91.2 %all-gather.7.cloned.1.call-start = ((), (), s32[]{:S(2)}) async-start(), calls=%async_computation.1 | async-start | bytes 5898240 | tf_op jit(solution)/shard_map/all_gather | solution.py:199
  99.5 75.1 %collective-permute-start.10 = (bf16[2,2,4,96,1536]{4,3,2,1,0:T(8,128)(2,1)}, bf16[2,2,4,96,1536]{4,3,2,1,0:T(8,128)(2,1)}, u32[]{:S(2)}, u32[]{:S(2)}) collective-permute-start(bf16[2,2,4,96,1536]{4,3,2,1,0:T(8,128)(2,1)} %bitcast.32), channel_id=1, source_target_pairs={{0,1},{1,0},{2,3},{3,2},{4,5},{5,4},{6,7},{7,6},{8,9},{9,8},{10,11... | collective-permute-start | bytes 14155784 | tf_op jit(solution)/shard_map/ppermute | solution.py:200
  100.5 8.8 %collective-permute-start.8 = (bf16[2,1,48,3072]{3,2,0,1:T(8,128)(2,1)S(1)}, bf16[2,1,48,3072]{3,2,0,1:T(8,128)(2,1)S(1)}, u32[]{:S(2)}, u32[]{:S(2)}) collective-permute-start(bf16[2,1,48,3072]{3,2,0,1:T(8,128)(2,1)S(1)} %get-tuple-element.21), channel_id=1, source_target_pairs={{0,1},{1,0},{2,3},{3,2},{4,5},{5,4},{6,7},{7,6},{8,9},{9,8},{10,11... | collective-permute-start | bytes 1769480 | tf_op jit(solution)/shard_map/ppermute | solution.py:170
  100.6 9.0 %collective-permute-start.4 = (bf16[192,1536]{1,0:T(8,128)(2,1)}, bf16[192,1536]{1,0:T(8,128)(2,1)S(1)}, u32[]{:S(2)}, u32[]{:S(2)}) collective-permute-start(bf16[192,1536]{1,0:T(8,128)(2,1)} %refs_0_.1), channel_id=1, source_target_pairs={{0,1},{1,0},{2,3},{3,2},{4,5},{5,4},{6,7},{7,6},{8,9},{9,8},{10,11... | collective-permute-start | bytes 1769480 | tf_op jit(solution)/shard_map/ppermute | solution.py:248
  101.1 11.8 %collective-permute-start.6 = (bf16[192,1536]{1,0:T(8,128)(2,1)}, bf16[192,1536]{1,0:T(8,128)(2,1)S(1)}, u32[]{:S(2)}, u32[]{:S(2)}) collective-permute-start(bf16[192,1536]{1,0:T(8,128)(2,1)} %refs_0_.1), channel_id=1, source_target_pairs={{1,2},{2,1},{5,6},{6,5},{9,10},{10,9},{13,14},{14,13},{17,18},{18,... | collective-permute-start | bytes 1769480 | tf_op jit(solution)/shard_map/ppermute | solution.py:248
  104.1 41.2 %collective-permute-start.2 = (bf16[192,1536]{1,0:T(8,128)(2,1)}, bf16[192,1536]{1,0:T(8,128)(2,1)}, u32[]{:S(2)}, u32[]{:S(2)}) collective-permute-start(bf16[192,1536]{1,0:T(8,128)(2,1)} %refs_0_.1), channel_id=1, source_target_pairs={{0,8},{8,0},{1,9},{9,1},{2,10},{10,2},{3,11},{11,3},{4,12},{12,4},... | collective-permute-start | bytes 1769480 | tf_op jit(solution)/shard_map/ppermute | solution.py:248
  109.3 7.3 %collective-permute-start.5 = (bf16[192,1536]{1,0:T(8,128)(2,1)}, bf16[192,1536]{1,0:T(8,128)(2,1)S(1)}, u32[]{:S(2)}, u32[]{:S(2)}) collective-permute-start(bf16[192,1536]{1,0:T(8,128)(2,1)} %refs_1_.1), channel_id=1, source_target_pairs={{0,1},{1,0},{2,3},{3,2},{4,5},{5,4},{6,7},{7,6},{8,9},{9,8},{10,11... | collective-permute-start | bytes 1769480 | tf_op jit(solution)/shard_map/ppermute | solution.py:248
  109.6 7.1 %copy-start.8 = (s32[1,6]{1,0:T(1,128)S(1)}, s32[1,6]{1,0:T(1,128)}, u32[]{:S(2)}) copy-start(s32[1,6]{1,0:T(1,128)} %param.15) | copy-start | bytes 76
  109.6 21.3 %copy-start.1 = (bf16[192,1536]{1,0:T(8,128)(2,1)S(1)}, bf16[192,1536]{1,0:T(8,128)(2,1)}, u32[]{:S(2)}) copy-start(bf16[192,1536]{1,0:T(8,128)(2,1)} %q.5) | copy-start | bytes 1769476
  109.6 47.1 %collective-permute-start.3 = (bf16[192,1536]{1,0:T(8,128)(2,1)}, bf16[192,1536]{1,0:T(8,128)(2,1)}, u32[]{:S(2)}, u32[]{:S(2)}) collective-permute-start(bf16[192,1536]{1,0:T(8,128)(2,1)} %refs_1_.1), channel_id=1, source_target_pairs={{0,8},{8,0},{1,9},{9,1},{2,10},{10,2},{3,11},{11,3},{4,12},{12,4},... | collective-permute-start | bytes 1769480 | tf_op jit(solution)/shard_map/ppermute | solution.py:248
  112.9 16.8 %collective-permute-start.7 = (bf16[192,1536]{1,0:T(8,128)(2,1)}, bf16[192,1536]{1,0:T(8,128)(2,1)S(1)}, u32[]{:S(2)}, u32[]{:S(2)}) collective-permute-start(bf16[192,1536]{1,0:T(8,128)(2,1)} %refs_1_.1), channel_id=1, source_target_pairs={{1,2},{2,1},{5,6},{6,5},{9,10},{10,9},{13,14},{14,13},{17,18},{18,... | collective-permute-start | bytes 1769480 | tf_op jit(solution)/shard_map/ppermute | solution.py:248
  116.6 43.0 %collective-permute-start.9 = (bf16[1,2,48,3072]{3,2,1,0:T(8,128)(2,1)}, bf16[1,2,48,3072]{3,2,1,0:T(8,128)(2,1)}, u32[]{:S(2)}, u32[]{:S(2)}) collective-permute-start(bf16[1,2,48,3072]{3,2,1,0:T(8,128)(2,1)} %get-tuple-element.19), channel_id=1, source_target_pairs={{0,2},{2,0},{1,3},{3,1},{4,6},{6,4},{5,7},{7,5},{8,10},{10,8},{9,1... | collective-permute-start | bytes 1769480 | tf_op jit(solution)/shard_map/ppermute | solution.py:170
  129.6 38.0 %collective-permute-start = (bf16[192,1536]{1,0:T(8,128)(2,1)}, bf16[192,1536]{1,0:T(8,128)(2,1)}, u32[]{:S(2)}, u32[]{:S(2)}) collective-permute-start(bf16[192,1536]{1,0:T(8,128)(2,1)} %refs_0_.1), channel_id=1, source_target_pairs={{0,4},{4,0},{1,5},{5,1},{2,6},{6,2},{3,7},{7,3},{8,12},{12,8},{9,1... | collective-permute-start | bytes 1769480 | tf_op jit(solution)/shard_map/ppermute | solution.py:248
  145.3 29.3 %collective-permute-start.1 = (bf16[192,1536]{1,0:T(8,128)(2,1)}, bf16[192,1536]{1,0:T(8,128)(2,1)}, u32[]{:S(2)}, u32[]{:S(2)}) collective-permute-start(bf16[192,1536]{1,0:T(8,128)(2,1)} %refs_1_.1), channel_id=1, source_target_pairs={{0,4},{4,0},{1,5},{5,1},{2,6},{6,2},{3,7},{7,3},{8,12},{12,8},{9,1... | collective-permute-start | bytes 1769480 | tf_op jit(solution)/shard_map/ppermute | solution.py:248
  156.7 3.0 %copy-start.6 = (bf16[1,1,2,48,3072]{4,3,2,1,0:T(8,128)(2,1)S(1)}, bf16[1,1,2,48,3072]{4,3,2,1,0:T(8,128)(2,1)}, u32[]{:S(2)}) copy-start(bf16[1,1,2,48,3072]{4,3,2,1,0:T(8,128)(2,1)} %get-tuple-element.18) | copy-start | bytes 1769476
  159.6 2.7 %copy-start.4 = (f32[192,1536]{1,0:T(8,128)}, f32[192,1536]{1,0:T(8,128)S(1)}, u32[]{:S(2)}) copy-start(f32[192,1536]{1,0:T(8,128)S(1)} %get-tuple-element.17.peak) | copy-start | bytes 3538948
  165.2 9.5 %copy-start.3 = (bf16[192,3072]{1,0:T(8,128)(2,1)S(1)}, bf16[192,3072]{1,0:T(8,128)(2,1)}, u32[]{:S(2)}) copy-start(bf16[192,3072]{1,0:T(8,128)(2,1)} %hidden.1) | copy-start | bytes 3538948
  165.2 9.5 %copy-start.5 = (f32[192,1536]{1,0:T(8,128)S(1)}, f32[192,1536]{1,0:T(8,128)}, u32[]{:S(2)}) copy-start(f32[192,1536]{1,0:T(8,128)} %copy-done.4) | copy-start | bytes 3538948
  174.7 2.3 %copy-start.2 = (bf16[16,96,1536]{2,1,0:T(8,128)(2,1)S(1)}, bf16[16,96,1536]{2,1,0:T(8,128)(2,1)}, u32[]{:S(2)}) copy-start(bf16[16,96,1536]{2,1,0:T(8,128)(2,1)} %all-gather.7.cloned.1.call-done) | copy-start | bytes 14155780
Sparse Core Ops, SparseCore 0:
  8.9 31.9 all-gather.4
  42.8 56.7 all-gather.6

commit v2 on v1

v2 whole, which is shorter than its diff:
```python
import functools
import math

import jax
import jax.numpy as jnp
from jax import lax
from jax.experimental import pallas as pl
from jax.experimental.pallas import tpu as pltpu
from jax.sharding import Mesh
from jax.sharding import PartitionSpec as P

HEAD_DIM = 128
TILE_W = 8
HALVES = 2
SCALE = HEAD_DIM**-0.5 * math.log2(math.e)
TILES = ("outer", "pair", "core")
VMEM_LIMIT = 40 * 1024 * 1024
VMEM = pl.BlockSpec(memory_space=pltpu.VMEM)
SMEM = pl.BlockSpec(memory_space=pltpu.SMEM)
ANY = pl.BlockSpec(memory_space=pl.ANY)


def after(x, *others):
    return lax.optimization_barrier((x, *others))[0]


def head_part(q, k, v):
    scores = lax.dot_general(q, k, (((1,), (1,)), ((), ())), preferred_element_type=jnp.float32)
    peak = jnp.max(scores, axis=1, keepdims=True)
    weights = jnp.exp2((scores - peak) * SCALE).astype(jnp.bfloat16)
    ones = jnp.ones((v.shape[0], HEAD_DIM), jnp.bfloat16)
    both = jnp.dot(weights, jnp.concatenate([v, ones], axis=1), preferred_element_type=jnp.float32)
    return both[:, :HEAD_DIM], both[:, HEAD_DIM:], jnp.broadcast_to(peak, v.shape)


def merge(old, new):
    part, total, peak = old
    part_new, total_new, peak_new = new
    top = jnp.maximum(peak, peak_new)
    f_old = jnp.exp2((peak - top) * SCALE)
    f_new = jnp.exp2((peak_new - top) * SCALE)
    return f_old * part + f_new * part_new, f_old * total + f_new * total_new, top


def fold(state, active, slot, q, first_head, kv):
    columns = kv.shape[1] // 2

    @pl.when(active[slot] == 1)
    def _():
        for h in range(columns // HEAD_DIM):
            at = pl.ds(h * HEAD_DIM, HEAD_DIM)
            new = head_part(
                q[:, pl.ds((first_head + h) * HEAD_DIM, HEAD_DIM)],
                kv[:, at],
                kv[:, pl.ds(columns + h * HEAD_DIM, HEAD_DIM)],
            )
            for r, x in zip(state, merge(tuple(r[:, at] for r in state), new)):
                r[:, at] = x


def attend_kernel(slots, first_head, active, q, own, *refs):
    near, state = refs[:slots], refs[slots:]
    columns = own.shape[1] // 2
    for h in range(columns // HEAD_DIM):
        at = pl.ds(h * HEAD_DIM, HEAD_DIM)
        new = head_part(
            q[:, pl.ds((first_head + h) * HEAD_DIM, HEAD_DIM)],
            own[:, at],
            own[:, pl.ds(columns + h * HEAD_DIM, HEAD_DIM)],
        )
        for r, x in zip(state, new):
            r[:, at] = x
    for slot in range(slots):
        fold(state, active, slot, q, first_head, near[slot])


def attend(active, q, first_head, own, near):
    rows, columns = own.shape[0], own.shape[1] // 2
    shape = jax.ShapeDtypeStruct((rows, columns), jnp.float32)
    return pl.pallas_call(
        functools.partial(attend_kernel, len(near), first_head),
        out_shape=[shape] * 3,
        in_specs=[SMEM] + [VMEM] * (2 + len(near)),
        out_specs=[VMEM] * 3,
        compiler_params=pltpu.CompilerParams(vmem_limit_bytes=VMEM_LIMIT),
        cost_estimate=pl.CostEstimate(
            flops=(1 + len(near)) * 6 * rows * rows * columns,
            bytes_accessed=rows * columns * (4 + 4 * len(near) + 12),
            transcendentals=0,
        ),
        name="attend",
    )(active, q, own, *near)


def close_kernel(slots, first_head, active, q, part, total, peak, *refs):
    near, out, state = refs[:slots], refs[slots], refs[slots + 1 :]
    for r, x in zip(state, (part, total, peak)):
        r[...] = x[...]
    for slot in range(slots):
        fold(state, active, slot, q, first_head, near[slot])
    out[...] = (state[0][...] / state[1][...]).astype(jnp.bfloat16)


def close(active, q, first_head, state, near):
    rows, columns = state[0].shape
    return pl.pallas_call(
        functools.partial(close_kernel, len(near), first_head),
        out_shape=jax.ShapeDtypeStruct((rows, columns), jnp.bfloat16),
        in_specs=[SMEM] + [VMEM] * (4 + len(near)),
        out_specs=VMEM,
        scratch_shapes=[pltpu.VMEM((rows, columns), jnp.float32)] * 3,
        compiler_params=pltpu.CompilerParams(vmem_limit_bytes=VMEM_LIMIT),
        cost_estimate=pl.CostEstimate(
            flops=len(near) * 6 * rows * rows * columns,
            bytes_accessed=rows * columns * (4 * len(near) + 16),
            transcendentals=0,
        ),
        name="close",
    )(active, q, *state, *near)


def finish_kernel(slots, blocks, moves, control_rows, place, active, q, ready, part, total, peak, *refs):
    near, refs = refs[:slots], refs[slots:]
    hidden, refs = refs[0], refs[1:]
    control, refs = refs[:blocks], refs[blocks:]
    pieces = len({m[0] for m in moves})
    weight, refs = refs[:pieces], refs[pieces:]
    out, attention, held, hidden_v, control_v, *state, sems, res_sems = refs
    copies = []
    for number, (piece, index, flips) in enumerate(moves):
        source = weight[piece].at[index] if index else weight[piece]
        if flips is None:
            target = held
        else:
            count = source.shape[0]
            (group, pair), outer_flip, core_flip = flips
            outer, core = place[1] ^ outer_flip, place[3] ^ core_flip
            start = pl.multiple_of(((outer * 2 + pair) * 2 + core) * count, count)
            target = held.at[group, pl.ds(start, count), :]
        copies.append(pltpu.make_async_copy(source, target, sems.at[number]))
    copies.append(pltpu.make_async_copy(hidden, hidden_v, res_sems.at[blocks]))
    for d in range(blocks):
        start = pl.multiple_of((place[4] ^ d) * control_rows, control_rows) if blocks > 1 else 0
        copies.append(
            pltpu.make_async_copy(control[d], control_v.at[pl.ds(start, control_rows), :], res_sems.at[d])
        )
    for copy in copies:
        copy.start()
    rows, done = ready.shape
    for r, x in zip(state, (part, total, peak)):
        r[...] = x[...]
    for slot in range(slots):
        fold(state, active, slot, q, done // HEAD_DIM, near[slot])
    attention[:, pl.ds(0, done)] = ready[...]
    attention[:, pl.ds(done, part.shape[1])] = (state[0][...] / state[1][...]).astype(jnp.bfloat16)
    for copy in copies:
        copy.wait()
    groups, _, columns = held.shape
    step = 512 if columns % 512 == 0 else columns
    for group in range(groups):
        for j in range(columns // step):
            at = pl.ds(group * columns + j * step, step)
            projected = jnp.dot(
                attention[...], held[group, :, pl.ds(j * step, step)], preferred_element_type=jnp.float32
            )
            out[:, at] = (
                hidden_v[:, at].astype(jnp.float32) + projected + control_v[:, at].astype(jnp.float32)
            ).astype(jnp.bfloat16)


def finish(place, active, q, ready, state, near, hidden, control, weight, moves):
    rows, inner = q.shape
    width = hidden.shape[1]
    groups = lax.axis_size("groups")
    control_rows = control[0].shape[0]
    columns = state[0].shape[1]
    return pl.pallas_call(
        functools.partial(finish_kernel, len(near), len(control), moves, control_rows),
        out_shape=jax.ShapeDtypeStruct((rows, width), jnp.bfloat16),
        in_specs=[SMEM] * 2 + [VMEM] * (5 + len(near)) + [ANY] * (1 + len(control) + len(weight)),
        out_specs=VMEM,
        scratch_shapes=[
            pltpu.VMEM((rows, inner), jnp.bfloat16),
            pltpu.VMEM((groups, inner, width // groups), jnp.bfloat16),
            pltpu.VMEM((rows, width), jnp.bfloat16),
            pltpu.VMEM((rows, width), jnp.bfloat16),
        ]
        + [pltpu.VMEM((rows, columns), jnp.float32)] * 3
        + [
            pltpu.SemaphoreType.DMA((len(moves),)),
            pltpu.SemaphoreType.DMA((len(control) + 1,)),
        ],
        compiler_params=pltpu.CompilerParams(vmem_limit_bytes=VMEM_LIMIT),
        cost_estimate=pl.CostEstimate(
            flops=2 * rows * inner * width, bytes_accessed=2 * inner * width + 6 * rows * width, transcendentals=0
        ),
        name="finish",
    )(place, active, q, ready, *state, *near, hidden, *control, *weight)


def flipped(block, axis, flip):
    return lax.ppermute(block, axis, [(i, i ^ flip) for i in range(lax.axis_size(axis))])


def control_blocks(control, across, grid_width, wait_for):
    rows, width = control.shape
    block = rows // grid_width
    lines = control.reshape(block // TILE_W, grid_width, TILE_W, width)
    blocks = []
    for d in range(grid_width):
        mine = lax.dynamic_index_in_dim(lines, across ^ d, 1, keepdims=False).reshape(block, width)
        blocks.append(flipped(after(mine, *wait_for) if d > 1 else mine, TILES, d) if d else mine)
    if block % 16 == 0:
        return blocks
    order = jnp.arange(grid_width, dtype=jnp.int32) ^ across
    return [jnp.take(jnp.stack(blocks), order, axis=0).reshape(rows, width)]


def gather_weight(out_weight):
    groups = lax.axis_size("groups")
    outer, pair, cores = (lax.axis_size(a) for a in TILES)
    rows, width = out_weight.shape
    columns = width // groups
    share = lax.dynamic_slice(out_weight, (0, lax.axis_index("groups") * columns), (rows, columns))
    line = share[None]
    flip = outer // 2
    while flip > 2:
        line = jnp.concatenate([line, flipped(line, "outer", flip)])
        flip //= 2
    far = flipped(line, "outer", 2)
    near = flipped(line, "outer", 1)
    last = flipped(far, "outer", 1)
    steps = [line, jnp.concatenate([far, near, last])]
    flips = [sum(((outer // 2) >> b) * (i >> b & 1) for b in range(outer.bit_length() - 1)) for i in range(outer // 4)]
    flips = [flips, [f ^ x for x in (2, 1, 3) for f in flips]]
    mine = [lax.all_gather(x, ("groups", "pair")) for x in steps]
    other = [flipped(x, "core", 1) for x in mine]
    if rows % 16 == 0:
        moves = tuple(
            (2 * step + core, (g * pair + p, i), ((g, p), f, core))
            for step in range(2)
            for core in range(2)
            for g in range(groups)
            for p in range(pair)
            for i, f in enumerate(flips[step])
        )
        return [x for pair_of in zip(mine, other) for x in pair_of], moves, far, last
    whole = [jnp.concatenate(x, axis=1) for x in (mine, other)]
    order = jnp.array([flips_all.index(f) for flips_all in [flips[0] + flips[1]] for f in range(outer)], jnp.int32)
    whole = [jnp.take(x, order[jnp.arange(outer) ^ lax.axis_index("outer")], axis=1) for x in whole]
    first = lax.axis_index("core") == 0
    both = jnp.stack([jnp.where(first, whole[0], whole[1]), jnp.where(first, whole[1], whole[0])], axis=2)
    both = both.reshape(groups, pair, outer, cores, rows, columns).transpose(0, 2, 1, 3, 4, 5)
    whole = both.reshape(groups, outer * pair * cores * rows, columns)
    return [whole], ((0, None, None),), far, last


def neighbour_slots(tile_count, strides, counts):
    slots = []
    for axis, (stride, count) in enumerate(zip(strides, counts)):
        for odd in range(2):
            route = []
            for t in range(tile_count):
                place = t // stride % count
                if place % 2 == odd and place + 1 < count:
                    route += [(t, t + stride), (t + stride, t)]
            if route:
                slots.append((axis, odd, route))
    return slots


def on_device(hidden, queries, keys, values, control, out_weight, pattern):
    sizes = [lax.axis_size(a) for a in TILES]
    tile_count = math.prod(sizes)
    grid_width = min(8, tile_count // 4)
    grid_height = min(4, tile_count // 8)
    layer = grid_width * grid_height
    strides = (layer, grid_width, 1)
    counts = (tile_count // layer, grid_height, grid_width)
    position = lax.axis_index(TILES)
    across = position % grid_width
    weight, moves, far, last = gather_weight(out_weight)
    columns = queries.shape[1] // HALVES
    kv = [
        jnp.concatenate([x[:, half * columns : (half + 1) * columns] for x in (keys, values)], axis=1)
        for half in range(HALVES)
    ]
    slots = neighbour_slots(tile_count, strides, counts)
    early = [s for s in slots if s[0] == 2]
    late = [s for s in slots if s[0] != 2]

    def flags(chosen):
        active = []
        for axis, odd, _ in chosen:
            place = position // strides[axis] % counts[axis]
            up = (place % 2 == odd).astype(jnp.int32)
            valid = jnp.where(up == 1, place + 1 < counts[axis], place >= 1)
            active.append((valid & (pattern[0, 2 * axis + up] == 1)).astype(jnp.int32))
        return jnp.stack(active)

    early_active, late_active = flags(early), flags(late)
    early_near, late_near = [], []
    for half in range(HALVES):
        early_near.append([])
        for axis, odd, route in early:
            block = kv[half] if odd == 0 else after(kv[half], far)
            early_near[half].append(lax.ppermute(block, TILES, route))
        waits = [far, last] if half == 0 else late_near[-1]
        late_near.append(
            [lax.ppermute(after(kv[half], waits[i % 2]), TILES, route) for i, (_, _, route) in enumerate(late)]
        )
    control_parts = control_blocks(control, across, grid_width, (far,))
    heads = columns // HEAD_DIM
    states = [attend(early_active, queries, half * heads, kv[half], early_near[half]) for half in range(HALVES)]
    ready = [close(late_active, queries, half * heads, states[half], late_near[half]) for half in range(HALVES - 1)]
    ready = ready[0] if len(ready) == 1 else jnp.concatenate(ready, axis=1)
    place = jnp.stack([lax.axis_index(a) for a in ("groups",) + TILES] + [across]).astype(jnp.int32)
    return finish(
        place, late_active, queries, ready, states[-1], late_near[-1], hidden, control_parts, weight, moves
    )


def solution(mesh):
    groups = mesh.shape["groups"]
    tiles = mesh.shape["tiles"]
    split = Mesh(mesh.devices.reshape(groups, tiles // 4, 2, 2), ("groups",) + TILES)
    rows = P(("groups",) + TILES, None)
    placed = (rows, rows, rows, rows, rows, P(TILES, None), rows)
    return jax.shard_map(
        on_device,
        mesh=split,
        in_specs=placed,
        out_specs=rows,
        check_vma=False,
    )
```

time: 192 us -> 167 us (0.87)
  waiting for transfers between devices: 134 us -> 102 us
  starting transfers between devices: 12.7 us -> 22 us
  other arithmetic: 4.68 us -> 1.24 us
  Pallas kernels: 14.5 us -> 16.6 us
  local copies, waits for them, and re-layouts: 9.65 us -> 7.56 us
    all_gather x2, waiting for transfers between devices: 90.3 us -> 54.6 us  [gather_weight(): mine = [lax.all_gather(x, ('groups', 'pair')) for x in steps]]
    ppermute x11 -> x16, starting transfers between devices: 12.7 us -> 22 us  [the longest x8 8 us: flipped(): lax.ppermute(block, axis, [(i, i ^ flip) for i in range(lax.axis_size(axi...]
    ppermute x11 -> x16, waiting for transfers between devices: 43.5 us -> 47.2 us  [the longest x8 27.6 us: flipped(): lax.ppermute(block, axis, [(i, i ^ flip) for i in range(lax.axis_size(axi...]
    gather x2 -> x0, local copies, waits for them, and re-layouts: 3.54 us -> none  [the longest x1 2.91 us: relay_control(): arranged = jnp.take(buffer, order, axis=0)]
    another operation x4 -> x2, other arithmetic: 2.88 us -> 0.15 us  [flags(): return jnp.stack(active)]
    pallas_call x3 -> x4, Pallas kernels: 14.5 us -> 16.6 us  [the longest x1 8.02 us: finish(): pl.pallas_call(functools.partial(finish_kernel, len(near), len(control),...]
    unnamed x20 -> x36, local copies, waits for them, and re-layouts: 4.61 us -> 5.03 us
  transfers between devices with their start and end apart: 13 -> 18, of which waited for: 9 -> 10; matrix products, arithmetic and copies ran while one was open for 5% -> 2% of each run, Pallas kernels for 4% -> 5%
where the time goes in v2:
time: 167 us; the launch traced here: 166 us
  waiting for transfers between devices  102 us (61%)
  starting transfers between devices  22 us (13%)
  Pallas kernels  16.6 us (10%)
  between operations  16.3 us (10%)
  local copies, waits for them, and re-layouts  7.56 us (5%)
    all_gather x2, waiting for transfers between devices, gather_weight(): mine = [lax.all_gather(x, ('groups', 'pair')) for x in steps]  54.6 us
    ppermute x8, waiting for transfers between devices, flipped(): lax.ppermute(block, axis, [(i, i ^ flip) for i in range(lax.axis_size(axi...  27.6 us
    ppermute x4, waiting for transfers between devices, on_device(): lax.ppermute(after(kv[half], waits[i % 2]), TILES, route)  14.4 us
    pallas_call x1, Pallas kernels, finish(): pl.pallas_call(functools.partial(finish_kernel, len(near), len(control),...  8.02 us
    ppermute x8, starting transfers between devices, flipped(): lax.ppermute(block, axis, [(i, i ^ flip) for i in range(lax.axis_size(axi...  8 us
    ppermute x4, starting transfers between devices, on_device(): early_near[half].append(lax.ppermute(block, TILES, route))  7.03 us
    ppermute x4, starting transfers between devices, on_device(): lax.ppermute(after(kv[half], waits[i % 2]), TILES, route)  6.94 us
    pallas_call x2, Pallas kernels, attend(): pl.pallas_call(functools.partial(attend_kernel, len(near), first_head), o...  6.26 us
  transfers between devices with their start and end apart: 18, of which 10 were waited for; matrix products, arithmetic and copies ran while one was open for 2% of the time, Pallas kernels for 5%

profile of v2, /device:TPU:1, one launch (start us, length us, event | category | flops | bytes accessed | tf_op | source)
XLA Modules:
  0.0 165.6 jit_solution(17045429077805457292)
XLA Ops:
  6.5 1.1 copy-done
  7.6 3.2 %collective-permute-start.1 = (bf16[1,96,1536]{2,1,0:T(8,128)(2,1)S(1)}, bf16[1,96,1536]{2,1,0:T(8,128)(2,1)S(1)}, u32[]{:S(2)}, u32[]{:S(2)}) collective-permute-start(bf16[1,96,1536]{2,1,0:T(8,128)(2,1)S(1)} %fusion.2), channel_id=1, source_target_pairs={{0,8},{4,12},{8,0},{12,4},{1,9},{5,13},{9,1},{13,5},{2,10},{6,14},... | collective-permute-start | bytes 884744 | tf_op jit(solution)/shard_map/ppermute | solution.py:202
  10.8 1.3 collective-permute-start.14
  12.1 11.8 %collective-permute-done.1 = bf16[1,96,1536]{2,1,0:T(8,128)(2,1)S(1)} collective-permute-done((bf16[1,96,1536]{2,1,0:T(8,128)(2,1)S(1)}, bf16[1,96,1536]{2,1,0:T(8,128)(2,1)S(1)}, u32[]{:S(2)}, u32[]{:S(2)}) %collective-permute-start.1) | collective-permute-done | bytes 294944 | tf_op jit(solution)/shard_map/ppermute | solution.py:202
  23.9 1.1 collective-permute-start.4
  25.1 6.1 %collective-permute-done.4 = bf16[1,96,1536]{2,1,0:T(8,128)(2,1)S(1)} collective-permute-done((bf16[1,96,1536]{2,1,0:T(8,128)(2,1)S(1)}, bf16[1,96,1536]{2,1,0:T(8,128)(2,1)S(1)}, u32[]{:S(2)}, u32[]{:S(2)}) %collective-permute-start.4) | collective-permute-done | bytes 294944 | tf_op jit(solution)/shard_map/ppermute | solution.py:202
  31.1 1.0 pad_maximum_fusion
  32.2 0.0 all-gather.7.cloned.1.call-update
  32.2 0.0 all-gather.5.cloned.1.call-start
  32.2 50.8 %all-gather.7.cloned.1.call-done = bf16[12,96,1536]{2,1,0:T(8,128)(2,1)} async-done(((bf16[3,96,1536]{2,1,0:T(8,128)(2,1)}), bf16[12,96,1536]{2,1,0:T(8,128)(2,1)}) %all-gather.7.cloned.1.call-update) | async-done | bytes 3538960 | tf_op jit(solution)/shard_map/all_gather | solution.py:236
  83.0 0.7 collective-permute-start.15
  83.7 0.7 constant_dynamic-slice_fusion
  84.4 0.0 all-gather.5.cloned.1.call-update
  84.5 0.0 copy-start.15
  84.5 0.9 dynamic-slice_bitcast_fusion
  85.5 0.0 collective-permute-start.10
  85.5 0.2 copy-done.15
  85.7 0.3 copy-done.16
  85.9 0.1 fusion
  86.1 0.1 collective-permute-start
  86.2 2.2 %collective-permute-start.3 = (bf16[192,1536]{1,0:T(8,128)(2,1)S(1)}, bf16[192,1536]{1,0:T(8,128)(2,1)S(1)}, u32[]{:S(2)}, u32[]{:S(2)}) collective-permute-start(bf16[192,1536]{1,0:T(8,128)(2,1)S(1)} %pad_maximum_fusion.1.own), channel_id=1, source_target_pairs={{0,8},{8,0},{1,9},{9,1},{2,10},{10,2},{3,11},{11,3},{4,12},{12,4},... | collective-permute-start | bytes 1769480 | tf_op jit(solution)/shard_map/ppermute | solution.py:310
  88.4 1.2 collective-permute-start.5
  89.6 0.4 collective-permute-done.10.refs_4_
  89.9 1.2 collective-permute-start.11
  91.2 9.3 %collective-permute-done.11.refs_5_ = bf16[48,3072]{1,0:T(8,128)(2,1)S(1)} collective-permute-done((bf16[48,3072]{1,0:T(8,128)(2,1)S(1)}, bf16[48,3072]{1,0:T(8,128)(2,1)S(1)}, u32[]{:S(2)}, u32[]{:S(2)}) %collective-permute-start.11) | collective-permute-done | bytes 294944 | tf_op jit(solution)/shard_map/ppermute | solution.py:202
  100.5 0.7 copy-done.12
  101.2 2.1 %collective-permute-start.6 = (bf16[192,1536]{1,0:T(8,128)(2,1)S(1)}, bf16[192,1536]{1,0:T(8,128)(2,1)}, u32[]{:S(2)}, u32[]{:S(2)}) collective-permute-start(bf16[192,1536]{1,0:T(8,128)(2,1)S(1)} %pad_maximum_fusion.2.own), channel_id=1, source_target_pairs={{0,1},{1,0},{2,3},{3,2},{4,5},{5,4},{6,7},{7,6},{8,9},{9,8},{10,11... | collective-permute-start | bytes 1769480 | tf_op jit(solution)/shard_map/ppermute | solution.py:307
  103.3 0.8 copy-done.6
  104.1 3.0 %collective-permute-start.2 = (bf16[192,1536]{1,0:T(8,128)(2,1)S(1)}, bf16[192,1536]{1,0:T(8,128)(2,1)}, u32[]{:S(2)}, u32[]{:S(2)}) collective-permute-start(bf16[192,1536]{1,0:T(8,128)(2,1)S(1)} %pad_maximum_fusion.1.own), channel_id=1, source_target_pairs={{1,2},{2,1},{5,6},{6,5},{9,10},{10,9},{13,14},{14,13},{17,18},{18,... | collective-permute-start | bytes 1769480 | tf_op jit(solution)/shard_map/ppermute | solution.py:307
  107.1 7.2 %collective-permute-done.3.refs_0_ = bf16[192,1536]{1,0:T(8,128)(2,1)S(1)} collective-permute-done((bf16[192,1536]{1,0:T(8,128)(2,1)S(1)}, bf16[192,1536]{1,0:T(8,128)(2,1)S(1)}, u32[]{:S(2)}, u32[]{:S(2)}) %collective-permute-start.3) | collective-permute-done | bytes 589856 | tf_op jit(solution)/shard_map/ppermute | solution.py:310
  114.3 0.8 copy-done.8
  115.1 3.8 %all-gather.5.cloned.1.call-done = bf16[384,1536]{1,0:T(8,128)(2,1)} async-done(((bf16[96,1536]{1,0:T(8,128)(2,1)}), bf16[384,1536]{1,0:T(8,128)(2,1)}) %all-gather.5.cloned.1.call-update) | async-done | bytes 1179664 | tf_op jit(solution)/shard_map/all_gather | solution.py:236
  118.9 0.5 collective-permute-start.13
  119.4 1.9 %collective-permute-start.7 = (bf16[192,1536]{1,0:T(8,128)(2,1)S(1)}, bf16[192,1536]{1,0:T(8,128)(2,1)}, u32[]{:S(2)}, u32[]{:S(2)}) collective-permute-start(bf16[192,1536]{1,0:T(8,128)(2,1)S(1)} %pad_maximum_fusion.2.own), channel_id=1, source_target_pairs={{1,2},{2,1},{5,6},{6,5},{9,10},{10,9},{13,14},{14,13},{17,18},{18,... | collective-permute-start | bytes 1769480 | tf_op jit(solution)/shard_map/ppermute | solution.py:307
  121.3 2.3 %collective-permute-start.8 = (bf16[192,1536]{1,0:T(8,128)(2,1)S(1)}, bf16[192,1536]{1,0:T(8,128)(2,1)}, u32[]{:S(2)}, u32[]{:S(2)}) collective-permute-start(bf16[192,1536]{1,0:T(8,128)(2,1)S(1)} %pad_maximum_fusion.2.own), channel_id=1, source_target_pairs={{0,8},{8,0},{1,9},{9,1},{2,10},{10,2},{3,11},{11,3},{4,12},{12,4},... | collective-permute-start | bytes 1769480 | tf_op jit(solution)/shard_map/ppermute | solution.py:310
  123.7 1.2 collective-permute-start.9
  124.9 0.7 constant_dynamic-slice_fusion.2
  126.8 5.3 %collective-permute-done.7.refs_1_ = bf16[192,1536]{1,0:T(8,128)(2,1)} collective-permute-done((bf16[192,1536]{1,0:T(8,128)(2,1)S(1)}, bf16[192,1536]{1,0:T(8,128)(2,1)}, u32[]{:S(2)}, u32[]{:S(2)}) %collective-permute-start.7) | collective-permute-done | bytes 589856 | tf_op jit(solution)/shard_map/ppermute | solution.py:307
  132.1 0.1 add_convert_fusion.1.active
  133.6 0.1 stack.49.place
  133.6 0.1 add_convert_fusion.active
  133.7 1.1 copy-done.7
  134.8 3.0 %attend.2 = (f32[192,768]{1,0:T(8,128)S(1)}, f32[192,768]{1,0:T(8,128)S(1)}, f32[192,768]{1,0:T(8,128)S(1)}) custom-call(s32[2]{0:T(128)S(1)} %add_convert_fusion.1.active, bf16[192,1536]{1,0:T(8,128)(2,1)S(1)} %copy-done.1, bf16[192,1536]{1,0:T(8,128)(2,1)S(1)} %pad_maximum_fusion.1.own, bf16[192,1536]{1,0:T(8,128)(2,1)S(1)} %copy-done.7, ...), custom_call_target="tpu_custom_call" | custom-call | flops 509607936 | bytes 3538944 | tf_op jit(solution)/shard_map/attend/pallas_call | solution.py:80
  137.8 3.2 %attend.3 = (f32[192,768]{1,0:T(8,128)S(1)}, f32[192,768]{1,0:T(8,128)S(1)}, f32[192,768]{1,0:T(8,128)S(1)}) custom-call(s32[2]{0:T(128)S(1)} %add_convert_fusion.1.active, bf16[192,1536]{1,0:T(8,128)(2,1)S(1)} %copy-done.1, bf16[192,1536]{1,0:T(8,128)(2,1)S(1)} %pad_maximum_fusion.2.own, bf16[192,1536]{1,0:T(8,128)(2,1)} %collective-permute-done.6.refs_0_, ...), custom_call_target="tpu_custom_call" | custom-call | flops 509607936 | bytes 3538944 | tf_op jit(solution)/shard_map/attend/pallas_call | solution.py:80
  141.1 2.4 %close.1.ready = bf16[192,768]{1,0:T(8,128)(2,1)S(1)} custom-call(s32[2]{0:T(128)S(1)} %add_convert_fusion.active, bf16[192,1536]{1,0:T(8,128)(2,1)S(1)} %copy-done.1, f32[192,768]{1,0:T(8,128)S(1)} %get-tuple-element.19.part, f32[192,768]{1,0:T(8,128)S(1)} %get-tuple-element.20.total, f32[192,768]{1,0:T(8,128)S(1)} %get-tuple-element.21.peak, ...), custom_call_target="tpu_custom_call" | custom-call | flops 339738624 | bytes 3538944 | tf_op jit(solution)/shard_map/close/pallas_call | solution.py:106
  143.5 6.9 %collective-permute-done.8.refs_0_ = bf16[192,1536]{1,0:T(8,128)(2,1)} collective-permute-done((bf16[192,1536]{1,0:T(8,128)(2,1)S(1)}, bf16[192,1536]{1,0:T(8,128)(2,1)}, u32[]{:S(2)}, u32[]{:S(2)}) %collective-permute-start.8) | collective-permute-done | bytes 589856 | tf_op jit(solution)/shard_map/ppermute | solution.py:310
  150.4 0.2 collective-permute-done.9.refs_1_
  150.7 8.0 %finish.1 = bf16[192,3072]{1,0:T(8,128)(2,1)} custom-call(s32[5]{0:T(128)S(1)} %stack.49.place, s32[2]{0:T(128)S(1)} %add_convert_fusion.active, bf16[192,1536]{1,0:T(8,128)(2,1)S(1)} %copy-done.1, bf16[192,768]{1,0:T(8,128)(2,1)S(1)} %close.1.ready, f32[192,768]{1,0:T(8,128)S(1)} %get-tuple-element.24.part, f32[192,768]{1,0:T(8,128)S(1)} %get-tuple-element.25.total, ...), custom_call_target="tpu_custom_call" | custom-call | flops 1811939328 | bytes 12976128 | tf_op jit(solution)/shard_map/finish/pallas_call | solution.py:177
  (41 shorter events, 0.2 us)
Async XLA Ops:
  6.5 1.1 copy-start
  6.5 76.5 %all-gather.7.cloned.1.call-start = ((), (), s32[]{:S(2)}) async-start(), calls=%async_computation.1 | async-start | bytes 4423680 | tf_op jit(solution)/shard_map/all_gather | solution.py:236
  7.6 16.3 %collective-permute-start.1 = (bf16[1,96,1536]{2,1,0:T(8,128)(2,1)S(1)}, bf16[1,96,1536]{2,1,0:T(8,128)(2,1)S(1)}, u32[]{:S(2)}, u32[]{:S(2)}) collective-permute-start(bf16[1,96,1536]{2,1,0:T(8,128)(2,1)S(1)} %fusion.2), channel_id=1, source_target_pairs={{0,8},{4,12},{8,0},{12,4},{1,9},{5,13},{9,1},{13,5},{2,10},{6,14},... | collective-permute-start | bytes 884744 | tf_op jit(solution)/shard_map/ppermute | solution.py:202
  10.8 14.2 %collective-permute-start.14 = (bf16[1,96,1536]{2,1,0:T(8,128)(2,1)S(1)}, bf16[1,96,1536]{2,1,0:T(8,128)(2,1)S(1)}, u32[]{:S(2)}, u32[]{:S(2)}) collective-permute-start(bf16[1,96,1536]{2,1,0:T(8,128)(2,1)S(1)} %fusion.2), channel_id=1, source_target_pairs={{0,4},{4,0},{8,12},{12,8},{1,5},{5,1},{9,13},{13,9},{2,6},{6,2},{1... | collective-permute-start | bytes 884744 | tf_op jit(solution)/shard_map/ppermute | solution.py:202
  23.9 7.2 %collective-permute-start.4 = (bf16[1,96,1536]{2,1,0:T(8,128)(2,1)S(1)}, bf16[1,96,1536]{2,1,0:T(8,128)(2,1)S(1)}, u32[]{:S(2)}, u32[]{:S(2)}) collective-permute-start(bf16[1,96,1536]{2,1,0:T(8,128)(2,1)S(1)} %collective-permute-done.1), channel_id=1, source_target_pairs={{0,4},{4,0},{8,12},{12,8},{1,5},{5,1},{9,13},{13,9},{2,6},{6,2},{1... | collective-permute-start | bytes 884744 | tf_op jit(solution)/shard_map/ppermute | solution.py:202
  32.1 52.3 %copy-start.14 = (bf16[192,3072]{1,0:T(8,128)(2,1)S(1)}, bf16[192,3072]{1,0:T(8,128)(2,1)}, u32[]{:S(2)}) copy-start(bf16[192,3072]{1,0:T(8,128)(2,1)} %param.11) | copy-start | bytes 3538948
  32.2 86.7 %all-gather.5.cloned.1.call-start = ((), (), s32[]{:S(2)}) async-start(), calls=%async_computation | async-start | bytes 1474560 | tf_op jit(solution)/shard_map/all_gather | solution.py:236
  83.0 67.6 %collective-permute-start.15 = (bf16[4,3,96,1536]{3,2,1,0:T(8,128)(2,1)}, bf16[4,3,96,1536]{3,2,1,0:T(8,128)(2,1)}, u32[]{:S(2)}, u32[]{:S(2)}) collective-permute-start(bf16[4,3,96,1536]{3,2,1,0:T(8,128)(2,1)} %bitcast.34), channel_id=1, source_target_pairs={{0,1},{1,0},{2,3},{3,2},{4,5},{5,4},{6,7},{7,6},{8,9},{9,8},{10,11... | collective-permute-start | bytes 10616840 | tf_op jit(solution)/shard_map/ppermute | solution.py:202
  84.5 1.2 copy-start.15
  84.5 1.4 copy-start.16
  85.5 4.5 %collective-permute-start.10 = (bf16[48,3072]{1,0:T(8,128)(2,1)S(1)}, bf16[48,3072]{1,0:T(8,128)(2,1)S(1)}, u32[]{:S(2)}, u32[]{:S(2)}) collective-permute-start(bf16[48,3072]{1,0:T(8,128)(2,1)S(1)} %get-tuple-element.33), channel_id=1, source_target_pairs={{0,1},{1,0},{2,3},{3,2},{4,5},{5,4},{6,7},{7,6},{8,9},{9,8},{10,11... | collective-permute-start | bytes 884744 | tf_op jit(solution)/shard_map/ppermute | solution.py:202
  86.0 38.9 %copy-start.17 = (s32[1,6]{1,0:T(1,128)S(1)}, s32[1,6]{1,0:T(1,128)}, u32[]{:S(2)}) copy-start(s32[1,6]{1,0:T(1,128)} %param.13) | copy-start | bytes 76
  86.0 47.7 %copy-start.1 = (bf16[192,1536]{1,0:T(8,128)(2,1)S(1)}, bf16[192,1536]{1,0:T(8,128)(2,1)}, u32[]{:S(2)}) copy-start(bf16[192,1536]{1,0:T(8,128)(2,1)} %q.7) | copy-start | bytes 1769476
  86.1 17.2 %collective-permute-start = (bf16[192,1536]{1,0:T(8,128)(2,1)S(1)}, bf16[192,1536]{1,0:T(8,128)(2,1)S(1)}, u32[]{:S(2)}, u32[]{:S(2)}) collective-permute-start(bf16[192,1536]{1,0:T(8,128)(2,1)S(1)} %pad_maximum_fusion.1.own), channel_id=1, source_target_pairs={{0,1},{1,0},{2,3},{3,2},{4,5},{5,4},{6,7},{7,6},{8,9},{9,8},{10,11... | collective-permute-start | bytes 1769480 | tf_op jit(solution)/shard_map/ppermute | solution.py:307
  86.2 28.1 %collective-permute-start.3 = (bf16[192,1536]{1,0:T(8,128)(2,1)S(1)}, bf16[192,1536]{1,0:T(8,128)(2,1)S(1)}, u32[]{:S(2)}, u32[]{:S(2)}) collective-permute-start(bf16[192,1536]{1,0:T(8,128)(2,1)S(1)} %pad_maximum_fusion.1.own), channel_id=1, source_target_pairs={{0,8},{8,0},{1,9},{9,1},{2,10},{10,2},{3,11},{11,3},{4,12},{12,4},... | collective-permute-start | bytes 1769480 | tf_op jit(solution)/shard_map/ppermute | solution.py:310
  88.4 31.0 %collective-permute-start.5 = (bf16[192,1536]{1,0:T(8,128)(2,1)S(1)}, bf16[192,1536]{1,0:T(8,128)(2,1)}, u32[]{:S(2)}, u32[]{:S(2)}) collective-permute-start(bf16[192,1536]{1,0:T(8,128)(2,1)S(1)} %pad_maximum_fusion.1.own), channel_id=1, source_target_pairs={{0,4},{4,0},{1,5},{5,1},{2,6},{6,2},{3,7},{7,3},{8,12},{12,8},{9,1... | collective-permute-start | bytes 1769480 | tf_op jit(solution)/shard_map/ppermute | solution.py:310
  89.9 13.3 %copy-start.10 = (bf16[48,3072]{1,0:T(8,128)(2,1)}, bf16[48,3072]{1,0:T(8,128)(2,1)S(1)}, u32[]{:S(2)}) copy-start(bf16[48,3072]{1,0:T(8,128)(2,1)S(1)} %collective-permute-done.10.refs_4_) | copy-start | bytes 884740
  89.9 10.5 %collective-permute-start.11 = (bf16[48,3072]{1,0:T(8,128)(2,1)S(1)}, bf16[48,3072]{1,0:T(8,128)(2,1)S(1)}, u32[]{:S(2)}, u32[]{:S(2)}) collective-permute-start(bf16[48,3072]{1,0:T(8,128)(2,1)S(1)} %get-tuple-element.29), channel_id=1, source_target_pairs={{0,2},{1,3},{2,0},{3,1},{4,6},{5,7},{6,4},{7,5},{8,10},{9,11},{10,... | collective-permute-start | bytes 884744 | tf_op jit(solution)/shard_map/ppermute | solution.py:202
  100.5 0.7 copy-start.12
  101.2 20.1 %collective-permute-start.6 = (bf16[192,1536]{1,0:T(8,128)(2,1)S(1)}, bf16[192,1536]{1,0:T(8,128)(2,1)}, u32[]{:S(2)}, u32[]{:S(2)}) collective-permute-start(bf16[192,1536]{1,0:T(8,128)(2,1)S(1)} %pad_maximum_fusion.2.own), channel_id=1, source_target_pairs={{0,1},{1,0},{2,3},{3,2},{4,5},{5,4},{6,7},{7,6},{8,9},{9,8},{10,11... | collective-permute-start | bytes 1769480 | tf_op jit(solution)/shard_map/ppermute | solution.py:307
  103.3 0.8 copy-start.6
  104.1 19.6 %collective-permute-start.2 = (bf16[192,1536]{1,0:T(8,128)(2,1)S(1)}, bf16[192,1536]{1,0:T(8,128)(2,1)}, u32[]{:S(2)}, u32[]{:S(2)}) collective-permute-start(bf16[192,1536]{1,0:T(8,128)(2,1)S(1)} %pad_maximum_fusion.1.own), channel_id=1, source_target_pairs={{1,2},{2,1},{5,6},{6,5},{9,10},{10,9},{13,14},{14,13},{17,18},{18,... | collective-permute-start | bytes 1769480 | tf_op jit(solution)/shard_map/ppermute | solution.py:307
  114.3 0.8 copy-start.8
  118.9 31.7 %collective-permute-start.13 = (bf16[4,1,96,1536]{3,2,1,0:T(8,128)(2,1)}, bf16[4,1,96,1536]{3,2,1,0:T(8,128)(2,1)S(1)}, u32[]{:S(2)}, u32[]{:S(2)}) collective-permute-start(bf16[4,1,96,1536]{3,2,1,0:T(8,128)(2,1)} %bitcast.36), channel_id=1, source_target_pairs={{0,1},{1,0},{2,3},{3,2},{4,5},{5,4},{6,7},{7,6},{8,9},{9,8},{10,11... | collective-permute-start | bytes 3538952 | tf_op jit(solution)/shard_map/ppermute | solution.py:202
  119.4 12.7 %collective-permute-start.7 = (bf16[192,1536]{1,0:T(8,128)(2,1)S(1)}, bf16[192,1536]{1,0:T(8,128)(2,1)}, u32[]{:S(2)}, u32[]{:S(2)}) collective-permute-start(bf16[192,1536]{1,0:T(8,128)(2,1)S(1)} %pad_maximum_fusion.2.own), channel_id=1, source_target_pairs={{1,2},{2,1},{5,6},{6,5},{9,10},{10,9},{13,14},{14,13},{17,18},{18,... | collective-permute-start | bytes 1769480 | tf_op jit(solution)/shard_map/ppermute | solution.py:307
  121.3 29.1 %collective-permute-start.8 = (bf16[192,1536]{1,0:T(8,128)(2,1)S(1)}, bf16[192,1536]{1,0:T(8,128)(2,1)}, u32[]{:S(2)}, u32[]{:S(2)}) collective-permute-start(bf16[192,1536]{1,0:T(8,128)(2,1)S(1)} %pad_maximum_fusion.2.own), channel_id=1, source_target_pairs={{0,8},{8,0},{1,9},{9,1},{2,10},{10,2},{3,11},{11,3},{4,12},{12,4},... | collective-permute-start | bytes 1769480 | tf_op jit(solution)/shard_map/ppermute | solution.py:310
  123.7 26.9 %collective-permute-start.9 = (bf16[192,1536]{1,0:T(8,128)(2,1)S(1)}, bf16[192,1536]{1,0:T(8,128)(2,1)}, u32[]{:S(2)}, u32[]{:S(2)}) collective-permute-start(bf16[192,1536]{1,0:T(8,128)(2,1)S(1)} %pad_maximum_fusion.2.own), channel_id=1, source_target_pairs={{0,4},{4,0},{1,5},{5,1},{2,6},{6,2},{3,7},{7,3},{8,12},{12,8},{9,1... | collective-permute-start | bytes 1769480 | tf_op jit(solution)/shard_map/ppermute | solution.py:310
  132.1 11.4 %collective-permute-start.12 = (bf16[48,3072]{1,0:T(8,128)(2,1)}, bf16[48,3072]{1,0:T(8,128)(2,1)}, u32[]{:S(2)}, u32[]{:S(2)}) collective-permute-start(bf16[48,3072]{1,0:T(8,128)(2,1)} %get-tuple-element.30), channel_id=1, source_target_pairs={{0,3},{1,2},{2,1},{3,0},{4,7},{5,6},{6,5},{7,4},{8,11},{9,10},{10,... | collective-permute-start | bytes 884744 | tf_op jit(solution)/shard_map/ppermute | solution.py:202
  133.7 1.1 copy-start.7
  134.8 6.3 %copy-start.9 = (bf16[192,1536]{1,0:T(8,128)(2,1)S(1)}, bf16[192,1536]{1,0:T(8,128)(2,1)}, u32[]{:S(2)}) copy-start(bf16[192,1536]{1,0:T(8,128)(2,1)} %copy-done.8) | copy-start | bytes 1769476
  134.8 15.8 %copy-start.11 = (bf16[48,3072]{1,0:T(8,128)(2,1)S(1)}, bf16[48,3072]{1,0:T(8,128)(2,1)}, u32[]{:S(2)}) copy-start(bf16[48,3072]{1,0:T(8,128)(2,1)} %copy-done.10) | copy-start | bytes 884740
  134.8 15.8 %copy-start.13 = (bf16[48,3072]{1,0:T(8,128)(2,1)S(1)}, bf16[48,3072]{1,0:T(8,128)(2,1)}, u32[]{:S(2)}) copy-start(bf16[48,3072]{1,0:T(8,128)(2,1)} %copy-done.12) | copy-start | bytes 884740
  137.8 12.8 %copy-start.3 = (bf16[192,3072]{1,0:T(8,128)(2,1)S(1)}, bf16[192,3072]{1,0:T(8,128)(2,1)}, u32[]{:S(2)}) copy-start(bf16[192,3072]{1,0:T(8,128)(2,1)} %refs_2_.1) | copy-start | bytes 3538948
  137.8 12.8 %copy-start.4 = (bf16[384,1536]{1,0:T(8,128)(2,1)S(1)}, bf16[384,1536]{1,0:T(8,128)(2,1)}, u32[]{:S(2)}) copy-start(bf16[384,1536]{1,0:T(8,128)(2,1)} %all-gather.5.cloned.1.call-done) | copy-start | bytes 3538948
  141.1 9.6 %copy-start.2 = (bf16[12,96,1536]{2,1,0:T(8,128)(2,1)S(1)}, bf16[12,96,1536]{2,1,0:T(8,128)(2,1)}, u32[]{:S(2)}) copy-start(bf16[12,96,1536]{2,1,0:T(8,128)(2,1)} %all-gather.7.cloned.1.call-done) | copy-start | bytes 10616836
  141.1 9.6 %copy-start.5 = (bf16[48,3072]{1,0:T(8,128)(2,1)S(1)}, bf16[48,3072]{1,0:T(8,128)(2,1)}, u32[]{:S(2)}) copy-start(bf16[48,3072]{1,0:T(8,128)(2,1)} %get-tuple-element.34.refs_3_) | copy-start | bytes 884740
Sparse Core Ops, SparseCore 0:
  32.3 50.6 all-gather.6
  84.8 34.0 all-gather.4

commit v3 on v2

--- a/solution.py
+++ b/solution.py
@@ -128,13 +128,12 @@
     out, attention, held, hidden_v, control_v, *state, sems, res_sems = refs
     copies = []
     for number, (piece, index, flips) in enumerate(moves):
-        source = weight[piece].at[index] if index else weight[piece]
+        source = weight[piece].at[index] if flips else weight[piece]
         if flips is None:
             target = held
         else:
             count = source.shape[0]
-            (group, pair), outer_flip, core_flip = flips
-            outer, core = place[1] ^ outer_flip, place[3] ^ core_flip
+            group, outer, pair, core = (place[i] ^ flip for i, flip in enumerate(flips))
             start = pl.multiple_of(((outer * 2 + pair) * 2 + core) * count, count)
             target = held.at[group, pl.ds(start, count), :]
         copies.append(pltpu.make_async_copy(source, target, sems.at[number]))
@@ -202,57 +201,59 @@
     return lax.ppermute(block, axis, [(i, i ^ flip) for i in range(lax.axis_size(axis))])
 
 
-def control_blocks(control, across, grid_width, wait_for):
-    rows, width = control.shape
-    block = rows // grid_width
-    lines = control.reshape(block // TILE_W, grid_width, TILE_W, width)
-    blocks = []
-    for d in range(grid_width):
-        mine = lax.dynamic_index_in_dim(lines, across ^ d, 1, keepdims=False).reshape(block, width)
-        blocks.append(flipped(after(mine, *wait_for) if d > 1 else mine, TILES, d) if d else mine)
-    if block % 16 == 0:
-        return blocks
-    order = jnp.arange(grid_width, dtype=jnp.int32) ^ across
-    return [jnp.take(jnp.stack(blocks), order, axis=0).reshape(rows, width)]
-
-
-def gather_weight(out_weight):
-    groups = lax.axis_size("groups")
-    outer, pair, cores = (lax.axis_size(a) for a in TILES)
-    rows, width = out_weight.shape
-    columns = width // groups
-    share = lax.dynamic_slice(out_weight, (0, lax.axis_index("groups") * columns), (rows, columns))
-    line = share[None]
-    flip = outer // 2
-    while flip > 2:
-        line = jnp.concatenate([line, flipped(line, "outer", flip)])
-        flip //= 2
-    far = flipped(line, "outer", 2)
-    near = flipped(line, "outer", 1)
-    last = flipped(far, "outer", 1)
-    steps = [line, jnp.concatenate([far, near, last])]
-    flips = [sum(((outer // 2) >> b) * (i >> b & 1) for b in range(outer.bit_length() - 1)) for i in range(outer // 4)]
-    flips = [flips, [f ^ x for x in (2, 1, 3) for f in flips]]
-    mine = [lax.all_gather(x, ("groups", "pair")) for x in steps]
-    other = [flipped(x, "core", 1) for x in mine]
-    if rows % 16 == 0:
-        moves = tuple(
-            (2 * step + core, (g * pair + p, i), ((g, p), f, core))
-            for step in range(2)
-            for core in range(2)
-            for g in range(groups)
-            for p in range(pair)
-            for i, f in enumerate(flips[step])
-        )
-        return [x for pair_of in zip(mine, other) for x in pair_of], moves, far, last
-    whole = [jnp.concatenate(x, axis=1) for x in (mine, other)]
-    order = jnp.array([flips_all.index(f) for flips_all in [flips[0] + flips[1]] for f in range(outer)], jnp.int32)
-    whole = [jnp.take(x, order[jnp.arange(outer) ^ lax.axis_index("outer")], axis=1) for x in whole]
-    first = lax.axis_index("core") == 0
-    both = jnp.stack([jnp.where(first, whole[0], whole[1]), jnp.where(first, whole[1], whole[0])], axis=2)
-    both = both.reshape(groups, pair, outer, cores, rows, columns).transpose(0, 2, 1, 3, 4, 5)
-    whole = both.reshape(groups, outer * pair * cores * rows, columns)
-    return [whole], ((0, None, None),), far, last
+class Lane:
+    def __init__(self):
+        self.last = None
+
+    def __call__(self, send, block, *others):
+        waits = [x for x in (self.last, *others) if x is not None]
+        self.last = send(after(block, *waits) if waits else block)
+        return self.last
+
+
+def swap(axis, flip):
+    return lambda block: flipped(block, axis, flip)
+
+
+def route_of(route):
+    return lambda block: lax.ppermute(block, TILES, route)
+
+
+def copy_kernel(count, moves, start, *refs):
+    sources, targets, sems = refs[:count], refs[count:-1], refs[-1]
+    copies = []
+    for number, (source, source_at, target, target_at) in enumerate(moves):
+        column, columns, times = source_at
+        column = pl.multiple_of(start[0] * columns, 128) if times else column
+        from_ref = sources[source].at[..., pl.ds(column, columns)]
+        copies.append(pltpu.make_async_copy(from_ref, targets[target].at[target_at], sems.at[number]))
+    for copy in copies:
+        copy.start()
+    for copy in copies:
+        copy.wait()
+
+
+def copied(start, arrays, shapes, moves, name):
+    return pl.pallas_call(
+        functools.partial(copy_kernel, len(arrays), moves),
+        out_shape=[jax.ShapeDtypeStruct(shape, jnp.bfloat16) for shape in shapes],
+        in_specs=[SMEM] + [ANY] * len(arrays),
+        out_specs=[ANY] * len(shapes),
+        scratch_shapes=[pltpu.SemaphoreType.DMA((len(moves),))],
+        cost_estimate=pl.CostEstimate(
+            flops=0, bytes_accessed=4 * sum(math.prod(shape) for shape in shapes), transcendentals=0
+        ),
+        name=name,
+    )(start, *arrays)
+
+
+def stacked(a, b):
+    if a.shape[1] % 16:
+        return jnp.concatenate([a, b])
+    n, rows, columns = a.shape
+    whole = (0, columns, False)
+    moves = ((0, whole, 0, pl.ds(0, n)), (1, whole, 0, pl.ds(n, n)))
+    return copied(jnp.zeros(1, jnp.int32), (a, b), [(2 * n, rows, columns)], moves, "stacked")[0]
 
 
 def neighbour_slots(tile_count, strides, counts):
@@ -270,8 +271,9 @@
 
 
 def on_device(hidden, queries, keys, values, control, out_weight, pattern):
-    sizes = [lax.axis_size(a) for a in TILES]
-    tile_count = math.prod(sizes)
+    groups = lax.axis_size("groups")
+    outer, pair, cores = (lax.axis_size(a) for a in TILES)
+    tile_count = outer * pair * cores
     grid_width = min(8, tile_count // 4)
     grid_height = min(4, tile_count // 8)
     layer = grid_width * grid_height
@@ -279,12 +281,10 @@
     counts = (tile_count // layer, grid_height, grid_width)
     position = lax.axis_index(TILES)
     across = position % grid_width
-    weight, moves, far, last = gather_weight(out_weight)
-    columns = queries.shape[1] // HALVES
-    kv = [
-        jnp.concatenate([x[:, half * columns : (half + 1) * columns] for x in (keys, values)], axis=1)
-        for half in range(HALVES)
-    ]
+    rows, inner = queries.shape
+    width = hidden.shape[1]
+    columns = inner // HALVES
+    heads = columns // HEAD_DIM
     slots = neighbour_slots(tile_count, strides, counts)
     early = [s for s in slots if s[0] == 2]
     late = [s for s in slots if s[0] != 2]
@@ -299,25 +299,107 @@
         return jnp.stack(active)
 
     early_active, late_active = flags(early), flags(late)
-    early_near, late_near = [], []
+    far_lane, near_lane, x_lane, y_lane, core_lane = (Lane() for _ in range(5))
+
+    shard, share = out_weight.shape[0], width // groups
+    group = lax.axis_index("groups").astype(jnp.int32)
+    line = copied(
+        group[None], (out_weight,), [(1, shard, share)], ((0, (0, share, True), 0, 0),), "share"
+    )[0]
+    line_flips = [0]
+    flip = outer // 2
+    while flip > 2:
+        line = jnp.concatenate([line, flipped(line, "outer", flip)])
+        line_flips += [f ^ flip for f in line_flips]
+        flip //= 2
+    far = far_lane(swap("outer", 2), line)
+    near = near_lane(swap("outer", 1), line)
+    last = near_lane(swap("outer", 1), far)
+    parts = [(line, 0), (far, 2), (near, 1), (last, 3)]
+
+    halves = copied(
+        group[None],
+        (keys, values),
+        [(rows, 2 * columns)] * HALVES,
+        tuple(
+            (source, (half * columns, columns, False), half, (slice(None), pl.ds(source * columns, columns)))
+            for half in range(HALVES)
+            for source in range(2)
+        ),
+        "halves",
+    )
+    block = rows // grid_width
+    lines = control.reshape(block // TILE_W, grid_width, TILE_W, width)
+    control_sent = [
+        lax.dynamic_index_in_dim(lines, across ^ d, 1, keepdims=False).reshape(block, width) for d in range(grid_width)
+    ]
+    control_parts = [control_sent[0]] + [None] * (grid_width - 1)
+    control_parts[1] = core_lane(swap(TILES, 1), control_sent[1])
+    early_near = [[None] * len(early) for _ in range(HALVES)]
     for half in range(HALVES):
-        early_near.append([])
-        for axis, odd, route in early:
-            block = kv[half] if odd == 0 else after(kv[half], far)
-            early_near[half].append(lax.ppermute(block, TILES, route))
-        waits = [far, last] if half == 0 else late_near[-1]
-        late_near.append(
-            [lax.ppermute(after(kv[half], waits[i % 2]), TILES, route) for i, (_, _, route) in enumerate(late)]
-        )
-    control_parts = control_blocks(control, across, grid_width, (far,))
-    heads = columns // HEAD_DIM
-    states = [attend(early_active, queries, half * heads, kv[half], early_near[half]) for half in range(HALVES)]
+        early_near[half][0] = core_lane(route_of(early[0][2]), halves[half])
+
+    held = []
+    for piece, _ in parts:
+        beside = x_lane(swap("pair", 1), piece)
+        plane = stacked(piece, beside)
+        held.append((plane, y_lane(swap("groups", 1), plane)))
+    order = [(0, 0), (0, 1), (1, 0), (2, 0), (1, 1), (3, 0), (2, 1), (3, 1)]
+    crossed = {at: core_lane(swap("core", 1), held[at[0]][at[1]]) for at in order}
+    weight, moves = [], []
+    for number, (_, outer_flip) in enumerate(parts):
+        for y_flip in range(2):
+            for core_flip in range(2):
+                n = len(line_flips)
+                moves += [
+                    (len(weight), i, (y_flip, line_flips[i % n] ^ outer_flip, i // n, core_flip)) for i in range(2 * n)
+                ]
+                weight.append(crossed[number, y_flip] if core_flip else held[number][y_flip])
+
+    late_near = []
+    lanes = [far_lane, near_lane]
+    for half in range(HALVES):
+        late_near.append([lanes[i % 2](route_of(route), halves[half]) for i, (_, _, route) in enumerate(late)])
+    for half in range(HALVES):
+        for i in range(1, len(early)):
+            early_near[half][i] = x_lane(route_of(early[i][2]), halves[half])
+        for d in range(2 + half, grid_width, HALVES):
+            control_parts[d] = x_lane(swap(TILES, d), control_sent[d])
+
+    states = [attend(early_active, queries, half * heads, halves[half], early_near[half]) for half in range(HALVES)]
     ready = [close(late_active, queries, half * heads, states[half], late_near[half]) for half in range(HALVES - 1)]
     ready = ready[0] if len(ready) == 1 else jnp.concatenate(ready, axis=1)
+    if block % 16:
+        control_parts = [
+            jnp.take(
+                jnp.stack(control_parts), jnp.arange(grid_width, dtype=jnp.int32) ^ across, axis=0
+            ).reshape(rows, width)
+        ]
     place = jnp.stack([lax.axis_index(a) for a in ("groups",) + TILES] + [across]).astype(jnp.int32)
+    if shard % 16:
+        weight, moves = [in_order(weight, moves, place, (groups, outer, pair, cores))], [(0, None, None)]
     return finish(
-        place, late_active, queries, ready, states[-1], late_near[-1], hidden, control_parts, weight, moves
+        place,
+        late_active,
+        queries,
+        ready,
+        states[-1],
+        late_near[-1],
+        hidden,
+        control_parts,
+        weight,
+        tuple(moves),
     )
+
+
+def in_order(weight, moves, place, sizes):
+    blocks = {flips: weight[piece][index] for piece, index, flips in moves}
+    whole = jnp.stack([blocks[flips] for flips in sorted(blocks)])
+    shard, columns = whole.shape[1:]
+    whole = whole.reshape(sizes + (shard, columns))
+    for axis, size in enumerate(sizes):
+        whole = jnp.take(whole, jnp.arange(size, dtype=jnp.int32) ^ place[axis], axis=axis)
+    return whole.reshape(sizes[0], -1, columns)
 
 
 def solution(mesh):

time: 167 us -> 270 us (1.62)
  Pallas kernels: 16.6 us -> 142 us
  waiting for transfers between devices: 102 us -> 73.2 us
  starting transfers between devices: 22 us -> 35.9 us
  between operations: 16.3 us -> 2.95 us
  local copies, waits for them, and re-layouts: 7.56 us -> 15.2 us
    pallas_call x0 -> x6, Pallas kernels: none -> 123 us  [copied(): pl.pallas_call(functools.partial(copy_kernel, len(arrays), moves), out_sh...]
    all_gather x2 -> x0, waiting for transfers between devices: 54.6 us -> none  [gather_weight(): mine = [lax.all_gather(x, ('groups', 'pair')) for x in steps]]
    ppermute x8 -> x22, waiting for transfers between devices: 27.6 us -> 55.5 us  [flipped(): lax.ppermute(block, axis, [(i, i ^ flip) for i in range(lax.axis_size(axi...]
    ppermute x8 -> x22, starting transfers between devices: 8 us -> 20.6 us  [flipped(): lax.ppermute(block, axis, [(i, i ^ flip) for i in range(lax.axis_size(axi...]
    unnamed x36 -> x66, local copies, waits for them, and re-layouts: 5.03 us -> 12.4 us
  transfers between devices with their start and end apart: 18 -> 30, of which waited for: 10 -> 13; matrix products, arithmetic and copies ran while one was open for 2% -> 0% of each run, Pallas kernels for 5% -> 50%
where the time goes in v3:
time: 270 us; the launch traced here: 269 us
  Pallas kernels  142 us (53%)
  waiting for transfers between devices  73.2 us (27%)
  starting transfers between devices  35.9 us (13%)
  local copies, waits for them, and re-layouts  15.2 us (6%)
  between operations  2.95 us (1%)
    pallas_call x6, Pallas kernels, copied(): pl.pallas_call(functools.partial(copy_kernel, len(arrays), moves), out_sh...  123 us
    ppermute x22, waiting for transfers between devices, flipped(): lax.ppermute(block, axis, [(i, i ^ flip) for i in range(lax.axis_size(axi...  55.5 us
    ppermute x22, starting transfers between devices, flipped(): lax.ppermute(block, axis, [(i, i ^ flip) for i in range(lax.axis_size(axi...  20.6 us
    ppermute x8, waiting for transfers between devices, route_of(): return lambda block: lax.ppermute(block, TILES, route)  17.7 us
    ppermute x8, starting transfers between devices, route_of(): return lambda block: lax.ppermute(block, TILES, route)  15.4 us
    unnamed x66, local copies, waits for them, and re-layouts  12.4 us
    pallas_call x1, Pallas kernels, finish(): pl.pallas_call(functools.partial(finish_kernel, len(near), len(control),...  8.54 us
    pallas_call x2, Pallas kernels, attend(): pl.pallas_call(functools.partial(attend_kernel, len(near), first_head), o...  7.87 us
  transfers between devices with their start and end apart: 30, of which 13 were waited for; matrix products, arithmetic and copies ran while one was open for 0% of the time, Pallas kernels for 50%

profile of v3, /device:TPU:1, one launch (start us, length us, event | category | flops | bytes accessed | tf_op | source)
XLA Modules:
  0.0 269.3 jit_solution(5632362497154406554)
XLA Ops:
  0.0 2.1 dynamic-slice_bitcast_fusion
  2.2 36.9 %halves.1 = (bf16[192,1536]{1,0:T(8,128)(2,1)}, bf16[192,1536]{1,0:T(8,128)(2,1)}) custom-call(s32[1]{0:T(128)} %bitcast.start, bf16[192,1536]{1,0:T(8,128)(2,1)} %refs_0_.2, bf16[192,1536]{1,0:T(8,128)(2,1)} %refs_1_.1), custom_call_target="tpu_custom_call" | custom-call | bytes 2359296 | tf_op jit(solution)/shard_map/halves/pallas_call | solution.py:237
  39.6 1.8 collective-permute-done.1.refs_0_
  41.8 10.0 %share.1.refs_0_ = bf16[1,96,1536]{2,1,0:T(8,128)(2,1)} custom-call(s32[1]{0:T(128)} %bitcast.start, bf16[96,3072]{1,0:T(8,128)(2,1)} %refs_0_.3), custom_call_target="tpu_custom_call" | custom-call | bytes 589824 | tf_op jit(solution)/shard_map/share/pallas_call | solution.py:237
  51.9 2.4 collective-permute-start.5
  54.3 7.3 %collective-permute-done.5.refs_1_ = bf16[1,96,1536]{2,1,0:T(8,128)(2,1)S(1)} collective-permute-done((bf16[1,96,1536]{2,1,0:T(8,128)(2,1)}, bf16[1,96,1536]{2,1,0:T(8,128)(2,1)S(1)}, u32[]{:S(2)}, u32[]{:S(2)}) %collective-permute-start.5) | collective-permute-done | bytes 294944 | tf_op jit(solution)/shard_map/ppermute | solution.py:201
  62.3 19.0 %stacked.4.refs_7_ = bf16[2,96,1536]{2,1,0:T(8,128)(2,1)} custom-call(s32[1]{0:T(128)} %constant.119.clone.1.start, bf16[1,96,1536]{2,1,0:T(8,128)(2,1)} %share.1.refs_0_, bf16[1,96,1536]{2,1,0:T(8,128)(2,1)} %copy-done.31), custom_call_target="tpu_custom_call" | custom-call | bytes 1179648 | tf_op jit(solution)/shard_map/stacked/pallas_call | solution.py:237
  81.3 1.2 collective-permute-start.19
  82.5 0.8 copy-done.15
  83.3 1.5 collective-permute-start.18
  84.8 2.3 collective-permute-start.2
  87.1 8.4 %collective-permute-done.19.refs_9_ = bf16[2,96,1536]{2,1,0:T(8,128)(2,1)S(1)} collective-permute-done((bf16[2,96,1536]{2,1,0:T(8,128)(2,1)}, bf16[2,96,1536]{2,1,0:T(8,128)(2,1)S(1)}, u32[]{:S(2)}, u32[]{:S(2)}) %collective-permute-start.19) | collective-permute-done | bytes 589856 | tf_op jit(solution)/shard_map/ppermute | solution.py:201
  95.5 1.8 collective-permute-start.20
  97.3 3.4 %collective-permute-done.2.refs_0_ = bf16[1,96,1536]{2,1,0:T(8,128)(2,1)S(1)} collective-permute-done((bf16[1,96,1536]{2,1,0:T(8,128)(2,1)S(1)}, bf16[1,96,1536]{2,1,0:T(8,128)(2,1)S(1)}, u32[]{:S(2)}, u32[]{:S(2)}) %collective-permute-start.2) | collective-permute-done | bytes 294944 | tf_op jit(solution)/shard_map/ppermute | solution.py:201
  100.7 1.2 collective-permute-start.6
  102.6 5.9 %collective-permute-done.6.refs_1_ = bf16[1,96,1536]{2,1,0:T(8,128)(2,1)S(1)} collective-permute-done((bf16[1,96,1536]{2,1,0:T(8,128)(2,1)S(1)}, bf16[1,96,1536]{2,1,0:T(8,128)(2,1)S(1)}, u32[]{:S(2)}, u32[]{:S(2)}) %collective-permute-start.6) | collective-permute-done | bytes 294944 | tf_op jit(solution)/shard_map/ppermute | solution.py:201
  109.3 19.0 %stacked.5.refs_11_ = bf16[2,96,1536]{2,1,0:T(8,128)(2,1)} custom-call(s32[1]{0:T(128)} %constant.119.clone.1.start, bf16[1,96,1536]{2,1,0:T(8,128)(2,1)} %copy-done.26, bf16[1,96,1536]{2,1,0:T(8,128)(2,1)} %copy-done.30), custom_call_target="tpu_custom_call" | custom-call | bytes 1179648 | tf_op jit(solution)/shard_map/stacked/pallas_call | solution.py:237
  128.3 1.6 collective-permute-start.21
  129.9 1.2 collective-permute-start.7
  131.4 7.4 %collective-permute-done.7.refs_1_ = bf16[1,96,1536]{2,1,0:T(8,128)(2,1)S(1)} collective-permute-done((bf16[1,96,1536]{2,1,0:T(8,128)(2,1)}, bf16[1,96,1536]{2,1,0:T(8,128)(2,1)S(1)}, u32[]{:S(2)}, u32[]{:S(2)}) %collective-permute-start.7) | collective-permute-done | bytes 294944 | tf_op jit(solution)/shard_map/ppermute | solution.py:201
  139.5 19.0 %stacked.6.refs_15_ = bf16[2,96,1536]{2,1,0:T(8,128)(2,1)} custom-call(s32[1]{0:T(128)} %constant.119.clone.1.start, bf16[1,96,1536]{2,1,0:T(8,128)(2,1)} %collective-permute-done.3.refs_0_, bf16[1,96,1536]{2,1,0:T(8,128)(2,1)} %copy-done.29), custom_call_target="tpu_custom_call" | custom-call | bytes 1179648 | tf_op jit(solution)/shard_map/stacked/pallas_call | solution.py:237
  158.5 0.8 collective-permute-start.23
  160.1 1.1 collective-permute-done.23.refs_16_
  162.4 5.8 %collective-permute-done.4.refs_0_ = bf16[1,96,1536]{2,1,0:T(8,128)(2,1)S(1)} collective-permute-done((bf16[1,96,1536]{2,1,0:T(8,128)(2,1)}, bf16[1,96,1536]{2,1,0:T(8,128)(2,1)S(1)}, u32[]{:S(2)}, u32[]{:S(2)}) %collective-permute-start.4) | collective-permute-done | bytes 294944 | tf_op jit(solution)/shard_map/ppermute | solution.py:201
  168.9 1.2 collective-permute-start.8
  170.1 6.5 %collective-permute-done.8.refs_1_ = bf16[1,96,1536]{2,1,0:T(8,128)(2,1)S(1)} collective-permute-done((bf16[1,96,1536]{2,1,0:T(8,128)(2,1)S(1)}, bf16[1,96,1536]{2,1,0:T(8,128)(2,1)S(1)}, u32[]{:S(2)}, u32[]{:S(2)}) %collective-permute-start.8) | collective-permute-done | bytes 294944 | tf_op jit(solution)/shard_map/ppermute | solution.py:201
  177.3 4.7 %collective-permute-start.9 = (bf16[192,1536]{1,0:T(8,128)(2,1)}, bf16[192,1536]{1,0:T(8,128)(2,1)}, u32[]{:S(2)}, u32[]{:S(2)}) collective-permute-start(bf16[192,1536]{1,0:T(8,128)(2,1)} %get-tuple-element.49.own), channel_id=1, source_target_pairs={{1,2},{2,1},{5,6},{6,5},{9,10},{10,9},{13,14},{14,13},{17,18},{18,... | collective-permute-start | bytes 1769480 | tf_op jit(solution)/shard_map/ppermute | solution.py:219
  182.1 19.0 %stacked.7.refs_19_ = bf16[2,96,1536]{2,1,0:T(8,128)(2,1)} custom-call(s32[1]{0:T(128)} %constant.119.clone.1.start, bf16[1,96,1536]{2,1,0:T(8,128)(2,1)} %copy-done.27, bf16[1,96,1536]{2,1,0:T(8,128)(2,1)} %copy-done.28), custom_call_target="tpu_custom_call" | custom-call | bytes 1179648 | tf_op jit(solution)/shard_map/stacked/pallas_call | solution.py:237
  201.8 2.6 collective-permute-start.10
  204.3 1.3 collective-permute-start.11
  205.6 9.8 %collective-permute-done.25.refs_17_ = bf16[2,96,1536]{2,1,0:T(8,128)(2,1)S(1)} collective-permute-done((bf16[2,96,1536]{2,1,0:T(8,128)(2,1)S(1)}, bf16[2,96,1536]{2,1,0:T(8,128)(2,1)S(1)}, u32[]{:S(2)}, u32[]{:S(2)}) %collective-permute-start.25) | collective-permute-done | bytes 589856 | tf_op jit(solution)/shard_map/ppermute | solution.py:201
  216.5 0.8 copy-done.7
  218.1 1.9 collective-permute-start.14
  220.0 10.6 %collective-permute-done.10.refs_0_ = bf16[192,1536]{1,0:T(8,128)(2,1)S(1)} collective-permute-done((bf16[192,1536]{1,0:T(8,128)(2,1)}, bf16[192,1536]{1,0:T(8,128)(2,1)S(1)}, u32[]{:S(2)}, u32[]{:S(2)}) %collective-permute-start.10) | collective-permute-done | bytes 589856 | tf_op jit(solution)/shard_map/ppermute | solution.py:219
  230.6 0.8 copy-done.19
  231.4 0.9 copy-done.21
  232.3 4.0 %collective-permute-start.16 = (bf16[192,1536]{1,0:T(8,128)(2,1)}, bf16[192,1536]{1,0:T(8,128)(2,1)}, u32[]{:S(2)}, u32[]{:S(2)}) collective-permute-start(bf16[192,1536]{1,0:T(8,128)(2,1)} %get-tuple-element.58.own), channel_id=1, source_target_pairs={{0,4},{4,0},{1,5},{5,1},{2,6},{6,2},{3,7},{7,3},{8,12},{12,8},{9,1... | collective-permute-start | bytes 1769480 | tf_op jit(solution)/shard_map/ppermute | solution.py:219
  236.3 0.8 copy-done.11
  237.1 1.0 collective-permute-start.29
  240.1 1.1 collective-permute-start.17
  242.7 1.1 copy-done.14
  243.7 1.1 copy-done.18
  244.8 3.9 %attend.2 = (f32[192,768]{1,0:T(8,128)S(1)}, f32[192,768]{1,0:T(8,128)S(1)}, f32[192,768]{1,0:T(8,128)S(1)}) custom-call(s32[2]{0:T(128)S(1)} %add_convert_fusion.1.active, bf16[192,1536]{1,0:T(8,128)(2,1)S(1)} %copy-done, bf16[192,1536]{1,0:T(8,128)(2,1)S(1)} %copy-done.14, bf16[192,1536]{1,0:T(8,128)(2,1)S(1)} %copy-done.18, ...), custom_call_target="tpu_custom_call" | custom-call | flops 509607936 | bytes 3538944 | tf_op jit(solution)/shard_map/attend/pallas_call | solution.py:80
  248.8 2.6 close.1.ready
  251.5 4.0 %attend.3 = (f32[192,768]{1,0:T(8,128)S(1)}, f32[192,768]{1,0:T(8,128)S(1)}, f32[192,768]{1,0:T(8,128)S(1)}) custom-call(s32[2]{0:T(128)S(1)} %add_convert_fusion.1.active, bf16[192,1536]{1,0:T(8,128)(2,1)S(1)} %copy-done, bf16[192,1536]{1,0:T(8,128)(2,1)S(1)} %copy-done.13, bf16[192,1536]{1,0:T(8,128)(2,1)S(1)} %copy-done.16, ...), custom_call_target="tpu_custom_call" | custom-call | flops 509607936 | bytes 3538944 | tf_op jit(solution)/shard_map/attend/pallas_call | solution.py:80
  255.4 3.7 %collective-permute-done.15.refs_0_ = bf16[192,1536]{1,0:T(8,128)(2,1)} collective-permute-done((bf16[192,1536]{1,0:T(8,128)(2,1)}, bf16[192,1536]{1,0:T(8,128)(2,1)}, u32[]{:S(2)}, u32[]{:S(2)}) %collective-permute-start.15) | collective-permute-done | bytes 589856 | tf_op jit(solution)/shard_map/ppermute | solution.py:219
  259.1 1.6 collective-permute-done.16.refs_1_
  260.8 8.5 %finish.1 = bf16[192,3072]{1,0:T(8,128)(2,1)} custom-call(s32[5]{0:T(128)S(1)} %stack.49.place, s32[2]{0:T(128)S(1)} %add_convert_fusion.active, bf16[192,1536]{1,0:T(8,128)(2,1)S(1)} %copy-done, bf16[192,768]{1,0:T(8,128)(2,1)S(1)} %close.1.ready, f32[192,768]{1,0:T(8,128)S(1)} %get-tuple-element.54.part, f32[192,768]{1,0:T(8,128)S(1)} %get-tuple-element.55.total, ...), custom_call_target="tpu_custom_call" | custom-call | flops 1811939328 | bytes 12976128 | tf_op jit(solution)/shard_map/finish/pallas_call | solution.py:176
  (93 shorter events, 11.0 us)
Async XLA Ops:
  2.1 36.9 %collective-permute-start = (bf16[48,3072]{1,0:T(8,128)(2,1)S(1)}, bf16[48,3072]{1,0:T(8,128)(2,1)S(1)}, u32[]{:S(2)}, u32[]{:S(2)}) collective-permute-start(bf16[48,3072]{1,0:T(8,128)(2,1)S(1)} %get-tuple-element.74), channel_id=1, source_target_pairs={{0,1},{1,0},{2,3},{3,2},{4,5},{5,4},{6,7},{7,6},{8,9},{9,8},{10,11... | collective-permute-start | bytes 884744 | tf_op jit(solution)/shard_map/ppermute | solution.py:201
  39.1 2.4 collective-permute-start.1
  41.4 20.1 %copy-start.17 = (bf16[192,1536]{1,0:T(8,128)(2,1)}, bf16[192,1536]{1,0:T(8,128)(2,1)S(1)}, u32[]{:S(2)}) copy-start(bf16[192,1536]{1,0:T(8,128)(2,1)S(1)} %collective-permute-done.1.refs_0_) | copy-start | bytes 1769476
  41.4 41.1 %collective-permute-start.12 = (bf16[192,1536]{1,0:T(8,128)(2,1)}, bf16[192,1536]{1,0:T(8,128)(2,1)S(1)}, u32[]{:S(2)}, u32[]{:S(2)}) collective-permute-start(bf16[192,1536]{1,0:T(8,128)(2,1)} %get-tuple-element.58.own), channel_id=1, source_target_pairs={{0,1},{1,0},{2,3},{3,2},{4,5},{5,4},{6,7},{7,6},{8,9},{9,8},{10,11... | collective-permute-start | bytes 1769480 | tf_op jit(solution)/shard_map/ppermute | solution.py:219
  51.8 33.0 %copy-start.25 = (bf16[1,96,1536]{2,1,0:T(8,128)(2,1)S(1)}, bf16[1,96,1536]{2,1,0:T(8,128)(2,1)}, u32[]{:S(2)}) copy-start(bf16[1,96,1536]{2,1,0:T(8,128)(2,1)} %share.1.refs_0_) | copy-start | bytes 884740
  51.9 9.7 %collective-permute-start.5 = (bf16[1,96,1536]{2,1,0:T(8,128)(2,1)}, bf16[1,96,1536]{2,1,0:T(8,128)(2,1)S(1)}, u32[]{:S(2)}, u32[]{:S(2)}) collective-permute-start(bf16[1,96,1536]{2,1,0:T(8,128)(2,1)} %share.1.refs_0_), channel_id=1, source_target_pairs={{0,2},{2,0},{1,3},{3,1},{4,6},{6,4},{5,7},{7,5},{8,10},{10,8},{9,1... | collective-permute-start | bytes 884744 | tf_op jit(solution)/shard_map/ppermute | solution.py:201
  81.3 14.2 %collective-permute-start.19 = (bf16[2,96,1536]{2,1,0:T(8,128)(2,1)}, bf16[2,96,1536]{2,1,0:T(8,128)(2,1)S(1)}, u32[]{:S(2)}, u32[]{:S(2)}) collective-permute-start(bf16[2,96,1536]{2,1,0:T(8,128)(2,1)} %stacked.4.refs_7_), channel_id=1, source_target_pairs={{0,16},{16,0},{1,17},{17,1},{2,18},{18,2},{3,19},{19,3},{4,20},{20... | collective-permute-start | bytes 1769480 | tf_op jit(solution)/shard_map/ppermute | solution.py:201
  83.3 12.2 %collective-permute-start.18 = (bf16[2,96,1536]{2,1,0:T(8,128)(2,1)}, bf16[2,96,1536]{2,1,0:T(8,128)(2,1)S(1)}, u32[]{:S(2)}, u32[]{:S(2)}) collective-permute-start(bf16[2,96,1536]{2,1,0:T(8,128)(2,1)} %stacked.4.refs_7_), channel_id=1, source_target_pairs={{0,1},{1,0},{2,3},{3,2},{4,5},{5,4},{6,7},{7,6},{8,9},{9,8},{10,11... | collective-permute-start | bytes 1769480 | tf_op jit(solution)/shard_map/ppermute | solution.py:201
  84.8 15.9 %collective-permute-start.2 = (bf16[1,96,1536]{2,1,0:T(8,128)(2,1)S(1)}, bf16[1,96,1536]{2,1,0:T(8,128)(2,1)S(1)}, u32[]{:S(2)}, u32[]{:S(2)}) collective-permute-start(bf16[1,96,1536]{2,1,0:T(8,128)(2,1)S(1)} %copy-done.25), channel_id=1, source_target_pairs={{0,8},{4,12},{8,0},{12,4},{1,9},{5,13},{9,1},{13,5},{2,10},{6,14},... | collective-permute-start | bytes 884744 | tf_op jit(solution)/shard_map/ppermute | solution.py:201
  95.5 32.8 %collective-permute-start.20 = (bf16[2,96,1536]{2,1,0:T(8,128)(2,1)S(1)}, bf16[2,96,1536]{2,1,0:T(8,128)(2,1)S(1)}, u32[]{:S(2)}, u32[]{:S(2)}) collective-permute-start(bf16[2,96,1536]{2,1,0:T(8,128)(2,1)S(1)} %collective-permute-done.19.refs_9_), channel_id=1, source_target_pairs={{0,1},{1,0},{2,3},{3,2},{4,5},{5,4},{6,7},{7,6},{8,9},{9,8},{10,11... | collective-permute-start | bytes 1769480 | tf_op jit(solution)/shard_map/ppermute | solution.py:201
  100.7 7.9 %copy-start.26 = (bf16[1,96,1536]{2,1,0:T(8,128)(2,1)}, bf16[1,96,1536]{2,1,0:T(8,128)(2,1)S(1)}, u32[]{:S(2)}) copy-start(bf16[1,96,1536]{2,1,0:T(8,128)(2,1)S(1)} %collective-permute-done.2.refs_0_) | copy-start | bytes 884740
  100.7 7.9 %collective-permute-start.6 = (bf16[1,96,1536]{2,1,0:T(8,128)(2,1)S(1)}, bf16[1,96,1536]{2,1,0:T(8,128)(2,1)S(1)}, u32[]{:S(2)}, u32[]{:S(2)}) collective-permute-start(bf16[1,96,1536]{2,1,0:T(8,128)(2,1)S(1)} %collective-permute-done.2.refs_0_), channel_id=1, source_target_pairs={{0,2},{2,0},{1,3},{3,1},{4,6},{6,4},{5,7},{7,5},{8,10},{10,8},{9,1... | collective-permute-start | bytes 884744 | tf_op jit(solution)/shard_map/ppermute | solution.py:201
  101.9 28.0 %collective-permute-start.3 = (bf16[1,96,1536]{2,1,0:T(8,128)(2,1)S(1)}, bf16[1,96,1536]{2,1,0:T(8,128)(2,1)}, u32[]{:S(2)}, u32[]{:S(2)}) collective-permute-start(bf16[1,96,1536]{2,1,0:T(8,128)(2,1)S(1)} %copy-done.25), channel_id=1, source_target_pairs={{0,4},{4,0},{8,12},{12,8},{1,5},{5,1},{9,13},{13,9},{2,6},{6,2},{1... | collective-permute-start | bytes 884744 | tf_op jit(solution)/shard_map/ppermute | solution.py:201
  128.2 109.9 %copy-start.32 = (s32[1,6]{1,0:T(1,128)S(1)}, s32[1,6]{1,0:T(1,128)}, u32[]{:S(2)}) copy-start(s32[1,6]{1,0:T(1,128)} %param.13) | copy-start | bytes 76
  128.3 114.4 %copy-start = (bf16[192,1536]{1,0:T(8,128)(2,1)S(1)}, bf16[192,1536]{1,0:T(8,128)(2,1)}, u32[]{:S(2)}) copy-start(bf16[192,1536]{1,0:T(8,128)(2,1)} %q.7) | copy-start | bytes 1769476
  128.3 30.3 %collective-permute-start.21 = (bf16[2,96,1536]{2,1,0:T(8,128)(2,1)}, bf16[2,96,1536]{2,1,0:T(8,128)(2,1)}, u32[]{:S(2)}, u32[]{:S(2)}) collective-permute-start(bf16[2,96,1536]{2,1,0:T(8,128)(2,1)} %stacked.5.refs_11_), channel_id=1, source_target_pairs={{0,1},{1,0},{2,3},{3,2},{4,5},{5,4},{6,7},{7,6},{8,9},{9,8},{10,11... | collective-permute-start | bytes 1769480 | tf_op jit(solution)/shard_map/ppermute | solution.py:201
  129.9 8.9 %collective-permute-start.7 = (bf16[1,96,1536]{2,1,0:T(8,128)(2,1)}, bf16[1,96,1536]{2,1,0:T(8,128)(2,1)S(1)}, u32[]{:S(2)}, u32[]{:S(2)}) collective-permute-start(bf16[1,96,1536]{2,1,0:T(8,128)(2,1)} %collective-permute-done.3.refs_0_), channel_id=1, source_target_pairs={{0,2},{2,0},{1,3},{3,1},{4,6},{6,4},{5,7},{7,5},{8,10},{10,8},{9,1... | collective-permute-start | bytes 884744 | tf_op jit(solution)/shard_map/ppermute | solution.py:201
  131.1 29.0 %collective-permute-start.22 = (bf16[2,96,1536]{2,1,0:T(8,128)(2,1)}, bf16[2,96,1536]{2,1,0:T(8,128)(2,1)}, u32[]{:S(2)}, u32[]{:S(2)}) collective-permute-start(bf16[2,96,1536]{2,1,0:T(8,128)(2,1)} %stacked.5.refs_11_), channel_id=1, source_target_pairs={{0,16},{16,0},{1,17},{17,1},{2,18},{18,2},{3,19},{19,3},{4,20},{20... | collective-permute-start | bytes 1769480 | tf_op jit(solution)/shard_map/ppermute | solution.py:201
  158.5 42.5 %copy-start.3 = (bf16[2,96,1536]{2,1,0:T(8,128)(2,1)S(1)}, bf16[2,96,1536]{2,1,0:T(8,128)(2,1)}, u32[]{:S(2)}) copy-start(bf16[2,96,1536]{2,1,0:T(8,128)(2,1)} %stacked.6.refs_15_) | copy-start | bytes 1769476
  158.5 2.7 collective-permute-start.23
  159.4 8.8 %collective-permute-start.4 = (bf16[1,96,1536]{2,1,0:T(8,128)(2,1)}, bf16[1,96,1536]{2,1,0:T(8,128)(2,1)S(1)}, u32[]{:S(2)}, u32[]{:S(2)}) collective-permute-start(bf16[1,96,1536]{2,1,0:T(8,128)(2,1)} %copy-done.26), channel_id=1, source_target_pairs={{0,4},{4,0},{8,12},{12,8},{1,5},{5,1},{9,13},{13,9},{2,6},{6,2},{1... | collective-permute-start | bytes 884744 | tf_op jit(solution)/shard_map/ppermute | solution.py:201
  162.0 39.3 %collective-permute-start.24 = (bf16[2,96,1536]{2,1,0:T(8,128)(2,1)}, bf16[2,96,1536]{2,1,0:T(8,128)(2,1)}, u32[]{:S(2)}, u32[]{:S(2)}) collective-permute-start(bf16[2,96,1536]{2,1,0:T(8,128)(2,1)} %collective-permute-done.22.refs_13_), channel_id=1, source_target_pairs={{0,1},{1,0},{2,3},{3,2},{4,5},{5,4},{6,7},{7,6},{8,9},{9,8},{10,11... | collective-permute-start | bytes 1769480 | tf_op jit(solution)/shard_map/ppermute | solution.py:201
  168.9 7.7 %collective-permute-start.8 = (bf16[1,96,1536]{2,1,0:T(8,128)(2,1)S(1)}, bf16[1,96,1536]{2,1,0:T(8,128)(2,1)S(1)}, u32[]{:S(2)}, u32[]{:S(2)}) collective-permute-start(bf16[1,96,1536]{2,1,0:T(8,128)(2,1)S(1)} %collective-permute-done.4.refs_0_), channel_id=1, source_target_pairs={{0,2},{2,0},{1,3},{3,1},{4,6},{6,4},{5,7},{7,5},{8,10},{10,8},{9,1... | collective-permute-start | bytes 884744 | tf_op jit(solution)/shard_map/ppermute | solution.py:201
  177.3 24.1 %collective-permute-start.9 = (bf16[192,1536]{1,0:T(8,128)(2,1)}, bf16[192,1536]{1,0:T(8,128)(2,1)}, u32[]{:S(2)}, u32[]{:S(2)}) collective-permute-start(bf16[192,1536]{1,0:T(8,128)(2,1)} %get-tuple-element.49.own), channel_id=1, source_target_pairs={{1,2},{2,1},{5,6},{6,5},{9,10},{10,9},{13,14},{14,13},{17,18},{18,... | collective-permute-start | bytes 1769480 | tf_op jit(solution)/shard_map/ppermute | solution.py:219
  201.1 14.3 %collective-permute-start.25 = (bf16[2,96,1536]{2,1,0:T(8,128)(2,1)S(1)}, bf16[2,96,1536]{2,1,0:T(8,128)(2,1)S(1)}, u32[]{:S(2)}, u32[]{:S(2)}) collective-permute-start(bf16[2,96,1536]{2,1,0:T(8,128)(2,1)S(1)} %copy-done.3), channel_id=1, source_target_pairs={{0,16},{16,0},{1,17},{17,1},{2,18},{18,2},{3,19},{19,3},{4,20},{20... | collective-permute-start | bytes 1769480 | tf_op jit(solution)/shard_map/ppermute | solution.py:201
  201.4 14.3 %collective-permute-start.26 = (bf16[2,96,1536]{2,1,0:T(8,128)(2,1)}, bf16[2,96,1536]{2,1,0:T(8,128)(2,1)S(1)}, u32[]{:S(2)}, u32[]{:S(2)}) collective-permute-start(bf16[2,96,1536]{2,1,0:T(8,128)(2,1)} %stacked.7.refs_19_), channel_id=1, source_target_pairs={{0,1},{1,0},{2,3},{3,2},{4,5},{5,4},{6,7},{7,6},{8,9},{9,8},{10,11... | collective-permute-start | bytes 1769480 | tf_op jit(solution)/shard_map/ppermute | solution.py:201
  201.4 16.0 %collective-permute-start.13 = (bf16[48,3072]{1,0:T(8,128)(2,1)}, bf16[48,3072]{1,0:T(8,128)(2,1)S(1)}, u32[]{:S(2)}, u32[]{:S(2)}) collective-permute-start(bf16[48,3072]{1,0:T(8,128)(2,1)} %get-tuple-element.52), channel_id=1, source_target_pairs={{0,2},{1,3},{2,0},{3,1},{4,6},{5,7},{6,4},{7,5},{8,10},{9,11},{10,... | collective-permute-start | bytes 884744 | tf_op jit(solution)/shard_map/ppermute | solution.py:201
  201.8 28.8 %collective-permute-start.10 = (bf16[192,1536]{1,0:T(8,128)(2,1)}, bf16[192,1536]{1,0:T(8,128)(2,1)S(1)}, u32[]{:S(2)}, u32[]{:S(2)}) collective-permute-start(bf16[192,1536]{1,0:T(8,128)(2,1)} %get-tuple-element.49.own), channel_id=1, source_target_pairs={{0,8},{8,0},{1,9},{9,1},{2,10},{10,2},{3,11},{11,3},{4,12},{12,4},... | collective-permute-start | bytes 1769480 | tf_op jit(solution)/shard_map/ppermute | solution.py:219
  204.3 27.0 %collective-permute-start.11 = (bf16[192,1536]{1,0:T(8,128)(2,1)}, bf16[192,1536]{1,0:T(8,128)(2,1)S(1)}, u32[]{:S(2)}, u32[]{:S(2)}) collective-permute-start(bf16[192,1536]{1,0:T(8,128)(2,1)} %get-tuple-element.49.own), channel_id=1, source_target_pairs={{0,4},{4,0},{1,5},{5,1},{2,6},{6,2},{3,7},{7,3},{8,12},{12,8},{9,1... | collective-permute-start | bytes 1769480 | tf_op jit(solution)/shard_map/ppermute | solution.py:219
  215.4 20.9 %collective-permute-start.28 = (bf16[2,96,1536]{2,1,0:T(8,128)(2,1)}, bf16[2,96,1536]{2,1,0:T(8,128)(2,1)}, u32[]{:S(2)}, u32[]{:S(2)}) collective-permute-start(bf16[2,96,1536]{2,1,0:T(8,128)(2,1)} %stacked.7.refs_19_), channel_id=1, source_target_pairs={{0,16},{16,0},{1,17},{17,1},{2,18},{18,2},{3,19},{19,3},{4,20},{20... | collective-permute-start | bytes 1769480 | tf_op jit(solution)/shard_map/ppermute | solution.py:201
  216.5 19.7 %collective-permute-start.27 = (bf16[2,96,1536]{2,1,0:T(8,128)(2,1)S(1)}, bf16[2,96,1536]{2,1,0:T(8,128)(2,1)S(1)}, u32[]{:S(2)}, u32[]{:S(2)}) collective-permute-start(bf16[2,96,1536]{2,1,0:T(8,128)(2,1)S(1)} %collective-permute-done.25.refs_17_), channel_id=1, source_target_pairs={{0,1},{1,0},{2,3},{3,2},{4,5},{5,4},{6,7},{7,6},{8,9},{9,8},{10,11... | collective-permute-start | bytes 1769480 | tf_op jit(solution)/shard_map/ppermute | solution.py:201
  218.1 22.0 %collective-permute-start.14 = (bf16[192,1536]{1,0:T(8,128)(2,1)}, bf16[192,1536]{1,0:T(8,128)(2,1)}, u32[]{:S(2)}, u32[]{:S(2)}) collective-permute-start(bf16[192,1536]{1,0:T(8,128)(2,1)} %get-tuple-element.58.own), channel_id=1, source_target_pairs={{1,2},{2,1},{5,6},{6,5},{9,10},{10,9},{13,14},{14,13},{17,18},{18,... | collective-permute-start | bytes 1769480 | tf_op jit(solution)/shard_map/ppermute | solution.py:219
  231.4 27.7 %collective-permute-start.15 = (bf16[192,1536]{1,0:T(8,128)(2,1)}, bf16[192,1536]{1,0:T(8,128)(2,1)}, u32[]{:S(2)}, u32[]{:S(2)}) collective-permute-start(bf16[192,1536]{1,0:T(8,128)(2,1)} %get-tuple-element.58.own), channel_id=1, source_target_pairs={{0,8},{8,0},{1,9},{9,1},{2,10},{10,2},{3,11},{11,3},{4,12},{12,4},... | collective-permute-start | bytes 1769480 | tf_op jit(solution)/shard_map/ppermute | solution.py:219
  232.3 28.5 %collective-permute-start.16 = (bf16[192,1536]{1,0:T(8,128)(2,1)}, bf16[192,1536]{1,0:T(8,128)(2,1)}, u32[]{:S(2)}, u32[]{:S(2)}) collective-permute-start(bf16[192,1536]{1,0:T(8,128)(2,1)} %get-tuple-element.58.own), channel_id=1, source_target_pairs={{0,4},{4,0},{1,5},{5,1},{2,6},{6,2},{3,7},{7,3},{8,12},{12,8},{9,1... | collective-permute-start | bytes 1769480 | tf_op jit(solution)/shard_map/ppermute | solution.py:219
  237.1 23.7 %collective-permute-start.29 = (bf16[2,96,1536]{2,1,0:T(8,128)(2,1)}, bf16[2,96,1536]{2,1,0:T(8,128)(2,1)}, u32[]{:S(2)}, u32[]{:S(2)}) collective-permute-start(bf16[2,96,1536]{2,1,0:T(8,128)(2,1)} %collective-permute-done.28.refs_21_), channel_id=1, source_target_pairs={{0,1},{1,0},{2,3},{3,2},{4,5},{5,4},{6,7},{7,6},{8,9},{9,8},{10,11... | collective-permute-start | bytes 1769480 | tf_op jit(solution)/shard_map/ppermute | solution.py:201
  240.1 20.7 %collective-permute-start.17 = (bf16[48,3072]{1,0:T(8,128)(2,1)}, bf16[48,3072]{1,0:T(8,128)(2,1)}, u32[]{:S(2)}, u32[]{:S(2)}) collective-permute-start(bf16[48,3072]{1,0:T(8,128)(2,1)} %get-tuple-element.59), channel_id=1, source_target_pairs={{0,3},{1,2},{2,1},{3,0},{4,7},{5,6},{6,5},{7,4},{8,11},{9,10},{10,... | collective-permute-start | bytes 884744 | tf_op jit(solution)/shard_map/ppermute | solution.py:201
  244.8 3.9 %copy-start.20 = (bf16[192,1536]{1,0:T(8,128)(2,1)S(1)}, bf16[192,1536]{1,0:T(8,128)(2,1)}, u32[]{:S(2)}) copy-start(bf16[192,1536]{1,0:T(8,128)(2,1)} %copy-done.19) | copy-start | bytes 1769476
  244.8 3.9 %copy-start.22 = (bf16[192,1536]{1,0:T(8,128)(2,1)S(1)}, bf16[192,1536]{1,0:T(8,128)(2,1)}, u32[]{:S(2)}) copy-start(bf16[192,1536]{1,0:T(8,128)(2,1)} %copy-done.21) | copy-start | bytes 1769476
  248.7 2.7 copy-start.13
  248.8 2.7 copy-start.16
  248.8 12.0 %copy-start.8 = (bf16[2,96,1536]{2,1,0:T(8,128)(2,1)S(1)}, bf16[2,96,1536]{2,1,0:T(8,128)(2,1)}, u32[]{:S(2)}) copy-start(bf16[2,96,1536]{2,1,0:T(8,128)(2,1)} %copy-done.7) | copy-start | bytes 1769476
  248.8 12.0 %copy-start.10 = (bf16[2,96,1536]{2,1,0:T(8,128)(2,1)S(1)}, bf16[2,96,1536]{2,1,0:T(8,128)(2,1)}, u32[]{:S(2)}) copy-start(bf16[2,96,1536]{2,1,0:T(8,128)(2,1)} %copy-done.9) | copy-start | bytes 1769476
  248.8 12.0 %copy-start.12 = (bf16[2,96,1536]{2,1,0:T(8,128)(2,1)S(1)}, bf16[2,96,1536]{2,1,0:T(8,128)(2,1)}, u32[]{:S(2)}) copy-start(bf16[2,96,1536]{2,1,0:T(8,128)(2,1)} %copy-done.11) | copy-start | bytes 1769476
  248.8 12.0 %copy-start.24 = (bf16[48,3072]{1,0:T(8,128)(2,1)S(1)}, bf16[48,3072]{1,0:T(8,128)(2,1)}, u32[]{:S(2)}) copy-start(bf16[48,3072]{1,0:T(8,128)(2,1)} %copy-done.23) | copy-start | bytes 884740
  251.4 9.4 %copy-start.1 = (bf16[2,96,1536]{2,1,0:T(8,128)(2,1)S(1)}, bf16[2,96,1536]{2,1,0:T(8,128)(2,1)}, u32[]{:S(2)}) copy-start(bf16[2,96,1536]{2,1,0:T(8,128)(2,1)} %stacked.4.refs_7_) | copy-start | bytes 1769476
  251.4 9.4 %copy-start.2 = (bf16[2,96,1536]{2,1,0:T(8,128)(2,1)S(1)}, bf16[2,96,1536]{2,1,0:T(8,128)(2,1)}, u32[]{:S(2)}) copy-start(bf16[2,96,1536]{2,1,0:T(8,128)(2,1)} %stacked.5.refs_11_) | copy-start | bytes 1769476
  251.4 9.4 %copy-start.4 = (bf16[2,96,1536]{2,1,0:T(8,128)(2,1)S(1)}, bf16[2,96,1536]{2,1,0:T(8,128)(2,1)}, u32[]{:S(2)}) copy-start(bf16[2,96,1536]{2,1,0:T(8,128)(2,1)} %stacked.7.refs_19_) | copy-start | bytes 1769476
  251.4 9.4 %copy-start.6 = (bf16[2,96,1536]{2,1,0:T(8,128)(2,1)S(1)}, bf16[2,96,1536]{2,1,0:T(8,128)(2,1)}, u32[]{:S(2)}) copy-start(bf16[2,96,1536]{2,1,0:T(8,128)(2,1)} %copy-done.5) | copy-start | bytes 1769476
  (15 other events, 12.3 us)

commit v4 on v3

--- a/solution.py
+++ b/solution.py
@@ -133,7 +133,8 @@
             target = held
         else:
             count = source.shape[0]
-            group, outer, pair, core = (place[i] ^ flip for i, flip in enumerate(flips))
+            group, pair, core, flip = flips
+            outer = place[1] ^ flip
             start = pl.multiple_of(((outer * 2 + pair) * 2 + core) * count, count)
             target = held.at[group, pl.ds(start, count), :]
         copies.append(pltpu.make_async_copy(source, target, sems.at[number]))
@@ -219,43 +220,6 @@
     return lambda block: lax.ppermute(block, TILES, route)
 
 
-def copy_kernel(count, moves, start, *refs):
-    sources, targets, sems = refs[:count], refs[count:-1], refs[-1]
-    copies = []
-    for number, (source, source_at, target, target_at) in enumerate(moves):
-        column, columns, times = source_at
-        column = pl.multiple_of(start[0] * columns, 128) if times else column
-        from_ref = sources[source].at[..., pl.ds(column, columns)]
-        copies.append(pltpu.make_async_copy(from_ref, targets[target].at[target_at], sems.at[number]))
-    for copy in copies:
-        copy.start()
-    for copy in copies:
-        copy.wait()
-
-
-def copied(start, arrays, shapes, moves, name):
-    return pl.pallas_call(
-        functools.partial(copy_kernel, len(arrays), moves),
-        out_shape=[jax.ShapeDtypeStruct(shape, jnp.bfloat16) for shape in shapes],
-        in_specs=[SMEM] + [ANY] * len(arrays),
-        out_specs=[ANY] * len(shapes),
-        scratch_shapes=[pltpu.SemaphoreType.DMA((len(moves),))],
-        cost_estimate=pl.CostEstimate(
-            flops=0, bytes_accessed=4 * sum(math.prod(shape) for shape in shapes), transcendentals=0
-        ),
-        name=name,
-    )(start, *arrays)
-
-
-def stacked(a, b):
-    if a.shape[1] % 16:
-        return jnp.concatenate([a, b])
-    n, rows, columns = a.shape
-    whole = (0, columns, False)
-    moves = ((0, whole, 0, pl.ds(0, n)), (1, whole, 0, pl.ds(n, n)))
-    return copied(jnp.zeros(1, jnp.int32), (a, b), [(2 * n, rows, columns)], moves, "stacked")[0]
-
-
 def neighbour_slots(tile_count, strides, counts):
     slots = []
     for axis, (stride, count) in enumerate(zip(strides, counts)):
@@ -302,10 +266,7 @@
     far_lane, near_lane, x_lane, y_lane, core_lane = (Lane() for _ in range(5))
 
     shard, share = out_weight.shape[0], width // groups
-    group = lax.axis_index("groups").astype(jnp.int32)
-    line = copied(
-        group[None], (out_weight,), [(1, shard, share)], ((0, (0, share, True), 0, 0),), "share"
-    )[0]
+    line = lax.dynamic_slice(out_weight, (0, lax.axis_index("groups") * share), (shard, share))[None]
     line_flips = [0]
     flip = outer // 2
     while flip > 2:
@@ -314,20 +275,11 @@
         flip //= 2
     far = far_lane(swap("outer", 2), line)
     near = near_lane(swap("outer", 1), line)
-    last = near_lane(swap("outer", 1), far)
-    parts = [(line, 0), (far, 2), (near, 1), (last, 3)]
-
-    halves = copied(
-        group[None],
-        (keys, values),
-        [(rows, 2 * columns)] * HALVES,
-        tuple(
-            (source, (half * columns, columns, False), half, (slice(None), pl.ds(source * columns, columns)))
-            for half in range(HALVES)
-            for source in range(2)
-        ),
-        "halves",
-    )
+
+    halves = [
+        jnp.concatenate([x[:, half * columns : (half + 1) * columns] for x in (keys, values)], axis=1)
+        for half in range(HALVES)
+    ]
     block = rows // grid_width
     lines = control.reshape(block // TILE_W, grid_width, TILE_W, width)
     control_sent = [
@@ -336,35 +288,41 @@
     control_parts = [control_sent[0]] + [None] * (grid_width - 1)
     control_parts[1] = core_lane(swap(TILES, 1), control_sent[1])
     early_near = [[None] * len(early) for _ in range(HALVES)]
+    x_done = [[] for _ in range(HALVES)]
     for half in range(HALVES):
-        early_near[half][0] = core_lane(route_of(early[0][2]), halves[half])
-
-    held = []
-    for piece, _ in parts:
-        beside = x_lane(swap("pair", 1), piece)
-        plane = stacked(piece, beside)
-        held.append((plane, y_lane(swap("groups", 1), plane)))
-    order = [(0, 0), (0, 1), (1, 0), (2, 0), (1, 1), (3, 0), (2, 1), (3, 1)]
-    crossed = {at: core_lane(swap("core", 1), held[at[0]][at[1]]) for at in order}
-    weight, moves = [], []
-    for number, (_, outer_flip) in enumerate(parts):
-        for y_flip in range(2):
-            for core_flip in range(2):
-                n = len(line_flips)
-                moves += [
-                    (len(weight), i, (y_flip, line_flips[i % n] ^ outer_flip, i // n, core_flip)) for i in range(2 * n)
-                ]
-                weight.append(crossed[number, y_flip] if core_flip else held[number][y_flip])
+        early_near[half][0] = core_lane(route_of(early[0][2]), halves[half], far, near)
+        for i in range(1, len(early)):
+            early_near[half][i] = x_lane(route_of(early[i][2]), halves[half])
+            x_done[half].append(early_near[half][i])
+        for d in range(2 + half, grid_width, HALVES):
+            control_parts[d] = x_lane(swap(TILES, d), control_sent[d])
+            x_done[half].append(control_parts[d])
+    last = near_lane(swap("outer", 1), far)
 
     late_near = []
     lanes = [far_lane, near_lane]
     for half in range(HALVES):
-        late_near.append([lanes[i % 2](route_of(route), halves[half]) for i, (_, _, route) in enumerate(late)])
-    for half in range(HALVES):
-        for i in range(1, len(early)):
-            early_near[half][i] = x_lane(route_of(early[i][2]), halves[half])
-        for d in range(2 + half, grid_width, HALVES):
-            control_parts[d] = x_lane(swap(TILES, d), control_sent[d])
+        late_near.append(
+            [
+                lanes[i % 2](route_of(route), halves[half], *(x_done[1] if half else []))
+                for i, (_, _, route) in enumerate(late)
+            ]
+        )
+
+    def plane(piece, *others):
+        return lax.all_gather(after(piece, *others) if others else piece, ("groups", "pair", "core"))
+
+    weight = [plane(line)]
+    weight.append(plane(jnp.concatenate([far, near, last]), weight[0], *x_done[0]))
+    steps = [line_flips, [f ^ x for x in (2, 1, 3) for f in line_flips]]
+    moves = [
+        (number, ((g * pair + p) * cores + c, i), (g, p, c, flip))
+        for number, flips in enumerate(steps)
+        for g in range(groups)
+        for p in range(pair)
+        for c in range(cores)
+        for i, flip in enumerate(flips)
+    ]
 
     states = [attend(early_active, queries, half * heads, halves[half], early_near[half]) for half in range(HALVES)]
     ready = [close(late_active, queries, half * heads, states[half], late_near[half]) for half in range(HALVES - 1)]
@@ -393,12 +351,11 @@
 
 
 def in_order(weight, moves, place, sizes):
-    blocks = {flips: weight[piece][index] for piece, index, flips in moves}
-    whole = jnp.stack([blocks[flips] for flips in sorted(blocks)])
+    blocks = {(g, flip, p, c): weight[piece][index] for piece, index, (g, p, c, flip) in moves}
+    whole = jnp.stack([blocks[at] for at in sorted(blocks)])
     shard, columns = whole.shape[1:]
     whole = whole.reshape(sizes + (shard, columns))
-    for axis, size in enumerate(sizes):
-        whole = jnp.take(whole, jnp.arange(size, dtype=jnp.int32) ^ place[axis], axis=axis)
+    whole = jnp.take(whole, jnp.arange(sizes[1], dtype=jnp.int32) ^ place[1], axis=1)
     return whole.reshape(sizes[0], -1, columns)
 
 

time: 270 us -> 133 us (0.49)
  Pallas kernels: 142 us -> 17.1 us
  starting transfers between devices: 35.9 us -> 17.8 us
  waiting for transfers between devices: 73.2 us -> 59.1 us
  between operations: 2.95 us -> 16.3 us
  local copies, waits for them, and re-layouts: 15.2 us -> 18.6 us
    pallas_call x6 -> x0, Pallas kernels: 123 us -> none  [copied(): pl.pallas_call(functools.partial(copy_kernel, len(arrays), moves), out_sh...]
    ppermute x22 -> x6, waiting for transfers between devices: 55.5 us -> 15.6 us  [flipped(): lax.ppermute(block, axis, [(i, i ^ flip) for i in range(lax.axis_size(axi...]
    ppermute x8, waiting for transfers between devices: 17.7 us -> 36.6 us  [route_of(): return lambda block: lax.ppermute(block, TILES, route)]
    ppermute x22 -> x6, starting transfers between devices: 20.6 us -> 6.19 us  [flipped(): lax.ppermute(block, axis, [(i, i ^ flip) for i in range(lax.axis_size(axi...]
    all_gather x0 -> x2, waiting for transfers between devices: none -> 6.86 us  [plane(): lax.all_gather(after(piece, *others) if others else piece, ('groups', 'pa...]
    ppermute x8, starting transfers between devices: 15.4 us -> 11.5 us  [route_of(): return lambda block: lax.ppermute(block, TILES, route)]
    unnamed x66 -> x54, local copies, waits for them, and re-layouts: 12.4 us -> 15.3 us
  transfers between devices with their start and end apart: 30 -> 16, of which waited for: 13 -> 8; matrix products, arithmetic and copies ran while one was open for 0% -> 4% of each run, Pallas kernels for 50% -> 7%
where the time goes in v4:
time: 133 us; the launch traced here: 131 us
  waiting for transfers between devices  59.1 us (44%)
  local copies, waits for them, and re-layouts  18.6 us (14%)
  starting transfers between devices  17.8 us (13%)
  Pallas kernels  17.1 us (13%)
  between operations  16.3 us (12%)
  other arithmetic  2.29 us (2%)
    ppermute x8, waiting for transfers between devices, route_of(): return lambda block: lax.ppermute(block, TILES, route)  36.6 us
    ppermute x6, waiting for transfers between devices, flipped(): lax.ppermute(block, axis, [(i, i ^ flip) for i in range(lax.axis_size(axi...  15.6 us
    unnamed x54, local copies, waits for them, and re-layouts  15.3 us
    ppermute x8, starting transfers between devices, route_of(): return lambda block: lax.ppermute(block, TILES, route)  11.5 us
    pallas_call x1, Pallas kernels, finish(): pl.pallas_call(functools.partial(finish_kernel, len(near), len(control),...  8.11 us
    pallas_call x2, Pallas kernels, attend(): pl.pallas_call(functools.partial(attend_kernel, len(near), first_head), o...  7.35 us
    all_gather x2, waiting for transfers between devices, plane(): lax.all_gather(after(piece, *others) if others else piece, ('groups', 'pa...  6.86 us
    ppermute x6, starting transfers between devices, flipped(): lax.ppermute(block, axis, [(i, i ^ flip) for i in range(lax.axis_size(axi...  6.19 us
  transfers between devices with their start and end apart: 16, of which 8 were waited for; matrix products, arithmetic and copies ran while one was open for 4% of the time, Pallas kernels for 7%

profile of v4, /device:TPU:1, one launch (start us, length us, event | category | flops | bytes accessed | tf_op | source)
XLA Modules:
  0.0 131.2 jit_solution(10067845628798531235)
XLA Ops:
  6.6 1.0 copy-done
  7.6 0.7 constant_dynamic-slice_fusion
  8.3 0.0 all-gather.5.cloned.1.call-update
  8.4 0.0 all-gather.7.cloned.1.call-start
  8.4 0.7 fusion.2
  9.1 3.1 %collective-permute-start.1 = (bf16[1,96,1536]{2,1,0:T(8,128)(2,1)}, bf16[1,96,1536]{2,1,0:T(8,128)(2,1)}, u32[]{:S(2)}, u32[]{:S(2)}) collective-permute-start(bf16[1,96,1536]{2,1,0:T(8,128)(2,1)} %fusion.2), channel_id=1, source_target_pairs={{0,8},{4,12},{8,0},{12,4},{1,9},{5,13},{9,1},{13,5},{2,10},{6,14},... | collective-permute-start | bytes 884744 | tf_op jit(solution)/shard_map/ppermute | solution.py:202
  12.3 1.3 collective-permute-start.2
  13.6 0.1 fusion
  13.7 4.4 %collective-permute-start.4 = (bf16[192,1536]{1,0:T(8,128)(2,1)S(1)}, bf16[192,1536]{1,0:T(8,128)(2,1)S(1)}, u32[]{:S(2)}, u32[]{:S(2)}) collective-permute-start(bf16[192,1536]{1,0:T(8,128)(2,1)S(1)} %pad_maximum_fusion.1.own), channel_id=1, source_target_pairs={{1,2},{2,1},{5,6},{6,5},{9,10},{10,9},{13,14},{14,13},{17,18},{18,... | collective-permute-start | bytes 1769480 | tf_op jit(solution)/shard_map/ppermute | solution.py:220
  18.1 7.5 %collective-permute-done.1 = bf16[1,96,1536]{2,1,0:T(8,128)(2,1)} collective-permute-done((bf16[1,96,1536]{2,1,0:T(8,128)(2,1)}, bf16[1,96,1536]{2,1,0:T(8,128)(2,1)}, u32[]{:S(2)}, u32[]{:S(2)}) %collective-permute-start.1) | collective-permute-done | bytes 294944 | tf_op jit(solution)/shard_map/ppermute | solution.py:202
  25.7 1.1 collective-permute-start.6
  26.8 1.0 dynamic-slice_bitcast_fusion
  27.9 0.9 collective-permute-done.4.refs_1_
  28.8 0.3 collective-permute-start.9
  29.1 3.8 %collective-permute-done.6 = bf16[1,96,1536]{2,1,0:T(8,128)(2,1)S(1)} collective-permute-done((bf16[1,96,1536]{2,1,0:T(8,128)(2,1)}, bf16[1,96,1536]{2,1,0:T(8,128)(2,1)S(1)}, u32[]{:S(2)}, u32[]{:S(2)}) %collective-permute-start.6) | collective-permute-done | bytes 294944 | tf_op jit(solution)/shard_map/ppermute | solution.py:202
  32.9 2.1 %pad_maximum_fusion = bf16[3,96,1536]{2,1,0:T(8,128)(2,1)} fusion(bf16[1,96,1536]{2,1,0:T(8,128)(2,1)S(1)} %collective-permute-done.6, bf16[1,96,1536]{2,1,0:T(8,128)(2,1)} %collective-permute-done.2, bf16[1,96,1536]{2,1,0:T(8,128)(2,1)} %collective-permute-done.1), kind=kLoop, calls=%fused_computation | loop fusion | flops 884736 | bytes 1769472 | tf_op jit(solution)/shard_map/concatenate | solution.py:316
  35.0 4.2 %collective-permute-done.9.refs_5_ = bf16[48,3072]{1,0:T(8,128)(2,1)S(1)} collective-permute-done((bf16[48,3072]{1,0:T(8,128)(2,1)}, bf16[48,3072]{1,0:T(8,128)(2,1)S(1)}, u32[]{:S(2)}, u32[]{:S(2)}) %collective-permute-start.9) | collective-permute-done | bytes 294944 | tf_op jit(solution)/shard_map/ppermute | solution.py:202
  39.2 6.9 %all-gather.5.cloned.1.call-done = bf16[768,1536]{1,0:T(8,128)(2,1)} async-done(((bf16[96,1536]{1,0:T(8,128)(2,1)}), bf16[768,1536]{1,0:T(8,128)(2,1)}) %all-gather.5.cloned.1.call-update) | async-done | bytes 2359312 | tf_op jit(solution)/shard_map/all_gather | solution.py:313
  46.1 0.3 collective-permute-start
  46.4 2.3 %collective-permute-start.10 = (bf16[192,1536]{1,0:T(8,128)(2,1)S(1)}, bf16[192,1536]{1,0:T(8,128)(2,1)S(1)}, u32[]{:S(2)}, u32[]{:S(2)}) collective-permute-start(bf16[192,1536]{1,0:T(8,128)(2,1)S(1)} %pad_maximum_fusion.2.own), channel_id=1, source_target_pairs={{1,2},{2,1},{5,6},{6,5},{9,10},{10,9},{13,14},{14,13},{17,18},{18,... | collective-permute-start | bytes 1769480 | tf_op jit(solution)/shard_map/ppermute | solution.py:220
  48.8 0.7 copy-done.19
  49.5 3.1 %collective-permute-start.5 = (bf16[192,1536]{1,0:T(8,128)(2,1)S(1)}, bf16[192,1536]{1,0:T(8,128)(2,1)S(1)}, u32[]{:S(2)}, u32[]{:S(2)}) collective-permute-start(bf16[192,1536]{1,0:T(8,128)(2,1)S(1)} %pad_maximum_fusion.1.own), channel_id=1, source_target_pairs={{0,8},{8,0},{1,9},{9,1},{2,10},{10,2},{3,11},{11,3},{4,12},{12,4},... | collective-permute-start | bytes 1769480 | tf_op jit(solution)/shard_map/ppermute | solution.py:220
  52.6 6.1 %collective-permute-done.10.refs_1_ = bf16[192,1536]{1,0:T(8,128)(2,1)S(1)} collective-permute-done((bf16[192,1536]{1,0:T(8,128)(2,1)S(1)}, bf16[192,1536]{1,0:T(8,128)(2,1)S(1)}, u32[]{:S(2)}, u32[]{:S(2)}) %collective-permute-start.10) | collective-permute-done | bytes 589856 | tf_op jit(solution)/shard_map/ppermute | solution.py:220
  58.7 0.8 copy-done.11
  59.5 19.3 %collective-permute-done.5.refs_0_ = bf16[192,1536]{1,0:T(8,128)(2,1)S(1)} collective-permute-done((bf16[192,1536]{1,0:T(8,128)(2,1)S(1)}, bf16[192,1536]{1,0:T(8,128)(2,1)S(1)}, u32[]{:S(2)}, u32[]{:S(2)}) %collective-permute-start.5) | collective-permute-done | bytes 589856 | tf_op jit(solution)/shard_map/ppermute | solution.py:220
  78.8 0.9 copy-done.13
  79.7 0.7 copy-done.21
  80.4 0.8 copy-done.15
  81.3 1.7 %collective-permute-start.13 = (bf16[192,1536]{1,0:T(8,128)(2,1)S(1)}, bf16[192,1536]{1,0:T(8,128)(2,1)}, u32[]{:S(2)}, u32[]{:S(2)}) collective-permute-start(bf16[192,1536]{1,0:T(8,128)(2,1)S(1)} %pad_maximum_fusion.2.own), channel_id=1, source_target_pairs={{0,4},{4,0},{1,5},{5,1},{2,6},{6,2},{3,7},{7,3},{8,12},{12,8},{9,1... | collective-permute-start | bytes 1769480 | tf_op jit(solution)/shard_map/ppermute | solution.py:220
  83.0 0.7 constant_dynamic-slice_fusion.2
  86.3 0.1 stack.49.place
  86.4 0.1 add_convert_fusion.active
  86.5 0.1 add_convert_fusion.1.active
  86.6 3.4 %attend.2 = (f32[192,768]{1,0:T(8,128)S(1)}, f32[192,768]{1,0:T(8,128)S(1)}, f32[192,768]{1,0:T(8,128)S(1)}) custom-call(s32[2]{0:T(128)S(1)} %add_convert_fusion.1.active, bf16[192,1536]{1,0:T(8,128)(2,1)S(1)} %copy-done.1, bf16[192,1536]{1,0:T(8,128)(2,1)S(1)} %pad_maximum_fusion.1.own, bf16[192,1536]{1,0:T(8,128)(2,1)S(1)} %collective-permute-done.3.refs_0_, ...), custom_call_target="tpu_custom_call" | custom-call | flops 509607936 | bytes 3538944 | tf_op jit(solution)/shard_map/attend/pallas_call | solution.py:80
  90.0 1.7 %close.1.ready = bf16[192,768]{1,0:T(8,128)(2,1)S(1)} custom-call(s32[2]{0:T(128)S(1)} %add_convert_fusion.active, bf16[192,1536]{1,0:T(8,128)(2,1)S(1)} %copy-done.1, f32[192,768]{1,0:T(8,128)S(1)} %get-tuple-element.23.part, f32[192,768]{1,0:T(8,128)S(1)} %get-tuple-element.24.total, f32[192,768]{1,0:T(8,128)S(1)} %get-tuple-element.25.peak, ...), custom_call_target="tpu_custom_call" | custom-call | flops 339738624 | bytes 3538944 | tf_op jit(solution)/shard_map/close/pallas_call | solution.py:106
  91.7 4.0 %attend.3 = (f32[192,768]{1,0:T(8,128)S(1)}, f32[192,768]{1,0:T(8,128)S(1)}, f32[192,768]{1,0:T(8,128)S(1)}) custom-call(s32[2]{0:T(128)S(1)} %add_convert_fusion.1.active, bf16[192,1536]{1,0:T(8,128)(2,1)S(1)} %copy-done.1, bf16[192,1536]{1,0:T(8,128)(2,1)S(1)} %pad_maximum_fusion.2.own, bf16[192,1536]{1,0:T(8,128)(2,1)} %collective-permute-done.8.refs_0_, ...), custom_call_target="tpu_custom_call" | custom-call | flops 509607936 | bytes 3538944 | tf_op jit(solution)/shard_map/attend/pallas_call | solution.py:80
  95.7 0.8 copy-done.5
  96.5 0.8 copy-done.7
  97.3 0.8 copy-done.9
  98.2 10.3 %collective-permute-done.12.refs_0_ = bf16[192,1536]{1,0:T(8,128)(2,1)} collective-permute-done((bf16[192,1536]{1,0:T(8,128)(2,1)S(1)}, bf16[192,1536]{1,0:T(8,128)(2,1)}, u32[]{:S(2)}, u32[]{:S(2)}) %collective-permute-start.12) | collective-permute-done | bytes 589856 | tf_op jit(solution)/shard_map/ppermute | solution.py:220
  108.5 1.7 %copy-done.2 = bf16[768,1536]{1,0:T(8,128)(2,1)S(1)} copy-done((bf16[768,1536]{1,0:T(8,128)(2,1)S(1)}, bf16[768,1536]{1,0:T(8,128)(2,1)}, u32[]{:S(2)}) %copy-start.2) | copy-done | bytes 2359320
  110.1 1.1 copy-done.6
  111.2 1.1 copy-done.8
  112.3 1.1 copy-done.10
  113.3 1.0 copy-done.18
  114.3 1.0 copy-done.20
  115.3 1.0 copy-done.22
  116.2 8.1 %finish.1 = bf16[192,3072]{1,0:T(8,128)(2,1)} custom-call(s32[5]{0:T(128)S(1)} %stack.49.place, s32[2]{0:T(128)S(1)} %add_convert_fusion.active, bf16[192,1536]{1,0:T(8,128)(2,1)S(1)} %copy-done.1, bf16[192,768]{1,0:T(8,128)(2,1)S(1)} %close.1.ready, f32[192,768]{1,0:T(8,128)S(1)} %copy-done.6, f32[192,768]{1,0:T(8,128)S(1)} %copy-done.8, ...), custom_call_target="tpu_custom_call" | custom-call | flops 1811939328 | bytes 12976128 | tf_op jit(solution)/shard_map/finish/pallas_call | solution.py:177
  (55 shorter events, 0.2 us)
Async XLA Ops:
  6.5 1.1 copy-start
  6.5 7.0 %copy-start.24 = (bf16[192,1536]{1,0:T(8,128)(2,1)S(1)}, bf16[192,1536]{1,0:T(8,128)(2,1)}, u32[]{:S(2)}) copy-start(bf16[192,1536]{1,0:T(8,128)(2,1)} %param.9) | copy-start | bytes 1769476
  6.5 7.0 %copy-start.25 = (bf16[192,1536]{1,0:T(8,128)(2,1)S(1)}, bf16[192,1536]{1,0:T(8,128)(2,1)}, u32[]{:S(2)}) copy-start(bf16[192,1536]{1,0:T(8,128)(2,1)} %param.10) | copy-start | bytes 1769476
  6.5 39.5 %all-gather.5.cloned.1.call-start = ((), (), s32[]{:S(2)}) async-start(), calls=%async_computation | async-start | bytes 2654208 | tf_op jit(solution)/shard_map/all_gather | solution.py:313
  8.4 100.1 %all-gather.7.cloned.1.call-start = ((), (), s32[]{:S(2)}) async-start(), calls=%async_computation.1 | async-start | bytes 7962624 | tf_op jit(solution)/shard_map/all_gather | solution.py:313
  9.1 16.6 %collective-permute-start.1 = (bf16[1,96,1536]{2,1,0:T(8,128)(2,1)}, bf16[1,96,1536]{2,1,0:T(8,128)(2,1)}, u32[]{:S(2)}, u32[]{:S(2)}) collective-permute-start(bf16[1,96,1536]{2,1,0:T(8,128)(2,1)} %fusion.2), channel_id=1, source_target_pairs={{0,8},{4,12},{8,0},{12,4},{1,9},{5,13},{9,1},{13,5},{2,10},{6,14},... | collective-permute-start | bytes 884744 | tf_op jit(solution)/shard_map/ppermute | solution.py:202
  12.3 13.4 %collective-permute-start.2 = (bf16[1,96,1536]{2,1,0:T(8,128)(2,1)}, bf16[1,96,1536]{2,1,0:T(8,128)(2,1)}, u32[]{:S(2)}, u32[]{:S(2)}) collective-permute-start(bf16[1,96,1536]{2,1,0:T(8,128)(2,1)} %fusion.2), channel_id=1, source_target_pairs={{0,4},{4,0},{8,12},{12,8},{1,5},{5,1},{9,13},{13,9},{2,6},{6,2},{1... | collective-permute-start | bytes 884744 | tf_op jit(solution)/shard_map/ppermute | solution.py:202
  13.7 13.2 %copy-start.23 = (bf16[192,3072]{1,0:T(8,128)(2,1)S(1)}, bf16[192,3072]{1,0:T(8,128)(2,1)}, u32[]{:S(2)}) copy-start(bf16[192,3072]{1,0:T(8,128)(2,1)} %param.11) | copy-start | bytes 3538948
  13.7 15.1 %collective-permute-start.4 = (bf16[192,1536]{1,0:T(8,128)(2,1)S(1)}, bf16[192,1536]{1,0:T(8,128)(2,1)S(1)}, u32[]{:S(2)}, u32[]{:S(2)}) collective-permute-start(bf16[192,1536]{1,0:T(8,128)(2,1)S(1)} %pad_maximum_fusion.1.own), channel_id=1, source_target_pairs={{1,2},{2,1},{5,6},{6,5},{9,10},{10,9},{13,14},{14,13},{17,18},{18,... | collective-permute-start | bytes 1769480 | tf_op jit(solution)/shard_map/ppermute | solution.py:220
  25.7 7.2 %collective-permute-start.6 = (bf16[1,96,1536]{2,1,0:T(8,128)(2,1)}, bf16[1,96,1536]{2,1,0:T(8,128)(2,1)S(1)}, u32[]{:S(2)}, u32[]{:S(2)}) collective-permute-start(bf16[1,96,1536]{2,1,0:T(8,128)(2,1)} %collective-permute-done.1), channel_id=1, source_target_pairs={{0,4},{4,0},{8,12},{12,8},{1,5},{5,1},{9,13},{13,9},{2,6},{6,2},{1... | collective-permute-start | bytes 884744 | tf_op jit(solution)/shard_map/ppermute | solution.py:202
  28.8 10.3 %collective-permute-start.9 = (bf16[48,3072]{1,0:T(8,128)(2,1)}, bf16[48,3072]{1,0:T(8,128)(2,1)S(1)}, u32[]{:S(2)}, u32[]{:S(2)}) collective-permute-start(bf16[48,3072]{1,0:T(8,128)(2,1)} %get-tuple-element.30), channel_id=1, source_target_pairs={{0,2},{1,3},{2,0},{3,1},{4,6},{5,7},{6,4},{7,5},{8,10},{9,11},{10,... | collective-permute-start | bytes 884744 | tf_op jit(solution)/shard_map/ppermute | solution.py:202
  35.0 48.0 %copy-start.26 = (s32[1,6]{1,0:T(1,128)S(1)}, s32[1,6]{1,0:T(1,128)}, u32[]{:S(2)}) copy-start(s32[1,6]{1,0:T(1,128)} %param.13) | copy-start | bytes 76
  35.0 51.5 %copy-start.1 = (bf16[192,1536]{1,0:T(8,128)(2,1)S(1)}, bf16[192,1536]{1,0:T(8,128)(2,1)}, u32[]{:S(2)}) copy-start(bf16[192,1536]{1,0:T(8,128)(2,1)} %q.7) | copy-start | bytes 1769476
  39.2 7.2 %copy-start.17 = (bf16[48,3072]{1,0:T(8,128)(2,1)}, bf16[48,3072]{1,0:T(8,128)(2,1)S(1)}, u32[]{:S(2)}) copy-start(bf16[48,3072]{1,0:T(8,128)(2,1)S(1)} %collective-permute-done.9.refs_5_) | copy-start | bytes 884740
  46.1 2.7 %collective-permute-start = (bf16[48,3072]{1,0:T(8,128)(2,1)}, bf16[48,3072]{1,0:T(8,128)(2,1)S(1)}, u32[]{:S(2)}, u32[]{:S(2)}) collective-permute-start(bf16[48,3072]{1,0:T(8,128)(2,1)} %get-tuple-element.42), channel_id=1, source_target_pairs={{0,1},{1,0},{2,3},{3,2},{4,5},{5,4},{6,7},{7,6},{8,9},{9,8},{10,11... | collective-permute-start | bytes 884744 | tf_op jit(solution)/shard_map/ppermute | solution.py:202
  46.4 12.2 %collective-permute-start.10 = (bf16[192,1536]{1,0:T(8,128)(2,1)S(1)}, bf16[192,1536]{1,0:T(8,128)(2,1)S(1)}, u32[]{:S(2)}, u32[]{:S(2)}) collective-permute-start(bf16[192,1536]{1,0:T(8,128)(2,1)S(1)} %pad_maximum_fusion.2.own), channel_id=1, source_target_pairs={{1,2},{2,1},{5,6},{6,5},{9,10},{10,9},{13,14},{14,13},{17,18},{18,... | collective-permute-start | bytes 1769480 | tf_op jit(solution)/shard_map/ppermute | solution.py:220
  48.8 0.7 copy-start.19
  49.5 10.0 %collective-permute-start.3 = (bf16[192,1536]{1,0:T(8,128)(2,1)S(1)}, bf16[192,1536]{1,0:T(8,128)(2,1)S(1)}, u32[]{:S(2)}, u32[]{:S(2)}) collective-permute-start(bf16[192,1536]{1,0:T(8,128)(2,1)S(1)} %pad_maximum_fusion.1.own), channel_id=1, source_target_pairs={{0,1},{1,0},{2,3},{3,2},{4,5},{5,4},{6,7},{7,6},{8,9},{9,8},{10,11... | collective-permute-start | bytes 1769480 | tf_op jit(solution)/shard_map/ppermute | solution.py:220
  49.5 29.3 %collective-permute-start.5 = (bf16[192,1536]{1,0:T(8,128)(2,1)S(1)}, bf16[192,1536]{1,0:T(8,128)(2,1)S(1)}, u32[]{:S(2)}, u32[]{:S(2)}) collective-permute-start(bf16[192,1536]{1,0:T(8,128)(2,1)S(1)} %pad_maximum_fusion.1.own), channel_id=1, source_target_pairs={{0,8},{8,0},{1,9},{9,1},{2,10},{10,2},{3,11},{11,3},{4,12},{12,4},... | collective-permute-start | bytes 1769480 | tf_op jit(solution)/shard_map/ppermute | solution.py:220
  52.6 27.8 %collective-permute-start.7 = (bf16[192,1536]{1,0:T(8,128)(2,1)S(1)}, bf16[192,1536]{1,0:T(8,128)(2,1)S(1)}, u32[]{:S(2)}, u32[]{:S(2)}) collective-permute-start(bf16[192,1536]{1,0:T(8,128)(2,1)S(1)} %pad_maximum_fusion.1.own), channel_id=1, source_target_pairs={{0,4},{4,0},{1,5},{5,1},{2,6},{6,2},{3,7},{7,3},{8,12},{12,8},{9,1... | collective-permute-start | bytes 1769480 | tf_op jit(solution)/shard_map/ppermute | solution.py:220
  58.7 0.8 copy-start.11
  59.5 20.2 %collective-permute-start.11 = (bf16[48,3072]{1,0:T(8,128)(2,1)}, bf16[48,3072]{1,0:T(8,128)(2,1)S(1)}, u32[]{:S(2)}, u32[]{:S(2)}) collective-permute-start(bf16[48,3072]{1,0:T(8,128)(2,1)} %get-tuple-element.35), channel_id=1, source_target_pairs={{0,3},{1,2},{2,1},{3,0},{4,7},{5,6},{6,5},{7,4},{8,11},{9,10},{10,... | collective-permute-start | bytes 884744 | tf_op jit(solution)/shard_map/ppermute | solution.py:202
  59.5 32.2 %collective-permute-start.8 = (bf16[192,1536]{1,0:T(8,128)(2,1)S(1)}, bf16[192,1536]{1,0:T(8,128)(2,1)}, u32[]{:S(2)}, u32[]{:S(2)}) collective-permute-start(bf16[192,1536]{1,0:T(8,128)(2,1)S(1)} %pad_maximum_fusion.2.own), channel_id=1, source_target_pairs={{0,1},{1,0},{2,3},{3,2},{4,5},{5,4},{6,7},{7,6},{8,9},{9,8},{10,11... | collective-permute-start | bytes 1769480 | tf_op jit(solution)/shard_map/ppermute | solution.py:220
  78.8 0.9 copy-start.13
  79.7 0.7 copy-start.21
  80.4 28.1 %collective-permute-start.12 = (bf16[192,1536]{1,0:T(8,128)(2,1)S(1)}, bf16[192,1536]{1,0:T(8,128)(2,1)}, u32[]{:S(2)}, u32[]{:S(2)}) collective-permute-start(bf16[192,1536]{1,0:T(8,128)(2,1)S(1)} %pad_maximum_fusion.2.own), channel_id=1, source_target_pairs={{0,8},{8,0},{1,9},{9,1},{2,10},{10,2},{3,11},{11,3},{4,12},{12,4},... | collective-permute-start | bytes 1769480 | tf_op jit(solution)/shard_map/ppermute | solution.py:220
  80.4 0.9 copy-start.15
  81.3 27.2 %collective-permute-start.13 = (bf16[192,1536]{1,0:T(8,128)(2,1)S(1)}, bf16[192,1536]{1,0:T(8,128)(2,1)}, u32[]{:S(2)}, u32[]{:S(2)}) collective-permute-start(bf16[192,1536]{1,0:T(8,128)(2,1)S(1)} %pad_maximum_fusion.2.own), channel_id=1, source_target_pairs={{0,4},{4,0},{1,5},{5,1},{2,6},{6,2},{3,7},{7,3},{8,12},{12,8},{9,1... | collective-permute-start | bytes 1769480 | tf_op jit(solution)/shard_map/ppermute | solution.py:220
  86.5 3.4 %copy-start.14 = (bf16[192,1536]{1,0:T(8,128)(2,1)S(1)}, bf16[192,1536]{1,0:T(8,128)(2,1)}, u32[]{:S(2)}) copy-start(bf16[192,1536]{1,0:T(8,128)(2,1)} %copy-done.13) | copy-start | bytes 1769476
  86.6 3.4 %copy-start.16 = (bf16[192,1536]{1,0:T(8,128)(2,1)S(1)}, bf16[192,1536]{1,0:T(8,128)(2,1)}, u32[]{:S(2)}) copy-start(bf16[192,1536]{1,0:T(8,128)(2,1)} %copy-done.15) | copy-start | bytes 1769476
  89.9 1.7 %copy-start.12 = (bf16[192,1536]{1,0:T(8,128)(2,1)S(1)}, bf16[192,1536]{1,0:T(8,128)(2,1)}, u32[]{:S(2)}) copy-start(bf16[192,1536]{1,0:T(8,128)(2,1)} %copy-done.11) | copy-start | bytes 1769476
  91.6 16.8 %copy-start.3 = (bf16[192,3072]{1,0:T(8,128)(2,1)S(1)}, bf16[192,3072]{1,0:T(8,128)(2,1)}, u32[]{:S(2)}) copy-start(bf16[192,3072]{1,0:T(8,128)(2,1)} %refs_2_.1) | copy-start | bytes 3538948
  91.6 16.8 %copy-start.4 = (bf16[48,3072]{1,0:T(8,128)(2,1)S(1)}, bf16[48,3072]{1,0:T(8,128)(2,1)}, u32[]{:S(2)}) copy-start(bf16[48,3072]{1,0:T(8,128)(2,1)} %get-tuple-element.39.refs_3_) | copy-start | bytes 884740
  95.7 0.8 copy-start.5
  96.5 0.8 copy-start.7
  97.3 0.9 copy-start.9
  108.5 1.7 %copy-start.2 = (bf16[768,1536]{1,0:T(8,128)(2,1)S(1)}, bf16[768,1536]{1,0:T(8,128)(2,1)}, u32[]{:S(2)}) copy-start(bf16[768,1536]{1,0:T(8,128)(2,1)} %all-gather.5.cloned.1.call-done) | copy-start | bytes 7077892
  110.1 1.1 copy-start.6
  111.2 1.1 copy-start.8
  112.3 1.1 copy-start.10
  113.3 1.0 copy-start.18
  114.3 1.0 copy-start.20
  115.3 1.0 copy-start.22
Sparse Core Ops, SparseCore 0:
  9.2 36.7 all-gather.4
  47.9 53.7 all-gather.6

commit v5 on v4

v5 whole, which is shorter than its diff:
```python
import functools
import math

import jax
import jax.numpy as jnp
from jax import lax
from jax.experimental import pallas as pl
from jax.experimental.pallas import tpu as pltpu
from jax.sharding import Mesh
from jax.sharding import PartitionSpec as P

HEAD_DIM = 128
TILE_W = 8
CHUNKS = (2, 5, 3, 2)
SCALE = HEAD_DIM**-0.5 * math.log2(math.e)
TILES = ("outer", "pair", "core")
VMEM_LIMIT = 24 * 1024 * 1024
SMEM = pl.BlockSpec(memory_space=pltpu.SMEM)
ANY = pl.BlockSpec(memory_space=pl.ANY)


def after(x, *others):
    return lax.optimization_barrier((x, *others))[0] if others else x


def head_part(q, k, v):
    scores = lax.dot_general(q, k, (((1,), (1,)), ((), ())), preferred_element_type=jnp.float32)
    peak = jnp.max(scores, axis=1, keepdims=True)
    weights = jnp.exp2((scores - peak) * SCALE).astype(jnp.bfloat16)
    ones = jnp.ones((v.shape[0], HEAD_DIM), jnp.bfloat16)
    both = jnp.dot(weights, jnp.concatenate([v, ones], axis=1), preferred_element_type=jnp.float32)
    return both[:, :HEAD_DIM], both[:, HEAD_DIM:], jnp.broadcast_to(peak, v.shape)


def merge(old, new):
    part, total, peak = old
    part_new, total_new, peak_new = new
    top = jnp.maximum(peak, peak_new)
    f_old = jnp.exp2((peak - top) * SCALE)
    f_new = jnp.exp2((peak_new - top) * SCALE)
    return f_old * part + f_new * part_new, f_old * total + f_new * total_new, top


def columns_of(h):
    return pl.ds(h * HEAD_DIM, HEAD_DIM)


def fold(state, active, q, k, v):
    @pl.when(active == 1)
    def _():
        for h in range(q.shape[1] // HEAD_DIM):
            at = columns_of(h)
            new = head_part(q[:, at], k[:, at], v[:, at])
            for r, x in zip(state, merge(tuple(r[:, at] for r in state), new)):
                r[:, at] = x


class Fetch:
    def __init__(self, sems):
        self.sems, self.count = sems, 0

    def __call__(self, source, target):
        copy = pltpu.make_async_copy(source, target, self.sems.at[self.count])
        self.count += 1
        copy.start()
        return copy


def attend_kernel(first, slots, active, q, *refs):
    kv, (part, stats), scratch = refs[: 2 * slots + 2], refs[2 * slots + 2 : 2 * slots + 4], refs[2 * slots + 4 :]
    q_v, kv_v, total_v, peak_v, part_v, stats_v, sems = (*scratch[:1], scratch[1 : 2 * slots + 3], *scratch[2 * slots + 3 :])
    fetch = Fetch(sems)
    at = pl.ds(first * HEAD_DIM, q_v.shape[1])
    copies = [fetch(source.at[:, at], target) for source, target in zip((q, *kv), (q_v, *kv_v))]
    for copy in copies[:3]:
        copy.wait()
    state = (part_v, total_v, peak_v)
    heads = q_v.shape[1] // HEAD_DIM
    for h in range(heads):
        at = columns_of(h)
        for r, x in zip(state, head_part(q_v[:, at], kv_v[0][:, at], kv_v[1][:, at])):
            r[:, at] = x
    for slot in range(slots):
        for copy in copies[3 + 2 * slot : 5 + 2 * slot]:
            copy.wait()
        fold(state, active[slot], q_v, kv_v[2 * slot + 2], kv_v[2 * slot + 3])
    lane = lax.broadcasted_iota(jnp.int32, stats_v.shape, 1)
    packed = jnp.zeros(stats_v.shape, jnp.float32)
    for h in range(heads):
        packed = jnp.where(lane == h, total_v[:, columns_of(h)], packed)
        packed = jnp.where(lane == HEAD_DIM // 2 + h, peak_v[:, columns_of(h)], packed)
    stats_v[...] = packed
    copies = [fetch(part_v, part), fetch(stats_v, stats)]
    for copy in copies:
        copy.wait()


def attend(active, q, kv, first, heads):
    rows, columns, slots = q.shape[0], heads * HEAD_DIM, len(kv) // 2 - 1
    return pl.pallas_call(
        functools.partial(attend_kernel, first, slots),
        out_shape=[
            jax.ShapeDtypeStruct((rows, columns), jnp.float32),
            jax.ShapeDtypeStruct((rows, HEAD_DIM), jnp.float32),
        ],
        in_specs=[SMEM] + [ANY] * (1 + len(kv)),
        out_specs=[ANY] * 2,
        scratch_shapes=[pltpu.VMEM((rows, columns), jnp.bfloat16)] * (1 + len(kv))
        + [pltpu.VMEM((rows, columns), jnp.float32)] * 3
        + [pltpu.VMEM((rows, HEAD_DIM), jnp.float32), pltpu.SemaphoreType.DMA((3 + len(kv),))],
        compiler_params=pltpu.CompilerParams(vmem_limit_bytes=VMEM_LIMIT),
        cost_estimate=pl.CostEstimate(
            flops=(1 + slots) * 6 * rows * rows * columns,
            bytes_accessed=rows * columns * (10 + 4 * slots),
            transcendentals=0,
        ),
        name="attend",
    )(active, q, *kv)


def close_heads(fetch, first, active, q, part, stats, near, q_v, near_v, state, stats_v, out, out_at):
    columns = state[0].shape[1]
    copies = [
        fetch(q.at[:, pl.ds(first * HEAD_DIM, columns)], q_v),
        fetch(part, state[0]),
        fetch(stats, stats_v),
    ] + [fetch(source, target) for source, target in zip(near, near_v)]
    for copy in copies[:3]:
        copy.wait()
    stats_now = stats_v[...]
    for h in range(columns // HEAD_DIM):
        for r, lane in zip(state[1:], (h, HEAD_DIM // 2 + h)):
            r[:, columns_of(h)] = jnp.broadcast_to(stats_now[:, lane : lane + 1], stats_now.shape)
    for slot, kv in enumerate(near_v):
        copies[3 + slot].wait()
        fold(state, active[slot], q_v, kv.at[:, pl.ds(0, columns)], kv.at[:, pl.ds(columns, columns)])
    out[:, out_at] = (state[0][...] / state[1][...]).astype(jnp.bfloat16)


def close_scratch(rows, columns, slots):
    return (
        [pltpu.VMEM((rows, columns), jnp.bfloat16)]
        + [pltpu.VMEM((rows, 2 * columns), jnp.bfloat16)] * slots
        + [pltpu.VMEM((rows, columns), jnp.float32)] * 3
        + [pltpu.VMEM((rows, HEAD_DIM), jnp.float32), pltpu.SemaphoreType.DMA((4 + slots,))]
    )


def close_kernel(first, slots, active, q, part, stats, *refs):
    near, out = refs[:slots], refs[slots]
    q_v, near_v, (*state, stats_v, sems, out_v) = refs[slots + 1], refs[slots + 2 : 2 * slots + 2], refs[2 * slots + 2 :]
    fetch = Fetch(sems)
    close_heads(fetch, first, active, q, part, stats, near, q_v, near_v, state, stats_v, out_v, slice(None))
    fetch(out_v, out).wait()


def close(active, q, state, near, first):
    rows, columns = state[0].shape
    return pl.pallas_call(
        functools.partial(close_kernel, first, len(near)),
        out_shape=jax.ShapeDtypeStruct((rows, columns), jnp.bfloat16),
        in_specs=[SMEM] + [ANY] * (3 + len(near)),
        out_specs=ANY,
        scratch_shapes=close_scratch(rows, columns, len(near)) + [pltpu.VMEM((rows, columns), jnp.bfloat16)],
        compiler_params=pltpu.CompilerParams(vmem_limit_bytes=VMEM_LIMIT),
        cost_estimate=pl.CostEstimate(
            flops=len(near) * 6 * rows * rows * columns,
            bytes_accessed=rows * columns * (4 * len(near) + 8),
            transcendentals=0,
        ),
        name="close",
    )(active, q, *state, *near)


def finish_kernel(counts, moves, control_rows, place, active, q, part, stats, *refs):
    groups_of = []
    for count in counts:
        groups_of.append(refs[:count])
        refs = refs[count:]
    near, ready, weight, control = groups_of
    slots, blocks = len(near), len(control)
    hidden, out, refs = refs[0], refs[1], refs[2:]
    q_v, near_v, refs = refs[0], refs[1 : slots + 1], refs[slots + 1 :]
    *state, stats_v, sems, attention, held, hidden_v, control_v, out_v, late_sems = refs
    fetch, late_fetch = Fetch(sems), Fetch(late_sems)
    late = []
    done = 0
    for block in ready:
        late.append(late_fetch(block, attention.at[:, pl.ds(done, block.shape[1])]))
        done += block.shape[1]

    def fetch_late():
        for piece, index, at in moves:
            source = weight[piece] if at is None else weight[piece].at[index]
            if at is None:
                target = held
            else:
                flip, group, outer, pair, core = at
                count = source.shape[0]
                outer = place[1] ^ outer
                if flip:
                    group, pair, core = place[0] ^ group, place[2] ^ pair, place[3] ^ core
                start = pl.multiple_of(((outer * 2 + pair) * 2 + core) * count, count)
                target = held.at[group, pl.ds(start, count), :]
            late.append(late_fetch(source, target))
        late.append(late_fetch(hidden, hidden_v))
        for d in range(blocks):
            start = pl.multiple_of((place[4] ^ d) * control_rows, control_rows) if blocks > 1 else 0
            late.append(late_fetch(control[d], control_v.at[pl.ds(start, control_rows), :]))

    fetch_late()
    close_heads(
        fetch,
        done // HEAD_DIM,
        active,
        q,
        part,
        stats,
        near,
        q_v,
        near_v,
        state,
        stats_v,
        attention,
        pl.ds(done, part.shape[1]),
    )
    for copy in late:
        copy.wait()
    groups, _, columns = held.shape
    step = 512 if columns % 512 == 0 else columns
    stores = []
    for group in range(groups):
        for j in range(columns // step):
            at = pl.ds(group * columns + j * step, step)
            projected = jnp.dot(
                attention[...], held[group, :, pl.ds(j * step, step)], preferred_element_type=jnp.float32
            )
            out_v[:, at] = (
                hidden_v[:, at].astype(jnp.float32) + projected + control_v[:, at].astype(jnp.float32)
            ).astype(jnp.bfloat16)
            stores.append(late_fetch(out_v.at[:, at], out.at[:, at]))
    for copy in stores:
        copy.wait()


def finish(place, active, q, state, near, ready, weight, control, hidden, moves):
    rows, inner = q.shape
    width = hidden.shape[1]
    groups = lax.axis_size("groups")
    control_rows = control[0].shape[0]
    columns = state[0].shape[1]
    share = width // groups
    lists = (near, ready, weight, control)
    counts = tuple(len(x) for x in lists)
    step = 512 if share % 512 == 0 else share
    return pl.pallas_call(
        functools.partial(finish_kernel, counts, moves, control_rows),
        out_shape=jax.ShapeDtypeStruct((rows, width), jnp.bfloat16),
        in_specs=[SMEM] * 2 + [ANY] * (4 + sum(counts)),
        out_specs=ANY,
        scratch_shapes=close_scratch(rows, columns, len(near))
        + [
            pltpu.VMEM((rows, inner), jnp.bfloat16),
            pltpu.VMEM((groups, inner, share), jnp.bfloat16),
            pltpu.VMEM((rows, width), jnp.bfloat16),
            pltpu.VMEM((rows, width), jnp.bfloat16),
            pltpu.VMEM((rows, width), jnp.bfloat16),
            pltpu.SemaphoreType.DMA((len(ready) + len(moves) + 1 + len(control) + width // step,)),
        ],
        compiler_params=pltpu.CompilerParams(vmem_limit_bytes=VMEM_LIMIT),
        cost_estimate=pl.CostEstimate(
            flops=2 * rows * inner * width, bytes_accessed=2 * inner * width + 6 * rows * width, transcendentals=0
        ),
        name="finish",
    )(place, active, q, *state, *near, *ready, *weight, *control, hidden)


def tied_kernel(x, other, out):
    del x, other, out


def tied(x, other):
    return pl.pallas_call(
        tied_kernel,
        out_shape=jax.ShapeDtypeStruct(x.shape, x.dtype),
        in_specs=[ANY, ANY],
        out_specs=ANY,
        input_output_aliases={0: 0},
        cost_estimate=pl.CostEstimate(flops=0, bytes_accessed=0, transcendentals=0),
        name="tied",
    )(x, other)


def flipped(block, axis, flip):
    return lax.ppermute(block, axis, [(i, i ^ flip) for i in range(lax.axis_size(axis))])


class Lane:
    def __init__(self):
        self.last = ()

    def __call__(self, send, block, *others):
        self.last = (send(after(block, *self.last, *others)),)
        return self.last[0]


def swap(axis, flip):
    return lambda block: flipped(block, axis, flip)


def route_of(route):
    return lambda block: lax.ppermute(block, TILES, route)


def neighbour_slots(tile_count, strides, counts):
    slots = []
    for axis, (stride, count) in enumerate(zip(strides, counts)):
        for odd in range(2):
            route = []
            for t in range(tile_count):
                place = t // stride % count
                if place % 2 == odd and place + 1 < count:
                    route += [(t, t + stride), (t + stride, t)]
            if route:
                slots.append((axis, odd, route))
    return slots


def on_device(hidden, queries, keys, values, control, out_weight, pattern):
    groups = lax.axis_size("groups")
    outer, pair, cores = (lax.axis_size(a) for a in TILES)
    tile_count = outer * pair * cores
    grid_width = min(8, tile_count // 4)
    grid_height = min(4, tile_count // 8)
    layer = grid_width * grid_height
    strides = (layer, grid_width, 1)
    counts = (tile_count // layer, grid_height, grid_width)
    position = lax.axis_index(TILES)
    across = position % grid_width
    rows = queries.shape[0]
    width = hidden.shape[1]
    slots = neighbour_slots(tile_count, strides, counts)
    early = [s for s in slots if s[0] == 2]
    late = [s for s in slots if s[0] != 2]

    def flags(chosen):
        active = []
        for axis, odd, _ in chosen:
            place = position // strides[axis] % counts[axis]
            up = (place % 2 == odd).astype(jnp.int32)
            valid = jnp.where(up == 1, place + 1 < counts[axis], place >= 1)
            active.append((valid & (pattern[0, 2 * axis + up] == 1)).astype(jnp.int32))
        return jnp.stack(active)

    early_active, late_active = flags(early), flags(late)
    far_lane, near_lane, x_lane, y_lane, core_lane = (Lane() for _ in range(5))

    shard, share = out_weight.shape[0], width // groups
    line = out_weight[:, :share]
    for g in range(1, groups):
        line = jnp.where(lax.axis_index("groups") == g, out_weight[:, g * share : (g + 1) * share], line)
    line = lax.optimization_barrier(line)[None]
    line_flips = [0]
    flip = outer // 2
    while flip > 2:
        line = jnp.concatenate([line, flipped(line, "outer", flip)])
        line_flips += [f ^ flip for f in line_flips]
        flip //= 2
    own = lax.all_gather(line, ("groups", "pair", "core"))
    far = far_lane(swap("outer", 2), line)
    near = near_lane(swap("outer", 1), line)
    last = near_lane(swap("outer", 1), far)

    firsts = [sum(CHUNKS[:i]) for i in range(len(CHUNKS))]
    chunks = [
        jnp.concatenate([x[:, f * HEAD_DIM : (f + n) * HEAD_DIM] for x in (keys, values)], axis=1)
        for f, n in zip(firsts, CHUNKS)
    ]
    block = rows // grid_width
    lines = after(control, line).reshape(block // TILE_W, grid_width, TILE_W, width)
    control_sent = [
        lax.dynamic_index_in_dim(lines, across ^ d, 1, keepdims=False).reshape(block, width) for d in range(grid_width)
    ]
    control_parts = [control_sent[0]] + [None] * (grid_width - 1)
    control_parts[1] = swap(TILES, 1)(control_sent[1])
    early_near = [[None, None] for _ in early]
    for i, x in enumerate((keys, values)):
        early_near[0][i] = core_lane(route_of(early[0][2]), x)

    def early_along_x(i):
        for slot in range(1, len(early)):
            early_near[slot][i] = x_lane(route_of(early[slot][2]), (keys, values)[i])

    late_near = []

    def along_z(number, *others):
        lanes = (far_lane, near_lane)
        others = others or ((), ())
        late_near.append(
            [lanes[i % 2](route_of(route), chunks[number], *others[i % 2]) for i, (_, _, route) in enumerate(late)]
        )

    x_lane.last = (line,)
    early_along_x(0)
    for d in range(2, grid_width - 1):
        control_parts[d] = swap(TILES, d)(control_sent[d])
    first = [far, near] + control_parts[2:-1]
    along_z(0)
    far_x, near_x = (x_lane(swap("pair", 1), x, *first) for x in (far, near))
    last_x = x_lane(swap("pair", 1), last)
    early_along_x(1)
    control_parts[-1] = x_lane(swap(TILES, grid_width - 1), tied(control_sent[-1], own))
    plane = jnp.concatenate([far, near, far_x, near_x])
    plane_y = y_lane(swap("groups", 1), plane, *late_near[0])
    along_z(1, (), (last_x,))
    plane_last = jnp.concatenate([last, last_x])
    plane_last_y = y_lane(swap("groups", 1), plane_last, *late_near[1])
    along_z(2)
    along_z(3)
    held = [plane, plane_y, plane_last, plane_last_y]
    gates = [(), late_near[1] + [control_parts[-1]], (), late_near[2]]
    crossed = [core_lane(swap("core", 1), x, *gate) for x, gate in zip(held, gates)]
    n = len(line_flips)
    moves = [
        (0, ((g * pair + p) * cores + c, i), (False, g, f, p, c))
        for g in range(groups)
        for p in range(pair)
        for c in range(cores)
        for i, f in enumerate(line_flips)
    ]
    weight = [own]
    for number, flips in enumerate(((2, 1), (2, 1), (3,), (3,))):
        for core_flip, pieces in enumerate((held, crossed)):
            moves += [
                (len(weight), ((p * len(flips) + i) * n + j,), (True, number % 2, f ^ at, p, core_flip))
                for p in range(pair)
                for i, at in enumerate(flips)
                for j, f in enumerate(line_flips)
            ]
            weight.append(pieces[number])

    early_kv = [keys, values] + [x for kv in early_near for x in kv]
    states = [attend(early_active, queries, early_kv, f, n) for f, n in zip(firsts, CHUNKS)]
    ready = [close(late_active, queries, states[i], late_near[i], firsts[i]) for i in range(len(CHUNKS) - 1)]
    if block % 16:
        control_parts = [
            jnp.take(
                jnp.stack(control_parts), jnp.arange(grid_width, dtype=jnp.int32) ^ across, axis=0
            ).reshape(rows, width)
        ]
    place = jnp.stack([lax.axis_index(a) for a in ("groups",) + TILES] + [across]).astype(jnp.int32)
    if shard % 16:
        weight, moves = [in_order(weight, moves, place, (groups, outer, pair, cores))], [(0, None, None)]
    return finish(
        place,
        late_active,
        queries,
        states[-1],
        late_near[-1],
        ready,
        weight,
        control_parts,
        hidden,
        tuple(moves),
    )


def in_order(weight, moves, place, sizes):
    groups, outer, pair, cores = sizes
    shard, columns = weight[0].shape[-2:]
    own = weight[0].reshape(groups, pair, cores, -1, shard, columns)
    for axis, at in enumerate((0, 2, 3)):
        own = jnp.take(own, jnp.arange(sizes[at], dtype=jnp.int32) ^ place[at], axis=axis)
    weight = [own.reshape(weight[0].shape)] + weight[1:]
    blocks = {at[1:]: weight[piece][index] for piece, index, at in moves}
    whole = jnp.stack([blocks[at] for at in sorted(blocks)]).reshape(sizes + (shard, columns))
    for axis, size in enumerate(sizes):
        whole = jnp.take(whole, jnp.arange(size, dtype=jnp.int32) ^ place[axis], axis=axis)
    return whole.reshape(groups, -1, columns)


def solution(mesh):
    groups = mesh.shape["groups"]
    tiles = mesh.shape["tiles"]
    split = Mesh(mesh.devices.reshape(groups, tiles // 4, 2, 2), ("groups",) + TILES)
    rows = P(("groups",) + TILES, None)
    placed = (rows, rows, rows, rows, rows, P(TILES, None), rows)
    return jax.shard_map(
        on_device,
        mesh=split,
        in_specs=placed,
        out_specs=rows,
        check_vma=False,
    )
```

time: 133 us -> 164 us (1.23)
  starting transfers between devices: 17.8 us -> 34.5 us
  Pallas kernels: 17.1 us -> 29 us
  other arithmetic: 2.29 us -> 4.5 us
    pallas_call x4 -> x9, Pallas kernels: 17.1 us -> 29 us  [the longest x4 10.3 us: attend(): pl.pallas_call(functools.partial(attend_kernel, first, slots), out_shape=...]
    ppermute x6 -> x15, starting transfers between devices: 6.19 us -> 16.9 us  [flipped(): lax.ppermute(block, axis, [(i, i ^ flip) for i in range(lax.axis_size(axi...]
    ppermute x6 -> x15, waiting for transfers between devices: 15.6 us -> 25.9 us  [flipped(): lax.ppermute(block, axis, [(i, i ^ flip) for i in range(lax.axis_size(axi...]
    all_gather x2 -> x1, waiting for transfers between devices: 6.86 us -> 0.01 us  [on_device(): own = lax.all_gather(line, ('groups', 'pair', 'core'))]
    ppermute x8 -> x12, starting transfers between devices: 11.5 us -> 17.6 us  [route_of(): return lambda block: lax.ppermute(block, TILES, route)]
    ppermute x8 -> x12, waiting for transfers between devices: 36.6 us -> 32.2 us  [route_of(): return lambda block: lax.ppermute(block, TILES, route)]
    unnamed x54 -> x64, local copies, waits for them, and re-layouts: 15.3 us -> 13.1 us
    select_n x0 -> x1, other arithmetic: none -> 1.86 us  [on_device(): jnp.where(lax.axis_index('groups') == g, out_weight[:, g * share:(g + 1)...]
  transfers between devices with their start and end apart: 16 -> 28, of which waited for: 8 -> 8; matrix products, arithmetic and copies ran while one was open for 4% -> 8% of each run, Pallas kernels for 7% -> 13%
where the time goes in v5:
time: 164 us; the launch traced here: 162 us
  waiting for transfers between devices  58.1 us (35%)
  starting transfers between devices  34.5 us (21%)
  Pallas kernels  29 us (18%)
  local copies, waits for them, and re-layouts  19.3 us (12%)
  between operations  16.5 us (10%)
  other arithmetic  4.5 us (3%)
    ppermute x12, waiting for transfers between devices, route_of(): return lambda block: lax.ppermute(block, TILES, route)  32.2 us
    ppermute x15, waiting for transfers between devices, flipped(): lax.ppermute(block, axis, [(i, i ^ flip) for i in range(lax.axis_size(axi...  25.9 us
    ppermute x12, starting transfers between devices, route_of(): return lambda block: lax.ppermute(block, TILES, route)  17.6 us
    ppermute x15, starting transfers between devices, flipped(): lax.ppermute(block, axis, [(i, i ^ flip) for i in range(lax.axis_size(axi...  16.9 us
    unnamed x64, local copies, waits for them, and re-layouts  13.1 us
    pallas_call x4, Pallas kernels, attend(): pl.pallas_call(functools.partial(attend_kernel, first, slots), out_shape=...  10.3 us
    pallas_call x3, Pallas kernels, close(): pl.pallas_call(functools.partial(close_kernel, first, len(near)), out_sha...  10.2 us
    pallas_call x1, Pallas kernels, finish(): pl.pallas_call(functools.partial(finish_kernel, counts, moves, control_ro...  8.47 us
  transfers between devices with their start and end apart: 28, of which 8 were waited for; matrix products, arithmetic and copies ran while one was open for 8% of the time, Pallas kernels for 13%

profile of v5, /device:TPU:1, one launch (start us, length us, event | category | flops | bytes accessed | tf_op | source)
XLA Modules:
  0.0 161.8 jit_solution(12629287481215956727)
XLA Ops:
  6.5 1.9 %slice_select_fusion = bf16[96,1536]{1,0:T(8,128)(2,1)} fusion(bf16[96,3072]{1,0:T(8,128)(2,1)} %param.12, pred[]{:T(512)S(6)} %eq.77), kind=kLoop, calls=%fused_computation.6 | loop fusion | flops 147456 | bytes 884737 | tf_op jit(solution)/shard_map/jit(_where)/select_n | solution.py:361
  8.4 2.2 %collective-permute-start.4 = (bf16[1,96,1536]{2,1,0:T(8,128)(2,1)}, bf16[1,96,1536]{2,1,0:T(8,128)(2,1)}, u32[]{:S(2)}, u32[]{:S(2)}) collective-permute-start(bf16[1,96,1536]{2,1,0:T(8,128)(2,1)} %bitcast.36), channel_id=1, source_target_pairs={{0,4},{4,0},{8,12},{12,8},{1,5},{5,1},{9,13},{13,9},{2,6},{6,2},{1... | collective-permute-start | bytes 884744 | tf_op jit(solution)/shard_map/ppermute | solution.py:295
  10.6 2.3 %collective-permute-start.3 = (bf16[1,96,1536]{2,1,0:T(8,128)(2,1)}, bf16[1,96,1536]{2,1,0:T(8,128)(2,1)S(1)}, u32[]{:S(2)}, u32[]{:S(2)}) collective-permute-start(bf16[1,96,1536]{2,1,0:T(8,128)(2,1)} %bitcast.37), channel_id=1, source_target_pairs={{0,8},{4,12},{8,0},{12,4},{1,9},{5,13},{9,1},{13,5},{2,10},{6,14},... | collective-permute-start | bytes 884744 | tf_op jit(solution)/shard_map/ppermute | solution.py:295
  12.9 1.2 collective-permute-start
  14.2 3.0 %collective-permute-start.2 = (bf16[192,1536]{1,0:T(8,128)(2,1)S(1)}, bf16[192,1536]{1,0:T(8,128)(2,1)S(1)}, u32[]{:S(2)}, u32[]{:S(2)}) collective-permute-start(bf16[192,1536]{1,0:T(8,128)(2,1)S(1)} %copy-done.1), channel_id=1, source_target_pairs={{1,2},{2,1},{5,6},{6,5},{9,10},{10,9},{13,14},{14,13},{17,18},{18,... | collective-permute-start | bytes 1769480 | tf_op jit(solution)/shard_map/ppermute | solution.py:312
  17.2 2.3 %dynamic-slice_bitcast_fusion = (bf16[48,3072]{1,0:T(8,128)(2,1)}, bf16[48,3072]{1,0:T(8,128)(2,1)}, bf16[48,3072]{1,0:T(8,128)(2,1)}, bf16[48,3072]{1,0:T(8,128)(2,1)S(1)}) fusion(bf16[6,4,8,3072]{3,2,1,0:T(8,128)(2,1)} %bitcast.38, s32[]{:T(128)S(6)} %select_n.109, s32[]{:T(128)S(6)} %select_n.108, s32[]{:T(128)S(6)} %select_n.107, s32[]{:T(128)S(6)} %select_n.106), kind=kLoop, calls=%fused_computation.2 | loop fusion | bytes 2359312 | tf_op jit(solution)/shard_map/reshape | solution.py:382
  20.8 3.0 %collective-permute-done.4 = bf16[1,96,1536]{2,1,0:T(8,128)(2,1)} collective-permute-done((bf16[1,96,1536]{2,1,0:T(8,128)(2,1)}, bf16[1,96,1536]{2,1,0:T(8,128)(2,1)}, u32[]{:S(2)}, u32[]{:S(2)}) %collective-permute-start.4) | collective-permute-done | bytes 294944 | tf_op jit(solution)/shard_map/ppermute | solution.py:295
  23.9 9.6 %collective-permute-done.6.refs_16_ = bf16[48,3072]{1,0:T(8,128)(2,1)S(1)} collective-permute-done((bf16[48,3072]{1,0:T(8,128)(2,1)S(1)}, bf16[48,3072]{1,0:T(8,128)(2,1)S(1)}, u32[]{:S(2)}, u32[]{:S(2)}) %collective-permute-start.6) | collective-permute-done | bytes 294944 | tf_op jit(solution)/shard_map/ppermute | solution.py:295
  34.2 1.9 %collective-permute-start.7 = (bf16[1,96,1536]{2,1,0:T(8,128)(2,1)S(1)}, bf16[1,96,1536]{2,1,0:T(8,128)(2,1)S(1)}, u32[]{:S(2)}, u32[]{:S(2)}) collective-permute-start(bf16[1,96,1536]{2,1,0:T(8,128)(2,1)S(1)} %collective-permute-done.3), channel_id=1, source_target_pairs={{0,2},{2,0},{1,3},{3,1},{4,6},{6,4},{5,7},{7,5},{8,10},{10,8},{9,1... | collective-permute-start | bytes 884744 | tf_op jit(solution)/shard_map/ppermute | solution.py:295
  36.4 0.7 constant_dynamic-update-slice_fusion.3
  37.6 10.2 %collective-permute-done.7 = bf16[1,96,1536]{2,1,0:T(8,128)(2,1)S(1)} collective-permute-done((bf16[1,96,1536]{2,1,0:T(8,128)(2,1)S(1)}, bf16[1,96,1536]{2,1,0:T(8,128)(2,1)S(1)}, u32[]{:S(2)}, u32[]{:S(2)}) %collective-permute-start.7) | collective-permute-done | bytes 294944 | tf_op jit(solution)/shard_map/ppermute | solution.py:295
  48.4 1.7 %constant_dynamic-update-slice_fusion.2 = bf16[4,96,1536]{2,1,0:T(8,128)(2,1)} fusion(bf16[4,96,1536]{2,1,0:T(8,128)(2,1)} %constant_dynamic-update-slice_fusion.3, bf16[1,96,1536]{2,1,0:T(8,128)(2,1)} %collective-permute-done.4), kind=kLoop, calls=%fused_computation.11 | loop fusion | bytes 589824
  50.2 1.4 collective-permute-start.15
  51.6 0.7 constant_dynamic-update-slice_fusion.1
  52.3 3.0 %collective-permute-done.8 = bf16[1,96,1536]{2,1,0:T(8,128)(2,1)S(1)} collective-permute-done((bf16[1,96,1536]{2,1,0:T(8,128)(2,1)}, bf16[1,96,1536]{2,1,0:T(8,128)(2,1)S(1)}, u32[]{:S(2)}, u32[]{:S(2)}) %collective-permute-start.8) | collective-permute-done | bytes 294944 | tf_op jit(solution)/shard_map/ppermute | solution.py:295
  55.3 1.4 collective-permute-start.9
  56.7 0.7 constant_dynamic-update-slice_fusion.refs_6_
  58.8 1.6 %collective-permute-start.19 = (bf16[4,96,1536]{2,1,0:T(8,128)(2,1)}, bf16[4,96,1536]{2,1,0:T(8,128)(2,1)}, u32[]{:S(2)}, u32[]{:S(2)}) collective-permute-start(bf16[4,96,1536]{2,1,0:T(8,128)(2,1)} %constant_dynamic-update-slice_fusion.refs_6_), channel_id=1, source_target_pairs={{0,1},{1,0},{2,3},{3,2},{4,5},{5,4},{6,7},{7,6},{8,9},{9,8},{10,11... | collective-permute-start | bytes 3538952 | tf_op jit(solution)/shard_map/ppermute | solution.py:295
  60.5 1.4 collective-permute-start.20
  61.9 6.0 %collective-permute-start.10 = (bf16[192,1536]{1,0:T(8,128)(2,1)S(1)}, bf16[192,1536]{1,0:T(8,128)(2,1)S(1)}, u32[]{:S(2)}, u32[]{:S(2)}) collective-permute-start(bf16[192,1536]{1,0:T(8,128)(2,1)S(1)} %copy-done.2), channel_id=1, source_target_pairs={{1,2},{2,1},{5,6},{6,5},{9,10},{10,9},{13,14},{14,13},{17,18},{18,... | collective-permute-start | bytes 1769480 | tf_op jit(solution)/shard_map/ppermute | solution.py:312
  68.0 0.8 pad_maximum_fusion
  68.8 2.7 %collective-permute-start.12 = (bf16[192,1280]{1,0:T(8,128)(2,1)}, bf16[192,1280]{1,0:T(8,128)(2,1)}, u32[]{:S(2)}, u32[]{:S(2)}) collective-permute-start(bf16[192,1280]{1,0:T(8,128)(2,1)} %pad_maximum_fusion), channel_id=1, source_target_pairs={{0,8},{8,0},{1,9},{9,1},{2,10},{10,2},{3,11},{11,3},{4,12},{12,4},... | collective-permute-start | bytes 1474568 | tf_op jit(solution)/shard_map/ppermute | solution.py:312
  71.8 6.3 %collective-permute-done.10.refs_5_ = bf16[192,1536]{1,0:T(8,128)(2,1)S(1)} collective-permute-done((bf16[192,1536]{1,0:T(8,128)(2,1)S(1)}, bf16[192,1536]{1,0:T(8,128)(2,1)S(1)}, u32[]{:S(2)}, u32[]{:S(2)}) %collective-permute-start.10) | collective-permute-done | bytes 589856 | tf_op jit(solution)/shard_map/ppermute | solution.py:312
  78.1 0.9 copy-done.3
  79.0 2.2 %collective-permute-start.21 = (bf16[48,3072]{1,0:T(8,128)(2,1)}, bf16[48,3072]{1,0:T(8,128)(2,1)S(1)}, u32[]{:S(2)}, u32[]{:S(2)}) collective-permute-start(bf16[48,3072]{1,0:T(8,128)(2,1)} %tied.1), channel_id=1, source_target_pairs={{0,3},{1,2},{2,1},{3,0},{4,7},{5,6},{6,5},{7,4},{8,11},{9,10},{10,... | collective-permute-start | bytes 884744 | tf_op jit(solution)/shard_map/ppermute | solution.py:295
  81.2 10.4 %collective-permute-done.12.refs_0_ = bf16[192,1280]{1,0:T(8,128)(2,1)} collective-permute-done((bf16[192,1280]{1,0:T(8,128)(2,1)}, bf16[192,1280]{1,0:T(8,128)(2,1)}, u32[]{:S(2)}, u32[]{:S(2)}) %collective-permute-start.12) | collective-permute-done | bytes 491552 | tf_op jit(solution)/shard_map/ppermute | solution.py:312
  93.0 1.0 constant_dynamic-update-slice_fusion.5
  94.0 1.0 constant_dynamic-update-slice_fusion.4.refs_10_
  95.1 1.4 collective-permute-start.24
  96.5 1.0 copy-done.10
  97.5 0.8 collective-permute-start.23
  98.3 0.9 copy-done.7
  100.4 14.8 %collective-permute-done.13.refs_0_ = bf16[192,768]{1,0:T(8,128)(2,1)S(1)} collective-permute-done((bf16[192,768]{1,0:T(8,128)(2,1)S(1)}, bf16[192,768]{1,0:T(8,128)(2,1)S(1)}, u32[]{:S(2)}, u32[]{:S(2)}) %collective-permute-start.13) | collective-permute-done | bytes 294944 | tf_op jit(solution)/shard_map/ppermute | solution.py:312
  115.1 0.7 copy-done.15
  115.9 0.7 copy-done.17
  116.6 0.8 copy-done.13
  117.4 0.8 collective-permute-start.25
  120.1 1.6 %pad_maximum_fusion.2 = bf16[192,512]{1,0:T(8,128)(2,1)} fusion(bf16[192,256]{1,0:T(8,128)(2,1)} %get-tuple-element.74, bf16[192,256]{1,0:T(8,128)(2,1)} %get-tuple-element.72), kind=kLoop, calls=%fused_computation.7 | loop fusion | flops 393216 | bytes 393216 | tf_op jit(solution)/shard_map/concatenate | solution.py:376
  123.4 1.0 collective-permute-start.18
  124.6 1.1 copy-done.4
  125.6 2.4 %attend.5 = (f32[192,256]{1,0:T(8,128)S(1)}, f32[192,128]{1,0:T(8,128)S(1)}) custom-call(s32[2]{0:T(128)S(1)} %add_convert_fusion.1.active, bf16[192,1536]{1,0:T(8,128)(2,1)S(1)} %copy-done, bf16[192,1536]{1,0:T(8,128)(2,1)S(1)} %copy-done.1, bf16[192,1536]{1,0:T(8,128)(2,1)S(1)} %copy-done.2, bf16[192,1536]{1,0:T(8,128)(2,1)S(1)} %collective-permute-done.refs_2_, ...), custom_call_target="tpu_custom_call" | custom-call | flops 169869312 | bytes 884736 | tf_op jit(solution)/shard_map/attend/pallas_call | solution.py:100
  128.1 3.2 %close.3.refs_2_ = bf16[192,256]{1,0:T(8,128)(2,1)S(1)} custom-call(s32[2]{0:T(128)S(1)} %add_convert_fusion.active, bf16[192,1536]{1,0:T(8,128)(2,1)S(1)} %copy-done, f32[192,256]{1,0:T(8,128)S(1)} %get-tuple-element.54.part, f32[192,128]{1,0:T(8,128)S(1)} %get-tuple-element.55.stats, bf16[192,512]{1,0:T(8,128)(2,1)S(1)} %copy-done.24, ...), custom_call_target="tpu_custom_call" | custom-call | flops 113246208 | bytes 786432 | tf_op jit(solution)/shard_map/close/pallas_call | solution.py:159
  131.3 2.4 %attend.4 = (f32[192,256]{1,0:T(8,128)S(1)}, f32[192,128]{1,0:T(8,128)S(1)}) custom-call(s32[2]{0:T(128)S(1)} %add_convert_fusion.1.active, bf16[192,1536]{1,0:T(8,128)(2,1)S(1)} %copy-done, bf16[192,1536]{1,0:T(8,128)(2,1)S(1)} %copy-done.1, bf16[192,1536]{1,0:T(8,128)(2,1)S(1)} %copy-done.2, bf16[192,1536]{1,0:T(8,128)(2,1)S(1)} %collective-permute-done.refs_2_, ...), custom_call_target="tpu_custom_call" | custom-call | flops 169869312 | bytes 884736 | tf_op jit(solution)/shard_map/attend/pallas_call | solution.py:100
  133.8 2.4 %attend.7 = (f32[192,384]{1,0:T(8,128)S(1)}, f32[192,128]{1,0:T(8,128)S(1)}) custom-call(s32[2]{0:T(128)S(1)} %add_convert_fusion.1.active, bf16[192,1536]{1,0:T(8,128)(2,1)S(1)} %copy-done, bf16[192,1536]{1,0:T(8,128)(2,1)S(1)} %copy-done.1, bf16[192,1536]{1,0:T(8,128)(2,1)S(1)} %copy-done.2, bf16[192,1536]{1,0:T(8,128)(2,1)S(1)} %collective-permute-done.refs_2_, ...), custom_call_target="tpu_custom_call" | custom-call | flops 254803968 | bytes 1327104 | tf_op jit(solution)/shard_map/attend/pallas_call | solution.py:100
  136.3 3.0 %attend.6 = (f32[192,640]{1,0:T(8,128)S(1)}, f32[192,128]{1,0:T(8,128)S(1)}) custom-call(s32[2]{0:T(128)S(1)} %add_convert_fusion.1.active, bf16[192,1536]{1,0:T(8,128)(2,1)S(1)} %copy-done, bf16[192,1536]{1,0:T(8,128)(2,1)S(1)} %copy-done.1, bf16[192,1536]{1,0:T(8,128)(2,1)S(1)} %copy-done.2, bf16[192,1536]{1,0:T(8,128)(2,1)S(1)} %collective-permute-done.refs_2_, ...), custom_call_target="tpu_custom_call" | custom-call | flops 424673280 | bytes 2211840 | tf_op jit(solution)/shard_map/attend/pallas_call | solution.py:100
  139.3 4.2 %close.4.refs_3_ = bf16[192,640]{1,0:T(8,128)(2,1)S(1)} custom-call(s32[2]{0:T(128)S(1)} %add_convert_fusion.active, bf16[192,1536]{1,0:T(8,128)(2,1)S(1)} %copy-done, f32[192,640]{1,0:T(8,128)S(1)} %get-tuple-element.56.part, f32[192,128]{1,0:T(8,128)S(1)} %get-tuple-element.57.stats, bf16[192,1280]{1,0:T(8,128)(2,1)} %collective-permute-done.12.refs_0_, ...), custom_call_target="tpu_custom_call" | custom-call | flops 283115520 | bytes 1966080 | tf_op jit(solution)/shard_map/close/pallas_call | solution.py:159
  143.5 2.8 %close.5.refs_4_ = bf16[192,384]{1,0:T(8,128)(2,1)S(1)} custom-call(s32[2]{0:T(128)S(1)} %add_convert_fusion.active, bf16[192,1536]{1,0:T(8,128)(2,1)S(1)} %copy-done, f32[192,384]{1,0:T(8,128)S(1)} %get-tuple-element.58.part, f32[192,128]{1,0:T(8,128)S(1)} %get-tuple-element.59.stats, bf16[192,768]{1,0:T(8,128)(2,1)S(1)} %copy-done.16, ...), custom_call_target="tpu_custom_call" | custom-call | flops 169869312 | bytes 1179648 | tf_op jit(solution)/shard_map/close/pallas_call | solution.py:159
  146.5 8.5 %finish.1 = bf16[192,3072]{1,0:T(8,128)(2,1)} custom-call(s32[5]{0:T(128)S(1)} %stack.49.place, s32[2]{0:T(128)S(1)} %add_convert_fusion.active, bf16[192,1536]{1,0:T(8,128)(2,1)S(1)} %copy-done, f32[192,256]{1,0:T(8,128)S(1)} %get-tuple-element.44.part, f32[192,128]{1,0:T(8,128)S(1)} %get-tuple-element.45.stats, ...), custom_call_target="tpu_custom_call" | custom-call | flops 1811939328 | bytes 12976128 | tf_op jit(solution)/shard_map/finish/pallas_call | solution.py:256
  (100 shorter events, 9.0 us)
Async XLA Ops:
  6.5 6.4 %copy-start.1 = (bf16[192,1536]{1,0:T(8,128)(2,1)S(1)}, bf16[192,1536]{1,0:T(8,128)(2,1)}, u32[]{:S(2)}) copy-start(bf16[192,1536]{1,0:T(8,128)(2,1)} %refs_0_.7) | copy-start | bytes 1769476
  6.5 65.3 %all-gather.3.cloned.1.call-start = ((), (), s32[]{:S(2)}) async-start(), calls=%async_computation | async-start | bytes 2654208 | tf_op jit(solution)/shard_map/all_gather | solution.py:369
  8.4 15.4 %collective-permute-start.4 = (bf16[1,96,1536]{2,1,0:T(8,128)(2,1)}, bf16[1,96,1536]{2,1,0:T(8,128)(2,1)}, u32[]{:S(2)}, u32[]{:S(2)}) collective-permute-start(bf16[1,96,1536]{2,1,0:T(8,128)(2,1)} %bitcast.36), channel_id=1, source_target_pairs={{0,4},{4,0},{8,12},{12,8},{1,5},{5,1},{9,13},{13,9},{2,6},{6,2},{1... | collective-permute-start | bytes 884744 | tf_op jit(solution)/shard_map/ppermute | solution.py:295
  10.6 13.2 %collective-permute-start.3 = (bf16[1,96,1536]{2,1,0:T(8,128)(2,1)}, bf16[1,96,1536]{2,1,0:T(8,128)(2,1)S(1)}, u32[]{:S(2)}, u32[]{:S(2)}) collective-permute-start(bf16[1,96,1536]{2,1,0:T(8,128)(2,1)} %bitcast.37), channel_id=1, source_target_pairs={{0,8},{4,12},{8,0},{12,4},{1,9},{5,13},{9,1},{13,5},{2,10},{6,14},... | collective-permute-start | bytes 884744 | tf_op jit(solution)/shard_map/ppermute | solution.py:295
  12.9 24.2 %collective-permute-start = (bf16[192,1536]{1,0:T(8,128)(2,1)S(1)}, bf16[192,1536]{1,0:T(8,128)(2,1)S(1)}, u32[]{:S(2)}, u32[]{:S(2)}) collective-permute-start(bf16[192,1536]{1,0:T(8,128)(2,1)S(1)} %copy-done.1), channel_id=1, source_target_pairs={{0,1},{1,0},{2,3},{3,2},{4,5},{5,4},{6,7},{7,6},{8,9},{9,8},{10,11... | collective-permute-start | bytes 1769480 | tf_op jit(solution)/shard_map/ppermute | solution.py:312
  14.2 20.0 %collective-permute-start.2 = (bf16[192,1536]{1,0:T(8,128)(2,1)S(1)}, bf16[192,1536]{1,0:T(8,128)(2,1)S(1)}, u32[]{:S(2)}, u32[]{:S(2)}) collective-permute-start(bf16[192,1536]{1,0:T(8,128)(2,1)S(1)} %copy-done.1), channel_id=1, source_target_pairs={{1,2},{2,1},{5,6},{6,5},{9,10},{10,9},{13,14},{14,13},{17,18},{18,... | collective-permute-start | bytes 1769480 | tf_op jit(solution)/shard_map/ppermute | solution.py:312
  17.2 3.0 %copy-start.2 = (bf16[192,1536]{1,0:T(8,128)(2,1)S(1)}, bf16[192,1536]{1,0:T(8,128)(2,1)}, u32[]{:S(2)}) copy-start(bf16[192,1536]{1,0:T(8,128)(2,1)} %refs_1_.7) | copy-start | bytes 1769476
  19.5 13.9 %collective-permute-start.6 = (bf16[48,3072]{1,0:T(8,128)(2,1)S(1)}, bf16[48,3072]{1,0:T(8,128)(2,1)S(1)}, u32[]{:S(2)}, u32[]{:S(2)}) collective-permute-start(bf16[48,3072]{1,0:T(8,128)(2,1)S(1)} %get-tuple-element.70), channel_id=1, source_target_pairs={{0,2},{1,3},{2,0},{3,1},{4,6},{5,7},{6,4},{7,5},{8,10},{9,11},{10,... | collective-permute-start | bytes 884744 | tf_op jit(solution)/shard_map/ppermute | solution.py:295
  34.2 13.6 %collective-permute-start.7 = (bf16[1,96,1536]{2,1,0:T(8,128)(2,1)S(1)}, bf16[1,96,1536]{2,1,0:T(8,128)(2,1)S(1)}, u32[]{:S(2)}, u32[]{:S(2)}) collective-permute-start(bf16[1,96,1536]{2,1,0:T(8,128)(2,1)S(1)} %collective-permute-done.3), channel_id=1, source_target_pairs={{0,2},{2,0},{1,3},{3,1},{4,6},{6,4},{5,7},{7,5},{8,10},{10,8},{9,1... | collective-permute-start | bytes 884744 | tf_op jit(solution)/shard_map/ppermute | solution.py:295
  36.1 21.4 %collective-permute-start.11 = (bf16[192,512]{1,0:T(8,128)(2,1)S(1)}, bf16[192,512]{1,0:T(8,128)(2,1)S(1)}, u32[]{:S(2)}, u32[]{:S(2)}) collective-permute-start(bf16[192,512]{1,0:T(8,128)(2,1)S(1)} %pad_maximum_fusion.3), channel_id=1, source_target_pairs={{0,8},{8,0},{1,9},{9,1},{2,10},{10,2},{3,11},{11,3},{4,12},{12,4},... | collective-permute-start | bytes 589832 | tf_op jit(solution)/shard_map/ppermute | solution.py:312
  36.2 14.0 %collective-permute-start.5 = (bf16[1,96,1536]{2,1,0:T(8,128)(2,1)S(1)}, bf16[1,96,1536]{2,1,0:T(8,128)(2,1)S(1)}, u32[]{:S(2)}, u32[]{:S(2)}) collective-permute-start(bf16[1,96,1536]{2,1,0:T(8,128)(2,1)S(1)} %collective-permute-done.3), channel_id=1, source_target_pairs={{0,4},{4,0},{8,12},{12,8},{1,5},{5,1},{9,13},{13,9},{2,6},{6,2},{1... | collective-permute-start | bytes 884744 | tf_op jit(solution)/shard_map/ppermute | solution.py:295
  37.1 21.7 %collective-permute-start.1 = (bf16[192,1536]{1,0:T(8,128)(2,1)S(1)}, bf16[192,1536]{1,0:T(8,128)(2,1)S(1)}, u32[]{:S(2)}, u32[]{:S(2)}) collective-permute-start(bf16[192,1536]{1,0:T(8,128)(2,1)S(1)} %copy-done.2), channel_id=1, source_target_pairs={{0,1},{1,0},{2,3},{3,2},{4,5},{5,4},{6,7},{7,6},{8,9},{9,8},{10,11... | collective-permute-start | bytes 1769480 | tf_op jit(solution)/shard_map/ppermute | solution.py:312
  47.8 7.6 %collective-permute-start.8 = (bf16[1,96,1536]{2,1,0:T(8,128)(2,1)}, bf16[1,96,1536]{2,1,0:T(8,128)(2,1)S(1)}, u32[]{:S(2)}, u32[]{:S(2)}) collective-permute-start(bf16[1,96,1536]{2,1,0:T(8,128)(2,1)} %collective-permute-done.4), channel_id=1, source_target_pairs={{0,2},{2,0},{1,3},{3,1},{4,6},{6,4},{5,7},{7,5},{8,10},{10,8},{9,1... | collective-permute-start | bytes 884744 | tf_op jit(solution)/shard_map/ppermute | solution.py:295
  50.2 17.8 %copy-start.27 = (bf16[1,96,1536]{2,1,0:T(8,128)(2,1)}, bf16[1,96,1536]{2,1,0:T(8,128)(2,1)S(1)}, u32[]{:S(2)}) copy-start(bf16[1,96,1536]{2,1,0:T(8,128)(2,1)S(1)} %collective-permute-done.5) | copy-start | bytes 884740
  50.2 8.0 %collective-permute-start.15 = (bf16[192,512]{1,0:T(8,128)(2,1)S(1)}, bf16[192,512]{1,0:T(8,128)(2,1)S(1)}, u32[]{:S(2)}, u32[]{:S(2)}) collective-permute-start(bf16[192,512]{1,0:T(8,128)(2,1)S(1)} %pad_maximum_fusion.3), channel_id=1, source_target_pairs={{0,4},{4,0},{1,5},{5,1},{2,6},{6,2},{3,7},{7,3},{8,12},{12,8},{9,1... | collective-permute-start | bytes 589832 | tf_op jit(solution)/shard_map/ppermute | solution.py:312
  55.3 6.6 %collective-permute-start.9 = (bf16[1,96,1536]{2,1,0:T(8,128)(2,1)S(1)}, bf16[1,96,1536]{2,1,0:T(8,128)(2,1)S(1)}, u32[]{:S(2)}, u32[]{:S(2)}) collective-permute-start(bf16[1,96,1536]{2,1,0:T(8,128)(2,1)S(1)} %collective-permute-done.5), channel_id=1, source_target_pairs={{0,2},{2,0},{1,3},{3,1},{4,6},{6,4},{5,7},{7,5},{8,10},{10,8},{9,1... | collective-permute-start | bytes 884744 | tf_op jit(solution)/shard_map/ppermute | solution.py:295
  58.8 33.5 %collective-permute-start.19 = (bf16[4,96,1536]{2,1,0:T(8,128)(2,1)}, bf16[4,96,1536]{2,1,0:T(8,128)(2,1)}, u32[]{:S(2)}, u32[]{:S(2)}) collective-permute-start(bf16[4,96,1536]{2,1,0:T(8,128)(2,1)} %constant_dynamic-update-slice_fusion.refs_6_), channel_id=1, source_target_pairs={{0,1},{1,0},{2,3},{3,2},{4,5},{5,4},{6,7},{7,6},{8,9},{9,8},{10,11... | collective-permute-start | bytes 3538952 | tf_op jit(solution)/shard_map/ppermute | solution.py:295
  60.5 31.8 %collective-permute-start.20 = (bf16[4,96,1536]{2,1,0:T(8,128)(2,1)}, bf16[4,96,1536]{2,1,0:T(8,128)(2,1)}, u32[]{:S(2)}, u32[]{:S(2)}) collective-permute-start(bf16[4,96,1536]{2,1,0:T(8,128)(2,1)} %constant_dynamic-update-slice_fusion.refs_6_), channel_id=1, source_target_pairs={{0,16},{16,0},{1,17},{17,1},{2,18},{18,2},{3,19},{19,3},{4,20},{20... | collective-permute-start | bytes 3538952 | tf_op jit(solution)/shard_map/ppermute | solution.py:295
  61.9 6.1 %copy-start.28 = (bf16[1,96,1536]{2,1,0:T(8,128)(2,1)}, bf16[1,96,1536]{2,1,0:T(8,128)(2,1)S(1)}, u32[]{:S(2)}) copy-start(bf16[1,96,1536]{2,1,0:T(8,128)(2,1)S(1)} %collective-permute-done.9) | copy-start | bytes 884740
  61.9 16.2 %collective-permute-start.10 = (bf16[192,1536]{1,0:T(8,128)(2,1)S(1)}, bf16[192,1536]{1,0:T(8,128)(2,1)S(1)}, u32[]{:S(2)}, u32[]{:S(2)}) collective-permute-start(bf16[192,1536]{1,0:T(8,128)(2,1)S(1)} %copy-done.2), channel_id=1, source_target_pairs={{1,2},{2,1},{5,6},{6,5},{9,10},{10,9},{13,14},{14,13},{17,18},{18,... | collective-permute-start | bytes 1769480 | tf_op jit(solution)/shard_map/ppermute | solution.py:312
  68.8 22.8 %collective-permute-start.12 = (bf16[192,1280]{1,0:T(8,128)(2,1)}, bf16[192,1280]{1,0:T(8,128)(2,1)}, u32[]{:S(2)}, u32[]{:S(2)}) collective-permute-start(bf16[192,1280]{1,0:T(8,128)(2,1)} %pad_maximum_fusion), channel_id=1, source_target_pairs={{0,8},{8,0},{1,9},{9,1},{2,10},{10,2},{3,11},{11,3},{4,12},{12,4},... | collective-permute-start | bytes 1474568 | tf_op jit(solution)/shard_map/ppermute | solution.py:312
  71.6 20.7 %collective-permute-start.16 = (bf16[192,1280]{1,0:T(8,128)(2,1)}, bf16[192,1280]{1,0:T(8,128)(2,1)}, u32[]{:S(2)}, u32[]{:S(2)}) collective-permute-start(bf16[192,1280]{1,0:T(8,128)(2,1)} %pad_maximum_fusion), channel_id=1, source_target_pairs={{0,4},{4,0},{1,5},{5,1},{2,6},{6,2},{3,7},{7,3},{8,12},{12,8},{9,1... | collective-permute-start | bytes 1474568 | tf_op jit(solution)/shard_map/ppermute | solution.py:312
  71.8 46.4 %copy-start.29 = (s32[1,6]{1,0:T(1,128)S(1)}, s32[1,6]{1,0:T(1,128)}, u32[]{:S(2)}) copy-start(s32[1,6]{1,0:T(1,128)} %param.13) | copy-start | bytes 76
  79.0 13.3 %collective-permute-start.21 = (bf16[48,3072]{1,0:T(8,128)(2,1)}, bf16[48,3072]{1,0:T(8,128)(2,1)S(1)}, u32[]{:S(2)}, u32[]{:S(2)}) collective-permute-start(bf16[48,3072]{1,0:T(8,128)(2,1)} %tied.1), channel_id=1, source_target_pairs={{0,3},{1,2},{2,1},{3,0},{4,7},{5,6},{6,5},{7,4},{8,11},{9,10},{10,... | collective-permute-start | bytes 884744 | tf_op jit(solution)/shard_map/ppermute | solution.py:295
  93.0 3.4 %collective-permute-start.22 = (bf16[4,96,1536]{2,1,0:T(8,128)(2,1)}, bf16[4,96,1536]{2,1,0:T(8,128)(2,1)S(1)}, u32[]{:S(2)}, u32[]{:S(2)}) collective-permute-start(bf16[4,96,1536]{2,1,0:T(8,128)(2,1)} %collective-permute-done.20.refs_8_), channel_id=1, source_target_pairs={{0,1},{1,0},{2,3},{3,2},{4,5},{5,4},{6,7},{7,6},{8,9},{9,8},{10,11... | collective-permute-start | bytes 3538952 | tf_op jit(solution)/shard_map/ppermute | solution.py:295
  94.0 30.6 %copy-start = (bf16[192,1536]{1,0:T(8,128)(2,1)S(1)}, bf16[192,1536]{1,0:T(8,128)(2,1)}, u32[]{:S(2)}) copy-start(bf16[192,1536]{1,0:T(8,128)(2,1)} %q.15) | copy-start | bytes 1769476
  95.1 21.5 %collective-permute-start.24 = (bf16[2,96,1536]{2,1,0:T(8,128)(2,1)S(1)}, bf16[2,96,1536]{2,1,0:T(8,128)(2,1)}, u32[]{:S(2)}, u32[]{:S(2)}) collective-permute-start(bf16[2,96,1536]{2,1,0:T(8,128)(2,1)S(1)} %constant_dynamic-update-slice_fusion.4.refs_10_), channel_id=1, source_target_pairs={{0,16},{16,0},{1,17},{17,1},{2,18},{18,2},{3,19},{19,3},{4,20},{20... | collective-permute-start | bytes 1769480 | tf_op jit(solution)/shard_map/ppermute | solution.py:295
  97.5 19.1 %collective-permute-start.23 = (bf16[2,96,1536]{2,1,0:T(8,128)(2,1)S(1)}, bf16[2,96,1536]{2,1,0:T(8,128)(2,1)S(1)}, u32[]{:S(2)}, u32[]{:S(2)}) collective-permute-start(bf16[2,96,1536]{2,1,0:T(8,128)(2,1)S(1)} %constant_dynamic-update-slice_fusion.4.refs_10_), channel_id=1, source_target_pairs={{0,1},{1,0},{2,3},{3,2},{4,5},{5,4},{6,7},{7,6},{8,9},{9,8},{10,11... | collective-permute-start | bytes 1769480 | tf_op jit(solution)/shard_map/ppermute | solution.py:295
  99.2 15.9 %collective-permute-start.13 = (bf16[192,768]{1,0:T(8,128)(2,1)S(1)}, bf16[192,768]{1,0:T(8,128)(2,1)S(1)}, u32[]{:S(2)}, u32[]{:S(2)}) collective-permute-start(bf16[192,768]{1,0:T(8,128)(2,1)S(1)} %pad_maximum_fusion.1), channel_id=1, source_target_pairs={{0,8},{8,0},{1,9},{9,1},{2,10},{10,2},{3,11},{11,3},{4,12},{12,4},... | collective-permute-start | bytes 884744 | tf_op jit(solution)/shard_map/ppermute | solution.py:312
  99.8 16.1 %collective-permute-start.17 = (bf16[192,768]{1,0:T(8,128)(2,1)S(1)}, bf16[192,768]{1,0:T(8,128)(2,1)S(1)}, u32[]{:S(2)}, u32[]{:S(2)}) collective-permute-start(bf16[192,768]{1,0:T(8,128)(2,1)S(1)} %pad_maximum_fusion.1), channel_id=1, source_target_pairs={{0,4},{4,0},{1,5},{5,1},{2,6},{6,2},{3,7},{7,3},{8,12},{12,8},{9,1... | collective-permute-start | bytes 884744 | tf_op jit(solution)/shard_map/ppermute | solution.py:312
  117.4 29.0 %collective-permute-start.25 = (bf16[2,96,1536]{2,1,0:T(8,128)(2,1)}, bf16[2,96,1536]{2,1,0:T(8,128)(2,1)}, u32[]{:S(2)}, u32[]{:S(2)}) collective-permute-start(bf16[2,96,1536]{2,1,0:T(8,128)(2,1)} %collective-permute-done.24.refs_12_), channel_id=1, source_target_pairs={{0,1},{1,0},{2,3},{3,2},{4,5},{5,4},{6,7},{7,6},{8,9},{9,8},{10,11... | collective-permute-start | bytes 1769480 | tf_op jit(solution)/shard_map/ppermute | solution.py:295
  118.2 28.2 %collective-permute-start.26 = (bf16[48,3072]{1,0:T(8,128)(2,1)}, bf16[48,3072]{1,0:T(8,128)(2,1)}, u32[]{:S(2)}, u32[]{:S(2)}) collective-permute-start(bf16[48,3072]{1,0:T(8,128)(2,1)} %get-tuple-element.67), channel_id=1, source_target_pairs={{0,1},{1,0},{2,3},{3,2},{4,5},{5,4},{6,7},{7,6},{8,9},{9,8},{10,11... | collective-permute-start | bytes 884744 | tf_op jit(solution)/shard_map/ppermute | solution.py:295
  123.2 23.2 %collective-permute-start.14 = (bf16[192,512]{1,0:T(8,128)(2,1)}, bf16[192,512]{1,0:T(8,128)(2,1)}, u32[]{:S(2)}, u32[]{:S(2)}) collective-permute-start(bf16[192,512]{1,0:T(8,128)(2,1)} %pad_maximum_fusion.2), channel_id=1, source_target_pairs={{0,8},{8,0},{1,9},{9,1},{2,10},{10,2},{3,11},{11,3},{4,12},{12,4},... | collective-permute-start | bytes 589832 | tf_op jit(solution)/shard_map/ppermute | solution.py:312
  123.4 23.0 %collective-permute-start.18 = (bf16[192,512]{1,0:T(8,128)(2,1)}, bf16[192,512]{1,0:T(8,128)(2,1)}, u32[]{:S(2)}, u32[]{:S(2)}) collective-permute-start(bf16[192,512]{1,0:T(8,128)(2,1)} %pad_maximum_fusion.2), channel_id=1, source_target_pairs={{0,4},{4,0},{1,5},{5,1},{2,6},{6,2},{3,7},{7,3},{8,12},{12,8},{9,1... | collective-permute-start | bytes 589832 | tf_op jit(solution)/shard_map/ppermute | solution.py:312
  124.6 1.1 copy-start.4
  125.6 2.5 %copy-start.24 = (bf16[192,512]{1,0:T(8,128)(2,1)S(1)}, bf16[192,512]{1,0:T(8,128)(2,1)}, u32[]{:S(2)}) copy-start(bf16[192,512]{1,0:T(8,128)(2,1)} %copy-done.23) | copy-start | bytes 589828
  125.6 2.5 %copy-start.26 = (bf16[192,512]{1,0:T(8,128)(2,1)S(1)}, bf16[192,512]{1,0:T(8,128)(2,1)}, u32[]{:S(2)}) copy-start(bf16[192,512]{1,0:T(8,128)(2,1)} %copy-done.25) | copy-start | bytes 589828
  128.1 3.2 %copy-start.5 = (bf16[192,1536]{1,0:T(8,128)(2,1)S(1)}, bf16[192,1536]{1,0:T(8,128)(2,1)}, u32[]{:S(2)}) copy-start(bf16[192,1536]{1,0:T(8,128)(2,1)} %copy-done.3) | copy-start | bytes 1769476
  136.2 7.3 %copy-start.16 = (bf16[192,768]{1,0:T(8,128)(2,1)S(1)}, bf16[192,768]{1,0:T(8,128)(2,1)}, u32[]{:S(2)}) copy-start(bf16[192,768]{1,0:T(8,128)(2,1)} %copy-done.15) | copy-start | bytes 884740
  136.2 7.3 %copy-start.18 = (bf16[192,768]{1,0:T(8,128)(2,1)S(1)}, bf16[192,768]{1,0:T(8,128)(2,1)}, u32[]{:S(2)}) copy-start(bf16[192,768]{1,0:T(8,128)(2,1)} %copy-done.17) | copy-start | bytes 884740
  136.2 10.2 %copy-start.11 = (bf16[4,96,1536]{2,1,0:T(8,128)(2,1)S(1)}, bf16[4,96,1536]{2,1,0:T(8,128)(2,1)}, u32[]{:S(2)}) copy-start(bf16[4,96,1536]{2,1,0:T(8,128)(2,1)} %copy-done.10) | copy-start | bytes 3538948
  136.2 10.2 %copy-start.12 = (bf16[48,3072]{1,0:T(8,128)(2,1)S(1)}, bf16[48,3072]{1,0:T(8,128)(2,1)}, u32[]{:S(2)}) copy-start(bf16[48,3072]{1,0:T(8,128)(2,1)} %get-tuple-element.68.refs_14_) | copy-start | bytes 884740
  136.2 10.2 %copy-start.14 = (bf16[2,96,1536]{2,1,0:T(8,128)(2,1)S(1)}, bf16[2,96,1536]{2,1,0:T(8,128)(2,1)}, u32[]{:S(2)}) copy-start(bf16[2,96,1536]{2,1,0:T(8,128)(2,1)} %copy-done.13) | copy-start | bytes 1769476
  136.3 10.2 %copy-start.20 = (bf16[48,3072]{1,0:T(8,128)(2,1)S(1)}, bf16[48,3072]{1,0:T(8,128)(2,1)}, u32[]{:S(2)}) copy-start(bf16[48,3072]{1,0:T(8,128)(2,1)} %copy-done.19) | copy-start | bytes 884740
  136.3 10.2 %copy-start.22 = (bf16[48,3072]{1,0:T(8,128)(2,1)S(1)}, bf16[48,3072]{1,0:T(8,128)(2,1)}, u32[]{:S(2)}) copy-start(bf16[48,3072]{1,0:T(8,128)(2,1)} %copy-done.21) | copy-start | bytes 884740
  139.2 7.2 %copy-start.6 = (bf16[768,1536]{1,0:T(8,128)(2,1)S(1)}, bf16[768,1536]{1,0:T(8,128)(2,1)}, u32[]{:S(2)}) copy-start(bf16[768,1536]{1,0:T(8,128)(2,1)} %all-gather.3.cloned.1.call-done) | copy-start | bytes 7077892
  139.3 7.2 %copy-start.9 = (bf16[192,3072]{1,0:T(8,128)(2,1)S(1)}, bf16[192,3072]{1,0:T(8,128)(2,1)}, u32[]{:S(2)}) copy-start(bf16[192,3072]{1,0:T(8,128)(2,1)} %refs_18_.1) | copy-start | bytes 3538948
  143.5 3.0 %copy-start.8 = (bf16[2,96,1536]{2,1,0:T(8,128)(2,1)S(1)}, bf16[2,96,1536]{2,1,0:T(8,128)(2,1)}, u32[]{:S(2)}) copy-start(bf16[2,96,1536]{2,1,0:T(8,128)(2,1)} %copy-done.7) | copy-start | bytes 1769476
  (10 other events, 7.8 us)
Sparse Core Ops, SparseCore 0:
  9.2 39.1 all-gather.2

commit v6 on v5

--- a/solution.py
+++ b/solution.py
@@ -11,12 +11,13 @@
 
 HEAD_DIM = 128
 TILE_W = 8
-CHUNKS = (2, 5, 3, 2)
+CHUNKS = (2, 6, 4)
 SCALE = HEAD_DIM**-0.5 * math.log2(math.e)
 TILES = ("outer", "pair", "core")
 VMEM_LIMIT = 24 * 1024 * 1024
 SMEM = pl.BlockSpec(memory_space=pltpu.SMEM)
 ANY = pl.BlockSpec(memory_space=pl.ANY)
+HBM = pl.BlockSpec(memory_space=pltpu.HBM)
 
 
 def after(x, *others):
@@ -66,12 +67,11 @@
         return copy
 
 
-def attend_kernel(first, slots, active, q, *refs):
+def attend_kernel(slots, active, q, *refs):
     kv, (part, stats), scratch = refs[: 2 * slots + 2], refs[2 * slots + 2 : 2 * slots + 4], refs[2 * slots + 4 :]
-    q_v, kv_v, total_v, peak_v, part_v, stats_v, sems = (*scratch[:1], scratch[1 : 2 * slots + 3], *scratch[2 * slots + 3 :])
+    q_v, kv_v, (part_v, total_v, peak_v, stats_v, sems) = scratch[0], scratch[1 : 2 * slots + 3], scratch[2 * slots + 3 :]
     fetch = Fetch(sems)
-    at = pl.ds(first * HEAD_DIM, q_v.shape[1])
-    copies = [fetch(source.at[:, at], target) for source, target in zip((q, *kv), (q_v, *kv_v))]
+    copies = [fetch(source, target) for source, target in zip((q, *kv), (q_v, *kv_v))]
     for copy in copies[:3]:
         copy.wait()
     state = (part_v, total_v, peak_v)
@@ -95,10 +95,11 @@
         copy.wait()
 
 
-def attend(active, q, kv, first, heads):
-    rows, columns, slots = q.shape[0], heads * HEAD_DIM, len(kv) // 2 - 1
+def attend(active, q, kv):
+    rows, columns = q.shape
+    slots = len(kv) // 2 - 1
     return pl.pallas_call(
-        functools.partial(attend_kernel, first, slots),
+        functools.partial(attend_kernel, slots),
         out_shape=[
             jax.ShapeDtypeStruct((rows, columns), jnp.float32),
             jax.ShapeDtypeStruct((rows, HEAD_DIM), jnp.float32),
@@ -122,14 +123,14 @@
     columns = state[0].shape[1]
     copies = [
         fetch(q.at[:, pl.ds(first * HEAD_DIM, columns)], q_v),
-        fetch(part, state[0]),
+        fetch(part.at[:, pl.ds(first * HEAD_DIM, columns)], state[0]),
         fetch(stats, stats_v),
     ] + [fetch(source, target) for source, target in zip(near, near_v)]
     for copy in copies[:3]:
         copy.wait()
     stats_now = stats_v[...]
     for h in range(columns // HEAD_DIM):
-        for r, lane in zip(state[1:], (h, HEAD_DIM // 2 + h)):
+        for r, lane in zip(state[1:], (first + h, HEAD_DIM // 2 + first + h)):
             r[:, columns_of(h)] = jnp.broadcast_to(stats_now[:, lane : lane + 1], stats_now.shape)
     for slot, kv in enumerate(near_v):
         copies[3 + slot].wait()
@@ -155,7 +156,7 @@
 
 
 def close(active, q, state, near, first):
-    rows, columns = state[0].shape
+    rows, columns = q.shape[0], near[0].shape[1] // 2
     return pl.pallas_call(
         functools.partial(close_kernel, first, len(near)),
         out_shape=jax.ShapeDtypeStruct((rows, columns), jnp.bfloat16),
@@ -222,14 +223,18 @@
         state,
         stats_v,
         attention,
-        pl.ds(done, part.shape[1]),
+        pl.ds(done, q_v.shape[1]),
     )
-    for copy in late:
+    for copy in late[len(ready) + len(moves) :] + late[: len(ready)]:
         copy.wait()
     groups, _, columns = held.shape
-    step = 512 if columns % 512 == 0 else columns
+    step = 256 if columns % 256 == 0 else columns
     stores = []
     for group in range(groups):
+        for number, (_, _, at) in enumerate(moves):
+            known = at is not None and not at[0]
+            if (at[1] == group) if known else group == 0:
+                late[len(ready) + number].wait()
         for j in range(columns // step):
             at = pl.ds(group * columns + j * step, step)
             projected = jnp.dot(
@@ -248,15 +253,20 @@
     width = hidden.shape[1]
     groups = lax.axis_size("groups")
     control_rows = control[0].shape[0]
-    columns = state[0].shape[1]
+    columns = near[0].shape[1] // 2
     share = width // groups
     lists = (near, ready, weight, control)
     counts = tuple(len(x) for x in lists)
-    step = 512 if share % 512 == 0 else share
+    step = 256 if share % 256 == 0 else share
     return pl.pallas_call(
         functools.partial(finish_kernel, counts, moves, control_rows),
         out_shape=jax.ShapeDtypeStruct((rows, width), jnp.bfloat16),
-        in_specs=[SMEM] * 2 + [ANY] * (4 + sum(counts)),
+        in_specs=[SMEM] * 2
+        + [HBM]
+        + [ANY] * (2 + len(near) + len(ready))
+        + [HBM]
+        + [ANY] * (len(weight) - 1 + len(control))
+        + [HBM],
         out_specs=ANY,
         scratch_shapes=close_scratch(rows, columns, len(near))
         + [
@@ -275,22 +285,6 @@
     )(place, active, q, *state, *near, *ready, *weight, *control, hidden)
 
 
-def tied_kernel(x, other, out):
-    del x, other, out
-
-
-def tied(x, other):
-    return pl.pallas_call(
-        tied_kernel,
-        out_shape=jax.ShapeDtypeStruct(x.shape, x.dtype),
-        in_specs=[ANY, ANY],
-        out_specs=ANY,
-        input_output_aliases={0: 0},
-        cost_estimate=pl.CostEstimate(flops=0, bytes_accessed=0, transcendentals=0),
-        name="tied",
-    )(x, other)
-
-
 def flipped(block, axis, flip):
     return lax.ppermute(block, axis, [(i, i ^ flip) for i in range(lax.axis_size(axis))])
 
@@ -353,7 +347,7 @@
         return jnp.stack(active)
 
     early_active, late_active = flags(early), flags(late)
-    far_lane, near_lane, x_lane, y_lane, core_lane = (Lane() for _ in range(5))
+    far_lane, near_lane = Lane(), Lane()
 
     shard, share = out_weight.shape[0], width // groups
     line = out_weight[:, :share]
@@ -366,10 +360,9 @@
         line = jnp.concatenate([line, flipped(line, "outer", flip)])
         line_flips += [f ^ flip for f in line_flips]
         flip //= 2
-    own = lax.all_gather(line, ("groups", "pair", "core"))
     far = far_lane(swap("outer", 2), line)
     near = near_lane(swap("outer", 1), line)
-    last = near_lane(swap("outer", 1), far)
+    last = swap("outer", 1)(far)
 
     firsts = [sum(CHUNKS[:i]) for i in range(len(CHUNKS))]
     chunks = [
@@ -381,67 +374,51 @@
     control_sent = [
         lax.dynamic_index_in_dim(lines, across ^ d, 1, keepdims=False).reshape(block, width) for d in range(grid_width)
     ]
-    control_parts = [control_sent[0]] + [None] * (grid_width - 1)
-    control_parts[1] = swap(TILES, 1)(control_sent[1])
-    early_near = [[None, None] for _ in early]
-    for i, x in enumerate((keys, values)):
-        early_near[0][i] = core_lane(route_of(early[0][2]), x)
-
-    def early_along_x(i):
-        for slot in range(1, len(early)):
-            early_near[slot][i] = x_lane(route_of(early[slot][2]), (keys, values)[i])
+    control_parts = [control_sent[0]] + [swap(TILES, d)(control_sent[d]) for d in range(1, grid_width)]
+    early_near = [tuple(lax.ppermute(x, TILES, route) for x in (keys, values)) for _, _, route in early]
+    early_kv = [keys, values] + [x for kv in early_near for x in kv]
+    state = attend(early_active, queries, early_kv)
+    first = [kv[0] for kv in early_near[1:]] + control_parts[2:-1]
+    second = [kv[1] for kv in early_near[1:]] + control_parts[-1:]
 
     late_near = []
 
     def along_z(number, *others):
         lanes = (far_lane, near_lane)
-        others = others or ((), ())
         late_near.append(
-            [lanes[i % 2](route_of(route), chunks[number], *others[i % 2]) for i, (_, _, route) in enumerate(late)]
+            [lanes[i % 2](route_of(route), chunks[number], *others) for i, (_, _, route) in enumerate(late)]
         )
 
-    x_lane.last = (line,)
-    early_along_x(0)
-    for d in range(2, grid_width - 1):
-        control_parts[d] = swap(TILES, d)(control_sent[d])
-    first = [far, near] + control_parts[2:-1]
     along_z(0)
-    far_x, near_x = (x_lane(swap("pair", 1), x, *first) for x in (far, near))
-    last_x = x_lane(swap("pair", 1), last)
-    early_along_x(1)
-    control_parts[-1] = x_lane(swap(TILES, grid_width - 1), tied(control_sent[-1], own))
-    plane = jnp.concatenate([far, near, far_x, near_x])
-    plane_y = y_lane(swap("groups", 1), plane, *late_near[0])
-    along_z(1, (), (last_x,))
-    plane_last = jnp.concatenate([last, last_x])
-    plane_last_y = y_lane(swap("groups", 1), plane_last, *late_near[1])
+    along_z(1)
     along_z(2)
-    along_z(3)
-    held = [plane, plane_y, plane_last, plane_last_y]
-    gates = [(), late_near[1] + [control_parts[-1]], (), late_near[2]]
-    crossed = [core_lane(swap("core", 1), x, *gate) for x, gate in zip(held, gates)]
+    most = lax.all_gather(
+        after(jnp.concatenate([line, far, near]), *first), ("groups", "pair", "core")
+    )
+    last_x = swap("pair", 1)(after(last, *late_near[0]))
+    plane = jnp.concatenate([last, last_x])
+    held = [plane, swap("groups", 1)(after(plane, *second))]
+    crossed = [swap("core", 1)(after(x, *late_near[1])) for x in held]
     n = len(line_flips)
     moves = [
-        (0, ((g * pair + p) * cores + c, i), (False, g, f, p, c))
+        (0, ((g * pair + p) * cores + c, i * n + j), (False, g, f ^ at, p, c))
         for g in range(groups)
         for p in range(pair)
         for c in range(cores)
-        for i, f in enumerate(line_flips)
+        for i, at in enumerate((0, 2, 1))
+        for j, f in enumerate(line_flips)
     ]
-    weight = [own]
-    for number, flips in enumerate(((2, 1), (2, 1), (3,), (3,))):
+    weight = [most]
+    for group_flip in range(2):
         for core_flip, pieces in enumerate((held, crossed)):
             moves += [
-                (len(weight), ((p * len(flips) + i) * n + j,), (True, number % 2, f ^ at, p, core_flip))
+                (len(weight), (p * n + j,), (True, group_flip, f ^ 3, p, core_flip))
                 for p in range(pair)
-                for i, at in enumerate(flips)
                 for j, f in enumerate(line_flips)
             ]
-            weight.append(pieces[number])
-
-    early_kv = [keys, values] + [x for kv in early_near for x in kv]
-    states = [attend(early_active, queries, early_kv, f, n) for f, n in zip(firsts, CHUNKS)]
-    ready = [close(late_active, queries, states[i], late_near[i], firsts[i]) for i in range(len(CHUNKS) - 1)]
+            weight.append(pieces[group_flip])
+
+    ready = [close(late_active, queries, state, late_near[i], firsts[i]) for i in range(len(CHUNKS) - 1)]
     if block % 16:
         control_parts = [
             jnp.take(
@@ -455,7 +432,7 @@
         place,
         late_active,
         queries,
-        states[-1],
+        state,
         late_near[-1],
         ready,
         weight,

time: 164 us -> 144 us (0.88)
  Pallas kernels: 29 us -> 19.3 us
  starting transfers between devices: 34.5 us -> 25.4 us
    ppermute x12 -> x6, starting transfers between devices: 17.6 us -> 4.28 us  [route_of(): return lambda block: lax.ppermute(block, TILES, route)]
    ppermute x12 -> x6, waiting for transfers between devices: 32.2 us -> 19.3 us  [route_of(): return lambda block: lax.ppermute(block, TILES, route)]
    ppermute x15 -> x10, waiting for transfers between devices: 25.9 us -> 38.5 us  [flipped(): lax.ppermute(block, axis, [(i, i ^ flip) for i in range(lax.axis_size(axi...]
    ppermute x0 -> x4, starting transfers between devices: none -> 9.6 us  [on_device(): lax.ppermute(x, TILES, route)]
    pallas_call x3 -> x2, Pallas kernels: 10.2 us -> 4.76 us  [close(): pl.pallas_call(functools.partial(close_kernel, first, len(near)), out_sha...]
    ppermute x15 -> x10, starting transfers between devices: 16.9 us -> 11.5 us  [flipped(): lax.ppermute(block, axis, [(i, i ^ flip) for i in range(lax.axis_size(axi...]
    pallas_call x5 -> x1, Pallas kernels: 10.3 us -> 5.97 us  [attend(): pl.pallas_call(functools.partial(attend_kernel, slots), out_shape=[jax.Sh...]
    concatenate x0 -> x1, other arithmetic: none -> 1.97 us  [on_device(): jnp.concatenate([line, far, near])]
  transfers between devices with their start and end apart: 28 -> 21, of which waited for: 8 -> 6; matrix products, arithmetic and copies ran while one was open for 8% -> 5% of each run, Pallas kernels for 13% -> 8%
where the time goes in v6:
time: 144 us; the launch traced here: 142 us
  waiting for transfers between devices  57.9 us (40%)
  starting transfers between devices  25.4 us (18%)
  Pallas kernels  19.3 us (13%)
  local copies, waits for them, and re-layouts  18.6 us (13%)
  between operations  16.3 us (11%)
  other arithmetic  4.08 us (3%)
    ppermute x10, waiting for transfers between devices, flipped(): lax.ppermute(block, axis, [(i, i ^ flip) for i in range(lax.axis_size(axi...  38.5 us
    ppermute x6, waiting for transfers between devices, route_of(): return lambda block: lax.ppermute(block, TILES, route)  19.3 us
    unnamed x57, local copies, waits for them, and re-layouts  14.9 us
    ppermute x10, starting transfers between devices, flipped(): lax.ppermute(block, axis, [(i, i ^ flip) for i in range(lax.axis_size(axi...  11.5 us
    ppermute x4, starting transfers between devices, on_device(): lax.ppermute(x, TILES, route)  9.6 us
    pallas_call x1, Pallas kernels, finish(): pl.pallas_call(functools.partial(finish_kernel, counts, moves, control_ro...  8.59 us
    pallas_call x1, Pallas kernels, attend(): pl.pallas_call(functools.partial(attend_kernel, slots), out_shape=[jax.Sh...  5.97 us
    pallas_call x2, Pallas kernels, close(): pl.pallas_call(functools.partial(close_kernel, first, len(near)), out_sha...  4.76 us
  transfers between devices with their start and end apart: 21, of which 6 were waited for; matrix products, arithmetic and copies ran while one was open for 5% of the time, Pallas kernels for 8%

profile of v6, /device:TPU:1, one launch (start us, length us, event | category | flops | bytes accessed | tf_op | source)
XLA Modules:
  0.0 141.5 jit_solution(3210939266252266996)
XLA Ops:
  6.5 1.1 slice_select_fusion
  7.6 2.2 %collective-permute-start.8 = (bf16[1,96,1536]{2,1,0:T(8,128)(2,1)S(1)}, bf16[1,96,1536]{2,1,0:T(8,128)(2,1)S(1)}, u32[]{:S(2)}, u32[]{:S(2)}) collective-permute-start(bf16[1,96,1536]{2,1,0:T(8,128)(2,1)S(1)} %bitcast.33), channel_id=1, source_target_pairs={{0,4},{4,0},{8,12},{12,8},{1,5},{5,1},{9,13},{13,9},{2,6},{6,2},{1... | collective-permute-start | bytes 884744 | tf_op jit(solution)/shard_map/ppermute | solution.py:289
  9.8 2.3 %collective-permute-start.4 = (bf16[1,96,1536]{2,1,0:T(8,128)(2,1)S(1)}, bf16[1,96,1536]{2,1,0:T(8,128)(2,1)}, u32[]{:S(2)}, u32[]{:S(2)}) collective-permute-start(bf16[1,96,1536]{2,1,0:T(8,128)(2,1)S(1)} %bitcast.34), channel_id=1, source_target_pairs={{0,8},{4,12},{8,0},{12,4},{1,9},{5,13},{9,1},{13,5},{2,10},{6,14},... | collective-permute-start | bytes 884744 | tf_op jit(solution)/shard_map/ppermute | solution.py:289
  12.1 4.2 %collective-permute-start.2 = (bf16[192,1536]{1,0:T(8,128)(2,1)}, bf16[192,1536]{1,0:T(8,128)(2,1)S(1)}, u32[]{:S(2)}, u32[]{:S(2)}) collective-permute-start(bf16[192,1536]{1,0:T(8,128)(2,1)} %refs_0_.1), channel_id=1, source_target_pairs={{1,2},{2,1},{5,6},{6,5},{9,10},{10,9},{13,14},{14,13},{17,18},{18,... | collective-permute-start | bytes 1769480 | tf_op jit(solution)/shard_map/ppermute | solution.py:378
  16.4 2.1 %dynamic-slice_bitcast_fusion = (bf16[48,3072]{1,0:T(8,128)(2,1)}, bf16[48,3072]{1,0:T(8,128)(2,1)S(1)}, bf16[48,3072]{1,0:T(8,128)(2,1)}, bf16[48,3072]{1,0:T(8,128)(2,1)S(1)}) fusion(bf16[6,4,8,3072]{3,2,1,0:T(8,128)(2,1)} %bitcast.36, s32[]{:T(128)S(6)} %select_n.109, s32[]{:T(128)S(6)} %select_n.108, s32[]{:T(128)S(6)} %select_n.107, s32[]{:T(128)S(6)} %select_n.106), kind=kLoop, calls=%fused_computation.3 | loop fusion | bytes 2359312 | tf_op jit(solution)/shard_map/reshape | solution.py:375
  18.6 4.3 %collective-permute-done.8 = bf16[1,96,1536]{2,1,0:T(8,128)(2,1)S(1)} collective-permute-done((bf16[1,96,1536]{2,1,0:T(8,128)(2,1)S(1)}, bf16[1,96,1536]{2,1,0:T(8,128)(2,1)S(1)}, u32[]{:S(2)}, u32[]{:S(2)}) %collective-permute-start.8) | collective-permute-done | bytes 294944 | tf_op jit(solution)/shard_map/ppermute | solution.py:289
  22.9 2.0 %pad_maximum_fusion = bf16[3,96,1536]{2,1,0:T(8,128)(2,1)} fusion(bf16[1,96,1536]{2,1,0:T(8,128)(2,1)S(1)} %collective-permute-done.8, bf16[1,96,1536]{2,1,0:T(8,128)(2,1)} %collective-permute-done.4, bf16[1,96,1536]{2,1,0:T(8,128)(2,1)S(1)} %bitcast.35), kind=kLoop, calls=%fused_computation | loop fusion | flops 884736 | bytes 1769472 | tf_op jit(solution)/shard_map/concatenate | solution.py:396
  24.8 4.9 %collective-permute-done.12.refs_11_ = bf16[48,3072]{1,0:T(8,128)(2,1)S(1)} collective-permute-done((bf16[48,3072]{1,0:T(8,128)(2,1)S(1)}, bf16[48,3072]{1,0:T(8,128)(2,1)S(1)}, u32[]{:S(2)}, u32[]{:S(2)}) %collective-permute-start.12) | collective-permute-done | bytes 294944 | tf_op jit(solution)/shard_map/ppermute | solution.py:289
  29.8 0.2 collective-permute-start.13
  30.0 1.4 collective-permute-start.9
  31.4 3.5 %collective-permute-start.3 = (bf16[192,1536]{1,0:T(8,128)(2,1)S(1)}, bf16[192,1536]{1,0:T(8,128)(2,1)S(1)}, u32[]{:S(2)}, u32[]{:S(2)}) collective-permute-start(bf16[192,1536]{1,0:T(8,128)(2,1)S(1)} %copy-done.3), channel_id=1, source_target_pairs={{1,2},{2,1},{5,6},{6,5},{9,10},{10,9},{13,14},{14,13},{17,18},{18,... | collective-permute-start | bytes 1769480 | tf_op jit(solution)/shard_map/ppermute | solution.py:378
  34.9 0.2 collective-permute-start.16
  35.2 10.4 %collective-permute-done.9.refs_1_ = bf16[192,512]{1,0:T(8,128)(2,1)S(1)} collective-permute-done((bf16[192,512]{1,0:T(8,128)(2,1)S(1)}, bf16[192,512]{1,0:T(8,128)(2,1)S(1)}, u32[]{:S(2)}, u32[]{:S(2)}) %collective-permute-start.9) | collective-permute-done | bytes 196640 | tf_op jit(solution)/shard_map/ppermute | solution.py:306
  45.6 3.2 %collective-permute-start.14 = (bf16[1,96,1536]{2,1,0:T(8,128)(2,1)S(1)}, bf16[1,96,1536]{2,1,0:T(8,128)(2,1)S(1)}, u32[]{:S(2)}, u32[]{:S(2)}) collective-permute-start(bf16[1,96,1536]{2,1,0:T(8,128)(2,1)S(1)} %collective-permute-done.13), channel_id=1, source_target_pairs={{0,2},{2,0},{1,3},{3,1},{4,6},{6,4},{5,7},{7,5},{8,10},{10,8},{9,1... | collective-permute-start | bytes 884744 | tf_op jit(solution)/shard_map/ppermute | solution.py:289
  48.9 0.7 collective-permute-start.6
  49.6 0.7 constant_dynamic-update-slice_fusion.1
  50.3 14.3 %collective-permute-done.14 = bf16[1,96,1536]{2,1,0:T(8,128)(2,1)S(1)} collective-permute-done((bf16[1,96,1536]{2,1,0:T(8,128)(2,1)S(1)}, bf16[1,96,1536]{2,1,0:T(8,128)(2,1)S(1)}, u32[]{:S(2)}, u32[]{:S(2)}) %collective-permute-start.14) | collective-permute-done | bytes 294944 | tf_op jit(solution)/shard_map/ppermute | solution.py:289
  64.6 0.7 constant_dynamic-update-slice_fusion.refs_5_
  65.3 0.7 copy-done.21
  66.0 0.5 collective-permute-start.17
  66.5 1.9 %collective-permute-start = (bf16[192,1536]{1,0:T(8,128)(2,1)S(1)}, bf16[192,1536]{1,0:T(8,128)(2,1)S(1)}, u32[]{:S(2)}, u32[]{:S(2)}) collective-permute-start(bf16[192,1536]{1,0:T(8,128)(2,1)S(1)} %copy-done.2), channel_id=1, source_target_pairs={{0,1},{1,0},{2,3},{3,2},{4,5},{5,4},{6,7},{7,6},{8,9},{9,8},{10,11... | collective-permute-start | bytes 1769480 | tf_op jit(solution)/shard_map/ppermute | solution.py:378
  68.4 8.9 %collective-permute-done.6.refs_0_ = bf16[192,1536]{1,0:T(8,128)(2,1)S(1)} collective-permute-done((bf16[192,1536]{1,0:T(8,128)(2,1)S(1)}, bf16[192,1536]{1,0:T(8,128)(2,1)S(1)}, u32[]{:S(2)}, u32[]{:S(2)}) %collective-permute-start.6) | collective-permute-done | bytes 589856 | tf_op jit(solution)/shard_map/ppermute | solution.py:306
  77.3 0.9 copy-done.17
  78.1 0.7 collective-permute-start.15
  78.8 15.1 %collective-permute-done.17.refs_7_ = bf16[2,96,1536]{2,1,0:T(8,128)(2,1)} collective-permute-done((bf16[2,96,1536]{2,1,0:T(8,128)(2,1)}, bf16[2,96,1536]{2,1,0:T(8,128)(2,1)}, u32[]{:S(2)}, u32[]{:S(2)}) %collective-permute-start.17) | collective-permute-done | bytes 589856 | tf_op jit(solution)/shard_map/ppermute | solution.py:289
  93.9 1.7 %collective-permute-start.18 = (bf16[2,96,1536]{2,1,0:T(8,128)(2,1)}, bf16[2,96,1536]{2,1,0:T(8,128)(2,1)}, u32[]{:S(2)}, u32[]{:S(2)}) collective-permute-start(bf16[2,96,1536]{2,1,0:T(8,128)(2,1)} %collective-permute-done.17.refs_7_), channel_id=1, source_target_pairs={{0,1},{1,0},{2,3},{3,2},{4,5},{5,4},{6,7},{7,6},{8,9},{9,8},{10,11... | collective-permute-start | bytes 1769480 | tf_op jit(solution)/shard_map/ppermute | solution.py:289
  95.6 0.8 pad_maximum_fusion.2
  96.4 2.0 %collective-permute-start.7 = (bf16[192,1024]{1,0:T(8,128)(2,1)}, bf16[192,1024]{1,0:T(8,128)(2,1)}, u32[]{:S(2)}, u32[]{:S(2)}) collective-permute-start(bf16[192,1024]{1,0:T(8,128)(2,1)} %pad_maximum_fusion.2), channel_id=1, source_target_pairs={{0,8},{8,0},{1,9},{9,1},{2,10},{10,2},{3,11},{11,3},{4,12},{12,4},... | collective-permute-start | bytes 1179656 | tf_op jit(solution)/shard_map/ppermute | solution.py:306
  98.5 0.8 copy-done.11
  99.3 0.1 collective-permute-start.11
  99.4 0.7 constant_dynamic-slice_fusion.1
  101.3 0.8 copy-done.13
  102.2 0.6 collective-permute-start.19
  102.7 0.1 add_convert_fusion.active
  104.1 0.1 stack.49.place
  104.3 1.1 copy-done.8
  105.4 1.1 copy-done.10
  106.4 1.1 copy-done.12
  107.5 1.1 copy-done.14
  108.6 6.0 %attend.1 = (f32[192,1536]{1,0:T(8,128)S(1)}, f32[192,128]{1,0:T(8,128)S(1)}) custom-call(s32[2]{0:T(128)S(1)} %add_convert_fusion.1.active, bf16[192,1536]{1,0:T(8,128)(2,1)S(1)} %copy-done, bf16[192,1536]{1,0:T(8,128)(2,1)S(1)} %copy-done.2, bf16[192,1536]{1,0:T(8,128)(2,1)S(1)} %copy-done.3, bf16[192,1536]{1,0:T(8,128)(2,1)S(1)} %copy-done.12, ...), custom_call_target="tpu_custom_call" | custom-call | flops 1019215872 | bytes 5308416 | tf_op jit(solution)/shard_map/attend/pallas_call | solution.py:101
  114.6 2.3 %close.2.refs_2_ = bf16[192,256]{1,0:T(8,128)(2,1)S(1)} custom-call(s32[2]{0:T(128)S(1)} %add_convert_fusion.active, bf16[192,1536]{1,0:T(8,128)(2,1)S(1)} %copy-done, f32[192,1536]{1,0:T(8,128)S(1)} %get-tuple-element.19.part, f32[192,128]{1,0:T(8,128)S(1)} %get-tuple-element.20.stats, bf16[192,512]{1,0:T(8,128)(2,1)S(1)} %copy-done.26, ...), custom_call_target="tpu_custom_call" | custom-call | flops 113246208 | bytes 786432 | tf_op jit(solution)/shard_map/close/pallas_call | solution.py:160
  116.9 2.5 %close.3.refs_3_ = bf16[192,768]{1,0:T(8,128)(2,1)S(1)} custom-call(s32[2]{0:T(128)S(1)} %add_convert_fusion.active, bf16[192,1536]{1,0:T(8,128)(2,1)S(1)} %copy-done, f32[192,1536]{1,0:T(8,128)S(1)} %get-tuple-element.19.part, f32[192,128]{1,0:T(8,128)S(1)} %get-tuple-element.20.stats, bf16[192,1536]{1,0:T(8,128)(2,1)S(1)} %copy-done.16, ...), custom_call_target="tpu_custom_call" | custom-call | flops 339738624 | bytes 2359296 | tf_op jit(solution)/shard_map/close/pallas_call | solution.py:160
  119.4 0.7 copy-done.5
  120.2 3.0 %copy-done.1 = bf16[24,96,1536]{2,1,0:T(8,128)(2,1)S(1)} copy-done((bf16[24,96,1536]{2,1,0:T(8,128)(2,1)S(1)}, bf16[24,96,1536]{2,1,0:T(8,128)(2,1)}, u32[]{:S(2)}) %copy-start.1) | copy-done | bytes 7077912
  123.2 1.0 copy-done.6
  124.2 1.0 copy-done.20
  125.1 1.0 copy-done.22
  126.1 8.6 %finish.1 = bf16[192,3072]{1,0:T(8,128)(2,1)} custom-call(s32[5]{0:T(128)S(1)} %stack.49.place, s32[2]{0:T(128)S(1)} %add_convert_fusion.active, bf16[192,1536]{1,0:T(8,128)(2,1)S(1)} %copy-done, f32[192,1536]{1,0:T(8,128)S(1)} %get-tuple-element.19.part, f32[192,128]{1,0:T(8,128)S(1)} %get-tuple-element.20.stats, ...), custom_call_target="tpu_custom_call" | custom-call | flops 1811939328 | bytes 12976128 | tf_op jit(solution)/shard_map/finish/pallas_call | solution.py:261
  (74 shorter events, 0.4 us)
Async XLA Ops:
  6.5 113.6 %all-gather.3.cloned.1.call-start = ((), (), s32[]{:S(2)}) async-start(), calls=%async_computation | async-start | bytes 7962624 | tf_op jit(solution)/shard_map/all_gather | solution.py:395
  7.6 15.2 %collective-permute-start.8 = (bf16[1,96,1536]{2,1,0:T(8,128)(2,1)S(1)}, bf16[1,96,1536]{2,1,0:T(8,128)(2,1)S(1)}, u32[]{:S(2)}, u32[]{:S(2)}) collective-permute-start(bf16[1,96,1536]{2,1,0:T(8,128)(2,1)S(1)} %bitcast.33), channel_id=1, source_target_pairs={{0,4},{4,0},{8,12},{12,8},{1,5},{5,1},{9,13},{13,9},{2,6},{6,2},{1... | collective-permute-start | bytes 884744 | tf_op jit(solution)/shard_map/ppermute | solution.py:289
  9.8 13.0 %collective-permute-start.4 = (bf16[1,96,1536]{2,1,0:T(8,128)(2,1)S(1)}, bf16[1,96,1536]{2,1,0:T(8,128)(2,1)}, u32[]{:S(2)}, u32[]{:S(2)}) collective-permute-start(bf16[1,96,1536]{2,1,0:T(8,128)(2,1)S(1)} %bitcast.34), channel_id=1, source_target_pairs={{0,8},{4,12},{8,0},{12,4},{1,9},{5,13},{9,1},{13,5},{2,10},{6,14},... | collective-permute-start | bytes 884744 | tf_op jit(solution)/shard_map/ppermute | solution.py:289
  12.1 17.6 %collective-permute-start.2 = (bf16[192,1536]{1,0:T(8,128)(2,1)}, bf16[192,1536]{1,0:T(8,128)(2,1)S(1)}, u32[]{:S(2)}, u32[]{:S(2)}) collective-permute-start(bf16[192,1536]{1,0:T(8,128)(2,1)} %refs_0_.1), channel_id=1, source_target_pairs={{1,2},{2,1},{5,6},{6,5},{9,10},{10,9},{13,14},{14,13},{17,18},{18,... | collective-permute-start | bytes 1769480 | tf_op jit(solution)/shard_map/ppermute | solution.py:378
  18.5 11.2 %copy-start.2 = (bf16[192,1536]{1,0:T(8,128)(2,1)S(1)}, bf16[192,1536]{1,0:T(8,128)(2,1)}, u32[]{:S(2)}) copy-start(bf16[192,1536]{1,0:T(8,128)(2,1)} %refs_0_.1) | copy-start | bytes 1769476
  18.5 11.5 %slice-start = ((bf16[192,1536]{1,0:T(8,128)(2,1)}), bf16[192,256]{1,0:T(8,128)(2,1)S(1)}, s32[]{:S(2)}) async-start(bf16[192,1536]{1,0:T(8,128)(2,1)} %refs_1_.1), calls=%async_computation.1 | async-start | bytes 196608 | tf_op jit(solution)/shard_map/slice | solution.py:369
  18.5 11.2 %collective-permute-start.12 = (bf16[48,3072]{1,0:T(8,128)(2,1)S(1)}, bf16[48,3072]{1,0:T(8,128)(2,1)S(1)}, u32[]{:S(2)}, u32[]{:S(2)}) collective-permute-start(bf16[48,3072]{1,0:T(8,128)(2,1)S(1)} %get-tuple-element.36), channel_id=1, source_target_pairs={{0,2},{1,3},{2,0},{3,1},{4,6},{5,7},{6,4},{7,5},{8,10},{9,11},{10,... | collective-permute-start | bytes 884744 | tf_op jit(solution)/shard_map/ppermute | solution.py:289
  24.8 6.6 %copy-start.3 = (bf16[192,1536]{1,0:T(8,128)(2,1)S(1)}, bf16[192,1536]{1,0:T(8,128)(2,1)}, u32[]{:S(2)}) copy-start(bf16[192,1536]{1,0:T(8,128)(2,1)} %refs_1_.1) | copy-start | bytes 1769476
  29.7 1.7 %copy-start.19 = (bf16[48,3072]{1,0:T(8,128)(2,1)}, bf16[48,3072]{1,0:T(8,128)(2,1)S(1)}, u32[]{:S(2)}) copy-start(bf16[48,3072]{1,0:T(8,128)(2,1)S(1)} %collective-permute-done.12.refs_11_) | copy-start | bytes 884740
  29.7 5.5 %copy-start.7 = (bf16[192,1536]{1,0:T(8,128)(2,1)}, bf16[192,1536]{1,0:T(8,128)(2,1)S(1)}, u32[]{:S(2)}) copy-start(bf16[192,1536]{1,0:T(8,128)(2,1)S(1)} %collective-permute-done.2.refs_4_) | copy-start | bytes 1769476
  29.8 15.9 %collective-permute-start.13 = (bf16[1,96,1536]{2,1,0:T(8,128)(2,1)}, bf16[1,96,1536]{2,1,0:T(8,128)(2,1)S(1)}, u32[]{:S(2)}, u32[]{:S(2)}) collective-permute-start(bf16[1,96,1536]{2,1,0:T(8,128)(2,1)} %collective-permute-done.4), channel_id=1, source_target_pairs={{0,4},{4,0},{8,12},{12,8},{1,5},{5,1},{9,13},{13,9},{2,6},{6,2},{1... | collective-permute-start | bytes 884744 | tf_op jit(solution)/shard_map/ppermute | solution.py:289
  30.0 15.6 %collective-permute-start.9 = (bf16[192,512]{1,0:T(8,128)(2,1)S(1)}, bf16[192,512]{1,0:T(8,128)(2,1)S(1)}, u32[]{:S(2)}, u32[]{:S(2)}) collective-permute-start(bf16[192,512]{1,0:T(8,128)(2,1)S(1)} %pad_maximum_fusion.3), channel_id=1, source_target_pairs={{0,4},{4,0},{1,5},{5,1},{2,6},{6,2},{3,7},{7,3},{8,12},{12,8},{9,1... | collective-permute-start | bytes 589832 | tf_op jit(solution)/shard_map/ppermute | solution.py:306
  31.4 14.3 %collective-permute-start.5 = (bf16[192,512]{1,0:T(8,128)(2,1)S(1)}, bf16[192,512]{1,0:T(8,128)(2,1)S(1)}, u32[]{:S(2)}, u32[]{:S(2)}) collective-permute-start(bf16[192,512]{1,0:T(8,128)(2,1)S(1)} %pad_maximum_fusion.3), channel_id=1, source_target_pairs={{0,8},{8,0},{1,9},{9,1},{2,10},{10,2},{3,11},{11,3},{4,12},{12,4},... | collective-permute-start | bytes 589832 | tf_op jit(solution)/shard_map/ppermute | solution.py:306
  31.4 34.6 %collective-permute-start.3 = (bf16[192,1536]{1,0:T(8,128)(2,1)S(1)}, bf16[192,1536]{1,0:T(8,128)(2,1)S(1)}, u32[]{:S(2)}, u32[]{:S(2)}) collective-permute-start(bf16[192,1536]{1,0:T(8,128)(2,1)S(1)} %copy-done.3), channel_id=1, source_target_pairs={{1,2},{2,1},{5,6},{6,5},{9,10},{10,9},{13,14},{14,13},{17,18},{18,... | collective-permute-start | bytes 1769480 | tf_op jit(solution)/shard_map/ppermute | solution.py:378
  34.9 30.4 %collective-permute-start.16 = (bf16[48,3072]{1,0:T(8,128)(2,1)}, bf16[48,3072]{1,0:T(8,128)(2,1)S(1)}, u32[]{:S(2)}, u32[]{:S(2)}) collective-permute-start(bf16[48,3072]{1,0:T(8,128)(2,1)} %get-tuple-element.35), channel_id=1, source_target_pairs={{0,3},{1,2},{2,1},{3,0},{4,7},{5,6},{6,5},{7,4},{8,11},{9,10},{10,... | collective-permute-start | bytes 884744 | tf_op jit(solution)/shard_map/ppermute | solution.py:289
  45.6 4.0 %copy-start.23 = (bf16[192,512]{1,0:T(8,128)(2,1)}, bf16[192,512]{1,0:T(8,128)(2,1)S(1)}, u32[]{:S(2)}) copy-start(bf16[192,512]{1,0:T(8,128)(2,1)S(1)} %collective-permute-done.9.refs_1_) | copy-start | bytes 589828
  45.6 4.0 %copy-start.25 = (bf16[192,512]{1,0:T(8,128)(2,1)}, bf16[192,512]{1,0:T(8,128)(2,1)S(1)}, u32[]{:S(2)}) copy-start(bf16[192,512]{1,0:T(8,128)(2,1)S(1)} %collective-permute-done.5.refs_0_) | copy-start | bytes 589828
  45.6 18.9 %collective-permute-start.14 = (bf16[1,96,1536]{2,1,0:T(8,128)(2,1)S(1)}, bf16[1,96,1536]{2,1,0:T(8,128)(2,1)S(1)}, u32[]{:S(2)}, u32[]{:S(2)}) collective-permute-start(bf16[1,96,1536]{2,1,0:T(8,128)(2,1)S(1)} %collective-permute-done.13), channel_id=1, source_target_pairs={{0,2},{2,0},{1,3},{3,1},{4,6},{6,4},{5,7},{7,5},{8,10},{10,8},{9,1... | collective-permute-start | bytes 884744 | tf_op jit(solution)/shard_map/ppermute | solution.py:289
  48.9 28.4 %collective-permute-start.6 = (bf16[192,1536]{1,0:T(8,128)(2,1)S(1)}, bf16[192,1536]{1,0:T(8,128)(2,1)S(1)}, u32[]{:S(2)}, u32[]{:S(2)}) collective-permute-start(bf16[192,1536]{1,0:T(8,128)(2,1)S(1)} %pad_maximum_fusion.1), channel_id=1, source_target_pairs={{0,8},{8,0},{1,9},{9,1},{2,10},{10,2},{3,11},{11,3},{4,12},{12,4},... | collective-permute-start | bytes 1769480 | tf_op jit(solution)/shard_map/ppermute | solution.py:306
  49.6 27.7 %collective-permute-start.10 = (bf16[192,1536]{1,0:T(8,128)(2,1)S(1)}, bf16[192,1536]{1,0:T(8,128)(2,1)S(1)}, u32[]{:S(2)}, u32[]{:S(2)}) collective-permute-start(bf16[192,1536]{1,0:T(8,128)(2,1)S(1)} %pad_maximum_fusion.1), channel_id=1, source_target_pairs={{0,4},{4,0},{1,5},{5,1},{2,6},{6,2},{3,7},{7,3},{8,12},{12,8},{9,1... | collective-permute-start | bytes 1769480 | tf_op jit(solution)/shard_map/ppermute | solution.py:306
  50.3 49.1 %copy-start.27 = (s32[1,6]{1,0:T(1,128)S(1)}, s32[1,6]{1,0:T(1,128)}, u32[]{:S(2)}) copy-start(s32[1,6]{1,0:T(1,128)} %param.13) | copy-start | bytes 76
  50.3 54.0 %copy-start = (bf16[192,1536]{1,0:T(8,128)(2,1)S(1)}, bf16[192,1536]{1,0:T(8,128)(2,1)}, u32[]{:S(2)}) copy-start(bf16[192,1536]{1,0:T(8,128)(2,1)} %q.7) | copy-start | bytes 1769476
  66.0 38.2 %copy-start.9 = (bf16[192,1536]{1,0:T(8,128)(2,1)}, bf16[192,1536]{1,0:T(8,128)(2,1)S(1)}, u32[]{:S(2)}) copy-start(bf16[192,1536]{1,0:T(8,128)(2,1)S(1)} %collective-permute-done.3.refs_5_) | copy-start | bytes 1769476
  66.0 27.8 %collective-permute-start.17 = (bf16[2,96,1536]{2,1,0:T(8,128)(2,1)}, bf16[2,96,1536]{2,1,0:T(8,128)(2,1)}, u32[]{:S(2)}, u32[]{:S(2)}) collective-permute-start(bf16[2,96,1536]{2,1,0:T(8,128)(2,1)} %constant_dynamic-update-slice_fusion.refs_5_), channel_id=1, source_target_pairs={{0,16},{16,0},{1,17},{17,1},{2,18},{18,2},{3,19},{19,3},{4,20},{20... | collective-permute-start | bytes 1769480 | tf_op jit(solution)/shard_map/ppermute | solution.py:289
  66.5 31.9 %collective-permute-start = (bf16[192,1536]{1,0:T(8,128)(2,1)S(1)}, bf16[192,1536]{1,0:T(8,128)(2,1)S(1)}, u32[]{:S(2)}, u32[]{:S(2)}) collective-permute-start(bf16[192,1536]{1,0:T(8,128)(2,1)S(1)} %copy-done.2), channel_id=1, source_target_pairs={{0,1},{1,0},{2,3},{3,2},{4,5},{5,4},{6,7},{7,6},{8,9},{9,8},{10,11... | collective-permute-start | bytes 1769480 | tf_op jit(solution)/shard_map/ppermute | solution.py:378
  68.4 32.9 %collective-permute-start.1 = (bf16[192,1536]{1,0:T(8,128)(2,1)S(1)}, bf16[192,1536]{1,0:T(8,128)(2,1)S(1)}, u32[]{:S(2)}, u32[]{:S(2)}) collective-permute-start(bf16[192,1536]{1,0:T(8,128)(2,1)S(1)} %copy-done.3), channel_id=1, source_target_pairs={{0,1},{1,0},{2,3},{3,2},{4,5},{5,4},{6,7},{7,6},{8,9},{9,8},{10,11... | collective-permute-start | bytes 1769480 | tf_op jit(solution)/shard_map/ppermute | solution.py:378
  77.3 21.2 %copy-start.15 = (bf16[192,1536]{1,0:T(8,128)(2,1)}, bf16[192,1536]{1,0:T(8,128)(2,1)S(1)}, u32[]{:S(2)}) copy-start(bf16[192,1536]{1,0:T(8,128)(2,1)S(1)} %collective-permute-done.6.refs_0_) | copy-start | bytes 1769476
  77.3 0.9 copy-start.17
  78.1 42.0 %collective-permute-start.15 = (bf16[2,96,1536]{2,1,0:T(8,128)(2,1)}, bf16[2,96,1536]{2,1,0:T(8,128)(2,1)}, u32[]{:S(2)}, u32[]{:S(2)}) collective-permute-start(bf16[2,96,1536]{2,1,0:T(8,128)(2,1)} %constant_dynamic-update-slice_fusion.refs_5_), channel_id=1, source_target_pairs={{0,1},{1,0},{2,3},{3,2},{4,5},{5,4},{6,7},{7,6},{8,9},{9,8},{10,11... | collective-permute-start | bytes 1769480 | tf_op jit(solution)/shard_map/ppermute | solution.py:289
  93.9 26.2 %collective-permute-start.18 = (bf16[2,96,1536]{2,1,0:T(8,128)(2,1)}, bf16[2,96,1536]{2,1,0:T(8,128)(2,1)}, u32[]{:S(2)}, u32[]{:S(2)}) collective-permute-start(bf16[2,96,1536]{2,1,0:T(8,128)(2,1)} %collective-permute-done.17.refs_7_), channel_id=1, source_target_pairs={{0,1},{1,0},{2,3},{3,2},{4,5},{5,4},{6,7},{7,6},{8,9},{9,8},{10,11... | collective-permute-start | bytes 1769480 | tf_op jit(solution)/shard_map/ppermute | solution.py:289
  96.4 23.7 %collective-permute-start.7 = (bf16[192,1024]{1,0:T(8,128)(2,1)}, bf16[192,1024]{1,0:T(8,128)(2,1)}, u32[]{:S(2)}, u32[]{:S(2)}) collective-permute-start(bf16[192,1024]{1,0:T(8,128)(2,1)} %pad_maximum_fusion.2), channel_id=1, source_target_pairs={{0,8},{8,0},{1,9},{9,1},{2,10},{10,2},{3,11},{11,3},{4,12},{12,4},... | collective-permute-start | bytes 1179656 | tf_op jit(solution)/shard_map/ppermute | solution.py:306
  98.5 0.8 copy-start.11
  99.3 20.8 %collective-permute-start.11 = (bf16[192,1024]{1,0:T(8,128)(2,1)}, bf16[192,1024]{1,0:T(8,128)(2,1)}, u32[]{:S(2)}, u32[]{:S(2)}) collective-permute-start(bf16[192,1024]{1,0:T(8,128)(2,1)} %pad_maximum_fusion.2), channel_id=1, source_target_pairs={{0,4},{4,0},{1,5},{5,1},{2,6},{6,2},{3,7},{7,3},{8,12},{12,8},{9,1... | collective-permute-start | bytes 1179656 | tf_op jit(solution)/shard_map/ppermute | solution.py:306
  101.3 0.8 copy-start.13
  102.2 17.9 %collective-permute-start.19 = (bf16[48,3072]{1,0:T(8,128)(2,1)}, bf16[48,3072]{1,0:T(8,128)(2,1)}, u32[]{:S(2)}, u32[]{:S(2)}) collective-permute-start(bf16[48,3072]{1,0:T(8,128)(2,1)} %get-tuple-element.33), channel_id=1, source_target_pairs={{0,1},{1,0},{2,3},{3,2},{4,5},{5,4},{6,7},{7,6},{8,9},{9,8},{10,11... | collective-permute-start | bytes 884744 | tf_op jit(solution)/shard_map/ppermute | solution.py:289
  104.3 1.1 copy-start.8
  105.4 1.1 copy-start.10
  106.4 1.1 copy-start.12
  107.5 1.1 copy-start.14
  108.6 6.0 %copy-start.24 = (bf16[192,512]{1,0:T(8,128)(2,1)S(1)}, bf16[192,512]{1,0:T(8,128)(2,1)}, u32[]{:S(2)}) copy-start(bf16[192,512]{1,0:T(8,128)(2,1)} %copy-done.23) | copy-start | bytes 589828
  108.6 6.0 %copy-start.26 = (bf16[192,512]{1,0:T(8,128)(2,1)S(1)}, bf16[192,512]{1,0:T(8,128)(2,1)}, u32[]{:S(2)}) copy-start(bf16[192,512]{1,0:T(8,128)(2,1)} %copy-done.25) | copy-start | bytes 589828
  114.6 2.3 %copy-start.16 = (bf16[192,1536]{1,0:T(8,128)(2,1)S(1)}, bf16[192,1536]{1,0:T(8,128)(2,1)}, u32[]{:S(2)}) copy-start(bf16[192,1536]{1,0:T(8,128)(2,1)} %copy-done.15) | copy-start | bytes 1769476
  114.6 2.3 %copy-start.18 = (bf16[192,1536]{1,0:T(8,128)(2,1)S(1)}, bf16[192,1536]{1,0:T(8,128)(2,1)}, u32[]{:S(2)}) copy-start(bf16[192,1536]{1,0:T(8,128)(2,1)} %copy-done.17) | copy-start | bytes 1769476
  116.9 3.3 %copy-start.4 = (bf16[192,3072]{1,0:T(8,128)(2,1)S(1)}, bf16[192,3072]{1,0:T(8,128)(2,1)}, u32[]{:S(2)}) copy-start(bf16[192,3072]{1,0:T(8,128)(2,1)} %refs_13_.1) | copy-start | bytes 3538948
  120.2 3.0 %copy-start.1 = (bf16[24,96,1536]{2,1,0:T(8,128)(2,1)S(1)}, bf16[24,96,1536]{2,1,0:T(8,128)(2,1)}, u32[]{:S(2)}) copy-start(bf16[24,96,1536]{2,1,0:T(8,128)(2,1)} %all-gather.3.cloned.1.call-done) | copy-start | bytes 21233668
  123.2 1.0 copy-start.6
  124.1 1.0 copy-start.20
  125.1 1.0 copy-start.22
  (2 other events, 1.4 us)
Sparse Core Ops, SparseCore 0:
  29.9 69.3 all-gather.2

commit v7 on v6

--- a/solution.py
+++ b/solution.py
@@ -11,13 +11,12 @@
 
 HEAD_DIM = 128
 TILE_W = 8
-CHUNKS = (2, 6, 4)
+CHUNKS = (6, 6)
 SCALE = HEAD_DIM**-0.5 * math.log2(math.e)
 TILES = ("outer", "pair", "core")
-VMEM_LIMIT = 24 * 1024 * 1024
+VMEM_LIMIT = 60 * 1024 * 1024
 SMEM = pl.BlockSpec(memory_space=pltpu.SMEM)
 ANY = pl.BlockSpec(memory_space=pl.ANY)
-HBM = pl.BlockSpec(memory_space=pltpu.HBM)
 
 
 def after(x, *others):
@@ -196,11 +195,9 @@
             if at is None:
                 target = held
             else:
-                flip, group, outer, pair, core = at
+                group, outer, pair, core = at
                 count = source.shape[0]
                 outer = place[1] ^ outer
-                if flip:
-                    group, pair, core = place[0] ^ group, place[2] ^ pair, place[3] ^ core
                 start = pl.multiple_of(((outer * 2 + pair) * 2 + core) * count, count)
                 target = held.at[group, pl.ds(start, count), :]
             late.append(late_fetch(source, target))
@@ -232,8 +229,7 @@
     stores = []
     for group in range(groups):
         for number, (_, _, at) in enumerate(moves):
-            known = at is not None and not at[0]
-            if (at[1] == group) if known else group == 0:
+            if group == (at[0] if at else 0):
                 late[len(ready) + number].wait()
         for j in range(columns // step):
             at = pl.ds(group * columns + j * step, step)
@@ -261,12 +257,7 @@
     return pl.pallas_call(
         functools.partial(finish_kernel, counts, moves, control_rows),
         out_shape=jax.ShapeDtypeStruct((rows, width), jnp.bfloat16),
-        in_specs=[SMEM] * 2
-        + [HBM]
-        + [ANY] * (2 + len(near) + len(ready))
-        + [HBM]
-        + [ANY] * (len(weight) - 1 + len(control))
-        + [HBM],
+        in_specs=[SMEM] * 2 + [ANY] * (4 + sum(counts)),
         out_specs=ANY,
         scratch_shapes=close_scratch(rows, columns, len(near))
         + [
@@ -374,50 +365,39 @@
     control_sent = [
         lax.dynamic_index_in_dim(lines, across ^ d, 1, keepdims=False).reshape(block, width) for d in range(grid_width)
     ]
-    control_parts = [control_sent[0]] + [swap(TILES, d)(control_sent[d]) for d in range(1, grid_width)]
-    early_near = [tuple(lax.ppermute(x, TILES, route) for x in (keys, values)) for _, _, route in early]
-    early_kv = [keys, values] + [x for kv in early_near for x in kv]
-    state = attend(early_active, queries, early_kv)
-    first = [kv[0] for kv in early_near[1:]] + control_parts[2:-1]
-    second = [kv[1] for kv in early_near[1:]] + control_parts[-1:]
-
-    late_near = []
-
-    def along_z(number, *others):
-        lanes = (far_lane, near_lane)
-        late_near.append(
-            [lanes[i % 2](route_of(route), chunks[number], *others) for i, (_, _, route) in enumerate(late)]
-        )
-
-    along_z(0)
-    along_z(1)
-    along_z(2)
-    most = lax.all_gather(
-        after(jnp.concatenate([line, far, near]), *first), ("groups", "pair", "core")
-    )
-    last_x = swap("pair", 1)(after(last, *late_near[0]))
-    plane = jnp.concatenate([last, last_x])
-    held = [plane, swap("groups", 1)(after(plane, *second))]
-    crossed = [swap("core", 1)(after(x, *late_near[1])) for x in held]
+    control_parts = list(control_sent)
+    early_near = [[None, None] for _ in early]
+    waits = (line,)
+    for i, x in enumerate((keys, values)):
+        sent = []
+        for slot in range(1, len(early)):
+            early_near[slot][i] = lax.ppermute(after(x, *waits), TILES, early[slot][2])
+            sent.append(early_near[slot][i])
+        for d in range(2 + i, grid_width, 2):
+            control_parts[d] = swap(TILES, d)(after(control_sent[d], *waits))
+            sent.append(control_parts[d])
+        waits = (far, near, *sent)
+    control_parts[1] = swap(TILES, 1)(control_sent[1])
+    for i, x in enumerate((keys, values)):
+        early_near[0][i] = lax.ppermute(x, TILES, early[0][2])
+    state = attend(early_active, queries, [keys, values] + [x for kv in early_near for x in kv])
+
+    steps = (line, far, near, last)
+    weight = [lax.all_gather(after(jnp.concatenate(steps), *sent), ("groups", "pair", "core"))]
     n = len(line_flips)
     moves = [
-        (0, ((g * pair + p) * cores + c, i * n + j), (False, g, f ^ at, p, c))
+        (0, ((g * pair + p) * cores + c, i * n + j), (g, f ^ at, p, c))
         for g in range(groups)
         for p in range(pair)
         for c in range(cores)
-        for i, at in enumerate((0, 2, 1))
+        for i, at in enumerate((0, 2, 1, 3))
         for j, f in enumerate(line_flips)
     ]
-    weight = [most]
-    for group_flip in range(2):
-        for core_flip, pieces in enumerate((held, crossed)):
-            moves += [
-                (len(weight), (p * n + j,), (True, group_flip, f ^ 3, p, core_flip))
-                for p in range(pair)
-                for j, f in enumerate(line_flips)
-            ]
-            weight.append(pieces[group_flip])
-
+
+    late_near = []
+    for chunk in chunks:
+        lanes = (far_lane, near_lane)
+        late_near.append([lanes[i % 2](route_of(route), chunk) for i, (_, _, route) in enumerate(late)])
     ready = [close(late_active, queries, state, late_near[i], firsts[i]) for i in range(len(CHUNKS) - 1)]
     if block % 16:
         control_parts = [
@@ -443,17 +423,12 @@
 
 
 def in_order(weight, moves, place, sizes):
-    groups, outer, pair, cores = sizes
-    shard, columns = weight[0].shape[-2:]
-    own = weight[0].reshape(groups, pair, cores, -1, shard, columns)
-    for axis, at in enumerate((0, 2, 3)):
-        own = jnp.take(own, jnp.arange(sizes[at], dtype=jnp.int32) ^ place[at], axis=axis)
-    weight = [own.reshape(weight[0].shape)] + weight[1:]
-    blocks = {at[1:]: weight[piece][index] for piece, index, at in moves}
-    whole = jnp.stack([blocks[at] for at in sorted(blocks)]).reshape(sizes + (shard, columns))
-    for axis, size in enumerate(sizes):
-        whole = jnp.take(whole, jnp.arange(size, dtype=jnp.int32) ^ place[axis], axis=axis)
-    return whole.reshape(groups, -1, columns)
+    blocks = {at: weight[piece][index] for piece, index, at in moves}
+    whole = jnp.stack([blocks[at] for at in sorted(blocks)])
+    shard, columns = whole.shape[1:]
+    whole = whole.reshape(sizes + (shard, columns))
+    whole = jnp.take(whole, jnp.arange(sizes[1], dtype=jnp.int32) ^ place[1], axis=1)
+    return whole.reshape(sizes[0], -1, columns)
 
 
 def solution(mesh):

time: 144 us -> 123 us (0.85)
  starting transfers between devices: 25.4 us -> 14.1 us
  local copies, waits for them, and re-layouts: 18.6 us -> 7.62 us
    ppermute x10 -> x6, waiting for transfers between devices: 38.5 us -> 23.2 us  [flipped(): lax.ppermute(block, axis, [(i, i ^ flip) for i in range(lax.axis_size(axi...]
    ppermute x6 -> x4, waiting for transfers between devices: 19.3 us -> 33.9 us  [route_of(): return lambda block: lax.ppermute(block, TILES, route)]
    unnamed x57 -> x24, local copies, waits for them, and re-layouts: 14.9 us -> 4.06 us
    ppermute x10 -> x6, starting transfers between devices: 11.5 us -> 6.33 us  [flipped(): lax.ppermute(block, axis, [(i, i ^ flip) for i in range(lax.axis_size(axi...]
    ppermute x6 -> x4, starting transfers between devices: 4.28 us -> 0.56 us  [route_of(): return lambda block: lax.ppermute(block, TILES, route)]
    ppermute x4, starting transfers between devices: 9.6 us -> 7.23 us  [the longest x2 6.72 us: on_device(): early_near[slot][i] = lax.ppermute(after(x, *waits), TILES, early[slot][2])]
    all_gather x1, waiting for transfers between devices: 0.02 us -> 1.69 us  [on_device(): lax.all_gather(after(jnp.concatenate(steps), *sent), ('groups', 'pair', '...]
    pallas_call x1, Pallas kernels: 8.59 us -> 10.1 us  [finish(): pl.pallas_call(functools.partial(finish_kernel, counts, moves, control_ro...]
  transfers between devices with their start and end apart: 21 -> 15, of which waited for: 6 -> 8; matrix products, arithmetic and copies ran while one was open for 5% -> 6% of each run, Pallas kernels for 8% -> 8%
where the time goes in v7:
time: 123 us; the launch traced here: 121 us
  waiting for transfers between devices  58.8 us (48%)
  Pallas kernels  20.2 us (16%)
  between operations  16.1 us (13%)
  starting transfers between devices  14.1 us (11%)
  local copies, waits for them, and re-layouts  7.62 us (6%)
  other arithmetic  4.47 us (4%)
    ppermute x4, waiting for transfers between devices, route_of(): return lambda block: lax.ppermute(block, TILES, route)  33.9 us
    ppermute x6, waiting for transfers between devices, flipped(): lax.ppermute(block, axis, [(i, i ^ flip) for i in range(lax.axis_size(axi...  23.2 us
    pallas_call x1, Pallas kernels, finish(): pl.pallas_call(functools.partial(finish_kernel, counts, moves, control_ro...  10.1 us
    ppermute x2, starting transfers between devices, on_device(): early_near[slot][i] = lax.ppermute(after(x, *waits), TILES, early[slot][2])  6.72 us
    ppermute x6, starting transfers between devices, flipped(): lax.ppermute(block, axis, [(i, i ^ flip) for i in range(lax.axis_size(axi...  6.33 us
    pallas_call x1, Pallas kernels, attend(): pl.pallas_call(functools.partial(attend_kernel, slots), out_shape=[jax.Sh...  5.98 us
    pallas_call x1, Pallas kernels, close(): pl.pallas_call(functools.partial(close_kernel, first, len(near)), out_sha...  4.13 us
    unnamed x24, local copies, waits for them, and re-layouts  4.06 us
  transfers between devices with their start and end apart: 15, of which 8 were waited for; matrix products, arithmetic and copies ran while one was open for 6% of the time, Pallas kernels for 8%

profile of v7, /device:TPU:1, one launch (start us, length us, event | category | flops | bytes accessed | tf_op | source)
XLA Modules:
  0.0 121.4 jit_solution(14157257166594291652)
XLA Ops:
  6.5 1.1 slice_select_fusion
  7.6 2.2 %collective-permute-start.4 = (bf16[1,96,1536]{2,1,0:T(8,128)(2,1)S(1)}, bf16[1,96,1536]{2,1,0:T(8,128)(2,1)S(1)}, u32[]{:S(2)}, u32[]{:S(2)}) collective-permute-start(bf16[1,96,1536]{2,1,0:T(8,128)(2,1)S(1)} %bitcast.33), channel_id=1, source_target_pairs={{0,4},{4,0},{8,12},{12,8},{1,5},{5,1},{9,13},{13,9},{2,6},{6,2},{1... | collective-permute-start | bytes 884744 | tf_op jit(solution)/shard_map/ppermute | solution.py:280
  9.8 2.3 %collective-permute-start.3 = (bf16[1,96,1536]{2,1,0:T(8,128)(2,1)S(1)}, bf16[1,96,1536]{2,1,0:T(8,128)(2,1)S(1)}, u32[]{:S(2)}, u32[]{:S(2)}) collective-permute-start(bf16[1,96,1536]{2,1,0:T(8,128)(2,1)S(1)} %bitcast.34), channel_id=1, source_target_pairs={{0,8},{4,12},{8,0},{12,4},{1,9},{5,13},{9,1},{13,5},{2,10},{6,14},... | collective-permute-start | bytes 884744 | tf_op jit(solution)/shard_map/ppermute | solution.py:280
  12.1 4.2 %collective-permute-start.2 = (bf16[192,1536]{1,0:T(8,128)(2,1)}, bf16[192,1536]{1,0:T(8,128)(2,1)S(1)}, u32[]{:S(2)}, u32[]{:S(2)}) collective-permute-start(bf16[192,1536]{1,0:T(8,128)(2,1)} %refs_0_.1), channel_id=1, source_target_pairs={{1,2},{2,1},{5,6},{6,5},{9,10},{10,9},{13,14},{14,13},{17,18},{18,... | collective-permute-start | bytes 1769480 | tf_op jit(solution)/shard_map/ppermute | solution.py:374
  16.4 0.0 copy-start.1
  16.4 2.2 %dynamic-slice_bitcast_fusion = (bf16[48,3072]{1,0:T(8,128)(2,1)}, bf16[48,3072]{1,0:T(8,128)(2,1)}, bf16[48,3072]{1,0:T(8,128)(2,1)S(1)}, bf16[48,3072]{1,0:T(8,128)(2,1)S(1)}) fusion(bf16[6,4,8,3072]{3,2,1,0:T(8,128)(2,1)} %bitcast.36, s32[]{:T(128)S(6)} %select_n.109, s32[]{:T(128)S(6)} %select_n.108, s32[]{:T(128)S(6)} %select_n.107, s32[]{:T(128)S(6)} %select_n.106), kind=kLoop, calls=%fused_computation.3 | loop fusion | bytes 2359312 | tf_op jit(solution)/shard_map/reshape | solution.py:366
  18.6 0.0 collective-permute-start.5
  18.6 4.1 %collective-permute-done.4 = bf16[1,96,1536]{2,1,0:T(8,128)(2,1)S(1)} collective-permute-done((bf16[1,96,1536]{2,1,0:T(8,128)(2,1)S(1)}, bf16[1,96,1536]{2,1,0:T(8,128)(2,1)S(1)}, u32[]{:S(2)}, u32[]{:S(2)}) %collective-permute-start.4) | collective-permute-done | bytes 294944 | tf_op jit(solution)/shard_map/ppermute | solution.py:280
  22.8 0.0 collective-permute-done.3
  22.8 6.9 %collective-permute-done.5.refs_6_ = bf16[48,3072]{1,0:T(8,128)(2,1)S(1)} collective-permute-done((bf16[48,3072]{1,0:T(8,128)(2,1)S(1)}, bf16[48,3072]{1,0:T(8,128)(2,1)S(1)}, u32[]{:S(2)}, u32[]{:S(2)}) %collective-permute-start.5) | collective-permute-done | bytes 294944 | tf_op jit(solution)/shard_map/ppermute | solution.py:280
  29.7 0.7 copy-done.9
  30.4 0.0 collective-permute-done.2.refs_4_
  30.4 2.5 %collective-permute-start.6 = (bf16[192,1536]{1,0:T(8,128)(2,1)S(1)}, bf16[192,1536]{1,0:T(8,128)(2,1)S(1)}, u32[]{:S(2)}, u32[]{:S(2)}) collective-permute-start(bf16[192,1536]{1,0:T(8,128)(2,1)S(1)} %copy-done.1), channel_id=1, source_target_pairs={{1,2},{2,1},{5,6},{6,5},{9,10},{10,9},{13,14},{14,13},{17,18},{18,... | collective-permute-start | bytes 1769480 | tf_op jit(solution)/shard_map/ppermute | solution.py:374
  32.9 0.2 collective-permute-start.11
  33.2 1.4 %collective-permute-start.12 = (bf16[48,3072]{1,0:T(8,128)(2,1)S(1)}, bf16[48,3072]{1,0:T(8,128)(2,1)S(1)}, u32[]{:S(2)}, u32[]{:S(2)}) collective-permute-start(bf16[48,3072]{1,0:T(8,128)(2,1)S(1)} %get-tuple-element.27), channel_id=1, source_target_pairs={{0,3},{1,2},{2,1},{3,0},{4,7},{5,6},{6,5},{7,4},{8,11},{9,10},{10,... | collective-permute-start | bytes 884744 | tf_op jit(solution)/shard_map/ppermute | solution.py:280
  34.6 7.3 %collective-permute-done.11 = bf16[1,96,1536]{2,1,0:T(8,128)(2,1)S(1)} collective-permute-done((bf16[1,96,1536]{2,1,0:T(8,128)(2,1)S(1)}, bf16[1,96,1536]{2,1,0:T(8,128)(2,1)S(1)}, u32[]{:S(2)}, u32[]{:S(2)}) %collective-permute-start.11) | collective-permute-done | bytes 294944 | tf_op jit(solution)/shard_map/ppermute | solution.py:280
  41.9 1.2 pad_maximum_fusion
  43.1 4.9 %collective-permute-done.12.refs_7_ = bf16[48,3072]{1,0:T(8,128)(2,1)S(1)} collective-permute-done((bf16[48,3072]{1,0:T(8,128)(2,1)S(1)}, bf16[48,3072]{1,0:T(8,128)(2,1)S(1)}, u32[]{:S(2)}, u32[]{:S(2)}) %collective-permute-start.12) | collective-permute-done | bytes 294944 | tf_op jit(solution)/shard_map/ppermute | solution.py:280
  47.9 0.0 collective-permute-done.6.refs_5_
  48.0 0.0 all-gather.3.cloned.1.call-update
  48.0 0.6 copy-done.10
  48.7 0.2 copy-done.3
  48.9 0.0 copy-start.11
  49.0 0.1 collective-permute-start.7
  49.1 0.2 collective-permute-start.9
  49.3 0.0 collective-permute-start
  49.3 0.5 collective-permute-start.1
  49.8 0.9 pad_maximum_fusion.1
  50.7 23.8 %collective-permute-done.7.refs_0_ = bf16[192,1536]{1,0:T(8,128)(2,1)} collective-permute-done((bf16[192,1536]{1,0:T(8,128)(2,1)S(1)}, bf16[192,1536]{1,0:T(8,128)(2,1)}, u32[]{:S(2)}, u32[]{:S(2)}) %collective-permute-start.7) | collective-permute-done | bytes 589856 | tf_op jit(solution)/shard_map/ppermute | solution.py:297
  74.4 0.0 collective-permute-start.8
  74.4 0.0 collective-permute-done.9.refs_1_
  74.5 0.8 copy-done.8
  75.3 0.2 collective-permute-start.10
  75.5 0.2 collective-permute-start.13
  75.7 0.7 constant_dynamic-slice_fusion.1
  77.6 0.7 add_convert_fusion.active
  79.6 0.6 stack.49.place
  80.2 0.7 add_convert_fusion.1.active
  80.8 0.0 collective-permute-done.refs_2_
  80.8 0.0 collective-permute-done.1.refs_3_
  80.9 0.8 copy-done.6
  81.7 0.8 copy-done.7
  82.5 6.0 %attend.1 = (f32[192,1536]{1,0:T(8,128)}, f32[192,128]{1,0:T(8,128)}) custom-call(s32[2]{0:T(128)} %add_convert_fusion.1.active, bf16[192,1536]{1,0:T(8,128)(2,1)} %q.5, bf16[192,1536]{1,0:T(8,128)(2,1)} %refs_0_.1, bf16[192,1536]{1,0:T(8,128)(2,1)} %refs_1_.1, bf16[192,1536]{1,0:T(8,128)(2,1)} %copy-done.6, bf16[192,1536]{1,0:T(8,128)(2,1)} %copy-done.7, ...), custom_call_target="tpu_custom_call" | custom-call | flops 1019215872 | bytes 5308416 | tf_op jit(solution)/shard_map/attend/pallas_call | solution.py:100
  88.5 4.1 %close.1.refs_2_ = bf16[192,768]{1,0:T(8,128)(2,1)} custom-call(s32[2]{0:T(128)} %add_convert_fusion.active, bf16[192,1536]{1,0:T(8,128)(2,1)} %q.5, f32[192,1536]{1,0:T(8,128)} %get-tuple-element.21.part, f32[192,128]{1,0:T(8,128)} %get-tuple-element.22.stats, bf16[192,1536]{1,0:T(8,128)(2,1)} %collective-permute-done.7.refs_0_, bf16[192,1536]{1,0:T(8,128)(2,1)} %copy-done.8), custom_call_target="tpu_custom_call" | custom-call | flops 339738624 | bytes 2359296 | tf_op jit(solution)/shard_map/close/pallas_call | solution.py:159
  92.6 8.2 %collective-permute-done.8.refs_0_ = bf16[192,1536]{1,0:T(8,128)(2,1)S(1)} collective-permute-done((bf16[192,1536]{1,0:T(8,128)(2,1)}, bf16[192,1536]{1,0:T(8,128)(2,1)S(1)}, u32[]{:S(2)}, u32[]{:S(2)}) %collective-permute-start.8) | collective-permute-done | bytes 589856 | tf_op jit(solution)/shard_map/ppermute | solution.py:297
  100.8 1.9 %collective-permute-done.10.refs_1_ = bf16[192,1536]{1,0:T(8,128)(2,1)S(1)} collective-permute-done((bf16[192,1536]{1,0:T(8,128)(2,1)}, bf16[192,1536]{1,0:T(8,128)(2,1)S(1)}, u32[]{:S(2)}, u32[]{:S(2)}) %collective-permute-start.10) | collective-permute-done | bytes 589856 | tf_op jit(solution)/shard_map/ppermute | solution.py:297
  102.7 1.7 %all-gather.3.cloned.1.call-done = bf16[32,96,1536]{2,1,0:T(8,128)(2,1)} async-done(((bf16[4,96,1536]{2,1,0:T(8,128)(2,1)}), bf16[32,96,1536]{2,1,0:T(8,128)(2,1)}) %all-gather.3.cloned.1.call-update) | async-done | bytes 9437200 | tf_op jit(solution)/shard_map/all_gather | solution.py:386
  104.4 10.1 %finish.1 = bf16[192,3072]{1,0:T(8,128)(2,1)} custom-call(s32[5]{0:T(128)} %stack.49.place, s32[2]{0:T(128)} %add_convert_fusion.active, bf16[192,1536]{1,0:T(8,128)(2,1)} %q.5, f32[192,1536]{1,0:T(8,128)} %get-tuple-element.21.part, f32[192,128]{1,0:T(8,128)} %get-tuple-element.22.stats, bf16[192,1536]{1,0:T(8,128)(2,1)} %copy-done.4, ...), custom_call_target="tpu_custom_call" | custom-call | flops 1811939328 | bytes 12976128 | tf_op jit(solution)/shard_map/finish/pallas_call | solution.py:257
  (21 shorter events, 0.2 us)
Async XLA Ops:
  6.5 97.9 %all-gather.3.cloned.1.call-start = ((), (), s32[]{:S(2)}) async-start(), calls=%async_computation | async-start | bytes 10616832 | tf_op jit(solution)/shard_map/all_gather | solution.py:386
  7.6 15.1 %collective-permute-start.4 = (bf16[1,96,1536]{2,1,0:T(8,128)(2,1)S(1)}, bf16[1,96,1536]{2,1,0:T(8,128)(2,1)S(1)}, u32[]{:S(2)}, u32[]{:S(2)}) collective-permute-start(bf16[1,96,1536]{2,1,0:T(8,128)(2,1)S(1)} %bitcast.33), channel_id=1, source_target_pairs={{0,4},{4,0},{8,12},{12,8},{1,5},{5,1},{9,13},{13,9},{2,6},{6,2},{1... | collective-permute-start | bytes 884744 | tf_op jit(solution)/shard_map/ppermute | solution.py:280
  9.8 12.9 %collective-permute-start.3 = (bf16[1,96,1536]{2,1,0:T(8,128)(2,1)S(1)}, bf16[1,96,1536]{2,1,0:T(8,128)(2,1)S(1)}, u32[]{:S(2)}, u32[]{:S(2)}) collective-permute-start(bf16[1,96,1536]{2,1,0:T(8,128)(2,1)S(1)} %bitcast.34), channel_id=1, source_target_pairs={{0,8},{4,12},{8,0},{12,4},{1,9},{5,13},{9,1},{13,5},{2,10},{6,14},... | collective-permute-start | bytes 884744 | tf_op jit(solution)/shard_map/ppermute | solution.py:280
  12.1 18.3 %collective-permute-start.2 = (bf16[192,1536]{1,0:T(8,128)(2,1)}, bf16[192,1536]{1,0:T(8,128)(2,1)S(1)}, u32[]{:S(2)}, u32[]{:S(2)}) collective-permute-start(bf16[192,1536]{1,0:T(8,128)(2,1)} %refs_0_.1), channel_id=1, source_target_pairs={{1,2},{2,1},{5,6},{6,5},{9,10},{10,9},{13,14},{14,13},{17,18},{18,... | collective-permute-start | bytes 1769480 | tf_op jit(solution)/shard_map/ppermute | solution.py:374
  16.4 14.0 %copy-start.1 = (bf16[192,1536]{1,0:T(8,128)(2,1)S(1)}, bf16[192,1536]{1,0:T(8,128)(2,1)}, u32[]{:S(2)}) copy-start(bf16[192,1536]{1,0:T(8,128)(2,1)} %refs_1_.1) | copy-start | bytes 1769476
  18.6 11.1 %collective-permute-start.5 = (bf16[48,3072]{1,0:T(8,128)(2,1)S(1)}, bf16[48,3072]{1,0:T(8,128)(2,1)S(1)}, u32[]{:S(2)}, u32[]{:S(2)}) collective-permute-start(bf16[48,3072]{1,0:T(8,128)(2,1)S(1)} %get-tuple-element.19), channel_id=1, source_target_pairs={{0,2},{1,3},{2,0},{3,1},{4,6},{5,7},{6,4},{7,5},{8,10},{9,11},{10,... | collective-permute-start | bytes 884744 | tf_op jit(solution)/shard_map/ppermute | solution.py:280
  29.7 0.7 copy-start.9
  30.4 12.7 %copy-start.2 = (bf16[192,1536]{1,0:T(8,128)(2,1)}, bf16[192,1536]{1,0:T(8,128)(2,1)S(1)}, u32[]{:S(2)}) copy-start(bf16[192,1536]{1,0:T(8,128)(2,1)S(1)} %collective-permute-done.2.refs_4_) | copy-start | bytes 1769476
  30.4 17.5 %collective-permute-start.6 = (bf16[192,1536]{1,0:T(8,128)(2,1)S(1)}, bf16[192,1536]{1,0:T(8,128)(2,1)S(1)}, u32[]{:S(2)}, u32[]{:S(2)}) collective-permute-start(bf16[192,1536]{1,0:T(8,128)(2,1)S(1)} %copy-done.1), channel_id=1, source_target_pairs={{1,2},{2,1},{5,6},{6,5},{9,10},{10,9},{13,14},{14,13},{17,18},{18,... | collective-permute-start | bytes 1769480 | tf_op jit(solution)/shard_map/ppermute | solution.py:374
  32.9 9.0 %collective-permute-start.11 = (bf16[1,96,1536]{2,1,0:T(8,128)(2,1)S(1)}, bf16[1,96,1536]{2,1,0:T(8,128)(2,1)S(1)}, u32[]{:S(2)}, u32[]{:S(2)}) collective-permute-start(bf16[1,96,1536]{2,1,0:T(8,128)(2,1)S(1)} %collective-permute-done.3), channel_id=1, source_target_pairs={{0,4},{4,0},{8,12},{12,8},{1,5},{5,1},{9,13},{13,9},{2,6},{6,2},{1... | collective-permute-start | bytes 884744 | tf_op jit(solution)/shard_map/ppermute | solution.py:280
  33.2 14.8 %collective-permute-start.12 = (bf16[48,3072]{1,0:T(8,128)(2,1)S(1)}, bf16[48,3072]{1,0:T(8,128)(2,1)S(1)}, u32[]{:S(2)}, u32[]{:S(2)}) collective-permute-start(bf16[48,3072]{1,0:T(8,128)(2,1)S(1)} %get-tuple-element.27), channel_id=1, source_target_pairs={{0,3},{1,2},{2,1},{3,0},{4,7},{5,6},{6,5},{7,4},{8,11},{9,10},{10,... | collective-permute-start | bytes 884744 | tf_op jit(solution)/shard_map/ppermute | solution.py:280
  43.1 4.9 %copy-start = (bf16[192,1536]{1,0:T(8,128)(2,1)S(1)}, bf16[192,1536]{1,0:T(8,128)(2,1)}, u32[]{:S(2)}) copy-start(bf16[192,1536]{1,0:T(8,128)(2,1)} %refs_0_.1) | copy-start | bytes 1769476
  47.9 0.7 copy-start.10
  48.0 0.9 copy-start.3
  48.9 26.8 %copy-start.11 = (s32[1,6]{1,0:T(1,128)S(1)}, s32[1,6]{1,0:T(1,128)}, u32[]{:S(2)}) copy-start(s32[1,6]{1,0:T(1,128)} %param.13) | copy-start | bytes 76
  49.0 25.5 %collective-permute-start.7 = (bf16[192,1536]{1,0:T(8,128)(2,1)S(1)}, bf16[192,1536]{1,0:T(8,128)(2,1)}, u32[]{:S(2)}, u32[]{:S(2)}) collective-permute-start(bf16[192,1536]{1,0:T(8,128)(2,1)S(1)} %pad_maximum_fusion.2), channel_id=1, source_target_pairs={{0,8},{8,0},{1,9},{9,1},{2,10},{10,2},{3,11},{11,3},{4,12},{12,4},... | collective-permute-start | bytes 1769480 | tf_op jit(solution)/shard_map/ppermute | solution.py:297
  49.1 25.4 %collective-permute-start.9 = (bf16[192,1536]{1,0:T(8,128)(2,1)S(1)}, bf16[192,1536]{1,0:T(8,128)(2,1)S(1)}, u32[]{:S(2)}, u32[]{:S(2)}) collective-permute-start(bf16[192,1536]{1,0:T(8,128)(2,1)S(1)} %pad_maximum_fusion.2), channel_id=1, source_target_pairs={{0,4},{4,0},{1,5},{5,1},{2,6},{6,2},{3,7},{7,3},{8,12},{12,8},{9,1... | collective-permute-start | bytes 1769480 | tf_op jit(solution)/shard_map/ppermute | solution.py:297
  49.3 31.6 %collective-permute-start = (bf16[192,1536]{1,0:T(8,128)(2,1)S(1)}, bf16[192,1536]{1,0:T(8,128)(2,1)S(1)}, u32[]{:S(2)}, u32[]{:S(2)}) collective-permute-start(bf16[192,1536]{1,0:T(8,128)(2,1)S(1)} %copy-done), channel_id=1, source_target_pairs={{0,1},{1,0},{2,3},{3,2},{4,5},{5,4},{6,7},{7,6},{8,9},{9,8},{10,11... | collective-permute-start | bytes 1769480 | tf_op jit(solution)/shard_map/ppermute | solution.py:382
  49.3 31.6 %collective-permute-start.1 = (bf16[192,1536]{1,0:T(8,128)(2,1)S(1)}, bf16[192,1536]{1,0:T(8,128)(2,1)S(1)}, u32[]{:S(2)}, u32[]{:S(2)}) collective-permute-start(bf16[192,1536]{1,0:T(8,128)(2,1)S(1)} %copy-done.1), channel_id=1, source_target_pairs={{0,1},{1,0},{2,3},{3,2},{4,5},{5,4},{6,7},{7,6},{8,9},{9,8},{10,11... | collective-permute-start | bytes 1769480 | tf_op jit(solution)/shard_map/ppermute | solution.py:382
  74.4 26.4 %collective-permute-start.8 = (bf16[192,1536]{1,0:T(8,128)(2,1)}, bf16[192,1536]{1,0:T(8,128)(2,1)S(1)}, u32[]{:S(2)}, u32[]{:S(2)}) collective-permute-start(bf16[192,1536]{1,0:T(8,128)(2,1)} %pad_maximum_fusion.1), channel_id=1, source_target_pairs={{0,8},{8,0},{1,9},{9,1},{2,10},{10,2},{3,11},{11,3},{4,12},{12,4},... | collective-permute-start | bytes 1769480 | tf_op jit(solution)/shard_map/ppermute | solution.py:297
  74.4 0.8 copy-start.8
  75.3 27.4 %collective-permute-start.10 = (bf16[192,1536]{1,0:T(8,128)(2,1)}, bf16[192,1536]{1,0:T(8,128)(2,1)S(1)}, u32[]{:S(2)}, u32[]{:S(2)}) collective-permute-start(bf16[192,1536]{1,0:T(8,128)(2,1)} %pad_maximum_fusion.1), channel_id=1, source_target_pairs={{0,4},{4,0},{1,5},{5,1},{2,6},{6,2},{3,7},{7,3},{8,12},{12,8},{9,1... | collective-permute-start | bytes 1769480 | tf_op jit(solution)/shard_map/ppermute | solution.py:297
  75.5 17.1 %collective-permute-start.13 = (bf16[48,3072]{1,0:T(8,128)(2,1)}, bf16[48,3072]{1,0:T(8,128)(2,1)}, u32[]{:S(2)}, u32[]{:S(2)}) collective-permute-start(bf16[48,3072]{1,0:T(8,128)(2,1)} %get-tuple-element.29), channel_id=1, source_target_pairs={{0,1},{1,0},{2,3},{3,2},{4,5},{5,4},{6,7},{7,6},{8,9},{9,8},{10,11... | collective-permute-start | bytes 884744 | tf_op jit(solution)/shard_map/ppermute | solution.py:280
  80.8 0.8 copy-start.6
  81.7 0.8 copy-start.7
  100.8 3.6 %copy-start.4 = (bf16[192,1536]{1,0:T(8,128)(2,1)}, bf16[192,1536]{1,0:T(8,128)(2,1)S(1)}, u32[]{:S(2)}) copy-start(bf16[192,1536]{1,0:T(8,128)(2,1)S(1)} %collective-permute-done.8.refs_0_) | copy-start | bytes 1769476
  102.7 1.7 %copy-start.5 = (bf16[192,1536]{1,0:T(8,128)(2,1)}, bf16[192,1536]{1,0:T(8,128)(2,1)S(1)}, u32[]{:S(2)}) copy-start(bf16[192,1536]{1,0:T(8,128)(2,1)S(1)} %collective-permute-done.10.refs_1_) | copy-start | bytes 1769476
Sparse Core Ops, SparseCore 0:
  48.1 56.2 all-gather.2

commit v8 on v7

--- a/solution.py
+++ b/solution.py
@@ -172,65 +172,46 @@
     )(active, q, *state, *near)
 
 
-def finish_kernel(counts, moves, control_rows, place, active, q, part, stats, *refs):
-    groups_of = []
+def finish_kernel(counts, moves, control_rows, place, hidden, *refs):
+    parts = []
     for count in counts:
-        groups_of.append(refs[:count])
+        parts.append(refs[:count])
         refs = refs[count:]
-    near, ready, weight, control = groups_of
-    slots, blocks = len(near), len(control)
-    hidden, out, refs = refs[0], refs[1], refs[2:]
-    q_v, near_v, refs = refs[0], refs[1 : slots + 1], refs[slots + 1 :]
-    *state, stats_v, sems, attention, held, hidden_v, control_v, out_v, late_sems = refs
-    fetch, late_fetch = Fetch(sems), Fetch(late_sems)
-    late = []
+    ready, weight, control = parts
+    out, attention, held, hidden_v, control_v, out_v, sems = refs
+    blocks = len(control)
+    fetch = Fetch(sems)
+    fetched, residual = [], []
     done = 0
     for block in ready:
-        late.append(late_fetch(block, attention.at[:, pl.ds(done, block.shape[1])]))
+        residual.append(fetch(block, attention.at[:, pl.ds(done, block.shape[1])]))
         done += block.shape[1]
-
-    def fetch_late():
-        for piece, index, at in moves:
-            source = weight[piece] if at is None else weight[piece].at[index]
-            if at is None:
-                target = held
-            else:
-                group, outer, pair, core = at
-                count = source.shape[0]
-                outer = place[1] ^ outer
-                start = pl.multiple_of(((outer * 2 + pair) * 2 + core) * count, count)
-                target = held.at[group, pl.ds(start, count), :]
-            late.append(late_fetch(source, target))
-        late.append(late_fetch(hidden, hidden_v))
-        for d in range(blocks):
-            start = pl.multiple_of((place[4] ^ d) * control_rows, control_rows) if blocks > 1 else 0
-            late.append(late_fetch(control[d], control_v.at[pl.ds(start, control_rows), :]))
-
-    fetch_late()
-    close_heads(
-        fetch,
-        done // HEAD_DIM,
-        active,
-        q,
-        part,
-        stats,
-        near,
-        q_v,
-        near_v,
-        state,
-        stats_v,
-        attention,
-        pl.ds(done, q_v.shape[1]),
-    )
-    for copy in late[len(ready) + len(moves) :] + late[: len(ready)]:
+    for piece, index, at in moves:
+        source = weight[piece] if at is None else weight[piece].at[index]
+        if at is None:
+            target = held
+        else:
+            flip, group, outer, pair, core = at
+            count = source.shape[0]
+            outer = place[1] ^ outer
+            if flip:
+                group, pair, core = place[0] ^ group, place[2] ^ pair, place[3] ^ core
+            start = pl.multiple_of(((outer * 2 + pair) * 2 + core) * count, count)
+            target = held.at[group, pl.ds(start, count), :]
+        fetched.append(fetch(source, target))
+    residual.append(fetch(hidden, hidden_v))
+    for d in range(blocks):
+        start = pl.multiple_of((place[4] ^ d) * control_rows, control_rows) if blocks > 1 else 0
+        residual.append(fetch(control[d], control_v.at[pl.ds(start, control_rows), :]))
+    for copy in residual:
         copy.wait()
     groups, _, columns = held.shape
-    step = 256 if columns % 256 == 0 else columns
+    step = 512 if columns % 512 == 0 else columns
     stores = []
     for group in range(groups):
-        for number, (_, _, at) in enumerate(moves):
-            if group == (at[0] if at else 0):
-                late[len(ready) + number].wait()
+        for copy, (_, _, at) in zip(fetched, moves):
+            if group == (0 if at is None or at[0] else at[1]):
+                copy.wait()
         for j in range(columns // step):
             at = pl.ds(group * columns + j * step, step)
             projected = jnp.dot(
@@ -239,28 +220,26 @@
             out_v[:, at] = (
                 hidden_v[:, at].astype(jnp.float32) + projected + control_v[:, at].astype(jnp.float32)
             ).astype(jnp.bfloat16)
-            stores.append(late_fetch(out_v.at[:, at], out.at[:, at]))
+            stores.append(fetch(out_v.at[:, at], out.at[:, at]))
     for copy in stores:
         copy.wait()
 
 
-def finish(place, active, q, state, near, ready, weight, control, hidden, moves):
-    rows, inner = q.shape
-    width = hidden.shape[1]
+def finish(place, ready, weight, control, hidden, moves):
+    rows, width = hidden.shape
+    inner = sum(x.shape[1] for x in ready)
     groups = lax.axis_size("groups")
     control_rows = control[0].shape[0]
-    columns = near[0].shape[1] // 2
     share = width // groups
-    lists = (near, ready, weight, control)
+    lists = (ready, weight, control)
     counts = tuple(len(x) for x in lists)
-    step = 256 if share % 256 == 0 else share
+    step = 512 if share % 512 == 0 else share
     return pl.pallas_call(
         functools.partial(finish_kernel, counts, moves, control_rows),
         out_shape=jax.ShapeDtypeStruct((rows, width), jnp.bfloat16),
-        in_specs=[SMEM] * 2 + [ANY] * (4 + sum(counts)),
+        in_specs=[SMEM] + [ANY] * (1 + sum(counts)),
         out_specs=ANY,
-        scratch_shapes=close_scratch(rows, columns, len(near))
-        + [
+        scratch_shapes=[
             pltpu.VMEM((rows, inner), jnp.bfloat16),
             pltpu.VMEM((groups, inner, share), jnp.bfloat16),
             pltpu.VMEM((rows, width), jnp.bfloat16),
@@ -273,7 +252,7 @@
             flops=2 * rows * inner * width, bytes_accessed=2 * inner * width + 6 * rows * width, transcendentals=0
         ),
         name="finish",
-    )(place, active, q, *state, *near, *ready, *weight, *control, hidden)
+    )(place, hidden, *ready, *weight, *control)
 
 
 def flipped(block, axis, flip):
@@ -353,7 +332,7 @@
         flip //= 2
     far = far_lane(swap("outer", 2), line)
     near = near_lane(swap("outer", 1), line)
-    last = swap("outer", 1)(far)
+    last = swap("outer", 1)(after(far, near))
 
     firsts = [sum(CHUNKS[:i]) for i in range(len(CHUNKS))]
     chunks = [
@@ -365,40 +344,44 @@
     control_sent = [
         lax.dynamic_index_in_dim(lines, across ^ d, 1, keepdims=False).reshape(block, width) for d in range(grid_width)
     ]
-    control_parts = list(control_sent)
-    early_near = [[None, None] for _ in early]
-    waits = (line,)
-    for i, x in enumerate((keys, values)):
-        sent = []
-        for slot in range(1, len(early)):
-            early_near[slot][i] = lax.ppermute(after(x, *waits), TILES, early[slot][2])
-            sent.append(early_near[slot][i])
-        for d in range(2 + i, grid_width, 2):
-            control_parts[d] = swap(TILES, d)(after(control_sent[d], *waits))
-            sent.append(control_parts[d])
-        waits = (far, near, *sent)
+    control_parts = [control_sent[0]] + [None] * (grid_width - 1)
+    early_x = []
+    for d in range(2, grid_width - 1):
+        control_parts[d] = swap(TILES, d)(after(control_sent[d], line))
+        early_x.append(control_parts[d])
+    control_parts[-1] = swap(TILES, grid_width - 1)(after(control_sent[-1], *early_x))
     control_parts[1] = swap(TILES, 1)(control_sent[1])
-    for i, x in enumerate((keys, values)):
-        early_near[0][i] = lax.ppermute(x, TILES, early[0][2])
+    plane = jnp.concatenate([line, swap("pair", 1)(line)])
+    held = [plane, swap("groups", 1)(plane)]
+    crossed = [swap("core", 1)(x) for x in held]
+    early_near = [[lax.ppermute(x, TILES, route) for x in (keys, values)] for _, _, route in early]
     state = attend(early_active, queries, [keys, values] + [x for kv in early_near for x in kv])
 
-    steps = (line, far, near, last)
-    weight = [lax.all_gather(after(jnp.concatenate(steps), *sent), ("groups", "pair", "core"))]
+    steps = after(jnp.concatenate([far, near, last]), control_parts[-1], held[1])
+    weight = [lax.all_gather(steps, ("groups", "pair", "core"))]
     n = len(line_flips)
     moves = [
-        (0, ((g * pair + p) * cores + c, i * n + j), (g, f ^ at, p, c))
+        (0, ((g * pair + p) * cores + c, i * n + j), (False, g, f ^ at, p, c))
         for g in range(groups)
         for p in range(pair)
         for c in range(cores)
-        for i, at in enumerate((0, 2, 1, 3))
+        for i, at in enumerate((2, 1, 3))
         for j, f in enumerate(line_flips)
     ]
+    for group_flip in range(2):
+        for core_flip, pieces in enumerate((held, crossed)):
+            moves += [
+                (len(weight), (p * n + j,), (True, group_flip, f, p, core_flip))
+                for p in range(pair)
+                for j, f in enumerate(line_flips)
+            ]
+            weight.append(pieces[group_flip])
 
     late_near = []
     for chunk in chunks:
         lanes = (far_lane, near_lane)
         late_near.append([lanes[i % 2](route_of(route), chunk) for i, (_, _, route) in enumerate(late)])
-    ready = [close(late_active, queries, state, late_near[i], firsts[i]) for i in range(len(CHUNKS) - 1)]
+    ready = [close(late_active, queries, state, late_near[i], firsts[i]) for i in range(len(CHUNKS))]
     if block % 16:
         control_parts = [
             jnp.take(
@@ -408,27 +391,21 @@
     place = jnp.stack([lax.axis_index(a) for a in ("groups",) + TILES] + [across]).astype(jnp.int32)
     if shard % 16:
         weight, moves = [in_order(weight, moves, place, (groups, outer, pair, cores))], [(0, None, None)]
-    return finish(
-        place,
-        late_active,
-        queries,
-        state,
-        late_near[-1],
-        ready,
-        weight,
-        control_parts,
-        hidden,
-        tuple(moves),
-    )
+    return finish(place, ready, weight, control_parts, hidden, tuple(moves))
 
 
 def in_order(weight, moves, place, sizes):
-    blocks = {at: weight[piece][index] for piece, index, at in moves}
-    whole = jnp.stack([blocks[at] for at in sorted(blocks)])
-    shard, columns = whole.shape[1:]
-    whole = whole.reshape(sizes + (shard, columns))
-    whole = jnp.take(whole, jnp.arange(sizes[1], dtype=jnp.int32) ^ place[1], axis=1)
-    return whole.reshape(sizes[0], -1, columns)
+    groups, outer, pair, cores = sizes
+    shard, columns = weight[0].shape[-2:]
+    gathered = weight[0].reshape(groups, pair, cores, -1, shard, columns)
+    for axis, at in enumerate((0, 2, 3)):
+        gathered = jnp.take(gathered, jnp.arange(sizes[at], dtype=jnp.int32) ^ place[at], axis=axis)
+    weight = [gathered.reshape(weight[0].shape)] + weight[1:]
+    blocks = {at[1:]: weight[piece][index] for piece, index, at in moves}
+    whole = jnp.stack([blocks[at] for at in sorted(blocks)]).reshape(sizes + (shard, columns))
+    for axis, size in enumerate(sizes):
+        whole = jnp.take(whole, jnp.arange(size, dtype=jnp.int32) ^ place[axis], axis=axis)
+    return whole.reshape(groups, -1, columns)
 
 
 def solution(mesh):

time: 123 us -> 117 us (0.951)
  the two profiles are of different devices: /device:TPU:1 before, /device:TPU:0 now
where the time goes in v8:
time: 117 us
  waiting for transfers between devices  48.2 us (41%)
  Pallas kernels  22.8 us (19%)
  starting transfers between devices  20.4 us (17%)
  between operations  16.1 us (14%)
  local copies, waits for them, and re-layouts  5 us (4%)
  other arithmetic  4.42 us (4%)
    ppermute x4, waiting for transfers between devices, route_of(): return lambda block: lax.ppermute(block, TILES, route)  32.5 us
    ppermute x10, waiting for transfers between devices, flipped(): lax.ppermute(block, axis, [(i, i ^ flip) for i in range(lax.axis_size(axi...  15.6 us
    ppermute x10, starting transfers between devices, flipped(): lax.ppermute(block, axis, [(i, i ^ flip) for i in range(lax.axis_size(axi...  10.8 us
    pallas_call x2, Pallas kernels, close(): pl.pallas_call(functools.partial(close_kernel, first, len(near)), out_sha...  9.86 us
    pallas_call x1, Pallas kernels, finish(): pl.pallas_call(functools.partial(finish_kernel, counts, moves, control_ro...  8.48 us
    ppermute x4, starting transfers between devices, route_of(): return lambda block: lax.ppermute(block, TILES, route)  5.45 us
    pallas_call x1, Pallas kernels, attend(): pl.pallas_call(functools.partial(attend_kernel, slots), out_shape=[jax.Sh...  4.42 us
    ppermute x4, starting transfers between devices, on_device(): lax.ppermute(x, TILES, route)  4.17 us
  transfers between devices with their start and end apart: 19, of which 8 were waited for; matrix products, arithmetic and copies ran while one was open for 6% of the time, Pallas kernels for 12%

profile of v8, /device:TPU:0, one launch (start us, length us, event | category | flops | bytes accessed | tf_op | source)
XLA Modules:
  0.0 116.9 jit_solution(14729772977160126778)
XLA Ops:
  6.5 1.1 slice_select_fusion
  7.6 3.0 %collective-permute-start.13 = (bf16[1,96,1536]{2,1,0:T(8,128)(2,1)S(1)}, bf16[1,96,1536]{2,1,0:T(8,128)(2,1)S(1)}, u32[]{:S(2)}, u32[]{:S(2)}) collective-permute-start(bf16[1,96,1536]{2,1,0:T(8,128)(2,1)S(1)} %bitcast.33), channel_id=1, source_target_pairs={{0,2},{2,0},{1,3},{3,1},{4,6},{6,4},{5,7},{7,5},{8,10},{10,8},{9,1... | collective-permute-start | bytes 884744 | tf_op jit(solution)/shard_map/ppermute | solution.py:259
  10.6 1.6 %collective-permute-start.6 = (bf16[1,96,1536]{2,1,0:T(8,128)(2,1)S(1)}, bf16[1,96,1536]{2,1,0:T(8,128)(2,1)S(1)}, u32[]{:S(2)}, u32[]{:S(2)}) collective-permute-start(bf16[1,96,1536]{2,1,0:T(8,128)(2,1)S(1)} %bitcast.34), channel_id=1, source_target_pairs={{0,4},{4,0},{8,12},{12,8},{1,5},{5,1},{9,13},{13,9},{2,6},{6,2},{1... | collective-permute-start | bytes 884744 | tf_op jit(solution)/shard_map/ppermute | solution.py:259
  12.2 2.6 %collective-permute-start.4 = (bf16[1,96,1536]{2,1,0:T(8,128)(2,1)S(1)}, bf16[1,96,1536]{2,1,0:T(8,128)(2,1)S(1)}, u32[]{:S(2)}, u32[]{:S(2)}) collective-permute-start(bf16[1,96,1536]{2,1,0:T(8,128)(2,1)S(1)} %bitcast.35), channel_id=1, source_target_pairs={{0,8},{4,12},{8,0},{12,4},{1,9},{5,13},{9,1},{13,5},{2,10},{6,14},... | collective-permute-start | bytes 884744 | tf_op jit(solution)/shard_map/ppermute | solution.py:259
  14.8 2.1 %dynamic-slice_bitcast_fusion = (bf16[48,3072]{1,0:T(8,128)(2,1)}, bf16[48,3072]{1,0:T(8,128)(2,1)}, bf16[48,3072]{1,0:T(8,128)(2,1)S(1)}, bf16[48,3072]{1,0:T(8,128)(2,1)S(1)}) fusion(bf16[6,4,8,3072]{3,2,1,0:T(8,128)(2,1)} %bitcast.37, s32[]{:T(128)S(6)} %select_n.109, s32[]{:T(128)S(6)} %select_n.108, s32[]{:T(128)S(6)} %select_n.107, s32[]{:T(128)S(6)} %select_n.106), kind=kLoop, calls=%fused_computation.4 | loop fusion | bytes 2359312 | tf_op jit(solution)/shard_map/reshape | solution.py:345
  16.9 0.5 collective-permute-start.11
  17.5 0.2 collective-permute-done.13
  17.6 0.1 pad_maximum_fusion.3.refs_3_
  17.7 1.8 %collective-permute-start.14 = (bf16[2,96,1536]{2,1,0:T(8,128)(2,1)S(1)}, bf16[2,96,1536]{2,1,0:T(8,128)(2,1)}, u32[]{:S(2)}, u32[]{:S(2)}) collective-permute-start(bf16[2,96,1536]{2,1,0:T(8,128)(2,1)S(1)} %pad_maximum_fusion.3.refs_3_), channel_id=1, source_target_pairs={{0,16},{16,0},{1,17},{17,1},{2,18},{18,2},{3,19},{19,3},{4,20},{20... | collective-permute-start | bytes 1769480 | tf_op jit(solution)/shard_map/ppermute | solution.py:259
  19.5 5.8 %collective-permute-done.6 = bf16[1,96,1536]{2,1,0:T(8,128)(2,1)S(1)} collective-permute-done((bf16[1,96,1536]{2,1,0:T(8,128)(2,1)S(1)}, bf16[1,96,1536]{2,1,0:T(8,128)(2,1)S(1)}, u32[]{:S(2)}, u32[]{:S(2)}) %collective-permute-start.6) | collective-permute-done | bytes 294944 | tf_op jit(solution)/shard_map/ppermute | solution.py:259
  25.3 2.4 %collective-permute-done.4 = bf16[1,96,1536]{2,1,0:T(8,128)(2,1)S(1)} collective-permute-done((bf16[1,96,1536]{2,1,0:T(8,128)(2,1)S(1)}, bf16[1,96,1536]{2,1,0:T(8,128)(2,1)S(1)}, u32[]{:S(2)}, u32[]{:S(2)}) %collective-permute-start.4) | collective-permute-done | bytes 294944 | tf_op jit(solution)/shard_map/ppermute | solution.py:259
  27.7 0.4 collective-permute-start.10
  28.1 0.0 collective-permute-done.11.refs_9_
  28.1 6.3 %collective-permute-done.10 = bf16[1,96,1536]{2,1,0:T(8,128)(2,1)S(1)} collective-permute-done((bf16[1,96,1536]{2,1,0:T(8,128)(2,1)S(1)}, bf16[1,96,1536]{2,1,0:T(8,128)(2,1)S(1)}, u32[]{:S(2)}, u32[]{:S(2)}) %collective-permute-start.10) | collective-permute-done | bytes 294944 | tf_op jit(solution)/shard_map/ppermute | solution.py:259
  34.4 1.1 pad_maximum_fusion
  35.5 1.1 collective-permute-done.12.refs_10_
  36.5 0.0 all-gather.3.cloned.1.call-update
  36.7 0.6 copy-done.10
  37.3 2.7 %collective-permute-start.5 = (bf16[192,1536]{1,0:T(8,128)(2,1)S(1)}, bf16[192,1536]{1,0:T(8,128)(2,1)S(1)}, u32[]{:S(2)}, u32[]{:S(2)}) collective-permute-start(bf16[192,1536]{1,0:T(8,128)(2,1)S(1)} %pad_maximum_fusion.1), channel_id=1, source_target_pairs={{0,8},{8,0},{1,9},{9,1},{2,10},{10,2},{3,11},{11,3},{4,12},{12,4},... | collective-permute-start | bytes 1769480 | tf_op jit(solution)/shard_map/ppermute | solution.py:276
  40.0 0.1 collective-permute-start.7
  40.1 0.7 collective-permute-start.2
  40.8 2.8 %collective-permute-start = (bf16[192,1536]{1,0:T(8,128)(2,1)S(1)}, bf16[192,1536]{1,0:T(8,128)(2,1)S(1)}, u32[]{:S(2)}, u32[]{:S(2)}) collective-permute-start(bf16[192,1536]{1,0:T(8,128)(2,1)S(1)} %copy-done), channel_id=1, source_target_pairs={{0,1},{1,0},{2,3},{3,2},{4,5},{5,4},{6,7},{7,6},{8,9},{9,8},{10,11... | collective-permute-start | bytes 1769480 | tf_op jit(solution)/shard_map/ppermute | solution.py:357
  43.6 0.7 collective-permute-start.3
  44.3 21.2 %collective-permute-done.5.refs_0_ = bf16[192,1536]{1,0:T(8,128)(2,1)S(1)} collective-permute-done((bf16[192,1536]{1,0:T(8,128)(2,1)S(1)}, bf16[192,1536]{1,0:T(8,128)(2,1)S(1)}, u32[]{:S(2)}, u32[]{:S(2)}) %collective-permute-start.5) | collective-permute-done | bytes 589856 | tf_op jit(solution)/shard_map/ppermute | solution.py:276
  65.5 0.0 collective-permute-start.1
  65.5 0.9 pad_maximum_fusion.2
  66.4 0.0 collective-permute-done.7.refs_1_
  66.4 0.5 collective-permute-start.8
  67.0 0.0 collective-permute-done.2.refs_4_
  67.0 2.1 %collective-permute-start.9 = (bf16[192,1536]{1,0:T(8,128)(2,1)}, bf16[192,1536]{1,0:T(8,128)(2,1)}, u32[]{:S(2)}, u32[]{:S(2)}) collective-permute-start(bf16[192,1536]{1,0:T(8,128)(2,1)} %pad_maximum_fusion.2), channel_id=1, source_target_pairs={{0,4},{4,0},{1,5},{5,1},{2,6},{6,2},{3,7},{7,3},{8,12},{12,8},{9,1... | collective-permute-start | bytes 1769480 | tf_op jit(solution)/shard_map/ppermute | solution.py:276
  69.1 0.0 collective-permute-done.refs_2_
  69.1 0.1 collective-permute-start.15
  69.2 0.5 collective-permute-start.16
  69.7 0.6 constant_dynamic-slice_fusion.1
  71.7 0.2 collective-permute-start.17
  71.9 0.6 add_convert_fusion.active
  73.7 0.7 stack.49.place
  74.3 0.6 add_convert_fusion.1.active
  75.0 4.4 %attend.1 = (f32[192,1536]{1,0:T(8,128)}, f32[192,128]{1,0:T(8,128)}) custom-call(s32[2]{0:T(128)} %add_convert_fusion.1.active, bf16[192,1536]{1,0:T(8,128)(2,1)} %q.5, bf16[192,1536]{1,0:T(8,128)(2,1)} %refs_0_.1, bf16[192,1536]{1,0:T(8,128)(2,1)} %refs_1_.1, bf16[192,1536]{1,0:T(8,128)(2,1)} %copy-done.4, ...), custom_call_target="tpu_custom_call" | custom-call | flops 1019215872 | bytes 5308416 | tf_op jit(solution)/shard_map/attend/pallas_call | solution.py:100
  79.4 4.9 %close.2.refs_0_ = bf16[192,768]{1,0:T(8,128)(2,1)} custom-call(s32[2]{0:T(128)} %add_convert_fusion.active, bf16[192,1536]{1,0:T(8,128)(2,1)} %q.5, f32[192,1536]{1,0:T(8,128)} %get-tuple-element.16.part, f32[192,128]{1,0:T(8,128)} %get-tuple-element.17.stats, bf16[192,1536]{1,0:T(8,128)(2,1)} %copy-done.6, bf16[192,1536]{1,0:T(8,128)(2,1)} %copy-done.7), custom_call_target="tpu_custom_call" | custom-call | flops 339738624 | bytes 2359296 | tf_op jit(solution)/shard_map/close/pallas_call | solution.py:159
  84.4 11.1 %collective-permute-done.8.refs_0_ = bf16[192,1536]{1,0:T(8,128)(2,1)} collective-permute-done((bf16[192,1536]{1,0:T(8,128)(2,1)}, bf16[192,1536]{1,0:T(8,128)(2,1)}, u32[]{:S(2)}, u32[]{:S(2)}) %collective-permute-start.8) | collective-permute-done | bytes 589856 | tf_op jit(solution)/shard_map/ppermute | solution.py:276
  95.5 0.2 collective-permute-done.9.refs_1_
  95.7 4.9 %close.3.refs_1_ = bf16[192,768]{1,0:T(8,128)(2,1)} custom-call(s32[2]{0:T(128)} %add_convert_fusion.active, bf16[192,1536]{1,0:T(8,128)(2,1)} %q.5, f32[192,1536]{1,0:T(8,128)} %get-tuple-element.16.part, f32[192,128]{1,0:T(8,128)} %get-tuple-element.17.stats, bf16[192,1536]{1,0:T(8,128)(2,1)} %collective-permute-done.8.refs_0_, ...), custom_call_target="tpu_custom_call" | custom-call | flops 339738624 | bytes 2359296 | tf_op jit(solution)/shard_map/close/pallas_call | solution.py:159
  100.7 0.0 collective-permute-done.15.refs_4_
  100.7 0.0 all-gather.3.cloned.1.call-done
  100.7 0.6 copy-done.11
  101.4 0.2 copy-done.8
  101.6 8.5 %finish.1 = bf16[192,3072]{1,0:T(8,128)(2,1)} custom-call(s32[5]{0:T(128)} %stack.49.place, bf16[192,3072]{1,0:T(8,128)(2,1)} %hidden.1, bf16[192,768]{1,0:T(8,128)(2,1)} %close.2.refs_0_, bf16[192,768]{1,0:T(8,128)(2,1)} %close.3.refs_1_, bf16[8,3,96,1536]{3,2,1,0:T(8,128)(2,1)} %bitcast.32, bf16[2,96,1536]{2,1,0:T(8,128)(2,1)} %copy-done.2, ...), custom_call_target="tpu_custom_call" | custom-call | flops 1811939328 | bytes 12976128 | tf_op jit(solution)/shard_map/finish/pallas_call | solution.py:237
  (33 shorter events, 0.2 us)
Async XLA Ops:
  6.5 94.2 %all-gather.3.cloned.1.call-start = ((), (), s32[]{:S(2)}) async-start(), calls=%async_computation | async-start | bytes 7962624 | tf_op jit(solution)/shard_map/all_gather | solution.py:361
  7.6 10.0 %collective-permute-start.13 = (bf16[1,96,1536]{2,1,0:T(8,128)(2,1)S(1)}, bf16[1,96,1536]{2,1,0:T(8,128)(2,1)S(1)}, u32[]{:S(2)}, u32[]{:S(2)}) collective-permute-start(bf16[1,96,1536]{2,1,0:T(8,128)(2,1)S(1)} %bitcast.33), channel_id=1, source_target_pairs={{0,2},{2,0},{1,3},{3,1},{4,6},{6,4},{5,7},{7,5},{8,10},{10,8},{9,1... | collective-permute-start | bytes 884744 | tf_op jit(solution)/shard_map/ppermute | solution.py:259
  10.6 14.7 %collective-permute-start.6 = (bf16[1,96,1536]{2,1,0:T(8,128)(2,1)S(1)}, bf16[1,96,1536]{2,1,0:T(8,128)(2,1)S(1)}, u32[]{:S(2)}, u32[]{:S(2)}) collective-permute-start(bf16[1,96,1536]{2,1,0:T(8,128)(2,1)S(1)} %bitcast.34), channel_id=1, source_target_pairs={{0,4},{4,0},{8,12},{12,8},{1,5},{5,1},{9,13},{13,9},{2,6},{6,2},{1... | collective-permute-start | bytes 884744 | tf_op jit(solution)/shard_map/ppermute | solution.py:259
  12.2 15.5 %collective-permute-start.4 = (bf16[1,96,1536]{2,1,0:T(8,128)(2,1)S(1)}, bf16[1,96,1536]{2,1,0:T(8,128)(2,1)S(1)}, u32[]{:S(2)}, u32[]{:S(2)}) collective-permute-start(bf16[1,96,1536]{2,1,0:T(8,128)(2,1)S(1)} %bitcast.35), channel_id=1, source_target_pairs={{0,8},{4,12},{8,0},{12,4},{1,9},{5,13},{9,1},{13,5},{2,10},{6,14},... | collective-permute-start | bytes 884744 | tf_op jit(solution)/shard_map/ppermute | solution.py:259
  16.9 11.2 %collective-permute-start.11 = (bf16[48,3072]{1,0:T(8,128)(2,1)S(1)}, bf16[48,3072]{1,0:T(8,128)(2,1)S(1)}, u32[]{:S(2)}, u32[]{:S(2)}) collective-permute-start(bf16[48,3072]{1,0:T(8,128)(2,1)S(1)} %get-tuple-element.24), channel_id=1, source_target_pairs={{0,2},{1,3},{2,0},{3,1},{4,6},{5,7},{6,4},{7,5},{8,10},{9,11},{10,... | collective-permute-start | bytes 884744 | tf_op jit(solution)/shard_map/ppermute | solution.py:259
  17.7 51.4 %copy-start.2 = (bf16[2,96,1536]{2,1,0:T(8,128)(2,1)}, bf16[2,96,1536]{2,1,0:T(8,128)(2,1)S(1)}, u32[]{:S(2)}) copy-start(bf16[2,96,1536]{2,1,0:T(8,128)(2,1)S(1)} %pad_maximum_fusion.3.refs_3_) | copy-start | bytes 1769476
  17.7 18.8 %collective-permute-start.14 = (bf16[2,96,1536]{2,1,0:T(8,128)(2,1)S(1)}, bf16[2,96,1536]{2,1,0:T(8,128)(2,1)}, u32[]{:S(2)}, u32[]{:S(2)}) collective-permute-start(bf16[2,96,1536]{2,1,0:T(8,128)(2,1)S(1)} %pad_maximum_fusion.3.refs_3_), channel_id=1, source_target_pairs={{0,16},{16,0},{1,17},{17,1},{2,18},{18,2},{3,19},{19,3},{4,20},{20... | collective-permute-start | bytes 1769480 | tf_op jit(solution)/shard_map/ppermute | solution.py:259
  27.7 6.7 %collective-permute-start.10 = (bf16[1,96,1536]{2,1,0:T(8,128)(2,1)S(1)}, bf16[1,96,1536]{2,1,0:T(8,128)(2,1)S(1)}, u32[]{:S(2)}, u32[]{:S(2)}) collective-permute-start(bf16[1,96,1536]{2,1,0:T(8,128)(2,1)S(1)} %collective-permute-done.4), channel_id=1, source_target_pairs={{0,4},{4,0},{8,12},{12,8},{1,5},{5,1},{9,13},{13,9},{2,6},{6,2},{1... | collective-permute-start | bytes 884744 | tf_op jit(solution)/shard_map/ppermute | solution.py:259
  28.1 8.4 %copy-start.9 = (bf16[48,3072]{1,0:T(8,128)(2,1)}, bf16[48,3072]{1,0:T(8,128)(2,1)S(1)}, u32[]{:S(2)}) copy-start(bf16[48,3072]{1,0:T(8,128)(2,1)S(1)} %collective-permute-done.11.refs_9_) | copy-start | bytes 884740
  28.1 8.4 %copy-start = (bf16[192,1536]{1,0:T(8,128)(2,1)S(1)}, bf16[192,1536]{1,0:T(8,128)(2,1)}, u32[]{:S(2)}) copy-start(bf16[192,1536]{1,0:T(8,128)(2,1)} %refs_0_.1) | copy-start | bytes 1769476
  28.1 8.4 %collective-permute-start.12 = (bf16[48,3072]{1,0:T(8,128)(2,1)S(1)}, bf16[48,3072]{1,0:T(8,128)(2,1)S(1)}, u32[]{:S(2)}, u32[]{:S(2)}) collective-permute-start(bf16[48,3072]{1,0:T(8,128)(2,1)S(1)} %get-tuple-element.25), channel_id=1, source_target_pairs={{0,3},{1,2},{2,1},{3,0},{4,7},{5,6},{6,5},{7,4},{8,11},{9,10},{10,... | collective-permute-start | bytes 884744 | tf_op jit(solution)/shard_map/ppermute | solution.py:259
  35.5 1.2 copy-start.1
  36.5 0.7 copy-start.10
  37.2 32.5 %copy-start.12 = (s32[1,6]{1,0:T(1,128)S(1)}, s32[1,6]{1,0:T(1,128)}, u32[]{:S(2)}) copy-start(s32[1,6]{1,0:T(1,128)} %param.13) | copy-start | bytes 76
  37.3 28.2 %collective-permute-start.5 = (bf16[192,1536]{1,0:T(8,128)(2,1)S(1)}, bf16[192,1536]{1,0:T(8,128)(2,1)S(1)}, u32[]{:S(2)}, u32[]{:S(2)}) collective-permute-start(bf16[192,1536]{1,0:T(8,128)(2,1)S(1)} %pad_maximum_fusion.1), channel_id=1, source_target_pairs={{0,8},{8,0},{1,9},{9,1},{2,10},{10,2},{3,11},{11,3},{4,12},{12,4},... | collective-permute-start | bytes 1769480 | tf_op jit(solution)/shard_map/ppermute | solution.py:276
  40.0 26.4 %collective-permute-start.7 = (bf16[192,1536]{1,0:T(8,128)(2,1)S(1)}, bf16[192,1536]{1,0:T(8,128)(2,1)S(1)}, u32[]{:S(2)}, u32[]{:S(2)}) collective-permute-start(bf16[192,1536]{1,0:T(8,128)(2,1)S(1)} %pad_maximum_fusion.1), channel_id=1, source_target_pairs={{0,4},{4,0},{1,5},{5,1},{2,6},{6,2},{3,7},{7,3},{8,12},{12,8},{9,1... | collective-permute-start | bytes 1769480 | tf_op jit(solution)/shard_map/ppermute | solution.py:276
  40.1 26.9 %collective-permute-start.2 = (bf16[192,1536]{1,0:T(8,128)(2,1)S(1)}, bf16[192,1536]{1,0:T(8,128)(2,1)S(1)}, u32[]{:S(2)}, u32[]{:S(2)}) collective-permute-start(bf16[192,1536]{1,0:T(8,128)(2,1)S(1)} %copy-done), channel_id=1, source_target_pairs={{1,2},{2,1},{5,6},{6,5},{9,10},{10,9},{13,14},{14,13},{17,18},{18,... | collective-permute-start | bytes 1769480 | tf_op jit(solution)/shard_map/ppermute | solution.py:357
  40.8 28.3 %collective-permute-start = (bf16[192,1536]{1,0:T(8,128)(2,1)S(1)}, bf16[192,1536]{1,0:T(8,128)(2,1)S(1)}, u32[]{:S(2)}, u32[]{:S(2)}) collective-permute-start(bf16[192,1536]{1,0:T(8,128)(2,1)S(1)} %copy-done), channel_id=1, source_target_pairs={{0,1},{1,0},{2,3},{3,2},{4,5},{5,4},{6,7},{7,6},{8,9},{9,8},{10,11... | collective-permute-start | bytes 1769480 | tf_op jit(solution)/shard_map/ppermute | solution.py:357
  43.6 25.5 %collective-permute-start.3 = (bf16[192,1536]{1,0:T(8,128)(2,1)S(1)}, bf16[192,1536]{1,0:T(8,128)(2,1)S(1)}, u32[]{:S(2)}, u32[]{:S(2)}) collective-permute-start(bf16[192,1536]{1,0:T(8,128)(2,1)S(1)} %copy-done.1), channel_id=1, source_target_pairs={{1,2},{2,1},{5,6},{6,5},{9,10},{10,9},{13,14},{14,13},{17,18},{18,... | collective-permute-start | bytes 1769480 | tf_op jit(solution)/shard_map/ppermute | solution.py:357
  65.5 3.7 %copy-start.6 = (bf16[192,1536]{1,0:T(8,128)(2,1)}, bf16[192,1536]{1,0:T(8,128)(2,1)S(1)}, u32[]{:S(2)}) copy-start(bf16[192,1536]{1,0:T(8,128)(2,1)S(1)} %collective-permute-done.5.refs_0_) | copy-start | bytes 1769476
  65.5 6.2 %collective-permute-start.1 = (bf16[192,1536]{1,0:T(8,128)(2,1)S(1)}, bf16[192,1536]{1,0:T(8,128)(2,1)}, u32[]{:S(2)}, u32[]{:S(2)}) collective-permute-start(bf16[192,1536]{1,0:T(8,128)(2,1)S(1)} %copy-done.1), channel_id=1, source_target_pairs={{0,1},{1,0},{2,3},{3,2},{4,5},{5,4},{6,7},{7,6},{8,9},{9,8},{10,11... | collective-permute-start | bytes 1769480 | tf_op jit(solution)/shard_map/ppermute | solution.py:357
  66.4 2.7 %copy-start.7 = (bf16[192,1536]{1,0:T(8,128)(2,1)}, bf16[192,1536]{1,0:T(8,128)(2,1)S(1)}, u32[]{:S(2)}) copy-start(bf16[192,1536]{1,0:T(8,128)(2,1)S(1)} %collective-permute-done.7.refs_1_) | copy-start | bytes 1769476
  66.4 29.1 %collective-permute-start.8 = (bf16[192,1536]{1,0:T(8,128)(2,1)}, bf16[192,1536]{1,0:T(8,128)(2,1)}, u32[]{:S(2)}, u32[]{:S(2)}) collective-permute-start(bf16[192,1536]{1,0:T(8,128)(2,1)} %pad_maximum_fusion.2), channel_id=1, source_target_pairs={{0,8},{8,0},{1,9},{9,1},{2,10},{10,2},{3,11},{11,3},{4,12},{12,4},... | collective-permute-start | bytes 1769480 | tf_op jit(solution)/shard_map/ppermute | solution.py:276
  67.0 8.0 %copy-start.3 = (bf16[192,1536]{1,0:T(8,128)(2,1)}, bf16[192,1536]{1,0:T(8,128)(2,1)S(1)}, u32[]{:S(2)}) copy-start(bf16[192,1536]{1,0:T(8,128)(2,1)S(1)} %collective-permute-done.2.refs_4_) | copy-start | bytes 1769476
  67.0 28.7 %collective-permute-start.9 = (bf16[192,1536]{1,0:T(8,128)(2,1)}, bf16[192,1536]{1,0:T(8,128)(2,1)}, u32[]{:S(2)}, u32[]{:S(2)}) collective-permute-start(bf16[192,1536]{1,0:T(8,128)(2,1)} %pad_maximum_fusion.2), channel_id=1, source_target_pairs={{0,4},{4,0},{1,5},{5,1},{2,6},{6,2},{3,7},{7,3},{8,12},{12,8},{9,1... | collective-permute-start | bytes 1769480 | tf_op jit(solution)/shard_map/ppermute | solution.py:276
  69.1 5.9 %copy-start.4 = (bf16[192,1536]{1,0:T(8,128)(2,1)}, bf16[192,1536]{1,0:T(8,128)(2,1)S(1)}, u32[]{:S(2)}) copy-start(bf16[192,1536]{1,0:T(8,128)(2,1)S(1)} %collective-permute-done.refs_2_) | copy-start | bytes 1769476
  69.1 31.6 %collective-permute-start.15 = (bf16[2,96,1536]{2,1,0:T(8,128)(2,1)S(1)}, bf16[2,96,1536]{2,1,0:T(8,128)(2,1)S(1)}, u32[]{:S(2)}, u32[]{:S(2)}) collective-permute-start(bf16[2,96,1536]{2,1,0:T(8,128)(2,1)S(1)} %pad_maximum_fusion.3.refs_3_), channel_id=1, source_target_pairs={{0,1},{1,0},{2,3},{3,2},{4,5},{5,4},{6,7},{7,6},{8,9},{9,8},{10,11... | collective-permute-start | bytes 1769480 | tf_op jit(solution)/shard_map/ppermute | solution.py:259
  69.2 5.8 %copy-start.5 = (bf16[192,1536]{1,0:T(8,128)(2,1)}, bf16[192,1536]{1,0:T(8,128)(2,1)S(1)}, u32[]{:S(2)}) copy-start(bf16[192,1536]{1,0:T(8,128)(2,1)S(1)} %collective-permute-done.3.refs_5_) | copy-start | bytes 1769476
  69.2 31.5 %collective-permute-start.16 = (bf16[2,96,1536]{2,1,0:T(8,128)(2,1)}, bf16[2,96,1536]{2,1,0:T(8,128)(2,1)}, u32[]{:S(2)}, u32[]{:S(2)}) collective-permute-start(bf16[2,96,1536]{2,1,0:T(8,128)(2,1)} %collective-permute-done.14.refs_5_), channel_id=1, source_target_pairs={{0,1},{1,0},{2,3},{3,2},{4,5},{5,4},{6,7},{7,6},{8,9},{9,8},{10,11... | collective-permute-start | bytes 1769480 | tf_op jit(solution)/shard_map/ppermute | solution.py:259
  71.7 29.0 %collective-permute-start.17 = (bf16[48,3072]{1,0:T(8,128)(2,1)}, bf16[48,3072]{1,0:T(8,128)(2,1)S(1)}, u32[]{:S(2)}, u32[]{:S(2)}) collective-permute-start(bf16[48,3072]{1,0:T(8,128)(2,1)} %get-tuple-element.27), channel_id=1, source_target_pairs={{0,1},{1,0},{2,3},{3,2},{4,5},{5,4},{6,7},{7,6},{8,9},{9,8},{10,11... | collective-permute-start | bytes 884744 | tf_op jit(solution)/shard_map/ppermute | solution.py:259
  100.6 0.7 copy-start.11
  100.7 0.9 copy-start.8
Sparse Core Ops, SparseCore 0:
  36.7 53.4 all-gather.2

commit v9 on v8

--- a/solution.py
+++ b/solution.py
@@ -59,9 +59,12 @@
     def __init__(self, sems):
         self.sems, self.count = sems, 0
 
+    def later(self, source, target):
+        self.count += 1
+        return pltpu.make_async_copy(source, target, self.sems.at[self.count - 1])
+
     def __call__(self, source, target):
-        copy = pltpu.make_async_copy(source, target, self.sems.at[self.count])
-        self.count += 1
+        copy = self.later(source, target)
         copy.start()
         return copy
 
@@ -118,13 +121,18 @@
     )(active, q, *kv)
 
 
-def close_heads(fetch, first, active, q, part, stats, near, q_v, near_v, state, stats_v, out, out_at):
+def close_open(fetch, first, q, part, stats, near, q_v, near_v, state, stats_v):
     columns = state[0].shape[1]
-    copies = [
-        fetch(q.at[:, pl.ds(first * HEAD_DIM, columns)], q_v),
-        fetch(part.at[:, pl.ds(first * HEAD_DIM, columns)], state[0]),
+    at = pl.ds(first * HEAD_DIM, columns)
+    return [
+        fetch(q.at[:, at], q_v),
+        fetch(part.at[:, at], state[0]),
         fetch(stats, stats_v),
     ] + [fetch(source, target) for source, target in zip(near, near_v)]
+
+
+def close_heads(copies, first, active, q_v, near_v, state, stats_v, out):
+    columns = state[0].shape[1]
     for copy in copies[:3]:
         copy.wait()
     stats_now = stats_v[...]
@@ -134,7 +142,7 @@
     for slot, kv in enumerate(near_v):
         copies[3 + slot].wait()
         fold(state, active[slot], q_v, kv.at[:, pl.ds(0, columns)], kv.at[:, pl.ds(columns, columns)])
-    out[:, out_at] = (state[0][...] / state[1][...]).astype(jnp.bfloat16)
+    out[...] = (state[0][...] / state[1][...]).astype(jnp.bfloat16)
 
 
 def close_scratch(rows, columns, slots):
@@ -150,7 +158,8 @@
     near, out = refs[:slots], refs[slots]
     q_v, near_v, (*state, stats_v, sems, out_v) = refs[slots + 1], refs[slots + 2 : 2 * slots + 2], refs[2 * slots + 2 :]
     fetch = Fetch(sems)
-    close_heads(fetch, first, active, q, part, stats, near, q_v, near_v, state, stats_v, out_v, slice(None))
+    opened = close_open(fetch, first, q, part, stats, near, q_v, near_v, state, stats_v)
+    close_heads(opened, first, active, q_v, near_v, state, stats_v, out_v)
     fetch(out_v, out).wait()
 
 
@@ -172,87 +181,154 @@
     )(active, q, *state, *near)
 
 
-def finish_kernel(counts, moves, control_rows, place, hidden, *refs):
-    parts = []
-    for count in counts:
-        parts.append(refs[:count])
-        refs = refs[count:]
-    ready, weight, control = parts
-    out, attention, held, hidden_v, control_v, out_v, sems = refs
-    blocks = len(control)
-    fetch = Fetch(sems)
-    fetched, residual = [], []
-    done = 0
-    for block in ready:
-        residual.append(fetch(block, attention.at[:, pl.ds(done, block.shape[1])]))
-        done += block.shape[1]
+def fetch_weight(fetch, moves, place, weight, held, low, high):
+    copies = []
     for piece, index, at in moves:
-        source = weight[piece] if at is None else weight[piece].at[index]
         if at is None:
-            target = held
-        else:
-            flip, group, outer, pair, core = at
-            count = source.shape[0]
-            outer = place[1] ^ outer
-            if flip:
-                group, pair, core = place[0] ^ group, place[2] ^ pair, place[3] ^ core
-            start = pl.multiple_of(((outer * 2 + pair) * 2 + core) * count, count)
-            target = held.at[group, pl.ds(start, count), :]
-        fetched.append(fetch(source, target))
-    residual.append(fetch(hidden, hidden_v))
-    for d in range(blocks):
-        start = pl.multiple_of((place[4] ^ d) * control_rows, control_rows) if blocks > 1 else 0
-        residual.append(fetch(control[d], control_v.at[pl.ds(start, control_rows), :]))
-    for copy in residual:
-        copy.wait()
+            copies.append((True, 0, fetch(weight[piece], held)))
+            continue
+        source = weight[piece].at[index]
+        flip, group, outer, pair, core = at
+        known = None if flip else group
+        count = source.shape[0]
+        outer = place[1] ^ outer
+        if flip:
+            group, pair, core = place[0] ^ group, place[2] ^ pair, place[3] ^ core
+        start = pl.multiple_of(((outer * 2 + pair) * 2 + core) * count, count)
+        needed = (start < high) & (start + count > low)
+        copy = fetch.later(source, held.at[group, pl.ds(start, count), :])
+        pl.when(needed)(copy.start)
+        copies.append((needed, 0 if known is None else known, copy))
+    return copies
+
+
+def project(copies, attention, held, low, out, add):
     groups, _, columns = held.shape
     step = 512 if columns % 512 == 0 else columns
-    stores = []
     for group in range(groups):
-        for copy, (_, _, at) in zip(fetched, moves):
-            if group == (0 if at is None or at[0] else at[1]):
-                copy.wait()
+        for needed, at, copy in copies:
+            if at == group:
+                if needed is True:
+                    copy.wait()
+                else:
+                    pl.when(needed)(copy.wait)
         for j in range(columns // step):
             at = pl.ds(group * columns + j * step, step)
             projected = jnp.dot(
-                attention[...], held[group, :, pl.ds(j * step, step)], preferred_element_type=jnp.float32
+                attention[...],
+                held[group, pl.ds(low, attention.shape[1]), pl.ds(j * step, step)],
+                preferred_element_type=jnp.float32,
             )
-            out_v[:, at] = (
-                hidden_v[:, at].astype(jnp.float32) + projected + control_v[:, at].astype(jnp.float32)
-            ).astype(jnp.bfloat16)
-            stores.append(fetch(out_v.at[:, at], out.at[:, at]))
+            out(at, add(at) + projected)
+
+
+def begin_kernel(counts, moves, control_rows, place, hidden, ready, *refs):
+    weight, control = refs[: counts[0]], refs[counts[0] : sum(counts)]
+    out, attention, held, hidden_v, control_v, out_v, sems = refs[sum(counts) :]
+    fetch = Fetch(sems)
+    residual = [fetch(ready, attention), fetch(hidden, hidden_v)]
+    copies = fetch_weight(fetch, moves, place, weight, held, 0, ready.shape[1])
+    for d, block in enumerate(control):
+        start = pl.multiple_of((place[4] ^ d) * control_rows, control_rows) if len(control) > 1 else 0
+        residual.append(fetch(block, control_v.at[pl.ds(start, control_rows), :]))
+    for copy in residual:
+        copy.wait()
+    stores = []
+
+    def store(at, x):
+        out_v[:, at] = x
+        stores.append(fetch(out_v.at[:, at], out.at[:, at]))
+
+    project(
+        copies,
+        attention,
+        held,
+        0,
+        store,
+        lambda at: hidden_v[:, at].astype(jnp.float32) + control_v[:, at].astype(jnp.float32),
+    )
     for copy in stores:
         copy.wait()
 
 
-def finish(place, ready, weight, control, hidden, moves):
+def finish_kernel(slots, pieces, moves, first, place, active, q, part, stats, so_far, *refs):
+    near, weight, out, refs = refs[:slots], refs[slots : slots + pieces], refs[slots + pieces], refs[slots + pieces + 1 :]
+    q_v, near_v, (*state, stats_v, sems, attention, held, sum_v, out_v, late_sems) = (
+        refs[0],
+        refs[1 : slots + 1],
+        refs[slots + 1 :],
+    )
+    fetch, late_fetch = Fetch(sems), Fetch(late_sems)
+    low = first * HEAD_DIM
+    opened = close_open(fetch, first, q, part, stats, near, q_v, near_v, state, stats_v)
+    copies = fetch_weight(late_fetch, moves, place, weight, held, low, low + q_v.shape[1])
+    so_far_copy = late_fetch(so_far, sum_v)
+    close_heads(opened, first, active, q_v, near_v, state, stats_v, attention)
+    so_far_copy.wait()
+    stores = []
+
+    def store(at, x):
+        out_v[:, at] = x.astype(jnp.bfloat16)
+        stores.append(late_fetch(out_v.at[:, at], out.at[:, at]))
+
+    project(copies, attention, held, low, store, lambda at: sum_v[:, at])
+    for copy in stores:
+        copy.wait()
+
+
+def project_scratch(rows, columns, groups, inner, width, dtype, copies):
+    share = width // groups
+    return [
+        pltpu.VMEM((rows, columns), jnp.bfloat16),
+        pltpu.VMEM((groups, inner, share), jnp.bfloat16),
+    ], [
+        pltpu.VMEM((rows, width), dtype),
+        pltpu.SemaphoreType.DMA((copies + width // (512 if share % 512 == 0 else share),)),
+    ]
+
+
+def begin(place, ready, weight, control, hidden, moves, inner):
     rows, width = hidden.shape
-    inner = sum(x.shape[1] for x in ready)
-    groups = lax.axis_size("groups")
-    control_rows = control[0].shape[0]
-    share = width // groups
-    lists = (ready, weight, control)
-    counts = tuple(len(x) for x in lists)
-    step = 512 if share % 512 == 0 else share
+    columns = ready.shape[1]
+    before, behind = project_scratch(
+        rows, columns, lax.axis_size("groups"), inner, width, jnp.float32, 2 + len(moves) + len(control)
+    )
     return pl.pallas_call(
-        functools.partial(finish_kernel, counts, moves, control_rows),
-        out_shape=jax.ShapeDtypeStruct((rows, width), jnp.bfloat16),
-        in_specs=[SMEM] + [ANY] * (1 + sum(counts)),
+        functools.partial(begin_kernel, (len(weight), len(control)), moves, control[0].shape[0]),
+        out_shape=jax.ShapeDtypeStruct((rows, width), jnp.float32),
+        in_specs=[SMEM] + [ANY] * (2 + len(weight) + len(control)),
         out_specs=ANY,
-        scratch_shapes=[
-            pltpu.VMEM((rows, inner), jnp.bfloat16),
-            pltpu.VMEM((groups, inner, share), jnp.bfloat16),
-            pltpu.VMEM((rows, width), jnp.bfloat16),
-            pltpu.VMEM((rows, width), jnp.bfloat16),
-            pltpu.VMEM((rows, width), jnp.bfloat16),
-            pltpu.SemaphoreType.DMA((len(ready) + len(moves) + 1 + len(control) + width // step,)),
-        ],
+        scratch_shapes=before + [pltpu.VMEM((rows, width), jnp.bfloat16)] * 2 + behind,
         compiler_params=pltpu.CompilerParams(vmem_limit_bytes=VMEM_LIMIT),
         cost_estimate=pl.CostEstimate(
-            flops=2 * rows * inner * width, bytes_accessed=2 * inner * width + 6 * rows * width, transcendentals=0
+            flops=2 * rows * columns * width, bytes_accessed=2 * columns * width + 8 * rows * width, transcendentals=0
+        ),
+        name="begin",
+    )(place, hidden, ready, *weight, *control)
+
+
+def finish(place, active, q, state, near, first, so_far, weight, moves):
+    rows, inner = q.shape
+    width = so_far.shape[1]
+    columns = near[0].shape[1] // 2
+    before, behind = project_scratch(
+        rows, columns, lax.axis_size("groups"), inner, width, jnp.bfloat16, 1 + len(moves)
+    )
+    return pl.pallas_call(
+        functools.partial(finish_kernel, len(near), len(weight), moves, first),
+        out_shape=jax.ShapeDtypeStruct((rows, width), jnp.bfloat16),
+        in_specs=[SMEM] * 2 + [ANY] * (4 + len(near) + len(weight)),
+        out_specs=ANY,
+        scratch_shapes=close_scratch(rows, columns, len(near))
+        + before
+        + [pltpu.VMEM((rows, width), jnp.float32)]
+        + behind,
+        compiler_params=pltpu.CompilerParams(vmem_limit_bytes=VMEM_LIMIT),
+        cost_estimate=pl.CostEstimate(
+            flops=2 * rows * columns * width, bytes_accessed=2 * columns * width + 6 * rows * width, transcendentals=0
         ),
         name="finish",
-    )(place, hidden, *ready, *weight, *control)
+    )(place, active, q, *state, so_far, *near, *weight)
 
 
 def flipped(block, axis, flip):
@@ -332,32 +408,31 @@
         flip //= 2
     far = far_lane(swap("outer", 2), line)
     near = near_lane(swap("outer", 1), line)
-    last = swap("outer", 1)(after(far, near))
 
     firsts = [sum(CHUNKS[:i]) for i in range(len(CHUNKS))]
     chunks = [
         jnp.concatenate([x[:, f * HEAD_DIM : (f + n) * HEAD_DIM] for x in (keys, values)], axis=1)
         for f, n in zip(firsts, CHUNKS)
     ]
+    chunks = lax.optimization_barrier(chunks)
     block = rows // grid_width
     lines = after(control, line).reshape(block // TILE_W, grid_width, TILE_W, width)
     control_sent = [
         lax.dynamic_index_in_dim(lines, across ^ d, 1, keepdims=False).reshape(block, width) for d in range(grid_width)
     ]
     control_parts = [control_sent[0]] + [None] * (grid_width - 1)
-    early_x = []
-    for d in range(2, grid_width - 1):
-        control_parts[d] = swap(TILES, d)(after(control_sent[d], line))
-        early_x.append(control_parts[d])
-    control_parts[-1] = swap(TILES, grid_width - 1)(after(control_sent[-1], *early_x))
+    beside = swap("pair", 1)(line)
+    for d in range(2, grid_width):
+        control_parts[d] = swap(TILES, d)(after(control_sent[d], line if d < grid_width - 1 else beside))
     control_parts[1] = swap(TILES, 1)(control_sent[1])
-    plane = jnp.concatenate([line, swap("pair", 1)(line)])
+    plane = jnp.concatenate([line, beside])
+    last = swap("outer", 1)(after(far, near, *control_parts[2:-1]))
     held = [plane, swap("groups", 1)(plane)]
     crossed = [swap("core", 1)(x) for x in held]
     early_near = [[lax.ppermute(x, TILES, route) for x in (keys, values)] for _, _, route in early]
     state = attend(early_active, queries, [keys, values] + [x for kv in early_near for x in kv])
 
-    steps = after(jnp.concatenate([far, near, last]), control_parts[-1], held[1])
+    steps = after(jnp.concatenate([far, near, last]), *control_parts[2:], held[1])
     weight = [lax.all_gather(steps, ("groups", "pair", "core"))]
     n = len(line_flips)
     moves = [
@@ -381,7 +456,8 @@
     for chunk in chunks:
         lanes = (far_lane, near_lane)
         late_near.append([lanes[i % 2](route_of(route), chunk) for i, (_, _, route) in enumerate(late)])
-    ready = [close(late_active, queries, state, late_near[i], firsts[i]) for i in range(len(CHUNKS))]
+    ready = [close(late_active, queries, state, late_near[i], firsts[i]) for i in range(len(CHUNKS) - 1)]
+    ready = ready[0] if len(ready) == 1 else jnp.concatenate(ready, axis=1)
     if block % 16:
         control_parts = [
             jnp.take(
@@ -391,7 +467,9 @@
     place = jnp.stack([lax.axis_index(a) for a in ("groups",) + TILES] + [across]).astype(jnp.int32)
     if shard % 16:
         weight, moves = [in_order(weight, moves, place, (groups, outer, pair, cores))], [(0, None, None)]
-    return finish(place, ready, weight, control_parts, hidden, tuple(moves))
+    moves = tuple(moves)
+    so_far = begin(place, ready, weight, control_parts, hidden, moves, queries.shape[1])
+    return finish(place, late_active, queries, state, late_near[-1], firsts[-1], so_far, weight, moves)
 
 
 def in_order(weight, moves, place, sizes):

time: 117 us -> 114 us (0.974)
  the two profiles are of different devices: /device:TPU:0 before, /device:TPU:1 now
where the time goes in v9:
time: 114 us; the launch traced here: 112 us
  waiting for transfers between devices  37.3 us (33%)
  Pallas kernels  24.6 us (22%)
  starting transfers between devices  24.1 us (21%)
  between operations  16.1 us (14%)
  local copies, waits for them, and re-layouts  5.52 us (5%)
  other arithmetic  4.32 us (4%)
    ppermute x4, waiting for transfers between devices, route_of(): return lambda block: lax.ppermute(block, TILES, route)  19.1 us
    ppermute x10, starting transfers between devices, flipped(): lax.ppermute(block, axis, [(i, i ^ flip) for i in range(lax.axis_size(axi...  13 us
    ppermute x10, waiting for transfers between devices, flipped(): lax.ppermute(block, axis, [(i, i ^ flip) for i in range(lax.axis_size(axi...  12.5 us
    pallas_call x1, Pallas kernels, attend(): pl.pallas_call(functools.partial(attend_kernel, slots), out_shape=[jax.Sh...  7.3 us
    pallas_call x1, Pallas kernels, finish(): pl.pallas_call(functools.partial(finish_kernel, len(near), len(weight), m...  7.07 us
    ppermute x4, starting transfers between devices, on_device(): lax.ppermute(x, TILES, route)  6.71 us
    pallas_call x1, Pallas kernels, begin(): pl.pallas_call(functools.partial(begin_kernel, (len(weight), len(control)...  6.22 us
    ppermute x4, waiting for transfers between devices, on_device(): lax.ppermute(x, TILES, route)  4.53 us
  transfers between devices with their start and end apart: 19, of which 9 were waited for; matrix products, arithmetic and copies ran while one was open for 6% of the time, Pallas kernels for 16%

profile of v9, /device:TPU:1, one launch (start us, length us, event | category | flops | bytes accessed | tf_op | source)
XLA Modules:
  0.0 112.0 jit_solution(520229385427390143)
XLA Ops:
  6.5 1.1 slice_select_fusion
  7.6 2.1 %collective-permute-start.10 = (bf16[1,96,1536]{2,1,0:T(8,128)(2,1)S(1)}, bf16[1,96,1536]{2,1,0:T(8,128)(2,1)S(1)}, u32[]{:S(2)}, u32[]{:S(2)}) collective-permute-start(bf16[1,96,1536]{2,1,0:T(8,128)(2,1)S(1)} %bitcast.34), channel_id=1, source_target_pairs={{0,2},{2,0},{1,3},{3,1},{4,6},{6,4},{5,7},{7,5},{8,10},{10,8},{9,1... | collective-permute-start | bytes 884744 | tf_op jit(solution)/shard_map/ppermute | solution.py:335
  9.7 1.3 %collective-permute-start.6 = (bf16[1,96,1536]{2,1,0:T(8,128)(2,1)S(1)}, bf16[1,96,1536]{2,1,0:T(8,128)(2,1)S(1)}, u32[]{:S(2)}, u32[]{:S(2)}) collective-permute-start(bf16[1,96,1536]{2,1,0:T(8,128)(2,1)S(1)} %bitcast.35), channel_id=1, source_target_pairs={{0,4},{4,0},{8,12},{12,8},{1,5},{5,1},{9,13},{13,9},{2,6},{6,2},{1... | collective-permute-start | bytes 884744 | tf_op jit(solution)/shard_map/ppermute | solution.py:335
  11.0 2.3 %collective-permute-start.4 = (bf16[1,96,1536]{2,1,0:T(8,128)(2,1)S(1)}, bf16[1,96,1536]{2,1,0:T(8,128)(2,1)S(1)}, u32[]{:S(2)}, u32[]{:S(2)}) collective-permute-start(bf16[1,96,1536]{2,1,0:T(8,128)(2,1)S(1)} %bitcast.36), channel_id=1, source_target_pairs={{0,8},{4,12},{8,0},{12,4},{1,9},{5,13},{9,1},{13,5},{2,10},{6,14},... | collective-permute-start | bytes 884744 | tf_op jit(solution)/shard_map/ppermute | solution.py:335
  13.3 2.1 %dynamic-slice_bitcast_fusion = (bf16[48,3072]{1,0:T(8,128)(2,1)}, bf16[48,3072]{1,0:T(8,128)(2,1)}, bf16[48,3072]{1,0:T(8,128)(2,1)S(1)}, bf16[48,3072]{1,0:T(8,128)(2,1)S(1)}) fusion(bf16[6,4,8,3072]{3,2,1,0:T(8,128)(2,1)} %bitcast.38, s32[]{:T(128)S(6)} %select_n.109, s32[]{:T(128)S(6)} %select_n.108, s32[]{:T(128)S(6)} %select_n.107, s32[]{:T(128)S(6)} %select_n.106), kind=kLoop, calls=%fused_computation.4 | loop fusion | bytes 2359312 | tf_op jit(solution)/shard_map/reshape | solution.py:421
  15.5 0.3 collective-permute-start.8
  15.7 0.7 collective-permute-done.10
  16.5 0.1 pad_maximum_fusion.3.refs_1_.refs_3_
  16.5 1.2 %collective-permute-start.12 = (bf16[2,96,1536]{2,1,0:T(8,128)(2,1)S(1)}, bf16[2,96,1536]{2,1,0:T(8,128)(2,1)S(1)}, u32[]{:S(2)}, u32[]{:S(2)}) collective-permute-start(bf16[2,96,1536]{2,1,0:T(8,128)(2,1)S(1)} %pad_maximum_fusion.3.refs_1_.refs_3_), channel_id=1, source_target_pairs={{0,16},{16,0},{1,17},{17,1},{2,18},{18,2},{3,19},{19,3},{4,20},{20... | collective-permute-start | bytes 1769480 | tf_op jit(solution)/shard_map/ppermute | solution.py:335
  17.8 5.7 %collective-permute-done.6 = bf16[1,96,1536]{2,1,0:T(8,128)(2,1)S(1)} collective-permute-done((bf16[1,96,1536]{2,1,0:T(8,128)(2,1)S(1)}, bf16[1,96,1536]{2,1,0:T(8,128)(2,1)S(1)}, u32[]{:S(2)}, u32[]{:S(2)}) %collective-permute-start.6) | collective-permute-done | bytes 294944 | tf_op jit(solution)/shard_map/ppermute | solution.py:335
  23.5 2.5 %collective-permute-start.9 = (bf16[1,96,1536]{2,1,0:T(8,128)(2,1)S(1)}, bf16[1,96,1536]{2,1,0:T(8,128)(2,1)S(1)}, u32[]{:S(2)}, u32[]{:S(2)}) collective-permute-start(bf16[1,96,1536]{2,1,0:T(8,128)(2,1)S(1)} %collective-permute-done.4), channel_id=1, source_target_pairs={{0,4},{4,0},{8,12},{12,8},{1,5},{5,1},{9,13},{13,9},{2,6},{6,2},{1... | collective-permute-start | bytes 884744 | tf_op jit(solution)/shard_map/ppermute | solution.py:335
  26.0 2.6 %collective-permute-start.11 = (bf16[48,3072]{1,0:T(8,128)(2,1)S(1)}, bf16[48,3072]{1,0:T(8,128)(2,1)}, u32[]{:S(2)}, u32[]{:S(2)}) collective-permute-start(bf16[48,3072]{1,0:T(8,128)(2,1)S(1)} %get-tuple-element.26), channel_id=1, source_target_pairs={{0,3},{1,2},{2,1},{3,0},{4,7},{5,6},{6,5},{7,4},{8,11},{9,10},{10,... | collective-permute-start | bytes 884744 | tf_op jit(solution)/shard_map/ppermute | solution.py:335
  28.6 1.9 %collective-permute-done.9 = bf16[1,96,1536]{2,1,0:T(8,128)(2,1)S(1)} collective-permute-done((bf16[1,96,1536]{2,1,0:T(8,128)(2,1)S(1)}, bf16[1,96,1536]{2,1,0:T(8,128)(2,1)S(1)}, u32[]{:S(2)}, u32[]{:S(2)}) %collective-permute-start.9) | collective-permute-done | bytes 294944 | tf_op jit(solution)/shard_map/ppermute | solution.py:335
  30.5 1.0 pad_maximum_fusion
  31.5 4.2 %collective-permute-done.11.refs_8_ = bf16[48,3072]{1,0:T(8,128)(2,1)} collective-permute-done((bf16[48,3072]{1,0:T(8,128)(2,1)S(1)}, bf16[48,3072]{1,0:T(8,128)(2,1)}, u32[]{:S(2)}, u32[]{:S(2)}) %collective-permute-start.11) | collective-permute-done | bytes 294944 | tf_op jit(solution)/shard_map/ppermute | solution.py:335
  35.6 0.0 collective-permute-done.12.refs_3_.refs_5_
  35.7 0.0 all-gather.3.cloned.1.call-update
  35.7 4.2 %collective-permute-start.2 = (bf16[192,1536]{1,0:T(8,128)(2,1)S(1)}, bf16[192,1536]{1,0:T(8,128)(2,1)S(1)}, u32[]{:S(2)}, u32[]{:S(2)}) collective-permute-start(bf16[192,1536]{1,0:T(8,128)(2,1)S(1)} %copy-done.4), channel_id=1, source_target_pairs={{1,2},{2,1},{5,6},{6,5},{9,10},{10,9},{13,14},{14,13},{17,18},{18,... | collective-permute-start | bytes 1769480 | tf_op jit(solution)/shard_map/ppermute | solution.py:432
  40.0 0.0 copy-start.12
  40.0 0.9 pad_maximum_fusion.1
  41.0 1.9 %collective-permute-start.5 = (bf16[192,1536]{1,0:T(8,128)(2,1)S(1)}, bf16[192,1536]{1,0:T(8,128)(2,1)}, u32[]{:S(2)}, u32[]{:S(2)}) collective-permute-start(bf16[192,1536]{1,0:T(8,128)(2,1)S(1)} %get-tuple-element.22), channel_id=1, source_target_pairs={{0,8},{8,0},{1,9},{9,1},{2,10},{10,2},{3,11},{11,3},{4,12},{12,4},... | collective-permute-start | bytes 1769480 | tf_op jit(solution)/shard_map/ppermute | solution.py:352
  42.9 0.4 collective-permute-start.7
  43.3 0.0 collective-permute-start
  43.3 2.5 %collective-permute-start.3 = (bf16[192,1536]{1,0:T(8,128)(2,1)S(1)}, bf16[192,1536]{1,0:T(8,128)(2,1)S(1)}, u32[]{:S(2)}, u32[]{:S(2)}) collective-permute-start(bf16[192,1536]{1,0:T(8,128)(2,1)S(1)} %copy-done.5), channel_id=1, source_target_pairs={{1,2},{2,1},{5,6},{6,5},{9,10},{10,9},{13,14},{14,13},{17,18},{18,... | collective-permute-start | bytes 1769480 | tf_op jit(solution)/shard_map/ppermute | solution.py:432
  45.8 4.5 %collective-permute-done.2.refs_4_ = bf16[192,1536]{1,0:T(8,128)(2,1)S(1)} collective-permute-done((bf16[192,1536]{1,0:T(8,128)(2,1)S(1)}, bf16[192,1536]{1,0:T(8,128)(2,1)S(1)}, u32[]{:S(2)}, u32[]{:S(2)}) %collective-permute-start.2) | collective-permute-done | bytes 589856 | tf_op jit(solution)/shard_map/ppermute | solution.py:432
  50.3 0.0 collective-permute-start.1
  50.4 17.6 %collective-permute-done.5.refs_0_ = bf16[192,1536]{1,0:T(8,128)(2,1)} collective-permute-done((bf16[192,1536]{1,0:T(8,128)(2,1)S(1)}, bf16[192,1536]{1,0:T(8,128)(2,1)}, u32[]{:S(2)}, u32[]{:S(2)}) %collective-permute-start.5) | collective-permute-done | bytes 589856 | tf_op jit(solution)/shard_map/ppermute | solution.py:352
  68.0 0.0 collective-permute-start.13
  68.0 0.5 collective-permute-done.7.refs_1_
  68.5 0.1 collective-permute-start.14
  68.5 0.5 collective-permute-start.16
  69.1 0.0 collective-permute-done.3.refs_5_
  69.1 0.3 copy-done.8
  69.4 0.8 copy-done.9
  70.2 1.5 %collective-permute-start.17 = (bf16[192,1536]{1,0:T(8,128)(2,1)}, bf16[192,1536]{1,0:T(8,128)(2,1)}, u32[]{:S(2)}, u32[]{:S(2)}) collective-permute-start(bf16[192,1536]{1,0:T(8,128)(2,1)} %get-tuple-element.30), channel_id=1, source_target_pairs={{0,4},{4,0},{1,5},{5,1},{2,6},{6,2},{3,7},{7,3},{8,12},{12,8},{9,1... | collective-permute-start | bytes 1769480 | tf_op jit(solution)/shard_map/ppermute | solution.py:352
  71.7 0.7 constant_dynamic-slice_fusion.1
  73.6 0.0 collective-permute-done.1.refs_3_
  73.6 0.7 collective-permute-start.15
  74.3 0.6 add_convert_fusion.active
  76.3 0.6 stack.49.place
  76.9 0.6 add_convert_fusion.1.active
  77.5 7.3 %attend.1 = (f32[192,1536]{1,0:T(8,128)}, f32[192,128]{1,0:T(8,128)}) custom-call(s32[2]{0:T(128)} %add_convert_fusion.1.active, bf16[192,1536]{1,0:T(8,128)(2,1)} %q.5, bf16[192,1536]{1,0:T(8,128)(2,1)} %refs_0_.1, bf16[192,1536]{1,0:T(8,128)(2,1)} %refs_1_.1, bf16[192,1536]{1,0:T(8,128)(2,1)} %copy-done.8, ...), custom_call_target="tpu_custom_call" | custom-call | flops 1019215872 | bytes 5308416 | tf_op jit(solution)/shard_map/attend/pallas_call | solution.py:103
  84.8 4.0 %close.1.ready = bf16[192,768]{1,0:T(8,128)(2,1)} custom-call(s32[2]{0:T(128)} %add_convert_fusion.active, bf16[192,1536]{1,0:T(8,128)(2,1)} %q.5, f32[192,1536]{1,0:T(8,128)} %get-tuple-element.18.part, f32[192,128]{1,0:T(8,128)} %get-tuple-element.19.stats, bf16[192,1536]{1,0:T(8,128)(2,1)} %collective-permute-done.5.refs_0_, ...), custom_call_target="tpu_custom_call" | custom-call | flops 339738624 | bytes 2359296 | tf_op jit(solution)/shard_map/close/pallas_call | solution.py:168
  88.9 1.1 %all-gather.3.cloned.1.call-done = bf16[24,96,1536]{2,1,0:T(8,128)(2,1)} async-done(((bf16[3,96,1536]{2,1,0:T(8,128)(2,1)}), bf16[24,96,1536]{2,1,0:T(8,128)(2,1)}) %all-gather.3.cloned.1.call-update) | async-done | bytes 7077904 | tf_op jit(solution)/shard_map/all_gather | solution.py:436
  90.0 6.2 %begin.1.so_far = f32[192,3072]{1,0:T(8,128)} custom-call(s32[5]{0:T(128)} %stack.49.place, bf16[192,3072]{1,0:T(8,128)(2,1)} %hidden.1, bf16[192,768]{1,0:T(8,128)(2,1)} %close.1.ready, bf16[8,3,96,1536]{3,2,1,0:T(8,128)(2,1)} %bitcast.32, bf16[2,96,1536]{2,1,0:T(8,128)(2,1)} %copy-done, bf16[2,96,1536]{2,1,0:T(8,128)(2,1)} %copy-done.2, ...), custom_call_target="tpu_custom_call" | custom-call | flops 905969664 | bytes 9437184 | tf_op jit(solution)/shard_map/begin/pallas_call | solution.py:296
  96.3 1.0 collective-permute-done.16.refs_0_
  97.3 0.8 copy-done.7
  98.1 7.1 %finish.1 = bf16[192,3072]{1,0:T(8,128)(2,1)} custom-call(s32[5]{0:T(128)} %stack.49.place, s32[2]{0:T(128)} %add_convert_fusion.active, bf16[192,1536]{1,0:T(8,128)(2,1)} %q.5, f32[192,1536]{1,0:T(8,128)} %get-tuple-element.18.part, f32[192,128]{1,0:T(8,128)} %get-tuple-element.19.stats, f32[192,3072]{1,0:T(8,128)} %begin.1.so_far, ...), custom_call_target="tpu_custom_call" | custom-call | flops 905969664 | bytes 8257536 | tf_op jit(solution)/shard_map/finish/pallas_call | solution.py:317
  (32 shorter events, 0.1 us)
Async XLA Ops:
  6.5 83.5 %all-gather.3.cloned.1.call-start = ((), (), s32[]{:S(2)}) async-start(), calls=%async_computation | async-start | bytes 7962624 | tf_op jit(solution)/shard_map/all_gather | solution.py:436
  7.6 8.8 %collective-permute-start.10 = (bf16[1,96,1536]{2,1,0:T(8,128)(2,1)S(1)}, bf16[1,96,1536]{2,1,0:T(8,128)(2,1)S(1)}, u32[]{:S(2)}, u32[]{:S(2)}) collective-permute-start(bf16[1,96,1536]{2,1,0:T(8,128)(2,1)S(1)} %bitcast.34), channel_id=1, source_target_pairs={{0,2},{2,0},{1,3},{3,1},{4,6},{6,4},{5,7},{7,5},{8,10},{10,8},{9,1... | collective-permute-start | bytes 884744 | tf_op jit(solution)/shard_map/ppermute | solution.py:335
  9.7 13.8 %collective-permute-start.6 = (bf16[1,96,1536]{2,1,0:T(8,128)(2,1)S(1)}, bf16[1,96,1536]{2,1,0:T(8,128)(2,1)S(1)}, u32[]{:S(2)}, u32[]{:S(2)}) collective-permute-start(bf16[1,96,1536]{2,1,0:T(8,128)(2,1)S(1)} %bitcast.35), channel_id=1, source_target_pairs={{0,4},{4,0},{8,12},{12,8},{1,5},{5,1},{9,13},{13,9},{2,6},{6,2},{1... | collective-permute-start | bytes 884744 | tf_op jit(solution)/shard_map/ppermute | solution.py:335
  11.0 12.5 %collective-permute-start.4 = (bf16[1,96,1536]{2,1,0:T(8,128)(2,1)S(1)}, bf16[1,96,1536]{2,1,0:T(8,128)(2,1)S(1)}, u32[]{:S(2)}, u32[]{:S(2)}) collective-permute-start(bf16[1,96,1536]{2,1,0:T(8,128)(2,1)S(1)} %bitcast.36), channel_id=1, source_target_pairs={{0,8},{4,12},{8,0},{12,4},{1,9},{5,13},{9,1},{13,5},{2,10},{6,14},... | collective-permute-start | bytes 884744 | tf_op jit(solution)/shard_map/ppermute | solution.py:335
  15.5 8.0 %collective-permute-start.8 = (bf16[48,3072]{1,0:T(8,128)(2,1)S(1)}, bf16[48,3072]{1,0:T(8,128)(2,1)S(1)}, u32[]{:S(2)}, u32[]{:S(2)}) collective-permute-start(bf16[48,3072]{1,0:T(8,128)(2,1)S(1)} %get-tuple-element.24), channel_id=1, source_target_pairs={{0,2},{1,3},{2,0},{3,1},{4,6},{5,7},{6,4},{7,5},{8,10},{9,11},{10,... | collective-permute-start | bytes 884744 | tf_op jit(solution)/shard_map/ppermute | solution.py:335
  16.5 51.5 %copy-start = (bf16[2,96,1536]{2,1,0:T(8,128)(2,1)}, bf16[2,96,1536]{2,1,0:T(8,128)(2,1)S(1)}, u32[]{:S(2)}) copy-start(bf16[2,96,1536]{2,1,0:T(8,128)(2,1)S(1)} %pad_maximum_fusion.3.refs_1_.refs_3_) | copy-start | bytes 1769476
  16.5 19.1 %collective-permute-start.12 = (bf16[2,96,1536]{2,1,0:T(8,128)(2,1)S(1)}, bf16[2,96,1536]{2,1,0:T(8,128)(2,1)S(1)}, u32[]{:S(2)}, u32[]{:S(2)}) collective-permute-start(bf16[2,96,1536]{2,1,0:T(8,128)(2,1)S(1)} %pad_maximum_fusion.3.refs_1_.refs_3_), channel_id=1, source_target_pairs={{0,16},{16,0},{1,17},{17,1},{2,18},{18,2},{3,19},{19,3},{4,20},{20... | collective-permute-start | bytes 1769480 | tf_op jit(solution)/shard_map/ppermute | solution.py:335
  23.5 2.5 %copy-start.10 = (bf16[48,3072]{1,0:T(8,128)(2,1)}, bf16[48,3072]{1,0:T(8,128)(2,1)S(1)}, u32[]{:S(2)}) copy-start(bf16[48,3072]{1,0:T(8,128)(2,1)S(1)} %collective-permute-done.8.refs_7_) | copy-start | bytes 884740
  23.5 7.0 %collective-permute-start.9 = (bf16[1,96,1536]{2,1,0:T(8,128)(2,1)S(1)}, bf16[1,96,1536]{2,1,0:T(8,128)(2,1)S(1)}, u32[]{:S(2)}, u32[]{:S(2)}) collective-permute-start(bf16[1,96,1536]{2,1,0:T(8,128)(2,1)S(1)} %collective-permute-done.4), channel_id=1, source_target_pairs={{0,4},{4,0},{8,12},{12,8},{1,5},{5,1},{9,13},{13,9},{2,6},{6,2},{1... | collective-permute-start | bytes 884744 | tf_op jit(solution)/shard_map/ppermute | solution.py:335
  26.0 9.7 %copy-start.4 = (bf16[192,1536]{1,0:T(8,128)(2,1)S(1)}, bf16[192,1536]{1,0:T(8,128)(2,1)}, u32[]{:S(2)}) copy-start(bf16[192,1536]{1,0:T(8,128)(2,1)} %refs_0_.1) | copy-start | bytes 1769476
  26.0 9.7 %collective-permute-start.11 = (bf16[48,3072]{1,0:T(8,128)(2,1)S(1)}, bf16[48,3072]{1,0:T(8,128)(2,1)}, u32[]{:S(2)}, u32[]{:S(2)}) collective-permute-start(bf16[48,3072]{1,0:T(8,128)(2,1)S(1)} %get-tuple-element.26), channel_id=1, source_target_pairs={{0,3},{1,2},{2,1},{3,0},{4,7},{5,6},{6,5},{7,4},{8,11},{9,10},{10,... | collective-permute-start | bytes 884744 | tf_op jit(solution)/shard_map/ppermute | solution.py:335
  31.5 8.5 %copy-start.5 = (bf16[192,1536]{1,0:T(8,128)(2,1)S(1)}, bf16[192,1536]{1,0:T(8,128)(2,1)}, u32[]{:S(2)}) copy-start(bf16[192,1536]{1,0:T(8,128)(2,1)} %refs_1_.1) | copy-start | bytes 1769476
  35.6 32.8 %copy-start.1 = (bf16[2,96,1536]{2,1,0:T(8,128)(2,1)}, bf16[2,96,1536]{2,1,0:T(8,128)(2,1)S(1)}, u32[]{:S(2)}) copy-start(bf16[2,96,1536]{2,1,0:T(8,128)(2,1)S(1)} %collective-permute-done.12.refs_3_.refs_5_) | copy-start | bytes 1769476
  35.7 14.7 %collective-permute-start.2 = (bf16[192,1536]{1,0:T(8,128)(2,1)S(1)}, bf16[192,1536]{1,0:T(8,128)(2,1)S(1)}, u32[]{:S(2)}, u32[]{:S(2)}) collective-permute-start(bf16[192,1536]{1,0:T(8,128)(2,1)S(1)} %copy-done.4), channel_id=1, source_target_pairs={{1,2},{2,1},{5,6},{6,5},{9,10},{10,9},{13,14},{14,13},{17,18},{18,... | collective-permute-start | bytes 1769480 | tf_op jit(solution)/shard_map/ppermute | solution.py:432
  40.0 31.7 %copy-start.12 = (s32[1,6]{1,0:T(1,128)S(1)}, s32[1,6]{1,0:T(1,128)}, u32[]{:S(2)}) copy-start(s32[1,6]{1,0:T(1,128)} %param.13) | copy-start | bytes 76
  41.0 27.0 %collective-permute-start.5 = (bf16[192,1536]{1,0:T(8,128)(2,1)S(1)}, bf16[192,1536]{1,0:T(8,128)(2,1)}, u32[]{:S(2)}, u32[]{:S(2)}) collective-permute-start(bf16[192,1536]{1,0:T(8,128)(2,1)S(1)} %get-tuple-element.22), channel_id=1, source_target_pairs={{0,8},{8,0},{1,9},{9,1},{2,10},{10,2},{3,11},{11,3},{4,12},{12,4},... | collective-permute-start | bytes 1769480 | tf_op jit(solution)/shard_map/ppermute | solution.py:352
  42.9 25.5 %collective-permute-start.7 = (bf16[192,1536]{1,0:T(8,128)(2,1)S(1)}, bf16[192,1536]{1,0:T(8,128)(2,1)}, u32[]{:S(2)}, u32[]{:S(2)}) collective-permute-start(bf16[192,1536]{1,0:T(8,128)(2,1)S(1)} %get-tuple-element.22), channel_id=1, source_target_pairs={{0,4},{4,0},{1,5},{5,1},{2,6},{6,2},{3,7},{7,3},{8,12},{12,8},{9,1... | collective-permute-start | bytes 1769480 | tf_op jit(solution)/shard_map/ppermute | solution.py:352
  43.3 25.2 %collective-permute-start = (bf16[192,1536]{1,0:T(8,128)(2,1)S(1)}, bf16[192,1536]{1,0:T(8,128)(2,1)S(1)}, u32[]{:S(2)}, u32[]{:S(2)}) collective-permute-start(bf16[192,1536]{1,0:T(8,128)(2,1)S(1)} %copy-done.4), channel_id=1, source_target_pairs={{0,1},{1,0},{2,3},{3,2},{4,5},{5,4},{6,7},{7,6},{8,9},{9,8},{10,11... | collective-permute-start | bytes 1769480 | tf_op jit(solution)/shard_map/ppermute | solution.py:432
  43.3 25.7 %collective-permute-start.3 = (bf16[192,1536]{1,0:T(8,128)(2,1)S(1)}, bf16[192,1536]{1,0:T(8,128)(2,1)S(1)}, u32[]{:S(2)}, u32[]{:S(2)}) collective-permute-start(bf16[192,1536]{1,0:T(8,128)(2,1)S(1)} %copy-done.5), channel_id=1, source_target_pairs={{1,2},{2,1},{5,6},{6,5},{9,10},{10,9},{13,14},{14,13},{17,18},{18,... | collective-permute-start | bytes 1769480 | tf_op jit(solution)/shard_map/ppermute | solution.py:432
  50.3 18.7 %copy-start.6 = (bf16[192,1536]{1,0:T(8,128)(2,1)}, bf16[192,1536]{1,0:T(8,128)(2,1)S(1)}, u32[]{:S(2)}) copy-start(bf16[192,1536]{1,0:T(8,128)(2,1)S(1)} %collective-permute-done.2.refs_4_) | copy-start | bytes 1769476
  50.3 23.2 %collective-permute-start.1 = (bf16[192,1536]{1,0:T(8,128)(2,1)S(1)}, bf16[192,1536]{1,0:T(8,128)(2,1)}, u32[]{:S(2)}, u32[]{:S(2)}) collective-permute-start(bf16[192,1536]{1,0:T(8,128)(2,1)S(1)} %copy-done.5), channel_id=1, source_target_pairs={{0,1},{1,0},{2,3},{3,2},{4,5},{5,4},{6,7},{7,6},{8,9},{9,8},{10,11... | collective-permute-start | bytes 1769480 | tf_op jit(solution)/shard_map/ppermute | solution.py:432
  68.0 20.8 %collective-permute-start.13 = (bf16[2,96,1536]{2,1,0:T(8,128)(2,1)S(1)}, bf16[2,96,1536]{2,1,0:T(8,128)(2,1)S(1)}, u32[]{:S(2)}, u32[]{:S(2)}) collective-permute-start(bf16[2,96,1536]{2,1,0:T(8,128)(2,1)S(1)} %pad_maximum_fusion.3.refs_1_.refs_3_), channel_id=1, source_target_pairs={{0,1},{1,0},{2,3},{3,2},{4,5},{5,4},{6,7},{7,6},{8,9},{9,8},{10,11... | collective-permute-start | bytes 1769480 | tf_op jit(solution)/shard_map/ppermute | solution.py:335
  68.5 20.4 %collective-permute-start.14 = (bf16[2,96,1536]{2,1,0:T(8,128)(2,1)S(1)}, bf16[2,96,1536]{2,1,0:T(8,128)(2,1)S(1)}, u32[]{:S(2)}, u32[]{:S(2)}) collective-permute-start(bf16[2,96,1536]{2,1,0:T(8,128)(2,1)S(1)} %collective-permute-done.12.refs_3_.refs_5_), channel_id=1, source_target_pairs={{0,1},{1,0},{2,3},{3,2},{4,5},{5,4},{6,7},{7,6},{8,9},{9,8},{10,11... | collective-permute-start | bytes 1769480 | tf_op jit(solution)/shard_map/ppermute | solution.py:335
  68.5 0.9 copy-start.8
  68.5 28.7 %collective-permute-start.16 = (bf16[192,1536]{1,0:T(8,128)(2,1)}, bf16[192,1536]{1,0:T(8,128)(2,1)S(1)}, u32[]{:S(2)}, u32[]{:S(2)}) collective-permute-start(bf16[192,1536]{1,0:T(8,128)(2,1)} %get-tuple-element.30), channel_id=1, source_target_pairs={{0,8},{8,0},{1,9},{9,1},{2,10},{10,2},{3,11},{11,3},{4,12},{12,4},... | collective-permute-start | bytes 1769480 | tf_op jit(solution)/shard_map/ppermute | solution.py:352
  69.4 0.8 copy-start.9
  70.2 27.1 %collective-permute-start.17 = (bf16[192,1536]{1,0:T(8,128)(2,1)}, bf16[192,1536]{1,0:T(8,128)(2,1)}, u32[]{:S(2)}, u32[]{:S(2)}) collective-permute-start(bf16[192,1536]{1,0:T(8,128)(2,1)} %get-tuple-element.30), channel_id=1, source_target_pairs={{0,4},{4,0},{1,5},{5,1},{2,6},{6,2},{3,7},{7,3},{8,12},{12,8},{9,1... | collective-permute-start | bytes 1769480 | tf_op jit(solution)/shard_map/ppermute | solution.py:352
  73.6 15.2 %collective-permute-start.15 = (bf16[48,3072]{1,0:T(8,128)(2,1)}, bf16[48,3072]{1,0:T(8,128)(2,1)S(1)}, u32[]{:S(2)}, u32[]{:S(2)}) collective-permute-start(bf16[48,3072]{1,0:T(8,128)(2,1)} %get-tuple-element.31), channel_id=1, source_target_pairs={{0,1},{1,0},{2,3},{3,2},{4,5},{5,4},{6,7},{7,6},{8,9},{9,8},{10,11... | collective-permute-start | bytes 884744 | tf_op jit(solution)/shard_map/ppermute | solution.py:335
  88.8 1.2 %copy-start.11 = (bf16[48,3072]{1,0:T(8,128)(2,1)}, bf16[48,3072]{1,0:T(8,128)(2,1)S(1)}, u32[]{:S(2)}) copy-start(bf16[48,3072]{1,0:T(8,128)(2,1)S(1)} %collective-permute-done.15.refs_6_) | copy-start | bytes 884740
  88.8 1.2 %copy-start.2 = (bf16[2,96,1536]{2,1,0:T(8,128)(2,1)}, bf16[2,96,1536]{2,1,0:T(8,128)(2,1)S(1)}, u32[]{:S(2)}) copy-start(bf16[2,96,1536]{2,1,0:T(8,128)(2,1)S(1)} %collective-permute-done.13.refs_2_.refs_4_) | copy-start | bytes 1769476
  88.9 1.2 %copy-start.3 = (bf16[2,96,1536]{2,1,0:T(8,128)(2,1)}, bf16[2,96,1536]{2,1,0:T(8,128)(2,1)S(1)}, u32[]{:S(2)}) copy-start(bf16[2,96,1536]{2,1,0:T(8,128)(2,1)S(1)} %collective-permute-done.14.refs_4_.refs_6_) | copy-start | bytes 1769476
  97.3 0.8 copy-start.7
Sparse Core Ops, SparseCore 0:
  35.8 54.1 all-gather.2

commit v10 on v9

--- a/solution.py
+++ b/solution.py
@@ -14,6 +14,7 @@
 CHUNKS = (6, 6)
 SCALE = HEAD_DIM**-0.5 * math.log2(math.e)
 TILES = ("outer", "pair", "core")
+PLACE = 5
 VMEM_LIMIT = 60 * 1024 * 1024
 SMEM = pl.BlockSpec(memory_space=pltpu.SMEM)
 ANY = pl.BlockSpec(memory_space=pl.ANY)
@@ -69,7 +70,7 @@
         return copy
 
 
-def attend_kernel(slots, active, q, *refs):
+def attend_kernel(slots, info, q, *refs):
     kv, (part, stats), scratch = refs[: 2 * slots + 2], refs[2 * slots + 2 : 2 * slots + 4], refs[2 * slots + 4 :]
     q_v, kv_v, (part_v, total_v, peak_v, stats_v, sems) = scratch[0], scratch[1 : 2 * slots + 3], scratch[2 * slots + 3 :]
     fetch = Fetch(sems)
@@ -85,7 +86,7 @@
     for slot in range(slots):
         for copy in copies[3 + 2 * slot : 5 + 2 * slot]:
             copy.wait()
-        fold(state, active[slot], q_v, kv_v[2 * slot + 2], kv_v[2 * slot + 3])
+        fold(state, info[PLACE + slot], q_v, kv_v[2 * slot + 2], kv_v[2 * slot + 3])
     lane = lax.broadcasted_iota(jnp.int32, stats_v.shape, 1)
     packed = jnp.zeros(stats_v.shape, jnp.float32)
     for h in range(heads):
@@ -97,7 +98,7 @@
         copy.wait()
 
 
-def attend(active, q, kv):
+def attend(info, q, kv):
     rows, columns = q.shape
     slots = len(kv) // 2 - 1
     return pl.pallas_call(
@@ -118,7 +119,7 @@
             transcendentals=0,
         ),
         name="attend",
-    )(active, q, *kv)
+    )(info, q, *kv)
 
 
 def close_open(fetch, first, q, part, stats, near, q_v, near_v, state, stats_v):
@@ -131,7 +132,7 @@
     ] + [fetch(source, target) for source, target in zip(near, near_v)]
 
 
-def close_heads(copies, first, active, q_v, near_v, state, stats_v, out):
+def close_heads(copies, first, info, q_v, near_v, state, stats_v, out):
     columns = state[0].shape[1]
     for copy in copies[:3]:
         copy.wait()
@@ -141,7 +142,7 @@
             r[:, columns_of(h)] = jnp.broadcast_to(stats_now[:, lane : lane + 1], stats_now.shape)
     for slot, kv in enumerate(near_v):
         copies[3 + slot].wait()
-        fold(state, active[slot], q_v, kv.at[:, pl.ds(0, columns)], kv.at[:, pl.ds(columns, columns)])
+        fold(state, info[info.shape[0] - len(near_v) + slot], q_v, kv.at[:, pl.ds(0, columns)], kv.at[:, pl.ds(columns, columns)])
     out[...] = (state[0][...] / state[1][...]).astype(jnp.bfloat16)
 
 
@@ -154,16 +155,16 @@
     )
 
 
-def close_kernel(first, slots, active, q, part, stats, *refs):
+def close_kernel(first, slots, info, q, part, stats, *refs):
     near, out = refs[:slots], refs[slots]
     q_v, near_v, (*state, stats_v, sems, out_v) = refs[slots + 1], refs[slots + 2 : 2 * slots + 2], refs[2 * slots + 2 :]
     fetch = Fetch(sems)
     opened = close_open(fetch, first, q, part, stats, near, q_v, near_v, state, stats_v)
-    close_heads(opened, first, active, q_v, near_v, state, stats_v, out_v)
+    close_heads(opened, first, info, q_v, near_v, state, stats_v, out_v)
     fetch(out_v, out).wait()
 
 
-def close(active, q, state, near, first):
+def close(info, q, state, near, first):
     rows, columns = q.shape[0], near[0].shape[1] // 2
     return pl.pallas_call(
         functools.partial(close_kernel, first, len(near)),
@@ -178,7 +179,7 @@
             transcendentals=0,
         ),
         name="close",
-    )(active, q, *state, *near)
+    )(info, q, *state, *near)
 
 
 def fetch_weight(fetch, moves, place, weight, held, low, high):
@@ -251,7 +252,7 @@
         copy.wait()
 
 
-def finish_kernel(slots, pieces, moves, first, place, active, q, part, stats, so_far, *refs):
+def finish_kernel(slots, pieces, moves, first, info, q, part, stats, so_far, *refs):
     near, weight, out, refs = refs[:slots], refs[slots : slots + pieces], refs[slots + pieces], refs[slots + pieces + 1 :]
     q_v, near_v, (*state, stats_v, sems, attention, held, sum_v, out_v, late_sems) = (
         refs[0],
@@ -261,9 +262,9 @@
     fetch, late_fetch = Fetch(sems), Fetch(late_sems)
     low = first * HEAD_DIM
     opened = close_open(fetch, first, q, part, stats, near, q_v, near_v, state, stats_v)
-    copies = fetch_weight(late_fetch, moves, place, weight, held, low, low + q_v.shape[1])
+    copies = fetch_weight(late_fetch, moves, info, weight, held, low, low + q_v.shape[1])
     so_far_copy = late_fetch(so_far, sum_v)
-    close_heads(opened, first, active, q_v, near_v, state, stats_v, attention)
+    close_heads(opened, first, info, q_v, near_v, state, stats_v, attention)
     so_far_copy.wait()
     stores = []
 
@@ -287,7 +288,7 @@
     ]
 
 
-def begin(place, ready, weight, control, hidden, moves, inner):
+def begin(info, ready, weight, control, hidden, moves, inner):
     rows, width = hidden.shape
     columns = ready.shape[1]
     before, behind = project_scratch(
@@ -304,10 +305,10 @@
             flops=2 * rows * columns * width, bytes_accessed=2 * columns * width + 8 * rows * width, transcendentals=0
         ),
         name="begin",
-    )(place, hidden, ready, *weight, *control)
-
-
-def finish(place, active, q, state, near, first, so_far, weight, moves):
+    )(info, hidden, ready, *weight, *control)
+
+
+def finish(info, q, state, near, first, so_far, weight, moves):
     rows, inner = q.shape
     width = so_far.shape[1]
     columns = near[0].shape[1] // 2
@@ -317,7 +318,7 @@
     return pl.pallas_call(
         functools.partial(finish_kernel, len(near), len(weight), moves, first),
         out_shape=jax.ShapeDtypeStruct((rows, width), jnp.bfloat16),
-        in_specs=[SMEM] * 2 + [ANY] * (4 + len(near) + len(weight)),
+        in_specs=[SMEM] + [ANY] * (4 + len(near) + len(weight)),
         out_specs=ANY,
         scratch_shapes=close_scratch(rows, columns, len(near))
         + before
@@ -328,7 +329,7 @@
             flops=2 * rows * columns * width, bytes_accessed=2 * columns * width + 6 * rows * width, transcendentals=0
         ),
         name="finish",
-    )(place, active, q, *state, so_far, *near, *weight)
+    )(info, q, *state, so_far, *near, *weight)
 
 
 def flipped(block, axis, flip):
@@ -383,16 +384,13 @@
     early = [s for s in slots if s[0] == 2]
     late = [s for s in slots if s[0] != 2]
 
-    def flags(chosen):
-        active = []
-        for axis, odd, _ in chosen:
-            place = position // strides[axis] % counts[axis]
-            up = (place % 2 == odd).astype(jnp.int32)
-            valid = jnp.where(up == 1, place + 1 < counts[axis], place >= 1)
-            active.append((valid & (pattern[0, 2 * axis + up] == 1)).astype(jnp.int32))
-        return jnp.stack(active)
-
-    early_active, late_active = flags(early), flags(late)
+    info = [lax.axis_index(a) for a in ("groups",) + TILES] + [across]
+    for axis, odd, _ in early + late:
+        place = position // strides[axis] % counts[axis]
+        down = jnp.where(place >= 1, pattern[0, 2 * axis], 0)
+        up = jnp.where(place + 1 < counts[axis], pattern[0, 2 * axis + 1], 0)
+        info.append(jnp.where(place % 2 == odd, up, down))
+    info = jnp.stack([x.astype(jnp.int32) for x in info])
     far_lane, near_lane = Lane(), Lane()
 
     shard, share = out_weight.shape[0], width // groups
@@ -414,7 +412,7 @@
         jnp.concatenate([x[:, f * HEAD_DIM : (f + n) * HEAD_DIM] for x in (keys, values)], axis=1)
         for f, n in zip(firsts, CHUNKS)
     ]
-    chunks = lax.optimization_barrier(chunks)
+    chunks, info = lax.optimization_barrier((chunks, info))
     block = rows // grid_width
     lines = after(control, line).reshape(block // TILE_W, grid_width, TILE_W, width)
     control_sent = [
@@ -422,17 +420,22 @@
     ]
     control_parts = [control_sent[0]] + [None] * (grid_width - 1)
     beside = swap("pair", 1)(line)
-    for d in range(2, grid_width):
-        control_parts[d] = swap(TILES, d)(after(control_sent[d], line if d < grid_width - 1 else beside))
+    early_near = [[None, None] for _ in early]
+    for slot in range(1, len(early)):
+        early_near[slot][0] = lax.ppermute(after(keys, beside), TILES, early[slot][2])
+        early_near[slot][1] = lax.ppermute(after(values, early_near[slot][0]), TILES, early[slot][2])
+    for i, x in enumerate((keys, values)):
+        early_near[0][i] = lax.ppermute(x, TILES, early[0][2])
+    for d in range(2, grid_width - 1):
+        control_parts[d] = swap(TILES, d)(after(control_sent[d], line))
     control_parts[1] = swap(TILES, 1)(control_sent[1])
     plane = jnp.concatenate([line, beside])
-    last = swap("outer", 1)(after(far, near, *control_parts[2:-1]))
+    last = swap("outer", 1)(after(far, near, *control_parts[2:-1], *chunks, info))
     held = [plane, swap("groups", 1)(plane)]
     crossed = [swap("core", 1)(x) for x in held]
-    early_near = [[lax.ppermute(x, TILES, route) for x in (keys, values)] for _, _, route in early]
-    state = attend(early_active, queries, [keys, values] + [x for kv in early_near for x in kv])
-
-    steps = after(jnp.concatenate([far, near, last]), *control_parts[2:], held[1])
+    state = attend(info, queries, [keys, values] + [x for kv in early_near for x in kv])
+
+    steps = after(jnp.concatenate([far, near, last]), *[kv[0] for kv in early_near[1:]], held[1])
     weight = [lax.all_gather(steps, ("groups", "pair", "core"))]
     n = len(line_flips)
     moves = [
@@ -456,7 +459,8 @@
     for chunk in chunks:
         lanes = (far_lane, near_lane)
         late_near.append([lanes[i % 2](route_of(route), chunk) for i, (_, _, route) in enumerate(late)])
-    ready = [close(late_active, queries, state, late_near[i], firsts[i]) for i in range(len(CHUNKS) - 1)]
+    control_parts[-1] = swap(TILES, grid_width - 1)(after(control_sent[-1], *late_near[0]))
+    ready = [close(info, queries, state, late_near[i], firsts[i]) for i in range(len(CHUNKS) - 1)]
     ready = ready[0] if len(ready) == 1 else jnp.concatenate(ready, axis=1)
     if block % 16:
         control_parts = [
@@ -464,12 +468,11 @@
                 jnp.stack(control_parts), jnp.arange(grid_width, dtype=jnp.int32) ^ across, axis=0
             ).reshape(rows, width)
         ]
-    place = jnp.stack([lax.axis_index(a) for a in ("groups",) + TILES] + [across]).astype(jnp.int32)
     if shard % 16:
-        weight, moves = [in_order(weight, moves, place, (groups, outer, pair, cores))], [(0, None, None)]
+        weight, moves = [in_order(weight, moves, info, (groups, outer, pair, cores))], [(0, None, None)]
     moves = tuple(moves)
-    so_far = begin(place, ready, weight, control_parts, hidden, moves, queries.shape[1])
-    return finish(place, late_active, queries, state, late_near[-1], firsts[-1], so_far, weight, moves)
+    so_far = begin(info, ready, weight, control_parts, hidden, moves, queries.shape[1])
+    return finish(info, queries, state, late_near[-1], firsts[-1], so_far, weight, moves)
 
 
 def in_order(weight, moves, place, sizes):

time: 114 us -> 122 us (1.070)
  waiting for transfers between devices: 37.3 us -> 47.3 us
  starting transfers between devices: 24.1 us -> 19.2 us
  between operations: 16.1 us -> 17.5 us
    all_gather x1, waiting for transfers between devices: 1.14 us -> 7.9 us  [on_device(): weight = [lax.all_gather(steps, ('groups', 'pair', 'core'))]]
    ppermute x4, waiting for transfers between devices: 19.1 us -> 25.2 us  [route_of(): return lambda block: lax.ppermute(block, TILES, route)]
    ppermute x10, starting transfers between devices: 13 us -> 8.3 us  [flipped(): lax.ppermute(block, axis, [(i, i ^ flip) for i in range(lax.axis_size(axi...]
    ppermute x4, waiting for transfers between devices: 4.53 us -> 0.01 us  [the longest x2 0.01 us: on_device(): early_near[0][i] = lax.ppermute(x, TILES, early[0][2])]
    ppermute x4, starting transfers between devices: 4.41 us -> 0.85 us  [route_of(): return lambda block: lax.ppermute(block, TILES, route)]
    ppermute x4, starting transfers between devices: 6.71 us -> 10.1 us  [the longest x1 7.19 us: on_device(): lax.ppermute(after(keys, beside), TILES, early[slot][2])]
    ppermute x10, waiting for transfers between devices: 12.5 us -> 14.2 us  [flipped(): lax.ppermute(block, axis, [(i, i ^ flip) for i in range(lax.axis_size(axi...]
    pallas_call x1, Pallas kernels: 7.3 us -> 5.84 us  [attend(): pl.pallas_call(functools.partial(attend_kernel, slots), out_shape=[jax.Sh...]
  transfers between devices with their start and end apart: 19 -> 19, of which waited for: 9 -> 6; matrix products, arithmetic and copies ran while one was open for 6% -> 6% of each run, Pallas kernels for 16% -> 14%
where the time goes in v10:
time: 122 us; the launch traced here: 121 us
  waiting for transfers between devices  47.3 us (39%)
  Pallas kernels  25 us (20%)
  starting transfers between devices  19.2 us (16%)
  between operations  17.5 us (14%)
  local copies, waits for them, and re-layouts  6.67 us (5%)
  other arithmetic  5.19 us (4%)
    ppermute x4, waiting for transfers between devices, route_of(): return lambda block: lax.ppermute(block, TILES, route)  25.2 us
    ppermute x10, waiting for transfers between devices, flipped(): lax.ppermute(block, axis, [(i, i ^ flip) for i in range(lax.axis_size(axi...  14.2 us
    ppermute x10, starting transfers between devices, flipped(): lax.ppermute(block, axis, [(i, i ^ flip) for i in range(lax.axis_size(axi...  8.3 us
    pallas_call x1, Pallas kernels, finish(): pl.pallas_call(functools.partial(finish_kernel, len(near), len(weight), m...  7.97 us
    all_gather x1, waiting for transfers between devices, on_device(): weight = [lax.all_gather(steps, ('groups', 'pair', 'core'))]  7.9 us
    ppermute x1, starting transfers between devices, on_device(): lax.ppermute(after(keys, beside), TILES, early[slot][2])  7.19 us
    pallas_call x1, Pallas kernels, begin(): pl.pallas_call(functools.partial(begin_kernel, (len(weight), len(control)...  6.25 us
    pallas_call x1, Pallas kernels, attend(): pl.pallas_call(functools.partial(attend_kernel, slots), out_shape=[jax.Sh...  5.84 us
  transfers between devices with their start and end apart: 19, of which 6 were waited for; matrix products, arithmetic and copies ran while one was open for 6% of the time, Pallas kernels for 14%

profile of v10, /device:TPU:1, one launch (start us, length us, event | category | flops | bytes accessed | tf_op | source)
XLA Modules:
  0.0 120.9 jit_solution(8602106925408224890)
XLA Ops:
  6.5 1.1 slice_select_fusion
  7.6 2.2 %collective-permute-start.7 = (bf16[1,96,1536]{2,1,0:T(8,128)(2,1)S(1)}, bf16[1,96,1536]{2,1,0:T(8,128)(2,1)S(1)}, u32[]{:S(2)}, u32[]{:S(2)}) collective-permute-start(bf16[1,96,1536]{2,1,0:T(8,128)(2,1)S(1)} %bitcast.36), channel_id=1, source_target_pairs={{0,4},{4,0},{8,12},{12,8},{1,5},{5,1},{9,13},{13,9},{2,6},{6,2},{1... | collective-permute-start | bytes 884744 | tf_op jit(solution)/shard_map/ppermute | solution.py:336
  9.8 2.3 %collective-permute-start.5 = (bf16[1,96,1536]{2,1,0:T(8,128)(2,1)S(1)}, bf16[1,96,1536]{2,1,0:T(8,128)(2,1)}, u32[]{:S(2)}, u32[]{:S(2)}) collective-permute-start(bf16[1,96,1536]{2,1,0:T(8,128)(2,1)S(1)} %bitcast.37), channel_id=1, source_target_pairs={{0,8},{4,12},{8,0},{12,4},{1,9},{5,13},{9,1},{13,5},{2,10},{6,14},... | collective-permute-start | bytes 884744 | tf_op jit(solution)/shard_map/ppermute | solution.py:336
  12.1 1.2 %collective-permute-start.2 = (bf16[1,96,1536]{2,1,0:T(8,128)(2,1)S(1)}, bf16[1,96,1536]{2,1,0:T(8,128)(2,1)}, u32[]{:S(2)}, u32[]{:S(2)}) collective-permute-start(bf16[1,96,1536]{2,1,0:T(8,128)(2,1)S(1)} %bitcast.38), channel_id=1, source_target_pairs={{0,2},{2,0},{1,3},{3,1},{4,6},{6,4},{5,7},{7,5},{8,10},{10,8},{9,1... | collective-permute-start | bytes 884744 | tf_op jit(solution)/shard_map/ppermute | solution.py:336
  13.3 2.3 %dynamic-slice_bitcast_fusion = (bf16[48,3072]{1,0:T(8,128)(2,1)}, bf16[48,3072]{1,0:T(8,128)(2,1)}, bf16[48,3072]{1,0:T(8,128)(2,1)}, bf16[48,3072]{1,0:T(8,128)(2,1)}) fusion(bf16[6,4,8,3072]{3,2,1,0:T(8,128)(2,1)} %bitcast.40, s32[]{:T(128)S(6)} %select_n.119, s32[]{:T(128)S(6)} %select_n.118, s32[]{:T(128)S(6)} %select_n.117, s32[]{:T(128)S(6)} %select_n.116), kind=kLoop, calls=%fused_computation.4 | loop fusion | bytes 2359312 | tf_op jit(solution)/shard_map/reshape | solution.py:419
  15.7 0.3 collective-permute-start.9
  16.0 0.8 copy-done.5
  16.8 1.1 pad_maximum_fusion.1
  17.9 1.6 %collective-permute-done.2 = bf16[1,96,1536]{2,1,0:T(8,128)(2,1)} collective-permute-done((bf16[1,96,1536]{2,1,0:T(8,128)(2,1)S(1)}, bf16[1,96,1536]{2,1,0:T(8,128)(2,1)}, u32[]{:S(2)}, u32[]{:S(2)}) %collective-permute-start.2) | collective-permute-done | bytes 294944 | tf_op jit(solution)/shard_map/ppermute | solution.py:336
  19.5 1.0 pad_maximum_fusion.3.refs_1_.refs_3_
  20.5 1.3 %collective-permute-start.11 = (bf16[2,96,1536]{2,1,0:T(8,128)(2,1)S(1)}, bf16[2,96,1536]{2,1,0:T(8,128)(2,1)S(1)}, u32[]{:S(2)}, u32[]{:S(2)}) collective-permute-start(bf16[2,96,1536]{2,1,0:T(8,128)(2,1)S(1)} %pad_maximum_fusion.3.refs_1_.refs_3_), channel_id=1, source_target_pairs={{0,16},{16,0},{1,17},{17,1},{2,18},{18,2},{3,19},{19,3},{4,20},{20... | collective-permute-start | bytes 1769480 | tf_op jit(solution)/shard_map/ppermute | solution.py:336
  21.8 7.2 %collective-permute-start.3 = (bf16[192,1536]{1,0:T(8,128)(2,1)S(1)}, bf16[192,1536]{1,0:T(8,128)(2,1)S(1)}, u32[]{:S(2)}, u32[]{:S(2)}) collective-permute-start(bf16[192,1536]{1,0:T(8,128)(2,1)S(1)} %copy-done.4), channel_id=1, source_target_pairs={{1,2},{2,1},{5,6},{6,5},{9,10},{10,9},{13,14},{14,13},{17,18},{18,... | collective-permute-start | bytes 1769480 | tf_op jit(solution)/shard_map/ppermute | solution.py:425
  29.0 0.7 fusion.2
  33.6 0.6 stack.39.info.place
  34.2 0.0 collective-permute-done.7
  34.2 0.0 collective-permute-done.5
  34.2 0.0 collective-permute-done.9.refs_7_
  34.2 0.2 collective-permute-start.10
  34.5 6.9 %collective-permute-done.10 = bf16[1,96,1536]{2,1,0:T(8,128)(2,1)S(1)} collective-permute-done((bf16[1,96,1536]{2,1,0:T(8,128)(2,1)}, bf16[1,96,1536]{2,1,0:T(8,128)(2,1)S(1)}, u32[]{:S(2)}, u32[]{:S(2)}) %collective-permute-start.10) | collective-permute-done | bytes 294944 | tf_op jit(solution)/shard_map/ppermute | solution.py:336
  41.4 2.0 %pad_maximum_fusion = bf16[3,96,1536]{2,1,0:T(8,128)(2,1)} fusion(bf16[1,96,1536]{2,1,0:T(8,128)(2,1)S(1)} %collective-permute-done.10, bf16[1,96,1536]{2,1,0:T(8,128)(2,1)S(1)} %collective-permute-done.7, bf16[1,96,1536]{2,1,0:T(8,128)(2,1)} %collective-permute-done.5), kind=kLoop, calls=%fused_computation | loop fusion | flops 884736 | bytes 1769472 | tf_op jit(solution)/shard_map/concatenate | solution.py:438
  43.4 0.0 collective-permute-done.11.refs_3_.refs_5_
  43.4 0.0 collective-permute-done.3.refs_4_
  43.4 0.0 all-gather.3.cloned.1.call-update
  43.4 0.1 collective-permute-start.14
  43.5 0.1 collective-permute-start.6
  43.6 0.2 collective-permute-start.8
  43.8 1.0 collective-permute-start
  44.8 0.0 collective-permute-start.1
  44.8 0.5 collective-permute-done.14.refs_6_
  45.3 1.9 %collective-permute-start.4 = (bf16[192,1536]{1,0:T(8,128)(2,1)S(1)}, bf16[192,1536]{1,0:T(8,128)(2,1)S(1)}, u32[]{:S(2)}, u32[]{:S(2)}) collective-permute-start(bf16[192,1536]{1,0:T(8,128)(2,1)S(1)} %copy-done.5), channel_id=1, source_target_pairs={{1,2},{2,1},{5,6},{6,5},{9,10},{10,9},{13,14},{14,13},{17,18},{18,... | collective-permute-start | bytes 1769480 | tf_op jit(solution)/shard_map/ppermute | solution.py:426
  47.2 25.2 %collective-permute-done.6.refs_0_ = bf16[192,1536]{1,0:T(8,128)(2,1)S(1)} collective-permute-done((bf16[192,1536]{1,0:T(8,128)(2,1)}, bf16[192,1536]{1,0:T(8,128)(2,1)S(1)}, u32[]{:S(2)}, u32[]{:S(2)}) %collective-permute-start.6) | collective-permute-done | bytes 589856 | tf_op jit(solution)/shard_map/ppermute | solution.py:353
  72.5 0.5 collective-permute-start.12
  73.0 0.0 collective-permute-done.8.refs_1_
  73.0 0.1 collective-permute-start.13
  73.1 0.2 collective-permute-start.16
  73.3 0.3 collective-permute-start.17
  73.6 0.2 copy-done.12
  73.8 0.2 copy-done.8
  74.0 0.2 copy-done.9
  74.2 0.8 copy-done.10
  75.0 0.2 collective-permute-start.15
  75.1 5.8 %attend.1 = (f32[192,1536]{1,0:T(8,128)}, f32[192,128]{1,0:T(8,128)}) custom-call(s32[9]{0:T(128)} %stack.39.info.place, bf16[192,1536]{1,0:T(8,128)(2,1)} %q.5, bf16[192,1536]{1,0:T(8,128)(2,1)} %refs_0_.1, bf16[192,1536]{1,0:T(8,128)(2,1)} %refs_1_.1, bf16[192,1536]{1,0:T(8,128)(2,1)} %copy-done.8, bf16[192,1536]{1,0:T(8,128)(2,1)} %copy-done.9, ...), custom_call_target="tpu_custom_call" | custom-call | flops 1019215872 | bytes 5308416 | tf_op jit(solution)/shard_map/attend/pallas_call | solution.py:104
  81.0 4.9 %close.1.ready = bf16[192,768]{1,0:T(8,128)(2,1)} custom-call(s32[9]{0:T(128)} %stack.39.info.place, bf16[192,1536]{1,0:T(8,128)(2,1)} %q.5, f32[192,1536]{1,0:T(8,128)} %get-tuple-element.24.part, f32[192,128]{1,0:T(8,128)} %get-tuple-element.25.stats, bf16[192,1536]{1,0:T(8,128)(2,1)} %copy-done.11, bf16[192,1536]{1,0:T(8,128)(2,1)} %copy-done.12), custom_call_target="tpu_custom_call" | custom-call | flops 339738624 | bytes 2359296 | tf_op jit(solution)/shard_map/close/pallas_call | solution.py:169
  86.0 5.1 %collective-permute-done.15.refs_8_ = bf16[48,3072]{1,0:T(8,128)(2,1)S(1)} collective-permute-done((bf16[48,3072]{1,0:T(8,128)(2,1)}, bf16[48,3072]{1,0:T(8,128)(2,1)S(1)}, u32[]{:S(2)}, u32[]{:S(2)}) %collective-permute-start.15) | collective-permute-done | bytes 294944 | tf_op jit(solution)/shard_map/ppermute | solution.py:336
  91.1 7.9 %all-gather.3.cloned.1.call-done = bf16[24,96,1536]{2,1,0:T(8,128)(2,1)} async-done(((bf16[3,96,1536]{2,1,0:T(8,128)(2,1)}), bf16[24,96,1536]{2,1,0:T(8,128)(2,1)}) %all-gather.3.cloned.1.call-update) | async-done | bytes 7077904 | tf_op jit(solution)/shard_map/all_gather | solution.py:439
  99.0 6.2 %begin.1.so_far = f32[192,3072]{1,0:T(8,128)} custom-call(s32[9]{0:T(128)} %stack.39.info.place, bf16[192,3072]{1,0:T(8,128)(2,1)} %hidden.1, bf16[192,768]{1,0:T(8,128)(2,1)} %close.1.ready, bf16[8,3,96,1536]{3,2,1,0:T(8,128)(2,1)} %bitcast.34, bf16[2,96,1536]{2,1,0:T(8,128)(2,1)} %copy-done, bf16[2,96,1536]{2,1,0:T(8,128)(2,1)} %copy-done.2, ...), custom_call_target="tpu_custom_call" | custom-call | flops 905969664 | bytes 9437184 | tf_op jit(solution)/shard_map/begin/pallas_call | solution.py:297
  105.3 0.8 copy-done.7
  106.1 8.0 %finish.1 = bf16[192,3072]{1,0:T(8,128)(2,1)} custom-call(s32[9]{0:T(128)} %stack.39.info.place, bf16[192,1536]{1,0:T(8,128)(2,1)} %q.5, f32[192,1536]{1,0:T(8,128)} %get-tuple-element.24.part, f32[192,128]{1,0:T(8,128)} %get-tuple-element.25.stats, f32[192,3072]{1,0:T(8,128)} %begin.1.so_far, bf16[192,1536]{1,0:T(8,128)(2,1)} %copy-done.7, ...), custom_call_target="tpu_custom_call" | custom-call | flops 905969664 | bytes 8257536 | tf_op jit(solution)/shard_map/finish/pallas_call | solution.py:318
  (36 shorter events, 0.1 us)
Async XLA Ops:
  6.5 92.4 %all-gather.3.cloned.1.call-start = ((), (), s32[]{:S(2)}) async-start(), calls=%async_computation | async-start | bytes 7962624 | tf_op jit(solution)/shard_map/all_gather | solution.py:439
  7.6 26.6 %collective-permute-start.7 = (bf16[1,96,1536]{2,1,0:T(8,128)(2,1)S(1)}, bf16[1,96,1536]{2,1,0:T(8,128)(2,1)S(1)}, u32[]{:S(2)}, u32[]{:S(2)}) collective-permute-start(bf16[1,96,1536]{2,1,0:T(8,128)(2,1)S(1)} %bitcast.36), channel_id=1, source_target_pairs={{0,4},{4,0},{8,12},{12,8},{1,5},{5,1},{9,13},{13,9},{2,6},{6,2},{1... | collective-permute-start | bytes 884744 | tf_op jit(solution)/shard_map/ppermute | solution.py:336
  9.8 24.4 %collective-permute-start.5 = (bf16[1,96,1536]{2,1,0:T(8,128)(2,1)S(1)}, bf16[1,96,1536]{2,1,0:T(8,128)(2,1)}, u32[]{:S(2)}, u32[]{:S(2)}) collective-permute-start(bf16[1,96,1536]{2,1,0:T(8,128)(2,1)S(1)} %bitcast.37), channel_id=1, source_target_pairs={{0,8},{4,12},{8,0},{12,4},{1,9},{5,13},{9,1},{13,5},{2,10},{6,14},... | collective-permute-start | bytes 884744 | tf_op jit(solution)/shard_map/ppermute | solution.py:336
  12.1 7.4 %collective-permute-start.2 = (bf16[1,96,1536]{2,1,0:T(8,128)(2,1)S(1)}, bf16[1,96,1536]{2,1,0:T(8,128)(2,1)}, u32[]{:S(2)}, u32[]{:S(2)}) collective-permute-start(bf16[1,96,1536]{2,1,0:T(8,128)(2,1)S(1)} %bitcast.38), channel_id=1, source_target_pairs={{0,2},{2,0},{1,3},{3,1},{4,6},{6,4},{5,7},{7,5},{8,10},{10,8},{9,1... | collective-permute-start | bytes 884744 | tf_op jit(solution)/shard_map/ppermute | solution.py:336
  13.3 2.6 %copy-start.4 = (bf16[192,1536]{1,0:T(8,128)(2,1)S(1)}, bf16[192,1536]{1,0:T(8,128)(2,1)}, u32[]{:S(2)}) copy-start(bf16[192,1536]{1,0:T(8,128)(2,1)} %refs_0_.1) | copy-start | bytes 1769476
  15.7 1.1 copy-start.5
  15.7 18.6 %collective-permute-start.9 = (bf16[48,3072]{1,0:T(8,128)(2,1)}, bf16[48,3072]{1,0:T(8,128)(2,1)}, u32[]{:S(2)}, u32[]{:S(2)}) collective-permute-start(bf16[48,3072]{1,0:T(8,128)(2,1)} %get-tuple-element.30), channel_id=1, source_target_pairs={{0,2},{1,3},{2,0},{3,1},{4,6},{5,7},{6,4},{7,5},{8,10},{9,11},{10,... | collective-permute-start | bytes 884744 | tf_op jit(solution)/shard_map/ppermute | solution.py:336
  17.9 11.2 %copy-start.15 = (s32[1,6]{1,0:T(1,128)S(1)}, s32[1,6]{1,0:T(1,128)}, u32[]{:S(2)}) copy-start(s32[1,6]{1,0:T(1,128)} %param.13) | copy-start | bytes 76
  20.5 52.0 %copy-start = (bf16[2,96,1536]{2,1,0:T(8,128)(2,1)}, bf16[2,96,1536]{2,1,0:T(8,128)(2,1)S(1)}, u32[]{:S(2)}) copy-start(bf16[2,96,1536]{2,1,0:T(8,128)(2,1)S(1)} %pad_maximum_fusion.3.refs_1_.refs_3_) | copy-start | bytes 1769476
  20.5 22.9 %collective-permute-start.11 = (bf16[2,96,1536]{2,1,0:T(8,128)(2,1)S(1)}, bf16[2,96,1536]{2,1,0:T(8,128)(2,1)S(1)}, u32[]{:S(2)}, u32[]{:S(2)}) collective-permute-start(bf16[2,96,1536]{2,1,0:T(8,128)(2,1)S(1)} %pad_maximum_fusion.3.refs_1_.refs_3_), channel_id=1, source_target_pairs={{0,16},{16,0},{1,17},{17,1},{2,18},{18,2},{3,19},{19,3},{4,20},{20... | collective-permute-start | bytes 1769480 | tf_op jit(solution)/shard_map/ppermute | solution.py:336
  21.8 21.6 %collective-permute-start.3 = (bf16[192,1536]{1,0:T(8,128)(2,1)S(1)}, bf16[192,1536]{1,0:T(8,128)(2,1)S(1)}, u32[]{:S(2)}, u32[]{:S(2)}) collective-permute-start(bf16[192,1536]{1,0:T(8,128)(2,1)S(1)} %copy-done.4), channel_id=1, source_target_pairs={{1,2},{2,1},{5,6},{6,5},{9,10},{10,9},{13,14},{14,13},{17,18},{18,... | collective-permute-start | bytes 1769480 | tf_op jit(solution)/shard_map/ppermute | solution.py:425
  34.2 7.2 %collective-permute-start.10 = (bf16[1,96,1536]{2,1,0:T(8,128)(2,1)}, bf16[1,96,1536]{2,1,0:T(8,128)(2,1)S(1)}, u32[]{:S(2)}, u32[]{:S(2)}) collective-permute-start(bf16[1,96,1536]{2,1,0:T(8,128)(2,1)} %collective-permute-done.5), channel_id=1, source_target_pairs={{0,4},{4,0},{8,12},{12,8},{1,5},{5,1},{9,13},{13,9},{2,6},{6,2},{1... | collective-permute-start | bytes 884744 | tf_op jit(solution)/shard_map/ppermute | solution.py:336
  43.4 37.6 %copy-start.1 = (bf16[2,96,1536]{2,1,0:T(8,128)(2,1)}, bf16[2,96,1536]{2,1,0:T(8,128)(2,1)S(1)}, u32[]{:S(2)}) copy-start(bf16[2,96,1536]{2,1,0:T(8,128)(2,1)S(1)} %collective-permute-done.11.refs_3_.refs_5_) | copy-start | bytes 1769476
  43.4 3.8 %copy-start.6 = (bf16[192,1536]{1,0:T(8,128)(2,1)}, bf16[192,1536]{1,0:T(8,128)(2,1)S(1)}, u32[]{:S(2)}) copy-start(bf16[192,1536]{1,0:T(8,128)(2,1)S(1)} %collective-permute-done.3.refs_4_) | copy-start | bytes 1769476
  43.4 1.9 %collective-permute-start.14 = (bf16[48,3072]{1,0:T(8,128)(2,1)}, bf16[48,3072]{1,0:T(8,128)(2,1)S(1)}, u32[]{:S(2)}, u32[]{:S(2)}) collective-permute-start(bf16[48,3072]{1,0:T(8,128)(2,1)} %get-tuple-element.38), channel_id=1, source_target_pairs={{0,1},{1,0},{2,3},{3,2},{4,5},{5,4},{6,7},{7,6},{8,9},{9,8},{10,11... | collective-permute-start | bytes 884744 | tf_op jit(solution)/shard_map/ppermute | solution.py:336
  43.5 29.0 %collective-permute-start.6 = (bf16[192,1536]{1,0:T(8,128)(2,1)}, bf16[192,1536]{1,0:T(8,128)(2,1)S(1)}, u32[]{:S(2)}, u32[]{:S(2)}) collective-permute-start(bf16[192,1536]{1,0:T(8,128)(2,1)} %get-tuple-element.28), channel_id=1, source_target_pairs={{0,8},{8,0},{1,9},{9,1},{2,10},{10,2},{3,11},{11,3},{4,12},{12,4},... | collective-permute-start | bytes 1769480 | tf_op jit(solution)/shard_map/ppermute | solution.py:353
  43.6 29.3 %collective-permute-start.8 = (bf16[192,1536]{1,0:T(8,128)(2,1)}, bf16[192,1536]{1,0:T(8,128)(2,1)S(1)}, u32[]{:S(2)}, u32[]{:S(2)}) collective-permute-start(bf16[192,1536]{1,0:T(8,128)(2,1)} %get-tuple-element.28), channel_id=1, source_target_pairs={{0,4},{4,0},{1,5},{5,1},{2,6},{6,2},{3,7},{7,3},{8,12},{12,8},{9,1... | collective-permute-start | bytes 1769480 | tf_op jit(solution)/shard_map/ppermute | solution.py:353
  43.8 29.2 %collective-permute-start = (bf16[192,1536]{1,0:T(8,128)(2,1)S(1)}, bf16[192,1536]{1,0:T(8,128)(2,1)S(1)}, u32[]{:S(2)}, u32[]{:S(2)}) collective-permute-start(bf16[192,1536]{1,0:T(8,128)(2,1)S(1)} %copy-done.4), channel_id=1, source_target_pairs={{0,1},{1,0},{2,3},{3,2},{4,5},{5,4},{6,7},{7,6},{8,9},{9,8},{10,11... | collective-permute-start | bytes 1769480 | tf_op jit(solution)/shard_map/ppermute | solution.py:428
  44.8 28.5 %collective-permute-start.1 = (bf16[192,1536]{1,0:T(8,128)(2,1)S(1)}, bf16[192,1536]{1,0:T(8,128)(2,1)S(1)}, u32[]{:S(2)}, u32[]{:S(2)}) collective-permute-start(bf16[192,1536]{1,0:T(8,128)(2,1)S(1)} %copy-done.5), channel_id=1, source_target_pairs={{0,1},{1,0},{2,3},{3,2},{4,5},{5,4},{6,7},{7,6},{8,9},{9,8},{10,11... | collective-permute-start | bytes 1769480 | tf_op jit(solution)/shard_map/ppermute | solution.py:428
  45.3 1.9 %copy-start.13 = (bf16[48,3072]{1,0:T(8,128)(2,1)}, bf16[48,3072]{1,0:T(8,128)(2,1)S(1)}, u32[]{:S(2)}) copy-start(bf16[48,3072]{1,0:T(8,128)(2,1)S(1)} %collective-permute-done.14.refs_6_) | copy-start | bytes 884740
  45.3 28.3 %collective-permute-start.4 = (bf16[192,1536]{1,0:T(8,128)(2,1)S(1)}, bf16[192,1536]{1,0:T(8,128)(2,1)S(1)}, u32[]{:S(2)}, u32[]{:S(2)}) collective-permute-start(bf16[192,1536]{1,0:T(8,128)(2,1)S(1)} %copy-done.5), channel_id=1, source_target_pairs={{1,2},{2,1},{5,6},{6,5},{9,10},{10,9},{13,14},{14,13},{17,18},{18,... | collective-permute-start | bytes 1769480 | tf_op jit(solution)/shard_map/ppermute | solution.py:426
  72.5 1.1 copy-start.11
  72.5 13.5 %collective-permute-start.12 = (bf16[2,96,1536]{2,1,0:T(8,128)(2,1)S(1)}, bf16[2,96,1536]{2,1,0:T(8,128)(2,1)S(1)}, u32[]{:S(2)}, u32[]{:S(2)}) collective-permute-start(bf16[2,96,1536]{2,1,0:T(8,128)(2,1)S(1)} %pad_maximum_fusion.3.refs_1_.refs_3_), channel_id=1, source_target_pairs={{0,1},{1,0},{2,3},{3,2},{4,5},{5,4},{6,7},{7,6},{8,9},{9,8},{10,11... | collective-permute-start | bytes 1769480 | tf_op jit(solution)/shard_map/ppermute | solution.py:336
  73.0 0.8 copy-start.12
  73.0 18.1 %collective-permute-start.13 = (bf16[2,96,1536]{2,1,0:T(8,128)(2,1)S(1)}, bf16[2,96,1536]{2,1,0:T(8,128)(2,1)S(1)}, u32[]{:S(2)}, u32[]{:S(2)}) collective-permute-start(bf16[2,96,1536]{2,1,0:T(8,128)(2,1)S(1)} %collective-permute-done.11.refs_3_.refs_5_), channel_id=1, source_target_pairs={{0,1},{1,0},{2,3},{3,2},{4,5},{5,4},{6,7},{7,6},{8,9},{9,8},{10,11... | collective-permute-start | bytes 1769480 | tf_op jit(solution)/shard_map/ppermute | solution.py:336
  73.1 0.9 copy-start.8
  73.1 32.2 %collective-permute-start.16 = (bf16[192,1536]{1,0:T(8,128)(2,1)}, bf16[192,1536]{1,0:T(8,128)(2,1)S(1)}, u32[]{:S(2)}, u32[]{:S(2)}) collective-permute-start(bf16[192,1536]{1,0:T(8,128)(2,1)} %get-tuple-element.36), channel_id=1, source_target_pairs={{0,8},{8,0},{1,9},{9,1},{2,10},{10,2},{3,11},{11,3},{4,12},{12,4},... | collective-permute-start | bytes 1769480 | tf_op jit(solution)/shard_map/ppermute | solution.py:353
  73.3 0.8 copy-start.9
  73.3 32.0 %collective-permute-start.17 = (bf16[192,1536]{1,0:T(8,128)(2,1)}, bf16[192,1536]{1,0:T(8,128)(2,1)}, u32[]{:S(2)}, u32[]{:S(2)}) collective-permute-start(bf16[192,1536]{1,0:T(8,128)(2,1)} %get-tuple-element.36), channel_id=1, source_target_pairs={{0,4},{4,0},{1,5},{5,1},{2,6},{6,2},{3,7},{7,3},{8,12},{12,8},{9,1... | collective-permute-start | bytes 1769480 | tf_op jit(solution)/shard_map/ppermute | solution.py:353
  74.1 0.8 copy-start.10
  75.0 16.1 %collective-permute-start.15 = (bf16[48,3072]{1,0:T(8,128)(2,1)}, bf16[48,3072]{1,0:T(8,128)(2,1)S(1)}, u32[]{:S(2)}, u32[]{:S(2)}) collective-permute-start(bf16[48,3072]{1,0:T(8,128)(2,1)} %get-tuple-element.34), channel_id=1, source_target_pairs={{0,3},{1,2},{2,1},{3,0},{4,7},{5,6},{6,5},{7,4},{8,11},{9,10},{10,... | collective-permute-start | bytes 884744 | tf_op jit(solution)/shard_map/ppermute | solution.py:336
  85.9 13.0 %copy-start.2 = (bf16[2,96,1536]{2,1,0:T(8,128)(2,1)}, bf16[2,96,1536]{2,1,0:T(8,128)(2,1)S(1)}, u32[]{:S(2)}) copy-start(bf16[2,96,1536]{2,1,0:T(8,128)(2,1)S(1)} %collective-permute-done.12.refs_2_.refs_4_) | copy-start | bytes 1769476
  91.1 7.9 %copy-start.14 = (bf16[48,3072]{1,0:T(8,128)(2,1)}, bf16[48,3072]{1,0:T(8,128)(2,1)S(1)}, u32[]{:S(2)}) copy-start(bf16[48,3072]{1,0:T(8,128)(2,1)S(1)} %collective-permute-done.15.refs_8_) | copy-start | bytes 884740
  91.1 7.9 %copy-start.3 = (bf16[2,96,1536]{2,1,0:T(8,128)(2,1)}, bf16[2,96,1536]{2,1,0:T(8,128)(2,1)S(1)}, u32[]{:S(2)}) copy-start(bf16[2,96,1536]{2,1,0:T(8,128)(2,1)S(1)} %collective-permute-done.13.refs_4_.refs_6_) | copy-start | bytes 1769476
  105.2 0.8 copy-start.7
Sparse Core Ops, SparseCore 0:
  43.5 55.3 all-gather.2

commit v11 on v9

--- a/solution.py
+++ b/solution.py
@@ -46,7 +46,7 @@
 
 
 def fold(state, active, q, k, v):
-    @pl.when(active == 1)
+    @pl.when(active)
     def _():
         for h in range(q.shape[1] // HEAD_DIM):
             at = columns_of(h)
@@ -69,7 +69,8 @@
         return copy
 
 
-def attend_kernel(slots, active, q, *refs):
+def attend_kernel(which, pattern, q, *refs):
+    slots, active = len(which), in_window(pattern, which)
     kv, (part, stats), scratch = refs[: 2 * slots + 2], refs[2 * slots + 2 : 2 * slots + 4], refs[2 * slots + 4 :]
     q_v, kv_v, (part_v, total_v, peak_v, stats_v, sems) = scratch[0], scratch[1 : 2 * slots + 3], scratch[2 * slots + 3 :]
     fetch = Fetch(sems)
@@ -97,11 +98,11 @@
         copy.wait()
 
 
-def attend(active, q, kv):
+def attend(which, pattern, q, kv):
     rows, columns = q.shape
     slots = len(kv) // 2 - 1
     return pl.pallas_call(
-        functools.partial(attend_kernel, slots),
+        functools.partial(attend_kernel, which),
         out_shape=[
             jax.ShapeDtypeStruct((rows, columns), jnp.float32),
             jax.ShapeDtypeStruct((rows, HEAD_DIM), jnp.float32),
@@ -118,7 +119,7 @@
             transcendentals=0,
         ),
         name="attend",
-    )(active, q, *kv)
+    )(pattern, q, *kv)
 
 
 def close_open(fetch, first, q, part, stats, near, q_v, near_v, state, stats_v):
@@ -154,7 +155,8 @@
     )
 
 
-def close_kernel(first, slots, active, q, part, stats, *refs):
+def close_kernel(first, which, pattern, q, part, stats, *refs):
+    slots, active = len(which), in_window(pattern, which)
     near, out = refs[:slots], refs[slots]
     q_v, near_v, (*state, stats_v, sems, out_v) = refs[slots + 1], refs[slots + 2 : 2 * slots + 2], refs[2 * slots + 2 :]
     fetch = Fetch(sems)
@@ -163,10 +165,10 @@
     fetch(out_v, out).wait()
 
 
-def close(active, q, state, near, first):
+def close(which, pattern, q, state, near, first):
     rows, columns = q.shape[0], near[0].shape[1] // 2
     return pl.pallas_call(
-        functools.partial(close_kernel, first, len(near)),
+        functools.partial(close_kernel, first, which),
         out_shape=jax.ShapeDtypeStruct((rows, columns), jnp.bfloat16),
         in_specs=[SMEM] + [ANY] * (3 + len(near)),
         out_specs=ANY,
@@ -178,7 +180,7 @@
             transcendentals=0,
         ),
         name="close",
-    )(active, q, *state, *near)
+    )(pattern, q, *state, *near)
 
 
 def fetch_weight(fetch, moves, place, weight, held, low, high):
@@ -222,14 +224,15 @@
             out(at, add(at) + projected)
 
 
-def begin_kernel(counts, moves, control_rows, place, hidden, ready, *refs):
+def begin_kernel(counts, moves, control_rows, hidden, ready, *refs):
+    place = device_place()
     weight, control = refs[: counts[0]], refs[counts[0] : sum(counts)]
     out, attention, held, hidden_v, control_v, out_v, sems = refs[sum(counts) :]
     fetch = Fetch(sems)
     residual = [fetch(ready, attention), fetch(hidden, hidden_v)]
     copies = fetch_weight(fetch, moves, place, weight, held, 0, ready.shape[1])
     for d, block in enumerate(control):
-        start = pl.multiple_of((place[4] ^ d) * control_rows, control_rows) if len(control) > 1 else 0
+        start = pl.multiple_of((device_column(place) ^ d) * control_rows, control_rows) if len(control) > 1 else 0
         residual.append(fetch(block, control_v.at[pl.ds(start, control_rows), :]))
     for copy in residual:
         copy.wait()
@@ -251,7 +254,8 @@
         copy.wait()
 
 
-def finish_kernel(slots, pieces, moves, first, place, active, q, part, stats, so_far, *refs):
+def finish_kernel(which, pieces, moves, first, pattern, q, part, stats, so_far, *refs):
+    slots, active = len(which), in_window(pattern, which)
     near, weight, out, refs = refs[:slots], refs[slots : slots + pieces], refs[slots + pieces], refs[slots + pieces + 1 :]
     q_v, near_v, (*state, stats_v, sems, attention, held, sum_v, out_v, late_sems) = (
         refs[0],
@@ -261,7 +265,7 @@
     fetch, late_fetch = Fetch(sems), Fetch(late_sems)
     low = first * HEAD_DIM
     opened = close_open(fetch, first, q, part, stats, near, q_v, near_v, state, stats_v)
-    copies = fetch_weight(late_fetch, moves, place, weight, held, low, low + q_v.shape[1])
+    copies = fetch_weight(late_fetch, moves, device_place(), weight, held, low, low + q_v.shape[1])
     so_far_copy = late_fetch(so_far, sum_v)
     close_heads(opened, first, active, q_v, near_v, state, stats_v, attention)
     so_far_copy.wait()
@@ -287,7 +291,7 @@
     ]
 
 
-def begin(place, ready, weight, control, hidden, moves, inner):
+def begin(ready, weight, control, hidden, moves, inner):
     rows, width = hidden.shape
     columns = ready.shape[1]
     before, behind = project_scratch(
@@ -296,7 +300,7 @@
     return pl.pallas_call(
         functools.partial(begin_kernel, (len(weight), len(control)), moves, control[0].shape[0]),
         out_shape=jax.ShapeDtypeStruct((rows, width), jnp.float32),
-        in_specs=[SMEM] + [ANY] * (2 + len(weight) + len(control)),
+        in_specs=[ANY] * (2 + len(weight) + len(control)),
         out_specs=ANY,
         scratch_shapes=before + [pltpu.VMEM((rows, width), jnp.bfloat16)] * 2 + behind,
         compiler_params=pltpu.CompilerParams(vmem_limit_bytes=VMEM_LIMIT),
@@ -304,10 +308,10 @@
             flops=2 * rows * columns * width, bytes_accessed=2 * columns * width + 8 * rows * width, transcendentals=0
         ),
         name="begin",
-    )(place, hidden, ready, *weight, *control)
-
-
-def finish(place, active, q, state, near, first, so_far, weight, moves):
+    )(hidden, ready, *weight, *control)
+
+
+def finish(which, pattern, q, state, near, first, so_far, weight, moves):
     rows, inner = q.shape
     width = so_far.shape[1]
     columns = near[0].shape[1] // 2
@@ -315,9 +319,9 @@
         rows, columns, lax.axis_size("groups"), inner, width, jnp.bfloat16, 1 + len(moves)
     )
     return pl.pallas_call(
-        functools.partial(finish_kernel, len(near), len(weight), moves, first),
+        functools.partial(finish_kernel, which, len(weight), moves, first),
         out_shape=jax.ShapeDtypeStruct((rows, width), jnp.bfloat16),
-        in_specs=[SMEM] * 2 + [ANY] * (4 + len(near) + len(weight)),
+        in_specs=[SMEM] + [ANY] * (4 + len(near) + len(weight)),
         out_specs=ANY,
         scratch_shapes=close_scratch(rows, columns, len(near))
         + before
@@ -328,7 +332,7 @@
             flops=2 * rows * columns * width, bytes_accessed=2 * columns * width + 6 * rows * width, transcendentals=0
         ),
         name="finish",
-    )(place, active, q, *state, so_far, *near, *weight)
+    )(pattern, q, *state, so_far, *near, *weight)
 
 
 def flipped(block, axis, flip):
@@ -350,6 +354,35 @@
 
 def route_of(route):
     return lambda block: lax.ppermute(block, TILES, route)
+
+
+def grid_of(tile_count):
+    width = min(8, tile_count // 4)
+    height = min(4, tile_count // 8)
+    return (width * height, width, 1), (tile_count // (width * height), height, width)
+
+
+def device_place():
+    return [lax.axis_index(a) for a in ("groups",) + TILES]
+
+
+def device_column(place):
+    _, outer, pair, core = place
+    tile_count = math.prod(lax.axis_size(a) for a in TILES)
+    return lax.rem((outer * 2 + pair) * 2 + core, grid_of(tile_count)[1][2])
+
+
+def in_window(pattern, slots):
+    _, outer, pair, core = device_place()
+    strides, counts = grid_of(math.prod(lax.axis_size(a) for a in TILES))
+    position = (outer * 2 + pair) * 2 + core
+    active = []
+    for axis, odd in slots:
+        place = lax.rem(lax.div(position, strides[axis]), counts[axis])
+        down = (place >= 1) & (pattern[0, 2 * axis] == 1)
+        up = (place + 1 < counts[axis]) & (pattern[0, 2 * axis + 1] == 1)
+        active.append(jnp.where(lax.rem(place, 2) == odd, up.astype(jnp.int32), down.astype(jnp.int32)) == 1)
+    return active
 
 
 def neighbour_slots(tile_count, strides, counts):
@@ -370,29 +403,15 @@
     groups = lax.axis_size("groups")
     outer, pair, cores = (lax.axis_size(a) for a in TILES)
     tile_count = outer * pair * cores
-    grid_width = min(8, tile_count // 4)
-    grid_height = min(4, tile_count // 8)
-    layer = grid_width * grid_height
-    strides = (layer, grid_width, 1)
-    counts = (tile_count // layer, grid_height, grid_width)
-    position = lax.axis_index(TILES)
-    across = position % grid_width
+    strides, counts = grid_of(tile_count)
+    grid_width = counts[2]
+    across = device_column(device_place())
     rows = queries.shape[0]
     width = hidden.shape[1]
     slots = neighbour_slots(tile_count, strides, counts)
     early = [s for s in slots if s[0] == 2]
     late = [s for s in slots if s[0] != 2]
 
-    def flags(chosen):
-        active = []
-        for axis, odd, _ in chosen:
-            place = position // strides[axis] % counts[axis]
-            up = (place % 2 == odd).astype(jnp.int32)
-            valid = jnp.where(up == 1, place + 1 < counts[axis], place >= 1)
-            active.append((valid & (pattern[0, 2 * axis + up] == 1)).astype(jnp.int32))
-        return jnp.stack(active)
-
-    early_active, late_active = flags(early), flags(late)
     far_lane, near_lane = Lane(), Lane()
 
     shard, share = out_weight.shape[0], width // groups
@@ -426,11 +445,15 @@
         control_parts[d] = swap(TILES, d)(after(control_sent[d], line if d < grid_width - 1 else beside))
     control_parts[1] = swap(TILES, 1)(control_sent[1])
     plane = jnp.concatenate([line, beside])
-    last = swap("outer", 1)(after(far, near, *control_parts[2:-1]))
+    last = swap("outer", 1)(after(far, near, *control_parts[2:-1], *chunks))
+    early_near = [[None, None] for _ in early]
+    for i, x in enumerate((keys, values)):
+        early_near[0][i] = lax.ppermute(x, TILES, early[0][2])
+        for slot in range(1, len(early)):
+            early_near[slot][i] = lax.ppermute(after(x, early_near[0][i]), TILES, early[slot][2])
     held = [plane, swap("groups", 1)(plane)]
     crossed = [swap("core", 1)(x) for x in held]
-    early_near = [[lax.ppermute(x, TILES, route) for x in (keys, values)] for _, _, route in early]
-    state = attend(early_active, queries, [keys, values] + [x for kv in early_near for x in kv])
+    state = attend(tuple(s[:2] for s in early), pattern, queries, [keys, values] + [x for kv in early_near for x in kv])
 
     steps = after(jnp.concatenate([far, near, last]), *control_parts[2:], held[1])
     weight = [lax.all_gather(steps, ("groups", "pair", "core"))]
@@ -456,7 +479,8 @@
     for chunk in chunks:
         lanes = (far_lane, near_lane)
         late_near.append([lanes[i % 2](route_of(route), chunk) for i, (_, _, route) in enumerate(late)])
-    ready = [close(late_active, queries, state, late_near[i], firsts[i]) for i in range(len(CHUNKS) - 1)]
+    which = tuple(s[:2] for s in late)
+    ready = [close(which, pattern, queries, state, late_near[i], firsts[i]) for i in range(len(CHUNKS) - 1)]
     ready = ready[0] if len(ready) == 1 else jnp.concatenate(ready, axis=1)
     if block % 16:
         control_parts = [
@@ -464,12 +488,11 @@
                 jnp.stack(control_parts), jnp.arange(grid_width, dtype=jnp.int32) ^ across, axis=0
             ).reshape(rows, width)
         ]
-    place = jnp.stack([lax.axis_index(a) for a in ("groups",) + TILES] + [across]).astype(jnp.int32)
     if shard % 16:
-        weight, moves = [in_order(weight, moves, place, (groups, outer, pair, cores))], [(0, None, None)]
+        weight, moves = [in_order(weight, moves, device_place(), (groups, outer, pair, cores))], [(0, None, None)]
     moves = tuple(moves)
-    so_far = begin(place, ready, weight, control_parts, hidden, moves, queries.shape[1])
-    return finish(place, late_active, queries, state, late_near[-1], firsts[-1], so_far, weight, moves)
+    so_far = begin(ready, weight, control_parts, hidden, moves, queries.shape[1])
+    return finish(which, pattern, queries, state, late_near[-1], firsts[-1], so_far, weight, moves)
 
 
 def in_order(weight, moves, place, sizes):

time: 114 us -> 112 us (0.982); the launches traced: 112 us -> 112 us
  between operations: 16.1 us -> 13.7 us
  starting transfers between devices: 24.1 us -> 25.4 us
    all_gather x1, waiting for transfers between devices: 1.14 us -> 7.69 us  [on_device(): weight = [lax.all_gather(steps, ('groups', 'pair', 'core'))]]
    ppermute x4, waiting for transfers between devices: 4.53 us -> 0.01 us  [the longest x2 0.01 us: on_device(): early_near[0][i] = lax.ppermute(x, TILES, early[0][2])]
    ppermute x10, waiting for transfers between devices: 12.5 us -> 9.5 us  [flipped(): lax.ppermute(block, axis, [(i, i ^ flip) for i in range(lax.axis_size(axi...]
    pallas_call x3, Pallas kernels: 18.4 us -> 20.2 us  [the longest x1 8 us: finish(): pl.pallas_call(functools.partial(finish_kernel, which, len(weight), moves...]
    another operation x2 -> x0, other arithmetic: 1.25 us -> none  [flags(): return jnp.stack(active)]
    unnamed x26 -> x32, local copies, waits for them, and re-layouts: 2 us -> 2.42 us
  transfers between devices with their start and end apart: 19 -> 19, of which waited for: 9 -> 5; matrix products, arithmetic and copies ran while one was open for 6% -> 5% of each run, Pallas kernels for 16% -> 16%
where the time goes in v11:
time: 112 us
  waiting for transfers between devices  37.5 us (33%)
  Pallas kernels  25.7 us (23%)
  starting transfers between devices  25.4 us (23%)
  between operations  13.7 us (12%)
  other arithmetic  4.98 us (4%)
  local copies, waits for them, and re-layouts  4.7 us (4%)
    ppermute x4, waiting for transfers between devices, route_of(): return lambda block: lax.ppermute(block, TILES, route)  20.2 us
    ppermute x10, starting transfers between devices, flipped(): lax.ppermute(block, axis, [(i, i ^ flip) for i in range(lax.axis_size(axi...  14.1 us
    ppermute x10, waiting for transfers between devices, flipped(): lax.ppermute(block, axis, [(i, i ^ flip) for i in range(lax.axis_size(axi...  9.5 us
    pallas_call x1, Pallas kernels, finish(): pl.pallas_call(functools.partial(finish_kernel, which, len(weight), moves...  8 us
    all_gather x1, waiting for transfers between devices, on_device(): weight = [lax.all_gather(steps, ('groups', 'pair', 'core'))]  7.69 us
    pallas_call x1, Pallas kernels, attend(): pl.pallas_call(functools.partial(attend_kernel, which), out_shape=[jax.Sh...  7.24 us
    ppermute x2, starting transfers between devices, on_device(): lax.ppermute(after(x, early_near[0][i]), TILES, early[slot][2])  5.56 us
    pallas_call x1, Pallas kernels, begin(): pl.pallas_call(functools.partial(begin_kernel, (len(weight), len(control)...  5.52 us
  transfers between devices with their start and end apart: 19, of which 5 were waited for; matrix products, arithmetic and copies ran while one was open for 5% of the time, Pallas kernels for 16%

profile of v11, /device:TPU:1, one launch (start us, length us, event | category | flops | bytes accessed | tf_op | source)
XLA Modules:
  0.0 111.9 jit_solution(4426404210534481447)
XLA Ops:
  6.5 1.8 %slice_select_fusion = bf16[96,1536]{1,0:T(8,128)(2,1)} fusion(bf16[96,3072]{1,0:T(8,128)(2,1)} %param.12, pred[]{:T(512)S(6)} %eq.3), kind=kLoop, calls=%fused_computation.8 | loop fusion | flops 147456 | bytes 884737 | tf_op jit(solution)/shard_map/jit(_where)/select_n | solution.py:420
  8.3 2.0 %collective-permute-start.10 = (bf16[1,96,1536]{2,1,0:T(8,128)(2,1)}, bf16[1,96,1536]{2,1,0:T(8,128)(2,1)S(1)}, u32[]{:S(2)}, u32[]{:S(2)}) collective-permute-start(bf16[1,96,1536]{2,1,0:T(8,128)(2,1)} %bitcast), channel_id=1, source_target_pairs={{0,2},{2,0},{1,3},{3,1},{4,6},{6,4},{5,7},{7,5},{8,10},{10,8},{9,1... | collective-permute-start | bytes 884744 | tf_op jit(solution)/shard_map/ppermute | solution.py:339
  10.4 1.3 %collective-permute-start.6 = (bf16[1,96,1536]{2,1,0:T(8,128)(2,1)}, bf16[1,96,1536]{2,1,0:T(8,128)(2,1)S(1)}, u32[]{:S(2)}, u32[]{:S(2)}) collective-permute-start(bf16[1,96,1536]{2,1,0:T(8,128)(2,1)} %bitcast), channel_id=1, source_target_pairs={{0,4},{4,0},{8,12},{12,8},{1,5},{5,1},{9,13},{13,9},{2,6},{6,2},{1... | collective-permute-start | bytes 884744 | tf_op jit(solution)/shard_map/ppermute | solution.py:339
  11.7 2.3 %collective-permute-start.4 = (bf16[1,96,1536]{2,1,0:T(8,128)(2,1)}, bf16[1,96,1536]{2,1,0:T(8,128)(2,1)S(1)}, u32[]{:S(2)}, u32[]{:S(2)}) collective-permute-start(bf16[1,96,1536]{2,1,0:T(8,128)(2,1)} %bitcast), channel_id=1, source_target_pairs={{0,8},{4,12},{8,0},{12,4},{1,9},{5,13},{9,1},{13,5},{2,10},{6,14},... | collective-permute-start | bytes 884744 | tf_op jit(solution)/shard_map/ppermute | solution.py:339
  14.0 2.2 %dynamic-slice_bitcast_fusion = (bf16[48,3072]{1,0:T(8,128)(2,1)}, bf16[48,3072]{1,0:T(8,128)(2,1)}, bf16[48,3072]{1,0:T(8,128)(2,1)S(1)}, bf16[48,3072]{1,0:T(8,128)(2,1)S(1)}) fusion(bf16[6,4,8,3072]{3,2,1,0:T(8,128)(2,1)} %bitcast.21, s32[]{:T(128)S(6)} %select_n.26, s32[]{:T(128)S(6)} %select_n.25, s32[]{:T(128)S(6)} %select_n.24, s32[]{:T(128)S(6)} %select_n.23), kind=kLoop, calls=%fused_computation.4 | loop fusion | bytes 2359312 | tf_op jit(solution)/shard_map/reshape | solution.py:440
  16.2 0.3 collective-permute-start.8
  16.5 0.8 copy-done.5
  17.3 0.0 collective-permute-done.10
  17.3 1.0 pad_maximum_fusion.3.refs_1_.refs_3_
  18.3 1.3 %collective-permute-start.12 = (bf16[2,96,1536]{2,1,0:T(8,128)(2,1)S(1)}, bf16[2,96,1536]{2,1,0:T(8,128)(2,1)S(1)}, u32[]{:S(2)}, u32[]{:S(2)}) collective-permute-start(bf16[2,96,1536]{2,1,0:T(8,128)(2,1)S(1)} %pad_maximum_fusion.3.refs_1_.refs_3_), channel_id=1, source_target_pairs={{0,16},{16,0},{1,17},{17,1},{2,18},{18,2},{3,19},{19,3},{4,20},{20... | collective-permute-start | bytes 1769480 | tf_op jit(solution)/shard_map/ppermute | solution.py:339
  19.7 1.2 %pad_maximum_fusion.1 = (bf16[192,1536]{1,0:T(8,128)(2,1)}, bf16[192,1536]{1,0:T(8,128)(2,1)}) fusion(bf16[192,768]{1,0:T(8,128)(2,1)S(1)} %get-tuple-element.42, bf16[192,768]{1,0:T(8,128)(2,1)S(1)} %get-tuple-element.40, bf16[192,768]{1,0:T(8,128)(2,1)S(1)} %get-tuple-element.41, bf16[192,768]{1,0:T(8,128)(2,1)S(1)} %get-tuple-element.39), kind=kLoop, calls=%fused_computation.1 | loop fusion | flops 2359296 | bytes 2359296 | tf_op jit(solution)/shard_map/concatenate | solution.py:433
  20.8 3.5 %collective-permute-done.6 = bf16[1,96,1536]{2,1,0:T(8,128)(2,1)S(1)} collective-permute-done((bf16[1,96,1536]{2,1,0:T(8,128)(2,1)}, bf16[1,96,1536]{2,1,0:T(8,128)(2,1)S(1)}, u32[]{:S(2)}, u32[]{:S(2)}) %collective-permute-start.6) | collective-permute-done | bytes 294944 | tf_op jit(solution)/shard_map/ppermute | solution.py:339
  24.3 0.0 collective-permute-done.4
  24.3 0.0 collective-permute-done.8.refs_7_
  24.3 2.5 %collective-permute-start.9 = (bf16[1,96,1536]{2,1,0:T(8,128)(2,1)S(1)}, bf16[1,96,1536]{2,1,0:T(8,128)(2,1)S(1)}, u32[]{:S(2)}, u32[]{:S(2)}) collective-permute-start(bf16[1,96,1536]{2,1,0:T(8,128)(2,1)S(1)} %collective-permute-done.4), channel_id=1, source_target_pairs={{0,4},{4,0},{8,12},{12,8},{1,5},{5,1},{9,13},{13,9},{2,6},{6,2},{1... | collective-permute-start | bytes 884744 | tf_op jit(solution)/shard_map/ppermute | solution.py:339
  26.8 2.3 %collective-permute-start.11 = (bf16[48,3072]{1,0:T(8,128)(2,1)S(1)}, bf16[48,3072]{1,0:T(8,128)(2,1)S(1)}, u32[]{:S(2)}, u32[]{:S(2)}) collective-permute-start(bf16[48,3072]{1,0:T(8,128)(2,1)S(1)} %get-tuple-element.31), channel_id=1, source_target_pairs={{0,3},{1,2},{2,1},{3,0},{4,7},{5,6},{6,5},{7,4},{8,11},{9,10},{10,... | collective-permute-start | bytes 884744 | tf_op jit(solution)/shard_map/ppermute | solution.py:339
  29.2 2.2 %collective-permute-done.9 = bf16[1,96,1536]{2,1,0:T(8,128)(2,1)S(1)} collective-permute-done((bf16[1,96,1536]{2,1,0:T(8,128)(2,1)S(1)}, bf16[1,96,1536]{2,1,0:T(8,128)(2,1)S(1)}, u32[]{:S(2)}, u32[]{:S(2)}) %collective-permute-start.9) | collective-permute-done | bytes 294944 | tf_op jit(solution)/shard_map/ppermute | solution.py:339
  31.4 1.0 pad_maximum_fusion
  32.4 3.8 %collective-permute-done.11.refs_8_ = bf16[48,3072]{1,0:T(8,128)(2,1)S(1)} collective-permute-done((bf16[48,3072]{1,0:T(8,128)(2,1)S(1)}, bf16[48,3072]{1,0:T(8,128)(2,1)S(1)}, u32[]{:S(2)}, u32[]{:S(2)}) %collective-permute-start.11) | collective-permute-done | bytes 294944 | tf_op jit(solution)/shard_map/ppermute | solution.py:339
  36.1 0.0 collective-permute-done.12.refs_3_.refs_5_
  36.1 0.0 all-gather.3.cloned.1.call-update
  36.2 1.4 %collective-permute-start = (bf16[192,1536]{1,0:T(8,128)(2,1)S(1)}, bf16[192,1536]{1,0:T(8,128)(2,1)S(1)}, u32[]{:S(2)}, u32[]{:S(2)}) collective-permute-start(bf16[192,1536]{1,0:T(8,128)(2,1)S(1)} %copy-done.4), channel_id=1, source_target_pairs={{0,1},{1,0},{2,3},{3,2},{4,5},{5,4},{6,7},{7,6},{8,9},{9,8},{10,11... | collective-permute-start | bytes 1769480 | tf_op jit(solution)/shard_map/ppermute | solution.py:451
  37.5 0.1 collective-permute-start.1
  37.6 2.3 %collective-permute-start.5 = (bf16[192,1536]{1,0:T(8,128)(2,1)}, bf16[192,1536]{1,0:T(8,128)(2,1)S(1)}, u32[]{:S(2)}, u32[]{:S(2)}) collective-permute-start(bf16[192,1536]{1,0:T(8,128)(2,1)} %get-tuple-element.26), channel_id=1, source_target_pairs={{0,8},{8,0},{1,9},{9,1},{2,10},{10,2},{3,11},{11,3},{4,12},{12,4},... | collective-permute-start | bytes 1769480 | tf_op jit(solution)/shard_map/ppermute | solution.py:356
  39.9 0.0 collective-permute-start.7
  39.9 0.0 collective-permute-done.refs_2_
  39.9 3.6 %collective-permute-start.2 = (bf16[192,1536]{1,0:T(8,128)(2,1)S(1)}, bf16[192,1536]{1,0:T(8,128)(2,1)S(1)}, u32[]{:S(2)}, u32[]{:S(2)}) collective-permute-start(bf16[192,1536]{1,0:T(8,128)(2,1)S(1)} %copy-done.4), channel_id=1, source_target_pairs={{1,2},{2,1},{5,6},{6,5},{9,10},{10,9},{13,14},{14,13},{17,18},{18,... | collective-permute-start | bytes 1769480 | tf_op jit(solution)/shard_map/ppermute | solution.py:453
  43.5 0.0 collective-permute-done.1.refs_3_
  43.6 2.0 %collective-permute-start.3 = (bf16[192,1536]{1,0:T(8,128)(2,1)S(1)}, bf16[192,1536]{1,0:T(8,128)(2,1)S(1)}, u32[]{:S(2)}, u32[]{:S(2)}) collective-permute-start(bf16[192,1536]{1,0:T(8,128)(2,1)S(1)} %copy-done.5), channel_id=1, source_target_pairs={{1,2},{2,1},{5,6},{6,5},{9,10},{10,9},{13,14},{14,13},{17,18},{18,... | collective-permute-start | bytes 1769480 | tf_op jit(solution)/shard_map/ppermute | solution.py:453
  45.5 0.1 collective-permute-start.13
  45.6 20.2 %collective-permute-done.5.refs_0_ = bf16[192,1536]{1,0:T(8,128)(2,1)S(1)} collective-permute-done((bf16[192,1536]{1,0:T(8,128)(2,1)}, bf16[192,1536]{1,0:T(8,128)(2,1)S(1)}, u32[]{:S(2)}, u32[]{:S(2)}) %collective-permute-start.5) | collective-permute-done | bytes 589856 | tf_op jit(solution)/shard_map/ppermute | solution.py:356
  65.9 1.3 %collective-permute-start.14 = (bf16[2,96,1536]{2,1,0:T(8,128)(2,1)S(1)}, bf16[2,96,1536]{2,1,0:T(8,128)(2,1)S(1)}, u32[]{:S(2)}, u32[]{:S(2)}) collective-permute-start(bf16[2,96,1536]{2,1,0:T(8,128)(2,1)S(1)} %collective-permute-done.12.refs_3_.refs_5_), channel_id=1, source_target_pairs={{0,1},{1,0},{2,3},{3,2},{4,5},{5,4},{6,7},{7,6},{8,9},{9,8},{10,11... | collective-permute-start | bytes 1769480 | tf_op jit(solution)/shard_map/ppermute | solution.py:339
  67.2 0.0 collective-permute-done.7.refs_1_
  67.2 0.0 collective-permute-start.16
  67.2 0.0 collective-permute-done.2.refs_4_
  67.2 2.0 %collective-permute-start.17 = (bf16[192,1536]{1,0:T(8,128)(2,1)}, bf16[192,1536]{1,0:T(8,128)(2,1)S(1)}, u32[]{:S(2)}, u32[]{:S(2)}) collective-permute-start(bf16[192,1536]{1,0:T(8,128)(2,1)} %get-tuple-element.34), channel_id=1, source_target_pairs={{0,4},{4,0},{1,5},{5,1},{2,6},{6,2},{3,7},{7,3},{8,12},{12,8},{9,1... | collective-permute-start | bytes 1769480 | tf_op jit(solution)/shard_map/ppermute | solution.py:356
  69.2 0.0 collective-permute-done.3.refs_5_
  69.2 0.8 copy-done.10
  70.0 0.6 collective-permute-start.15
  70.7 7.2 %attend.1 = (f32[192,1536]{1,0:T(8,128)}, f32[192,128]{1,0:T(8,128)}) custom-call(s32[1,6]{1,0:T(1,128)} %pattern.5, bf16[192,1536]{1,0:T(8,128)(2,1)} %q.5, bf16[192,1536]{1,0:T(8,128)(2,1)} %refs_0_.1, bf16[192,1536]{1,0:T(8,128)(2,1)} %refs_1_.1, bf16[192,1536]{1,0:T(8,128)(2,1)} %copy-done.6, bf16[192,1536]{1,0:T(8,128)(2,1)} %copy-done.7, ...), custom_call_target="tpu_custom_call" | custom-call | flops 1019215872 | bytes 5308416 | tf_op jit(solution)/shard_map/attend/pallas_call | solution.py:104
  77.9 4.9 %close.1.ready = bf16[192,768]{1,0:T(8,128)(2,1)} custom-call(s32[1,6]{1,0:T(1,128)} %pattern.5, bf16[192,1536]{1,0:T(8,128)(2,1)} %q.5, f32[192,1536]{1,0:T(8,128)} %get-tuple-element.22.part, f32[192,128]{1,0:T(8,128)} %get-tuple-element.23.stats, bf16[192,1536]{1,0:T(8,128)(2,1)} %copy-done.11, bf16[192,1536]{1,0:T(8,128)(2,1)} %copy-done.12), custom_call_target="tpu_custom_call" | custom-call | flops 339738624 | bytes 2359296 | tf_op jit(solution)/shard_map/close/pallas_call | solution.py:170
  82.9 0.0 collective-permute-done.15.refs_6_
  82.9 0.0 collective-permute-done.13.refs_2_.refs_4_
  82.9 7.7 %all-gather.3.cloned.1.call-done = bf16[24,96,1536]{2,1,0:T(8,128)(2,1)} async-done(((bf16[3,96,1536]{2,1,0:T(8,128)(2,1)}), bf16[24,96,1536]{2,1,0:T(8,128)(2,1)}) %all-gather.3.cloned.1.call-update) | async-done | bytes 7077904 | tf_op jit(solution)/shard_map/all_gather | solution.py:459
  90.6 5.5 %begin.1.so_far = f32[192,3072]{1,0:T(8,128)} custom-call(bf16[192,3072]{1,0:T(8,128)(2,1)} %hidden.1, bf16[192,768]{1,0:T(8,128)(2,1)} %close.1.ready, bf16[8,3,96,1536]{3,2,1,0:T(8,128)(2,1)} %bitcast.19, bf16[2,96,1536]{2,1,0:T(8,128)(2,1)} %copy-done, bf16[2,96,1536]{2,1,0:T(8,128)(2,1)} %copy-done.2, bf16[2,96,1536]{2,1,0:T(8,128)(2,1)} %copy-done.1, ...), custom_call_target="tpu_custom_call" | custom-call | flops 905969664 | bytes 9437184 | tf_op jit(solution)/shard_map/begin/pallas_call | solution.py:300
  96.2 0.0 collective-permute-done.17.refs_1_
  96.2 0.8 copy-done.8
  97.0 8.0 %finish.1 = bf16[192,3072]{1,0:T(8,128)(2,1)} custom-call(s32[1,6]{1,0:T(1,128)} %pattern.5, bf16[192,1536]{1,0:T(8,128)(2,1)} %q.5, f32[192,1536]{1,0:T(8,128)} %get-tuple-element.22.part, f32[192,128]{1,0:T(8,128)} %get-tuple-element.23.stats, f32[192,3072]{1,0:T(8,128)} %begin.1.so_far, bf16[192,1536]{1,0:T(8,128)(2,1)} %collective-permute-done.16.refs_0_, ...), custom_call_target="tpu_custom_call" | custom-call | flops 905969664 | bytes 8257536 | tf_op jit(solution)/shard_map/finish/pallas_call | solution.py:321
  (34 shorter events, 0.1 us)
Async XLA Ops:
  6.5 84.1 %all-gather.3.cloned.1.call-start = ((), (), s32[]{:S(2)}) async-start(), calls=%async_computation | async-start | bytes 7962624 | tf_op jit(solution)/shard_map/all_gather | solution.py:459
  8.3 9.0 %collective-permute-start.10 = (bf16[1,96,1536]{2,1,0:T(8,128)(2,1)}, bf16[1,96,1536]{2,1,0:T(8,128)(2,1)S(1)}, u32[]{:S(2)}, u32[]{:S(2)}) collective-permute-start(bf16[1,96,1536]{2,1,0:T(8,128)(2,1)} %bitcast), channel_id=1, source_target_pairs={{0,2},{2,0},{1,3},{3,1},{4,6},{6,4},{5,7},{7,5},{8,10},{10,8},{9,1... | collective-permute-start | bytes 884744 | tf_op jit(solution)/shard_map/ppermute | solution.py:339
  10.4 14.0 %collective-permute-start.6 = (bf16[1,96,1536]{2,1,0:T(8,128)(2,1)}, bf16[1,96,1536]{2,1,0:T(8,128)(2,1)S(1)}, u32[]{:S(2)}, u32[]{:S(2)}) collective-permute-start(bf16[1,96,1536]{2,1,0:T(8,128)(2,1)} %bitcast), channel_id=1, source_target_pairs={{0,4},{4,0},{8,12},{12,8},{1,5},{5,1},{9,13},{13,9},{2,6},{6,2},{1... | collective-permute-start | bytes 884744 | tf_op jit(solution)/shard_map/ppermute | solution.py:339
  11.7 12.7 %collective-permute-start.4 = (bf16[1,96,1536]{2,1,0:T(8,128)(2,1)}, bf16[1,96,1536]{2,1,0:T(8,128)(2,1)S(1)}, u32[]{:S(2)}, u32[]{:S(2)}) collective-permute-start(bf16[1,96,1536]{2,1,0:T(8,128)(2,1)} %bitcast), channel_id=1, source_target_pairs={{0,8},{4,12},{8,0},{12,4},{1,9},{5,13},{9,1},{13,5},{2,10},{6,14},... | collective-permute-start | bytes 884744 | tf_op jit(solution)/shard_map/ppermute | solution.py:339
  14.0 2.5 %copy-start.4 = (bf16[192,1536]{1,0:T(8,128)(2,1)S(1)}, bf16[192,1536]{1,0:T(8,128)(2,1)}, u32[]{:S(2)}) copy-start(bf16[192,1536]{1,0:T(8,128)(2,1)} %refs_0_.1) | copy-start | bytes 1769476
  16.2 1.1 copy-start.5
  16.2 8.1 %collective-permute-start.8 = (bf16[48,3072]{1,0:T(8,128)(2,1)S(1)}, bf16[48,3072]{1,0:T(8,128)(2,1)S(1)}, u32[]{:S(2)}, u32[]{:S(2)}) collective-permute-start(bf16[48,3072]{1,0:T(8,128)(2,1)S(1)} %get-tuple-element.28), channel_id=1, source_target_pairs={{0,2},{1,3},{2,0},{3,1},{4,6},{5,7},{6,4},{7,5},{8,10},{9,11},{10,... | collective-permute-start | bytes 884744 | tf_op jit(solution)/shard_map/ppermute | solution.py:339
  18.3 27.2 %copy-start = (bf16[2,96,1536]{2,1,0:T(8,128)(2,1)}, bf16[2,96,1536]{2,1,0:T(8,128)(2,1)S(1)}, u32[]{:S(2)}) copy-start(bf16[2,96,1536]{2,1,0:T(8,128)(2,1)S(1)} %pad_maximum_fusion.3.refs_1_.refs_3_) | copy-start | bytes 1769476
  18.3 17.8 %collective-permute-start.12 = (bf16[2,96,1536]{2,1,0:T(8,128)(2,1)S(1)}, bf16[2,96,1536]{2,1,0:T(8,128)(2,1)S(1)}, u32[]{:S(2)}, u32[]{:S(2)}) collective-permute-start(bf16[2,96,1536]{2,1,0:T(8,128)(2,1)S(1)} %pad_maximum_fusion.3.refs_1_.refs_3_), channel_id=1, source_target_pairs={{0,16},{16,0},{1,17},{17,1},{2,18},{18,2},{3,19},{19,3},{4,20},{20... | collective-permute-start | bytes 1769480 | tf_op jit(solution)/shard_map/ppermute | solution.py:339
  24.3 7.0 %copy-start.13 = (bf16[48,3072]{1,0:T(8,128)(2,1)}, bf16[48,3072]{1,0:T(8,128)(2,1)S(1)}, u32[]{:S(2)}) copy-start(bf16[48,3072]{1,0:T(8,128)(2,1)S(1)} %collective-permute-done.8.refs_7_) | copy-start | bytes 884740
  24.3 7.0 %collective-permute-start.9 = (bf16[1,96,1536]{2,1,0:T(8,128)(2,1)S(1)}, bf16[1,96,1536]{2,1,0:T(8,128)(2,1)S(1)}, u32[]{:S(2)}, u32[]{:S(2)}) collective-permute-start(bf16[1,96,1536]{2,1,0:T(8,128)(2,1)S(1)} %collective-permute-done.4), channel_id=1, source_target_pairs={{0,4},{4,0},{8,12},{12,8},{1,5},{5,1},{9,13},{13,9},{2,6},{6,2},{1... | collective-permute-start | bytes 884744 | tf_op jit(solution)/shard_map/ppermute | solution.py:339
  26.8 9.3 %collective-permute-start.11 = (bf16[48,3072]{1,0:T(8,128)(2,1)S(1)}, bf16[48,3072]{1,0:T(8,128)(2,1)S(1)}, u32[]{:S(2)}, u32[]{:S(2)}) collective-permute-start(bf16[48,3072]{1,0:T(8,128)(2,1)S(1)} %get-tuple-element.31), channel_id=1, source_target_pairs={{0,3},{1,2},{2,1},{3,0},{4,7},{5,6},{6,5},{7,4},{8,11},{9,10},{10,... | collective-permute-start | bytes 884744 | tf_op jit(solution)/shard_map/ppermute | solution.py:339
  36.1 9.5 %copy-start.14 = (bf16[48,3072]{1,0:T(8,128)(2,1)}, bf16[48,3072]{1,0:T(8,128)(2,1)S(1)}, u32[]{:S(2)}) copy-start(bf16[48,3072]{1,0:T(8,128)(2,1)S(1)} %collective-permute-done.11.refs_8_) | copy-start | bytes 884740
  36.1 41.8 %copy-start.1 = (bf16[2,96,1536]{2,1,0:T(8,128)(2,1)}, bf16[2,96,1536]{2,1,0:T(8,128)(2,1)S(1)}, u32[]{:S(2)}) copy-start(bf16[2,96,1536]{2,1,0:T(8,128)(2,1)S(1)} %collective-permute-done.12.refs_3_.refs_5_) | copy-start | bytes 1769476
  36.2 3.8 %collective-permute-start = (bf16[192,1536]{1,0:T(8,128)(2,1)S(1)}, bf16[192,1536]{1,0:T(8,128)(2,1)S(1)}, u32[]{:S(2)}, u32[]{:S(2)}) collective-permute-start(bf16[192,1536]{1,0:T(8,128)(2,1)S(1)} %copy-done.4), channel_id=1, source_target_pairs={{0,1},{1,0},{2,3},{3,2},{4,5},{5,4},{6,7},{7,6},{8,9},{9,8},{10,11... | collective-permute-start | bytes 1769480 | tf_op jit(solution)/shard_map/ppermute | solution.py:451
  37.5 6.0 %collective-permute-start.1 = (bf16[192,1536]{1,0:T(8,128)(2,1)S(1)}, bf16[192,1536]{1,0:T(8,128)(2,1)S(1)}, u32[]{:S(2)}, u32[]{:S(2)}) collective-permute-start(bf16[192,1536]{1,0:T(8,128)(2,1)S(1)} %copy-done.5), channel_id=1, source_target_pairs={{0,1},{1,0},{2,3},{3,2},{4,5},{5,4},{6,7},{7,6},{8,9},{9,8},{10,11... | collective-permute-start | bytes 1769480 | tf_op jit(solution)/shard_map/ppermute | solution.py:451
  37.6 28.3 %collective-permute-start.5 = (bf16[192,1536]{1,0:T(8,128)(2,1)}, bf16[192,1536]{1,0:T(8,128)(2,1)S(1)}, u32[]{:S(2)}, u32[]{:S(2)}) collective-permute-start(bf16[192,1536]{1,0:T(8,128)(2,1)} %get-tuple-element.26), channel_id=1, source_target_pairs={{0,8},{8,0},{1,9},{9,1},{2,10},{10,2},{3,11},{11,3},{4,12},{12,4},... | collective-permute-start | bytes 1769480 | tf_op jit(solution)/shard_map/ppermute | solution.py:356
  39.9 27.3 %collective-permute-start.7 = (bf16[192,1536]{1,0:T(8,128)(2,1)}, bf16[192,1536]{1,0:T(8,128)(2,1)S(1)}, u32[]{:S(2)}, u32[]{:S(2)}) collective-permute-start(bf16[192,1536]{1,0:T(8,128)(2,1)} %get-tuple-element.26), channel_id=1, source_target_pairs={{0,4},{4,0},{1,5},{5,1},{2,6},{6,2},{3,7},{7,3},{8,12},{12,8},{9,1... | collective-permute-start | bytes 1769480 | tf_op jit(solution)/shard_map/ppermute | solution.py:356
  39.9 3.6 %copy-start.6 = (bf16[192,1536]{1,0:T(8,128)(2,1)}, bf16[192,1536]{1,0:T(8,128)(2,1)S(1)}, u32[]{:S(2)}) copy-start(bf16[192,1536]{1,0:T(8,128)(2,1)S(1)} %collective-permute-done.refs_2_) | copy-start | bytes 1769476
  39.9 27.3 %collective-permute-start.2 = (bf16[192,1536]{1,0:T(8,128)(2,1)S(1)}, bf16[192,1536]{1,0:T(8,128)(2,1)S(1)}, u32[]{:S(2)}, u32[]{:S(2)}) collective-permute-start(bf16[192,1536]{1,0:T(8,128)(2,1)S(1)} %copy-done.4), channel_id=1, source_target_pairs={{1,2},{2,1},{5,6},{6,5},{9,10},{10,9},{13,14},{14,13},{17,18},{18,... | collective-permute-start | bytes 1769480 | tf_op jit(solution)/shard_map/ppermute | solution.py:453
  43.5 2.1 %copy-start.7 = (bf16[192,1536]{1,0:T(8,128)(2,1)}, bf16[192,1536]{1,0:T(8,128)(2,1)S(1)}, u32[]{:S(2)}) copy-start(bf16[192,1536]{1,0:T(8,128)(2,1)S(1)} %collective-permute-done.1.refs_3_) | copy-start | bytes 1769476
  43.6 25.7 %collective-permute-start.3 = (bf16[192,1536]{1,0:T(8,128)(2,1)S(1)}, bf16[192,1536]{1,0:T(8,128)(2,1)S(1)}, u32[]{:S(2)}, u32[]{:S(2)}) collective-permute-start(bf16[192,1536]{1,0:T(8,128)(2,1)S(1)} %copy-done.5), channel_id=1, source_target_pairs={{1,2},{2,1},{5,6},{6,5},{9,10},{10,9},{13,14},{14,13},{17,18},{18,... | collective-permute-start | bytes 1769480 | tf_op jit(solution)/shard_map/ppermute | solution.py:453
  45.5 37.4 %collective-permute-start.13 = (bf16[2,96,1536]{2,1,0:T(8,128)(2,1)S(1)}, bf16[2,96,1536]{2,1,0:T(8,128)(2,1)S(1)}, u32[]{:S(2)}, u32[]{:S(2)}) collective-permute-start(bf16[2,96,1536]{2,1,0:T(8,128)(2,1)S(1)} %pad_maximum_fusion.3.refs_1_.refs_3_), channel_id=1, source_target_pairs={{0,1},{1,0},{2,3},{3,2},{4,5},{5,4},{6,7},{7,6},{8,9},{9,8},{10,11... | collective-permute-start | bytes 1769480 | tf_op jit(solution)/shard_map/ppermute | solution.py:339
  65.9 3.4 %copy-start.11 = (bf16[192,1536]{1,0:T(8,128)(2,1)}, bf16[192,1536]{1,0:T(8,128)(2,1)S(1)}, u32[]{:S(2)}) copy-start(bf16[192,1536]{1,0:T(8,128)(2,1)S(1)} %collective-permute-done.5.refs_0_) | copy-start | bytes 1769476
  65.9 17.0 %collective-permute-start.14 = (bf16[2,96,1536]{2,1,0:T(8,128)(2,1)S(1)}, bf16[2,96,1536]{2,1,0:T(8,128)(2,1)S(1)}, u32[]{:S(2)}, u32[]{:S(2)}) collective-permute-start(bf16[2,96,1536]{2,1,0:T(8,128)(2,1)S(1)} %collective-permute-done.12.refs_3_.refs_5_), channel_id=1, source_target_pairs={{0,1},{1,0},{2,3},{3,2},{4,5},{5,4},{6,7},{7,6},{8,9},{9,8},{10,11... | collective-permute-start | bytes 1769480 | tf_op jit(solution)/shard_map/ppermute | solution.py:339
  67.2 2.0 %copy-start.12 = (bf16[192,1536]{1,0:T(8,128)(2,1)}, bf16[192,1536]{1,0:T(8,128)(2,1)S(1)}, u32[]{:S(2)}) copy-start(bf16[192,1536]{1,0:T(8,128)(2,1)S(1)} %collective-permute-done.7.refs_1_) | copy-start | bytes 1769476
  67.2 29.0 %collective-permute-start.16 = (bf16[192,1536]{1,0:T(8,128)(2,1)}, bf16[192,1536]{1,0:T(8,128)(2,1)}, u32[]{:S(2)}, u32[]{:S(2)}) collective-permute-start(bf16[192,1536]{1,0:T(8,128)(2,1)} %get-tuple-element.34), channel_id=1, source_target_pairs={{0,8},{8,0},{1,9},{9,1},{2,10},{10,2},{3,11},{11,3},{4,12},{12,4},... | collective-permute-start | bytes 1769480 | tf_op jit(solution)/shard_map/ppermute | solution.py:356
  67.2 2.0 %copy-start.9 = (bf16[192,1536]{1,0:T(8,128)(2,1)}, bf16[192,1536]{1,0:T(8,128)(2,1)S(1)}, u32[]{:S(2)}) copy-start(bf16[192,1536]{1,0:T(8,128)(2,1)S(1)} %collective-permute-done.2.refs_4_) | copy-start | bytes 1769476
  67.2 28.9 %collective-permute-start.17 = (bf16[192,1536]{1,0:T(8,128)(2,1)}, bf16[192,1536]{1,0:T(8,128)(2,1)S(1)}, u32[]{:S(2)}, u32[]{:S(2)}) collective-permute-start(bf16[192,1536]{1,0:T(8,128)(2,1)} %get-tuple-element.34), channel_id=1, source_target_pairs={{0,4},{4,0},{1,5},{5,1},{2,6},{6,2},{3,7},{7,3},{8,12},{12,8},{9,1... | collective-permute-start | bytes 1769480 | tf_op jit(solution)/shard_map/ppermute | solution.py:356
  69.2 0.8 copy-start.10
  70.0 12.8 %collective-permute-start.15 = (bf16[48,3072]{1,0:T(8,128)(2,1)}, bf16[48,3072]{1,0:T(8,128)(2,1)S(1)}, u32[]{:S(2)}, u32[]{:S(2)}) collective-permute-start(bf16[48,3072]{1,0:T(8,128)(2,1)} %get-tuple-element.35), channel_id=1, source_target_pairs={{0,1},{1,0},{2,3},{3,2},{4,5},{5,4},{6,7},{7,6},{8,9},{9,8},{10,11... | collective-permute-start | bytes 884744 | tf_op jit(solution)/shard_map/ppermute | solution.py:339
  82.9 7.7 %copy-start.15 = (bf16[48,3072]{1,0:T(8,128)(2,1)}, bf16[48,3072]{1,0:T(8,128)(2,1)S(1)}, u32[]{:S(2)}) copy-start(bf16[48,3072]{1,0:T(8,128)(2,1)S(1)} %collective-permute-done.15.refs_6_) | copy-start | bytes 884740
  82.9 7.7 %copy-start.2 = (bf16[2,96,1536]{2,1,0:T(8,128)(2,1)}, bf16[2,96,1536]{2,1,0:T(8,128)(2,1)S(1)}, u32[]{:S(2)}) copy-start(bf16[2,96,1536]{2,1,0:T(8,128)(2,1)S(1)} %collective-permute-done.13.refs_2_.refs_4_) | copy-start | bytes 1769476
  82.9 7.7 %copy-start.3 = (bf16[2,96,1536]{2,1,0:T(8,128)(2,1)}, bf16[2,96,1536]{2,1,0:T(8,128)(2,1)S(1)}, u32[]{:S(2)}) copy-start(bf16[2,96,1536]{2,1,0:T(8,128)(2,1)S(1)} %collective-permute-done.14.refs_4_.refs_6_) | copy-start | bytes 1769476
  96.2 0.8 copy-start.8
Sparse Core Ops, SparseCore 0:
  36.3 54.3 all-gather.2

commit v12 on v11

--- a/solution.py
+++ b/solution.py
@@ -11,7 +11,7 @@
 
 HEAD_DIM = 128
 TILE_W = 8
-CHUNKS = (6, 6)
+CHUNKS = (7, 5)
 SCALE = HEAD_DIM**-0.5 * math.log2(math.e)
 TILES = ("outer", "pair", "core")
 VMEM_LIMIT = 60 * 1024 * 1024
@@ -433,52 +433,57 @@
         jnp.concatenate([x[:, f * HEAD_DIM : (f + n) * HEAD_DIM] for x in (keys, values)], axis=1)
         for f, n in zip(firsts, CHUNKS)
     ]
-    chunks = lax.optimization_barrier(chunks)
     block = rows // grid_width
     lines = after(control, line).reshape(block // TILE_W, grid_width, TILE_W, width)
     control_sent = [
         lax.dynamic_index_in_dim(lines, across ^ d, 1, keepdims=False).reshape(block, width) for d in range(grid_width)
     ]
+    chunks, control_sent = lax.optimization_barrier((chunks, control_sent))
     control_parts = [control_sent[0]] + [None] * (grid_width - 1)
     beside = swap("pair", 1)(line)
+    plane = jnp.concatenate([line, beside])
+    early_near = [[None, None]] + [
+        [lax.ppermute(after(x, wait), TILES, route) for x, wait in ((keys, line), (values, plane))]
+        for _, _, route in early[1:]
+    ]
+    held = [plane, swap("groups", 1)(plane)]
+    last = swap("outer", 1)(after(far, near, *[kv[0] for kv in early_near[1:]], *chunks))
+    last_x = swap("pair", 1)(after(last, held[1]))
+    early_near[0][0] = lax.ppermute(keys, TILES, early[0][2])
+    early_near[0][1] = lax.ppermute(after(values, early_near[0][0]), TILES, early[0][2])
+    crossed = [swap("core", 1)(x) for x in held]
+    plane = jnp.concatenate([last, last_x])
+    held += [plane, swap("groups", 1)(plane)]
+    crossed += [swap("core", 1)(x) for x in held[2:]]
     for d in range(2, grid_width):
-        control_parts[d] = swap(TILES, d)(after(control_sent[d], line if d < grid_width - 1 else beside))
-    control_parts[1] = swap(TILES, 1)(control_sent[1])
-    plane = jnp.concatenate([line, beside])
-    last = swap("outer", 1)(after(far, near, *control_parts[2:-1], *chunks))
-    early_near = [[None, None] for _ in early]
-    for i, x in enumerate((keys, values)):
-        early_near[0][i] = lax.ppermute(x, TILES, early[0][2])
-        for slot in range(1, len(early)):
-            early_near[slot][i] = lax.ppermute(after(x, early_near[0][i]), TILES, early[slot][2])
-    held = [plane, swap("groups", 1)(plane)]
-    crossed = [swap("core", 1)(x) for x in held]
+        control_parts[d] = swap(TILES, d)(after(control_sent[d], last_x))
     state = attend(tuple(s[:2] for s in early), pattern, queries, [keys, values] + [x for kv in early_near for x in kv])
 
-    steps = after(jnp.concatenate([far, near, last]), *control_parts[2:], held[1])
-    weight = [lax.all_gather(steps, ("groups", "pair", "core"))]
+    weight = [lax.all_gather(after(jnp.concatenate([far, near]), held[1], last, *[kv[1] for kv in early_near[1:]]), ("groups", "pair", "core"))]
     n = len(line_flips)
     moves = [
         (0, ((g * pair + p) * cores + c, i * n + j), (False, g, f ^ at, p, c))
         for g in range(groups)
         for p in range(pair)
         for c in range(cores)
-        for i, at in enumerate((2, 1, 3))
+        for i, at in enumerate((2, 1))
         for j, f in enumerate(line_flips)
     ]
-    for group_flip in range(2):
+    for number, (group_flip, at) in enumerate(((0, 0), (1, 0), (0, 3), (1, 3))):
         for core_flip, pieces in enumerate((held, crossed)):
             moves += [
-                (len(weight), (p * n + j,), (True, group_flip, f, p, core_flip))
+                (len(weight), (p * n + j,), (True, group_flip, f ^ at, p, core_flip))
                 for p in range(pair)
                 for j, f in enumerate(line_flips)
             ]
-            weight.append(pieces[group_flip])
+            weight.append(pieces[number])
 
     late_near = []
     for chunk in chunks:
         lanes = (far_lane, near_lane)
-        late_near.append([lanes[i % 2](route_of(route), chunk) for i, (_, _, route) in enumerate(late)])
+        waits = [early_near[0][1], *crossed[:1]] if late_near else []
+        late_near.append([lanes[i % 2](route_of(route), chunk, *waits) for i, (_, _, route) in enumerate(late)])
+    control_parts[1] = swap(TILES, 1)(after(control_sent[1], *late_near[0]))
     which = tuple(s[:2] for s in late)
     ready = [close(which, pattern, queries, state, late_near[i], firsts[i]) for i in range(len(CHUNKS) - 1)]
     ready = ready[0] if len(ready) == 1 else jnp.concatenate(ready, axis=1)

time: 112 us -> 121 us (1.080)
  waiting for transfers between devices: 37.5 us -> 44.6 us
  local copies, waits for them, and re-layouts: 4.7 us -> 7.98 us
  starting transfers between devices: 25.4 us -> 24 us
    ppermute x10 -> x14, waiting for transfers between devices: 9.5 us -> 17.4 us  [flipped(): lax.ppermute(block, axis, [(i, i ^ flip) for i in range(lax.axis_size(axi...]
    all_gather x1, waiting for transfers between devices: 7.69 us -> 0.01 us  [on_device(): lax.all_gather(after(jnp.concatenate([far, near]), held[1], last, *[kv[1]...]
    ppermute x4, waiting for transfers between devices: 20.2 us -> 24.4 us  [route_of(): return lambda block: lax.ppermute(block, TILES, route)]
    ppermute x4, starting transfers between devices: 7.01 us -> 10.3 us  [the longest x2 10.1 us: on_device(): lax.ppermute(after(x, wait), TILES, route)]
    slice x2 -> x4, local copies, waits for them, and re-layouts: 0.08 us -> 3 us  [on_device(): x[:, f * HEAD_DIM:(f + n) * HEAD_DIM]]
    ppermute x4, waiting for transfers between devices: 0.01 us -> 2.85 us  [the longest x2 2.39 us: on_device(): lax.ppermute(after(x, wait), TILES, route)]
    ppermute x10 -> x14, starting transfers between devices: 14.1 us -> 11.3 us  [flipped(): lax.ppermute(block, axis, [(i, i ^ flip) for i in range(lax.axis_size(axi...]
    ppermute x4, starting transfers between devices: 4.31 us -> 2.27 us  [route_of(): return lambda block: lax.ppermute(block, TILES, route)]
  transfers between devices with their start and end apart: 19 -> 23, of which waited for: 5 -> 7; matrix products, arithmetic and copies ran while one was open for 5% -> 7% of each run, Pallas kernels for 16% -> 14%
where the time goes in v12:
time: 121 us; the launch traced here: 120 us
  waiting for transfers between devices  44.6 us (37%)
  Pallas kernels  24.7 us (20%)
  starting transfers between devices  24 us (20%)
  between operations  13.7 us (11%)
  local copies, waits for them, and re-layouts  7.98 us (7%)
  other arithmetic  4.93 us (4%)
    ppermute x4, waiting for transfers between devices, route_of(): return lambda block: lax.ppermute(block, TILES, route)  24.4 us
    ppermute x14, waiting for transfers between devices, flipped(): lax.ppermute(block, axis, [(i, i ^ flip) for i in range(lax.axis_size(axi...  17.4 us
    ppermute x14, starting transfers between devices, flipped(): lax.ppermute(block, axis, [(i, i ^ flip) for i in range(lax.axis_size(axi...  11.3 us
    ppermute x2, starting transfers between devices, on_device(): lax.ppermute(after(x, wait), TILES, route)  10.1 us
    pallas_call x1, Pallas kernels, finish(): pl.pallas_call(functools.partial(finish_kernel, which, len(weight), moves...  7.38 us
    pallas_call x1, Pallas kernels, begin(): pl.pallas_call(functools.partial(begin_kernel, (len(weight), len(control)...  6.2 us
    pallas_call x1, Pallas kernels, attend(): pl.pallas_call(functools.partial(attend_kernel, which), out_shape=[jax.Sh...  5.93 us
    pallas_call x1, Pallas kernels, close(): pl.pallas_call(functools.partial(close_kernel, first, which), out_shape=j...  5.23 us
  transfers between devices with their start and end apart: 23, of which 7 were waited for; matrix products, arithmetic and copies ran while one was open for 7% of the time, Pallas kernels for 14%

profile of v12, /device:TPU:1, one launch (start us, length us, event | category | flops | bytes accessed | tf_op | source)
XLA Modules:
  0.0 119.9 jit_solution(9778779321424998329)
XLA Ops:
  6.5 1.2 slice_select_fusion
  7.7 2.2 %collective-permute-start.7 = (bf16[1,96,1536]{2,1,0:T(8,128)(2,1)S(1)}, bf16[1,96,1536]{2,1,0:T(8,128)(2,1)}, u32[]{:S(2)}, u32[]{:S(2)}) collective-permute-start(bf16[1,96,1536]{2,1,0:T(8,128)(2,1)S(1)} %bitcast.21), channel_id=1, source_target_pairs={{0,4},{4,0},{8,12},{12,8},{1,5},{5,1},{9,13},{13,9},{2,6},{6,2},{1... | collective-permute-start | bytes 884744 | tf_op jit(solution)/shard_map/ppermute | solution.py:339
  9.9 2.3 %collective-permute-start.5 = (bf16[1,96,1536]{2,1,0:T(8,128)(2,1)S(1)}, bf16[1,96,1536]{2,1,0:T(8,128)(2,1)S(1)}, u32[]{:S(2)}, u32[]{:S(2)}) collective-permute-start(bf16[1,96,1536]{2,1,0:T(8,128)(2,1)S(1)} %bitcast.22), channel_id=1, source_target_pairs={{0,8},{4,12},{8,0},{12,4},{1,9},{5,13},{9,1},{13,5},{2,10},{6,14},... | collective-permute-start | bytes 884744 | tf_op jit(solution)/shard_map/ppermute | solution.py:339
  12.2 1.2 %collective-permute-start.3 = (bf16[1,96,1536]{2,1,0:T(8,128)(2,1)S(1)}, bf16[1,96,1536]{2,1,0:T(8,128)(2,1)S(1)}, u32[]{:S(2)}, u32[]{:S(2)}) collective-permute-start(bf16[1,96,1536]{2,1,0:T(8,128)(2,1)S(1)} %bitcast.23), channel_id=1, source_target_pairs={{0,2},{2,0},{1,3},{3,1},{4,6},{6,4},{5,7},{7,5},{8,10},{10,8},{9,1... | collective-permute-start | bytes 884744 | tf_op jit(solution)/shard_map/ppermute | solution.py:339
  13.4 3.6 %collective-permute-start.2 = (bf16[192,1536]{1,0:T(8,128)(2,1)}, bf16[192,1536]{1,0:T(8,128)(2,1)S(1)}, u32[]{:S(2)}, u32[]{:S(2)}) collective-permute-start(bf16[192,1536]{1,0:T(8,128)(2,1)} %refs_0_.1), channel_id=1, source_target_pairs={{1,2},{2,1},{5,6},{6,5},{9,10},{10,9},{13,14},{14,13},{17,18},{18,... | collective-permute-start | bytes 1769480 | tf_op jit(solution)/shard_map/ppermute | solution.py:446
  17.0 1.0 slice.22
  18.0 1.0 slice.23
  19.0 1.1 dynamic-slice_bitcast_fusion
  20.1 0.1 pad_maximum_fusion.1.refs_1_.refs_3_
  20.2 1.3 %collective-permute-start.9 = (bf16[2,96,1536]{2,1,0:T(8,128)(2,1)S(1)}, bf16[2,96,1536]{2,1,0:T(8,128)(2,1)S(1)}, u32[]{:S(2)}, u32[]{:S(2)}) collective-permute-start(bf16[2,96,1536]{2,1,0:T(8,128)(2,1)S(1)} %pad_maximum_fusion.1.refs_1_.refs_3_), channel_id=1, source_target_pairs={{0,16},{16,0},{1,17},{17,1},{2,18},{18,2},{3,19},{19,3},{4,20},{20... | collective-permute-start | bytes 1769480 | tf_op jit(solution)/shard_map/ppermute | solution.py:339
  21.5 6.6 %collective-permute-start.4 = (bf16[192,1536]{1,0:T(8,128)(2,1)}, bf16[192,1536]{1,0:T(8,128)(2,1)}, u32[]{:S(2)}, u32[]{:S(2)}) collective-permute-start(bf16[192,1536]{1,0:T(8,128)(2,1)} %refs_1_.1), channel_id=1, source_target_pairs={{1,2},{2,1},{5,6},{6,5},{9,10},{10,9},{13,14},{14,13},{17,18},{18,... | collective-permute-start | bytes 1769480 | tf_op jit(solution)/shard_map/ppermute | solution.py:446
  28.1 0.8 pad_maximum_fusion.3
  28.9 1.0 slice.21
  29.9 0.9 pad_maximum_fusion
  30.8 0.7 copy-done.14
  31.6 0.2 collective-permute-start.10
  31.8 2.0 %pad_maximum_fusion.2 = bf16[2,96,1536]{2,1,0:T(8,128)(2,1)} fusion(bf16[1,96,1536]{2,1,0:T(8,128)(2,1)} %collective-permute-done.7, bf16[1,96,1536]{2,1,0:T(8,128)(2,1)} %copy-done.14), kind=kLoop, calls=%fused_computation.2 | loop fusion | flops 294912 | bytes 1179648 | tf_op jit(solution)/shard_map/concatenate | solution.py:462
  33.7 2.4 %collective-permute-done.4.refs_5_ = bf16[192,1536]{1,0:T(8,128)(2,1)} collective-permute-done((bf16[192,1536]{1,0:T(8,128)(2,1)}, bf16[192,1536]{1,0:T(8,128)(2,1)}, u32[]{:S(2)}, u32[]{:S(2)}) %collective-permute-start.4) | collective-permute-done | bytes 589856 | tf_op jit(solution)/shard_map/ppermute | solution.py:446
  36.1 2.4 %collective-permute-done.10 = bf16[1,96,1536]{2,1,0:T(8,128)(2,1)S(1)} collective-permute-done((bf16[1,96,1536]{2,1,0:T(8,128)(2,1)}, bf16[1,96,1536]{2,1,0:T(8,128)(2,1)S(1)}, u32[]{:S(2)}, u32[]{:S(2)}) %collective-permute-start.10) | collective-permute-done | bytes 294944 | tf_op jit(solution)/shard_map/ppermute | solution.py:339
  38.5 0.0 all-gather.3.cloned.1.call-update
  38.5 0.1 collective-permute-start
  38.6 0.2 collective-permute-start.13
  38.8 0.1 collective-permute-start.6
  38.8 0.6 collective-permute-start.11
  39.4 0.7 collective-permute-start.8
  40.1 0.5 collective-permute-done.refs_2_
  40.6 0.8 copy-done.12
  41.4 0.1 collective-permute-start.1
  41.6 5.8 %collective-permute-done.13 = bf16[1,96,1536]{2,1,0:T(8,128)(2,1)S(1)} collective-permute-done((bf16[1,96,1536]{2,1,0:T(8,128)(2,1)S(1)}, bf16[1,96,1536]{2,1,0:T(8,128)(2,1)S(1)}, u32[]{:S(2)}, u32[]{:S(2)}) %collective-permute-start.13) | collective-permute-done | bytes 294944 | tf_op jit(solution)/shard_map/ppermute | solution.py:339
  47.4 0.1 collective-permute-start.15
  47.5 24.4 %collective-permute-done.6.refs_0_ = bf16[192,1792]{1,0:T(8,128)(2,1)S(1)} collective-permute-done((bf16[192,1792]{1,0:T(8,128)(2,1)}, bf16[192,1792]{1,0:T(8,128)(2,1)S(1)}, u32[]{:S(2)}, u32[]{:S(2)}) %collective-permute-start.6) | collective-permute-done | bytes 688160 | tf_op jit(solution)/shard_map/ppermute | solution.py:356
  71.9 0.5 collective-permute-start.12
  72.4 0.1 collective-permute-start.17
  72.4 1.5 %collective-permute-start.18 = (bf16[48,3072]{1,0:T(8,128)(2,1)}, bf16[48,3072]{1,0:T(8,128)(2,1)S(1)}, u32[]{:S(2)}, u32[]{:S(2)}) collective-permute-start(bf16[48,3072]{1,0:T(8,128)(2,1)} %get-tuple-element.44), channel_id=1, source_target_pairs={{0,2},{1,3},{2,0},{3,1},{4,6},{5,7},{6,4},{7,5},{8,10},{9,11},{10,... | collective-permute-start | bytes 884744 | tf_op jit(solution)/shard_map/ppermute | solution.py:339
  74.0 0.6 collective-permute-start.14
  74.6 0.1 collective-permute-start.16
  74.7 0.2 collective-permute-done.17.refs_10_
  75.0 1.5 %collective-permute-start.21 = (bf16[192,1280]{1,0:T(8,128)(2,1)}, bf16[192,1280]{1,0:T(8,128)(2,1)}, u32[]{:S(2)}, u32[]{:S(2)}) collective-permute-start(bf16[192,1280]{1,0:T(8,128)(2,1)} %pad_maximum_fusion.3), channel_id=1, source_target_pairs={{0,4},{4,0},{1,5},{5,1},{2,6},{6,2},{3,7},{7,3},{8,12},{12,8},{9,1... | collective-permute-start | bytes 1474568 | tf_op jit(solution)/shard_map/ppermute | solution.py:356
  76.5 9.0 %collective-permute-done.18.refs_11_ = bf16[48,3072]{1,0:T(8,128)(2,1)S(1)} collective-permute-done((bf16[48,3072]{1,0:T(8,128)(2,1)}, bf16[48,3072]{1,0:T(8,128)(2,1)S(1)}, u32[]{:S(2)}, u32[]{:S(2)}) %collective-permute-start.18) | collective-permute-done | bytes 294944 | tf_op jit(solution)/shard_map/ppermute | solution.py:339
  85.5 0.7 copy-done.16
  86.2 0.5 collective-permute-start.19
  86.6 5.9 %attend.1 = (f32[192,1536]{1,0:T(8,128)}, f32[192,128]{1,0:T(8,128)}) custom-call(s32[1,6]{1,0:T(1,128)} %pattern.5, bf16[192,1536]{1,0:T(8,128)(2,1)} %q.5, bf16[192,1536]{1,0:T(8,128)(2,1)} %refs_0_.1, bf16[192,1536]{1,0:T(8,128)(2,1)} %refs_1_.1, bf16[192,1536]{1,0:T(8,128)(2,1)} %copy-done.12, bf16[192,1536]{1,0:T(8,128)(2,1)} %copy-done.13, ...), custom_call_target="tpu_custom_call" | custom-call | flops 1019215872 | bytes 5308416 | tf_op jit(solution)/shard_map/attend/pallas_call | solution.py:104
  92.6 5.2 %close.1.ready = bf16[192,896]{1,0:T(8,128)(2,1)} custom-call(s32[1,6]{1,0:T(1,128)} %pattern.5, bf16[192,1536]{1,0:T(8,128)(2,1)} %q.5, f32[192,1536]{1,0:T(8,128)} %get-tuple-element.30.part, f32[192,128]{1,0:T(8,128)} %get-tuple-element.31.stats, bf16[192,1792]{1,0:T(8,128)(2,1)} %copy-done.9, bf16[192,1792]{1,0:T(8,128)(2,1)} %copy-done.10), custom_call_target="tpu_custom_call" | custom-call | flops 396361728 | bytes 2752512 | tf_op jit(solution)/shard_map/close/pallas_call | solution.py:170
  97.9 0.0 copy-start.17
  97.9 0.7 copy-done.17
  98.6 0.8 copy-done.6
  99.4 6.2 %begin.1.so_far = f32[192,3072]{1,0:T(8,128)} custom-call(bf16[192,3072]{1,0:T(8,128)(2,1)} %hidden.1, bf16[192,896]{1,0:T(8,128)(2,1)} %close.1.ready, bf16[8,2,96,1536]{3,2,1,0:T(8,128)(2,1)} %bitcast.19, bf16[2,96,1536]{2,1,0:T(8,128)(2,1)} %copy-done, bf16[2,96,1536]{2,1,0:T(8,128)(2,1)} %copy-done.3, bf16[2,96,1536]{2,1,0:T(8,128)(2,1)} %copy-done.2, ...), custom_call_target="tpu_custom_call" | custom-call | flops 1056964608 | bytes 10223616 | tf_op jit(solution)/shard_map/begin/pallas_call | solution.py:300
  105.7 7.4 %finish.1 = bf16[192,3072]{1,0:T(8,128)(2,1)} custom-call(s32[1,6]{1,0:T(1,128)} %pattern.5, bf16[192,1536]{1,0:T(8,128)(2,1)} %q.5, f32[192,1536]{1,0:T(8,128)} %get-tuple-element.30.part, f32[192,128]{1,0:T(8,128)} %get-tuple-element.31.stats, f32[192,3072]{1,0:T(8,128)} %begin.1.so_far, bf16[192,1280]{1,0:T(8,128)(2,1)} %collective-permute-done.20.refs_0_, ...), custom_call_target="tpu_custom_call" | custom-call | flops 754974720 | bytes 7471104 | tf_op jit(solution)/shard_map/finish/pallas_call | solution.py:321
  (51 shorter events, 0.2 us)
Async XLA Ops:
  6.5 12.5 %copy-start.8 = (bf16[192,3072]{1,0:T(8,128)(2,1)S(1)}, bf16[192,3072]{1,0:T(8,128)(2,1)}, u32[]{:S(2)}) copy-start(bf16[192,3072]{1,0:T(8,128)(2,1)} %param.11) | copy-start | bytes 3538948
  6.5 92.1 %all-gather.3.cloned.1.call-start = ((), (), s32[]{:S(2)}) async-start(), calls=%async_computation | async-start | bytes 5308416 | tf_op jit(solution)/shard_map/all_gather | solution.py:462
  7.7 23.1 %collective-permute-start.7 = (bf16[1,96,1536]{2,1,0:T(8,128)(2,1)S(1)}, bf16[1,96,1536]{2,1,0:T(8,128)(2,1)}, u32[]{:S(2)}, u32[]{:S(2)}) collective-permute-start(bf16[1,96,1536]{2,1,0:T(8,128)(2,1)S(1)} %bitcast.21), channel_id=1, source_target_pairs={{0,4},{4,0},{8,12},{12,8},{1,5},{5,1},{9,13},{13,9},{2,6},{6,2},{1... | collective-permute-start | bytes 884744 | tf_op jit(solution)/shard_map/ppermute | solution.py:339
  9.9 20.9 %collective-permute-start.5 = (bf16[1,96,1536]{2,1,0:T(8,128)(2,1)S(1)}, bf16[1,96,1536]{2,1,0:T(8,128)(2,1)S(1)}, u32[]{:S(2)}, u32[]{:S(2)}) collective-permute-start(bf16[1,96,1536]{2,1,0:T(8,128)(2,1)S(1)} %bitcast.22), channel_id=1, source_target_pairs={{0,8},{4,12},{8,0},{12,4},{1,9},{5,13},{9,1},{13,5},{2,10},{6,14},... | collective-permute-start | bytes 884744 | tf_op jit(solution)/shard_map/ppermute | solution.py:339
  12.2 7.9 %collective-permute-start.3 = (bf16[1,96,1536]{2,1,0:T(8,128)(2,1)S(1)}, bf16[1,96,1536]{2,1,0:T(8,128)(2,1)S(1)}, u32[]{:S(2)}, u32[]{:S(2)}) collective-permute-start(bf16[1,96,1536]{2,1,0:T(8,128)(2,1)S(1)} %bitcast.23), channel_id=1, source_target_pairs={{0,2},{2,0},{1,3},{3,1},{4,6},{6,4},{5,7},{7,5},{8,10},{10,8},{9,1... | collective-permute-start | bytes 884744 | tf_op jit(solution)/shard_map/ppermute | solution.py:339
  13.4 18.1 %collective-permute-start.2 = (bf16[192,1536]{1,0:T(8,128)(2,1)}, bf16[192,1536]{1,0:T(8,128)(2,1)S(1)}, u32[]{:S(2)}, u32[]{:S(2)}) collective-permute-start(bf16[192,1536]{1,0:T(8,128)(2,1)} %refs_0_.1), channel_id=1, source_target_pairs={{1,2},{2,1},{5,6},{6,5},{9,10},{10,9},{13,14},{14,13},{17,18},{18,... | collective-permute-start | bytes 1769480 | tf_op jit(solution)/shard_map/ppermute | solution.py:446
  20.1 8.8 %copy-start.7 = (bf16[192,1536]{1,0:T(8,128)(2,1)S(1)}, bf16[192,1536]{1,0:T(8,128)(2,1)}, u32[]{:S(2)}) copy-start(bf16[192,1536]{1,0:T(8,128)(2,1)} %refs_0_.1) | copy-start | bytes 1769476
  20.2 18.6 %copy-start = (bf16[2,96,1536]{2,1,0:T(8,128)(2,1)}, bf16[2,96,1536]{2,1,0:T(8,128)(2,1)S(1)}, u32[]{:S(2)}) copy-start(bf16[2,96,1536]{2,1,0:T(8,128)(2,1)S(1)} %pad_maximum_fusion.1.refs_1_.refs_3_) | copy-start | bytes 1769476
  20.2 16.0 %collective-permute-start.9 = (bf16[2,96,1536]{2,1,0:T(8,128)(2,1)S(1)}, bf16[2,96,1536]{2,1,0:T(8,128)(2,1)S(1)}, u32[]{:S(2)}, u32[]{:S(2)}) collective-permute-start(bf16[2,96,1536]{2,1,0:T(8,128)(2,1)S(1)} %pad_maximum_fusion.1.refs_1_.refs_3_), channel_id=1, source_target_pairs={{0,16},{16,0},{1,17},{17,1},{2,18},{18,2},{3,19},{19,3},{4,20},{20... | collective-permute-start | bytes 1769480 | tf_op jit(solution)/shard_map/ppermute | solution.py:339
  21.5 14.6 %collective-permute-start.4 = (bf16[192,1536]{1,0:T(8,128)(2,1)}, bf16[192,1536]{1,0:T(8,128)(2,1)}, u32[]{:S(2)}, u32[]{:S(2)}) collective-permute-start(bf16[192,1536]{1,0:T(8,128)(2,1)} %refs_1_.1), channel_id=1, source_target_pairs={{1,2},{2,1},{5,6},{6,5},{9,10},{10,9},{13,14},{14,13},{17,18},{18,... | collective-permute-start | bytes 1769480 | tf_op jit(solution)/shard_map/ppermute | solution.py:446
  30.8 0.7 copy-start.14
  31.6 15.8 %copy-start.11 = (bf16[192,1536]{1,0:T(8,128)(2,1)}, bf16[192,1536]{1,0:T(8,128)(2,1)S(1)}, u32[]{:S(2)}) copy-start(bf16[192,1536]{1,0:T(8,128)(2,1)S(1)} %collective-permute-done.2.refs_4_) | copy-start | bytes 1769476
  31.6 6.9 %collective-permute-start.10 = (bf16[1,96,1536]{2,1,0:T(8,128)(2,1)}, bf16[1,96,1536]{2,1,0:T(8,128)(2,1)S(1)}, u32[]{:S(2)}, u32[]{:S(2)}) collective-permute-start(bf16[1,96,1536]{2,1,0:T(8,128)(2,1)} %copy-done.14), channel_id=1, source_target_pairs={{0,4},{4,0},{8,12},{12,8},{1,5},{5,1},{9,13},{13,9},{2,6},{6,2},{1... | collective-permute-start | bytes 884744 | tf_op jit(solution)/shard_map/ppermute | solution.py:339
  36.1 56.5 %copy-start.2 = (bf16[2,96,1536]{2,1,0:T(8,128)(2,1)}, bf16[2,96,1536]{2,1,0:T(8,128)(2,1)S(1)}, u32[]{:S(2)}) copy-start(bf16[2,96,1536]{2,1,0:T(8,128)(2,1)S(1)} %collective-permute-done.9.refs_3_.refs_5_) | copy-start | bytes 1769476
  38.5 2.1 %collective-permute-start = (bf16[192,1536]{1,0:T(8,128)(2,1)S(1)}, bf16[192,1536]{1,0:T(8,128)(2,1)S(1)}, u32[]{:S(2)}, u32[]{:S(2)}) collective-permute-start(bf16[192,1536]{1,0:T(8,128)(2,1)S(1)} %copy-done.7), channel_id=1, source_target_pairs={{0,1},{1,0},{2,3},{3,2},{4,5},{5,4},{6,7},{7,6},{8,9},{9,8},{10,11... | collective-permute-start | bytes 1769480 | tf_op jit(solution)/shard_map/ppermute | solution.py:452
  38.6 8.8 %collective-permute-start.13 = (bf16[1,96,1536]{2,1,0:T(8,128)(2,1)S(1)}, bf16[1,96,1536]{2,1,0:T(8,128)(2,1)S(1)}, u32[]{:S(2)}, u32[]{:S(2)}) collective-permute-start(bf16[1,96,1536]{2,1,0:T(8,128)(2,1)S(1)} %collective-permute-done.10), channel_id=1, source_target_pairs={{0,2},{2,0},{1,3},{3,1},{4,6},{6,4},{5,7},{7,5},{8,10},{10,8},{9,1... | collective-permute-start | bytes 884744 | tf_op jit(solution)/shard_map/ppermute | solution.py:339
  38.8 33.1 %collective-permute-start.6 = (bf16[192,1792]{1,0:T(8,128)(2,1)}, bf16[192,1792]{1,0:T(8,128)(2,1)S(1)}, u32[]{:S(2)}, u32[]{:S(2)}) collective-permute-start(bf16[192,1792]{1,0:T(8,128)(2,1)} %pad_maximum_fusion), channel_id=1, source_target_pairs={{0,8},{8,0},{1,9},{9,1},{2,10},{10,2},{3,11},{11,3},{4,12},{12,4},... | collective-permute-start | bytes 2064392 | tf_op jit(solution)/shard_map/ppermute | solution.py:356
  38.8 33.6 %collective-permute-start.11 = (bf16[2,96,1536]{2,1,0:T(8,128)(2,1)S(1)}, bf16[2,96,1536]{2,1,0:T(8,128)(2,1)S(1)}, u32[]{:S(2)}, u32[]{:S(2)}) collective-permute-start(bf16[2,96,1536]{2,1,0:T(8,128)(2,1)S(1)} %pad_maximum_fusion.1.refs_1_.refs_3_), channel_id=1, source_target_pairs={{0,1},{1,0},{2,3},{3,2},{4,5},{5,4},{6,7},{7,6},{8,9},{9,8},{10,11... | collective-permute-start | bytes 1769480 | tf_op jit(solution)/shard_map/ppermute | solution.py:339
  39.4 32.9 %collective-permute-start.8 = (bf16[192,1792]{1,0:T(8,128)(2,1)}, bf16[192,1792]{1,0:T(8,128)(2,1)S(1)}, u32[]{:S(2)}, u32[]{:S(2)}) collective-permute-start(bf16[192,1792]{1,0:T(8,128)(2,1)} %pad_maximum_fusion), channel_id=1, source_target_pairs={{0,4},{4,0},{1,5},{5,1},{2,6},{6,2},{3,7},{7,3},{8,12},{12,8},{9,1... | collective-permute-start | bytes 2064392 | tf_op jit(solution)/shard_map/ppermute | solution.py:356
  40.6 0.8 copy-start.12
  41.4 32.6 %collective-permute-start.1 = (bf16[192,1536]{1,0:T(8,128)(2,1)}, bf16[192,1536]{1,0:T(8,128)(2,1)S(1)}, u32[]{:S(2)}, u32[]{:S(2)}) collective-permute-start(bf16[192,1536]{1,0:T(8,128)(2,1)} %refs_1_.1), channel_id=1, source_target_pairs={{0,1},{1,0},{2,3},{3,2},{4,5},{5,4},{6,7},{7,6},{8,9},{9,8},{10,11... | collective-permute-start | bytes 1769480 | tf_op jit(solution)/shard_map/ppermute | solution.py:453
  47.4 45.2 %copy-start.1 = (bf16[2,96,1536]{2,1,0:T(8,128)(2,1)}, bf16[2,96,1536]{2,1,0:T(8,128)(2,1)S(1)}, u32[]{:S(2)}) copy-start(bf16[2,96,1536]{2,1,0:T(8,128)(2,1)S(1)} %constant_dynamic-update-slice_fusion.refs_5_.refs_7_) | copy-start | bytes 1769476
  47.4 27.2 %collective-permute-start.15 = (bf16[2,96,1536]{2,1,0:T(8,128)(2,1)S(1)}, bf16[2,96,1536]{2,1,0:T(8,128)(2,1)S(1)}, u32[]{:S(2)}, u32[]{:S(2)}) collective-permute-start(bf16[2,96,1536]{2,1,0:T(8,128)(2,1)S(1)} %constant_dynamic-update-slice_fusion.refs_5_.refs_7_), channel_id=1, source_target_pairs={{0,16},{16,0},{1,17},{17,1},{2,18},{18,2},{3,19},{19,3},{4,20},{20... | collective-permute-start | bytes 1769480 | tf_op jit(solution)/shard_map/ppermute | solution.py:339
  71.9 3.1 %copy-start.9 = (bf16[192,1792]{1,0:T(8,128)(2,1)}, bf16[192,1792]{1,0:T(8,128)(2,1)S(1)}, u32[]{:S(2)}) copy-start(bf16[192,1792]{1,0:T(8,128)(2,1)S(1)} %collective-permute-done.6.refs_0_) | copy-start | bytes 2064388
  71.9 3.1 %collective-permute-start.12 = (bf16[2,96,1536]{2,1,0:T(8,128)(2,1)S(1)}, bf16[2,96,1536]{2,1,0:T(8,128)(2,1)S(1)}, u32[]{:S(2)}, u32[]{:S(2)}) collective-permute-start(bf16[2,96,1536]{2,1,0:T(8,128)(2,1)S(1)} %collective-permute-done.9.refs_3_.refs_5_), channel_id=1, source_target_pairs={{0,1},{1,0},{2,3},{3,2},{4,5},{5,4},{6,7},{7,6},{8,9},{9,8},{10,11... | collective-permute-start | bytes 1769480 | tf_op jit(solution)/shard_map/ppermute | solution.py:339
  72.3 4.1 %copy-start.10 = (bf16[192,1792]{1,0:T(8,128)(2,1)}, bf16[192,1792]{1,0:T(8,128)(2,1)S(1)}, u32[]{:S(2)}) copy-start(bf16[192,1792]{1,0:T(8,128)(2,1)S(1)} %collective-permute-done.8.refs_1_) | copy-start | bytes 2064388
  72.4 2.6 %collective-permute-start.17 = (bf16[48,3072]{1,0:T(8,128)(2,1)}, bf16[48,3072]{1,0:T(8,128)(2,1)S(1)}, u32[]{:S(2)}, u32[]{:S(2)}) collective-permute-start(bf16[48,3072]{1,0:T(8,128)(2,1)} %get-tuple-element.42), channel_id=1, source_target_pairs={{0,1},{1,0},{2,3},{3,2},{4,5},{5,4},{6,7},{7,6},{8,9},{9,8},{10,11... | collective-permute-start | bytes 884744 | tf_op jit(solution)/shard_map/ppermute | solution.py:339
  72.4 20.2 %copy-start.3 = (bf16[2,96,1536]{2,1,0:T(8,128)(2,1)}, bf16[2,96,1536]{2,1,0:T(8,128)(2,1)S(1)}, u32[]{:S(2)}) copy-start(bf16[2,96,1536]{2,1,0:T(8,128)(2,1)S(1)} %collective-permute-done.11.refs_2_.refs_4_) | copy-start | bytes 1769476
  72.4 13.0 %collective-permute-start.18 = (bf16[48,3072]{1,0:T(8,128)(2,1)}, bf16[48,3072]{1,0:T(8,128)(2,1)S(1)}, u32[]{:S(2)}, u32[]{:S(2)}) collective-permute-start(bf16[48,3072]{1,0:T(8,128)(2,1)} %get-tuple-element.44), channel_id=1, source_target_pairs={{0,2},{1,3},{2,0},{3,1},{4,6},{5,7},{6,4},{7,5},{8,10},{9,11},{10,... | collective-permute-start | bytes 884744 | tf_op jit(solution)/shard_map/ppermute | solution.py:339
  74.0 11.5 %copy-start.13 = (bf16[192,1536]{1,0:T(8,128)(2,1)}, bf16[192,1536]{1,0:T(8,128)(2,1)S(1)}, u32[]{:S(2)}) copy-start(bf16[192,1536]{1,0:T(8,128)(2,1)S(1)} %collective-permute-done.1.refs_3_) | copy-start | bytes 1769476
  74.0 23.9 %collective-permute-start.14 = (bf16[2,96,1536]{2,1,0:T(8,128)(2,1)S(1)}, bf16[2,96,1536]{2,1,0:T(8,128)(2,1)S(1)}, u32[]{:S(2)}, u32[]{:S(2)}) collective-permute-start(bf16[2,96,1536]{2,1,0:T(8,128)(2,1)S(1)} %constant_dynamic-update-slice_fusion.refs_5_.refs_7_), channel_id=1, source_target_pairs={{0,1},{1,0},{2,3},{3,2},{4,5},{5,4},{6,7},{7,6},{8,9},{9,8},{10,11... | collective-permute-start | bytes 1769480 | tf_op jit(solution)/shard_map/ppermute | solution.py:339
  74.6 18.0 %copy-start.4 = (bf16[2,96,1536]{2,1,0:T(8,128)(2,1)}, bf16[2,96,1536]{2,1,0:T(8,128)(2,1)S(1)}, u32[]{:S(2)}) copy-start(bf16[2,96,1536]{2,1,0:T(8,128)(2,1)S(1)} %collective-permute-done.15.refs_7_.refs_9_) | copy-start | bytes 1769476
  74.6 24.0 %collective-permute-start.16 = (bf16[2,96,1536]{2,1,0:T(8,128)(2,1)S(1)}, bf16[2,96,1536]{2,1,0:T(8,128)(2,1)}, u32[]{:S(2)}, u32[]{:S(2)}) collective-permute-start(bf16[2,96,1536]{2,1,0:T(8,128)(2,1)S(1)} %collective-permute-done.15.refs_7_.refs_9_), channel_id=1, source_target_pairs={{0,1},{1,0},{2,3},{3,2},{4,5},{5,4},{6,7},{7,6},{8,9},{9,8},{10,11... | collective-permute-start | bytes 1769480 | tf_op jit(solution)/shard_map/ppermute | solution.py:339
  74.9 10.5 %copy-start.15 = (bf16[48,3072]{1,0:T(8,128)(2,1)}, bf16[48,3072]{1,0:T(8,128)(2,1)S(1)}, u32[]{:S(2)}) copy-start(bf16[48,3072]{1,0:T(8,128)(2,1)S(1)} %collective-permute-done.17.refs_10_) | copy-start | bytes 884740
  74.9 30.7 %collective-permute-start.20 = (bf16[192,1280]{1,0:T(8,128)(2,1)}, bf16[192,1280]{1,0:T(8,128)(2,1)}, u32[]{:S(2)}, u32[]{:S(2)}) collective-permute-start(bf16[192,1280]{1,0:T(8,128)(2,1)} %pad_maximum_fusion.3), channel_id=1, source_target_pairs={{0,8},{8,0},{1,9},{9,1},{2,10},{10,2},{3,11},{11,3},{4,12},{12,4},... | collective-permute-start | bytes 1474568 | tf_op jit(solution)/shard_map/ppermute | solution.py:356
  74.9 17.7 %copy-start.5 = (bf16[2,96,1536]{2,1,0:T(8,128)(2,1)}, bf16[2,96,1536]{2,1,0:T(8,128)(2,1)S(1)}, u32[]{:S(2)}) copy-start(bf16[2,96,1536]{2,1,0:T(8,128)(2,1)S(1)} %collective-permute-done.12.refs_4_.refs_6_) | copy-start | bytes 1769476
  75.0 30.7 %collective-permute-start.21 = (bf16[192,1280]{1,0:T(8,128)(2,1)}, bf16[192,1280]{1,0:T(8,128)(2,1)}, u32[]{:S(2)}, u32[]{:S(2)}) collective-permute-start(bf16[192,1280]{1,0:T(8,128)(2,1)} %pad_maximum_fusion.3), channel_id=1, source_target_pairs={{0,4},{4,0},{1,5},{5,1},{2,6},{6,2},{3,7},{7,3},{8,12},{12,8},{9,1... | collective-permute-start | bytes 1474568 | tf_op jit(solution)/shard_map/ppermute | solution.py:356
  85.4 0.7 copy-start.16
  86.2 11.7 %collective-permute-start.19 = (bf16[48,3072]{1,0:T(8,128)(2,1)}, bf16[48,3072]{1,0:T(8,128)(2,1)S(1)}, u32[]{:S(2)}, u32[]{:S(2)}) collective-permute-start(bf16[48,3072]{1,0:T(8,128)(2,1)} %get-tuple-element.46), channel_id=1, source_target_pairs={{0,3},{1,2},{2,1},{3,0},{4,7},{5,6},{6,5},{7,4},{8,11},{9,10},{10,... | collective-permute-start | bytes 884744 | tf_op jit(solution)/shard_map/ppermute | solution.py:339
  97.9 0.7 copy-start.17
  98.6 0.8 copy-start.6
Sparse Core Ops, SparseCore 0:
  38.6 46.1 all-gather.2

commit v13 on v11

--- a/solution.py
+++ b/solution.py
@@ -11,7 +11,7 @@
 
 HEAD_DIM = 128
 TILE_W = 8
-CHUNKS = (6, 6)
+CHUNKS = (7, 5)
 SCALE = HEAD_DIM**-0.5 * math.log2(math.e)
 TILES = ("outer", "pair", "core")
 VMEM_LIMIT = 60 * 1024 * 1024
@@ -433,12 +433,12 @@
         jnp.concatenate([x[:, f * HEAD_DIM : (f + n) * HEAD_DIM] for x in (keys, values)], axis=1)
         for f, n in zip(firsts, CHUNKS)
     ]
-    chunks = lax.optimization_barrier(chunks)
     block = rows // grid_width
     lines = after(control, line).reshape(block // TILE_W, grid_width, TILE_W, width)
     control_sent = [
         lax.dynamic_index_in_dim(lines, across ^ d, 1, keepdims=False).reshape(block, width) for d in range(grid_width)
     ]
+    chunks, control_sent = lax.optimization_barrier((chunks, control_sent))
     control_parts = [control_sent[0]] + [None] * (grid_width - 1)
     beside = swap("pair", 1)(line)
     for d in range(2, grid_width):
@@ -446,39 +446,43 @@
     control_parts[1] = swap(TILES, 1)(control_sent[1])
     plane = jnp.concatenate([line, beside])
     last = swap("outer", 1)(after(far, near, *control_parts[2:-1], *chunks))
+    near_x = swap("pair", 1)(near)
+    held = []
+    for both in (plane, jnp.concatenate([near, near_x])):
+        held += [both, swap("groups", 1)(both)]
     early_near = [[None, None] for _ in early]
     for i, x in enumerate((keys, values)):
         early_near[0][i] = lax.ppermute(x, TILES, early[0][2])
         for slot in range(1, len(early)):
             early_near[slot][i] = lax.ppermute(after(x, early_near[0][i]), TILES, early[slot][2])
-    held = [plane, swap("groups", 1)(plane)]
+    state = attend(tuple(s[:2] for s in early), pattern, queries, [keys, values] + [x for kv in early_near for x in kv])
+
+    late_near = []
+    for chunk in chunks:
+        lanes = (far_lane, near_lane)
+        late_near.append([lanes[i % 2](route_of(route), chunk) for i, (_, _, route) in enumerate(late)])
     crossed = [swap("core", 1)(x) for x in held]
-    state = attend(tuple(s[:2] for s in early), pattern, queries, [keys, values] + [x for kv in early_near for x in kv])
-
-    steps = after(jnp.concatenate([far, near, last]), *control_parts[2:], held[1])
-    weight = [lax.all_gather(steps, ("groups", "pair", "core"))]
+
+    gates = [*control_parts[2:], near_x, held[1]]
+    weight = [lax.all_gather(after(jnp.concatenate([far, last]), *gates), ("groups", "pair", "core"))]
     n = len(line_flips)
     moves = [
         (0, ((g * pair + p) * cores + c, i * n + j), (False, g, f ^ at, p, c))
         for g in range(groups)
         for p in range(pair)
         for c in range(cores)
-        for i, at in enumerate((2, 1, 3))
+        for i, at in enumerate((2, 3))
         for j, f in enumerate(line_flips)
     ]
-    for group_flip in range(2):
+    for number, (group_flip, at) in enumerate(((0, 0), (1, 0), (0, 1), (1, 1))):
         for core_flip, pieces in enumerate((held, crossed)):
             moves += [
-                (len(weight), (p * n + j,), (True, group_flip, f, p, core_flip))
+                (len(weight), (p * n + j,), (True, group_flip, f ^ at, p, core_flip))
                 for p in range(pair)
                 for j, f in enumerate(line_flips)
             ]
-            weight.append(pieces[group_flip])
-
-    late_near = []
-    for chunk in chunks:
-        lanes = (far_lane, near_lane)
-        late_near.append([lanes[i % 2](route_of(route), chunk) for i, (_, _, route) in enumerate(late)])
+            weight.append(pieces[number])
+
     which = tuple(s[:2] for s in late)
     ready = [close(which, pattern, queries, state, late_near[i], firsts[i]) for i in range(len(CHUNKS) - 1)]
     ready = ready[0] if len(ready) == 1 else jnp.concatenate(ready, axis=1)

time: 112 us -> 118 us (1.054); the launches traced: 112 us -> 116 us
  waiting for transfers between devices: 37.5 us -> 43.5 us
  Pallas kernels: 25.7 us -> 23.3 us
  local copies, waits for them, and re-layouts: 4.7 us -> 6.9 us
    all_gather x1, waiting for transfers between devices: 7.69 us -> 0.02 us  [on_device(): lax.all_gather(after(jnp.concatenate([far, last]), *gates), ('groups', 'p...]
    ppermute x4, waiting for transfers between devices: 20.2 us -> 27.3 us  [route_of(): return lambda block: lax.ppermute(block, TILES, route)]
    ppermute x10 -> x14, waiting for transfers between devices: 9.5 us -> 15.3 us  [flipped(): lax.ppermute(block, axis, [(i, i ^ flip) for i in range(lax.axis_size(axi...]
    slice x2 -> x4, local copies, waits for them, and re-layouts: 0.08 us -> 3.95 us  [on_device(): x[:, f * HEAD_DIM:(f + n) * HEAD_DIM]]
    pallas_call x1, Pallas kernels: 4.95 us -> 3.21 us  [close(): pl.pallas_call(functools.partial(close_kernel, first, which), out_shape=j...]
    pallas_call x1, Pallas kernels: 8 us -> 6.55 us  [finish(): pl.pallas_call(functools.partial(finish_kernel, which, len(weight), moves...]
    reshape x1, local copies, waits for them, and re-layouts: 2.21 us -> 0.82 us  [on_device(): lax.dynamic_index_in_dim(lines, across ^ d, 1, keepdims=False)]
    ppermute x10 -> x14, starting transfers between devices: 14.1 us -> 15.3 us  [flipped(): lax.ppermute(block, axis, [(i, i ^ flip) for i in range(lax.axis_size(axi...]
  transfers between devices with their start and end apart: 19 -> 23, of which waited for: 5 -> 9; matrix products, arithmetic and copies ran while one was open for 5% -> 6% of each run, Pallas kernels for 16% -> 14%
where the time goes in v13:
time: 118 us; the launch traced here: 116 us
  waiting for transfers between devices  43.5 us (37%)
  starting transfers between devices  24.7 us (21%)
  Pallas kernels  23.3 us (20%)
  between operations  13.7 us (12%)
  local copies, waits for them, and re-layouts  6.9 us (6%)
  other arithmetic  3.83 us (3%)
    ppermute x4, waiting for transfers between devices, route_of(): return lambda block: lax.ppermute(block, TILES, route)  27.3 us
    ppermute x14, starting transfers between devices, flipped(): lax.ppermute(block, axis, [(i, i ^ flip) for i in range(lax.axis_size(axi...  15.3 us
    ppermute x14, waiting for transfers between devices, flipped(): lax.ppermute(block, axis, [(i, i ^ flip) for i in range(lax.axis_size(axi...  15.3 us
    pallas_call x1, Pallas kernels, attend(): pl.pallas_call(functools.partial(attend_kernel, which), out_shape=[jax.Sh...  7.38 us
    pallas_call x1, Pallas kernels, finish(): pl.pallas_call(functools.partial(finish_kernel, which, len(weight), moves...  6.55 us
    pallas_call x1, Pallas kernels, begin(): pl.pallas_call(functools.partial(begin_kernel, (len(weight), len(control)...  6.18 us
    ppermute x2, starting transfers between devices, on_device(): lax.ppermute(after(x, early_near[0][i]), TILES, early[slot][2])  5.56 us
    slice x4, local copies, waits for them, and re-layouts, on_device(): x[:, f * HEAD_DIM:(f + n) * HEAD_DIM]  3.95 us
  transfers between devices with their start and end apart: 23, of which 9 were waited for; matrix products, arithmetic and copies ran while one was open for 6% of the time, Pallas kernels for 14%

profile of v13, /device:TPU:1, one launch (start us, length us, event | category | flops | bytes accessed | tf_op | source)
XLA Modules:
  0.0 115.9 jit_solution(11825714412442595789)
XLA Ops:
  6.5 1.2 %slice_select_fusion = bf16[96,1536]{1,0:T(8,128)(2,1)S(1)} fusion(bf16[96,3072]{1,0:T(8,128)(2,1)} %param.12, pred[]{:T(512)S(6)} %eq.3), kind=kLoop, calls=%fused_computation.8 | loop fusion | flops 147456 | bytes 884737 | tf_op jit(solution)/shard_map/jit(_where)/select_n | solution.py:420
  7.7 2.1 %collective-permute-start.10 = (bf16[1,96,1536]{2,1,0:T(8,128)(2,1)S(1)}, bf16[1,96,1536]{2,1,0:T(8,128)(2,1)S(1)}, u32[]{:S(2)}, u32[]{:S(2)}) collective-permute-start(bf16[1,96,1536]{2,1,0:T(8,128)(2,1)S(1)} %bitcast.21), channel_id=1, source_target_pairs={{0,2},{2,0},{1,3},{3,1},{4,6},{6,4},{5,7},{7,5},{8,10},{10,8},{9,1... | collective-permute-start | bytes 884744 | tf_op jit(solution)/shard_map/ppermute | solution.py:339
  9.8 1.3 %collective-permute-start.6 = (bf16[1,96,1536]{2,1,0:T(8,128)(2,1)S(1)}, bf16[1,96,1536]{2,1,0:T(8,128)(2,1)S(1)}, u32[]{:S(2)}, u32[]{:S(2)}) collective-permute-start(bf16[1,96,1536]{2,1,0:T(8,128)(2,1)S(1)} %bitcast.22), channel_id=1, source_target_pairs={{0,4},{4,0},{8,12},{12,8},{1,5},{5,1},{9,13},{13,9},{2,6},{6,2},{1... | collective-permute-start | bytes 884744 | tf_op jit(solution)/shard_map/ppermute | solution.py:339
  11.1 2.3 %collective-permute-start.4 = (bf16[1,96,1536]{2,1,0:T(8,128)(2,1)S(1)}, bf16[1,96,1536]{2,1,0:T(8,128)(2,1)S(1)}, u32[]{:S(2)}, u32[]{:S(2)}) collective-permute-start(bf16[1,96,1536]{2,1,0:T(8,128)(2,1)S(1)} %bitcast.23), channel_id=1, source_target_pairs={{0,8},{4,12},{8,0},{12,4},{1,9},{5,13},{9,1},{13,5},{2,10},{6,14},... | collective-permute-start | bytes 884744 | tf_op jit(solution)/shard_map/ppermute | solution.py:339
  13.4 1.0 slice.20
  14.4 1.0 slice.21
  15.4 0.8 dynamic-slice_bitcast_fusion
  16.2 0.8 pad_maximum_fusion.3
  17.0 1.0 slice.18
  18.0 1.0 slice.19
  19.1 0.9 pad_maximum_fusion
  20.0 0.3 collective-permute-start.8
  20.3 1.3 %collective-permute-start.13 = (bf16[2,96,1536]{2,1,0:T(8,128)(2,1)S(1)}, bf16[2,96,1536]{2,1,0:T(8,128)(2,1)S(1)}, u32[]{:S(2)}, u32[]{:S(2)}) collective-permute-start(bf16[2,96,1536]{2,1,0:T(8,128)(2,1)S(1)} %pad_maximum_fusion.2.refs_1_.refs_3_), channel_id=1, source_target_pairs={{0,16},{16,0},{1,17},{17,1},{2,18},{18,2},{3,19},{19,3},{4,20},{20... | collective-permute-start | bytes 1769480 | tf_op jit(solution)/shard_map/ppermute | solution.py:339
  21.6 2.0 %collective-permute-done.6 = bf16[1,96,1536]{2,1,0:T(8,128)(2,1)S(1)} collective-permute-done((bf16[1,96,1536]{2,1,0:T(8,128)(2,1)S(1)}, bf16[1,96,1536]{2,1,0:T(8,128)(2,1)S(1)}, u32[]{:S(2)}, u32[]{:S(2)}) %collective-permute-start.6) | collective-permute-done | bytes 294944 | tf_op jit(solution)/shard_map/ppermute | solution.py:339
  23.6 3.4 %collective-permute-done.8.refs_11_ = bf16[48,3072]{1,0:T(8,128)(2,1)} collective-permute-done((bf16[48,3072]{1,0:T(8,128)(2,1)S(1)}, bf16[48,3072]{1,0:T(8,128)(2,1)}, u32[]{:S(2)}, u32[]{:S(2)}) %collective-permute-start.8) | collective-permute-done | bytes 294944 | tf_op jit(solution)/shard_map/ppermute | solution.py:339
  27.0 0.2 collective-permute-start.9
  27.2 0.3 collective-permute-start.12
  27.5 4.1 %collective-permute-start.11 = (bf16[48,3072]{1,0:T(8,128)(2,1)S(1)}, bf16[48,3072]{1,0:T(8,128)(2,1)S(1)}, u32[]{:S(2)}, u32[]{:S(2)}) collective-permute-start(bf16[48,3072]{1,0:T(8,128)(2,1)S(1)} %get-tuple-element.37), channel_id=1, source_target_pairs={{0,3},{1,2},{2,1},{3,0},{4,7},{5,6},{6,5},{7,4},{8,11},{9,10},{10,... | collective-permute-start | bytes 884744 | tf_op jit(solution)/shard_map/ppermute | solution.py:339
  31.6 1.5 %collective-permute-done.9 = bf16[1,96,1536]{2,1,0:T(8,128)(2,1)S(1)} collective-permute-done((bf16[1,96,1536]{2,1,0:T(8,128)(2,1)S(1)}, bf16[1,96,1536]{2,1,0:T(8,128)(2,1)S(1)}, u32[]{:S(2)}, u32[]{:S(2)}) %collective-permute-start.9) | collective-permute-done | bytes 294944 | tf_op jit(solution)/shard_map/ppermute | solution.py:339
  33.1 0.9 pad_maximum_fusion.1
  34.0 8.3 %collective-permute-done.11.refs_12_ = bf16[48,3072]{1,0:T(8,128)(2,1)S(1)} collective-permute-done((bf16[48,3072]{1,0:T(8,128)(2,1)S(1)}, bf16[48,3072]{1,0:T(8,128)(2,1)S(1)}, u32[]{:S(2)}, u32[]{:S(2)}) %collective-permute-start.11) | collective-permute-done | bytes 294944 | tf_op jit(solution)/shard_map/ppermute | solution.py:339
  42.3 0.1 collective-permute-start
  42.4 0.5 collective-permute-start.1
  42.9 0.1 collective-permute-start.19
  43.0 0.4 collective-permute-start.14
  43.4 0.6 collective-permute-start.5
  44.1 0.7 collective-permute-done.refs_2_
  44.7 1.3 %collective-permute-start.7 = (bf16[192,1792]{1,0:T(8,128)(2,1)}, bf16[192,1792]{1,0:T(8,128)(2,1)S(1)}, u32[]{:S(2)}, u32[]{:S(2)}) collective-permute-start(bf16[192,1792]{1,0:T(8,128)(2,1)} %pad_maximum_fusion), channel_id=1, source_target_pairs={{0,4},{4,0},{1,5},{5,1},{2,6},{6,2},{3,7},{7,3},{8,12},{12,8},{9,1... | collective-permute-start | bytes 2064392 | tf_op jit(solution)/shard_map/ppermute | solution.py:356
  46.1 0.2 collective-permute-done.1.refs_3_
  46.2 1.2 %collective-permute-start.17 = (bf16[2,96,1536]{2,1,0:T(8,128)(2,1)S(1)}, bf16[2,96,1536]{2,1,0:T(8,128)(2,1)S(1)}, u32[]{:S(2)}, u32[]{:S(2)}) collective-permute-start(bf16[2,96,1536]{2,1,0:T(8,128)(2,1)S(1)} %constant_dynamic-update-slice_fusion.refs_5_.refs_7_), channel_id=1, source_target_pairs={{0,16},{16,0},{1,17},{17,1},{2,18},{18,2},{3,19},{19,3},{4,20},{20... | collective-permute-start | bytes 1769480 | tf_op jit(solution)/shard_map/ppermute | solution.py:339
  47.5 2.7 %collective-permute-start.2 = (bf16[192,1536]{1,0:T(8,128)(2,1)}, bf16[192,1536]{1,0:T(8,128)(2,1)S(1)}, u32[]{:S(2)}, u32[]{:S(2)}) collective-permute-start(bf16[192,1536]{1,0:T(8,128)(2,1)} %refs_0_.1), channel_id=1, source_target_pairs={{1,2},{2,1},{5,6},{6,5},{9,10},{10,9},{13,14},{14,13},{17,18},{18,... | collective-permute-start | bytes 1769480 | tf_op jit(solution)/shard_map/ppermute | solution.py:457
  50.2 2.9 %collective-permute-start.3 = (bf16[192,1536]{1,0:T(8,128)(2,1)}, bf16[192,1536]{1,0:T(8,128)(2,1)S(1)}, u32[]{:S(2)}, u32[]{:S(2)}) collective-permute-start(bf16[192,1536]{1,0:T(8,128)(2,1)} %refs_1_.1), channel_id=1, source_target_pairs={{1,2},{2,1},{5,6},{6,5},{9,10},{10,9},{13,14},{14,13},{17,18},{18,... | collective-permute-start | bytes 1769480 | tf_op jit(solution)/shard_map/ppermute | solution.py:457
  53.1 23.2 %collective-permute-done.5.refs_0_ = bf16[192,1792]{1,0:T(8,128)(2,1)S(1)} collective-permute-done((bf16[192,1792]{1,0:T(8,128)(2,1)}, bf16[192,1792]{1,0:T(8,128)(2,1)S(1)}, u32[]{:S(2)}, u32[]{:S(2)}) %collective-permute-start.5) | collective-permute-done | bytes 688160 | tf_op jit(solution)/shard_map/ppermute | solution.py:356
  76.2 0.9 collective-permute-start.16
  77.1 0.1 collective-permute-start.15
  77.2 0.8 collective-permute-start.18
  78.0 0.6 collective-permute-start.20
  78.6 0.2 copy-done.11
  78.9 0.8 copy-done.12
  79.7 0.7 collective-permute-start.21
  80.4 7.4 %attend.1 = (f32[192,1536]{1,0:T(8,128)}, f32[192,128]{1,0:T(8,128)}) custom-call(s32[1,6]{1,0:T(1,128)} %pattern.5, bf16[192,1536]{1,0:T(8,128)(2,1)} %q.5, bf16[192,1536]{1,0:T(8,128)(2,1)} %refs_0_.1, bf16[192,1536]{1,0:T(8,128)(2,1)} %refs_1_.1, bf16[192,1536]{1,0:T(8,128)(2,1)} %collective-permute-done.refs_2_, bf16[192,1536]{1,0:T(8,128)(2,1)} %copy-done.10, ...), custom_call_target="tpu_custom_call" | custom-call | flops 1019215872 | bytes 5308416 | tf_op jit(solution)/shard_map/attend/pallas_call | solution.py:104
  87.8 3.2 %close.1.ready = bf16[192,896]{1,0:T(8,128)(2,1)} custom-call(s32[1,6]{1,0:T(1,128)} %pattern.5, bf16[192,1536]{1,0:T(8,128)(2,1)} %q.5, f32[192,1536]{1,0:T(8,128)} %get-tuple-element.26.part, f32[192,128]{1,0:T(8,128)} %get-tuple-element.27.stats, bf16[192,1792]{1,0:T(8,128)(2,1)} %copy-done.8, bf16[192,1792]{1,0:T(8,128)(2,1)} %copy-done.9), custom_call_target="tpu_custom_call" | custom-call | flops 396361728 | bytes 2752512 | tf_op jit(solution)/shard_map/close/pallas_call | solution.py:170
  91.2 0.8 copy-done.5
  91.9 0.2 copy-done.6
  92.1 6.2 %begin.1.so_far = f32[192,3072]{1,0:T(8,128)} custom-call(bf16[192,3072]{1,0:T(8,128)(2,1)} %hidden.1, bf16[192,896]{1,0:T(8,128)(2,1)} %close.1.ready, bf16[8,2,96,1536]{3,2,1,0:T(8,128)(2,1)} %bitcast.19, bf16[2,96,1536]{2,1,0:T(8,128)(2,1)} %copy-done, bf16[2,96,1536]{2,1,0:T(8,128)(2,1)} %copy-done.3, bf16[2,96,1536]{2,1,0:T(8,128)(2,1)} %copy-done.2, ...), custom_call_target="tpu_custom_call" | custom-call | flops 1056964608 | bytes 10223616 | tf_op jit(solution)/shard_map/begin/pallas_call | solution.py:300
  98.3 3.6 %collective-permute-done.20.refs_0_ = bf16[192,1280]{1,0:T(8,128)(2,1)} collective-permute-done((bf16[192,1280]{1,0:T(8,128)(2,1)}, bf16[192,1280]{1,0:T(8,128)(2,1)}, u32[]{:S(2)}, u32[]{:S(2)}) %collective-permute-start.20) | collective-permute-done | bytes 491552 | tf_op jit(solution)/shard_map/ppermute | solution.py:356
  101.9 0.6 collective-permute-done.21.refs_1_
  102.5 6.5 %finish.1 = bf16[192,3072]{1,0:T(8,128)(2,1)} custom-call(s32[1,6]{1,0:T(1,128)} %pattern.5, bf16[192,1536]{1,0:T(8,128)(2,1)} %q.5, f32[192,1536]{1,0:T(8,128)} %get-tuple-element.26.part, f32[192,128]{1,0:T(8,128)} %get-tuple-element.27.stats, f32[192,3072]{1,0:T(8,128)} %begin.1.so_far, bf16[192,1280]{1,0:T(8,128)(2,1)} %collective-permute-done.20.refs_0_, ...), custom_call_target="tpu_custom_call" | custom-call | flops 754974720 | bytes 7471104 | tf_op jit(solution)/shard_map/finish/pallas_call | solution.py:321
  (45 shorter events, 0.2 us)
Async XLA Ops:
  6.5 8.9 %copy-start.7 = (bf16[192,3072]{1,0:T(8,128)(2,1)S(1)}, bf16[192,3072]{1,0:T(8,128)(2,1)}, u32[]{:S(2)}) copy-start(bf16[192,3072]{1,0:T(8,128)(2,1)} %param.11) | copy-start | bytes 3538948
  6.5 84.6 %all-gather.3.cloned.1.call-start = ((), (), s32[]{:S(2)}) async-start(), calls=%async_computation | async-start | bytes 5308416 | tf_op jit(solution)/shard_map/all_gather | solution.py:467
  7.7 12.5 %collective-permute-start.10 = (bf16[1,96,1536]{2,1,0:T(8,128)(2,1)S(1)}, bf16[1,96,1536]{2,1,0:T(8,128)(2,1)S(1)}, u32[]{:S(2)}, u32[]{:S(2)}) collective-permute-start(bf16[1,96,1536]{2,1,0:T(8,128)(2,1)S(1)} %bitcast.21), channel_id=1, source_target_pairs={{0,2},{2,0},{1,3},{3,1},{4,6},{6,4},{5,7},{7,5},{8,10},{10,8},{9,1... | collective-permute-start | bytes 884744 | tf_op jit(solution)/shard_map/ppermute | solution.py:339
  9.8 13.8 %collective-permute-start.6 = (bf16[1,96,1536]{2,1,0:T(8,128)(2,1)S(1)}, bf16[1,96,1536]{2,1,0:T(8,128)(2,1)S(1)}, u32[]{:S(2)}, u32[]{:S(2)}) collective-permute-start(bf16[1,96,1536]{2,1,0:T(8,128)(2,1)S(1)} %bitcast.22), channel_id=1, source_target_pairs={{0,4},{4,0},{8,12},{12,8},{1,5},{5,1},{9,13},{13,9},{2,6},{6,2},{1... | collective-permute-start | bytes 884744 | tf_op jit(solution)/shard_map/ppermute | solution.py:339
  11.1 12.5 %collective-permute-start.4 = (bf16[1,96,1536]{2,1,0:T(8,128)(2,1)S(1)}, bf16[1,96,1536]{2,1,0:T(8,128)(2,1)S(1)}, u32[]{:S(2)}, u32[]{:S(2)}) collective-permute-start(bf16[1,96,1536]{2,1,0:T(8,128)(2,1)S(1)} %bitcast.23), channel_id=1, source_target_pairs={{0,8},{4,12},{8,0},{12,4},{1,9},{5,13},{9,1},{13,5},{2,10},{6,14},... | collective-permute-start | bytes 884744 | tf_op jit(solution)/shard_map/ppermute | solution.py:339
  20.0 7.1 %collective-permute-start.8 = (bf16[48,3072]{1,0:T(8,128)(2,1)S(1)}, bf16[48,3072]{1,0:T(8,128)(2,1)}, u32[]{:S(2)}, u32[]{:S(2)}) collective-permute-start(bf16[48,3072]{1,0:T(8,128)(2,1)S(1)} %get-tuple-element.33), channel_id=1, source_target_pairs={{0,2},{1,3},{2,0},{3,1},{4,6},{5,7},{6,4},{7,5},{8,10},{9,11},{10,... | collective-permute-start | bytes 884744 | tf_op jit(solution)/shard_map/ppermute | solution.py:339
  20.3 25.8 %copy-start = (bf16[2,96,1536]{2,1,0:T(8,128)(2,1)}, bf16[2,96,1536]{2,1,0:T(8,128)(2,1)S(1)}, u32[]{:S(2)}) copy-start(bf16[2,96,1536]{2,1,0:T(8,128)(2,1)S(1)} %pad_maximum_fusion.2.refs_1_.refs_3_) | copy-start | bytes 1769476
  20.3 22.0 %collective-permute-start.13 = (bf16[2,96,1536]{2,1,0:T(8,128)(2,1)S(1)}, bf16[2,96,1536]{2,1,0:T(8,128)(2,1)S(1)}, u32[]{:S(2)}, u32[]{:S(2)}) collective-permute-start(bf16[2,96,1536]{2,1,0:T(8,128)(2,1)S(1)} %pad_maximum_fusion.2.refs_1_.refs_3_), channel_id=1, source_target_pairs={{0,16},{16,0},{1,17},{17,1},{2,18},{18,2},{3,19},{19,3},{4,20},{20... | collective-permute-start | bytes 1769480 | tf_op jit(solution)/shard_map/ppermute | solution.py:339
  27.0 6.1 %collective-permute-start.9 = (bf16[1,96,1536]{2,1,0:T(8,128)(2,1)S(1)}, bf16[1,96,1536]{2,1,0:T(8,128)(2,1)S(1)}, u32[]{:S(2)}, u32[]{:S(2)}) collective-permute-start(bf16[1,96,1536]{2,1,0:T(8,128)(2,1)S(1)} %collective-permute-done.4), channel_id=1, source_target_pairs={{0,4},{4,0},{8,12},{12,8},{1,5},{5,1},{9,13},{13,9},{2,6},{6,2},{1... | collective-permute-start | bytes 884744 | tf_op jit(solution)/shard_map/ppermute | solution.py:339
  27.2 6.8 %collective-permute-start.12 = (bf16[1,96,1536]{2,1,0:T(8,128)(2,1)S(1)}, bf16[1,96,1536]{2,1,0:T(8,128)(2,1)S(1)}, u32[]{:S(2)}, u32[]{:S(2)}) collective-permute-start(bf16[1,96,1536]{2,1,0:T(8,128)(2,1)S(1)} %collective-permute-done.6), channel_id=1, source_target_pairs={{0,2},{2,0},{1,3},{3,1},{4,6},{6,4},{5,7},{7,5},{8,10},{10,8},{9,1... | collective-permute-start | bytes 884744 | tf_op jit(solution)/shard_map/ppermute | solution.py:339
  27.5 14.8 %collective-permute-start.11 = (bf16[48,3072]{1,0:T(8,128)(2,1)S(1)}, bf16[48,3072]{1,0:T(8,128)(2,1)S(1)}, u32[]{:S(2)}, u32[]{:S(2)}) collective-permute-start(bf16[48,3072]{1,0:T(8,128)(2,1)S(1)} %get-tuple-element.37), channel_id=1, source_target_pairs={{0,3},{1,2},{2,1},{3,0},{4,7},{5,6},{6,5},{7,4},{8,11},{9,10},{10,... | collective-permute-start | bytes 884744 | tf_op jit(solution)/shard_map/ppermute | solution.py:339
  42.3 1.1 copy-start.13
  42.3 45.5 %copy-start.2 = (bf16[2,96,1536]{2,1,0:T(8,128)(2,1)}, bf16[2,96,1536]{2,1,0:T(8,128)(2,1)S(1)}, u32[]{:S(2)}) copy-start(bf16[2,96,1536]{2,1,0:T(8,128)(2,1)S(1)} %collective-permute-done.13.refs_3_.refs_5_) | copy-start | bytes 1769476
  42.3 2.4 %collective-permute-start = (bf16[192,1536]{1,0:T(8,128)(2,1)}, bf16[192,1536]{1,0:T(8,128)(2,1)}, u32[]{:S(2)}, u32[]{:S(2)}) collective-permute-start(bf16[192,1536]{1,0:T(8,128)(2,1)} %refs_0_.1), channel_id=1, source_target_pairs={{0,1},{1,0},{2,3},{3,2},{4,5},{5,4},{6,7},{7,6},{8,9},{9,8},{10,11... | collective-permute-start | bytes 1769480 | tf_op jit(solution)/shard_map/ppermute | solution.py:455
  42.4 3.9 %collective-permute-start.1 = (bf16[192,1536]{1,0:T(8,128)(2,1)}, bf16[192,1536]{1,0:T(8,128)(2,1)S(1)}, u32[]{:S(2)}, u32[]{:S(2)}) collective-permute-start(bf16[192,1536]{1,0:T(8,128)(2,1)} %refs_1_.1), channel_id=1, source_target_pairs={{0,1},{1,0},{2,3},{3,2},{4,5},{5,4},{6,7},{7,6},{8,9},{9,8},{10,11... | collective-permute-start | bytes 1769480 | tf_op jit(solution)/shard_map/ppermute | solution.py:455
  42.9 4.6 %collective-permute-start.19 = (bf16[48,3072]{1,0:T(8,128)(2,1)S(1)}, bf16[48,3072]{1,0:T(8,128)(2,1)S(1)}, u32[]{:S(2)}, u32[]{:S(2)}) collective-permute-start(bf16[48,3072]{1,0:T(8,128)(2,1)S(1)} %get-tuple-element.40), channel_id=1, source_target_pairs={{0,1},{1,0},{2,3},{3,2},{4,5},{5,4},{6,7},{7,6},{8,9},{9,8},{10,11... | collective-permute-start | bytes 884744 | tf_op jit(solution)/shard_map/ppermute | solution.py:339
  43.0 7.2 %collective-permute-start.14 = (bf16[2,96,1536]{2,1,0:T(8,128)(2,1)S(1)}, bf16[2,96,1536]{2,1,0:T(8,128)(2,1)S(1)}, u32[]{:S(2)}, u32[]{:S(2)}) collective-permute-start(bf16[2,96,1536]{2,1,0:T(8,128)(2,1)S(1)} %pad_maximum_fusion.2.refs_1_.refs_3_), channel_id=1, source_target_pairs={{0,1},{1,0},{2,3},{3,2},{4,5},{5,4},{6,7},{7,6},{8,9},{9,8},{10,11... | collective-permute-start | bytes 1769480 | tf_op jit(solution)/shard_map/ppermute | solution.py:339
  43.4 32.9 %collective-permute-start.5 = (bf16[192,1792]{1,0:T(8,128)(2,1)}, bf16[192,1792]{1,0:T(8,128)(2,1)S(1)}, u32[]{:S(2)}, u32[]{:S(2)}) collective-permute-start(bf16[192,1792]{1,0:T(8,128)(2,1)} %pad_maximum_fusion), channel_id=1, source_target_pairs={{0,8},{8,0},{1,9},{9,1},{2,10},{10,2},{3,11},{11,3},{4,12},{12,4},... | collective-permute-start | bytes 2064392 | tf_op jit(solution)/shard_map/ppermute | solution.py:356
  44.7 32.4 %collective-permute-start.7 = (bf16[192,1792]{1,0:T(8,128)(2,1)}, bf16[192,1792]{1,0:T(8,128)(2,1)S(1)}, u32[]{:S(2)}, u32[]{:S(2)}) collective-permute-start(bf16[192,1792]{1,0:T(8,128)(2,1)} %pad_maximum_fusion), channel_id=1, source_target_pairs={{0,4},{4,0},{1,5},{5,1},{2,6},{6,2},{3,7},{7,3},{8,12},{12,8},{9,1... | collective-permute-start | bytes 2064392 | tf_op jit(solution)/shard_map/ppermute | solution.py:356
  46.1 41.7 %copy-start.1 = (bf16[2,96,1536]{2,1,0:T(8,128)(2,1)}, bf16[2,96,1536]{2,1,0:T(8,128)(2,1)S(1)}, u32[]{:S(2)}) copy-start(bf16[2,96,1536]{2,1,0:T(8,128)(2,1)S(1)} %constant_dynamic-update-slice_fusion.refs_5_.refs_7_) | copy-start | bytes 1769476
  46.2 31.8 %copy-start.10 = (bf16[192,1536]{1,0:T(8,128)(2,1)}, bf16[192,1536]{1,0:T(8,128)(2,1)S(1)}, u32[]{:S(2)}) copy-start(bf16[192,1536]{1,0:T(8,128)(2,1)S(1)} %collective-permute-done.1.refs_3_) | copy-start | bytes 1769476
  46.2 31.0 %collective-permute-start.17 = (bf16[2,96,1536]{2,1,0:T(8,128)(2,1)S(1)}, bf16[2,96,1536]{2,1,0:T(8,128)(2,1)S(1)}, u32[]{:S(2)}, u32[]{:S(2)}) collective-permute-start(bf16[2,96,1536]{2,1,0:T(8,128)(2,1)S(1)} %constant_dynamic-update-slice_fusion.refs_5_.refs_7_), channel_id=1, source_target_pairs={{0,16},{16,0},{1,17},{17,1},{2,18},{18,2},{3,19},{19,3},{4,20},{20... | collective-permute-start | bytes 1769480 | tf_op jit(solution)/shard_map/ppermute | solution.py:339
  47.5 43.7 %copy-start.14 = (bf16[48,3072]{1,0:T(8,128)(2,1)}, bf16[48,3072]{1,0:T(8,128)(2,1)S(1)}, u32[]{:S(2)}) copy-start(bf16[48,3072]{1,0:T(8,128)(2,1)S(1)} %collective-permute-done.19.refs_10_) | copy-start | bytes 884740
  47.5 30.5 %collective-permute-start.2 = (bf16[192,1536]{1,0:T(8,128)(2,1)}, bf16[192,1536]{1,0:T(8,128)(2,1)S(1)}, u32[]{:S(2)}, u32[]{:S(2)}) collective-permute-start(bf16[192,1536]{1,0:T(8,128)(2,1)} %refs_0_.1), channel_id=1, source_target_pairs={{1,2},{2,1},{5,6},{6,5},{9,10},{10,9},{13,14},{14,13},{17,18},{18,... | collective-permute-start | bytes 1769480 | tf_op jit(solution)/shard_map/ppermute | solution.py:457
  50.2 37.6 %copy-start.3 = (bf16[2,96,1536]{2,1,0:T(8,128)(2,1)}, bf16[2,96,1536]{2,1,0:T(8,128)(2,1)S(1)}, u32[]{:S(2)}) copy-start(bf16[2,96,1536]{2,1,0:T(8,128)(2,1)S(1)} %collective-permute-done.14.refs_2_.refs_4_) | copy-start | bytes 1769476
  50.2 28.7 %collective-permute-start.3 = (bf16[192,1536]{1,0:T(8,128)(2,1)}, bf16[192,1536]{1,0:T(8,128)(2,1)S(1)}, u32[]{:S(2)}, u32[]{:S(2)}) collective-permute-start(bf16[192,1536]{1,0:T(8,128)(2,1)} %refs_1_.1), channel_id=1, source_target_pairs={{1,2},{2,1},{5,6},{6,5},{9,10},{10,9},{13,14},{14,13},{17,18},{18,... | collective-permute-start | bytes 1769480 | tf_op jit(solution)/shard_map/ppermute | solution.py:457
  76.2 1.0 copy-start.8
  76.2 14.8 %collective-permute-start.16 = (bf16[2,96,1536]{2,1,0:T(8,128)(2,1)S(1)}, bf16[2,96,1536]{2,1,0:T(8,128)(2,1)S(1)}, u32[]{:S(2)}, u32[]{:S(2)}) collective-permute-start(bf16[2,96,1536]{2,1,0:T(8,128)(2,1)S(1)} %constant_dynamic-update-slice_fusion.refs_5_.refs_7_), channel_id=1, source_target_pairs={{0,1},{1,0},{2,3},{3,2},{4,5},{5,4},{6,7},{7,6},{8,9},{9,8},{10,11... | collective-permute-start | bytes 1769480 | tf_op jit(solution)/shard_map/ppermute | solution.py:339
  77.1 0.9 copy-start.9
  77.1 14.0 %collective-permute-start.15 = (bf16[2,96,1536]{2,1,0:T(8,128)(2,1)S(1)}, bf16[2,96,1536]{2,1,0:T(8,128)(2,1)S(1)}, u32[]{:S(2)}, u32[]{:S(2)}) collective-permute-start(bf16[2,96,1536]{2,1,0:T(8,128)(2,1)S(1)} %collective-permute-done.13.refs_3_.refs_5_), channel_id=1, source_target_pairs={{0,1},{1,0},{2,3},{3,2},{4,5},{5,4},{6,7},{7,6},{8,9},{9,8},{10,11... | collective-permute-start | bytes 1769480 | tf_op jit(solution)/shard_map/ppermute | solution.py:339
  77.2 10.6 %copy-start.4 = (bf16[2,96,1536]{2,1,0:T(8,128)(2,1)}, bf16[2,96,1536]{2,1,0:T(8,128)(2,1)S(1)}, u32[]{:S(2)}) copy-start(bf16[2,96,1536]{2,1,0:T(8,128)(2,1)S(1)} %collective-permute-done.17.refs_7_.refs_9_) | copy-start | bytes 1769476
  77.2 13.9 %collective-permute-start.18 = (bf16[2,96,1536]{2,1,0:T(8,128)(2,1)S(1)}, bf16[2,96,1536]{2,1,0:T(8,128)(2,1)}, u32[]{:S(2)}, u32[]{:S(2)}) collective-permute-start(bf16[2,96,1536]{2,1,0:T(8,128)(2,1)S(1)} %collective-permute-done.17.refs_7_.refs_9_), channel_id=1, source_target_pairs={{0,1},{1,0},{2,3},{3,2},{4,5},{5,4},{6,7},{7,6},{8,9},{9,8},{10,11... | collective-permute-start | bytes 1769480 | tf_op jit(solution)/shard_map/ppermute | solution.py:339
  78.0 0.9 copy-start.11
  78.0 23.9 %collective-permute-start.20 = (bf16[192,1280]{1,0:T(8,128)(2,1)}, bf16[192,1280]{1,0:T(8,128)(2,1)}, u32[]{:S(2)}, u32[]{:S(2)}) collective-permute-start(bf16[192,1280]{1,0:T(8,128)(2,1)} %pad_maximum_fusion.3), channel_id=1, source_target_pairs={{0,8},{8,0},{1,9},{9,1},{2,10},{10,2},{3,11},{11,3},{4,12},{12,4},... | collective-permute-start | bytes 1474568 | tf_op jit(solution)/shard_map/ppermute | solution.py:356
  78.9 0.8 copy-start.12
  79.7 22.8 %collective-permute-start.21 = (bf16[192,1280]{1,0:T(8,128)(2,1)}, bf16[192,1280]{1,0:T(8,128)(2,1)}, u32[]{:S(2)}, u32[]{:S(2)}) collective-permute-start(bf16[192,1280]{1,0:T(8,128)(2,1)} %pad_maximum_fusion.3), channel_id=1, source_target_pairs={{0,4},{4,0},{1,5},{5,1},{2,6},{6,2},{3,7},{7,3},{8,12},{12,8},{9,1... | collective-permute-start | bytes 1474568 | tf_op jit(solution)/shard_map/ppermute | solution.py:356
  91.1 0.9 copy-start.5
  91.1 1.0 copy-start.6
Sparse Core Ops, SparseCore 0:
  42.4 43.5 all-gather.2

commit v14 on v13

--- a/solution.py
+++ b/solution.py
@@ -11,7 +11,7 @@
 
 HEAD_DIM = 128
 TILE_W = 8
-CHUNKS = (7, 5)
+CHUNKS = (6, 6)
 SCALE = HEAD_DIM**-0.5 * math.log2(math.e)
 TILES = ("outer", "pair", "core")
 VMEM_LIMIT = 60 * 1024 * 1024
@@ -441,9 +441,8 @@
     chunks, control_sent = lax.optimization_barrier((chunks, control_sent))
     control_parts = [control_sent[0]] + [None] * (grid_width - 1)
     beside = swap("pair", 1)(line)
-    for d in range(2, grid_width):
-        control_parts[d] = swap(TILES, d)(after(control_sent[d], line if d < grid_width - 1 else beside))
-    control_parts[1] = swap(TILES, 1)(control_sent[1])
+    for d in range(2, grid_width - 1):
+        control_parts[d] = swap(TILES, d)(after(control_sent[d], line))
     plane = jnp.concatenate([line, beside])
     last = swap("outer", 1)(after(far, near, *control_parts[2:-1], *chunks))
     near_x = swap("pair", 1)(near)
@@ -462,8 +461,10 @@
         lanes = (far_lane, near_lane)
         late_near.append([lanes[i % 2](route_of(route), chunk) for i, (_, _, route) in enumerate(late)])
     crossed = [swap("core", 1)(x) for x in held]
-
-    gates = [*control_parts[2:], near_x, held[1]]
+    for d in (1, grid_width - 1):
+        control_parts[d] = swap(TILES, d)(after(control_sent[d], *[x for kv in early_near[1:] for x in kv]))
+
+    gates = [*control_parts[2:-1], near_x, held[1]]
     weight = [lax.all_gather(after(jnp.concatenate([far, last]), *gates), ("groups", "pair", "core"))]
     n = len(line_flips)
     moves = [

time: 118 us -> 110 us (0.932)
  waiting for transfers between devices: 43.5 us -> 39.6 us
  local copies, waits for them, and re-layouts: 6.9 us -> 3.26 us
  starting transfers between devices: 24.7 us -> 26.6 us
    ppermute x4, waiting for transfers between devices: 27.3 us -> 22.6 us  [route_of(): return lambda block: lax.ppermute(block, TILES, route)]
    ppermute x2, starting transfers between devices: 0.57 us -> 3.27 us  [on_device(): early_near[0][i] = lax.ppermute(x, TILES, early[0][2])]
    ppermute x14, starting transfers between devices: 15.3 us -> 12.9 us  [flipped(): lax.ppermute(block, axis, [(i, i ^ flip) for i in range(lax.axis_size(axi...]
    unnamed x31, local copies, waits for them, and re-layouts: 2.1 us -> 0.08 us
    slice x4 -> x2, local copies, waits for them, and re-layouts: 3.95 us -> 2.18 us  [on_device(): x[:, f * HEAD_DIM:(f + n) * HEAD_DIM]]
    ppermute x4, starting transfers between devices: 3.26 us -> 4.94 us  [route_of(): return lambda block: lax.ppermute(block, TILES, route)]
    all_gather x1, waiting for transfers between devices: 0.02 us -> 1.48 us  [on_device(): lax.all_gather(after(jnp.concatenate([far, last]), *gates), ('groups', 'p...]
    pallas_call x1, Pallas kernels: 7.38 us -> 5.97 us  [attend(): pl.pallas_call(functools.partial(attend_kernel, which), out_shape=[jax.Sh...]
  transfers between devices with their start and end apart: 23 -> 23, of which waited for: 9 -> 8; matrix products, arithmetic and copies ran while one was open for 6% -> 5% of each run, Pallas kernels for 14% -> 14%
where the time goes in v14:
time: 110 us; the launch traced here: 109 us
  waiting for transfers between devices  39.6 us (36%)
  starting transfers between devices  26.6 us (24%)
  Pallas kernels  22.6 us (21%)
  between operations  13.7 us (12%)
  local copies, waits for them, and re-layouts  3.26 us (3%)
  other arithmetic  3.09 us (3%)
    ppermute x4, waiting for transfers between devices, route_of(): return lambda block: lax.ppermute(block, TILES, route)  22.6 us
    ppermute x14, waiting for transfers between devices, flipped(): lax.ppermute(block, axis, [(i, i ^ flip) for i in range(lax.axis_size(axi...  15.5 us
    ppermute x14, starting transfers between devices, flipped(): lax.ppermute(block, axis, [(i, i ^ flip) for i in range(lax.axis_size(axi...  12.9 us
    pallas_call x1, Pallas kernels, finish(): pl.pallas_call(functools.partial(finish_kernel, which, len(weight), moves...  7.07 us
    pallas_call x1, Pallas kernels, attend(): pl.pallas_call(functools.partial(attend_kernel, which), out_shape=[jax.Sh...  5.97 us
    ppermute x2, starting transfers between devices, on_device(): lax.ppermute(after(x, early_near[0][i]), TILES, early[slot][2])  5.56 us
    pallas_call x1, Pallas kernels, begin(): pl.pallas_call(functools.partial(begin_kernel, (len(weight), len(control)...  5.53 us
    ppermute x4, starting transfers between devices, route_of(): return lambda block: lax.ppermute(block, TILES, route)  4.94 us
  transfers between devices with their start and end apart: 23, of which 8 were waited for; matrix products, arithmetic and copies ran while one was open for 5% of the time, Pallas kernels for 14%

profile of v14, /device:TPU:1, one launch (start us, length us, event | category | flops | bytes accessed | tf_op | source)
XLA Modules:
  0.0 108.9 jit_solution(10595415016824253454)
XLA Ops:
  6.5 1.2 %slice_select_fusion = bf16[96,1536]{1,0:T(8,128)(2,1)S(1)} fusion(bf16[96,3072]{1,0:T(8,128)(2,1)} %param.12, pred[]{:T(512)S(6)} %eq.3), kind=kLoop, calls=%fused_computation.8 | loop fusion | flops 147456 | bytes 884737 | tf_op jit(solution)/shard_map/jit(_where)/select_n | solution.py:420
  7.7 2.1 %collective-permute-start.11 = (bf16[1,96,1536]{2,1,0:T(8,128)(2,1)S(1)}, bf16[1,96,1536]{2,1,0:T(8,128)(2,1)S(1)}, u32[]{:S(2)}, u32[]{:S(2)}) collective-permute-start(bf16[1,96,1536]{2,1,0:T(8,128)(2,1)S(1)} %bitcast.21), channel_id=1, source_target_pairs={{0,2},{2,0},{1,3},{3,1},{4,6},{6,4},{5,7},{7,5},{8,10},{10,8},{9,1... | collective-permute-start | bytes 884744 | tf_op jit(solution)/shard_map/ppermute | solution.py:339
  9.8 1.3 %collective-permute-start.6 = (bf16[1,96,1536]{2,1,0:T(8,128)(2,1)S(1)}, bf16[1,96,1536]{2,1,0:T(8,128)(2,1)S(1)}, u32[]{:S(2)}, u32[]{:S(2)}) collective-permute-start(bf16[1,96,1536]{2,1,0:T(8,128)(2,1)S(1)} %bitcast.22), channel_id=1, source_target_pairs={{0,4},{4,0},{8,12},{12,8},{1,5},{5,1},{9,13},{13,9},{2,6},{6,2},{1... | collective-permute-start | bytes 884744 | tf_op jit(solution)/shard_map/ppermute | solution.py:339
  11.1 2.3 %collective-permute-start.4 = (bf16[1,96,1536]{2,1,0:T(8,128)(2,1)S(1)}, bf16[1,96,1536]{2,1,0:T(8,128)(2,1)S(1)}, u32[]{:S(2)}, u32[]{:S(2)}) collective-permute-start(bf16[1,96,1536]{2,1,0:T(8,128)(2,1)S(1)} %bitcast.23), channel_id=1, source_target_pairs={{0,8},{4,12},{8,0},{12,4},{1,9},{5,13},{9,1},{13,5},{2,10},{6,14},... | collective-permute-start | bytes 884744 | tf_op jit(solution)/shard_map/ppermute | solution.py:339
  13.4 1.1 %fusion = (bf16[192,768]{1,0:T(8,128)(2,1)S(1)}, bf16[192,768]{1,0:T(8,128)(2,1)S(1)}) fusion(bf16[192,1536]{1,0:T(8,128)(2,1)} %refs_0_.1), kind=kLoop, calls=%fused_computation.11 | loop fusion | bytes 1179648 | tf_op jit(solution)/shard_map/slice | solution.py:433
  14.6 1.0 dynamic-slice_bitcast_fusion
  15.5 1.1 %fusion.1 = (bf16[192,768]{1,0:T(8,128)(2,1)S(1)}, bf16[192,768]{1,0:T(8,128)(2,1)S(1)}) fusion(bf16[192,1536]{1,0:T(8,128)(2,1)} %refs_1_.1), kind=kLoop, calls=%fused_computation.12 | loop fusion | bytes 1179648 | tf_op jit(solution)/shard_map/slice | solution.py:433
  16.6 1.0 pad_maximum_fusion
  17.6 0.3 collective-permute-start.8
  17.8 0.1 pad_maximum_fusion.3.refs_1_.refs_3_
  17.9 1.3 %collective-permute-start.12 = (bf16[2,96,1536]{2,1,0:T(8,128)(2,1)S(1)}, bf16[2,96,1536]{2,1,0:T(8,128)(2,1)S(1)}, u32[]{:S(2)}, u32[]{:S(2)}) collective-permute-start(bf16[2,96,1536]{2,1,0:T(8,128)(2,1)S(1)} %pad_maximum_fusion.3.refs_1_.refs_3_), channel_id=1, source_target_pairs={{0,16},{16,0},{1,17},{17,1},{2,18},{18,2},{3,19},{19,3},{4,20},{20... | collective-permute-start | bytes 1769480 | tf_op jit(solution)/shard_map/ppermute | solution.py:339
  19.2 4.5 %collective-permute-done.6 = bf16[1,96,1536]{2,1,0:T(8,128)(2,1)S(1)} collective-permute-done((bf16[1,96,1536]{2,1,0:T(8,128)(2,1)S(1)}, bf16[1,96,1536]{2,1,0:T(8,128)(2,1)S(1)}, u32[]{:S(2)}, u32[]{:S(2)}) %collective-permute-start.6) | collective-permute-done | bytes 294944 | tf_op jit(solution)/shard_map/ppermute | solution.py:339
  23.7 0.0 collective-permute-done.4
  23.7 1.0 collective-permute-done.8.refs_11_
  24.7 1.4 %collective-permute-start.9 = (bf16[1,96,1536]{2,1,0:T(8,128)(2,1)S(1)}, bf16[1,96,1536]{2,1,0:T(8,128)(2,1)S(1)}, u32[]{:S(2)}, u32[]{:S(2)}) collective-permute-start(bf16[1,96,1536]{2,1,0:T(8,128)(2,1)S(1)} %collective-permute-done.4), channel_id=1, source_target_pairs={{0,4},{4,0},{8,12},{12,8},{1,5},{5,1},{9,13},{13,9},{2,6},{6,2},{1... | collective-permute-start | bytes 884744 | tf_op jit(solution)/shard_map/ppermute | solution.py:339
  26.1 0.3 collective-permute-start.10
  26.3 4.3 %collective-permute-done.9 = bf16[1,96,1536]{2,1,0:T(8,128)(2,1)S(1)} collective-permute-done((bf16[1,96,1536]{2,1,0:T(8,128)(2,1)S(1)}, bf16[1,96,1536]{2,1,0:T(8,128)(2,1)S(1)}, u32[]{:S(2)}, u32[]{:S(2)}) %collective-permute-start.9) | collective-permute-done | bytes 294944 | tf_op jit(solution)/shard_map/ppermute | solution.py:339
  30.6 0.9 pad_maximum_fusion.2
  31.5 0.9 collective-permute-done.10
  32.4 0.0 collective-permute-done.12.refs_3_.refs_5_
  32.4 0.0 all-gather.3.cloned.1.call-update
  32.4 3.2 %collective-permute-start = (bf16[192,1536]{1,0:T(8,128)(2,1)}, bf16[192,1536]{1,0:T(8,128)(2,1)S(1)}, u32[]{:S(2)}, u32[]{:S(2)}) collective-permute-start(bf16[192,1536]{1,0:T(8,128)(2,1)} %refs_0_.1), channel_id=1, source_target_pairs={{0,1},{1,0},{2,3},{3,2},{4,5},{5,4},{6,7},{7,6},{8,9},{9,8},{10,11... | collective-permute-start | bytes 1769480 | tf_op jit(solution)/shard_map/ppermute | solution.py:454
  35.6 0.1 collective-permute-start.1
  35.7 0.4 collective-permute-start.13
  36.1 1.9 %collective-permute-start.5 = (bf16[192,1536]{1,0:T(8,128)(2,1)S(1)}, bf16[192,1536]{1,0:T(8,128)(2,1)S(1)}, u32[]{:S(2)}, u32[]{:S(2)}) collective-permute-start(bf16[192,1536]{1,0:T(8,128)(2,1)S(1)} %get-tuple-element.32), channel_id=1, source_target_pairs={{0,8},{8,0},{1,9},{9,1},{2,10},{10,2},{3,11},{11,3},{4,12},{12,4},... | collective-permute-start | bytes 1769480 | tf_op jit(solution)/shard_map/ppermute | solution.py:356
  38.0 0.6 collective-permute-start.7
  38.7 0.0 copy-start.8
  38.7 1.3 %collective-permute-start.16 = (bf16[2,96,1536]{2,1,0:T(8,128)(2,1)S(1)}, bf16[2,96,1536]{2,1,0:T(8,128)(2,1)S(1)}, u32[]{:S(2)}, u32[]{:S(2)}) collective-permute-start(bf16[2,96,1536]{2,1,0:T(8,128)(2,1)S(1)} %constant_dynamic-update-slice_fusion.refs_5_.refs_7_), channel_id=1, source_target_pairs={{0,16},{16,0},{1,17},{17,1},{2,18},{18,2},{3,19},{19,3},{4,20},{20... | collective-permute-start | bytes 1769480 | tf_op jit(solution)/shard_map/ppermute | solution.py:339
  40.0 2.9 %collective-permute-start.2 = (bf16[192,1536]{1,0:T(8,128)(2,1)}, bf16[192,1536]{1,0:T(8,128)(2,1)S(1)}, u32[]{:S(2)}, u32[]{:S(2)}) collective-permute-start(bf16[192,1536]{1,0:T(8,128)(2,1)} %refs_0_.1), channel_id=1, source_target_pairs={{1,2},{2,1},{5,6},{6,5},{9,10},{10,9},{13,14},{14,13},{17,18},{18,... | collective-permute-start | bytes 1769480 | tf_op jit(solution)/shard_map/ppermute | solution.py:456
  42.9 2.7 %collective-permute-start.3 = (bf16[192,1536]{1,0:T(8,128)(2,1)}, bf16[192,1536]{1,0:T(8,128)(2,1)S(1)}, u32[]{:S(2)}, u32[]{:S(2)}) collective-permute-start(bf16[192,1536]{1,0:T(8,128)(2,1)} %refs_1_.1), channel_id=1, source_target_pairs={{1,2},{2,1},{5,6},{6,5},{9,10},{10,9},{13,14},{14,13},{17,18},{18,... | collective-permute-start | bytes 1769480 | tf_op jit(solution)/shard_map/ppermute | solution.py:456
  45.6 19.0 %collective-permute-done.5.refs_0_ = bf16[192,1536]{1,0:T(8,128)(2,1)S(1)} collective-permute-done((bf16[192,1536]{1,0:T(8,128)(2,1)S(1)}, bf16[192,1536]{1,0:T(8,128)(2,1)S(1)}, u32[]{:S(2)}, u32[]{:S(2)}) %collective-permute-start.5) | collective-permute-done | bytes 589856 | tf_op jit(solution)/shard_map/ppermute | solution.py:356
  64.6 0.9 collective-permute-start.15
  65.5 0.0 collective-permute-done.7.refs_1_
  65.5 0.2 collective-permute-start.14
  65.7 0.4 collective-permute-start.17
  66.0 0.0 collective-permute-done.2.refs_4_
  66.0 0.4 collective-permute-start.20
  66.4 0.0 collective-permute-done.3.refs_5_
  66.4 2.0 %collective-permute-start.21 = (bf16[192,1536]{1,0:T(8,128)(2,1)}, bf16[192,1536]{1,0:T(8,128)(2,1)}, u32[]{:S(2)}, u32[]{:S(2)}) collective-permute-start(bf16[192,1536]{1,0:T(8,128)(2,1)} %get-tuple-element.44), channel_id=1, source_target_pairs={{0,4},{4,0},{1,5},{5,1},{2,6},{6,2},{3,7},{7,3},{8,12},{12,8},{9,1... | collective-permute-start | bytes 1769480 | tf_op jit(solution)/shard_map/ppermute | solution.py:356
  68.5 0.7 collective-permute-start.19
  69.2 0.1 collective-permute-start.18
  69.3 6.0 %attend.1 = (f32[192,1536]{1,0:T(8,128)}, f32[192,128]{1,0:T(8,128)}) custom-call(s32[1,6]{1,0:T(1,128)} %pattern.5, bf16[192,1536]{1,0:T(8,128)(2,1)} %q.5, bf16[192,1536]{1,0:T(8,128)(2,1)} %refs_0_.1, bf16[192,1536]{1,0:T(8,128)(2,1)} %refs_1_.1, bf16[192,1536]{1,0:T(8,128)(2,1)} %copy-done.8, bf16[192,1536]{1,0:T(8,128)(2,1)} %copy-done.9, ...), custom_call_target="tpu_custom_call" | custom-call | flops 1019215872 | bytes 5308416 | tf_op jit(solution)/shard_map/attend/pallas_call | solution.py:104
  75.4 4.0 %close.1.ready = bf16[192,768]{1,0:T(8,128)(2,1)} custom-call(s32[1,6]{1,0:T(1,128)} %pattern.5, bf16[192,1536]{1,0:T(8,128)(2,1)} %q.5, f32[192,1536]{1,0:T(8,128)} %get-tuple-element.27.part, f32[192,128]{1,0:T(8,128)} %get-tuple-element.28.stats, bf16[192,1536]{1,0:T(8,128)(2,1)} %copy-done.12, bf16[192,1536]{1,0:T(8,128)(2,1)} %copy-done.13), custom_call_target="tpu_custom_call" | custom-call | flops 339738624 | bytes 2359296 | tf_op jit(solution)/shard_map/close/pallas_call | solution.py:170
  79.4 4.9 %collective-permute-done.19.refs_12_ = bf16[48,3072]{1,0:T(8,128)(2,1)S(1)} collective-permute-done((bf16[48,3072]{1,0:T(8,128)(2,1)}, bf16[48,3072]{1,0:T(8,128)(2,1)S(1)}, u32[]{:S(2)}, u32[]{:S(2)}) %collective-permute-start.19) | collective-permute-done | bytes 294944 | tf_op jit(solution)/shard_map/ppermute | solution.py:339
  84.3 1.5 %all-gather.3.cloned.1.call-done = bf16[16,96,1536]{2,1,0:T(8,128)(2,1)} async-done(((bf16[2,96,1536]{2,1,0:T(8,128)(2,1)}), bf16[16,96,1536]{2,1,0:T(8,128)(2,1)}) %all-gather.3.cloned.1.call-update) | async-done | bytes 4718608 | tf_op jit(solution)/shard_map/all_gather | solution.py:468
  85.8 5.5 %begin.1.so_far = f32[192,3072]{1,0:T(8,128)} custom-call(bf16[192,3072]{1,0:T(8,128)(2,1)} %hidden.1, bf16[192,768]{1,0:T(8,128)(2,1)} %close.1.ready, bf16[8,2,96,1536]{3,2,1,0:T(8,128)(2,1)} %bitcast.19, bf16[2,96,1536]{2,1,0:T(8,128)(2,1)} %copy-done, bf16[2,96,1536]{2,1,0:T(8,128)(2,1)} %copy-done.3, bf16[2,96,1536]{2,1,0:T(8,128)(2,1)} %copy-done.2, ...), custom_call_target="tpu_custom_call" | custom-call | flops 905969664 | bytes 9437184 | tf_op jit(solution)/shard_map/begin/pallas_call | solution.py:300
  91.3 3.6 %collective-permute-done.20.refs_0_ = bf16[192,1536]{1,0:T(8,128)(2,1)} collective-permute-done((bf16[192,1536]{1,0:T(8,128)(2,1)}, bf16[192,1536]{1,0:T(8,128)(2,1)}, u32[]{:S(2)}, u32[]{:S(2)}) %collective-permute-start.20) | collective-permute-done | bytes 589856 | tf_op jit(solution)/shard_map/ppermute | solution.py:356
  94.9 7.1 %finish.1 = bf16[192,3072]{1,0:T(8,128)(2,1)} custom-call(s32[1,6]{1,0:T(1,128)} %pattern.5, bf16[192,1536]{1,0:T(8,128)(2,1)} %q.5, f32[192,1536]{1,0:T(8,128)} %get-tuple-element.27.part, f32[192,128]{1,0:T(8,128)} %get-tuple-element.28.stats, f32[192,3072]{1,0:T(8,128)} %begin.1.so_far, bf16[192,1536]{1,0:T(8,128)(2,1)} %collective-permute-done.20.refs_0_, ...), custom_call_target="tpu_custom_call" | custom-call | flops 905969664 | bytes 8257536 | tf_op jit(solution)/shard_map/finish/pallas_call | solution.py:321
  (42 shorter events, 0.1 us)
Async XLA Ops:
  6.5 8.0 %copy-start.7 = (bf16[192,3072]{1,0:T(8,128)(2,1)S(1)}, bf16[192,3072]{1,0:T(8,128)(2,1)}, u32[]{:S(2)}) copy-start(bf16[192,3072]{1,0:T(8,128)(2,1)} %param.11) | copy-start | bytes 3538948
  6.5 79.3 %all-gather.3.cloned.1.call-start = ((), (), s32[]{:S(2)}) async-start(), calls=%async_computation | async-start | bytes 5308416 | tf_op jit(solution)/shard_map/all_gather | solution.py:468
  7.7 10.1 %collective-permute-start.11 = (bf16[1,96,1536]{2,1,0:T(8,128)(2,1)S(1)}, bf16[1,96,1536]{2,1,0:T(8,128)(2,1)S(1)}, u32[]{:S(2)}, u32[]{:S(2)}) collective-permute-start(bf16[1,96,1536]{2,1,0:T(8,128)(2,1)S(1)} %bitcast.21), channel_id=1, source_target_pairs={{0,2},{2,0},{1,3},{3,1},{4,6},{6,4},{5,7},{7,5},{8,10},{10,8},{9,1... | collective-permute-start | bytes 884744 | tf_op jit(solution)/shard_map/ppermute | solution.py:339
  9.8 13.9 %collective-permute-start.6 = (bf16[1,96,1536]{2,1,0:T(8,128)(2,1)S(1)}, bf16[1,96,1536]{2,1,0:T(8,128)(2,1)S(1)}, u32[]{:S(2)}, u32[]{:S(2)}) collective-permute-start(bf16[1,96,1536]{2,1,0:T(8,128)(2,1)S(1)} %bitcast.22), channel_id=1, source_target_pairs={{0,4},{4,0},{8,12},{12,8},{1,5},{5,1},{9,13},{13,9},{2,6},{6,2},{1... | collective-permute-start | bytes 884744 | tf_op jit(solution)/shard_map/ppermute | solution.py:339
  11.1 12.6 %collective-permute-start.4 = (bf16[1,96,1536]{2,1,0:T(8,128)(2,1)S(1)}, bf16[1,96,1536]{2,1,0:T(8,128)(2,1)S(1)}, u32[]{:S(2)}, u32[]{:S(2)}) collective-permute-start(bf16[1,96,1536]{2,1,0:T(8,128)(2,1)S(1)} %bitcast.23), channel_id=1, source_target_pairs={{0,8},{4,12},{8,0},{12,4},{1,9},{5,13},{9,1},{13,5},{2,10},{6,14},... | collective-permute-start | bytes 884744 | tf_op jit(solution)/shard_map/ppermute | solution.py:339
  17.6 7.1 %collective-permute-start.8 = (bf16[48,3072]{1,0:T(8,128)(2,1)S(1)}, bf16[48,3072]{1,0:T(8,128)(2,1)}, u32[]{:S(2)}, u32[]{:S(2)}) collective-permute-start(bf16[48,3072]{1,0:T(8,128)(2,1)S(1)} %get-tuple-element.34), channel_id=1, source_target_pairs={{0,2},{1,3},{2,0},{3,1},{4,6},{5,7},{6,4},{7,5},{8,10},{9,11},{10,... | collective-permute-start | bytes 884744 | tf_op jit(solution)/shard_map/ppermute | solution.py:339
  17.9 20.7 %copy-start = (bf16[2,96,1536]{2,1,0:T(8,128)(2,1)}, bf16[2,96,1536]{2,1,0:T(8,128)(2,1)S(1)}, u32[]{:S(2)}) copy-start(bf16[2,96,1536]{2,1,0:T(8,128)(2,1)S(1)} %pad_maximum_fusion.3.refs_1_.refs_3_) | copy-start | bytes 1769476
  17.9 14.5 %collective-permute-start.12 = (bf16[2,96,1536]{2,1,0:T(8,128)(2,1)S(1)}, bf16[2,96,1536]{2,1,0:T(8,128)(2,1)S(1)}, u32[]{:S(2)}, u32[]{:S(2)}) collective-permute-start(bf16[2,96,1536]{2,1,0:T(8,128)(2,1)S(1)} %pad_maximum_fusion.3.refs_1_.refs_3_), channel_id=1, source_target_pairs={{0,16},{16,0},{1,17},{17,1},{2,18},{18,2},{3,19},{19,3},{4,20},{20... | collective-permute-start | bytes 1769480 | tf_op jit(solution)/shard_map/ppermute | solution.py:339
  24.7 5.9 %collective-permute-start.9 = (bf16[1,96,1536]{2,1,0:T(8,128)(2,1)S(1)}, bf16[1,96,1536]{2,1,0:T(8,128)(2,1)S(1)}, u32[]{:S(2)}, u32[]{:S(2)}) collective-permute-start(bf16[1,96,1536]{2,1,0:T(8,128)(2,1)S(1)} %collective-permute-done.4), channel_id=1, source_target_pairs={{0,4},{4,0},{8,12},{12,8},{1,5},{5,1},{9,13},{13,9},{2,6},{6,2},{1... | collective-permute-start | bytes 884744 | tf_op jit(solution)/shard_map/ppermute | solution.py:339
  26.1 6.3 %collective-permute-start.10 = (bf16[1,96,1536]{2,1,0:T(8,128)(2,1)S(1)}, bf16[1,96,1536]{2,1,0:T(8,128)(2,1)S(1)}, u32[]{:S(2)}, u32[]{:S(2)}) collective-permute-start(bf16[1,96,1536]{2,1,0:T(8,128)(2,1)S(1)} %collective-permute-done.6), channel_id=1, source_target_pairs={{0,2},{2,0},{1,3},{3,1},{4,6},{6,4},{5,7},{7,5},{8,10},{10,8},{9,1... | collective-permute-start | bytes 884744 | tf_op jit(solution)/shard_map/ppermute | solution.py:339
  32.4 42.9 %copy-start.2 = (bf16[2,96,1536]{2,1,0:T(8,128)(2,1)}, bf16[2,96,1536]{2,1,0:T(8,128)(2,1)S(1)}, u32[]{:S(2)}) copy-start(bf16[2,96,1536]{2,1,0:T(8,128)(2,1)S(1)} %collective-permute-done.12.refs_3_.refs_5_) | copy-start | bytes 1769476
  32.4 6.3 %collective-permute-start = (bf16[192,1536]{1,0:T(8,128)(2,1)}, bf16[192,1536]{1,0:T(8,128)(2,1)S(1)}, u32[]{:S(2)}, u32[]{:S(2)}) collective-permute-start(bf16[192,1536]{1,0:T(8,128)(2,1)} %refs_0_.1), channel_id=1, source_target_pairs={{0,1},{1,0},{2,3},{3,2},{4,5},{5,4},{6,7},{7,6},{8,9},{9,8},{10,11... | collective-permute-start | bytes 1769480 | tf_op jit(solution)/shard_map/ppermute | solution.py:454
  35.6 4.4 %collective-permute-start.1 = (bf16[192,1536]{1,0:T(8,128)(2,1)}, bf16[192,1536]{1,0:T(8,128)(2,1)S(1)}, u32[]{:S(2)}, u32[]{:S(2)}) collective-permute-start(bf16[192,1536]{1,0:T(8,128)(2,1)} %refs_1_.1), channel_id=1, source_target_pairs={{0,1},{1,0},{2,3},{3,2},{4,5},{5,4},{6,7},{7,6},{8,9},{9,8},{10,11... | collective-permute-start | bytes 1769480 | tf_op jit(solution)/shard_map/ppermute | solution.py:454
  35.7 7.2 %collective-permute-start.13 = (bf16[2,96,1536]{2,1,0:T(8,128)(2,1)S(1)}, bf16[2,96,1536]{2,1,0:T(8,128)(2,1)S(1)}, u32[]{:S(2)}, u32[]{:S(2)}) collective-permute-start(bf16[2,96,1536]{2,1,0:T(8,128)(2,1)S(1)} %pad_maximum_fusion.3.refs_1_.refs_3_), channel_id=1, source_target_pairs={{0,1},{1,0},{2,3},{3,2},{4,5},{5,4},{6,7},{7,6},{8,9},{9,8},{10,11... | collective-permute-start | bytes 1769480 | tf_op jit(solution)/shard_map/ppermute | solution.py:339
  36.1 28.5 %collective-permute-start.5 = (bf16[192,1536]{1,0:T(8,128)(2,1)S(1)}, bf16[192,1536]{1,0:T(8,128)(2,1)S(1)}, u32[]{:S(2)}, u32[]{:S(2)}) collective-permute-start(bf16[192,1536]{1,0:T(8,128)(2,1)S(1)} %get-tuple-element.32), channel_id=1, source_target_pairs={{0,8},{8,0},{1,9},{9,1},{2,10},{10,2},{3,11},{11,3},{4,12},{12,4},... | collective-permute-start | bytes 1769480 | tf_op jit(solution)/shard_map/ppermute | solution.py:356
  38.0 27.5 %collective-permute-start.7 = (bf16[192,1536]{1,0:T(8,128)(2,1)S(1)}, bf16[192,1536]{1,0:T(8,128)(2,1)S(1)}, u32[]{:S(2)}, u32[]{:S(2)}) collective-permute-start(bf16[192,1536]{1,0:T(8,128)(2,1)S(1)} %get-tuple-element.32), channel_id=1, source_target_pairs={{0,4},{4,0},{1,5},{5,1},{2,6},{6,2},{3,7},{7,3},{8,12},{12,8},{9,1... | collective-permute-start | bytes 1769480 | tf_op jit(solution)/shard_map/ppermute | solution.py:356
  38.7 36.6 %copy-start.1 = (bf16[2,96,1536]{2,1,0:T(8,128)(2,1)}, bf16[2,96,1536]{2,1,0:T(8,128)(2,1)S(1)}, u32[]{:S(2)}) copy-start(bf16[2,96,1536]{2,1,0:T(8,128)(2,1)S(1)} %constant_dynamic-update-slice_fusion.refs_5_.refs_7_) | copy-start | bytes 1769476
  38.7 30.4 %copy-start.8 = (bf16[192,1536]{1,0:T(8,128)(2,1)}, bf16[192,1536]{1,0:T(8,128)(2,1)S(1)}, u32[]{:S(2)}) copy-start(bf16[192,1536]{1,0:T(8,128)(2,1)S(1)} %collective-permute-done.refs_2_) | copy-start | bytes 1769476
  38.7 27.0 %collective-permute-start.16 = (bf16[2,96,1536]{2,1,0:T(8,128)(2,1)S(1)}, bf16[2,96,1536]{2,1,0:T(8,128)(2,1)S(1)}, u32[]{:S(2)}, u32[]{:S(2)}) collective-permute-start(bf16[2,96,1536]{2,1,0:T(8,128)(2,1)S(1)} %constant_dynamic-update-slice_fusion.refs_5_.refs_7_), channel_id=1, source_target_pairs={{0,16},{16,0},{1,17},{17,1},{2,18},{18,2},{3,19},{19,3},{4,20},{20... | collective-permute-start | bytes 1769480 | tf_op jit(solution)/shard_map/ppermute | solution.py:339
  40.0 29.1 %copy-start.9 = (bf16[192,1536]{1,0:T(8,128)(2,1)}, bf16[192,1536]{1,0:T(8,128)(2,1)S(1)}, u32[]{:S(2)}) copy-start(bf16[192,1536]{1,0:T(8,128)(2,1)S(1)} %collective-permute-done.1.refs_3_) | copy-start | bytes 1769476
  40.0 26.0 %collective-permute-start.2 = (bf16[192,1536]{1,0:T(8,128)(2,1)}, bf16[192,1536]{1,0:T(8,128)(2,1)S(1)}, u32[]{:S(2)}, u32[]{:S(2)}) collective-permute-start(bf16[192,1536]{1,0:T(8,128)(2,1)} %refs_0_.1), channel_id=1, source_target_pairs={{1,2},{2,1},{5,6},{6,5},{9,10},{10,9},{13,14},{14,13},{17,18},{18,... | collective-permute-start | bytes 1769480 | tf_op jit(solution)/shard_map/ppermute | solution.py:456
  42.9 32.4 %copy-start.3 = (bf16[2,96,1536]{2,1,0:T(8,128)(2,1)}, bf16[2,96,1536]{2,1,0:T(8,128)(2,1)S(1)}, u32[]{:S(2)}) copy-start(bf16[2,96,1536]{2,1,0:T(8,128)(2,1)S(1)} %collective-permute-done.13.refs_2_.refs_4_) | copy-start | bytes 1769476
  42.9 23.5 %collective-permute-start.3 = (bf16[192,1536]{1,0:T(8,128)(2,1)}, bf16[192,1536]{1,0:T(8,128)(2,1)S(1)}, u32[]{:S(2)}, u32[]{:S(2)}) collective-permute-start(bf16[192,1536]{1,0:T(8,128)(2,1)} %refs_1_.1), channel_id=1, source_target_pairs={{1,2},{2,1},{5,6},{6,5},{9,10},{10,9},{13,14},{14,13},{17,18},{18,... | collective-permute-start | bytes 1769480 | tf_op jit(solution)/shard_map/ppermute | solution.py:456
  64.6 4.6 %copy-start.12 = (bf16[192,1536]{1,0:T(8,128)(2,1)}, bf16[192,1536]{1,0:T(8,128)(2,1)S(1)}, u32[]{:S(2)}) copy-start(bf16[192,1536]{1,0:T(8,128)(2,1)S(1)} %collective-permute-done.5.refs_0_) | copy-start | bytes 1769476
  64.6 3.9 %collective-permute-start.15 = (bf16[2,96,1536]{2,1,0:T(8,128)(2,1)S(1)}, bf16[2,96,1536]{2,1,0:T(8,128)(2,1)S(1)}, u32[]{:S(2)}, u32[]{:S(2)}) collective-permute-start(bf16[2,96,1536]{2,1,0:T(8,128)(2,1)S(1)} %constant_dynamic-update-slice_fusion.refs_5_.refs_7_), channel_id=1, source_target_pairs={{0,1},{1,0},{2,3},{3,2},{4,5},{5,4},{6,7},{7,6},{8,9},{9,8},{10,11... | collective-permute-start | bytes 1769480 | tf_op jit(solution)/shard_map/ppermute | solution.py:339
  65.5 3.7 %copy-start.13 = (bf16[192,1536]{1,0:T(8,128)(2,1)}, bf16[192,1536]{1,0:T(8,128)(2,1)S(1)}, u32[]{:S(2)}) copy-start(bf16[192,1536]{1,0:T(8,128)(2,1)S(1)} %collective-permute-done.7.refs_1_) | copy-start | bytes 1769476
  65.5 3.6 %collective-permute-start.14 = (bf16[2,96,1536]{2,1,0:T(8,128)(2,1)S(1)}, bf16[2,96,1536]{2,1,0:T(8,128)(2,1)S(1)}, u32[]{:S(2)}, u32[]{:S(2)}) collective-permute-start(bf16[2,96,1536]{2,1,0:T(8,128)(2,1)S(1)} %collective-permute-done.12.refs_3_.refs_5_), channel_id=1, source_target_pairs={{0,1},{1,0},{2,3},{3,2},{4,5},{5,4},{6,7},{7,6},{8,9},{9,8},{10,11... | collective-permute-start | bytes 1769480 | tf_op jit(solution)/shard_map/ppermute | solution.py:339
  65.7 9.7 %copy-start.4 = (bf16[2,96,1536]{2,1,0:T(8,128)(2,1)}, bf16[2,96,1536]{2,1,0:T(8,128)(2,1)S(1)}, u32[]{:S(2)}) copy-start(bf16[2,96,1536]{2,1,0:T(8,128)(2,1)S(1)} %collective-permute-done.16.refs_7_.refs_9_) | copy-start | bytes 1769476
  65.7 18.6 %collective-permute-start.17 = (bf16[2,96,1536]{2,1,0:T(8,128)(2,1)S(1)}, bf16[2,96,1536]{2,1,0:T(8,128)(2,1)}, u32[]{:S(2)}, u32[]{:S(2)}) collective-permute-start(bf16[2,96,1536]{2,1,0:T(8,128)(2,1)S(1)} %collective-permute-done.16.refs_7_.refs_9_), channel_id=1, source_target_pairs={{0,1},{1,0},{2,3},{3,2},{4,5},{5,4},{6,7},{7,6},{8,9},{9,8},{10,11... | collective-permute-start | bytes 1769480 | tf_op jit(solution)/shard_map/ppermute | solution.py:339
  66.0 3.2 %copy-start.10 = (bf16[192,1536]{1,0:T(8,128)(2,1)}, bf16[192,1536]{1,0:T(8,128)(2,1)S(1)}, u32[]{:S(2)}) copy-start(bf16[192,1536]{1,0:T(8,128)(2,1)S(1)} %collective-permute-done.2.refs_4_) | copy-start | bytes 1769476
  66.0 28.9 %collective-permute-start.20 = (bf16[192,1536]{1,0:T(8,128)(2,1)}, bf16[192,1536]{1,0:T(8,128)(2,1)}, u32[]{:S(2)}, u32[]{:S(2)}) collective-permute-start(bf16[192,1536]{1,0:T(8,128)(2,1)} %get-tuple-element.44), channel_id=1, source_target_pairs={{0,8},{8,0},{1,9},{9,1},{2,10},{10,2},{3,11},{11,3},{4,12},{12,4},... | collective-permute-start | bytes 1769480 | tf_op jit(solution)/shard_map/ppermute | solution.py:356
  66.4 2.7 %copy-start.11 = (bf16[192,1536]{1,0:T(8,128)(2,1)}, bf16[192,1536]{1,0:T(8,128)(2,1)S(1)}, u32[]{:S(2)}) copy-start(bf16[192,1536]{1,0:T(8,128)(2,1)S(1)} %collective-permute-done.3.refs_5_) | copy-start | bytes 1769476
  66.4 28.5 %collective-permute-start.21 = (bf16[192,1536]{1,0:T(8,128)(2,1)}, bf16[192,1536]{1,0:T(8,128)(2,1)}, u32[]{:S(2)}, u32[]{:S(2)}) collective-permute-start(bf16[192,1536]{1,0:T(8,128)(2,1)} %get-tuple-element.44), channel_id=1, source_target_pairs={{0,4},{4,0},{1,5},{5,1},{2,6},{6,2},{3,7},{7,3},{8,12},{12,8},{9,1... | collective-permute-start | bytes 1769480 | tf_op jit(solution)/shard_map/ppermute | solution.py:356
  68.5 6.9 %copy-start.5 = (bf16[2,96,1536]{2,1,0:T(8,128)(2,1)}, bf16[2,96,1536]{2,1,0:T(8,128)(2,1)S(1)}, u32[]{:S(2)}) copy-start(bf16[2,96,1536]{2,1,0:T(8,128)(2,1)S(1)} %collective-permute-done.15.refs_6_.refs_8_) | copy-start | bytes 1769476
  68.5 15.8 %collective-permute-start.19 = (bf16[48,3072]{1,0:T(8,128)(2,1)}, bf16[48,3072]{1,0:T(8,128)(2,1)S(1)}, u32[]{:S(2)}, u32[]{:S(2)}) collective-permute-start(bf16[48,3072]{1,0:T(8,128)(2,1)} %get-tuple-element.42), channel_id=1, source_target_pairs={{0,3},{1,2},{2,1},{3,0},{4,7},{5,6},{6,5},{7,4},{8,11},{9,10},{10,... | collective-permute-start | bytes 884744 | tf_op jit(solution)/shard_map/ppermute | solution.py:339
  69.2 6.1 %copy-start.6 = (bf16[2,96,1536]{2,1,0:T(8,128)(2,1)}, bf16[2,96,1536]{2,1,0:T(8,128)(2,1)S(1)}, u32[]{:S(2)}) copy-start(bf16[2,96,1536]{2,1,0:T(8,128)(2,1)S(1)} %collective-permute-done.14.refs_4_.refs_6_) | copy-start | bytes 1769476
  69.2 15.1 %collective-permute-start.18 = (bf16[48,3072]{1,0:T(8,128)(2,1)}, bf16[48,3072]{1,0:T(8,128)(2,1)}, u32[]{:S(2)}, u32[]{:S(2)}) collective-permute-start(bf16[48,3072]{1,0:T(8,128)(2,1)} %get-tuple-element.40), channel_id=1, source_target_pairs={{0,1},{1,0},{2,3},{3,2},{4,5},{5,4},{6,7},{7,6},{8,9},{9,8},{10,11... | collective-permute-start | bytes 884744 | tf_op jit(solution)/shard_map/ppermute | solution.py:339
  84.3 1.5 %copy-start.14 = (bf16[48,3072]{1,0:T(8,128)(2,1)}, bf16[48,3072]{1,0:T(8,128)(2,1)S(1)}, u32[]{:S(2)}) copy-start(bf16[48,3072]{1,0:T(8,128)(2,1)S(1)} %collective-permute-done.19.refs_12_) | copy-start | bytes 884740
Sparse Core Ops, SparseCore 0:
  32.5 53.2 all-gather.2

commit v15 on v14

--- a/solution.py
+++ b/solution.py
@@ -445,7 +445,7 @@
         control_parts[d] = swap(TILES, d)(after(control_sent[d], line))
     plane = jnp.concatenate([line, beside])
     last = swap("outer", 1)(after(far, near, *control_parts[2:-1], *chunks))
-    near_x = swap("pair", 1)(near)
+    near_x = swap("pair", 1)(after(near, beside))
     held = []
     for both in (plane, jnp.concatenate([near, near_x])):
         held += [both, swap("groups", 1)(both)]
@@ -453,7 +453,7 @@
     for i, x in enumerate((keys, values)):
         early_near[0][i] = lax.ppermute(x, TILES, early[0][2])
         for slot in range(1, len(early)):
-            early_near[slot][i] = lax.ppermute(after(x, early_near[0][i]), TILES, early[slot][2])
+            early_near[slot][i] = lax.ppermute(after(x, early_near[0][i], held[1]), TILES, early[slot][2])
     state = attend(tuple(s[:2] for s in early), pattern, queries, [keys, values] + [x for kv in early_near for x in kv])
 
     late_near = []
@@ -464,7 +464,7 @@
     for d in (1, grid_width - 1):
         control_parts[d] = swap(TILES, d)(after(control_sent[d], *[x for kv in early_near[1:] for x in kv]))
 
-    gates = [*control_parts[2:-1], near_x, held[1]]
+    gates = [*control_parts[2:-1], near_x]
     weight = [lax.all_gather(after(jnp.concatenate([far, last]), *gates), ("groups", "pair", "core"))]
     n = len(line_flips)
     moves = [

time: 110 us -> 132 us (1.20)
  waiting for transfers between devices: 39.6 us -> 57.3 us
  Pallas kernels: 22.6 us -> 25.9 us
  local copies, waits for them, and re-layouts: 3.26 us -> 5.51 us
    ppermute x14, waiting for transfers between devices: 15.5 us -> 46.2 us  [flipped(): lax.ppermute(block, axis, [(i, i ^ flip) for i in range(lax.axis_size(axi...]
    ppermute x4, waiting for transfers between devices: 22.6 us -> 4.73 us  [route_of(): return lambda block: lax.ppermute(block, TILES, route)]
    ppermute x2, waiting for transfers between devices: 0.01 us -> 6.31 us  [on_device(): lax.ppermute(after(x, early_near[0][i], held[1]), TILES, early[slot][2])]
    ppermute x4, starting transfers between devices: 4.94 us -> 0.96 us  [route_of(): return lambda block: lax.ppermute(block, TILES, route)]
    ppermute x14, starting transfers between devices: 12.9 us -> 15.6 us  [flipped(): lax.ppermute(block, axis, [(i, i ^ flip) for i in range(lax.axis_size(axi...]
    unnamed x31 -> x33, local copies, waits for them, and re-layouts: 0.08 us -> 2.36 us
    all_gather x1, waiting for transfers between devices: 1.48 us -> 0.02 us  [on_device(): lax.all_gather(after(jnp.concatenate([far, last]), *gates), ('groups', 'p...]
    pallas_call x1, Pallas kernels: 5.97 us -> 7.37 us  [attend(): pl.pallas_call(functools.partial(attend_kernel, which), out_shape=[jax.Sh...]
  transfers between devices with their start and end apart: 23 -> 23, of which waited for: 8 -> 10; matrix products, arithmetic and copies ran while one was open for 5% -> 4% of each run, Pallas kernels for 14% -> 14%
where the time goes in v15:
time: 132 us
  waiting for transfers between devices  57.3 us (43%)
  starting transfers between devices  26.1 us (20%)
  Pallas kernels  25.9 us (20%)
  between operations  13.7 us (10%)
  local copies, waits for them, and re-layouts  5.51 us (4%)
  other arithmetic  3.19 us (2%)
    ppermute x14, waiting for transfers between devices, flipped(): lax.ppermute(block, axis, [(i, i ^ flip) for i in range(lax.axis_size(axi...  46.2 us
    ppermute x14, starting transfers between devices, flipped(): lax.ppermute(block, axis, [(i, i ^ flip) for i in range(lax.axis_size(axi...  15.6 us
    pallas_call x1, Pallas kernels, finish(): pl.pallas_call(functools.partial(finish_kernel, which, len(weight), moves...  8 us
    pallas_call x1, Pallas kernels, attend(): pl.pallas_call(functools.partial(attend_kernel, which), out_shape=[jax.Sh...  7.37 us
    ppermute x2, waiting for transfers between devices, on_device(): lax.ppermute(after(x, early_near[0][i], held[1]), TILES, early[slot][2])  6.31 us
    ppermute x2, starting transfers between devices, on_device(): lax.ppermute(after(x, early_near[0][i], held[1]), TILES, early[slot][2])  6 us
    pallas_call x1, Pallas kernels, begin(): pl.pallas_call(functools.partial(begin_kernel, (len(weight), len(control)...  5.57 us
    pallas_call x1, Pallas kernels, close(): pl.pallas_call(functools.partial(close_kernel, first, which), out_shape=j...  4.94 us
  transfers between devices with their start and end apart: 23, of which 10 were waited for; matrix products, arithmetic and copies ran while one was open for 4% of the time, Pallas kernels for 14%

profile of v15, /device:TPU:1, one launch (start us, length us, event | category | flops | bytes accessed | tf_op | source)
XLA Modules:
  0.0 131.6 jit_solution(4465962431279161073)
XLA Ops:
  6.5 1.1 slice_select_fusion
  7.6 2.2 %collective-permute-start.8 = (bf16[1,96,1536]{2,1,0:T(8,128)(2,1)S(1)}, bf16[1,96,1536]{2,1,0:T(8,128)(2,1)S(1)}, u32[]{:S(2)}, u32[]{:S(2)}) collective-permute-start(bf16[1,96,1536]{2,1,0:T(8,128)(2,1)S(1)} %bitcast.21), channel_id=1, source_target_pairs={{0,4},{4,0},{8,12},{12,8},{1,5},{5,1},{9,13},{13,9},{2,6},{6,2},{1... | collective-permute-start | bytes 884744 | tf_op jit(solution)/shard_map/ppermute | solution.py:339
  9.8 2.3 %collective-permute-start.6 = (bf16[1,96,1536]{2,1,0:T(8,128)(2,1)S(1)}, bf16[1,96,1536]{2,1,0:T(8,128)(2,1)S(1)}, u32[]{:S(2)}, u32[]{:S(2)}) collective-permute-start(bf16[1,96,1536]{2,1,0:T(8,128)(2,1)S(1)} %bitcast.22), channel_id=1, source_target_pairs={{0,8},{4,12},{8,0},{12,4},{1,9},{5,13},{9,1},{13,5},{2,10},{6,14},... | collective-permute-start | bytes 884744 | tf_op jit(solution)/shard_map/ppermute | solution.py:339
  12.1 1.1 fusion
  13.2 1.1 fusion.1
  14.3 0.0 copy-start.7
  14.3 1.1 pad_maximum_fusion.1
  15.5 0.6 copy-done.7
  16.0 0.9 dynamic-slice_bitcast_fusion
  17.0 1.2 collective-permute-start.10
  18.2 0.3 collective-permute-start.2
  18.4 4.3 %collective-permute-done.8 = bf16[1,96,1536]{2,1,0:T(8,128)(2,1)S(1)} collective-permute-done((bf16[1,96,1536]{2,1,0:T(8,128)(2,1)S(1)}, bf16[1,96,1536]{2,1,0:T(8,128)(2,1)S(1)}, u32[]{:S(2)}, u32[]{:S(2)}) %collective-permute-start.8) | collective-permute-done | bytes 294944 | tf_op jit(solution)/shard_map/ppermute | solution.py:339
  22.8 1.5 %collective-permute-done.10.refs_11_ = bf16[48,3072]{1,0:T(8,128)(2,1)S(1)} collective-permute-done((bf16[48,3072]{1,0:T(8,128)(2,1)S(1)}, bf16[48,3072]{1,0:T(8,128)(2,1)S(1)}, u32[]{:S(2)}, u32[]{:S(2)}) %collective-permute-start.10) | collective-permute-done | bytes 294944 | tf_op jit(solution)/shard_map/ppermute | solution.py:339
  24.2 0.8 collective-permute-start.11
  25.1 5.5 %collective-permute-done.2 = bf16[1,96,1536]{2,1,0:T(8,128)(2,1)S(1)} collective-permute-done((bf16[1,96,1536]{2,1,0:T(8,128)(2,1)S(1)}, bf16[1,96,1536]{2,1,0:T(8,128)(2,1)S(1)}, u32[]{:S(2)}, u32[]{:S(2)}) %collective-permute-start.2) | collective-permute-done | bytes 294944 | tf_op jit(solution)/shard_map/ppermute | solution.py:339
  30.6 1.2 collective-permute-start.12
  31.8 0.0 collective-permute-done.11
  31.8 0.9 pad_maximum_fusion.3
  32.7 4.2 %collective-permute-done.12 = bf16[1,96,1536]{2,1,0:T(8,128)(2,1)S(1)} collective-permute-done((bf16[1,96,1536]{2,1,0:T(8,128)(2,1)S(1)}, bf16[1,96,1536]{2,1,0:T(8,128)(2,1)S(1)}, u32[]{:S(2)}, u32[]{:S(2)}) %collective-permute-start.12) | collective-permute-done | bytes 294944 | tf_op jit(solution)/shard_map/ppermute | solution.py:339
  36.9 0.0 all-gather.3.cloned.1.call-update
  36.9 3.1 %collective-permute-start = (bf16[192,1536]{1,0:T(8,128)(2,1)}, bf16[192,1536]{1,0:T(8,128)(2,1)S(1)}, u32[]{:S(2)}, u32[]{:S(2)}) collective-permute-start(bf16[192,1536]{1,0:T(8,128)(2,1)} %refs_0_.1), channel_id=1, source_target_pairs={{0,1},{1,0},{2,3},{3,2},{4,5},{5,4},{6,7},{7,6},{8,9},{9,8},{10,11... | collective-permute-start | bytes 1769480 | tf_op jit(solution)/shard_map/ppermute | solution.py:454
  40.1 0.1 pad_maximum_fusion.refs_1_.refs_3_
  40.2 1.3 collective-permute-start.3
  41.5 0.3 collective-permute-start.1
  41.8 0.2 collective-permute-start.13
  42.0 0.1 collective-permute-start.7
  42.0 0.8 copy-done.8
  42.9 0.2 collective-permute-start.9
  43.1 18.4 %collective-permute-done.3.refs_3_.refs_5_ = bf16[2,96,1536]{2,1,0:T(8,128)(2,1)S(1)} collective-permute-done((bf16[2,96,1536]{2,1,0:T(8,128)(2,1)S(1)}, bf16[2,96,1536]{2,1,0:T(8,128)(2,1)S(1)}, u32[]{:S(2)}, u32[]{:S(2)}) %collective-permute-start.3) | collective-permute-done | bytes 589856 | tf_op jit(solution)/shard_map/ppermute | solution.py:339
  61.5 1.2 collective-permute-start.16
  62.7 4.1 %collective-permute-start.4 = (bf16[192,1536]{1,0:T(8,128)(2,1)}, bf16[192,1536]{1,0:T(8,128)(2,1)S(1)}, u32[]{:S(2)}, u32[]{:S(2)}) collective-permute-start(bf16[192,1536]{1,0:T(8,128)(2,1)} %refs_0_.1), channel_id=1, source_target_pairs={{1,2},{2,1},{5,6},{6,5},{9,10},{10,9},{13,14},{14,13},{17,18},{18,... | collective-permute-start | bytes 1769480 | tf_op jit(solution)/shard_map/ppermute | solution.py:456
  66.8 1.9 %collective-permute-start.5 = (bf16[192,1536]{1,0:T(8,128)(2,1)}, bf16[192,1536]{1,0:T(8,128)(2,1)S(1)}, u32[]{:S(2)}, u32[]{:S(2)}) collective-permute-start(bf16[192,1536]{1,0:T(8,128)(2,1)} %refs_1_.1), channel_id=1, source_target_pairs={{1,2},{2,1},{5,6},{6,5},{9,10},{10,9},{13,14},{14,13},{17,18},{18,... | collective-permute-start | bytes 1769480 | tf_op jit(solution)/shard_map/ppermute | solution.py:456
  68.8 2.2 %collective-permute-done.7.refs_0_ = bf16[192,1536]{1,0:T(8,128)(2,1)S(1)} collective-permute-done((bf16[192,1536]{1,0:T(8,128)(2,1)}, bf16[192,1536]{1,0:T(8,128)(2,1)S(1)}, u32[]{:S(2)}, u32[]{:S(2)}) %collective-permute-start.7) | collective-permute-done | bytes 589856 | tf_op jit(solution)/shard_map/ppermute | solution.py:356
  70.9 0.5 collective-permute-start.15
  71.5 0.1 collective-permute-start.14
  71.5 12.3 %collective-permute-done.16.refs_7_.refs_9_ = bf16[2,96,1536]{2,1,0:T(8,128)(2,1)S(1)} collective-permute-done((bf16[2,96,1536]{2,1,0:T(8,128)(2,1)S(1)}, bf16[2,96,1536]{2,1,0:T(8,128)(2,1)S(1)}, u32[]{:S(2)}, u32[]{:S(2)}) %collective-permute-start.16) | collective-permute-done | bytes 589856 | tf_op jit(solution)/shard_map/ppermute | solution.py:339
  83.9 4.3 %collective-permute-start.17 = (bf16[2,96,1536]{2,1,0:T(8,128)(2,1)S(1)}, bf16[2,96,1536]{2,1,0:T(8,128)(2,1)}, u32[]{:S(2)}, u32[]{:S(2)}) collective-permute-start(bf16[2,96,1536]{2,1,0:T(8,128)(2,1)S(1)} %collective-permute-done.16.refs_7_.refs_9_), channel_id=1, source_target_pairs={{0,1},{1,0},{2,3},{3,2},{4,5},{5,4},{6,7},{7,6},{8,9},{9,8},{10,11... | collective-permute-start | bytes 1769480 | tf_op jit(solution)/shard_map/ppermute | solution.py:339
  88.1 6.3 %collective-permute-done.5.refs_5_ = bf16[192,1536]{1,0:T(8,128)(2,1)S(1)} collective-permute-done((bf16[192,1536]{1,0:T(8,128)(2,1)}, bf16[192,1536]{1,0:T(8,128)(2,1)S(1)}, u32[]{:S(2)}, u32[]{:S(2)}) %collective-permute-start.5) | collective-permute-done | bytes 589856 | tf_op jit(solution)/shard_map/ppermute | solution.py:456
  94.5 0.7 collective-permute-start.21
  95.2 0.0 copy-done.11
  95.3 0.9 copy-done.6
  96.2 7.4 %attend.1 = (f32[192,1536]{1,0:T(8,128)}, f32[192,128]{1,0:T(8,128)}) custom-call(s32[1,6]{1,0:T(1,128)} %pattern.5, bf16[192,1536]{1,0:T(8,128)(2,1)} %q.5, bf16[192,1536]{1,0:T(8,128)(2,1)} %refs_0_.1, bf16[192,1536]{1,0:T(8,128)(2,1)} %refs_1_.1, bf16[192,1536]{1,0:T(8,128)(2,1)} %copy-done.8, bf16[192,1536]{1,0:T(8,128)(2,1)} %copy-done.9, ...), custom_call_target="tpu_custom_call" | custom-call | flops 1019215872 | bytes 5308416 | tf_op jit(solution)/shard_map/attend/pallas_call | solution.py:104
  103.6 4.9 %close.1.ready = bf16[192,768]{1,0:T(8,128)(2,1)} custom-call(s32[1,6]{1,0:T(1,128)} %pattern.5, bf16[192,1536]{1,0:T(8,128)(2,1)} %q.5, f32[192,1536]{1,0:T(8,128)} %get-tuple-element.28.part, f32[192,128]{1,0:T(8,128)} %get-tuple-element.29.stats, bf16[192,1536]{1,0:T(8,128)(2,1)} %copy-done.12, bf16[192,1536]{1,0:T(8,128)(2,1)} %copy-done.13), custom_call_target="tpu_custom_call" | custom-call | flops 339738624 | bytes 2359296 | tf_op jit(solution)/shard_map/close/pallas_call | solution.py:170
  108.6 0.0 all-gather.3.cloned.1.call-done
  108.6 5.6 %begin.1.so_far = f32[192,3072]{1,0:T(8,128)} custom-call(bf16[192,3072]{1,0:T(8,128)(2,1)} %hidden.1, bf16[192,768]{1,0:T(8,128)(2,1)} %close.1.ready, bf16[8,2,96,1536]{3,2,1,0:T(8,128)(2,1)} %bitcast.19, bf16[2,96,1536]{2,1,0:T(8,128)(2,1)} %copy-done, bf16[2,96,1536]{2,1,0:T(8,128)(2,1)} %copy-done.3, bf16[2,96,1536]{2,1,0:T(8,128)(2,1)} %copy-done.2, ...), custom_call_target="tpu_custom_call" | custom-call | flops 905969664 | bytes 9437184 | tf_op jit(solution)/shard_map/begin/pallas_call | solution.py:300
  114.2 2.2 %collective-permute-done.20.refs_0_ = bf16[192,1536]{1,0:T(8,128)(2,1)} collective-permute-done((bf16[192,1536]{1,0:T(8,128)(2,1)}, bf16[192,1536]{1,0:T(8,128)(2,1)}, u32[]{:S(2)}, u32[]{:S(2)}) %collective-permute-start.20) | collective-permute-done | bytes 589856 | tf_op jit(solution)/shard_map/ppermute | solution.py:356
  116.4 0.4 collective-permute-done.21.refs_1_
  116.8 8.0 %finish.1 = bf16[192,3072]{1,0:T(8,128)(2,1)} custom-call(s32[1,6]{1,0:T(1,128)} %pattern.5, bf16[192,1536]{1,0:T(8,128)(2,1)} %q.5, f32[192,1536]{1,0:T(8,128)} %get-tuple-element.28.part, f32[192,128]{1,0:T(8,128)} %get-tuple-element.29.stats, f32[192,3072]{1,0:T(8,128)} %begin.1.so_far, bf16[192,1536]{1,0:T(8,128)(2,1)} %collective-permute-done.20.refs_0_, ...), custom_call_target="tpu_custom_call" | custom-call | flops 905969664 | bytes 8257536 | tf_op jit(solution)/shard_map/finish/pallas_call | solution.py:321
  (44 shorter events, 0.1 us)
Async XLA Ops:
  6.5 102.1 %all-gather.3.cloned.1.call-start = ((), (), s32[]{:S(2)}) async-start(), calls=%async_computation | async-start | bytes 5308416 | tf_op jit(solution)/shard_map/all_gather | solution.py:468
  7.6 15.1 %collective-permute-start.8 = (bf16[1,96,1536]{2,1,0:T(8,128)(2,1)S(1)}, bf16[1,96,1536]{2,1,0:T(8,128)(2,1)S(1)}, u32[]{:S(2)}, u32[]{:S(2)}) collective-permute-start(bf16[1,96,1536]{2,1,0:T(8,128)(2,1)S(1)} %bitcast.21), channel_id=1, source_target_pairs={{0,4},{4,0},{8,12},{12,8},{1,5},{5,1},{9,13},{13,9},{2,6},{6,2},{1... | collective-permute-start | bytes 884744 | tf_op jit(solution)/shard_map/ppermute | solution.py:339
  9.8 12.9 %collective-permute-start.6 = (bf16[1,96,1536]{2,1,0:T(8,128)(2,1)S(1)}, bf16[1,96,1536]{2,1,0:T(8,128)(2,1)S(1)}, u32[]{:S(2)}, u32[]{:S(2)}) collective-permute-start(bf16[1,96,1536]{2,1,0:T(8,128)(2,1)S(1)} %bitcast.22), channel_id=1, source_target_pairs={{0,8},{4,12},{8,0},{12,4},{1,9},{5,13},{9,1},{13,5},{2,10},{6,14},... | collective-permute-start | bytes 884744 | tf_op jit(solution)/shard_map/ppermute | solution.py:339
  14.3 1.7 %copy-start.7 = (bf16[192,3072]{1,0:T(8,128)(2,1)S(1)}, bf16[192,3072]{1,0:T(8,128)(2,1)}, u32[]{:S(2)}) copy-start(bf16[192,3072]{1,0:T(8,128)(2,1)} %param.11) | copy-start | bytes 3538948
  17.0 7.3 %collective-permute-start.10 = (bf16[48,3072]{1,0:T(8,128)(2,1)S(1)}, bf16[48,3072]{1,0:T(8,128)(2,1)S(1)}, u32[]{:S(2)}, u32[]{:S(2)}) collective-permute-start(bf16[48,3072]{1,0:T(8,128)(2,1)S(1)} %get-tuple-element.35), channel_id=1, source_target_pairs={{0,2},{1,3},{2,0},{3,1},{4,6},{5,7},{6,4},{7,5},{8,10},{9,11},{10,... | collective-permute-start | bytes 884744 | tf_op jit(solution)/shard_map/ppermute | solution.py:339
  18.2 12.4 %collective-permute-start.2 = (bf16[1,96,1536]{2,1,0:T(8,128)(2,1)S(1)}, bf16[1,96,1536]{2,1,0:T(8,128)(2,1)S(1)}, u32[]{:S(2)}, u32[]{:S(2)}) collective-permute-start(bf16[1,96,1536]{2,1,0:T(8,128)(2,1)S(1)} %bitcast.23), channel_id=1, source_target_pairs={{0,2},{2,0},{1,3},{3,1},{4,6},{6,4},{5,7},{7,5},{8,10},{10,8},{9,1... | collective-permute-start | bytes 884744 | tf_op jit(solution)/shard_map/ppermute | solution.py:339
  24.2 6.3 %copy-start.15 = (bf16[48,3072]{1,0:T(8,128)(2,1)}, bf16[48,3072]{1,0:T(8,128)(2,1)S(1)}, u32[]{:S(2)}) copy-start(bf16[48,3072]{1,0:T(8,128)(2,1)S(1)} %collective-permute-done.10.refs_11_) | copy-start | bytes 884740
  24.2 7.5 %collective-permute-start.11 = (bf16[1,96,1536]{2,1,0:T(8,128)(2,1)S(1)}, bf16[1,96,1536]{2,1,0:T(8,128)(2,1)S(1)}, u32[]{:S(2)}, u32[]{:S(2)}) collective-permute-start(bf16[1,96,1536]{2,1,0:T(8,128)(2,1)S(1)} %collective-permute-done.6), channel_id=1, source_target_pairs={{0,4},{4,0},{8,12},{12,8},{1,5},{5,1},{9,13},{13,9},{2,6},{6,2},{1... | collective-permute-start | bytes 884744 | tf_op jit(solution)/shard_map/ppermute | solution.py:339
  30.6 6.3 %collective-permute-start.12 = (bf16[1,96,1536]{2,1,0:T(8,128)(2,1)S(1)}, bf16[1,96,1536]{2,1,0:T(8,128)(2,1)S(1)}, u32[]{:S(2)}, u32[]{:S(2)}) collective-permute-start(bf16[1,96,1536]{2,1,0:T(8,128)(2,1)S(1)} %collective-permute-done.8), channel_id=1, source_target_pairs={{0,2},{2,0},{1,3},{3,1},{4,6},{6,4},{5,7},{7,5},{8,10},{10,8},{9,1... | collective-permute-start | bytes 884744 | tf_op jit(solution)/shard_map/ppermute | solution.py:339
  36.9 59.2 %copy-start.14 = (bf16[48,3072]{1,0:T(8,128)(2,1)S(1)}, bf16[48,3072]{1,0:T(8,128)(2,1)}, u32[]{:S(2)}) copy-start(bf16[48,3072]{1,0:T(8,128)(2,1)} %get-tuple-element.42) | copy-start | bytes 884740
  36.9 5.1 %collective-permute-start = (bf16[192,1536]{1,0:T(8,128)(2,1)}, bf16[192,1536]{1,0:T(8,128)(2,1)S(1)}, u32[]{:S(2)}, u32[]{:S(2)}) collective-permute-start(bf16[192,1536]{1,0:T(8,128)(2,1)} %refs_0_.1), channel_id=1, source_target_pairs={{0,1},{1,0},{2,3},{3,2},{4,5},{5,4},{6,7},{7,6},{8,9},{9,8},{10,11... | collective-permute-start | bytes 1769480 | tf_op jit(solution)/shard_map/ppermute | solution.py:454
  40.2 63.4 %copy-start = (bf16[2,96,1536]{2,1,0:T(8,128)(2,1)}, bf16[2,96,1536]{2,1,0:T(8,128)(2,1)S(1)}, u32[]{:S(2)}) copy-start(bf16[2,96,1536]{2,1,0:T(8,128)(2,1)S(1)} %pad_maximum_fusion.refs_1_.refs_3_) | copy-start | bytes 1769476
  40.2 21.3 %collective-permute-start.3 = (bf16[2,96,1536]{2,1,0:T(8,128)(2,1)S(1)}, bf16[2,96,1536]{2,1,0:T(8,128)(2,1)S(1)}, u32[]{:S(2)}, u32[]{:S(2)}) collective-permute-start(bf16[2,96,1536]{2,1,0:T(8,128)(2,1)S(1)} %pad_maximum_fusion.refs_1_.refs_3_), channel_id=1, source_target_pairs={{0,16},{16,0},{1,17},{17,1},{2,18},{18,2},{3,19},{19,3},{4,20},{20... | collective-permute-start | bytes 1769480 | tf_op jit(solution)/shard_map/ppermute | solution.py:339
  41.5 21.3 %collective-permute-start.1 = (bf16[192,1536]{1,0:T(8,128)(2,1)}, bf16[192,1536]{1,0:T(8,128)(2,1)S(1)}, u32[]{:S(2)}, u32[]{:S(2)}) collective-permute-start(bf16[192,1536]{1,0:T(8,128)(2,1)} %refs_1_.1), channel_id=1, source_target_pairs={{0,1},{1,0},{2,3},{3,2},{4,5},{5,4},{6,7},{7,6},{8,9},{9,8},{10,11... | collective-permute-start | bytes 1769480 | tf_op jit(solution)/shard_map/ppermute | solution.py:454
  41.8 25.1 %collective-permute-start.13 = (bf16[2,96,1536]{2,1,0:T(8,128)(2,1)S(1)}, bf16[2,96,1536]{2,1,0:T(8,128)(2,1)S(1)}, u32[]{:S(2)}, u32[]{:S(2)}) collective-permute-start(bf16[2,96,1536]{2,1,0:T(8,128)(2,1)S(1)} %pad_maximum_fusion.refs_1_.refs_3_), channel_id=1, source_target_pairs={{0,1},{1,0},{2,3},{3,2},{4,5},{5,4},{6,7},{7,6},{8,9},{9,8},{10,11... | collective-permute-start | bytes 1769480 | tf_op jit(solution)/shard_map/ppermute | solution.py:339
  42.0 28.9 %collective-permute-start.7 = (bf16[192,1536]{1,0:T(8,128)(2,1)}, bf16[192,1536]{1,0:T(8,128)(2,1)S(1)}, u32[]{:S(2)}, u32[]{:S(2)}) collective-permute-start(bf16[192,1536]{1,0:T(8,128)(2,1)} %get-tuple-element.33), channel_id=1, source_target_pairs={{0,8},{8,0},{1,9},{9,1},{2,10},{10,2},{3,11},{11,3},{4,12},{12,4},... | collective-permute-start | bytes 1769480 | tf_op jit(solution)/shard_map/ppermute | solution.py:356
  42.0 0.8 copy-start.8
  42.9 28.6 %collective-permute-start.9 = (bf16[192,1536]{1,0:T(8,128)(2,1)}, bf16[192,1536]{1,0:T(8,128)(2,1)S(1)}, u32[]{:S(2)}, u32[]{:S(2)}) collective-permute-start(bf16[192,1536]{1,0:T(8,128)(2,1)} %get-tuple-element.33), channel_id=1, source_target_pairs={{0,4},{4,0},{1,5},{5,1},{2,6},{6,2},{3,7},{7,3},{8,12},{12,8},{9,1... | collective-permute-start | bytes 1769480 | tf_op jit(solution)/shard_map/ppermute | solution.py:356
  43.1 60.5 %copy-start.1 = (bf16[2,96,1536]{2,1,0:T(8,128)(2,1)}, bf16[2,96,1536]{2,1,0:T(8,128)(2,1)S(1)}, u32[]{:S(2)}) copy-start(bf16[2,96,1536]{2,1,0:T(8,128)(2,1)S(1)} %constant_dynamic-update-slice_fusion.refs_5_.refs_7_) | copy-start | bytes 1769476
  61.5 42.1 %copy-start.2 = (bf16[2,96,1536]{2,1,0:T(8,128)(2,1)}, bf16[2,96,1536]{2,1,0:T(8,128)(2,1)S(1)}, u32[]{:S(2)}) copy-start(bf16[2,96,1536]{2,1,0:T(8,128)(2,1)S(1)} %collective-permute-done.3.refs_3_.refs_5_) | copy-start | bytes 1769476
  61.5 22.4 %collective-permute-start.16 = (bf16[2,96,1536]{2,1,0:T(8,128)(2,1)S(1)}, bf16[2,96,1536]{2,1,0:T(8,128)(2,1)S(1)}, u32[]{:S(2)}, u32[]{:S(2)}) collective-permute-start(bf16[2,96,1536]{2,1,0:T(8,128)(2,1)S(1)} %constant_dynamic-update-slice_fusion.refs_5_.refs_7_), channel_id=1, source_target_pairs={{0,16},{16,0},{1,17},{17,1},{2,18},{18,2},{3,19},{19,3},{4,20},{20... | collective-permute-start | bytes 1769480 | tf_op jit(solution)/shard_map/ppermute | solution.py:339
  62.7 32.5 %copy-start.9 = (bf16[192,1536]{1,0:T(8,128)(2,1)}, bf16[192,1536]{1,0:T(8,128)(2,1)S(1)}, u32[]{:S(2)}) copy-start(bf16[192,1536]{1,0:T(8,128)(2,1)S(1)} %collective-permute-done.1.refs_3_) | copy-start | bytes 1769476
  62.7 25.4 %collective-permute-start.4 = (bf16[192,1536]{1,0:T(8,128)(2,1)}, bf16[192,1536]{1,0:T(8,128)(2,1)S(1)}, u32[]{:S(2)}, u32[]{:S(2)}) collective-permute-start(bf16[192,1536]{1,0:T(8,128)(2,1)} %refs_0_.1), channel_id=1, source_target_pairs={{1,2},{2,1},{5,6},{6,5},{9,10},{10,9},{13,14},{14,13},{17,18},{18,... | collective-permute-start | bytes 1769480 | tf_op jit(solution)/shard_map/ppermute | solution.py:456
  66.8 36.8 %copy-start.3 = (bf16[2,96,1536]{2,1,0:T(8,128)(2,1)}, bf16[2,96,1536]{2,1,0:T(8,128)(2,1)S(1)}, u32[]{:S(2)}) copy-start(bf16[2,96,1536]{2,1,0:T(8,128)(2,1)S(1)} %collective-permute-done.13.refs_2_.refs_4_) | copy-start | bytes 1769476
  66.8 27.6 %collective-permute-start.5 = (bf16[192,1536]{1,0:T(8,128)(2,1)}, bf16[192,1536]{1,0:T(8,128)(2,1)S(1)}, u32[]{:S(2)}, u32[]{:S(2)}) collective-permute-start(bf16[192,1536]{1,0:T(8,128)(2,1)} %refs_1_.1), channel_id=1, source_target_pairs={{1,2},{2,1},{5,6},{6,5},{9,10},{10,9},{13,14},{14,13},{17,18},{18,... | collective-permute-start | bytes 1769480 | tf_op jit(solution)/shard_map/ppermute | solution.py:456
  70.9 24.3 %copy-start.12 = (bf16[192,1536]{1,0:T(8,128)(2,1)}, bf16[192,1536]{1,0:T(8,128)(2,1)S(1)}, u32[]{:S(2)}) copy-start(bf16[192,1536]{1,0:T(8,128)(2,1)S(1)} %collective-permute-done.7.refs_0_) | copy-start | bytes 1769476
  70.9 24.3 %collective-permute-start.15 = (bf16[2,96,1536]{2,1,0:T(8,128)(2,1)S(1)}, bf16[2,96,1536]{2,1,0:T(8,128)(2,1)S(1)}, u32[]{:S(2)}, u32[]{:S(2)}) collective-permute-start(bf16[2,96,1536]{2,1,0:T(8,128)(2,1)S(1)} %constant_dynamic-update-slice_fusion.refs_5_.refs_7_), channel_id=1, source_target_pairs={{0,1},{1,0},{2,3},{3,2},{4,5},{5,4},{6,7},{7,6},{8,9},{9,8},{10,11... | collective-permute-start | bytes 1769480 | tf_op jit(solution)/shard_map/ppermute | solution.py:339
  71.5 23.8 %copy-start.13 = (bf16[192,1536]{1,0:T(8,128)(2,1)}, bf16[192,1536]{1,0:T(8,128)(2,1)S(1)}, u32[]{:S(2)}) copy-start(bf16[192,1536]{1,0:T(8,128)(2,1)S(1)} %collective-permute-done.9.refs_1_) | copy-start | bytes 1769476
  71.5 23.7 %collective-permute-start.14 = (bf16[2,96,1536]{2,1,0:T(8,128)(2,1)S(1)}, bf16[2,96,1536]{2,1,0:T(8,128)(2,1)S(1)}, u32[]{:S(2)}, u32[]{:S(2)}) collective-permute-start(bf16[2,96,1536]{2,1,0:T(8,128)(2,1)S(1)} %collective-permute-done.3.refs_3_.refs_5_), channel_id=1, source_target_pairs={{0,1},{1,0},{2,3},{3,2},{4,5},{5,4},{6,7},{7,6},{8,9},{9,8},{10,11... | collective-permute-start | bytes 1769480 | tf_op jit(solution)/shard_map/ppermute | solution.py:339
  83.9 19.7 %copy-start.4 = (bf16[2,96,1536]{2,1,0:T(8,128)(2,1)}, bf16[2,96,1536]{2,1,0:T(8,128)(2,1)S(1)}, u32[]{:S(2)}) copy-start(bf16[2,96,1536]{2,1,0:T(8,128)(2,1)S(1)} %collective-permute-done.16.refs_7_.refs_9_) | copy-start | bytes 1769476
  83.9 24.7 %collective-permute-start.17 = (bf16[2,96,1536]{2,1,0:T(8,128)(2,1)S(1)}, bf16[2,96,1536]{2,1,0:T(8,128)(2,1)}, u32[]{:S(2)}, u32[]{:S(2)}) collective-permute-start(bf16[2,96,1536]{2,1,0:T(8,128)(2,1)S(1)} %collective-permute-done.16.refs_7_.refs_9_), channel_id=1, source_target_pairs={{0,1},{1,0},{2,3},{3,2},{4,5},{5,4},{6,7},{7,6},{8,9},{9,8},{10,11... | collective-permute-start | bytes 1769480 | tf_op jit(solution)/shard_map/ppermute | solution.py:339
  88.1 7.1 %copy-start.10 = (bf16[192,1536]{1,0:T(8,128)(2,1)}, bf16[192,1536]{1,0:T(8,128)(2,1)S(1)}, u32[]{:S(2)}) copy-start(bf16[192,1536]{1,0:T(8,128)(2,1)S(1)} %collective-permute-done.4.refs_4_) | copy-start | bytes 1769476
  88.1 28.2 %collective-permute-start.20 = (bf16[192,1536]{1,0:T(8,128)(2,1)}, bf16[192,1536]{1,0:T(8,128)(2,1)}, u32[]{:S(2)}, u32[]{:S(2)}) collective-permute-start(bf16[192,1536]{1,0:T(8,128)(2,1)} %get-tuple-element.46), channel_id=1, source_target_pairs={{0,8},{8,0},{1,9},{9,1},{2,10},{10,2},{3,11},{11,3},{4,12},{12,4},... | collective-permute-start | bytes 1769480 | tf_op jit(solution)/shard_map/ppermute | solution.py:356
  94.5 0.8 copy-start.11
  94.5 22.3 %collective-permute-start.21 = (bf16[192,1536]{1,0:T(8,128)(2,1)}, bf16[192,1536]{1,0:T(8,128)(2,1)}, u32[]{:S(2)}, u32[]{:S(2)}) collective-permute-start(bf16[192,1536]{1,0:T(8,128)(2,1)} %get-tuple-element.46), channel_id=1, source_target_pairs={{0,4},{4,0},{1,5},{5,1},{2,6},{6,2},{3,7},{7,3},{8,12},{12,8},{9,1... | collective-permute-start | bytes 1769480 | tf_op jit(solution)/shard_map/ppermute | solution.py:356
  95.2 8.4 %copy-start.5 = (bf16[2,96,1536]{2,1,0:T(8,128)(2,1)}, bf16[2,96,1536]{2,1,0:T(8,128)(2,1)S(1)}, u32[]{:S(2)}) copy-start(bf16[2,96,1536]{2,1,0:T(8,128)(2,1)S(1)} %collective-permute-done.15.refs_6_.refs_8_) | copy-start | bytes 1769476
  95.2 13.4 %collective-permute-start.19 = (bf16[48,3072]{1,0:T(8,128)(2,1)}, bf16[48,3072]{1,0:T(8,128)(2,1)}, u32[]{:S(2)}, u32[]{:S(2)}) collective-permute-start(bf16[48,3072]{1,0:T(8,128)(2,1)} %get-tuple-element.44), channel_id=1, source_target_pairs={{0,3},{1,2},{2,1},{3,0},{4,7},{5,6},{6,5},{7,4},{8,11},{9,10},{10,... | collective-permute-start | bytes 884744 | tf_op jit(solution)/shard_map/ppermute | solution.py:339
  95.3 0.9 copy-start.6
  96.2 12.4 %collective-permute-start.18 = (bf16[48,3072]{1,0:T(8,128)(2,1)S(1)}, bf16[48,3072]{1,0:T(8,128)(2,1)}, u32[]{:S(2)}, u32[]{:S(2)}) collective-permute-start(bf16[48,3072]{1,0:T(8,128)(2,1)S(1)} %copy-done.14), channel_id=1, source_target_pairs={{0,1},{1,0},{2,3},{3,2},{4,5},{5,4},{6,7},{7,6},{8,9},{9,8},{10,11... | collective-permute-start | bytes 884744 | tf_op jit(solution)/shard_map/ppermute | solution.py:339
Sparse Core Ops, SparseCore 0:
  37.1 54.2 all-gather.2

commit v16 on v14

--- a/solution.py
+++ b/solution.py
@@ -133,24 +133,33 @@
 
 
 def close_heads(copies, first, active, q_v, near_v, state, stats_v, out):
-    columns = state[0].shape[1]
-    for copy in copies[:3]:
+    part_v = state[0]
+    columns = part_v.shape[1]
+    for copy in copies:
         copy.wait()
     stats_now = stats_v[...]
     for h in range(columns // HEAD_DIM):
-        for r, lane in zip(state[1:], (first + h, HEAD_DIM // 2 + first + h)):
-            r[:, columns_of(h)] = jnp.broadcast_to(stats_now[:, lane : lane + 1], stats_now.shape)
-    for slot, kv in enumerate(near_v):
-        copies[3 + slot].wait()
-        fold(state, active[slot], q_v, kv.at[:, pl.ds(0, columns)], kv.at[:, pl.ds(columns, columns)])
-    out[...] = (state[0][...] / state[1][...]).astype(jnp.bfloat16)
+        at = columns_of(h)
+        total, peak = (
+            jnp.broadcast_to(stats_now[:, lane : lane + 1], stats_now.shape)
+            for lane in (first + h, HEAD_DIM // 2 + first + h)
+        )
+        terms = [(part_v[:, at], total, peak)]
+        for slot, kv in enumerate(near_v):
+            part, total, peak = head_part(q_v[:, at], kv[:, at], kv[:, pl.ds(columns + h * HEAD_DIM, HEAD_DIM)])
+            terms.append((part, total, jnp.where(active[slot], peak, -1e30)))
+        top = functools.reduce(jnp.maximum, [peak for _, _, peak in terms])
+        factors = [jnp.exp2((peak - top) * SCALE) for _, _, peak in terms]
+        numerator = sum(f * part for f, (part, _, _) in zip(factors, terms))
+        denominator = sum(f * total for f, (_, total, _) in zip(factors, terms))
+        out[:, at] = (numerator / denominator).astype(jnp.bfloat16)
 
 
 def close_scratch(rows, columns, slots):
     return (
         [pltpu.VMEM((rows, columns), jnp.bfloat16)]
         + [pltpu.VMEM((rows, 2 * columns), jnp.bfloat16)] * slots
-        + [pltpu.VMEM((rows, columns), jnp.float32)] * 3
+        + [pltpu.VMEM((rows, columns), jnp.float32)]
         + [pltpu.VMEM((rows, HEAD_DIM), jnp.float32), pltpu.SemaphoreType.DMA((4 + slots,))]
     )
 

time: 110 us -> 110 us (level)
  Pallas kernels: 22.6 us -> 25 us
  waiting for transfers between devices: 39.6 us -> 37.7 us
    ppermute x14, waiting for transfers between devices: 15.5 us -> 13.6 us  [flipped(): lax.ppermute(block, axis, [(i, i ^ flip) for i in range(lax.axis_size(axi...]
    pallas_call x1, Pallas kernels: 5.97 us -> 7.39 us  [attend(): pl.pallas_call(functools.partial(attend_kernel, which), out_shape=[jax.Sh...]
  transfers between devices with their start and end apart: 23 -> 23, of which waited for: 8 -> 8; matrix products, arithmetic and copies ran while one was open for 5% -> 5% of each run, Pallas kernels for 14% -> 16%
where the time goes in v16:
time: 110 us; the launch traced here: 109 us
  waiting for transfers between devices  37.7 us (34%)
  starting transfers between devices  26.6 us (24%)
  Pallas kernels  25 us (23%)
  between operations  13.7 us (12%)
  local copies, waits for them, and re-layouts  3.26 us (3%)
  other arithmetic  3.09 us (3%)
    ppermute x4, waiting for transfers between devices, route_of(): return lambda block: lax.ppermute(block, TILES, route)  22.6 us
    ppermute x14, waiting for transfers between devices, flipped(): lax.ppermute(block, axis, [(i, i ^ flip) for i in range(lax.axis_size(axi...  13.6 us
    ppermute x14, starting transfers between devices, flipped(): lax.ppermute(block, axis, [(i, i ^ flip) for i in range(lax.axis_size(axi...  12.9 us
    pallas_call x1, Pallas kernels, finish(): pl.pallas_call(functools.partial(finish_kernel, which, len(weight), moves...  7.57 us
    pallas_call x1, Pallas kernels, attend(): pl.pallas_call(functools.partial(attend_kernel, which), out_shape=[jax.Sh...  7.39 us
    ppermute x2, starting transfers between devices, on_device(): lax.ppermute(after(x, early_near[0][i]), TILES, early[slot][2])  5.56 us
    pallas_call x1, Pallas kernels, begin(): pl.pallas_call(functools.partial(begin_kernel, (len(weight), len(control)...  5.53 us
    ppermute x4, starting transfers between devices, route_of(): return lambda block: lax.ppermute(block, TILES, route)  4.94 us
  transfers between devices with their start and end apart: 23, of which 8 were waited for; matrix products, arithmetic and copies ran while one was open for 5% of the time, Pallas kernels for 16%

profile of v16, /device:TPU:1, one launch (start us, length us, event | category | flops | bytes accessed | tf_op | source)
XLA Modules:
  0.0 109.4 jit_solution(14391061484133002858)
XLA Ops:
  6.5 1.2 %slice_select_fusion = bf16[96,1536]{1,0:T(8,128)(2,1)S(1)} fusion(bf16[96,3072]{1,0:T(8,128)(2,1)} %param.12, pred[]{:T(512)S(6)} %eq.3), kind=kLoop, calls=%fused_computation.8 | loop fusion | flops 147456 | bytes 884737 | tf_op jit(solution)/shard_map/jit(_where)/select_n | solution.py:429
  7.7 2.1 %collective-permute-start.11 = (bf16[1,96,1536]{2,1,0:T(8,128)(2,1)S(1)}, bf16[1,96,1536]{2,1,0:T(8,128)(2,1)S(1)}, u32[]{:S(2)}, u32[]{:S(2)}) collective-permute-start(bf16[1,96,1536]{2,1,0:T(8,128)(2,1)S(1)} %bitcast.21), channel_id=1, source_target_pairs={{0,2},{2,0},{1,3},{3,1},{4,6},{6,4},{5,7},{7,5},{8,10},{10,8},{9,1... | collective-permute-start | bytes 884744 | tf_op jit(solution)/shard_map/ppermute | solution.py:348
  9.8 1.3 %collective-permute-start.6 = (bf16[1,96,1536]{2,1,0:T(8,128)(2,1)S(1)}, bf16[1,96,1536]{2,1,0:T(8,128)(2,1)S(1)}, u32[]{:S(2)}, u32[]{:S(2)}) collective-permute-start(bf16[1,96,1536]{2,1,0:T(8,128)(2,1)S(1)} %bitcast.22), channel_id=1, source_target_pairs={{0,4},{4,0},{8,12},{12,8},{1,5},{5,1},{9,13},{13,9},{2,6},{6,2},{1... | collective-permute-start | bytes 884744 | tf_op jit(solution)/shard_map/ppermute | solution.py:348
  11.1 2.3 %collective-permute-start.4 = (bf16[1,96,1536]{2,1,0:T(8,128)(2,1)S(1)}, bf16[1,96,1536]{2,1,0:T(8,128)(2,1)S(1)}, u32[]{:S(2)}, u32[]{:S(2)}) collective-permute-start(bf16[1,96,1536]{2,1,0:T(8,128)(2,1)S(1)} %bitcast.23), channel_id=1, source_target_pairs={{0,8},{4,12},{8,0},{12,4},{1,9},{5,13},{9,1},{13,5},{2,10},{6,14},... | collective-permute-start | bytes 884744 | tf_op jit(solution)/shard_map/ppermute | solution.py:348
  13.4 1.1 fusion
  14.6 1.0 dynamic-slice_bitcast_fusion
  15.5 1.1 fusion.1
  16.6 1.0 pad_maximum_fusion
  17.6 0.3 collective-permute-start.8
  17.8 0.0 collective-permute-done.11
  17.8 0.1 pad_maximum_fusion.3.refs_1_.refs_3_
  17.9 1.3 %collective-permute-start.12 = (bf16[2,96,1536]{2,1,0:T(8,128)(2,1)S(1)}, bf16[2,96,1536]{2,1,0:T(8,128)(2,1)S(1)}, u32[]{:S(2)}, u32[]{:S(2)}) collective-permute-start(bf16[2,96,1536]{2,1,0:T(8,128)(2,1)S(1)} %pad_maximum_fusion.3.refs_1_.refs_3_), channel_id=1, source_target_pairs={{0,16},{16,0},{1,17},{17,1},{2,18},{18,2},{3,19},{19,3},{4,20},{20... | collective-permute-start | bytes 1769480 | tf_op jit(solution)/shard_map/ppermute | solution.py:348
  19.2 4.5 %collective-permute-done.6 = bf16[1,96,1536]{2,1,0:T(8,128)(2,1)S(1)} collective-permute-done((bf16[1,96,1536]{2,1,0:T(8,128)(2,1)S(1)}, bf16[1,96,1536]{2,1,0:T(8,128)(2,1)S(1)}, u32[]{:S(2)}, u32[]{:S(2)}) %collective-permute-start.6) | collective-permute-done | bytes 294944 | tf_op jit(solution)/shard_map/ppermute | solution.py:348
  23.7 1.0 collective-permute-done.8.refs_11_
  24.7 1.4 %collective-permute-start.9 = (bf16[1,96,1536]{2,1,0:T(8,128)(2,1)S(1)}, bf16[1,96,1536]{2,1,0:T(8,128)(2,1)S(1)}, u32[]{:S(2)}, u32[]{:S(2)}) collective-permute-start(bf16[1,96,1536]{2,1,0:T(8,128)(2,1)S(1)} %collective-permute-done.4), channel_id=1, source_target_pairs={{0,4},{4,0},{8,12},{12,8},{1,5},{5,1},{9,13},{13,9},{2,6},{6,2},{1... | collective-permute-start | bytes 884744 | tf_op jit(solution)/shard_map/ppermute | solution.py:348
  26.1 0.3 collective-permute-start.10
  26.3 4.3 %collective-permute-done.9 = bf16[1,96,1536]{2,1,0:T(8,128)(2,1)S(1)} collective-permute-done((bf16[1,96,1536]{2,1,0:T(8,128)(2,1)S(1)}, bf16[1,96,1536]{2,1,0:T(8,128)(2,1)S(1)}, u32[]{:S(2)}, u32[]{:S(2)}) %collective-permute-start.9) | collective-permute-done | bytes 294944 | tf_op jit(solution)/shard_map/ppermute | solution.py:348
  30.6 0.9 pad_maximum_fusion.2
  31.5 0.9 collective-permute-done.10
  32.4 0.0 all-gather.3.cloned.1.call-update
  32.4 3.2 %collective-permute-start = (bf16[192,1536]{1,0:T(8,128)(2,1)}, bf16[192,1536]{1,0:T(8,128)(2,1)S(1)}, u32[]{:S(2)}, u32[]{:S(2)}) collective-permute-start(bf16[192,1536]{1,0:T(8,128)(2,1)} %refs_0_.1), channel_id=1, source_target_pairs={{0,1},{1,0},{2,3},{3,2},{4,5},{5,4},{6,7},{7,6},{8,9},{9,8},{10,11... | collective-permute-start | bytes 1769480 | tf_op jit(solution)/shard_map/ppermute | solution.py:463
  35.6 0.1 collective-permute-start.1
  35.7 0.4 collective-permute-start.13
  36.1 1.9 %collective-permute-start.5 = (bf16[192,1536]{1,0:T(8,128)(2,1)S(1)}, bf16[192,1536]{1,0:T(8,128)(2,1)S(1)}, u32[]{:S(2)}, u32[]{:S(2)}) collective-permute-start(bf16[192,1536]{1,0:T(8,128)(2,1)S(1)} %get-tuple-element.32), channel_id=1, source_target_pairs={{0,8},{8,0},{1,9},{9,1},{2,10},{10,2},{3,11},{11,3},{4,12},{12,4},... | collective-permute-start | bytes 1769480 | tf_op jit(solution)/shard_map/ppermute | solution.py:365
  38.0 0.6 collective-permute-start.7
  38.7 0.0 collective-permute-done.refs_2_
  38.7 0.0 copy-start.8
  38.7 1.3 %collective-permute-start.16 = (bf16[2,96,1536]{2,1,0:T(8,128)(2,1)S(1)}, bf16[2,96,1536]{2,1,0:T(8,128)(2,1)S(1)}, u32[]{:S(2)}, u32[]{:S(2)}) collective-permute-start(bf16[2,96,1536]{2,1,0:T(8,128)(2,1)S(1)} %constant_dynamic-update-slice_fusion.refs_5_.refs_7_), channel_id=1, source_target_pairs={{0,16},{16,0},{1,17},{17,1},{2,18},{18,2},{3,19},{19,3},{4,20},{20... | collective-permute-start | bytes 1769480 | tf_op jit(solution)/shard_map/ppermute | solution.py:348
  40.0 2.9 %collective-permute-start.2 = (bf16[192,1536]{1,0:T(8,128)(2,1)}, bf16[192,1536]{1,0:T(8,128)(2,1)S(1)}, u32[]{:S(2)}, u32[]{:S(2)}) collective-permute-start(bf16[192,1536]{1,0:T(8,128)(2,1)} %refs_0_.1), channel_id=1, source_target_pairs={{1,2},{2,1},{5,6},{6,5},{9,10},{10,9},{13,14},{14,13},{17,18},{18,... | collective-permute-start | bytes 1769480 | tf_op jit(solution)/shard_map/ppermute | solution.py:465
  42.9 0.0 collective-permute-done.13.refs_2_.refs_4_
  42.9 2.7 %collective-permute-start.3 = (bf16[192,1536]{1,0:T(8,128)(2,1)}, bf16[192,1536]{1,0:T(8,128)(2,1)S(1)}, u32[]{:S(2)}, u32[]{:S(2)}) collective-permute-start(bf16[192,1536]{1,0:T(8,128)(2,1)} %refs_1_.1), channel_id=1, source_target_pairs={{1,2},{2,1},{5,6},{6,5},{9,10},{10,9},{13,14},{14,13},{17,18},{18,... | collective-permute-start | bytes 1769480 | tf_op jit(solution)/shard_map/ppermute | solution.py:465
  45.6 19.0 %collective-permute-done.5.refs_0_ = bf16[192,1536]{1,0:T(8,128)(2,1)S(1)} collective-permute-done((bf16[192,1536]{1,0:T(8,128)(2,1)S(1)}, bf16[192,1536]{1,0:T(8,128)(2,1)S(1)}, u32[]{:S(2)}, u32[]{:S(2)}) %collective-permute-start.5) | collective-permute-done | bytes 589856 | tf_op jit(solution)/shard_map/ppermute | solution.py:365
  64.6 0.9 collective-permute-start.15
  65.5 0.0 collective-permute-done.7.refs_1_
  65.5 0.2 collective-permute-start.14
  65.7 0.0 collective-permute-done.16.refs_7_.refs_9_
  65.7 0.4 collective-permute-start.17
  66.0 0.4 collective-permute-start.20
  66.4 2.0 %collective-permute-start.21 = (bf16[192,1536]{1,0:T(8,128)(2,1)}, bf16[192,1536]{1,0:T(8,128)(2,1)}, u32[]{:S(2)}, u32[]{:S(2)}) collective-permute-start(bf16[192,1536]{1,0:T(8,128)(2,1)} %get-tuple-element.44), channel_id=1, source_target_pairs={{0,4},{4,0},{1,5},{5,1},{2,6},{6,2},{3,7},{7,3},{8,12},{12,8},{9,1... | collective-permute-start | bytes 1769480 | tf_op jit(solution)/shard_map/ppermute | solution.py:365
  68.5 0.7 collective-permute-start.19
  69.2 0.1 collective-permute-start.18
  69.3 7.4 %attend.1 = (f32[192,1536]{1,0:T(8,128)}, f32[192,128]{1,0:T(8,128)}) custom-call(s32[1,6]{1,0:T(1,128)} %pattern.5, bf16[192,1536]{1,0:T(8,128)(2,1)} %q.5, bf16[192,1536]{1,0:T(8,128)(2,1)} %refs_0_.1, bf16[192,1536]{1,0:T(8,128)(2,1)} %refs_1_.1, bf16[192,1536]{1,0:T(8,128)(2,1)} %copy-done.8, bf16[192,1536]{1,0:T(8,128)(2,1)} %copy-done.9, ...), custom_call_target="tpu_custom_call" | custom-call | flops 1019215872 | bytes 5308416 | tf_op jit(solution)/shard_map/attend/pallas_call | solution.py:104
  76.8 4.6 %close.1.ready = bf16[192,768]{1,0:T(8,128)(2,1)} custom-call(s32[1,6]{1,0:T(1,128)} %pattern.5, bf16[192,1536]{1,0:T(8,128)(2,1)} %q.5, f32[192,1536]{1,0:T(8,128)} %get-tuple-element.27.part, f32[192,128]{1,0:T(8,128)} %get-tuple-element.28.stats, bf16[192,1536]{1,0:T(8,128)(2,1)} %copy-done.12, bf16[192,1536]{1,0:T(8,128)(2,1)} %copy-done.13), custom_call_target="tpu_custom_call" | custom-call | flops 339738624 | bytes 2359296 | tf_op jit(solution)/shard_map/close/pallas_call | solution.py:179
  81.3 3.0 %collective-permute-done.19.refs_12_ = bf16[48,3072]{1,0:T(8,128)(2,1)S(1)} collective-permute-done((bf16[48,3072]{1,0:T(8,128)(2,1)}, bf16[48,3072]{1,0:T(8,128)(2,1)S(1)}, u32[]{:S(2)}, u32[]{:S(2)}) %collective-permute-start.19) | collective-permute-done | bytes 294944 | tf_op jit(solution)/shard_map/ppermute | solution.py:348
  84.3 1.5 %all-gather.3.cloned.1.call-done = bf16[16,96,1536]{2,1,0:T(8,128)(2,1)} async-done(((bf16[2,96,1536]{2,1,0:T(8,128)(2,1)}), bf16[16,96,1536]{2,1,0:T(8,128)(2,1)}) %all-gather.3.cloned.1.call-update) | async-done | bytes 4718608 | tf_op jit(solution)/shard_map/all_gather | solution.py:477
  85.8 5.5 %begin.1.so_far = f32[192,3072]{1,0:T(8,128)} custom-call(bf16[192,3072]{1,0:T(8,128)(2,1)} %hidden.1, bf16[192,768]{1,0:T(8,128)(2,1)} %close.1.ready, bf16[8,2,96,1536]{3,2,1,0:T(8,128)(2,1)} %bitcast.19, bf16[2,96,1536]{2,1,0:T(8,128)(2,1)} %copy-done, bf16[2,96,1536]{2,1,0:T(8,128)(2,1)} %copy-done.3, bf16[2,96,1536]{2,1,0:T(8,128)(2,1)} %copy-done.2, ...), custom_call_target="tpu_custom_call" | custom-call | flops 905969664 | bytes 9437184 | tf_op jit(solution)/shard_map/begin/pallas_call | solution.py:309
  91.3 3.6 %collective-permute-done.20.refs_0_ = bf16[192,1536]{1,0:T(8,128)(2,1)} collective-permute-done((bf16[192,1536]{1,0:T(8,128)(2,1)}, bf16[192,1536]{1,0:T(8,128)(2,1)}, u32[]{:S(2)}, u32[]{:S(2)}) %collective-permute-start.20) | collective-permute-done | bytes 589856 | tf_op jit(solution)/shard_map/ppermute | solution.py:365
  94.9 7.6 %finish.1 = bf16[192,3072]{1,0:T(8,128)(2,1)} custom-call(s32[1,6]{1,0:T(1,128)} %pattern.5, bf16[192,1536]{1,0:T(8,128)(2,1)} %q.5, f32[192,1536]{1,0:T(8,128)} %get-tuple-element.27.part, f32[192,128]{1,0:T(8,128)} %get-tuple-element.28.stats, f32[192,3072]{1,0:T(8,128)} %begin.1.so_far, bf16[192,1536]{1,0:T(8,128)(2,1)} %collective-permute-done.20.refs_0_, ...), custom_call_target="tpu_custom_call" | custom-call | flops 905969664 | bytes 8257536 | tf_op jit(solution)/shard_map/finish/pallas_call | solution.py:330
  (42 shorter events, 0.1 us)
Async XLA Ops:
  6.5 8.0 %copy-start.7 = (bf16[192,3072]{1,0:T(8,128)(2,1)S(1)}, bf16[192,3072]{1,0:T(8,128)(2,1)}, u32[]{:S(2)}) copy-start(bf16[192,3072]{1,0:T(8,128)(2,1)} %param.11) | copy-start | bytes 3538948
  6.5 79.3 %all-gather.3.cloned.1.call-start = ((), (), s32[]{:S(2)}) async-start(), calls=%async_computation | async-start | bytes 5308416 | tf_op jit(solution)/shard_map/all_gather | solution.py:477
  7.7 10.1 %collective-permute-start.11 = (bf16[1,96,1536]{2,1,0:T(8,128)(2,1)S(1)}, bf16[1,96,1536]{2,1,0:T(8,128)(2,1)S(1)}, u32[]{:S(2)}, u32[]{:S(2)}) collective-permute-start(bf16[1,96,1536]{2,1,0:T(8,128)(2,1)S(1)} %bitcast.21), channel_id=1, source_target_pairs={{0,2},{2,0},{1,3},{3,1},{4,6},{6,4},{5,7},{7,5},{8,10},{10,8},{9,1... | collective-permute-start | bytes 884744 | tf_op jit(solution)/shard_map/ppermute | solution.py:348
  9.8 13.9 %collective-permute-start.6 = (bf16[1,96,1536]{2,1,0:T(8,128)(2,1)S(1)}, bf16[1,96,1536]{2,1,0:T(8,128)(2,1)S(1)}, u32[]{:S(2)}, u32[]{:S(2)}) collective-permute-start(bf16[1,96,1536]{2,1,0:T(8,128)(2,1)S(1)} %bitcast.22), channel_id=1, source_target_pairs={{0,4},{4,0},{8,12},{12,8},{1,5},{5,1},{9,13},{13,9},{2,6},{6,2},{1... | collective-permute-start | bytes 884744 | tf_op jit(solution)/shard_map/ppermute | solution.py:348
  11.1 12.6 %collective-permute-start.4 = (bf16[1,96,1536]{2,1,0:T(8,128)(2,1)S(1)}, bf16[1,96,1536]{2,1,0:T(8,128)(2,1)S(1)}, u32[]{:S(2)}, u32[]{:S(2)}) collective-permute-start(bf16[1,96,1536]{2,1,0:T(8,128)(2,1)S(1)} %bitcast.23), channel_id=1, source_target_pairs={{0,8},{4,12},{8,0},{12,4},{1,9},{5,13},{9,1},{13,5},{2,10},{6,14},... | collective-permute-start | bytes 884744 | tf_op jit(solution)/shard_map/ppermute | solution.py:348
  17.6 7.1 %collective-permute-start.8 = (bf16[48,3072]{1,0:T(8,128)(2,1)S(1)}, bf16[48,3072]{1,0:T(8,128)(2,1)}, u32[]{:S(2)}, u32[]{:S(2)}) collective-permute-start(bf16[48,3072]{1,0:T(8,128)(2,1)S(1)} %get-tuple-element.34), channel_id=1, source_target_pairs={{0,2},{1,3},{2,0},{3,1},{4,6},{5,7},{6,4},{7,5},{8,10},{9,11},{10,... | collective-permute-start | bytes 884744 | tf_op jit(solution)/shard_map/ppermute | solution.py:348
  17.9 20.7 %copy-start = (bf16[2,96,1536]{2,1,0:T(8,128)(2,1)}, bf16[2,96,1536]{2,1,0:T(8,128)(2,1)S(1)}, u32[]{:S(2)}) copy-start(bf16[2,96,1536]{2,1,0:T(8,128)(2,1)S(1)} %pad_maximum_fusion.3.refs_1_.refs_3_) | copy-start | bytes 1769476
  17.9 14.5 %collective-permute-start.12 = (bf16[2,96,1536]{2,1,0:T(8,128)(2,1)S(1)}, bf16[2,96,1536]{2,1,0:T(8,128)(2,1)S(1)}, u32[]{:S(2)}, u32[]{:S(2)}) collective-permute-start(bf16[2,96,1536]{2,1,0:T(8,128)(2,1)S(1)} %pad_maximum_fusion.3.refs_1_.refs_3_), channel_id=1, source_target_pairs={{0,16},{16,0},{1,17},{17,1},{2,18},{18,2},{3,19},{19,3},{4,20},{20... | collective-permute-start | bytes 1769480 | tf_op jit(solution)/shard_map/ppermute | solution.py:348
  24.7 5.9 %collective-permute-start.9 = (bf16[1,96,1536]{2,1,0:T(8,128)(2,1)S(1)}, bf16[1,96,1536]{2,1,0:T(8,128)(2,1)S(1)}, u32[]{:S(2)}, u32[]{:S(2)}) collective-permute-start(bf16[1,96,1536]{2,1,0:T(8,128)(2,1)S(1)} %collective-permute-done.4), channel_id=1, source_target_pairs={{0,4},{4,0},{8,12},{12,8},{1,5},{5,1},{9,13},{13,9},{2,6},{6,2},{1... | collective-permute-start | bytes 884744 | tf_op jit(solution)/shard_map/ppermute | solution.py:348
  26.1 6.3 %collective-permute-start.10 = (bf16[1,96,1536]{2,1,0:T(8,128)(2,1)S(1)}, bf16[1,96,1536]{2,1,0:T(8,128)(2,1)S(1)}, u32[]{:S(2)}, u32[]{:S(2)}) collective-permute-start(bf16[1,96,1536]{2,1,0:T(8,128)(2,1)S(1)} %collective-permute-done.6), channel_id=1, source_target_pairs={{0,2},{2,0},{1,3},{3,1},{4,6},{6,4},{5,7},{7,5},{8,10},{10,8},{9,1... | collective-permute-start | bytes 884744 | tf_op jit(solution)/shard_map/ppermute | solution.py:348
  32.4 44.3 %copy-start.2 = (bf16[2,96,1536]{2,1,0:T(8,128)(2,1)}, bf16[2,96,1536]{2,1,0:T(8,128)(2,1)S(1)}, u32[]{:S(2)}) copy-start(bf16[2,96,1536]{2,1,0:T(8,128)(2,1)S(1)} %collective-permute-done.12.refs_3_.refs_5_) | copy-start | bytes 1769476
  32.4 6.3 %collective-permute-start = (bf16[192,1536]{1,0:T(8,128)(2,1)}, bf16[192,1536]{1,0:T(8,128)(2,1)S(1)}, u32[]{:S(2)}, u32[]{:S(2)}) collective-permute-start(bf16[192,1536]{1,0:T(8,128)(2,1)} %refs_0_.1), channel_id=1, source_target_pairs={{0,1},{1,0},{2,3},{3,2},{4,5},{5,4},{6,7},{7,6},{8,9},{9,8},{10,11... | collective-permute-start | bytes 1769480 | tf_op jit(solution)/shard_map/ppermute | solution.py:463
  35.6 4.4 %collective-permute-start.1 = (bf16[192,1536]{1,0:T(8,128)(2,1)}, bf16[192,1536]{1,0:T(8,128)(2,1)S(1)}, u32[]{:S(2)}, u32[]{:S(2)}) collective-permute-start(bf16[192,1536]{1,0:T(8,128)(2,1)} %refs_1_.1), channel_id=1, source_target_pairs={{0,1},{1,0},{2,3},{3,2},{4,5},{5,4},{6,7},{7,6},{8,9},{9,8},{10,11... | collective-permute-start | bytes 1769480 | tf_op jit(solution)/shard_map/ppermute | solution.py:463
  35.7 7.2 %collective-permute-start.13 = (bf16[2,96,1536]{2,1,0:T(8,128)(2,1)S(1)}, bf16[2,96,1536]{2,1,0:T(8,128)(2,1)S(1)}, u32[]{:S(2)}, u32[]{:S(2)}) collective-permute-start(bf16[2,96,1536]{2,1,0:T(8,128)(2,1)S(1)} %pad_maximum_fusion.3.refs_1_.refs_3_), channel_id=1, source_target_pairs={{0,1},{1,0},{2,3},{3,2},{4,5},{5,4},{6,7},{7,6},{8,9},{9,8},{10,11... | collective-permute-start | bytes 1769480 | tf_op jit(solution)/shard_map/ppermute | solution.py:348
  36.1 28.5 %collective-permute-start.5 = (bf16[192,1536]{1,0:T(8,128)(2,1)S(1)}, bf16[192,1536]{1,0:T(8,128)(2,1)S(1)}, u32[]{:S(2)}, u32[]{:S(2)}) collective-permute-start(bf16[192,1536]{1,0:T(8,128)(2,1)S(1)} %get-tuple-element.32), channel_id=1, source_target_pairs={{0,8},{8,0},{1,9},{9,1},{2,10},{10,2},{3,11},{11,3},{4,12},{12,4},... | collective-permute-start | bytes 1769480 | tf_op jit(solution)/shard_map/ppermute | solution.py:365
  38.0 27.5 %collective-permute-start.7 = (bf16[192,1536]{1,0:T(8,128)(2,1)S(1)}, bf16[192,1536]{1,0:T(8,128)(2,1)S(1)}, u32[]{:S(2)}, u32[]{:S(2)}) collective-permute-start(bf16[192,1536]{1,0:T(8,128)(2,1)S(1)} %get-tuple-element.32), channel_id=1, source_target_pairs={{0,4},{4,0},{1,5},{5,1},{2,6},{6,2},{3,7},{7,3},{8,12},{12,8},{9,1... | collective-permute-start | bytes 1769480 | tf_op jit(solution)/shard_map/ppermute | solution.py:365
  38.7 38.0 %copy-start.1 = (bf16[2,96,1536]{2,1,0:T(8,128)(2,1)}, bf16[2,96,1536]{2,1,0:T(8,128)(2,1)S(1)}, u32[]{:S(2)}) copy-start(bf16[2,96,1536]{2,1,0:T(8,128)(2,1)S(1)} %constant_dynamic-update-slice_fusion.refs_5_.refs_7_) | copy-start | bytes 1769476
  38.7 30.4 %copy-start.8 = (bf16[192,1536]{1,0:T(8,128)(2,1)}, bf16[192,1536]{1,0:T(8,128)(2,1)S(1)}, u32[]{:S(2)}) copy-start(bf16[192,1536]{1,0:T(8,128)(2,1)S(1)} %collective-permute-done.refs_2_) | copy-start | bytes 1769476
  38.7 27.0 %collective-permute-start.16 = (bf16[2,96,1536]{2,1,0:T(8,128)(2,1)S(1)}, bf16[2,96,1536]{2,1,0:T(8,128)(2,1)S(1)}, u32[]{:S(2)}, u32[]{:S(2)}) collective-permute-start(bf16[2,96,1536]{2,1,0:T(8,128)(2,1)S(1)} %constant_dynamic-update-slice_fusion.refs_5_.refs_7_), channel_id=1, source_target_pairs={{0,16},{16,0},{1,17},{17,1},{2,18},{18,2},{3,19},{19,3},{4,20},{20... | collective-permute-start | bytes 1769480 | tf_op jit(solution)/shard_map/ppermute | solution.py:348
  40.0 29.1 %copy-start.9 = (bf16[192,1536]{1,0:T(8,128)(2,1)}, bf16[192,1536]{1,0:T(8,128)(2,1)S(1)}, u32[]{:S(2)}) copy-start(bf16[192,1536]{1,0:T(8,128)(2,1)S(1)} %collective-permute-done.1.refs_3_) | copy-start | bytes 1769476
  40.0 26.0 %collective-permute-start.2 = (bf16[192,1536]{1,0:T(8,128)(2,1)}, bf16[192,1536]{1,0:T(8,128)(2,1)S(1)}, u32[]{:S(2)}, u32[]{:S(2)}) collective-permute-start(bf16[192,1536]{1,0:T(8,128)(2,1)} %refs_0_.1), channel_id=1, source_target_pairs={{1,2},{2,1},{5,6},{6,5},{9,10},{10,9},{13,14},{14,13},{17,18},{18,... | collective-permute-start | bytes 1769480 | tf_op jit(solution)/shard_map/ppermute | solution.py:465
  42.9 33.8 %copy-start.3 = (bf16[2,96,1536]{2,1,0:T(8,128)(2,1)}, bf16[2,96,1536]{2,1,0:T(8,128)(2,1)S(1)}, u32[]{:S(2)}) copy-start(bf16[2,96,1536]{2,1,0:T(8,128)(2,1)S(1)} %collective-permute-done.13.refs_2_.refs_4_) | copy-start | bytes 1769476
  42.9 23.5 %collective-permute-start.3 = (bf16[192,1536]{1,0:T(8,128)(2,1)}, bf16[192,1536]{1,0:T(8,128)(2,1)S(1)}, u32[]{:S(2)}, u32[]{:S(2)}) collective-permute-start(bf16[192,1536]{1,0:T(8,128)(2,1)} %refs_1_.1), channel_id=1, source_target_pairs={{1,2},{2,1},{5,6},{6,5},{9,10},{10,9},{13,14},{14,13},{17,18},{18,... | collective-permute-start | bytes 1769480 | tf_op jit(solution)/shard_map/ppermute | solution.py:465
  64.6 4.6 %copy-start.12 = (bf16[192,1536]{1,0:T(8,128)(2,1)}, bf16[192,1536]{1,0:T(8,128)(2,1)S(1)}, u32[]{:S(2)}) copy-start(bf16[192,1536]{1,0:T(8,128)(2,1)S(1)} %collective-permute-done.5.refs_0_) | copy-start | bytes 1769476
  64.6 3.9 %collective-permute-start.15 = (bf16[2,96,1536]{2,1,0:T(8,128)(2,1)S(1)}, bf16[2,96,1536]{2,1,0:T(8,128)(2,1)S(1)}, u32[]{:S(2)}, u32[]{:S(2)}) collective-permute-start(bf16[2,96,1536]{2,1,0:T(8,128)(2,1)S(1)} %constant_dynamic-update-slice_fusion.refs_5_.refs_7_), channel_id=1, source_target_pairs={{0,1},{1,0},{2,3},{3,2},{4,5},{5,4},{6,7},{7,6},{8,9},{9,8},{10,11... | collective-permute-start | bytes 1769480 | tf_op jit(solution)/shard_map/ppermute | solution.py:348
  65.5 3.7 %copy-start.13 = (bf16[192,1536]{1,0:T(8,128)(2,1)}, bf16[192,1536]{1,0:T(8,128)(2,1)S(1)}, u32[]{:S(2)}) copy-start(bf16[192,1536]{1,0:T(8,128)(2,1)S(1)} %collective-permute-done.7.refs_1_) | copy-start | bytes 1769476
  65.5 3.6 %collective-permute-start.14 = (bf16[2,96,1536]{2,1,0:T(8,128)(2,1)S(1)}, bf16[2,96,1536]{2,1,0:T(8,128)(2,1)S(1)}, u32[]{:S(2)}, u32[]{:S(2)}) collective-permute-start(bf16[2,96,1536]{2,1,0:T(8,128)(2,1)S(1)} %collective-permute-done.12.refs_3_.refs_5_), channel_id=1, source_target_pairs={{0,1},{1,0},{2,3},{3,2},{4,5},{5,4},{6,7},{7,6},{8,9},{9,8},{10,11... | collective-permute-start | bytes 1769480 | tf_op jit(solution)/shard_map/ppermute | solution.py:348
  65.7 11.1 %copy-start.4 = (bf16[2,96,1536]{2,1,0:T(8,128)(2,1)}, bf16[2,96,1536]{2,1,0:T(8,128)(2,1)S(1)}, u32[]{:S(2)}) copy-start(bf16[2,96,1536]{2,1,0:T(8,128)(2,1)S(1)} %collective-permute-done.16.refs_7_.refs_9_) | copy-start | bytes 1769476
  65.7 18.6 %collective-permute-start.17 = (bf16[2,96,1536]{2,1,0:T(8,128)(2,1)S(1)}, bf16[2,96,1536]{2,1,0:T(8,128)(2,1)}, u32[]{:S(2)}, u32[]{:S(2)}) collective-permute-start(bf16[2,96,1536]{2,1,0:T(8,128)(2,1)S(1)} %collective-permute-done.16.refs_7_.refs_9_), channel_id=1, source_target_pairs={{0,1},{1,0},{2,3},{3,2},{4,5},{5,4},{6,7},{7,6},{8,9},{9,8},{10,11... | collective-permute-start | bytes 1769480 | tf_op jit(solution)/shard_map/ppermute | solution.py:348
  66.0 3.2 %copy-start.10 = (bf16[192,1536]{1,0:T(8,128)(2,1)}, bf16[192,1536]{1,0:T(8,128)(2,1)S(1)}, u32[]{:S(2)}) copy-start(bf16[192,1536]{1,0:T(8,128)(2,1)S(1)} %collective-permute-done.2.refs_4_) | copy-start | bytes 1769476
  66.0 28.9 %collective-permute-start.20 = (bf16[192,1536]{1,0:T(8,128)(2,1)}, bf16[192,1536]{1,0:T(8,128)(2,1)}, u32[]{:S(2)}, u32[]{:S(2)}) collective-permute-start(bf16[192,1536]{1,0:T(8,128)(2,1)} %get-tuple-element.44), channel_id=1, source_target_pairs={{0,8},{8,0},{1,9},{9,1},{2,10},{10,2},{3,11},{11,3},{4,12},{12,4},... | collective-permute-start | bytes 1769480 | tf_op jit(solution)/shard_map/ppermute | solution.py:365
  66.4 2.7 %copy-start.11 = (bf16[192,1536]{1,0:T(8,128)(2,1)}, bf16[192,1536]{1,0:T(8,128)(2,1)S(1)}, u32[]{:S(2)}) copy-start(bf16[192,1536]{1,0:T(8,128)(2,1)S(1)} %collective-permute-done.3.refs_5_) | copy-start | bytes 1769476
  66.4 28.5 %collective-permute-start.21 = (bf16[192,1536]{1,0:T(8,128)(2,1)}, bf16[192,1536]{1,0:T(8,128)(2,1)}, u32[]{:S(2)}, u32[]{:S(2)}) collective-permute-start(bf16[192,1536]{1,0:T(8,128)(2,1)} %get-tuple-element.44), channel_id=1, source_target_pairs={{0,4},{4,0},{1,5},{5,1},{2,6},{6,2},{3,7},{7,3},{8,12},{12,8},{9,1... | collective-permute-start | bytes 1769480 | tf_op jit(solution)/shard_map/ppermute | solution.py:365
  68.5 8.3 %copy-start.5 = (bf16[2,96,1536]{2,1,0:T(8,128)(2,1)}, bf16[2,96,1536]{2,1,0:T(8,128)(2,1)S(1)}, u32[]{:S(2)}) copy-start(bf16[2,96,1536]{2,1,0:T(8,128)(2,1)S(1)} %collective-permute-done.15.refs_6_.refs_8_) | copy-start | bytes 1769476
  68.5 15.8 %collective-permute-start.19 = (bf16[48,3072]{1,0:T(8,128)(2,1)}, bf16[48,3072]{1,0:T(8,128)(2,1)S(1)}, u32[]{:S(2)}, u32[]{:S(2)}) collective-permute-start(bf16[48,3072]{1,0:T(8,128)(2,1)} %get-tuple-element.42), channel_id=1, source_target_pairs={{0,3},{1,2},{2,1},{3,0},{4,7},{5,6},{6,5},{7,4},{8,11},{9,10},{10,... | collective-permute-start | bytes 884744 | tf_op jit(solution)/shard_map/ppermute | solution.py:348
  69.2 7.6 %copy-start.6 = (bf16[2,96,1536]{2,1,0:T(8,128)(2,1)}, bf16[2,96,1536]{2,1,0:T(8,128)(2,1)S(1)}, u32[]{:S(2)}) copy-start(bf16[2,96,1536]{2,1,0:T(8,128)(2,1)S(1)} %collective-permute-done.14.refs_4_.refs_6_) | copy-start | bytes 1769476
  69.2 15.1 %collective-permute-start.18 = (bf16[48,3072]{1,0:T(8,128)(2,1)}, bf16[48,3072]{1,0:T(8,128)(2,1)}, u32[]{:S(2)}, u32[]{:S(2)}) collective-permute-start(bf16[48,3072]{1,0:T(8,128)(2,1)} %get-tuple-element.40), channel_id=1, source_target_pairs={{0,1},{1,0},{2,3},{3,2},{4,5},{5,4},{6,7},{7,6},{8,9},{9,8},{10,11... | collective-permute-start | bytes 884744 | tf_op jit(solution)/shard_map/ppermute | solution.py:348
  84.3 1.5 %copy-start.14 = (bf16[48,3072]{1,0:T(8,128)(2,1)}, bf16[48,3072]{1,0:T(8,128)(2,1)S(1)}, u32[]{:S(2)}) copy-start(bf16[48,3072]{1,0:T(8,128)(2,1)S(1)} %collective-permute-done.19.refs_12_) | copy-start | bytes 884740
Sparse Core Ops, SparseCore 0:
  32.5 53.2 all-gather.2

commit v17 on v16

--- a/solution.py
+++ b/solution.py
@@ -193,36 +193,45 @@
 
 
 def fetch_weight(fetch, moves, place, weight, held, low, high):
-    copies = []
-    for piece, index, at in moves:
-        if at is None:
-            copies.append((True, 0, fetch(weight[piece], held)))
-            continue
-        source = weight[piece].at[index]
-        flip, group, outer, pair, core = at
-        known = None if flip else group
-        count = source.shape[0]
-        outer = place[1] ^ outer
-        if flip:
-            group, pair, core = place[0] ^ group, place[2] ^ pair, place[3] ^ core
-        start = pl.multiple_of(((outer * 2 + pair) * 2 + core) * count, count)
-        needed = (start < high) & (start + count > low)
-        copy = fetch.later(source, held.at[group, pl.ds(start, count), :])
-        pl.when(needed)(copy.start)
-        copies.append((needed, 0 if known is None else known, copy))
-    return copies
+    if moves[0][2] is None:
+        return [(True, 0, [fetch(weight[piece], held)]) for piece, _, _ in moves]
+    starts = []
+    for outer_flip in sorted({at[2] for _, _, at in moves}):
+        blocks = [move for move in moves if move[2][2] == outer_flip]
+        count = weight[0].shape[-2]
+        span = len(blocks) // held.shape[0] * count
+        outer = place[1] ^ outer_flip
+        needed = (outer * span < high) & ((outer + 1) * span > low)
+        copies = {}
+        for piece, index, (flip, group, _, pair, core) in blocks:
+            known = 0 if flip else group
+            if flip:
+                group, pair, core = place[0] ^ group, place[2] ^ pair, place[3] ^ core
+            start = pl.multiple_of(((outer * 2 + pair) * 2 + core) * count, count)
+            copy = fetch.later(weight[piece].at[index], held.at[group, pl.ds(start, count), :])
+            copies.setdefault(known, []).append(copy)
+
+        @pl.when(needed)
+        def _():
+            for each in copies.values():
+                for copy in each:
+                    copy.start()
+
+        starts += [(needed, known, each) for known, each in copies.items()]
+    return starts
 
 
 def project(copies, attention, held, low, out, add):
     groups, _, columns = held.shape
     step = 512 if columns % 512 == 0 else columns
     for group in range(groups):
-        for needed, at, copy in copies:
+        for needed, at, each in copies:
             if at == group:
-                if needed is True:
-                    copy.wait()
-                else:
-                    pl.when(needed)(copy.wait)
+
+                @pl.when(needed)
+                def _():
+                    for copy in each:
+                        copy.wait()
         for j in range(columns // step):
             at = pl.ds(group * columns + j * step, step)
             projected = jnp.dot(

time: 110 us -> 110 us (level)
  no operation moved by 1% of the time
where the time goes in v17:
time: 110 us; the launch traced here: 109 us
  waiting for transfers between devices  37.6 us (34%)
  starting transfers between devices  26.6 us (24%)
  Pallas kernels  25.1 us (23%)
  between operations  13.7 us (12%)
  local copies, waits for them, and re-layouts  3.26 us (3%)
  other arithmetic  3.09 us (3%)
    ppermute x4, waiting for transfers between devices, route_of(): return lambda block: lax.ppermute(block, TILES, route)  22.5 us
    ppermute x14, waiting for transfers between devices, flipped(): lax.ppermute(block, axis, [(i, i ^ flip) for i in range(lax.axis_size(axi...  13.6 us
    ppermute x14, starting transfers between devices, flipped(): lax.ppermute(block, axis, [(i, i ^ flip) for i in range(lax.axis_size(axi...  12.9 us
    pallas_call x1, Pallas kernels, finish(): pl.pallas_call(functools.partial(finish_kernel, which, len(weight), moves...  7.6 us
    pallas_call x1, Pallas kernels, attend(): pl.pallas_call(functools.partial(attend_kernel, which), out_shape=[jax.Sh...  7.39 us
    ppermute x2, starting transfers between devices, on_device(): lax.ppermute(after(x, early_near[0][i]), TILES, early[slot][2])  5.56 us
    pallas_call x1, Pallas kernels, begin(): pl.pallas_call(functools.partial(begin_kernel, (len(weight), len(control)...  5.54 us
    ppermute x4, starting transfers between devices, route_of(): return lambda block: lax.ppermute(block, TILES, route)  4.94 us
  transfers between devices with their start and end apart: 23, of which 8 were waited for; matrix products, arithmetic and copies ran while one was open for 5% of the time, Pallas kernels for 16%

profile of v17, /device:TPU:1, one launch (start us, length us, event | category | flops | bytes accessed | tf_op | source)
XLA Modules:
  0.0 109.4 jit_solution(861803037181722199)
XLA Ops:
  6.5 1.2 %slice_select_fusion = bf16[96,1536]{1,0:T(8,128)(2,1)S(1)} fusion(bf16[96,3072]{1,0:T(8,128)(2,1)} %param.12, pred[]{:T(512)S(6)} %eq.3), kind=kLoop, calls=%fused_computation.8 | loop fusion | flops 147456 | bytes 884737 | tf_op jit(solution)/shard_map/jit(_where)/select_n | solution.py:438
  7.7 2.1 %collective-permute-start.11 = (bf16[1,96,1536]{2,1,0:T(8,128)(2,1)S(1)}, bf16[1,96,1536]{2,1,0:T(8,128)(2,1)S(1)}, u32[]{:S(2)}, u32[]{:S(2)}) collective-permute-start(bf16[1,96,1536]{2,1,0:T(8,128)(2,1)S(1)} %bitcast.21), channel_id=1, source_target_pairs={{0,2},{2,0},{1,3},{3,1},{4,6},{6,4},{5,7},{7,5},{8,10},{10,8},{9,1... | collective-permute-start | bytes 884744 | tf_op jit(solution)/shard_map/ppermute | solution.py:357
  9.8 1.3 %collective-permute-start.6 = (bf16[1,96,1536]{2,1,0:T(8,128)(2,1)S(1)}, bf16[1,96,1536]{2,1,0:T(8,128)(2,1)S(1)}, u32[]{:S(2)}, u32[]{:S(2)}) collective-permute-start(bf16[1,96,1536]{2,1,0:T(8,128)(2,1)S(1)} %bitcast.22), channel_id=1, source_target_pairs={{0,4},{4,0},{8,12},{12,8},{1,5},{5,1},{9,13},{13,9},{2,6},{6,2},{1... | collective-permute-start | bytes 884744 | tf_op jit(solution)/shard_map/ppermute | solution.py:357
  11.1 2.3 %collective-permute-start.4 = (bf16[1,96,1536]{2,1,0:T(8,128)(2,1)S(1)}, bf16[1,96,1536]{2,1,0:T(8,128)(2,1)S(1)}, u32[]{:S(2)}, u32[]{:S(2)}) collective-permute-start(bf16[1,96,1536]{2,1,0:T(8,128)(2,1)S(1)} %bitcast.23), channel_id=1, source_target_pairs={{0,8},{4,12},{8,0},{12,4},{1,9},{5,13},{9,1},{13,5},{2,10},{6,14},... | collective-permute-start | bytes 884744 | tf_op jit(solution)/shard_map/ppermute | solution.py:357
  13.4 1.1 fusion
  14.6 1.0 dynamic-slice_bitcast_fusion
  15.5 1.1 fusion.1
  16.6 1.0 pad_maximum_fusion
  17.6 0.3 collective-permute-start.8
  17.8 0.0 collective-permute-done.11
  17.8 0.1 pad_maximum_fusion.3.refs_1_.refs_3_
  17.9 1.3 %collective-permute-start.12 = (bf16[2,96,1536]{2,1,0:T(8,128)(2,1)S(1)}, bf16[2,96,1536]{2,1,0:T(8,128)(2,1)S(1)}, u32[]{:S(2)}, u32[]{:S(2)}) collective-permute-start(bf16[2,96,1536]{2,1,0:T(8,128)(2,1)S(1)} %pad_maximum_fusion.3.refs_1_.refs_3_), channel_id=1, source_target_pairs={{0,16},{16,0},{1,17},{17,1},{2,18},{18,2},{3,19},{19,3},{4,20},{20... | collective-permute-start | bytes 1769480 | tf_op jit(solution)/shard_map/ppermute | solution.py:357
  19.2 4.5 %collective-permute-done.6 = bf16[1,96,1536]{2,1,0:T(8,128)(2,1)S(1)} collective-permute-done((bf16[1,96,1536]{2,1,0:T(8,128)(2,1)S(1)}, bf16[1,96,1536]{2,1,0:T(8,128)(2,1)S(1)}, u32[]{:S(2)}, u32[]{:S(2)}) %collective-permute-start.6) | collective-permute-done | bytes 294944 | tf_op jit(solution)/shard_map/ppermute | solution.py:357
  23.7 0.0 collective-permute-done.4
  23.7 1.0 collective-permute-done.8.refs_11_
  24.7 1.4 %collective-permute-start.9 = (bf16[1,96,1536]{2,1,0:T(8,128)(2,1)S(1)}, bf16[1,96,1536]{2,1,0:T(8,128)(2,1)S(1)}, u32[]{:S(2)}, u32[]{:S(2)}) collective-permute-start(bf16[1,96,1536]{2,1,0:T(8,128)(2,1)S(1)} %collective-permute-done.4), channel_id=1, source_target_pairs={{0,4},{4,0},{8,12},{12,8},{1,5},{5,1},{9,13},{13,9},{2,6},{6,2},{1... | collective-permute-start | bytes 884744 | tf_op jit(solution)/shard_map/ppermute | solution.py:357
  26.1 0.3 collective-permute-start.10
  26.3 4.3 %collective-permute-done.9 = bf16[1,96,1536]{2,1,0:T(8,128)(2,1)S(1)} collective-permute-done((bf16[1,96,1536]{2,1,0:T(8,128)(2,1)S(1)}, bf16[1,96,1536]{2,1,0:T(8,128)(2,1)S(1)}, u32[]{:S(2)}, u32[]{:S(2)}) %collective-permute-start.9) | collective-permute-done | bytes 294944 | tf_op jit(solution)/shard_map/ppermute | solution.py:357
  30.6 0.9 pad_maximum_fusion.2
  31.5 0.9 collective-permute-done.10
  32.4 0.0 all-gather.3.cloned.1.call-update
  32.4 3.2 %collective-permute-start = (bf16[192,1536]{1,0:T(8,128)(2,1)}, bf16[192,1536]{1,0:T(8,128)(2,1)S(1)}, u32[]{:S(2)}, u32[]{:S(2)}) collective-permute-start(bf16[192,1536]{1,0:T(8,128)(2,1)} %refs_0_.1), channel_id=1, source_target_pairs={{0,1},{1,0},{2,3},{3,2},{4,5},{5,4},{6,7},{7,6},{8,9},{9,8},{10,11... | collective-permute-start | bytes 1769480 | tf_op jit(solution)/shard_map/ppermute | solution.py:472
  35.6 0.1 collective-permute-start.1
  35.7 0.4 collective-permute-start.13
  36.1 1.9 %collective-permute-start.5 = (bf16[192,1536]{1,0:T(8,128)(2,1)S(1)}, bf16[192,1536]{1,0:T(8,128)(2,1)S(1)}, u32[]{:S(2)}, u32[]{:S(2)}) collective-permute-start(bf16[192,1536]{1,0:T(8,128)(2,1)S(1)} %get-tuple-element.32), channel_id=1, source_target_pairs={{0,8},{8,0},{1,9},{9,1},{2,10},{10,2},{3,11},{11,3},{4,12},{12,4},... | collective-permute-start | bytes 1769480 | tf_op jit(solution)/shard_map/ppermute | solution.py:374
  38.0 0.6 collective-permute-start.7
  38.7 0.0 collective-permute-done.refs_2_
  38.7 0.0 copy-start.8
  38.7 1.3 %collective-permute-start.16 = (bf16[2,96,1536]{2,1,0:T(8,128)(2,1)S(1)}, bf16[2,96,1536]{2,1,0:T(8,128)(2,1)S(1)}, u32[]{:S(2)}, u32[]{:S(2)}) collective-permute-start(bf16[2,96,1536]{2,1,0:T(8,128)(2,1)S(1)} %constant_dynamic-update-slice_fusion.refs_5_.refs_7_), channel_id=1, source_target_pairs={{0,16},{16,0},{1,17},{17,1},{2,18},{18,2},{3,19},{19,3},{4,20},{20... | collective-permute-start | bytes 1769480 | tf_op jit(solution)/shard_map/ppermute | solution.py:357
  40.0 0.0 collective-permute-done.1.refs_3_
  40.0 2.9 %collective-permute-start.2 = (bf16[192,1536]{1,0:T(8,128)(2,1)}, bf16[192,1536]{1,0:T(8,128)(2,1)S(1)}, u32[]{:S(2)}, u32[]{:S(2)}) collective-permute-start(bf16[192,1536]{1,0:T(8,128)(2,1)} %refs_0_.1), channel_id=1, source_target_pairs={{1,2},{2,1},{5,6},{6,5},{9,10},{10,9},{13,14},{14,13},{17,18},{18,... | collective-permute-start | bytes 1769480 | tf_op jit(solution)/shard_map/ppermute | solution.py:474
  42.9 0.0 collective-permute-done.13.refs_2_.refs_4_
  42.9 2.7 %collective-permute-start.3 = (bf16[192,1536]{1,0:T(8,128)(2,1)}, bf16[192,1536]{1,0:T(8,128)(2,1)S(1)}, u32[]{:S(2)}, u32[]{:S(2)}) collective-permute-start(bf16[192,1536]{1,0:T(8,128)(2,1)} %refs_1_.1), channel_id=1, source_target_pairs={{1,2},{2,1},{5,6},{6,5},{9,10},{10,9},{13,14},{14,13},{17,18},{18,... | collective-permute-start | bytes 1769480 | tf_op jit(solution)/shard_map/ppermute | solution.py:474
  45.6 19.0 %collective-permute-done.5.refs_0_ = bf16[192,1536]{1,0:T(8,128)(2,1)S(1)} collective-permute-done((bf16[192,1536]{1,0:T(8,128)(2,1)S(1)}, bf16[192,1536]{1,0:T(8,128)(2,1)S(1)}, u32[]{:S(2)}, u32[]{:S(2)}) %collective-permute-start.5) | collective-permute-done | bytes 589856 | tf_op jit(solution)/shard_map/ppermute | solution.py:374
  64.6 0.9 collective-permute-start.15
  65.5 0.2 collective-permute-start.14
  65.7 0.4 collective-permute-start.17
  66.0 0.4 collective-permute-start.20
  66.4 2.0 %collective-permute-start.21 = (bf16[192,1536]{1,0:T(8,128)(2,1)}, bf16[192,1536]{1,0:T(8,128)(2,1)}, u32[]{:S(2)}, u32[]{:S(2)}) collective-permute-start(bf16[192,1536]{1,0:T(8,128)(2,1)} %get-tuple-element.44), channel_id=1, source_target_pairs={{0,4},{4,0},{1,5},{5,1},{2,6},{6,2},{3,7},{7,3},{8,12},{12,8},{9,1... | collective-permute-start | bytes 1769480 | tf_op jit(solution)/shard_map/ppermute | solution.py:374
  68.5 0.7 collective-permute-start.19
  69.2 0.1 collective-permute-start.18
  69.3 7.4 %attend.1 = (f32[192,1536]{1,0:T(8,128)}, f32[192,128]{1,0:T(8,128)}) custom-call(s32[1,6]{1,0:T(1,128)} %pattern.5, bf16[192,1536]{1,0:T(8,128)(2,1)} %q.5, bf16[192,1536]{1,0:T(8,128)(2,1)} %refs_0_.1, bf16[192,1536]{1,0:T(8,128)(2,1)} %refs_1_.1, bf16[192,1536]{1,0:T(8,128)(2,1)} %copy-done.8, bf16[192,1536]{1,0:T(8,128)(2,1)} %copy-done.9, ...), custom_call_target="tpu_custom_call" | custom-call | flops 1019215872 | bytes 5308416 | tf_op jit(solution)/shard_map/attend/pallas_call | solution.py:104
  76.8 4.6 %close.1.ready = bf16[192,768]{1,0:T(8,128)(2,1)} custom-call(s32[1,6]{1,0:T(1,128)} %pattern.5, bf16[192,1536]{1,0:T(8,128)(2,1)} %q.5, f32[192,1536]{1,0:T(8,128)} %get-tuple-element.27.part, f32[192,128]{1,0:T(8,128)} %get-tuple-element.28.stats, bf16[192,1536]{1,0:T(8,128)(2,1)} %copy-done.12, bf16[192,1536]{1,0:T(8,128)(2,1)} %copy-done.13), custom_call_target="tpu_custom_call" | custom-call | flops 339738624 | bytes 2359296 | tf_op jit(solution)/shard_map/close/pallas_call | solution.py:179
  81.3 3.0 %collective-permute-done.19.refs_12_ = bf16[48,3072]{1,0:T(8,128)(2,1)S(1)} collective-permute-done((bf16[48,3072]{1,0:T(8,128)(2,1)}, bf16[48,3072]{1,0:T(8,128)(2,1)S(1)}, u32[]{:S(2)}, u32[]{:S(2)}) %collective-permute-start.19) | collective-permute-done | bytes 294944 | tf_op jit(solution)/shard_map/ppermute | solution.py:357
  84.3 1.5 %all-gather.3.cloned.1.call-done = bf16[16,96,1536]{2,1,0:T(8,128)(2,1)} async-done(((bf16[2,96,1536]{2,1,0:T(8,128)(2,1)}), bf16[16,96,1536]{2,1,0:T(8,128)(2,1)}) %all-gather.3.cloned.1.call-update) | async-done | bytes 4718608 | tf_op jit(solution)/shard_map/all_gather | solution.py:486
  85.8 5.5 %begin.1.so_far = f32[192,3072]{1,0:T(8,128)} custom-call(bf16[192,3072]{1,0:T(8,128)(2,1)} %hidden.1, bf16[192,768]{1,0:T(8,128)(2,1)} %close.1.ready, bf16[8,2,96,1536]{3,2,1,0:T(8,128)(2,1)} %bitcast.19, bf16[2,96,1536]{2,1,0:T(8,128)(2,1)} %copy-done, bf16[2,96,1536]{2,1,0:T(8,128)(2,1)} %copy-done.3, bf16[2,96,1536]{2,1,0:T(8,128)(2,1)} %copy-done.2, ...), custom_call_target="tpu_custom_call" | custom-call | flops 905969664 | bytes 9437184 | tf_op jit(solution)/shard_map/begin/pallas_call | solution.py:318
  91.3 3.6 %collective-permute-done.20.refs_0_ = bf16[192,1536]{1,0:T(8,128)(2,1)} collective-permute-done((bf16[192,1536]{1,0:T(8,128)(2,1)}, bf16[192,1536]{1,0:T(8,128)(2,1)}, u32[]{:S(2)}, u32[]{:S(2)}) %collective-permute-start.20) | collective-permute-done | bytes 589856 | tf_op jit(solution)/shard_map/ppermute | solution.py:374
  94.9 7.6 %finish.1 = bf16[192,3072]{1,0:T(8,128)(2,1)} custom-call(s32[1,6]{1,0:T(1,128)} %pattern.5, bf16[192,1536]{1,0:T(8,128)(2,1)} %q.5, f32[192,1536]{1,0:T(8,128)} %get-tuple-element.27.part, f32[192,128]{1,0:T(8,128)} %get-tuple-element.28.stats, f32[192,3072]{1,0:T(8,128)} %begin.1.so_far, bf16[192,1536]{1,0:T(8,128)(2,1)} %collective-permute-done.20.refs_0_, ...), custom_call_target="tpu_custom_call" | custom-call | flops 905969664 | bytes 8257536 | tf_op jit(solution)/shard_map/finish/pallas_call | solution.py:339
  (42 shorter events, 0.1 us)
Async XLA Ops:
  6.5 8.0 %copy-start.7 = (bf16[192,3072]{1,0:T(8,128)(2,1)S(1)}, bf16[192,3072]{1,0:T(8,128)(2,1)}, u32[]{:S(2)}) copy-start(bf16[192,3072]{1,0:T(8,128)(2,1)} %param.11) | copy-start | bytes 3538948
  6.5 79.3 %all-gather.3.cloned.1.call-start = ((), (), s32[]{:S(2)}) async-start(), calls=%async_computation | async-start | bytes 5308416 | tf_op jit(solution)/shard_map/all_gather | solution.py:486
  7.7 10.1 %collective-permute-start.11 = (bf16[1,96,1536]{2,1,0:T(8,128)(2,1)S(1)}, bf16[1,96,1536]{2,1,0:T(8,128)(2,1)S(1)}, u32[]{:S(2)}, u32[]{:S(2)}) collective-permute-start(bf16[1,96,1536]{2,1,0:T(8,128)(2,1)S(1)} %bitcast.21), channel_id=1, source_target_pairs={{0,2},{2,0},{1,3},{3,1},{4,6},{6,4},{5,7},{7,5},{8,10},{10,8},{9,1... | collective-permute-start | bytes 884744 | tf_op jit(solution)/shard_map/ppermute | solution.py:357
  9.8 13.9 %collective-permute-start.6 = (bf16[1,96,1536]{2,1,0:T(8,128)(2,1)S(1)}, bf16[1,96,1536]{2,1,0:T(8,128)(2,1)S(1)}, u32[]{:S(2)}, u32[]{:S(2)}) collective-permute-start(bf16[1,96,1536]{2,1,0:T(8,128)(2,1)S(1)} %bitcast.22), channel_id=1, source_target_pairs={{0,4},{4,0},{8,12},{12,8},{1,5},{5,1},{9,13},{13,9},{2,6},{6,2},{1... | collective-permute-start | bytes 884744 | tf_op jit(solution)/shard_map/ppermute | solution.py:357
  11.1 12.6 %collective-permute-start.4 = (bf16[1,96,1536]{2,1,0:T(8,128)(2,1)S(1)}, bf16[1,96,1536]{2,1,0:T(8,128)(2,1)S(1)}, u32[]{:S(2)}, u32[]{:S(2)}) collective-permute-start(bf16[1,96,1536]{2,1,0:T(8,128)(2,1)S(1)} %bitcast.23), channel_id=1, source_target_pairs={{0,8},{4,12},{8,0},{12,4},{1,9},{5,13},{9,1},{13,5},{2,10},{6,14},... | collective-permute-start | bytes 884744 | tf_op jit(solution)/shard_map/ppermute | solution.py:357
  17.6 7.1 %collective-permute-start.8 = (bf16[48,3072]{1,0:T(8,128)(2,1)S(1)}, bf16[48,3072]{1,0:T(8,128)(2,1)}, u32[]{:S(2)}, u32[]{:S(2)}) collective-permute-start(bf16[48,3072]{1,0:T(8,128)(2,1)S(1)} %get-tuple-element.34), channel_id=1, source_target_pairs={{0,2},{1,3},{2,0},{3,1},{4,6},{5,7},{6,4},{7,5},{8,10},{9,11},{10,... | collective-permute-start | bytes 884744 | tf_op jit(solution)/shard_map/ppermute | solution.py:357
  17.9 20.7 %copy-start = (bf16[2,96,1536]{2,1,0:T(8,128)(2,1)}, bf16[2,96,1536]{2,1,0:T(8,128)(2,1)S(1)}, u32[]{:S(2)}) copy-start(bf16[2,96,1536]{2,1,0:T(8,128)(2,1)S(1)} %pad_maximum_fusion.3.refs_1_.refs_3_) | copy-start | bytes 1769476
  17.9 14.5 %collective-permute-start.12 = (bf16[2,96,1536]{2,1,0:T(8,128)(2,1)S(1)}, bf16[2,96,1536]{2,1,0:T(8,128)(2,1)S(1)}, u32[]{:S(2)}, u32[]{:S(2)}) collective-permute-start(bf16[2,96,1536]{2,1,0:T(8,128)(2,1)S(1)} %pad_maximum_fusion.3.refs_1_.refs_3_), channel_id=1, source_target_pairs={{0,16},{16,0},{1,17},{17,1},{2,18},{18,2},{3,19},{19,3},{4,20},{20... | collective-permute-start | bytes 1769480 | tf_op jit(solution)/shard_map/ppermute | solution.py:357
  24.7 5.9 %collective-permute-start.9 = (bf16[1,96,1536]{2,1,0:T(8,128)(2,1)S(1)}, bf16[1,96,1536]{2,1,0:T(8,128)(2,1)S(1)}, u32[]{:S(2)}, u32[]{:S(2)}) collective-permute-start(bf16[1,96,1536]{2,1,0:T(8,128)(2,1)S(1)} %collective-permute-done.4), channel_id=1, source_target_pairs={{0,4},{4,0},{8,12},{12,8},{1,5},{5,1},{9,13},{13,9},{2,6},{6,2},{1... | collective-permute-start | bytes 884744 | tf_op jit(solution)/shard_map/ppermute | solution.py:357
  26.1 6.3 %collective-permute-start.10 = (bf16[1,96,1536]{2,1,0:T(8,128)(2,1)S(1)}, bf16[1,96,1536]{2,1,0:T(8,128)(2,1)S(1)}, u32[]{:S(2)}, u32[]{:S(2)}) collective-permute-start(bf16[1,96,1536]{2,1,0:T(8,128)(2,1)S(1)} %collective-permute-done.6), channel_id=1, source_target_pairs={{0,2},{2,0},{1,3},{3,1},{4,6},{6,4},{5,7},{7,5},{8,10},{10,8},{9,1... | collective-permute-start | bytes 884744 | tf_op jit(solution)/shard_map/ppermute | solution.py:357
  32.4 44.3 %copy-start.2 = (bf16[2,96,1536]{2,1,0:T(8,128)(2,1)}, bf16[2,96,1536]{2,1,0:T(8,128)(2,1)S(1)}, u32[]{:S(2)}) copy-start(bf16[2,96,1536]{2,1,0:T(8,128)(2,1)S(1)} %collective-permute-done.12.refs_3_.refs_5_) | copy-start | bytes 1769476
  32.4 6.3 %collective-permute-start = (bf16[192,1536]{1,0:T(8,128)(2,1)}, bf16[192,1536]{1,0:T(8,128)(2,1)S(1)}, u32[]{:S(2)}, u32[]{:S(2)}) collective-permute-start(bf16[192,1536]{1,0:T(8,128)(2,1)} %refs_0_.1), channel_id=1, source_target_pairs={{0,1},{1,0},{2,3},{3,2},{4,5},{5,4},{6,7},{7,6},{8,9},{9,8},{10,11... | collective-permute-start | bytes 1769480 | tf_op jit(solution)/shard_map/ppermute | solution.py:472
  35.6 4.4 %collective-permute-start.1 = (bf16[192,1536]{1,0:T(8,128)(2,1)}, bf16[192,1536]{1,0:T(8,128)(2,1)S(1)}, u32[]{:S(2)}, u32[]{:S(2)}) collective-permute-start(bf16[192,1536]{1,0:T(8,128)(2,1)} %refs_1_.1), channel_id=1, source_target_pairs={{0,1},{1,0},{2,3},{3,2},{4,5},{5,4},{6,7},{7,6},{8,9},{9,8},{10,11... | collective-permute-start | bytes 1769480 | tf_op jit(solution)/shard_map/ppermute | solution.py:472
  35.7 7.2 %collective-permute-start.13 = (bf16[2,96,1536]{2,1,0:T(8,128)(2,1)S(1)}, bf16[2,96,1536]{2,1,0:T(8,128)(2,1)S(1)}, u32[]{:S(2)}, u32[]{:S(2)}) collective-permute-start(bf16[2,96,1536]{2,1,0:T(8,128)(2,1)S(1)} %pad_maximum_fusion.3.refs_1_.refs_3_), channel_id=1, source_target_pairs={{0,1},{1,0},{2,3},{3,2},{4,5},{5,4},{6,7},{7,6},{8,9},{9,8},{10,11... | collective-permute-start | bytes 1769480 | tf_op jit(solution)/shard_map/ppermute | solution.py:357
  36.1 28.5 %collective-permute-start.5 = (bf16[192,1536]{1,0:T(8,128)(2,1)S(1)}, bf16[192,1536]{1,0:T(8,128)(2,1)S(1)}, u32[]{:S(2)}, u32[]{:S(2)}) collective-permute-start(bf16[192,1536]{1,0:T(8,128)(2,1)S(1)} %get-tuple-element.32), channel_id=1, source_target_pairs={{0,8},{8,0},{1,9},{9,1},{2,10},{10,2},{3,11},{11,3},{4,12},{12,4},... | collective-permute-start | bytes 1769480 | tf_op jit(solution)/shard_map/ppermute | solution.py:374
  38.0 27.5 %collective-permute-start.7 = (bf16[192,1536]{1,0:T(8,128)(2,1)S(1)}, bf16[192,1536]{1,0:T(8,128)(2,1)S(1)}, u32[]{:S(2)}, u32[]{:S(2)}) collective-permute-start(bf16[192,1536]{1,0:T(8,128)(2,1)S(1)} %get-tuple-element.32), channel_id=1, source_target_pairs={{0,4},{4,0},{1,5},{5,1},{2,6},{6,2},{3,7},{7,3},{8,12},{12,8},{9,1... | collective-permute-start | bytes 1769480 | tf_op jit(solution)/shard_map/ppermute | solution.py:374
  38.7 38.0 %copy-start.1 = (bf16[2,96,1536]{2,1,0:T(8,128)(2,1)}, bf16[2,96,1536]{2,1,0:T(8,128)(2,1)S(1)}, u32[]{:S(2)}) copy-start(bf16[2,96,1536]{2,1,0:T(8,128)(2,1)S(1)} %constant_dynamic-update-slice_fusion.refs_5_.refs_7_) | copy-start | bytes 1769476
  38.7 30.4 %copy-start.8 = (bf16[192,1536]{1,0:T(8,128)(2,1)}, bf16[192,1536]{1,0:T(8,128)(2,1)S(1)}, u32[]{:S(2)}) copy-start(bf16[192,1536]{1,0:T(8,128)(2,1)S(1)} %collective-permute-done.refs_2_) | copy-start | bytes 1769476
  38.7 27.0 %collective-permute-start.16 = (bf16[2,96,1536]{2,1,0:T(8,128)(2,1)S(1)}, bf16[2,96,1536]{2,1,0:T(8,128)(2,1)S(1)}, u32[]{:S(2)}, u32[]{:S(2)}) collective-permute-start(bf16[2,96,1536]{2,1,0:T(8,128)(2,1)S(1)} %constant_dynamic-update-slice_fusion.refs_5_.refs_7_), channel_id=1, source_target_pairs={{0,16},{16,0},{1,17},{17,1},{2,18},{18,2},{3,19},{19,3},{4,20},{20... | collective-permute-start | bytes 1769480 | tf_op jit(solution)/shard_map/ppermute | solution.py:357
  40.0 29.1 %copy-start.9 = (bf16[192,1536]{1,0:T(8,128)(2,1)}, bf16[192,1536]{1,0:T(8,128)(2,1)S(1)}, u32[]{:S(2)}) copy-start(bf16[192,1536]{1,0:T(8,128)(2,1)S(1)} %collective-permute-done.1.refs_3_) | copy-start | bytes 1769476
  40.0 26.0 %collective-permute-start.2 = (bf16[192,1536]{1,0:T(8,128)(2,1)}, bf16[192,1536]{1,0:T(8,128)(2,1)S(1)}, u32[]{:S(2)}, u32[]{:S(2)}) collective-permute-start(bf16[192,1536]{1,0:T(8,128)(2,1)} %refs_0_.1), channel_id=1, source_target_pairs={{1,2},{2,1},{5,6},{6,5},{9,10},{10,9},{13,14},{14,13},{17,18},{18,... | collective-permute-start | bytes 1769480 | tf_op jit(solution)/shard_map/ppermute | solution.py:474
  42.9 33.8 %copy-start.3 = (bf16[2,96,1536]{2,1,0:T(8,128)(2,1)}, bf16[2,96,1536]{2,1,0:T(8,128)(2,1)S(1)}, u32[]{:S(2)}) copy-start(bf16[2,96,1536]{2,1,0:T(8,128)(2,1)S(1)} %collective-permute-done.13.refs_2_.refs_4_) | copy-start | bytes 1769476
  42.9 23.5 %collective-permute-start.3 = (bf16[192,1536]{1,0:T(8,128)(2,1)}, bf16[192,1536]{1,0:T(8,128)(2,1)S(1)}, u32[]{:S(2)}, u32[]{:S(2)}) collective-permute-start(bf16[192,1536]{1,0:T(8,128)(2,1)} %refs_1_.1), channel_id=1, source_target_pairs={{1,2},{2,1},{5,6},{6,5},{9,10},{10,9},{13,14},{14,13},{17,18},{18,... | collective-permute-start | bytes 1769480 | tf_op jit(solution)/shard_map/ppermute | solution.py:474
  64.6 4.6 %copy-start.12 = (bf16[192,1536]{1,0:T(8,128)(2,1)}, bf16[192,1536]{1,0:T(8,128)(2,1)S(1)}, u32[]{:S(2)}) copy-start(bf16[192,1536]{1,0:T(8,128)(2,1)S(1)} %collective-permute-done.5.refs_0_) | copy-start | bytes 1769476
  64.6 3.9 %collective-permute-start.15 = (bf16[2,96,1536]{2,1,0:T(8,128)(2,1)S(1)}, bf16[2,96,1536]{2,1,0:T(8,128)(2,1)S(1)}, u32[]{:S(2)}, u32[]{:S(2)}) collective-permute-start(bf16[2,96,1536]{2,1,0:T(8,128)(2,1)S(1)} %constant_dynamic-update-slice_fusion.refs_5_.refs_7_), channel_id=1, source_target_pairs={{0,1},{1,0},{2,3},{3,2},{4,5},{5,4},{6,7},{7,6},{8,9},{9,8},{10,11... | collective-permute-start | bytes 1769480 | tf_op jit(solution)/shard_map/ppermute | solution.py:357
  65.5 3.7 %copy-start.13 = (bf16[192,1536]{1,0:T(8,128)(2,1)}, bf16[192,1536]{1,0:T(8,128)(2,1)S(1)}, u32[]{:S(2)}) copy-start(bf16[192,1536]{1,0:T(8,128)(2,1)S(1)} %collective-permute-done.7.refs_1_) | copy-start | bytes 1769476
  65.5 3.6 %collective-permute-start.14 = (bf16[2,96,1536]{2,1,0:T(8,128)(2,1)S(1)}, bf16[2,96,1536]{2,1,0:T(8,128)(2,1)S(1)}, u32[]{:S(2)}, u32[]{:S(2)}) collective-permute-start(bf16[2,96,1536]{2,1,0:T(8,128)(2,1)S(1)} %collective-permute-done.12.refs_3_.refs_5_), channel_id=1, source_target_pairs={{0,1},{1,0},{2,3},{3,2},{4,5},{5,4},{6,7},{7,6},{8,9},{9,8},{10,11... | collective-permute-start | bytes 1769480 | tf_op jit(solution)/shard_map/ppermute | solution.py:357
  65.7 11.1 %copy-start.4 = (bf16[2,96,1536]{2,1,0:T(8,128)(2,1)}, bf16[2,96,1536]{2,1,0:T(8,128)(2,1)S(1)}, u32[]{:S(2)}) copy-start(bf16[2,96,1536]{2,1,0:T(8,128)(2,1)S(1)} %collective-permute-done.16.refs_7_.refs_9_) | copy-start | bytes 1769476
  65.7 18.6 %collective-permute-start.17 = (bf16[2,96,1536]{2,1,0:T(8,128)(2,1)S(1)}, bf16[2,96,1536]{2,1,0:T(8,128)(2,1)}, u32[]{:S(2)}, u32[]{:S(2)}) collective-permute-start(bf16[2,96,1536]{2,1,0:T(8,128)(2,1)S(1)} %collective-permute-done.16.refs_7_.refs_9_), channel_id=1, source_target_pairs={{0,1},{1,0},{2,3},{3,2},{4,5},{5,4},{6,7},{7,6},{8,9},{9,8},{10,11... | collective-permute-start | bytes 1769480 | tf_op jit(solution)/shard_map/ppermute | solution.py:357
  66.0 3.2 %copy-start.10 = (bf16[192,1536]{1,0:T(8,128)(2,1)}, bf16[192,1536]{1,0:T(8,128)(2,1)S(1)}, u32[]{:S(2)}) copy-start(bf16[192,1536]{1,0:T(8,128)(2,1)S(1)} %collective-permute-done.2.refs_4_) | copy-start | bytes 1769476
  66.0 28.9 %collective-permute-start.20 = (bf16[192,1536]{1,0:T(8,128)(2,1)}, bf16[192,1536]{1,0:T(8,128)(2,1)}, u32[]{:S(2)}, u32[]{:S(2)}) collective-permute-start(bf16[192,1536]{1,0:T(8,128)(2,1)} %get-tuple-element.44), channel_id=1, source_target_pairs={{0,8},{8,0},{1,9},{9,1},{2,10},{10,2},{3,11},{11,3},{4,12},{12,4},... | collective-permute-start | bytes 1769480 | tf_op jit(solution)/shard_map/ppermute | solution.py:374
  66.4 2.7 %copy-start.11 = (bf16[192,1536]{1,0:T(8,128)(2,1)}, bf16[192,1536]{1,0:T(8,128)(2,1)S(1)}, u32[]{:S(2)}) copy-start(bf16[192,1536]{1,0:T(8,128)(2,1)S(1)} %collective-permute-done.3.refs_5_) | copy-start | bytes 1769476
  66.4 28.5 %collective-permute-start.21 = (bf16[192,1536]{1,0:T(8,128)(2,1)}, bf16[192,1536]{1,0:T(8,128)(2,1)}, u32[]{:S(2)}, u32[]{:S(2)}) collective-permute-start(bf16[192,1536]{1,0:T(8,128)(2,1)} %get-tuple-element.44), channel_id=1, source_target_pairs={{0,4},{4,0},{1,5},{5,1},{2,6},{6,2},{3,7},{7,3},{8,12},{12,8},{9,1... | collective-permute-start | bytes 1769480 | tf_op jit(solution)/shard_map/ppermute | solution.py:374
  68.5 8.3 %copy-start.5 = (bf16[2,96,1536]{2,1,0:T(8,128)(2,1)}, bf16[2,96,1536]{2,1,0:T(8,128)(2,1)S(1)}, u32[]{:S(2)}) copy-start(bf16[2,96,1536]{2,1,0:T(8,128)(2,1)S(1)} %collective-permute-done.15.refs_6_.refs_8_) | copy-start | bytes 1769476
  68.5 15.8 %collective-permute-start.19 = (bf16[48,3072]{1,0:T(8,128)(2,1)}, bf16[48,3072]{1,0:T(8,128)(2,1)S(1)}, u32[]{:S(2)}, u32[]{:S(2)}) collective-permute-start(bf16[48,3072]{1,0:T(8,128)(2,1)} %get-tuple-element.42), channel_id=1, source_target_pairs={{0,3},{1,2},{2,1},{3,0},{4,7},{5,6},{6,5},{7,4},{8,11},{9,10},{10,... | collective-permute-start | bytes 884744 | tf_op jit(solution)/shard_map/ppermute | solution.py:357
  69.2 7.6 %copy-start.6 = (bf16[2,96,1536]{2,1,0:T(8,128)(2,1)}, bf16[2,96,1536]{2,1,0:T(8,128)(2,1)S(1)}, u32[]{:S(2)}) copy-start(bf16[2,96,1536]{2,1,0:T(8,128)(2,1)S(1)} %collective-permute-done.14.refs_4_.refs_6_) | copy-start | bytes 1769476
  69.2 15.1 %collective-permute-start.18 = (bf16[48,3072]{1,0:T(8,128)(2,1)}, bf16[48,3072]{1,0:T(8,128)(2,1)}, u32[]{:S(2)}, u32[]{:S(2)}) collective-permute-start(bf16[48,3072]{1,0:T(8,128)(2,1)} %get-tuple-element.40), channel_id=1, source_target_pairs={{0,1},{1,0},{2,3},{3,2},{4,5},{5,4},{6,7},{7,6},{8,9},{9,8},{10,11... | collective-permute-start | bytes 884744 | tf_op jit(solution)/shard_map/ppermute | solution.py:357
  84.3 1.5 %copy-start.14 = (bf16[48,3072]{1,0:T(8,128)(2,1)}, bf16[48,3072]{1,0:T(8,128)(2,1)S(1)}, u32[]{:S(2)}) copy-start(bf16[48,3072]{1,0:T(8,128)(2,1)S(1)} %collective-permute-done.19.refs_12_) | copy-start | bytes 884740
Sparse Core Ops, SparseCore 0:
  32.5 53.2 all-gather.2

commit v18 on v17

--- a/solution.py
+++ b/solution.py
@@ -482,7 +482,7 @@
     for d in (1, grid_width - 1):
         control_parts[d] = swap(TILES, d)(after(control_sent[d], *[x for kv in early_near[1:] for x in kv]))
 
-    gates = [*control_parts[2:-1], near_x, held[1]]
+    gates = [*control_parts[2:-1], near_x, held[1], crossed[0]]
     weight = [lax.all_gather(after(jnp.concatenate([far, last]), *gates), ("groups", "pair", "core"))]
     n = len(line_flips)
     moves = [

time: 110 us -> 111 us (level)
    ppermute x14, starting transfers between devices: 12.9 us -> 14.9 us  [flipped(): lax.ppermute(block, axis, [(i, i ^ flip) for i in range(lax.axis_size(axi...]
where the time goes in v18:
time: 111 us; the launch traced here: 110 us
  waiting for transfers between devices  36.6 us (33%)
  starting transfers between devices  27.4 us (25%)
  Pallas kernels  25.1 us (23%)
  between operations  13.7 us (12%)
  other arithmetic  4.05 us (4%)
  local copies, waits for them, and re-layouts  3.23 us (3%)
    ppermute x4, waiting for transfers between devices, route_of(): return lambda block: lax.ppermute(block, TILES, route)  21.7 us
    ppermute x14, starting transfers between devices, flipped(): lax.ppermute(block, axis, [(i, i ^ flip) for i in range(lax.axis_size(axi...  14.9 us
    ppermute x14, waiting for transfers between devices, flipped(): lax.ppermute(block, axis, [(i, i ^ flip) for i in range(lax.axis_size(axi...  13 us
    pallas_call x1, Pallas kernels, finish(): pl.pallas_call(functools.partial(finish_kernel, which, len(weight), moves...  7.6 us
    pallas_call x1, Pallas kernels, attend(): pl.pallas_call(functools.partial(attend_kernel, which), out_shape=[jax.Sh...  7.38 us
    ppermute x2, starting transfers between devices, on_device(): lax.ppermute(after(x, early_near[0][i]), TILES, early[slot][2])  5.59 us
    pallas_call x1, Pallas kernels, begin(): pl.pallas_call(functools.partial(begin_kernel, (len(weight), len(control)...  5.57 us
    ppermute x4, starting transfers between devices, route_of(): return lambda block: lax.ppermute(block, TILES, route)  4.64 us
  transfers between devices with their start and end apart: 23, of which 8 were waited for; matrix products, arithmetic and copies ran while one was open for 5% of the time, Pallas kernels for 16%

profile of v18, /device:TPU:1, one launch (start us, length us, event | category | flops | bytes accessed | tf_op | source)
XLA Modules:
  0.0 110.0 jit_solution(6663226784197412089)
XLA Ops:
  6.5 1.2 %slice_select_fusion = bf16[96,1536]{1,0:T(8,128)(2,1)S(1)} fusion(bf16[96,3072]{1,0:T(8,128)(2,1)} %param.12, pred[]{:T(512)S(6)} %eq.3), kind=kLoop, calls=%fused_computation.8 | loop fusion | flops 147456 | bytes 884737 | tf_op jit(solution)/shard_map/jit(_where)/select_n | solution.py:438
  7.7 2.1 %collective-permute-start.11 = (bf16[1,96,1536]{2,1,0:T(8,128)(2,1)S(1)}, bf16[1,96,1536]{2,1,0:T(8,128)(2,1)S(1)}, u32[]{:S(2)}, u32[]{:S(2)}) collective-permute-start(bf16[1,96,1536]{2,1,0:T(8,128)(2,1)S(1)} %bitcast.21), channel_id=1, source_target_pairs={{0,2},{2,0},{1,3},{3,1},{4,6},{6,4},{5,7},{7,5},{8,10},{10,8},{9,1... | collective-permute-start | bytes 884744 | tf_op jit(solution)/shard_map/ppermute | solution.py:357
  9.8 1.3 %collective-permute-start.6 = (bf16[1,96,1536]{2,1,0:T(8,128)(2,1)S(1)}, bf16[1,96,1536]{2,1,0:T(8,128)(2,1)S(1)}, u32[]{:S(2)}, u32[]{:S(2)}) collective-permute-start(bf16[1,96,1536]{2,1,0:T(8,128)(2,1)S(1)} %bitcast.22), channel_id=1, source_target_pairs={{0,4},{4,0},{8,12},{12,8},{1,5},{5,1},{9,13},{13,9},{2,6},{6,2},{1... | collective-permute-start | bytes 884744 | tf_op jit(solution)/shard_map/ppermute | solution.py:357
  11.1 2.3 %collective-permute-start.4 = (bf16[1,96,1536]{2,1,0:T(8,128)(2,1)S(1)}, bf16[1,96,1536]{2,1,0:T(8,128)(2,1)}, u32[]{:S(2)}, u32[]{:S(2)}) collective-permute-start(bf16[1,96,1536]{2,1,0:T(8,128)(2,1)S(1)} %bitcast.23), channel_id=1, source_target_pairs={{0,8},{4,12},{8,0},{12,4},{1,9},{5,13},{9,1},{13,5},{2,10},{6,14},... | collective-permute-start | bytes 884744 | tf_op jit(solution)/shard_map/ppermute | solution.py:357
  13.4 1.1 fusion
  14.6 1.0 dynamic-slice_bitcast_fusion
  15.5 1.1 fusion.1
  16.6 1.0 pad_maximum_fusion
  17.6 0.3 collective-permute-start.8
  17.8 0.0 collective-permute-done.11
  17.8 0.1 pad_maximum_fusion.3.refs_1_.refs_3_
  17.9 1.9 %collective-permute-start.13 = (bf16[2,96,1536]{2,1,0:T(8,128)(2,1)S(1)}, bf16[2,96,1536]{2,1,0:T(8,128)(2,1)S(1)}, u32[]{:S(2)}, u32[]{:S(2)}) collective-permute-start(bf16[2,96,1536]{2,1,0:T(8,128)(2,1)S(1)} %pad_maximum_fusion.3.refs_1_.refs_3_), channel_id=1, source_target_pairs={{0,1},{1,0},{2,3},{3,2},{4,5},{5,4},{6,7},{7,6},{8,9},{9,8},{10,11... | collective-permute-start | bytes 1769480 | tf_op jit(solution)/shard_map/ppermute | solution.py:357
  19.7 1.3 %collective-permute-start.12 = (bf16[2,96,1536]{2,1,0:T(8,128)(2,1)S(1)}, bf16[2,96,1536]{2,1,0:T(8,128)(2,1)S(1)}, u32[]{:S(2)}, u32[]{:S(2)}) collective-permute-start(bf16[2,96,1536]{2,1,0:T(8,128)(2,1)S(1)} %pad_maximum_fusion.3.refs_1_.refs_3_), channel_id=1, source_target_pairs={{0,16},{16,0},{1,17},{17,1},{2,18},{18,2},{3,19},{19,3},{4,20},{20... | collective-permute-start | bytes 1769480 | tf_op jit(solution)/shard_map/ppermute | solution.py:357
  21.0 2.7 %collective-permute-done.6 = bf16[1,96,1536]{2,1,0:T(8,128)(2,1)S(1)} collective-permute-done((bf16[1,96,1536]{2,1,0:T(8,128)(2,1)S(1)}, bf16[1,96,1536]{2,1,0:T(8,128)(2,1)S(1)}, u32[]{:S(2)}, u32[]{:S(2)}) %collective-permute-start.6) | collective-permute-done | bytes 294944 | tf_op jit(solution)/shard_map/ppermute | solution.py:357
  23.7 0.0 collective-permute-done.4
  23.7 0.9 collective-permute-done.8.refs_11_
  24.6 1.5 %collective-permute-start.9 = (bf16[1,96,1536]{2,1,0:T(8,128)(2,1)}, bf16[1,96,1536]{2,1,0:T(8,128)(2,1)S(1)}, u32[]{:S(2)}, u32[]{:S(2)}) collective-permute-start(bf16[1,96,1536]{2,1,0:T(8,128)(2,1)} %collective-permute-done.4), channel_id=1, source_target_pairs={{0,4},{4,0},{8,12},{12,8},{1,5},{5,1},{9,13},{13,9},{2,6},{6,2},{1... | collective-permute-start | bytes 884744 | tf_op jit(solution)/shard_map/ppermute | solution.py:357
  26.2 0.3 collective-permute-start.10
  26.4 4.4 %collective-permute-done.9 = bf16[1,96,1536]{2,1,0:T(8,128)(2,1)S(1)} collective-permute-done((bf16[1,96,1536]{2,1,0:T(8,128)(2,1)}, bf16[1,96,1536]{2,1,0:T(8,128)(2,1)S(1)}, u32[]{:S(2)}, u32[]{:S(2)}) %collective-permute-start.9) | collective-permute-done | bytes 294944 | tf_op jit(solution)/shard_map/ppermute | solution.py:357
  30.9 1.9 %pad_maximum_fusion.2 = bf16[2,96,1536]{2,1,0:T(8,128)(2,1)} fusion(bf16[1,96,1536]{2,1,0:T(8,128)(2,1)S(1)} %collective-permute-done.9, bf16[1,96,1536]{2,1,0:T(8,128)(2,1)} %collective-permute-done.4), kind=kLoop, calls=%fused_computation.2 | loop fusion | flops 294912 | bytes 1179648 | tf_op jit(solution)/shard_map/concatenate | solution.py:486
  32.7 0.0 collective-permute-done.13.refs_2_.refs_4_
  32.7 1.9 %collective-permute-done.12.refs_3_.refs_5_ = bf16[2,96,1536]{2,1,0:T(8,128)(2,1)S(1)} collective-permute-done((bf16[2,96,1536]{2,1,0:T(8,128)(2,1)S(1)}, bf16[2,96,1536]{2,1,0:T(8,128)(2,1)S(1)}, u32[]{:S(2)}, u32[]{:S(2)}) %collective-permute-start.12) | collective-permute-done | bytes 589856 | tf_op jit(solution)/shard_map/ppermute | solution.py:357
  34.7 0.0 all-gather.3.cloned.1.call-update
  34.7 2.2 %collective-permute-start = (bf16[192,1536]{1,0:T(8,128)(2,1)}, bf16[192,1536]{1,0:T(8,128)(2,1)S(1)}, u32[]{:S(2)}, u32[]{:S(2)}) collective-permute-start(bf16[192,1536]{1,0:T(8,128)(2,1)} %refs_0_.1), channel_id=1, source_target_pairs={{0,1},{1,0},{2,3},{3,2},{4,5},{5,4},{6,7},{7,6},{8,9},{9,8},{10,11... | collective-permute-start | bytes 1769480 | tf_op jit(solution)/shard_map/ppermute | solution.py:472
  36.8 0.1 collective-permute-start.1
  36.9 0.8 collective-permute-start.5
  37.8 1.7 %collective-permute-start.7 = (bf16[192,1536]{1,0:T(8,128)(2,1)S(1)}, bf16[192,1536]{1,0:T(8,128)(2,1)S(1)}, u32[]{:S(2)}, u32[]{:S(2)}) collective-permute-start(bf16[192,1536]{1,0:T(8,128)(2,1)S(1)} %get-tuple-element.32), channel_id=1, source_target_pairs={{0,4},{4,0},{1,5},{5,1},{2,6},{6,2},{3,7},{7,3},{8,12},{12,8},{9,1... | collective-permute-start | bytes 1769480 | tf_op jit(solution)/shard_map/ppermute | solution.py:374
  39.5 1.3 %collective-permute-start.16 = (bf16[2,96,1536]{2,1,0:T(8,128)(2,1)S(1)}, bf16[2,96,1536]{2,1,0:T(8,128)(2,1)S(1)}, u32[]{:S(2)}, u32[]{:S(2)}) collective-permute-start(bf16[2,96,1536]{2,1,0:T(8,128)(2,1)S(1)} %constant_dynamic-update-slice_fusion.refs_5_.refs_7_), channel_id=1, source_target_pairs={{0,16},{16,0},{1,17},{17,1},{2,18},{18,2},{3,19},{19,3},{4,20},{20... | collective-permute-start | bytes 1769480 | tf_op jit(solution)/shard_map/ppermute | solution.py:357
  40.8 0.0 collective-permute-done.refs_2_
  40.8 3.7 %collective-permute-start.2 = (bf16[192,1536]{1,0:T(8,128)(2,1)}, bf16[192,1536]{1,0:T(8,128)(2,1)S(1)}, u32[]{:S(2)}, u32[]{:S(2)}) collective-permute-start(bf16[192,1536]{1,0:T(8,128)(2,1)} %refs_0_.1), channel_id=1, source_target_pairs={{1,2},{2,1},{5,6},{6,5},{9,10},{10,9},{13,14},{14,13},{17,18},{18,... | collective-permute-start | bytes 1769480 | tf_op jit(solution)/shard_map/ppermute | solution.py:474
  44.5 1.9 %collective-permute-start.3 = (bf16[192,1536]{1,0:T(8,128)(2,1)}, bf16[192,1536]{1,0:T(8,128)(2,1)S(1)}, u32[]{:S(2)}, u32[]{:S(2)}) collective-permute-start(bf16[192,1536]{1,0:T(8,128)(2,1)} %refs_1_.1), channel_id=1, source_target_pairs={{1,2},{2,1},{5,6},{6,5},{9,10},{10,9},{13,14},{14,13},{17,18},{18,... | collective-permute-start | bytes 1769480 | tf_op jit(solution)/shard_map/ppermute | solution.py:474
  46.5 18.7 %collective-permute-done.5.refs_0_ = bf16[192,1536]{1,0:T(8,128)(2,1)} collective-permute-done((bf16[192,1536]{1,0:T(8,128)(2,1)S(1)}, bf16[192,1536]{1,0:T(8,128)(2,1)}, u32[]{:S(2)}, u32[]{:S(2)}) %collective-permute-start.5) | collective-permute-done | bytes 589856 | tf_op jit(solution)/shard_map/ppermute | solution.py:374
  65.2 1.1 %collective-permute-start.15 = (bf16[2,96,1536]{2,1,0:T(8,128)(2,1)S(1)}, bf16[2,96,1536]{2,1,0:T(8,128)(2,1)S(1)}, u32[]{:S(2)}, u32[]{:S(2)}) collective-permute-start(bf16[2,96,1536]{2,1,0:T(8,128)(2,1)S(1)} %constant_dynamic-update-slice_fusion.refs_5_.refs_7_), channel_id=1, source_target_pairs={{0,1},{1,0},{2,3},{3,2},{4,5},{5,4},{6,7},{7,6},{8,9},{9,8},{10,11... | collective-permute-start | bytes 1769480 | tf_op jit(solution)/shard_map/ppermute | solution.py:357
  66.3 0.1 collective-permute-start.14
  66.4 0.4 collective-permute-start.17
  66.8 0.5 collective-permute-start.20
  67.3 1.7 %collective-permute-start.21 = (bf16[192,1536]{1,0:T(8,128)(2,1)}, bf16[192,1536]{1,0:T(8,128)(2,1)}, u32[]{:S(2)}, u32[]{:S(2)}) collective-permute-start(bf16[192,1536]{1,0:T(8,128)(2,1)} %get-tuple-element.44), channel_id=1, source_target_pairs={{0,4},{4,0},{1,5},{5,1},{2,6},{6,2},{3,7},{7,3},{8,12},{12,8},{9,1... | collective-permute-start | bytes 1769480 | tf_op jit(solution)/shard_map/ppermute | solution.py:374
  69.0 0.0 collective-permute-done.15.refs_6_.refs_8_
  69.0 0.9 collective-permute-start.19
  69.9 0.2 collective-permute-start.18
  70.1 7.4 %attend.1 = (f32[192,1536]{1,0:T(8,128)}, f32[192,128]{1,0:T(8,128)}) custom-call(s32[1,6]{1,0:T(1,128)} %pattern.5, bf16[192,1536]{1,0:T(8,128)(2,1)} %q.5, bf16[192,1536]{1,0:T(8,128)(2,1)} %refs_0_.1, bf16[192,1536]{1,0:T(8,128)(2,1)} %refs_1_.1, bf16[192,1536]{1,0:T(8,128)(2,1)} %copy-done.8, bf16[192,1536]{1,0:T(8,128)(2,1)} %copy-done.9, ...), custom_call_target="tpu_custom_call" | custom-call | flops 1019215872 | bytes 5308416 | tf_op jit(solution)/shard_map/attend/pallas_call | solution.py:104
  77.6 4.5 %close.1.ready = bf16[192,768]{1,0:T(8,128)(2,1)} custom-call(s32[1,6]{1,0:T(1,128)} %pattern.5, bf16[192,1536]{1,0:T(8,128)(2,1)} %q.5, f32[192,1536]{1,0:T(8,128)} %get-tuple-element.27.part, f32[192,128]{1,0:T(8,128)} %get-tuple-element.28.stats, bf16[192,1536]{1,0:T(8,128)(2,1)} %collective-permute-done.5.refs_0_, bf16[192,1536]{1,0:T(8,128)(2,1)} %copy-done.12), custom_call_target="tpu_custom_call" | custom-call | flops 339738624 | bytes 2359296 | tf_op jit(solution)/shard_map/close/pallas_call | solution.py:179
  82.1 3.0 %collective-permute-done.19.refs_12_ = bf16[48,3072]{1,0:T(8,128)(2,1)} collective-permute-done((bf16[48,3072]{1,0:T(8,128)(2,1)}, bf16[48,3072]{1,0:T(8,128)(2,1)}, u32[]{:S(2)}, u32[]{:S(2)}) %collective-permute-start.19) | collective-permute-done | bytes 294944 | tf_op jit(solution)/shard_map/ppermute | solution.py:357
  85.1 0.0 collective-permute-done.17.refs_8_.refs_10_
  85.1 1.8 %all-gather.3.cloned.1.call-done = bf16[16,96,1536]{2,1,0:T(8,128)(2,1)} async-done(((bf16[2,96,1536]{2,1,0:T(8,128)(2,1)}), bf16[16,96,1536]{2,1,0:T(8,128)(2,1)}) %all-gather.3.cloned.1.call-update) | async-done | bytes 4718608 | tf_op jit(solution)/shard_map/all_gather | solution.py:486
  86.9 5.6 %begin.1.so_far = f32[192,3072]{1,0:T(8,128)} custom-call(bf16[192,3072]{1,0:T(8,128)(2,1)} %hidden.1, bf16[192,768]{1,0:T(8,128)(2,1)} %close.1.ready, bf16[8,2,96,1536]{3,2,1,0:T(8,128)(2,1)} %bitcast.19, bf16[2,96,1536]{2,1,0:T(8,128)(2,1)} %copy-done, bf16[2,96,1536]{2,1,0:T(8,128)(2,1)} %copy-done.2, bf16[2,96,1536]{2,1,0:T(8,128)(2,1)} %copy-done.3, ...), custom_call_target="tpu_custom_call" | custom-call | flops 905969664 | bytes 9437184 | tf_op jit(solution)/shard_map/begin/pallas_call | solution.py:318
  92.5 3.0 %collective-permute-done.20.refs_0_ = bf16[192,1536]{1,0:T(8,128)(2,1)} collective-permute-done((bf16[192,1536]{1,0:T(8,128)(2,1)}, bf16[192,1536]{1,0:T(8,128)(2,1)}, u32[]{:S(2)}, u32[]{:S(2)}) %collective-permute-start.20) | collective-permute-done | bytes 589856 | tf_op jit(solution)/shard_map/ppermute | solution.py:374
  95.5 7.6 %finish.1 = bf16[192,3072]{1,0:T(8,128)(2,1)} custom-call(s32[1,6]{1,0:T(1,128)} %pattern.5, bf16[192,1536]{1,0:T(8,128)(2,1)} %q.5, f32[192,1536]{1,0:T(8,128)} %get-tuple-element.27.part, f32[192,128]{1,0:T(8,128)} %get-tuple-element.28.stats, f32[192,3072]{1,0:T(8,128)} %begin.1.so_far, bf16[192,1536]{1,0:T(8,128)(2,1)} %collective-permute-done.20.refs_0_, ...), custom_call_target="tpu_custom_call" | custom-call | flops 905969664 | bytes 8257536 | tf_op jit(solution)/shard_map/finish/pallas_call | solution.py:339
  (40 shorter events, 0.1 us)
Async XLA Ops:
  6.5 8.0 %copy-start.7 = (bf16[192,3072]{1,0:T(8,128)(2,1)S(1)}, bf16[192,3072]{1,0:T(8,128)(2,1)}, u32[]{:S(2)}) copy-start(bf16[192,3072]{1,0:T(8,128)(2,1)} %param.11) | copy-start | bytes 3538948
  6.5 80.4 %all-gather.3.cloned.1.call-start = ((), (), s32[]{:S(2)}) async-start(), calls=%async_computation | async-start | bytes 5308416 | tf_op jit(solution)/shard_map/all_gather | solution.py:486
  7.7 10.1 %collective-permute-start.11 = (bf16[1,96,1536]{2,1,0:T(8,128)(2,1)S(1)}, bf16[1,96,1536]{2,1,0:T(8,128)(2,1)S(1)}, u32[]{:S(2)}, u32[]{:S(2)}) collective-permute-start(bf16[1,96,1536]{2,1,0:T(8,128)(2,1)S(1)} %bitcast.21), channel_id=1, source_target_pairs={{0,2},{2,0},{1,3},{3,1},{4,6},{6,4},{5,7},{7,5},{8,10},{10,8},{9,1... | collective-permute-start | bytes 884744 | tf_op jit(solution)/shard_map/ppermute | solution.py:357
  9.8 13.9 %collective-permute-start.6 = (bf16[1,96,1536]{2,1,0:T(8,128)(2,1)S(1)}, bf16[1,96,1536]{2,1,0:T(8,128)(2,1)S(1)}, u32[]{:S(2)}, u32[]{:S(2)}) collective-permute-start(bf16[1,96,1536]{2,1,0:T(8,128)(2,1)S(1)} %bitcast.22), channel_id=1, source_target_pairs={{0,4},{4,0},{8,12},{12,8},{1,5},{5,1},{9,13},{13,9},{2,6},{6,2},{1... | collective-permute-start | bytes 884744 | tf_op jit(solution)/shard_map/ppermute | solution.py:357
  11.1 12.6 %collective-permute-start.4 = (bf16[1,96,1536]{2,1,0:T(8,128)(2,1)S(1)}, bf16[1,96,1536]{2,1,0:T(8,128)(2,1)}, u32[]{:S(2)}, u32[]{:S(2)}) collective-permute-start(bf16[1,96,1536]{2,1,0:T(8,128)(2,1)S(1)} %bitcast.23), channel_id=1, source_target_pairs={{0,8},{4,12},{8,0},{12,4},{1,9},{5,13},{9,1},{13,5},{2,10},{6,14},... | collective-permute-start | bytes 884744 | tf_op jit(solution)/shard_map/ppermute | solution.py:357
  17.6 7.1 %collective-permute-start.8 = (bf16[48,3072]{1,0:T(8,128)(2,1)S(1)}, bf16[48,3072]{1,0:T(8,128)(2,1)S(1)}, u32[]{:S(2)}, u32[]{:S(2)}) collective-permute-start(bf16[48,3072]{1,0:T(8,128)(2,1)S(1)} %get-tuple-element.34), channel_id=1, source_target_pairs={{0,2},{1,3},{2,0},{3,1},{4,6},{5,7},{6,4},{7,5},{8,10},{9,11},{10,... | collective-permute-start | bytes 884744 | tf_op jit(solution)/shard_map/ppermute | solution.py:357
  17.9 21.6 %copy-start = (bf16[2,96,1536]{2,1,0:T(8,128)(2,1)}, bf16[2,96,1536]{2,1,0:T(8,128)(2,1)S(1)}, u32[]{:S(2)}) copy-start(bf16[2,96,1536]{2,1,0:T(8,128)(2,1)S(1)} %pad_maximum_fusion.3.refs_1_.refs_3_) | copy-start | bytes 1769476
  17.9 14.9 %collective-permute-start.13 = (bf16[2,96,1536]{2,1,0:T(8,128)(2,1)S(1)}, bf16[2,96,1536]{2,1,0:T(8,128)(2,1)S(1)}, u32[]{:S(2)}, u32[]{:S(2)}) collective-permute-start(bf16[2,96,1536]{2,1,0:T(8,128)(2,1)S(1)} %pad_maximum_fusion.3.refs_1_.refs_3_), channel_id=1, source_target_pairs={{0,1},{1,0},{2,3},{3,2},{4,5},{5,4},{6,7},{7,6},{8,9},{9,8},{10,11... | collective-permute-start | bytes 1769480 | tf_op jit(solution)/shard_map/ppermute | solution.py:357
  19.7 14.9 %collective-permute-start.12 = (bf16[2,96,1536]{2,1,0:T(8,128)(2,1)S(1)}, bf16[2,96,1536]{2,1,0:T(8,128)(2,1)S(1)}, u32[]{:S(2)}, u32[]{:S(2)}) collective-permute-start(bf16[2,96,1536]{2,1,0:T(8,128)(2,1)S(1)} %pad_maximum_fusion.3.refs_1_.refs_3_), channel_id=1, source_target_pairs={{0,16},{16,0},{1,17},{17,1},{2,18},{18,2},{3,19},{19,3},{4,20},{20... | collective-permute-start | bytes 1769480 | tf_op jit(solution)/shard_map/ppermute | solution.py:357
  24.6 13.1 %copy-start.13 = (bf16[48,3072]{1,0:T(8,128)(2,1)}, bf16[48,3072]{1,0:T(8,128)(2,1)S(1)}, u32[]{:S(2)}) copy-start(bf16[48,3072]{1,0:T(8,128)(2,1)S(1)} %collective-permute-done.8.refs_11_) | copy-start | bytes 884740
  24.6 6.2 %collective-permute-start.9 = (bf16[1,96,1536]{2,1,0:T(8,128)(2,1)}, bf16[1,96,1536]{2,1,0:T(8,128)(2,1)S(1)}, u32[]{:S(2)}, u32[]{:S(2)}) collective-permute-start(bf16[1,96,1536]{2,1,0:T(8,128)(2,1)} %collective-permute-done.4), channel_id=1, source_target_pairs={{0,4},{4,0},{8,12},{12,8},{1,5},{5,1},{9,13},{13,9},{2,6},{6,2},{1... | collective-permute-start | bytes 884744 | tf_op jit(solution)/shard_map/ppermute | solution.py:357
  26.2 6.6 %collective-permute-start.10 = (bf16[1,96,1536]{2,1,0:T(8,128)(2,1)S(1)}, bf16[1,96,1536]{2,1,0:T(8,128)(2,1)S(1)}, u32[]{:S(2)}, u32[]{:S(2)}) collective-permute-start(bf16[1,96,1536]{2,1,0:T(8,128)(2,1)S(1)} %collective-permute-done.6), channel_id=1, source_target_pairs={{0,2},{2,0},{1,3},{3,1},{4,6},{6,4},{5,7},{7,5},{8,10},{10,8},{9,1... | collective-permute-start | bytes 884744 | tf_op jit(solution)/shard_map/ppermute | solution.py:357
  32.7 44.8 %copy-start.2 = (bf16[2,96,1536]{2,1,0:T(8,128)(2,1)}, bf16[2,96,1536]{2,1,0:T(8,128)(2,1)S(1)}, u32[]{:S(2)}) copy-start(bf16[2,96,1536]{2,1,0:T(8,128)(2,1)S(1)} %collective-permute-done.13.refs_2_.refs_4_) | copy-start | bytes 1769476
  34.7 42.9 %copy-start.3 = (bf16[2,96,1536]{2,1,0:T(8,128)(2,1)}, bf16[2,96,1536]{2,1,0:T(8,128)(2,1)S(1)}, u32[]{:S(2)}) copy-start(bf16[2,96,1536]{2,1,0:T(8,128)(2,1)S(1)} %collective-permute-done.12.refs_3_.refs_5_) | copy-start | bytes 1769476
  34.7 6.2 %collective-permute-start = (bf16[192,1536]{1,0:T(8,128)(2,1)}, bf16[192,1536]{1,0:T(8,128)(2,1)S(1)}, u32[]{:S(2)}, u32[]{:S(2)}) collective-permute-start(bf16[192,1536]{1,0:T(8,128)(2,1)} %refs_0_.1), channel_id=1, source_target_pairs={{0,1},{1,0},{2,3},{3,2},{4,5},{5,4},{6,7},{7,6},{8,9},{9,8},{10,11... | collective-permute-start | bytes 1769480 | tf_op jit(solution)/shard_map/ppermute | solution.py:472
  36.8 7.7 %collective-permute-start.1 = (bf16[192,1536]{1,0:T(8,128)(2,1)}, bf16[192,1536]{1,0:T(8,128)(2,1)S(1)}, u32[]{:S(2)}, u32[]{:S(2)}) collective-permute-start(bf16[192,1536]{1,0:T(8,128)(2,1)} %refs_1_.1), channel_id=1, source_target_pairs={{0,1},{1,0},{2,3},{3,2},{4,5},{5,4},{6,7},{7,6},{8,9},{9,8},{10,11... | collective-permute-start | bytes 1769480 | tf_op jit(solution)/shard_map/ppermute | solution.py:472
  36.9 28.2 %collective-permute-start.5 = (bf16[192,1536]{1,0:T(8,128)(2,1)S(1)}, bf16[192,1536]{1,0:T(8,128)(2,1)}, u32[]{:S(2)}, u32[]{:S(2)}) collective-permute-start(bf16[192,1536]{1,0:T(8,128)(2,1)S(1)} %get-tuple-element.32), channel_id=1, source_target_pairs={{0,8},{8,0},{1,9},{9,1},{2,10},{10,2},{3,11},{11,3},{4,12},{12,4},... | collective-permute-start | bytes 1769480 | tf_op jit(solution)/shard_map/ppermute | solution.py:374
  37.8 28.6 %collective-permute-start.7 = (bf16[192,1536]{1,0:T(8,128)(2,1)S(1)}, bf16[192,1536]{1,0:T(8,128)(2,1)S(1)}, u32[]{:S(2)}, u32[]{:S(2)}) collective-permute-start(bf16[192,1536]{1,0:T(8,128)(2,1)S(1)} %get-tuple-element.32), channel_id=1, source_target_pairs={{0,4},{4,0},{1,5},{5,1},{2,6},{6,2},{3,7},{7,3},{8,12},{12,8},{9,1... | collective-permute-start | bytes 1769480 | tf_op jit(solution)/shard_map/ppermute | solution.py:374
  39.5 38.0 %copy-start.1 = (bf16[2,96,1536]{2,1,0:T(8,128)(2,1)}, bf16[2,96,1536]{2,1,0:T(8,128)(2,1)S(1)}, u32[]{:S(2)}) copy-start(bf16[2,96,1536]{2,1,0:T(8,128)(2,1)S(1)} %constant_dynamic-update-slice_fusion.refs_5_.refs_7_) | copy-start | bytes 1769476
  39.5 26.9 %collective-permute-start.16 = (bf16[2,96,1536]{2,1,0:T(8,128)(2,1)S(1)}, bf16[2,96,1536]{2,1,0:T(8,128)(2,1)S(1)}, u32[]{:S(2)}, u32[]{:S(2)}) collective-permute-start(bf16[2,96,1536]{2,1,0:T(8,128)(2,1)S(1)} %constant_dynamic-update-slice_fusion.refs_5_.refs_7_), channel_id=1, source_target_pairs={{0,16},{16,0},{1,17},{17,1},{2,18},{18,2},{3,19},{19,3},{4,20},{20... | collective-permute-start | bytes 1769480 | tf_op jit(solution)/shard_map/ppermute | solution.py:357
  40.8 29.1 %copy-start.8 = (bf16[192,1536]{1,0:T(8,128)(2,1)}, bf16[192,1536]{1,0:T(8,128)(2,1)S(1)}, u32[]{:S(2)}) copy-start(bf16[192,1536]{1,0:T(8,128)(2,1)S(1)} %collective-permute-done.refs_2_) | copy-start | bytes 1769476
  40.8 26.0 %collective-permute-start.2 = (bf16[192,1536]{1,0:T(8,128)(2,1)}, bf16[192,1536]{1,0:T(8,128)(2,1)S(1)}, u32[]{:S(2)}, u32[]{:S(2)}) collective-permute-start(bf16[192,1536]{1,0:T(8,128)(2,1)} %refs_0_.1), channel_id=1, source_target_pairs={{1,2},{2,1},{5,6},{6,5},{9,10},{10,9},{13,14},{14,13},{17,18},{18,... | collective-permute-start | bytes 1769480 | tf_op jit(solution)/shard_map/ppermute | solution.py:474
  44.5 25.4 %copy-start.9 = (bf16[192,1536]{1,0:T(8,128)(2,1)}, bf16[192,1536]{1,0:T(8,128)(2,1)S(1)}, u32[]{:S(2)}) copy-start(bf16[192,1536]{1,0:T(8,128)(2,1)S(1)} %collective-permute-done.1.refs_3_) | copy-start | bytes 1769476
  44.5 22.8 %collective-permute-start.3 = (bf16[192,1536]{1,0:T(8,128)(2,1)}, bf16[192,1536]{1,0:T(8,128)(2,1)S(1)}, u32[]{:S(2)}, u32[]{:S(2)}) collective-permute-start(bf16[192,1536]{1,0:T(8,128)(2,1)} %refs_1_.1), channel_id=1, source_target_pairs={{1,2},{2,1},{5,6},{6,5},{9,10},{10,9},{13,14},{14,13},{17,18},{18,... | collective-permute-start | bytes 1769480 | tf_op jit(solution)/shard_map/ppermute | solution.py:474
  65.2 3.8 %collective-permute-start.15 = (bf16[2,96,1536]{2,1,0:T(8,128)(2,1)S(1)}, bf16[2,96,1536]{2,1,0:T(8,128)(2,1)S(1)}, u32[]{:S(2)}, u32[]{:S(2)}) collective-permute-start(bf16[2,96,1536]{2,1,0:T(8,128)(2,1)S(1)} %constant_dynamic-update-slice_fusion.refs_5_.refs_7_), channel_id=1, source_target_pairs={{0,1},{1,0},{2,3},{3,2},{4,5},{5,4},{6,7},{7,6},{8,9},{9,8},{10,11... | collective-permute-start | bytes 1769480 | tf_op jit(solution)/shard_map/ppermute | solution.py:357
  66.3 3.6 %copy-start.12 = (bf16[192,1536]{1,0:T(8,128)(2,1)}, bf16[192,1536]{1,0:T(8,128)(2,1)S(1)}, u32[]{:S(2)}) copy-start(bf16[192,1536]{1,0:T(8,128)(2,1)S(1)} %collective-permute-done.7.refs_1_) | copy-start | bytes 1769476
  66.3 3.6 %collective-permute-start.14 = (bf16[2,96,1536]{2,1,0:T(8,128)(2,1)S(1)}, bf16[2,96,1536]{2,1,0:T(8,128)(2,1)S(1)}, u32[]{:S(2)}, u32[]{:S(2)}) collective-permute-start(bf16[2,96,1536]{2,1,0:T(8,128)(2,1)S(1)} %collective-permute-done.12.refs_3_.refs_5_), channel_id=1, source_target_pairs={{0,1},{1,0},{2,3},{3,2},{4,5},{5,4},{6,7},{7,6},{8,9},{9,8},{10,11... | collective-permute-start | bytes 1769480 | tf_op jit(solution)/shard_map/ppermute | solution.py:357
  66.4 11.1 %copy-start.4 = (bf16[2,96,1536]{2,1,0:T(8,128)(2,1)}, bf16[2,96,1536]{2,1,0:T(8,128)(2,1)S(1)}, u32[]{:S(2)}) copy-start(bf16[2,96,1536]{2,1,0:T(8,128)(2,1)S(1)} %collective-permute-done.16.refs_7_.refs_9_) | copy-start | bytes 1769476
  66.4 18.7 %collective-permute-start.17 = (bf16[2,96,1536]{2,1,0:T(8,128)(2,1)S(1)}, bf16[2,96,1536]{2,1,0:T(8,128)(2,1)}, u32[]{:S(2)}, u32[]{:S(2)}) collective-permute-start(bf16[2,96,1536]{2,1,0:T(8,128)(2,1)S(1)} %collective-permute-done.16.refs_7_.refs_9_), channel_id=1, source_target_pairs={{0,1},{1,0},{2,3},{3,2},{4,5},{5,4},{6,7},{7,6},{8,9},{9,8},{10,11... | collective-permute-start | bytes 1769480 | tf_op jit(solution)/shard_map/ppermute | solution.py:357
  66.8 3.1 %copy-start.10 = (bf16[192,1536]{1,0:T(8,128)(2,1)}, bf16[192,1536]{1,0:T(8,128)(2,1)S(1)}, u32[]{:S(2)}) copy-start(bf16[192,1536]{1,0:T(8,128)(2,1)S(1)} %collective-permute-done.2.refs_4_) | copy-start | bytes 1769476
  66.8 28.7 %collective-permute-start.20 = (bf16[192,1536]{1,0:T(8,128)(2,1)}, bf16[192,1536]{1,0:T(8,128)(2,1)}, u32[]{:S(2)}, u32[]{:S(2)}) collective-permute-start(bf16[192,1536]{1,0:T(8,128)(2,1)} %get-tuple-element.44), channel_id=1, source_target_pairs={{0,8},{8,0},{1,9},{9,1},{2,10},{10,2},{3,11},{11,3},{4,12},{12,4},... | collective-permute-start | bytes 1769480 | tf_op jit(solution)/shard_map/ppermute | solution.py:374
  67.3 2.6 %copy-start.11 = (bf16[192,1536]{1,0:T(8,128)(2,1)}, bf16[192,1536]{1,0:T(8,128)(2,1)S(1)}, u32[]{:S(2)}) copy-start(bf16[192,1536]{1,0:T(8,128)(2,1)S(1)} %collective-permute-done.3.refs_5_) | copy-start | bytes 1769476
  67.3 28.2 %collective-permute-start.21 = (bf16[192,1536]{1,0:T(8,128)(2,1)}, bf16[192,1536]{1,0:T(8,128)(2,1)}, u32[]{:S(2)}, u32[]{:S(2)}) collective-permute-start(bf16[192,1536]{1,0:T(8,128)(2,1)} %get-tuple-element.44), channel_id=1, source_target_pairs={{0,4},{4,0},{1,5},{5,1},{2,6},{6,2},{3,7},{7,3},{8,12},{12,8},{9,1... | collective-permute-start | bytes 1769480 | tf_op jit(solution)/shard_map/ppermute | solution.py:374
  69.0 8.6 %copy-start.5 = (bf16[2,96,1536]{2,1,0:T(8,128)(2,1)}, bf16[2,96,1536]{2,1,0:T(8,128)(2,1)S(1)}, u32[]{:S(2)}) copy-start(bf16[2,96,1536]{2,1,0:T(8,128)(2,1)S(1)} %collective-permute-done.15.refs_6_.refs_8_) | copy-start | bytes 1769476
  69.0 16.1 %collective-permute-start.19 = (bf16[48,3072]{1,0:T(8,128)(2,1)}, bf16[48,3072]{1,0:T(8,128)(2,1)}, u32[]{:S(2)}, u32[]{:S(2)}) collective-permute-start(bf16[48,3072]{1,0:T(8,128)(2,1)} %get-tuple-element.42), channel_id=1, source_target_pairs={{0,3},{1,2},{2,1},{3,0},{4,7},{5,6},{6,5},{7,4},{8,11},{9,10},{10,... | collective-permute-start | bytes 884744 | tf_op jit(solution)/shard_map/ppermute | solution.py:357
  69.9 7.6 %copy-start.6 = (bf16[2,96,1536]{2,1,0:T(8,128)(2,1)}, bf16[2,96,1536]{2,1,0:T(8,128)(2,1)S(1)}, u32[]{:S(2)}) copy-start(bf16[2,96,1536]{2,1,0:T(8,128)(2,1)S(1)} %collective-permute-done.14.refs_4_.refs_6_) | copy-start | bytes 1769476
  69.9 15.2 %collective-permute-start.18 = (bf16[48,3072]{1,0:T(8,128)(2,1)}, bf16[48,3072]{1,0:T(8,128)(2,1)}, u32[]{:S(2)}, u32[]{:S(2)}) collective-permute-start(bf16[48,3072]{1,0:T(8,128)(2,1)} %get-tuple-element.40), channel_id=1, source_target_pairs={{0,1},{1,0},{2,3},{3,2},{4,5},{5,4},{6,7},{7,6},{8,9},{9,8},{10,11... | collective-permute-start | bytes 884744 | tf_op jit(solution)/shard_map/ppermute | solution.py:357
Sparse Core Ops, SparseCore 0:
  34.8 52.0 all-gather.2

commit v19 on v17

--- a/solution.py
+++ b/solution.py
@@ -223,7 +223,7 @@
 
 def project(copies, attention, held, low, out, add):
     groups, _, columns = held.shape
-    step = 512 if columns % 512 == 0 else columns
+    step = columns
     for group in range(groups):
         for needed, at, each in copies:
             if at == group:

time: 110 us -> 110 us (level)
  waiting for transfers between devices: 37.6 us -> 38.9 us
  Pallas kernels: 25.1 us -> 24 us
    ppermute x14, waiting for transfers between devices: 13.6 us -> 15.1 us  [flipped(): lax.ppermute(block, axis, [(i, i ^ flip) for i in range(lax.axis_size(axi...]
    pallas_call x1, Pallas kernels: 7.39 us -> 5.98 us  [attend(): pl.pallas_call(functools.partial(attend_kernel, which), out_shape=[jax.Sh...]
  transfers between devices with their start and end apart: 23 -> 23, of which waited for: 8 -> 8; matrix products, arithmetic and copies ran while one was open for 5% -> 5% of each run, Pallas kernels for 16% -> 15%
where the time goes in v19:
time: 110 us
  waiting for transfers between devices  38.9 us (35%)
  starting transfers between devices  26.6 us (24%)
  Pallas kernels  24 us (22%)
  between operations  13.7 us (12%)
  local copies, waits for them, and re-layouts  3.26 us (3%)
  other arithmetic  3.09 us (3%)
    ppermute x4, waiting for transfers between devices, route_of(): return lambda block: lax.ppermute(block, TILES, route)  22.3 us
    ppermute x14, waiting for transfers between devices, flipped(): lax.ppermute(block, axis, [(i, i ^ flip) for i in range(lax.axis_size(axi...  15.1 us
    ppermute x14, starting transfers between devices, flipped(): lax.ppermute(block, axis, [(i, i ^ flip) for i in range(lax.axis_size(axi...  12.9 us
    pallas_call x1, Pallas kernels, finish(): pl.pallas_call(functools.partial(finish_kernel, which, len(weight), moves...  7.74 us
    pallas_call x1, Pallas kernels, attend(): pl.pallas_call(functools.partial(attend_kernel, which), out_shape=[jax.Sh...  5.98 us
    pallas_call x1, Pallas kernels, begin(): pl.pallas_call(functools.partial(begin_kernel, (len(weight), len(control)...  5.79 us
    ppermute x2, starting transfers between devices, on_device(): lax.ppermute(after(x, early_near[0][i]), TILES, early[slot][2])  5.56 us
    ppermute x4, starting transfers between devices, route_of(): return lambda block: lax.ppermute(block, TILES, route)  4.94 us
  transfers between devices with their start and end apart: 23, of which 8 were waited for; matrix products, arithmetic and copies ran while one was open for 5% of the time, Pallas kernels for 15%

profile of v19, /device:TPU:1, one launch (start us, length us, event | category | flops | bytes accessed | tf_op | source)
XLA Modules:
  0.0 109.5 jit_solution(6893576601013010269)
XLA Ops:
  6.5 1.2 %slice_select_fusion = bf16[96,1536]{1,0:T(8,128)(2,1)S(1)} fusion(bf16[96,3072]{1,0:T(8,128)(2,1)} %param.12, pred[]{:T(512)S(6)} %eq.3), kind=kLoop, calls=%fused_computation.8 | loop fusion | flops 147456 | bytes 884737 | tf_op jit(solution)/shard_map/jit(_where)/select_n | solution.py:438
  7.7 2.1 %collective-permute-start.11 = (bf16[1,96,1536]{2,1,0:T(8,128)(2,1)S(1)}, bf16[1,96,1536]{2,1,0:T(8,128)(2,1)S(1)}, u32[]{:S(2)}, u32[]{:S(2)}) collective-permute-start(bf16[1,96,1536]{2,1,0:T(8,128)(2,1)S(1)} %bitcast.21), channel_id=1, source_target_pairs={{0,2},{2,0},{1,3},{3,1},{4,6},{6,4},{5,7},{7,5},{8,10},{10,8},{9,1... | collective-permute-start | bytes 884744 | tf_op jit(solution)/shard_map/ppermute | solution.py:357
  9.8 1.3 %collective-permute-start.6 = (bf16[1,96,1536]{2,1,0:T(8,128)(2,1)S(1)}, bf16[1,96,1536]{2,1,0:T(8,128)(2,1)S(1)}, u32[]{:S(2)}, u32[]{:S(2)}) collective-permute-start(bf16[1,96,1536]{2,1,0:T(8,128)(2,1)S(1)} %bitcast.22), channel_id=1, source_target_pairs={{0,4},{4,0},{8,12},{12,8},{1,5},{5,1},{9,13},{13,9},{2,6},{6,2},{1... | collective-permute-start | bytes 884744 | tf_op jit(solution)/shard_map/ppermute | solution.py:357
  11.1 2.3 %collective-permute-start.4 = (bf16[1,96,1536]{2,1,0:T(8,128)(2,1)S(1)}, bf16[1,96,1536]{2,1,0:T(8,128)(2,1)S(1)}, u32[]{:S(2)}, u32[]{:S(2)}) collective-permute-start(bf16[1,96,1536]{2,1,0:T(8,128)(2,1)S(1)} %bitcast.23), channel_id=1, source_target_pairs={{0,8},{4,12},{8,0},{12,4},{1,9},{5,13},{9,1},{13,5},{2,10},{6,14},... | collective-permute-start | bytes 884744 | tf_op jit(solution)/shard_map/ppermute | solution.py:357
  13.4 1.1 fusion
  14.6 1.0 dynamic-slice_bitcast_fusion
  15.5 1.1 fusion.1
  16.6 1.0 pad_maximum_fusion
  17.6 0.3 collective-permute-start.8
  17.8 0.0 collective-permute-done.11
  17.8 0.1 pad_maximum_fusion.3.refs_1_.refs_3_
  17.9 1.3 %collective-permute-start.12 = (bf16[2,96,1536]{2,1,0:T(8,128)(2,1)S(1)}, bf16[2,96,1536]{2,1,0:T(8,128)(2,1)S(1)}, u32[]{:S(2)}, u32[]{:S(2)}) collective-permute-start(bf16[2,96,1536]{2,1,0:T(8,128)(2,1)S(1)} %pad_maximum_fusion.3.refs_1_.refs_3_), channel_id=1, source_target_pairs={{0,16},{16,0},{1,17},{17,1},{2,18},{18,2},{3,19},{19,3},{4,20},{20... | collective-permute-start | bytes 1769480 | tf_op jit(solution)/shard_map/ppermute | solution.py:357
  19.2 4.5 %collective-permute-done.6 = bf16[1,96,1536]{2,1,0:T(8,128)(2,1)S(1)} collective-permute-done((bf16[1,96,1536]{2,1,0:T(8,128)(2,1)S(1)}, bf16[1,96,1536]{2,1,0:T(8,128)(2,1)S(1)}, u32[]{:S(2)}, u32[]{:S(2)}) %collective-permute-start.6) | collective-permute-done | bytes 294944 | tf_op jit(solution)/shard_map/ppermute | solution.py:357
  23.7 0.0 collective-permute-done.4
  23.7 1.0 collective-permute-done.8.refs_11_
  24.7 1.4 %collective-permute-start.9 = (bf16[1,96,1536]{2,1,0:T(8,128)(2,1)S(1)}, bf16[1,96,1536]{2,1,0:T(8,128)(2,1)S(1)}, u32[]{:S(2)}, u32[]{:S(2)}) collective-permute-start(bf16[1,96,1536]{2,1,0:T(8,128)(2,1)S(1)} %collective-permute-done.4), channel_id=1, source_target_pairs={{0,4},{4,0},{8,12},{12,8},{1,5},{5,1},{9,13},{13,9},{2,6},{6,2},{1... | collective-permute-start | bytes 884744 | tf_op jit(solution)/shard_map/ppermute | solution.py:357
  26.1 0.3 collective-permute-start.10
  26.3 4.3 %collective-permute-done.9 = bf16[1,96,1536]{2,1,0:T(8,128)(2,1)S(1)} collective-permute-done((bf16[1,96,1536]{2,1,0:T(8,128)(2,1)S(1)}, bf16[1,96,1536]{2,1,0:T(8,128)(2,1)S(1)}, u32[]{:S(2)}, u32[]{:S(2)}) %collective-permute-start.9) | collective-permute-done | bytes 294944 | tf_op jit(solution)/shard_map/ppermute | solution.py:357
  30.6 0.9 pad_maximum_fusion.2
  31.5 0.9 collective-permute-done.10
  32.4 0.0 all-gather.3.cloned.1.call-update
  32.4 3.2 %collective-permute-start = (bf16[192,1536]{1,0:T(8,128)(2,1)}, bf16[192,1536]{1,0:T(8,128)(2,1)S(1)}, u32[]{:S(2)}, u32[]{:S(2)}) collective-permute-start(bf16[192,1536]{1,0:T(8,128)(2,1)} %refs_0_.1), channel_id=1, source_target_pairs={{0,1},{1,0},{2,3},{3,2},{4,5},{5,4},{6,7},{7,6},{8,9},{9,8},{10,11... | collective-permute-start | bytes 1769480 | tf_op jit(solution)/shard_map/ppermute | solution.py:472
  35.6 0.1 collective-permute-start.1
  35.7 0.4 collective-permute-start.13
  36.1 1.9 %collective-permute-start.5 = (bf16[192,1536]{1,0:T(8,128)(2,1)S(1)}, bf16[192,1536]{1,0:T(8,128)(2,1)S(1)}, u32[]{:S(2)}, u32[]{:S(2)}) collective-permute-start(bf16[192,1536]{1,0:T(8,128)(2,1)S(1)} %get-tuple-element.32), channel_id=1, source_target_pairs={{0,8},{8,0},{1,9},{9,1},{2,10},{10,2},{3,11},{11,3},{4,12},{12,4},... | collective-permute-start | bytes 1769480 | tf_op jit(solution)/shard_map/ppermute | solution.py:374
  38.0 0.6 collective-permute-start.7
  38.7 0.0 collective-permute-done.refs_2_
  38.7 0.0 copy-start.8
  38.7 1.3 %collective-permute-start.16 = (bf16[2,96,1536]{2,1,0:T(8,128)(2,1)S(1)}, bf16[2,96,1536]{2,1,0:T(8,128)(2,1)S(1)}, u32[]{:S(2)}, u32[]{:S(2)}) collective-permute-start(bf16[2,96,1536]{2,1,0:T(8,128)(2,1)S(1)} %constant_dynamic-update-slice_fusion.refs_5_.refs_7_), channel_id=1, source_target_pairs={{0,16},{16,0},{1,17},{17,1},{2,18},{18,2},{3,19},{19,3},{4,20},{20... | collective-permute-start | bytes 1769480 | tf_op jit(solution)/shard_map/ppermute | solution.py:357
  40.0 0.0 collective-permute-done.1.refs_3_
  40.0 2.9 %collective-permute-start.2 = (bf16[192,1536]{1,0:T(8,128)(2,1)}, bf16[192,1536]{1,0:T(8,128)(2,1)S(1)}, u32[]{:S(2)}, u32[]{:S(2)}) collective-permute-start(bf16[192,1536]{1,0:T(8,128)(2,1)} %refs_0_.1), channel_id=1, source_target_pairs={{1,2},{2,1},{5,6},{6,5},{9,10},{10,9},{13,14},{14,13},{17,18},{18,... | collective-permute-start | bytes 1769480 | tf_op jit(solution)/shard_map/ppermute | solution.py:474
  42.9 0.0 collective-permute-done.13.refs_2_.refs_4_
  42.9 2.7 %collective-permute-start.3 = (bf16[192,1536]{1,0:T(8,128)(2,1)}, bf16[192,1536]{1,0:T(8,128)(2,1)S(1)}, u32[]{:S(2)}, u32[]{:S(2)}) collective-permute-start(bf16[192,1536]{1,0:T(8,128)(2,1)} %refs_1_.1), channel_id=1, source_target_pairs={{1,2},{2,1},{5,6},{6,5},{9,10},{10,9},{13,14},{14,13},{17,18},{18,... | collective-permute-start | bytes 1769480 | tf_op jit(solution)/shard_map/ppermute | solution.py:474
  45.6 19.0 %collective-permute-done.5.refs_0_ = bf16[192,1536]{1,0:T(8,128)(2,1)S(1)} collective-permute-done((bf16[192,1536]{1,0:T(8,128)(2,1)S(1)}, bf16[192,1536]{1,0:T(8,128)(2,1)S(1)}, u32[]{:S(2)}, u32[]{:S(2)}) %collective-permute-start.5) | collective-permute-done | bytes 589856 | tf_op jit(solution)/shard_map/ppermute | solution.py:374
  64.6 0.9 collective-permute-start.15
  65.5 0.2 collective-permute-start.14
  65.7 0.4 collective-permute-start.17
  66.0 0.4 collective-permute-start.20
  66.4 2.0 %collective-permute-start.21 = (bf16[192,1536]{1,0:T(8,128)(2,1)}, bf16[192,1536]{1,0:T(8,128)(2,1)}, u32[]{:S(2)}, u32[]{:S(2)}) collective-permute-start(bf16[192,1536]{1,0:T(8,128)(2,1)} %get-tuple-element.44), channel_id=1, source_target_pairs={{0,4},{4,0},{1,5},{5,1},{2,6},{6,2},{3,7},{7,3},{8,12},{12,8},{9,1... | collective-permute-start | bytes 1769480 | tf_op jit(solution)/shard_map/ppermute | solution.py:374
  68.5 0.7 collective-permute-start.19
  69.2 0.1 collective-permute-start.18
  69.3 6.0 %attend.1 = (f32[192,1536]{1,0:T(8,128)}, f32[192,128]{1,0:T(8,128)}) custom-call(s32[1,6]{1,0:T(1,128)} %pattern.5, bf16[192,1536]{1,0:T(8,128)(2,1)} %q.5, bf16[192,1536]{1,0:T(8,128)(2,1)} %refs_0_.1, bf16[192,1536]{1,0:T(8,128)(2,1)} %refs_1_.1, bf16[192,1536]{1,0:T(8,128)(2,1)} %copy-done.8, bf16[192,1536]{1,0:T(8,128)(2,1)} %copy-done.9, ...), custom_call_target="tpu_custom_call" | custom-call | flops 1019215872 | bytes 5308416 | tf_op jit(solution)/shard_map/attend/pallas_call | solution.py:104
  75.4 4.5 %close.1.ready = bf16[192,768]{1,0:T(8,128)(2,1)} custom-call(s32[1,6]{1,0:T(1,128)} %pattern.5, bf16[192,1536]{1,0:T(8,128)(2,1)} %q.5, f32[192,1536]{1,0:T(8,128)} %get-tuple-element.27.part, f32[192,128]{1,0:T(8,128)} %get-tuple-element.28.stats, bf16[192,1536]{1,0:T(8,128)(2,1)} %copy-done.12, bf16[192,1536]{1,0:T(8,128)(2,1)} %copy-done.13), custom_call_target="tpu_custom_call" | custom-call | flops 339738624 | bytes 2359296 | tf_op jit(solution)/shard_map/close/pallas_call | solution.py:179
  79.9 4.5 %collective-permute-done.19.refs_12_ = bf16[48,3072]{1,0:T(8,128)(2,1)S(1)} collective-permute-done((bf16[48,3072]{1,0:T(8,128)(2,1)}, bf16[48,3072]{1,0:T(8,128)(2,1)S(1)}, u32[]{:S(2)}, u32[]{:S(2)}) %collective-permute-start.19) | collective-permute-done | bytes 294944 | tf_op jit(solution)/shard_map/ppermute | solution.py:357
  84.3 1.5 %all-gather.3.cloned.1.call-done = bf16[16,96,1536]{2,1,0:T(8,128)(2,1)} async-done(((bf16[2,96,1536]{2,1,0:T(8,128)(2,1)}), bf16[16,96,1536]{2,1,0:T(8,128)(2,1)}) %all-gather.3.cloned.1.call-update) | async-done | bytes 4718608 | tf_op jit(solution)/shard_map/all_gather | solution.py:486
  85.8 5.8 %begin.1.so_far = f32[192,3072]{1,0:T(8,128)} custom-call(bf16[192,3072]{1,0:T(8,128)(2,1)} %hidden.1, bf16[192,768]{1,0:T(8,128)(2,1)} %close.1.ready, bf16[8,2,96,1536]{3,2,1,0:T(8,128)(2,1)} %bitcast.19, bf16[2,96,1536]{2,1,0:T(8,128)(2,1)} %copy-done, bf16[2,96,1536]{2,1,0:T(8,128)(2,1)} %copy-done.3, bf16[2,96,1536]{2,1,0:T(8,128)(2,1)} %copy-done.2, ...), custom_call_target="tpu_custom_call" | custom-call | flops 905969664 | bytes 9437184 | tf_op jit(solution)/shard_map/begin/pallas_call | solution.py:318
  91.6 3.3 %collective-permute-done.20.refs_0_ = bf16[192,1536]{1,0:T(8,128)(2,1)} collective-permute-done((bf16[192,1536]{1,0:T(8,128)(2,1)}, bf16[192,1536]{1,0:T(8,128)(2,1)}, u32[]{:S(2)}, u32[]{:S(2)}) %collective-permute-start.20) | collective-permute-done | bytes 589856 | tf_op jit(solution)/shard_map/ppermute | solution.py:374
  94.9 7.7 %finish.1 = bf16[192,3072]{1,0:T(8,128)(2,1)} custom-call(s32[1,6]{1,0:T(1,128)} %pattern.5, bf16[192,1536]{1,0:T(8,128)(2,1)} %q.5, f32[192,1536]{1,0:T(8,128)} %get-tuple-element.27.part, f32[192,128]{1,0:T(8,128)} %get-tuple-element.28.stats, f32[192,3072]{1,0:T(8,128)} %begin.1.so_far, bf16[192,1536]{1,0:T(8,128)(2,1)} %collective-permute-done.20.refs_0_, ...), custom_call_target="tpu_custom_call" | custom-call | flops 905969664 | bytes 8257536 | tf_op jit(solution)/shard_map/finish/pallas_call | solution.py:339
  (42 shorter events, 0.1 us)
Async XLA Ops:
  6.5 8.0 %copy-start.7 = (bf16[192,3072]{1,0:T(8,128)(2,1)S(1)}, bf16[192,3072]{1,0:T(8,128)(2,1)}, u32[]{:S(2)}) copy-start(bf16[192,3072]{1,0:T(8,128)(2,1)} %param.11) | copy-start | bytes 3538948
  6.5 79.3 %all-gather.3.cloned.1.call-start = ((), (), s32[]{:S(2)}) async-start(), calls=%async_computation | async-start | bytes 5308416 | tf_op jit(solution)/shard_map/all_gather | solution.py:486
  7.7 10.1 %collective-permute-start.11 = (bf16[1,96,1536]{2,1,0:T(8,128)(2,1)S(1)}, bf16[1,96,1536]{2,1,0:T(8,128)(2,1)S(1)}, u32[]{:S(2)}, u32[]{:S(2)}) collective-permute-start(bf16[1,96,1536]{2,1,0:T(8,128)(2,1)S(1)} %bitcast.21), channel_id=1, source_target_pairs={{0,2},{2,0},{1,3},{3,1},{4,6},{6,4},{5,7},{7,5},{8,10},{10,8},{9,1... | collective-permute-start | bytes 884744 | tf_op jit(solution)/shard_map/ppermute | solution.py:357
  9.8 13.9 %collective-permute-start.6 = (bf16[1,96,1536]{2,1,0:T(8,128)(2,1)S(1)}, bf16[1,96,1536]{2,1,0:T(8,128)(2,1)S(1)}, u32[]{:S(2)}, u32[]{:S(2)}) collective-permute-start(bf16[1,96,1536]{2,1,0:T(8,128)(2,1)S(1)} %bitcast.22), channel_id=1, source_target_pairs={{0,4},{4,0},{8,12},{12,8},{1,5},{5,1},{9,13},{13,9},{2,6},{6,2},{1... | collective-permute-start | bytes 884744 | tf_op jit(solution)/shard_map/ppermute | solution.py:357
  11.1 12.6 %collective-permute-start.4 = (bf16[1,96,1536]{2,1,0:T(8,128)(2,1)S(1)}, bf16[1,96,1536]{2,1,0:T(8,128)(2,1)S(1)}, u32[]{:S(2)}, u32[]{:S(2)}) collective-permute-start(bf16[1,96,1536]{2,1,0:T(8,128)(2,1)S(1)} %bitcast.23), channel_id=1, source_target_pairs={{0,8},{4,12},{8,0},{12,4},{1,9},{5,13},{9,1},{13,5},{2,10},{6,14},... | collective-permute-start | bytes 884744 | tf_op jit(solution)/shard_map/ppermute | solution.py:357
  17.6 7.1 %collective-permute-start.8 = (bf16[48,3072]{1,0:T(8,128)(2,1)S(1)}, bf16[48,3072]{1,0:T(8,128)(2,1)}, u32[]{:S(2)}, u32[]{:S(2)}) collective-permute-start(bf16[48,3072]{1,0:T(8,128)(2,1)S(1)} %get-tuple-element.34), channel_id=1, source_target_pairs={{0,2},{1,3},{2,0},{3,1},{4,6},{5,7},{6,4},{7,5},{8,10},{9,11},{10,... | collective-permute-start | bytes 884744 | tf_op jit(solution)/shard_map/ppermute | solution.py:357
  17.9 20.7 %copy-start = (bf16[2,96,1536]{2,1,0:T(8,128)(2,1)}, bf16[2,96,1536]{2,1,0:T(8,128)(2,1)S(1)}, u32[]{:S(2)}) copy-start(bf16[2,96,1536]{2,1,0:T(8,128)(2,1)S(1)} %pad_maximum_fusion.3.refs_1_.refs_3_) | copy-start | bytes 1769476
  17.9 14.5 %collective-permute-start.12 = (bf16[2,96,1536]{2,1,0:T(8,128)(2,1)S(1)}, bf16[2,96,1536]{2,1,0:T(8,128)(2,1)S(1)}, u32[]{:S(2)}, u32[]{:S(2)}) collective-permute-start(bf16[2,96,1536]{2,1,0:T(8,128)(2,1)S(1)} %pad_maximum_fusion.3.refs_1_.refs_3_), channel_id=1, source_target_pairs={{0,16},{16,0},{1,17},{17,1},{2,18},{18,2},{3,19},{19,3},{4,20},{20... | collective-permute-start | bytes 1769480 | tf_op jit(solution)/shard_map/ppermute | solution.py:357
  24.7 5.9 %collective-permute-start.9 = (bf16[1,96,1536]{2,1,0:T(8,128)(2,1)S(1)}, bf16[1,96,1536]{2,1,0:T(8,128)(2,1)S(1)}, u32[]{:S(2)}, u32[]{:S(2)}) collective-permute-start(bf16[1,96,1536]{2,1,0:T(8,128)(2,1)S(1)} %collective-permute-done.4), channel_id=1, source_target_pairs={{0,4},{4,0},{8,12},{12,8},{1,5},{5,1},{9,13},{13,9},{2,6},{6,2},{1... | collective-permute-start | bytes 884744 | tf_op jit(solution)/shard_map/ppermute | solution.py:357
  26.1 6.3 %collective-permute-start.10 = (bf16[1,96,1536]{2,1,0:T(8,128)(2,1)S(1)}, bf16[1,96,1536]{2,1,0:T(8,128)(2,1)S(1)}, u32[]{:S(2)}, u32[]{:S(2)}) collective-permute-start(bf16[1,96,1536]{2,1,0:T(8,128)(2,1)S(1)} %collective-permute-done.6), channel_id=1, source_target_pairs={{0,2},{2,0},{1,3},{3,1},{4,6},{6,4},{5,7},{7,5},{8,10},{10,8},{9,1... | collective-permute-start | bytes 884744 | tf_op jit(solution)/shard_map/ppermute | solution.py:357
  32.4 42.9 %copy-start.2 = (bf16[2,96,1536]{2,1,0:T(8,128)(2,1)}, bf16[2,96,1536]{2,1,0:T(8,128)(2,1)S(1)}, u32[]{:S(2)}) copy-start(bf16[2,96,1536]{2,1,0:T(8,128)(2,1)S(1)} %collective-permute-done.12.refs_3_.refs_5_) | copy-start | bytes 1769476
  32.4 6.3 %collective-permute-start = (bf16[192,1536]{1,0:T(8,128)(2,1)}, bf16[192,1536]{1,0:T(8,128)(2,1)S(1)}, u32[]{:S(2)}, u32[]{:S(2)}) collective-permute-start(bf16[192,1536]{1,0:T(8,128)(2,1)} %refs_0_.1), channel_id=1, source_target_pairs={{0,1},{1,0},{2,3},{3,2},{4,5},{5,4},{6,7},{7,6},{8,9},{9,8},{10,11... | collective-permute-start | bytes 1769480 | tf_op jit(solution)/shard_map/ppermute | solution.py:472
  35.6 4.4 %collective-permute-start.1 = (bf16[192,1536]{1,0:T(8,128)(2,1)}, bf16[192,1536]{1,0:T(8,128)(2,1)S(1)}, u32[]{:S(2)}, u32[]{:S(2)}) collective-permute-start(bf16[192,1536]{1,0:T(8,128)(2,1)} %refs_1_.1), channel_id=1, source_target_pairs={{0,1},{1,0},{2,3},{3,2},{4,5},{5,4},{6,7},{7,6},{8,9},{9,8},{10,11... | collective-permute-start | bytes 1769480 | tf_op jit(solution)/shard_map/ppermute | solution.py:472
  35.7 7.2 %collective-permute-start.13 = (bf16[2,96,1536]{2,1,0:T(8,128)(2,1)S(1)}, bf16[2,96,1536]{2,1,0:T(8,128)(2,1)S(1)}, u32[]{:S(2)}, u32[]{:S(2)}) collective-permute-start(bf16[2,96,1536]{2,1,0:T(8,128)(2,1)S(1)} %pad_maximum_fusion.3.refs_1_.refs_3_), channel_id=1, source_target_pairs={{0,1},{1,0},{2,3},{3,2},{4,5},{5,4},{6,7},{7,6},{8,9},{9,8},{10,11... | collective-permute-start | bytes 1769480 | tf_op jit(solution)/shard_map/ppermute | solution.py:357
  36.1 28.5 %collective-permute-start.5 = (bf16[192,1536]{1,0:T(8,128)(2,1)S(1)}, bf16[192,1536]{1,0:T(8,128)(2,1)S(1)}, u32[]{:S(2)}, u32[]{:S(2)}) collective-permute-start(bf16[192,1536]{1,0:T(8,128)(2,1)S(1)} %get-tuple-element.32), channel_id=1, source_target_pairs={{0,8},{8,0},{1,9},{9,1},{2,10},{10,2},{3,11},{11,3},{4,12},{12,4},... | collective-permute-start | bytes 1769480 | tf_op jit(solution)/shard_map/ppermute | solution.py:374
  38.0 27.5 %collective-permute-start.7 = (bf16[192,1536]{1,0:T(8,128)(2,1)S(1)}, bf16[192,1536]{1,0:T(8,128)(2,1)S(1)}, u32[]{:S(2)}, u32[]{:S(2)}) collective-permute-start(bf16[192,1536]{1,0:T(8,128)(2,1)S(1)} %get-tuple-element.32), channel_id=1, source_target_pairs={{0,4},{4,0},{1,5},{5,1},{2,6},{6,2},{3,7},{7,3},{8,12},{12,8},{9,1... | collective-permute-start | bytes 1769480 | tf_op jit(solution)/shard_map/ppermute | solution.py:374
  38.7 36.6 %copy-start.1 = (bf16[2,96,1536]{2,1,0:T(8,128)(2,1)}, bf16[2,96,1536]{2,1,0:T(8,128)(2,1)S(1)}, u32[]{:S(2)}) copy-start(bf16[2,96,1536]{2,1,0:T(8,128)(2,1)S(1)} %constant_dynamic-update-slice_fusion.refs_5_.refs_7_) | copy-start | bytes 1769476
  38.7 30.4 %copy-start.8 = (bf16[192,1536]{1,0:T(8,128)(2,1)}, bf16[192,1536]{1,0:T(8,128)(2,1)S(1)}, u32[]{:S(2)}) copy-start(bf16[192,1536]{1,0:T(8,128)(2,1)S(1)} %collective-permute-done.refs_2_) | copy-start | bytes 1769476
  38.7 27.0 %collective-permute-start.16 = (bf16[2,96,1536]{2,1,0:T(8,128)(2,1)S(1)}, bf16[2,96,1536]{2,1,0:T(8,128)(2,1)S(1)}, u32[]{:S(2)}, u32[]{:S(2)}) collective-permute-start(bf16[2,96,1536]{2,1,0:T(8,128)(2,1)S(1)} %constant_dynamic-update-slice_fusion.refs_5_.refs_7_), channel_id=1, source_target_pairs={{0,16},{16,0},{1,17},{17,1},{2,18},{18,2},{3,19},{19,3},{4,20},{20... | collective-permute-start | bytes 1769480 | tf_op jit(solution)/shard_map/ppermute | solution.py:357
  40.0 29.1 %copy-start.9 = (bf16[192,1536]{1,0:T(8,128)(2,1)}, bf16[192,1536]{1,0:T(8,128)(2,1)S(1)}, u32[]{:S(2)}) copy-start(bf16[192,1536]{1,0:T(8,128)(2,1)S(1)} %collective-permute-done.1.refs_3_) | copy-start | bytes 1769476
  40.0 26.0 %collective-permute-start.2 = (bf16[192,1536]{1,0:T(8,128)(2,1)}, bf16[192,1536]{1,0:T(8,128)(2,1)S(1)}, u32[]{:S(2)}, u32[]{:S(2)}) collective-permute-start(bf16[192,1536]{1,0:T(8,128)(2,1)} %refs_0_.1), channel_id=1, source_target_pairs={{1,2},{2,1},{5,6},{6,5},{9,10},{10,9},{13,14},{14,13},{17,18},{18,... | collective-permute-start | bytes 1769480 | tf_op jit(solution)/shard_map/ppermute | solution.py:474
  42.9 32.4 %copy-start.3 = (bf16[2,96,1536]{2,1,0:T(8,128)(2,1)}, bf16[2,96,1536]{2,1,0:T(8,128)(2,1)S(1)}, u32[]{:S(2)}) copy-start(bf16[2,96,1536]{2,1,0:T(8,128)(2,1)S(1)} %collective-permute-done.13.refs_2_.refs_4_) | copy-start | bytes 1769476
  42.9 23.5 %collective-permute-start.3 = (bf16[192,1536]{1,0:T(8,128)(2,1)}, bf16[192,1536]{1,0:T(8,128)(2,1)S(1)}, u32[]{:S(2)}, u32[]{:S(2)}) collective-permute-start(bf16[192,1536]{1,0:T(8,128)(2,1)} %refs_1_.1), channel_id=1, source_target_pairs={{1,2},{2,1},{5,6},{6,5},{9,10},{10,9},{13,14},{14,13},{17,18},{18,... | collective-permute-start | bytes 1769480 | tf_op jit(solution)/shard_map/ppermute | solution.py:474
  64.6 4.6 %copy-start.12 = (bf16[192,1536]{1,0:T(8,128)(2,1)}, bf16[192,1536]{1,0:T(8,128)(2,1)S(1)}, u32[]{:S(2)}) copy-start(bf16[192,1536]{1,0:T(8,128)(2,1)S(1)} %collective-permute-done.5.refs_0_) | copy-start | bytes 1769476
  64.6 3.9 %collective-permute-start.15 = (bf16[2,96,1536]{2,1,0:T(8,128)(2,1)S(1)}, bf16[2,96,1536]{2,1,0:T(8,128)(2,1)S(1)}, u32[]{:S(2)}, u32[]{:S(2)}) collective-permute-start(bf16[2,96,1536]{2,1,0:T(8,128)(2,1)S(1)} %constant_dynamic-update-slice_fusion.refs_5_.refs_7_), channel_id=1, source_target_pairs={{0,1},{1,0},{2,3},{3,2},{4,5},{5,4},{6,7},{7,6},{8,9},{9,8},{10,11... | collective-permute-start | bytes 1769480 | tf_op jit(solution)/shard_map/ppermute | solution.py:357
  65.5 3.7 %copy-start.13 = (bf16[192,1536]{1,0:T(8,128)(2,1)}, bf16[192,1536]{1,0:T(8,128)(2,1)S(1)}, u32[]{:S(2)}) copy-start(bf16[192,1536]{1,0:T(8,128)(2,1)S(1)} %collective-permute-done.7.refs_1_) | copy-start | bytes 1769476
  65.5 3.6 %collective-permute-start.14 = (bf16[2,96,1536]{2,1,0:T(8,128)(2,1)S(1)}, bf16[2,96,1536]{2,1,0:T(8,128)(2,1)S(1)}, u32[]{:S(2)}, u32[]{:S(2)}) collective-permute-start(bf16[2,96,1536]{2,1,0:T(8,128)(2,1)S(1)} %collective-permute-done.12.refs_3_.refs_5_), channel_id=1, source_target_pairs={{0,1},{1,0},{2,3},{3,2},{4,5},{5,4},{6,7},{7,6},{8,9},{9,8},{10,11... | collective-permute-start | bytes 1769480 | tf_op jit(solution)/shard_map/ppermute | solution.py:357
  65.7 9.7 %copy-start.4 = (bf16[2,96,1536]{2,1,0:T(8,128)(2,1)}, bf16[2,96,1536]{2,1,0:T(8,128)(2,1)S(1)}, u32[]{:S(2)}) copy-start(bf16[2,96,1536]{2,1,0:T(8,128)(2,1)S(1)} %collective-permute-done.16.refs_7_.refs_9_) | copy-start | bytes 1769476
  65.7 18.6 %collective-permute-start.17 = (bf16[2,96,1536]{2,1,0:T(8,128)(2,1)S(1)}, bf16[2,96,1536]{2,1,0:T(8,128)(2,1)}, u32[]{:S(2)}, u32[]{:S(2)}) collective-permute-start(bf16[2,96,1536]{2,1,0:T(8,128)(2,1)S(1)} %collective-permute-done.16.refs_7_.refs_9_), channel_id=1, source_target_pairs={{0,1},{1,0},{2,3},{3,2},{4,5},{5,4},{6,7},{7,6},{8,9},{9,8},{10,11... | collective-permute-start | bytes 1769480 | tf_op jit(solution)/shard_map/ppermute | solution.py:357
  66.0 3.2 %copy-start.10 = (bf16[192,1536]{1,0:T(8,128)(2,1)}, bf16[192,1536]{1,0:T(8,128)(2,1)S(1)}, u32[]{:S(2)}) copy-start(bf16[192,1536]{1,0:T(8,128)(2,1)S(1)} %collective-permute-done.2.refs_4_) | copy-start | bytes 1769476
  66.0 28.9 %collective-permute-start.20 = (bf16[192,1536]{1,0:T(8,128)(2,1)}, bf16[192,1536]{1,0:T(8,128)(2,1)}, u32[]{:S(2)}, u32[]{:S(2)}) collective-permute-start(bf16[192,1536]{1,0:T(8,128)(2,1)} %get-tuple-element.44), channel_id=1, source_target_pairs={{0,8},{8,0},{1,9},{9,1},{2,10},{10,2},{3,11},{11,3},{4,12},{12,4},... | collective-permute-start | bytes 1769480 | tf_op jit(solution)/shard_map/ppermute | solution.py:374
  66.4 2.7 %copy-start.11 = (bf16[192,1536]{1,0:T(8,128)(2,1)}, bf16[192,1536]{1,0:T(8,128)(2,1)S(1)}, u32[]{:S(2)}) copy-start(bf16[192,1536]{1,0:T(8,128)(2,1)S(1)} %collective-permute-done.3.refs_5_) | copy-start | bytes 1769476
  66.4 28.5 %collective-permute-start.21 = (bf16[192,1536]{1,0:T(8,128)(2,1)}, bf16[192,1536]{1,0:T(8,128)(2,1)}, u32[]{:S(2)}, u32[]{:S(2)}) collective-permute-start(bf16[192,1536]{1,0:T(8,128)(2,1)} %get-tuple-element.44), channel_id=1, source_target_pairs={{0,4},{4,0},{1,5},{5,1},{2,6},{6,2},{3,7},{7,3},{8,12},{12,8},{9,1... | collective-permute-start | bytes 1769480 | tf_op jit(solution)/shard_map/ppermute | solution.py:374
  68.5 6.9 %copy-start.5 = (bf16[2,96,1536]{2,1,0:T(8,128)(2,1)}, bf16[2,96,1536]{2,1,0:T(8,128)(2,1)S(1)}, u32[]{:S(2)}) copy-start(bf16[2,96,1536]{2,1,0:T(8,128)(2,1)S(1)} %collective-permute-done.15.refs_6_.refs_8_) | copy-start | bytes 1769476
  68.5 15.8 %collective-permute-start.19 = (bf16[48,3072]{1,0:T(8,128)(2,1)}, bf16[48,3072]{1,0:T(8,128)(2,1)S(1)}, u32[]{:S(2)}, u32[]{:S(2)}) collective-permute-start(bf16[48,3072]{1,0:T(8,128)(2,1)} %get-tuple-element.42), channel_id=1, source_target_pairs={{0,3},{1,2},{2,1},{3,0},{4,7},{5,6},{6,5},{7,4},{8,11},{9,10},{10,... | collective-permute-start | bytes 884744 | tf_op jit(solution)/shard_map/ppermute | solution.py:357
  69.2 6.1 %copy-start.6 = (bf16[2,96,1536]{2,1,0:T(8,128)(2,1)}, bf16[2,96,1536]{2,1,0:T(8,128)(2,1)S(1)}, u32[]{:S(2)}) copy-start(bf16[2,96,1536]{2,1,0:T(8,128)(2,1)S(1)} %collective-permute-done.14.refs_4_.refs_6_) | copy-start | bytes 1769476
  69.2 15.1 %collective-permute-start.18 = (bf16[48,3072]{1,0:T(8,128)(2,1)}, bf16[48,3072]{1,0:T(8,128)(2,1)}, u32[]{:S(2)}, u32[]{:S(2)}) collective-permute-start(bf16[48,3072]{1,0:T(8,128)(2,1)} %get-tuple-element.40), channel_id=1, source_target_pairs={{0,1},{1,0},{2,3},{3,2},{4,5},{5,4},{6,7},{7,6},{8,9},{9,8},{10,11... | collective-permute-start | bytes 884744 | tf_op jit(solution)/shard_map/ppermute | solution.py:357
  84.3 1.5 %copy-start.14 = (bf16[48,3072]{1,0:T(8,128)(2,1)}, bf16[48,3072]{1,0:T(8,128)(2,1)S(1)}, u32[]{:S(2)}) copy-start(bf16[48,3072]{1,0:T(8,128)(2,1)S(1)} %collective-permute-done.19.refs_12_) | copy-start | bytes 884740
Sparse Core Ops, SparseCore 0:
  32.5 53.2 all-gather.2

commit v20 on v14

--- a/solution.py
+++ b/solution.py
@@ -459,7 +459,12 @@
     late_near = []
     for chunk in chunks:
         lanes = (far_lane, near_lane)
-        late_near.append([lanes[i % 2](route_of(route), chunk) for i, (_, _, route) in enumerate(late)])
+        if not late_near:
+            sent = [lanes[i % 2](route_of(route), chunk) for i, (_, _, route) in enumerate(late)]
+        else:
+            waits = [kv[0] for kv in early_near[1:]]
+            sent = [lax.ppermute(after(chunk, *waits), TILES, route) for _, _, route in late]
+        late_near.append(sent)
     crossed = [swap("core", 1)(x) for x in held]
     for d in (1, grid_width - 1):
         control_parts[d] = swap(TILES, d)(after(control_sent[d], *[x for kv in early_near[1:] for x in kv]))

time: 110 us -> 113 us (1.027)
  waiting for transfers between devices: 39.6 us -> 44 us
  starting transfers between devices: 26.6 us -> 25.1 us
    ppermute x0 -> x2, waiting for transfers between devices: none -> 8.29 us  [on_device(): lax.ppermute(after(chunk, *waits), TILES, route)]
    ppermute x4 -> x2, starting transfers between devices: 4.94 us -> 2.59 us  [route_of(): return lambda block: lax.ppermute(block, TILES, route)]
    all_gather x1, waiting for transfers between devices: 1.48 us -> 0.01 us  [on_device(): lax.all_gather(after(jnp.concatenate([far, last]), *gates), ('groups', 'p...]
    ppermute x0 -> x2, starting transfers between devices: none -> 1.44 us  [on_device(): lax.ppermute(after(chunk, *waits), TILES, route)]
    ppermute x14, waiting for transfers between devices: 15.5 us -> 14.2 us  [flipped(): lax.ppermute(block, axis, [(i, i ^ flip) for i in range(lax.axis_size(axi...]
    ppermute x4 -> x2, waiting for transfers between devices: 22.6 us -> 21.5 us  [route_of(): return lambda block: lax.ppermute(block, TILES, route)]
  transfers between devices with their start and end apart: 23 -> 23, of which waited for: 8 -> 9; matrix products, arithmetic and copies ran while one was open for 5% -> 5% of each run, Pallas kernels for 14% -> 14%
where the time goes in v20:
time: 113 us; the launch traced here: 112 us
  waiting for transfers between devices  44 us (39%)
  starting transfers between devices  25.1 us (22%)
  Pallas kernels  22.7 us (20%)
  between operations  13.7 us (12%)
  other arithmetic  3.27 us (3%)
  local copies, waits for them, and re-layouts  3.2 us (3%)
    ppermute x2, waiting for transfers between devices, route_of(): return lambda block: lax.ppermute(block, TILES, route)  21.5 us
    ppermute x14, waiting for transfers between devices, flipped(): lax.ppermute(block, axis, [(i, i ^ flip) for i in range(lax.axis_size(axi...  14.2 us
    ppermute x14, starting transfers between devices, flipped(): lax.ppermute(block, axis, [(i, i ^ flip) for i in range(lax.axis_size(axi...  12 us
    ppermute x2, waiting for transfers between devices, on_device(): lax.ppermute(after(chunk, *waits), TILES, route)  8.29 us
    pallas_call x1, Pallas kernels, finish(): pl.pallas_call(functools.partial(finish_kernel, which, len(weight), moves...  7.07 us
    pallas_call x1, Pallas kernels, attend(): pl.pallas_call(functools.partial(attend_kernel, which), out_shape=[jax.Sh...  6.02 us
    ppermute x2, starting transfers between devices, on_device(): lax.ppermute(after(x, early_near[0][i]), TILES, early[slot][2])  5.82 us
    pallas_call x1, Pallas kernels, begin(): pl.pallas_call(functools.partial(begin_kernel, (len(weight), len(control)...  5.59 us
  transfers between devices with their start and end apart: 23, of which 9 were waited for; matrix products, arithmetic and copies ran while one was open for 5% of the time, Pallas kernels for 14%

profile of v20, /device:TPU:1, one launch (start us, length us, event | category | flops | bytes accessed | tf_op | source)
XLA Modules:
  0.0 112.0 jit_solution(9038914364710104706)
XLA Ops:
  6.5 1.2 %slice_select_fusion = bf16[96,1536]{1,0:T(8,128)(2,1)S(1)} fusion(bf16[96,3072]{1,0:T(8,128)(2,1)} %param.12, pred[]{:T(512)S(6)} %eq.3), kind=kLoop, calls=%fused_computation.8 | loop fusion | flops 147456 | bytes 884737 | tf_op jit(solution)/shard_map/jit(_where)/select_n | solution.py:420
  7.7 2.1 %collective-permute-start.11 = (bf16[1,96,1536]{2,1,0:T(8,128)(2,1)S(1)}, bf16[1,96,1536]{2,1,0:T(8,128)(2,1)S(1)}, u32[]{:S(2)}, u32[]{:S(2)}) collective-permute-start(bf16[1,96,1536]{2,1,0:T(8,128)(2,1)S(1)} %bitcast.21), channel_id=1, source_target_pairs={{0,2},{2,0},{1,3},{3,1},{4,6},{6,4},{5,7},{7,5},{8,10},{10,8},{9,1... | collective-permute-start | bytes 884744 | tf_op jit(solution)/shard_map/ppermute | solution.py:339
  9.8 1.3 %collective-permute-start.6 = (bf16[1,96,1536]{2,1,0:T(8,128)(2,1)S(1)}, bf16[1,96,1536]{2,1,0:T(8,128)(2,1)S(1)}, u32[]{:S(2)}, u32[]{:S(2)}) collective-permute-start(bf16[1,96,1536]{2,1,0:T(8,128)(2,1)S(1)} %bitcast.22), channel_id=1, source_target_pairs={{0,4},{4,0},{8,12},{12,8},{1,5},{5,1},{9,13},{13,9},{2,6},{6,2},{1... | collective-permute-start | bytes 884744 | tf_op jit(solution)/shard_map/ppermute | solution.py:339
  11.1 2.3 %collective-permute-start.4 = (bf16[1,96,1536]{2,1,0:T(8,128)(2,1)S(1)}, bf16[1,96,1536]{2,1,0:T(8,128)(2,1)S(1)}, u32[]{:S(2)}, u32[]{:S(2)}) collective-permute-start(bf16[1,96,1536]{2,1,0:T(8,128)(2,1)S(1)} %bitcast.23), channel_id=1, source_target_pairs={{0,8},{4,12},{8,0},{12,4},{1,9},{5,13},{9,1},{13,5},{2,10},{6,14},... | collective-permute-start | bytes 884744 | tf_op jit(solution)/shard_map/ppermute | solution.py:339
  13.4 1.1 fusion
  14.6 0.9 dynamic-slice_bitcast_fusion
  15.5 1.1 fusion.1
  16.6 1.1 %pad_maximum_fusion = (bf16[192,1536]{1,0:T(8,128)(2,1)}, bf16[192,1536]{1,0:T(8,128)(2,1)}) fusion(bf16[192,768]{1,0:T(8,128)(2,1)S(1)} %get-tuple-element.50, bf16[192,768]{1,0:T(8,128)(2,1)S(1)} %get-tuple-element.48, bf16[192,768]{1,0:T(8,128)(2,1)S(1)} %get-tuple-element.49, bf16[192,768]{1,0:T(8,128)(2,1)S(1)} %get-tuple-element.47), kind=kLoop, calls=%fused_computation | loop fusion | flops 2359296 | bytes 2359296 | tf_op jit(solution)/shard_map/concatenate | solution.py:433
  17.7 0.3 collective-permute-start.8
  18.0 0.0 collective-permute-done.11
  18.0 0.1 pad_maximum_fusion.3.refs_1_.refs_3_
  18.0 1.3 %collective-permute-start.12 = (bf16[2,96,1536]{2,1,0:T(8,128)(2,1)S(1)}, bf16[2,96,1536]{2,1,0:T(8,128)(2,1)S(1)}, u32[]{:S(2)}, u32[]{:S(2)}) collective-permute-start(bf16[2,96,1536]{2,1,0:T(8,128)(2,1)S(1)} %pad_maximum_fusion.3.refs_1_.refs_3_), channel_id=1, source_target_pairs={{0,16},{16,0},{1,17},{17,1},{2,18},{18,2},{3,19},{19,3},{4,20},{20... | collective-permute-start | bytes 1769480 | tf_op jit(solution)/shard_map/ppermute | solution.py:339
  19.3 4.4 %collective-permute-done.6 = bf16[1,96,1536]{2,1,0:T(8,128)(2,1)S(1)} collective-permute-done((bf16[1,96,1536]{2,1,0:T(8,128)(2,1)S(1)}, bf16[1,96,1536]{2,1,0:T(8,128)(2,1)S(1)}, u32[]{:S(2)}, u32[]{:S(2)}) %collective-permute-start.6) | collective-permute-done | bytes 294944 | tf_op jit(solution)/shard_map/ppermute | solution.py:339
  23.7 1.1 collective-permute-done.8.refs_11_
  24.8 1.3 %collective-permute-start.9 = (bf16[1,96,1536]{2,1,0:T(8,128)(2,1)S(1)}, bf16[1,96,1536]{2,1,0:T(8,128)(2,1)S(1)}, u32[]{:S(2)}, u32[]{:S(2)}) collective-permute-start(bf16[1,96,1536]{2,1,0:T(8,128)(2,1)S(1)} %collective-permute-done.4), channel_id=1, source_target_pairs={{0,4},{4,0},{8,12},{12,8},{1,5},{5,1},{9,13},{13,9},{2,6},{6,2},{1... | collective-permute-start | bytes 884744 | tf_op jit(solution)/shard_map/ppermute | solution.py:339
  26.1 0.3 collective-permute-start.10
  26.3 4.4 %collective-permute-done.9 = bf16[1,96,1536]{2,1,0:T(8,128)(2,1)S(1)} collective-permute-done((bf16[1,96,1536]{2,1,0:T(8,128)(2,1)S(1)}, bf16[1,96,1536]{2,1,0:T(8,128)(2,1)S(1)}, u32[]{:S(2)}, u32[]{:S(2)}) %collective-permute-start.9) | collective-permute-done | bytes 294944 | tf_op jit(solution)/shard_map/ppermute | solution.py:339
  30.7 0.9 pad_maximum_fusion.2
  31.6 0.8 collective-permute-done.10
  32.4 0.0 all-gather.3.cloned.1.call-update
  32.4 3.2 %collective-permute-start = (bf16[192,1536]{1,0:T(8,128)(2,1)}, bf16[192,1536]{1,0:T(8,128)(2,1)S(1)}, u32[]{:S(2)}, u32[]{:S(2)}) collective-permute-start(bf16[192,1536]{1,0:T(8,128)(2,1)} %refs_0_.1), channel_id=1, source_target_pairs={{0,1},{1,0},{2,3},{3,2},{4,5},{5,4},{6,7},{7,6},{8,9},{9,8},{10,11... | collective-permute-start | bytes 1769480 | tf_op jit(solution)/shard_map/ppermute | solution.py:454
  35.6 0.1 collective-permute-start.1
  35.7 0.4 collective-permute-start.13
  36.1 1.9 %collective-permute-start.5 = (bf16[192,1536]{1,0:T(8,128)(2,1)}, bf16[192,1536]{1,0:T(8,128)(2,1)S(1)}, u32[]{:S(2)}, u32[]{:S(2)}) collective-permute-start(bf16[192,1536]{1,0:T(8,128)(2,1)} %get-tuple-element.31), channel_id=1, source_target_pairs={{0,8},{8,0},{1,9},{9,1},{2,10},{10,2},{3,11},{11,3},{4,12},{12,4},... | collective-permute-start | bytes 1769480 | tf_op jit(solution)/shard_map/ppermute | solution.py:356
  38.1 1.3 %collective-permute-start.16 = (bf16[2,96,1536]{2,1,0:T(8,128)(2,1)S(1)}, bf16[2,96,1536]{2,1,0:T(8,128)(2,1)S(1)}, u32[]{:S(2)}, u32[]{:S(2)}) collective-permute-start(bf16[2,96,1536]{2,1,0:T(8,128)(2,1)S(1)} %constant_dynamic-update-slice_fusion.refs_5_.refs_7_), channel_id=1, source_target_pairs={{0,16},{16,0},{1,17},{17,1},{2,18},{18,2},{3,19},{19,3},{4,20},{20... | collective-permute-start | bytes 1769480 | tf_op jit(solution)/shard_map/ppermute | solution.py:339
  39.4 0.0 collective-permute-done.refs_2_
  39.4 2.6 %collective-permute-start.2 = (bf16[192,1536]{1,0:T(8,128)(2,1)}, bf16[192,1536]{1,0:T(8,128)(2,1)S(1)}, u32[]{:S(2)}, u32[]{:S(2)}) collective-permute-start(bf16[192,1536]{1,0:T(8,128)(2,1)} %refs_0_.1), channel_id=1, source_target_pairs={{1,2},{2,1},{5,6},{6,5},{9,10},{10,9},{13,14},{14,13},{17,18},{18,... | collective-permute-start | bytes 1769480 | tf_op jit(solution)/shard_map/ppermute | solution.py:456
  42.0 0.0 collective-permute-done.1.refs_3_
  42.0 0.7 collective-permute-start.7
  42.7 3.2 %collective-permute-start.3 = (bf16[192,1536]{1,0:T(8,128)(2,1)}, bf16[192,1536]{1,0:T(8,128)(2,1)S(1)}, u32[]{:S(2)}, u32[]{:S(2)}) collective-permute-start(bf16[192,1536]{1,0:T(8,128)(2,1)} %refs_1_.1), channel_id=1, source_target_pairs={{1,2},{2,1},{5,6},{6,5},{9,10},{10,9},{13,14},{14,13},{17,18},{18,... | collective-permute-start | bytes 1769480 | tf_op jit(solution)/shard_map/ppermute | solution.py:456
  45.9 18.9 %collective-permute-done.5.refs_0_ = bf16[192,1536]{1,0:T(8,128)(2,1)S(1)} collective-permute-done((bf16[192,1536]{1,0:T(8,128)(2,1)}, bf16[192,1536]{1,0:T(8,128)(2,1)S(1)}, u32[]{:S(2)}, u32[]{:S(2)}) %collective-permute-start.5) | collective-permute-done | bytes 589856 | tf_op jit(solution)/shard_map/ppermute | solution.py:356
  64.8 0.9 collective-permute-start.15
  65.7 0.1 collective-permute-start.14
  65.8 0.0 collective-permute-done.2.refs_4_
  65.8 0.4 collective-permute-start.17
  66.2 2.6 %collective-permute-done.7.refs_1_ = bf16[192,1536]{1,0:T(8,128)(2,1)S(1)} collective-permute-done((bf16[192,1536]{1,0:T(8,128)(2,1)}, bf16[192,1536]{1,0:T(8,128)(2,1)S(1)}, u32[]{:S(2)}, u32[]{:S(2)}) %collective-permute-start.7) | collective-permute-done | bytes 589856 | tf_op jit(solution)/shard_map/ppermute | solution.py:356
  68.8 0.0 collective-permute-start.21
  68.8 0.0 collective-permute-done.3.refs_5_
  68.9 1.4 %collective-permute-start.20 = (bf16[192,1536]{1,0:T(8,128)(2,1)}, bf16[192,1536]{1,0:T(8,128)(2,1)}, u32[]{:S(2)}, u32[]{:S(2)}) collective-permute-start(bf16[192,1536]{1,0:T(8,128)(2,1)} %get-tuple-element.42), channel_id=1, source_target_pairs={{0,8},{8,0},{1,9},{9,1},{2,10},{10,2},{3,11},{11,3},{4,12},{12,4},... | collective-permute-start | bytes 1769480 | tf_op jit(solution)/shard_map/ppermute | solution.py:466
  70.4 0.1 collective-permute-start.18
  70.5 6.0 %attend.1 = (f32[192,1536]{1,0:T(8,128)}, f32[192,128]{1,0:T(8,128)}) custom-call(s32[1,6]{1,0:T(1,128)} %pattern.5, bf16[192,1536]{1,0:T(8,128)(2,1)} %q.5, bf16[192,1536]{1,0:T(8,128)(2,1)} %refs_0_.1, bf16[192,1536]{1,0:T(8,128)(2,1)} %refs_1_.1, bf16[192,1536]{1,0:T(8,128)(2,1)} %copy-done.8, bf16[192,1536]{1,0:T(8,128)(2,1)} %copy-done.9, ...), custom_call_target="tpu_custom_call" | custom-call | flops 1019215872 | bytes 5308416 | tf_op jit(solution)/shard_map/attend/pallas_call | solution.py:104
  76.5 4.0 %close.1.ready = bf16[192,768]{1,0:T(8,128)(2,1)} custom-call(s32[1,6]{1,0:T(1,128)} %pattern.5, bf16[192,1536]{1,0:T(8,128)(2,1)} %q.5, f32[192,1536]{1,0:T(8,128)} %get-tuple-element.26.part, f32[192,128]{1,0:T(8,128)} %get-tuple-element.27.stats, bf16[192,1536]{1,0:T(8,128)(2,1)} %copy-done.12, bf16[192,1536]{1,0:T(8,128)(2,1)} %copy-done.13), custom_call_target="tpu_custom_call" | custom-call | flops 339738624 | bytes 2359296 | tf_op jit(solution)/shard_map/close/pallas_call | solution.py:170
  80.6 3.6 %collective-permute-done.19.refs_12_ = bf16[48,3072]{1,0:T(8,128)(2,1)} collective-permute-done((bf16[48,3072]{1,0:T(8,128)(2,1)}, bf16[48,3072]{1,0:T(8,128)(2,1)}, u32[]{:S(2)}, u32[]{:S(2)}) %collective-permute-start.19) | collective-permute-done | bytes 294944 | tf_op jit(solution)/shard_map/ppermute | solution.py:339
  84.2 0.0 all-gather.3.cloned.1.call-done
  84.2 5.6 %begin.1.so_far = f32[192,3072]{1,0:T(8,128)} custom-call(bf16[192,3072]{1,0:T(8,128)(2,1)} %hidden.1, bf16[192,768]{1,0:T(8,128)(2,1)} %close.1.ready, bf16[8,2,96,1536]{3,2,1,0:T(8,128)(2,1)} %bitcast.19, bf16[2,96,1536]{2,1,0:T(8,128)(2,1)} %copy-done, bf16[2,96,1536]{2,1,0:T(8,128)(2,1)} %copy-done.3, bf16[2,96,1536]{2,1,0:T(8,128)(2,1)} %copy-done.2, ...), custom_call_target="tpu_custom_call" | custom-call | flops 905969664 | bytes 9437184 | tf_op jit(solution)/shard_map/begin/pallas_call | solution.py:300
  89.8 5.7 %collective-permute-done.21.refs_1_ = bf16[192,1536]{1,0:T(8,128)(2,1)} collective-permute-done((bf16[192,1536]{1,0:T(8,128)(2,1)}, bf16[192,1536]{1,0:T(8,128)(2,1)}, u32[]{:S(2)}, u32[]{:S(2)}) %collective-permute-start.21) | collective-permute-done | bytes 589856 | tf_op jit(solution)/shard_map/ppermute | solution.py:466
  95.5 2.6 %collective-permute-done.20.refs_0_ = bf16[192,1536]{1,0:T(8,128)(2,1)} collective-permute-done((bf16[192,1536]{1,0:T(8,128)(2,1)}, bf16[192,1536]{1,0:T(8,128)(2,1)}, u32[]{:S(2)}, u32[]{:S(2)}) %collective-permute-start.20) | collective-permute-done | bytes 589856 | tf_op jit(solution)/shard_map/ppermute | solution.py:466
  98.1 7.1 %finish.1 = bf16[192,3072]{1,0:T(8,128)(2,1)} custom-call(s32[1,6]{1,0:T(1,128)} %pattern.5, bf16[192,1536]{1,0:T(8,128)(2,1)} %q.5, f32[192,1536]{1,0:T(8,128)} %get-tuple-element.26.part, f32[192,128]{1,0:T(8,128)} %get-tuple-element.27.stats, f32[192,3072]{1,0:T(8,128)} %begin.1.so_far, bf16[192,1536]{1,0:T(8,128)(2,1)} %collective-permute-done.20.refs_0_, ...), custom_call_target="tpu_custom_call" | custom-call | flops 905969664 | bytes 8257536 | tf_op jit(solution)/shard_map/finish/pallas_call | solution.py:321
  (40 shorter events, 0.1 us)
Async XLA Ops:
  6.5 8.0 %copy-start.7 = (bf16[192,3072]{1,0:T(8,128)(2,1)S(1)}, bf16[192,3072]{1,0:T(8,128)(2,1)}, u32[]{:S(2)}) copy-start(bf16[192,3072]{1,0:T(8,128)(2,1)} %param.11) | copy-start | bytes 3538948
  6.5 77.7 %all-gather.3.cloned.1.call-start = ((), (), s32[]{:S(2)}) async-start(), calls=%async_computation | async-start | bytes 5308416 | tf_op jit(solution)/shard_map/all_gather | solution.py:473
  7.7 10.2 %collective-permute-start.11 = (bf16[1,96,1536]{2,1,0:T(8,128)(2,1)S(1)}, bf16[1,96,1536]{2,1,0:T(8,128)(2,1)S(1)}, u32[]{:S(2)}, u32[]{:S(2)}) collective-permute-start(bf16[1,96,1536]{2,1,0:T(8,128)(2,1)S(1)} %bitcast.21), channel_id=1, source_target_pairs={{0,2},{2,0},{1,3},{3,1},{4,6},{6,4},{5,7},{7,5},{8,10},{10,8},{9,1... | collective-permute-start | bytes 884744 | tf_op jit(solution)/shard_map/ppermute | solution.py:339
  9.8 13.9 %collective-permute-start.6 = (bf16[1,96,1536]{2,1,0:T(8,128)(2,1)S(1)}, bf16[1,96,1536]{2,1,0:T(8,128)(2,1)S(1)}, u32[]{:S(2)}, u32[]{:S(2)}) collective-permute-start(bf16[1,96,1536]{2,1,0:T(8,128)(2,1)S(1)} %bitcast.22), channel_id=1, source_target_pairs={{0,4},{4,0},{8,12},{12,8},{1,5},{5,1},{9,13},{13,9},{2,6},{6,2},{1... | collective-permute-start | bytes 884744 | tf_op jit(solution)/shard_map/ppermute | solution.py:339
  11.1 12.6 %collective-permute-start.4 = (bf16[1,96,1536]{2,1,0:T(8,128)(2,1)S(1)}, bf16[1,96,1536]{2,1,0:T(8,128)(2,1)S(1)}, u32[]{:S(2)}, u32[]{:S(2)}) collective-permute-start(bf16[1,96,1536]{2,1,0:T(8,128)(2,1)S(1)} %bitcast.23), channel_id=1, source_target_pairs={{0,8},{4,12},{8,0},{12,4},{1,9},{5,13},{9,1},{13,5},{2,10},{6,14},... | collective-permute-start | bytes 884744 | tf_op jit(solution)/shard_map/ppermute | solution.py:339
  17.7 7.1 %collective-permute-start.8 = (bf16[48,3072]{1,0:T(8,128)(2,1)S(1)}, bf16[48,3072]{1,0:T(8,128)(2,1)}, u32[]{:S(2)}, u32[]{:S(2)}) collective-permute-start(bf16[48,3072]{1,0:T(8,128)(2,1)S(1)} %get-tuple-element.33), channel_id=1, source_target_pairs={{0,2},{1,3},{2,0},{3,1},{4,6},{5,7},{6,4},{7,5},{8,10},{9,11},{10,... | collective-permute-start | bytes 884744 | tf_op jit(solution)/shard_map/ppermute | solution.py:339
  18.0 20.0 %copy-start = (bf16[2,96,1536]{2,1,0:T(8,128)(2,1)}, bf16[2,96,1536]{2,1,0:T(8,128)(2,1)S(1)}, u32[]{:S(2)}) copy-start(bf16[2,96,1536]{2,1,0:T(8,128)(2,1)S(1)} %pad_maximum_fusion.3.refs_1_.refs_3_) | copy-start | bytes 1769476
  18.0 14.3 %collective-permute-start.12 = (bf16[2,96,1536]{2,1,0:T(8,128)(2,1)S(1)}, bf16[2,96,1536]{2,1,0:T(8,128)(2,1)S(1)}, u32[]{:S(2)}, u32[]{:S(2)}) collective-permute-start(bf16[2,96,1536]{2,1,0:T(8,128)(2,1)S(1)} %pad_maximum_fusion.3.refs_1_.refs_3_), channel_id=1, source_target_pairs={{0,16},{16,0},{1,17},{17,1},{2,18},{18,2},{3,19},{19,3},{4,20},{20... | collective-permute-start | bytes 1769480 | tf_op jit(solution)/shard_map/ppermute | solution.py:339
  24.8 5.9 %collective-permute-start.9 = (bf16[1,96,1536]{2,1,0:T(8,128)(2,1)S(1)}, bf16[1,96,1536]{2,1,0:T(8,128)(2,1)S(1)}, u32[]{:S(2)}, u32[]{:S(2)}) collective-permute-start(bf16[1,96,1536]{2,1,0:T(8,128)(2,1)S(1)} %collective-permute-done.4), channel_id=1, source_target_pairs={{0,4},{4,0},{8,12},{12,8},{1,5},{5,1},{9,13},{13,9},{2,6},{6,2},{1... | collective-permute-start | bytes 884744 | tf_op jit(solution)/shard_map/ppermute | solution.py:339
  26.1 6.3 %collective-permute-start.10 = (bf16[1,96,1536]{2,1,0:T(8,128)(2,1)S(1)}, bf16[1,96,1536]{2,1,0:T(8,128)(2,1)S(1)}, u32[]{:S(2)}, u32[]{:S(2)}) collective-permute-start(bf16[1,96,1536]{2,1,0:T(8,128)(2,1)S(1)} %collective-permute-done.6), channel_id=1, source_target_pairs={{0,2},{2,0},{1,3},{3,1},{4,6},{6,4},{5,7},{7,5},{8,10},{10,8},{9,1... | collective-permute-start | bytes 884744 | tf_op jit(solution)/shard_map/ppermute | solution.py:339
  32.4 44.1 %copy-start.2 = (bf16[2,96,1536]{2,1,0:T(8,128)(2,1)}, bf16[2,96,1536]{2,1,0:T(8,128)(2,1)S(1)}, u32[]{:S(2)}) copy-start(bf16[2,96,1536]{2,1,0:T(8,128)(2,1)S(1)} %collective-permute-done.12.refs_3_.refs_5_) | copy-start | bytes 1769476
  32.4 7.0 %collective-permute-start = (bf16[192,1536]{1,0:T(8,128)(2,1)}, bf16[192,1536]{1,0:T(8,128)(2,1)S(1)}, u32[]{:S(2)}, u32[]{:S(2)}) collective-permute-start(bf16[192,1536]{1,0:T(8,128)(2,1)} %refs_0_.1), channel_id=1, source_target_pairs={{0,1},{1,0},{2,3},{3,2},{4,5},{5,4},{6,7},{7,6},{8,9},{9,8},{10,11... | collective-permute-start | bytes 1769480 | tf_op jit(solution)/shard_map/ppermute | solution.py:454
  35.6 6.4 %collective-permute-start.1 = (bf16[192,1536]{1,0:T(8,128)(2,1)}, bf16[192,1536]{1,0:T(8,128)(2,1)S(1)}, u32[]{:S(2)}, u32[]{:S(2)}) collective-permute-start(bf16[192,1536]{1,0:T(8,128)(2,1)} %refs_1_.1), channel_id=1, source_target_pairs={{0,1},{1,0},{2,3},{3,2},{4,5},{5,4},{6,7},{7,6},{8,9},{9,8},{10,11... | collective-permute-start | bytes 1769480 | tf_op jit(solution)/shard_map/ppermute | solution.py:454
  35.7 7.0 %collective-permute-start.13 = (bf16[2,96,1536]{2,1,0:T(8,128)(2,1)S(1)}, bf16[2,96,1536]{2,1,0:T(8,128)(2,1)S(1)}, u32[]{:S(2)}, u32[]{:S(2)}) collective-permute-start(bf16[2,96,1536]{2,1,0:T(8,128)(2,1)S(1)} %pad_maximum_fusion.3.refs_1_.refs_3_), channel_id=1, source_target_pairs={{0,1},{1,0},{2,3},{3,2},{4,5},{5,4},{6,7},{7,6},{8,9},{9,8},{10,11... | collective-permute-start | bytes 1769480 | tf_op jit(solution)/shard_map/ppermute | solution.py:339
  36.1 28.7 %collective-permute-start.5 = (bf16[192,1536]{1,0:T(8,128)(2,1)}, bf16[192,1536]{1,0:T(8,128)(2,1)S(1)}, u32[]{:S(2)}, u32[]{:S(2)}) collective-permute-start(bf16[192,1536]{1,0:T(8,128)(2,1)} %get-tuple-element.31), channel_id=1, source_target_pairs={{0,8},{8,0},{1,9},{9,1},{2,10},{10,2},{3,11},{11,3},{4,12},{12,4},... | collective-permute-start | bytes 1769480 | tf_op jit(solution)/shard_map/ppermute | solution.py:356
  38.1 38.4 %copy-start.1 = (bf16[2,96,1536]{2,1,0:T(8,128)(2,1)}, bf16[2,96,1536]{2,1,0:T(8,128)(2,1)S(1)}, u32[]{:S(2)}) copy-start(bf16[2,96,1536]{2,1,0:T(8,128)(2,1)S(1)} %constant_dynamic-update-slice_fusion.refs_5_.refs_7_) | copy-start | bytes 1769476
  38.1 27.6 %collective-permute-start.16 = (bf16[2,96,1536]{2,1,0:T(8,128)(2,1)S(1)}, bf16[2,96,1536]{2,1,0:T(8,128)(2,1)S(1)}, u32[]{:S(2)}, u32[]{:S(2)}) collective-permute-start(bf16[2,96,1536]{2,1,0:T(8,128)(2,1)S(1)} %constant_dynamic-update-slice_fusion.refs_5_.refs_7_), channel_id=1, source_target_pairs={{0,16},{16,0},{1,17},{17,1},{2,18},{18,2},{3,19},{19,3},{4,20},{20... | collective-permute-start | bytes 1769480 | tf_op jit(solution)/shard_map/ppermute | solution.py:339
  39.4 30.9 %copy-start.8 = (bf16[192,1536]{1,0:T(8,128)(2,1)}, bf16[192,1536]{1,0:T(8,128)(2,1)S(1)}, u32[]{:S(2)}) copy-start(bf16[192,1536]{1,0:T(8,128)(2,1)S(1)} %collective-permute-done.refs_2_) | copy-start | bytes 1769476
  39.4 26.4 %collective-permute-start.2 = (bf16[192,1536]{1,0:T(8,128)(2,1)}, bf16[192,1536]{1,0:T(8,128)(2,1)S(1)}, u32[]{:S(2)}, u32[]{:S(2)}) collective-permute-start(bf16[192,1536]{1,0:T(8,128)(2,1)} %refs_0_.1), channel_id=1, source_target_pairs={{1,2},{2,1},{5,6},{6,5},{9,10},{10,9},{13,14},{14,13},{17,18},{18,... | collective-permute-start | bytes 1769480 | tf_op jit(solution)/shard_map/ppermute | solution.py:456
  42.0 28.3 %copy-start.9 = (bf16[192,1536]{1,0:T(8,128)(2,1)}, bf16[192,1536]{1,0:T(8,128)(2,1)S(1)}, u32[]{:S(2)}) copy-start(bf16[192,1536]{1,0:T(8,128)(2,1)S(1)} %collective-permute-done.1.refs_3_) | copy-start | bytes 1769476
  42.0 26.8 %collective-permute-start.7 = (bf16[192,1536]{1,0:T(8,128)(2,1)}, bf16[192,1536]{1,0:T(8,128)(2,1)S(1)}, u32[]{:S(2)}, u32[]{:S(2)}) collective-permute-start(bf16[192,1536]{1,0:T(8,128)(2,1)} %get-tuple-element.31), channel_id=1, source_target_pairs={{0,4},{4,0},{1,5},{5,1},{2,6},{6,2},{3,7},{7,3},{8,12},{12,8},{9,1... | collective-permute-start | bytes 1769480 | tf_op jit(solution)/shard_map/ppermute | solution.py:356
  42.7 33.8 %copy-start.3 = (bf16[2,96,1536]{2,1,0:T(8,128)(2,1)}, bf16[2,96,1536]{2,1,0:T(8,128)(2,1)S(1)}, u32[]{:S(2)}) copy-start(bf16[2,96,1536]{2,1,0:T(8,128)(2,1)S(1)} %collective-permute-done.13.refs_2_.refs_4_) | copy-start | bytes 1769476
  42.7 26.1 %collective-permute-start.3 = (bf16[192,1536]{1,0:T(8,128)(2,1)}, bf16[192,1536]{1,0:T(8,128)(2,1)S(1)}, u32[]{:S(2)}, u32[]{:S(2)}) collective-permute-start(bf16[192,1536]{1,0:T(8,128)(2,1)} %refs_1_.1), channel_id=1, source_target_pairs={{1,2},{2,1},{5,6},{6,5},{9,10},{10,9},{13,14},{14,13},{17,18},{18,... | collective-permute-start | bytes 1769480 | tf_op jit(solution)/shard_map/ppermute | solution.py:456
  64.8 5.5 %copy-start.12 = (bf16[192,1536]{1,0:T(8,128)(2,1)}, bf16[192,1536]{1,0:T(8,128)(2,1)S(1)}, u32[]{:S(2)}) copy-start(bf16[192,1536]{1,0:T(8,128)(2,1)S(1)} %collective-permute-done.5.refs_0_) | copy-start | bytes 1769476
  64.8 5.5 %collective-permute-start.15 = (bf16[2,96,1536]{2,1,0:T(8,128)(2,1)S(1)}, bf16[2,96,1536]{2,1,0:T(8,128)(2,1)S(1)}, u32[]{:S(2)}, u32[]{:S(2)}) collective-permute-start(bf16[2,96,1536]{2,1,0:T(8,128)(2,1)S(1)} %constant_dynamic-update-slice_fusion.refs_5_.refs_7_), channel_id=1, source_target_pairs={{0,1},{1,0},{2,3},{3,2},{4,5},{5,4},{6,7},{7,6},{8,9},{9,8},{10,11... | collective-permute-start | bytes 1769480 | tf_op jit(solution)/shard_map/ppermute | solution.py:339
  65.7 10.8 %copy-start.4 = (bf16[2,96,1536]{2,1,0:T(8,128)(2,1)}, bf16[2,96,1536]{2,1,0:T(8,128)(2,1)S(1)}, u32[]{:S(2)}) copy-start(bf16[2,96,1536]{2,1,0:T(8,128)(2,1)S(1)} %collective-permute-done.16.refs_7_.refs_9_) | copy-start | bytes 1769476
  65.7 4.6 %collective-permute-start.14 = (bf16[2,96,1536]{2,1,0:T(8,128)(2,1)S(1)}, bf16[2,96,1536]{2,1,0:T(8,128)(2,1)S(1)}, u32[]{:S(2)}, u32[]{:S(2)}) collective-permute-start(bf16[2,96,1536]{2,1,0:T(8,128)(2,1)S(1)} %collective-permute-done.12.refs_3_.refs_5_), channel_id=1, source_target_pairs={{0,1},{1,0},{2,3},{3,2},{4,5},{5,4},{6,7},{7,6},{8,9},{9,8},{10,11... | collective-permute-start | bytes 1769480 | tf_op jit(solution)/shard_map/ppermute | solution.py:339
  65.8 4.5 %copy-start.10 = (bf16[192,1536]{1,0:T(8,128)(2,1)}, bf16[192,1536]{1,0:T(8,128)(2,1)S(1)}, u32[]{:S(2)}) copy-start(bf16[192,1536]{1,0:T(8,128)(2,1)S(1)} %collective-permute-done.2.refs_4_) | copy-start | bytes 1769476
  65.8 18.4 %collective-permute-start.17 = (bf16[2,96,1536]{2,1,0:T(8,128)(2,1)S(1)}, bf16[2,96,1536]{2,1,0:T(8,128)(2,1)}, u32[]{:S(2)}, u32[]{:S(2)}) collective-permute-start(bf16[2,96,1536]{2,1,0:T(8,128)(2,1)S(1)} %collective-permute-done.16.refs_7_.refs_9_), channel_id=1, source_target_pairs={{0,1},{1,0},{2,3},{3,2},{4,5},{5,4},{6,7},{7,6},{8,9},{9,8},{10,11... | collective-permute-start | bytes 1769480 | tf_op jit(solution)/shard_map/ppermute | solution.py:339
  68.8 1.5 %copy-start.13 = (bf16[192,1536]{1,0:T(8,128)(2,1)}, bf16[192,1536]{1,0:T(8,128)(2,1)S(1)}, u32[]{:S(2)}) copy-start(bf16[192,1536]{1,0:T(8,128)(2,1)S(1)} %collective-permute-done.7.refs_1_) | copy-start | bytes 1769476
  68.8 26.7 %collective-permute-start.21 = (bf16[192,1536]{1,0:T(8,128)(2,1)}, bf16[192,1536]{1,0:T(8,128)(2,1)}, u32[]{:S(2)}, u32[]{:S(2)}) collective-permute-start(bf16[192,1536]{1,0:T(8,128)(2,1)} %get-tuple-element.42), channel_id=1, source_target_pairs={{0,4},{4,0},{1,5},{5,1},{2,6},{6,2},{3,7},{7,3},{8,12},{12,8},{9,1... | collective-permute-start | bytes 1769480 | tf_op jit(solution)/shard_map/ppermute | solution.py:466
  68.8 1.5 %copy-start.11 = (bf16[192,1536]{1,0:T(8,128)(2,1)}, bf16[192,1536]{1,0:T(8,128)(2,1)S(1)}, u32[]{:S(2)}) copy-start(bf16[192,1536]{1,0:T(8,128)(2,1)S(1)} %collective-permute-done.3.refs_5_) | copy-start | bytes 1769476
  68.9 29.2 %collective-permute-start.20 = (bf16[192,1536]{1,0:T(8,128)(2,1)}, bf16[192,1536]{1,0:T(8,128)(2,1)}, u32[]{:S(2)}, u32[]{:S(2)}) collective-permute-start(bf16[192,1536]{1,0:T(8,128)(2,1)} %get-tuple-element.42), channel_id=1, source_target_pairs={{0,8},{8,0},{1,9},{9,1},{2,10},{10,2},{3,11},{11,3},{4,12},{12,4},... | collective-permute-start | bytes 1769480 | tf_op jit(solution)/shard_map/ppermute | solution.py:466
  70.3 6.2 %copy-start.5 = (bf16[2,96,1536]{2,1,0:T(8,128)(2,1)}, bf16[2,96,1536]{2,1,0:T(8,128)(2,1)S(1)}, u32[]{:S(2)}) copy-start(bf16[2,96,1536]{2,1,0:T(8,128)(2,1)S(1)} %collective-permute-done.15.refs_6_.refs_8_) | copy-start | bytes 1769476
  70.3 13.9 %collective-permute-start.19 = (bf16[48,3072]{1,0:T(8,128)(2,1)}, bf16[48,3072]{1,0:T(8,128)(2,1)}, u32[]{:S(2)}, u32[]{:S(2)}) collective-permute-start(bf16[48,3072]{1,0:T(8,128)(2,1)} %get-tuple-element.41), channel_id=1, source_target_pairs={{0,3},{1,2},{2,1},{3,0},{4,7},{5,6},{6,5},{7,4},{8,11},{9,10},{10,... | collective-permute-start | bytes 884744 | tf_op jit(solution)/shard_map/ppermute | solution.py:339
  70.4 6.2 %copy-start.6 = (bf16[2,96,1536]{2,1,0:T(8,128)(2,1)}, bf16[2,96,1536]{2,1,0:T(8,128)(2,1)S(1)}, u32[]{:S(2)}) copy-start(bf16[2,96,1536]{2,1,0:T(8,128)(2,1)S(1)} %collective-permute-done.14.refs_4_.refs_6_) | copy-start | bytes 1769476
  70.4 13.8 %collective-permute-start.18 = (bf16[48,3072]{1,0:T(8,128)(2,1)S(1)}, bf16[48,3072]{1,0:T(8,128)(2,1)}, u32[]{:S(2)}, u32[]{:S(2)}) collective-permute-start(bf16[48,3072]{1,0:T(8,128)(2,1)S(1)} %get-tuple-element.39), channel_id=1, source_target_pairs={{0,1},{1,0},{2,3},{3,2},{4,5},{5,4},{6,7},{7,6},{8,9},{9,8},{10,11... | collective-permute-start | bytes 884744 | tf_op jit(solution)/shard_map/ppermute | solution.py:339
Sparse Core Ops, SparseCore 0:
  32.5 51.5 all-gather.2
